TPU v7x, 32 devices: a whole 2x2x4 slice. The times are simulated.
32 devices in a mesh: rep: 2 (over x), sec: 8 (over z, y), term: 2 (over core).
Axes of the slice: x: 2, y: 2, z: 4, core: 2. Of those that a mesh axis runs over, the one named last changes fastest.
Arguments:
- wavefunction: bfloat16 [512, 128, 128], P(('rep', 'sec')), parts along dimension 0, may hold values from -6 to 6
- left_operator: bfloat16 [4, 512, 128, 128], P('term', ('rep', 'sec')), parts along dimension 1, may hold values from -3 to 3
- right_operator: bfloat16 [4, 512, 128, 128], P('term', ('rep', 'sec')), parts along dimension 1, may hold values from -3 to 3
- target_owner: int32 [4, 512, 1], P('term', ('rep', 'sec')), parts along dimension 1, may hold values from 0 to 7; in each aligned block of 32 rows (0 to 31, 32 to 63, ..., all dimensions but the last counted through in order) at most 8 rows name the same one
- target_local: int32 [4, 512], P('term', ('rep', 'sec')), parts along dimension 1, may hold values from 0 to 31
Outputs:
- sigma_two: bfloat16 [512, 128, 128], P(('rep', 'sec'), 'term'), parts along dimension 0
- rayleigh: float32 [2], P('rep'), parts along dimension 0
There are 2 independent parts, one for each index of `rep`. A program takes and returns all parts, laid end to end along the dimension named above; each array names one. Nothing has to cross between parts.
Inputs may be any that keep to these rules, and one draw needn't show every extreme that they name: `target_owner`: among the 32 source blocks of one term on one owner no owner is named more than 8 times, and one is named exactly 8 times.
All inputs are finite; a program needn't handle non-finite values.
Results may differ from a plain program's by a relative error of at most 0.006.
Values may be sent and summed in bfloat16 or wider, within the bound.
No kernel may reach another device: no remote copies, remote signals or barrier semaphores. Data moves between devices by JAX's collectives and lax.ppermute only.
A program may use at most 64 MiB of HBM per device.

v0:
```python
import jax
import jax.numpy as jnp
from jax import lax
from jax.sharding import PartitionSpec as P


def contribute(vector, left_operator, right_operator, target_owner, target_local):
    owners = lax.axis_size("sec")
    blocks = vector.shape[0]
    capacity = 2 * blocks // owners
    totals = jnp.zeros(vector.shape, jnp.float32)
    owner_ids = jnp.arange(owners, dtype=jnp.int32)
    for term_index in range(left_operator.shape[0]):
        partial_value = jnp.einsum(
            "bij,bjr->bir", left_operator[term_index], vector, preferred_element_type=jnp.float32
        ).astype(jnp.bfloat16)
        device = target_owner[term_index, :, 0]
        onehot = (device[:, None] == owner_ids[None, :]).astype(jnp.int32)
        earlier = jnp.cumsum(onehot, axis=0) - onehot
        position = jnp.sum(earlier * onehot, axis=1)
        slot_index = device * capacity + position
        outgoing = (
            jnp.zeros((owners * capacity,) + vector.shape[1:], jnp.bfloat16)
            .at[slot_index]
            .set(partial_value)
        )
        labels = (
            jnp.full((owners * capacity,), blocks, jnp.int32)
            .at[slot_index]
            .set(target_local[term_index])
        )
        outgoing = outgoing.reshape((owners, capacity) + vector.shape[1:])
        labels = labels.reshape(owners, capacity)
        right_blocks = right_operator[term_index]
        pieces = lax.all_to_all(outgoing, "sec", split_axis=0, concat_axis=0, tiled=True)
        labels_in = lax.all_to_all(labels, "sec", split_axis=0, concat_axis=0, tiled=True)
        picked = right_blocks[jnp.clip(labels_in, 0, blocks - 1)]
        result = jnp.einsum("scir,scrq->sciq", pieces, picked, preferred_element_type=jnp.float32)
        products, labels_in = (result, labels_in)
        totals = totals.at[labels_in.reshape(-1)].add(
            products.reshape((-1,) + vector.shape[1:]), mode="drop"
        )
    return totals


def per_device(wavefunction, left_operator, right_operator, target_owner, target_local):
    partial_one = contribute(
        wavefunction, left_operator, right_operator, target_owner, target_local
    )
    row_share = wavefunction.shape[1] // lax.axis_size("term")
    start = lax.axis_index("term") * row_share
    own_rows = lax.dynamic_slice_in_dim(wavefunction, start, row_share, 1).astype(jnp.float32)
    sigma_rows = lax.psum_scatter(partial_one, "term", scatter_dimension=1, tiled=True)
    cross_dot, self_dot = lax.psum(
        (jnp.sum(own_rows * sigma_rows), jnp.sum(own_rows * own_rows)), ("sec", "term")
    )
    rayleigh = cross_dot / self_dot
    residual_rows = sigma_rows - rayleigh * own_rows
    residual_sq = lax.psum(jnp.sum(residual_rows * residual_rows), ("sec", "term"))
    entries = (
        wavefunction.shape[0] * lax.axis_size("sec") * wavefunction.shape[1] * wavefunction.shape[2]
    )
    factor = lax.rsqrt(residual_sq / entries + 1e-06)
    direction = lax.all_gather(
        (residual_rows * factor).astype(jnp.bfloat16), "term", axis=1, tiled=True
    )
    partial_two = contribute(direction, left_operator, right_operator, target_owner, target_local)
    sigma_two = lax.psum_scatter(partial_two, "term", scatter_dimension=1, tiled=True).astype(
        jnp.bfloat16
    )
    return (sigma_two, jnp.reshape(rayleigh, (1,)))


def solution(mesh):
    placed = (
        P(("rep", "sec"), None, None),
        P("term", ("rep", "sec"), None, None),
        P("term", ("rep", "sec"), None, None),
        P("term", ("rep", "sec"), None),
        P("term", ("rep", "sec")),
    )
    return jax.shard_map(
        per_device,
        mesh=mesh,
        in_specs=placed,
        out_specs=(P(("rep", "sec"), "term", None), P("rep")),
        check_vma=False,
    )
```

profile of v0, /device:TPU:0, one launch (start us, length us, event | category | flops | bytes accessed | tf_op | source)
XLA Modules:
  0.0 392.8 jit_solution(5292790139937241001)
XLA Ops:
  7.2 0.7 slice_bitcast_fusion.4
  8.1 0.8 slice_bitcast_fusion.2
  9.0 0.7 fusion.17
  11.1 7.3 %all-to-all-start = ((s32[8,1,8]{2,1,0:T(1,128)}), s32[8,1,8]{2,1,0:T(1,128)S(1)}, u32[]{:S(2)}, u32[]{:S(2)}) async-start(s32[8,1,8]{2,1,0:T(1,128)} %bitcast.5), calls=%async_computation | async-start | bytes 8192 | tf_op jit(solution)/shard_map/all_to_all | solution.py:36
  19.7 5.0 %all-to-all-done = s32[8,1,8]{2,1,0:T(1,128)S(1)} async-done(((s32[8,1,8]{2,1,0:T(1,128)}), s32[8,1,8]{2,1,0:T(1,128)S(1)}, u32[]{:S(2)}, u32[]{:S(2)}) %all-to-all-start) | async-done | bytes 288 | tf_op jit(solution)/shard_map/all_to_all | solution.py:36
  24.7 3.3 all-to-all-start.2
  28.1 2.0 convolution_convert_fusion.3
  30.1 1.8 broadcast.174.clone.1
  31.9 4.6 %scatter_fusion = bf16[64,128,128]{2,1,0:T(8,128)(2,1)} fusion(bf16[64,128,128]{2,1,0:T(8,128)(2,1)} %broadcast.174.clone.1, s32[32]{0:T(128)S(1)} %get-tuple-element.11, bf16[32,128,128]{2,1,0:T(8,128)(2,1)S(1)} %convolution_convert_fusion.3), kind=kCustom, calls=%fused_computation.3 | custom fusion | bytes 3145856 | tf_op jit(solution)/shard_map/scatter | solution.py:25
  36.5 6.2 %all-to-all-start.1 = ((bf16[8,8,128,128]{3,2,1,0:T(8,128)(2,1)}), bf16[8,8,128,128]{3,2,1,0:T(8,128)(2,1)}, u32[]{:S(2)}, u32[]{:S(2)}) async-start(bf16[8,8,128,128]{3,2,1,0:T(8,128)(2,1)} %bitcast.8), calls=%async_computation.1 | async-start | bytes 4194304 | tf_op jit(solution)/shard_map/all_to_all | solution.py:35
  42.7 1.4 convolution_convert_fusion.2
  44.1 1.9 broadcast.174.clone.2
  46.0 4.6 %scatter_fusion.2 = bf16[64,128,128]{2,1,0:T(8,128)(2,1)} fusion(bf16[64,128,128]{2,1,0:T(8,128)(2,1)} %broadcast.174.clone.2, s32[32]{0:T(128)S(1)} %get-tuple-element.10, bf16[32,128,128]{2,1,0:T(8,128)(2,1)S(1)} %copy-done.10), kind=kCustom, calls=%fused_computation.6 | custom fusion | bytes 3145856 | tf_op jit(solution)/shard_map/scatter | solution.py:25
  50.6 38.9 %all-to-all-done.1 = bf16[8,8,128,128]{3,2,1,0:T(8,128)(2,1)} async-done(((bf16[8,8,128,128]{3,2,1,0:T(8,128)(2,1)}), bf16[8,8,128,128]{3,2,1,0:T(8,128)(2,1)}, u32[]{:S(2)}, u32[]{:S(2)}) %all-to-all-start.1) | async-done | bytes 2097184 | tf_op jit(solution)/shard_map/all_to_all | solution.py:35
  89.4 4.5 %all-to-all-start.3 = ((bf16[8,8,128,128]{3,2,1,0:T(8,128)(2,1)}), bf16[8,8,128,128]{3,2,1,0:T(8,128)(2,1)}, u32[]{:S(2)}, u32[]{:S(2)}) async-start(bf16[8,8,128,128]{3,2,1,0:T(8,128)(2,1)} %bitcast.22), calls=%async_computation.3 | async-start | bytes 4194304 | tf_op jit(solution)/shard_map/all_to_all | solution.py:35
  94.0 1.5 slice_bitcast_fusion
  97.7 2.2 gather_fusion
  99.9 4.1 %gather_fusion.1 = bf16[64,128,128]{2,1,0:T(8,128)(2,1)} fusion(bf16[32,128,128]{2,1,0:T(8,128)(2,1)} %get-tuple-element.6, s32[1024]{0:T(1024)S(1)} %pad_clamp_fusion), kind=kCustom, calls=%fused_computation.1 | custom fusion | bytes 4194560 | tf_op jit(solution)/shard_map/gather | solution.py:37
  104.0 4.2 %fusion.23 = f32[8,8,128,128]{3,2,1,0:T(8,128)} fusion(bf16[8,8,128,128]{3,2,1,0:T(8,128)(2,1)} %all-to-all-done.1, bf16[8,8,128,128]{3,2,1,0:T(8,128)(2,1)S(1)} %bitcast.83), kind=kOutput, calls=%fused_computation.64 | convolution fusion | flops 268435456 | bytes 8388608 | tf_op jit(solution)/shard_map/scir,scrq->sciq/dot_general | solution.py:38
  108.5 8.8 %scatter_fusion.1 = f32[32,128,128]{2,1,0:T(8,128)S(1)} fusion(f32[32,128,128]{2,1,0:T(8,128)S(1)} %broadcast.166.clone, s32[64]{0:T(128)S(1)} %fusion.16, f32[64,128,128]{2,1,0:T(8,128)} %bitcast.87), kind=kCustom, calls=%fused_computation.4 | custom fusion | flops 1048576 | bytes 12583168 | tf_op jit(solution)/shard_map/scatter-add | solution.py:40
  117.3 24.3 %all-to-all-done.3 = bf16[8,8,128,128]{3,2,1,0:T(8,128)(2,1)} async-done(((bf16[8,8,128,128]{3,2,1,0:T(8,128)(2,1)}), bf16[8,8,128,128]{3,2,1,0:T(8,128)(2,1)}, u32[]{:S(2)}, u32[]{:S(2)}) %all-to-all-start.3) | async-done | bytes 2097184 | tf_op jit(solution)/shard_map/all_to_all | solution.py:35
  141.6 4.8 %fusion.24 = f32[8,8,128,128]{3,2,1,0:T(8,128)} fusion(bf16[8,8,128,128]{3,2,1,0:T(8,128)(2,1)} %all-to-all-done.3, bf16[8,8,128,128]{3,2,1,0:T(8,128)(2,1)} %bitcast.81), kind=kOutput, calls=%fused_computation.65 | convolution fusion | flops 268435456 | bytes 8388608 | tf_op jit(solution)/shard_map/scir,scrq->sciq/dot_general | solution.py:38
  146.4 8.8 %scatter_fusion.3 = f32[32,128,128]{2,1,0:T(8,128)S(1)} fusion(f32[32,128,128]{2,1,0:T(8,128)S(1)} %scatter_fusion.1, s32[64]{0:T(128)S(1)} %fusion.18, f32[64,128,128]{2,1,0:T(8,128)} %bitcast.88), kind=kCustom, calls=%fused_computation.7 | custom fusion | flops 1048576 | bytes 12583168 | tf_op jit(solution)/shard_map/scatter-add | solution.py:40
  155.2 1.3 copy-done.1
  156.6 8.7 %reduce-scatter.3.cloned.1.call-done = f32[32,64,128]{2,1,0:T(8,128)} async-done(((f32[32,128,128]{2,1,0:T(8,128)}), f32[32,64,128]{2,1,0:T(8,128)}) %reduce-scatter.3.cloned.1.call-update) | async-done | bytes 1048592 | tf_op jit(solution)/shard_map/reduce_scatter | solution.py:53
  165.4 2.2 fusion.3
  167.6 34.5 %all-reduce = (f32[]{:T(128)}, f32[]{:T(128)}) all-reduce(f32[]{:T(128)} %get-tuple-element.3, f32[]{:T(128)} %get-tuple-element.2), channel_id=1, replica_groups=mesh['rep'=2,'sec'=8,'term'=2] {'sec','term'}, use_global_device_ids=true, to_apply=%region_12.13 | all-reduce | flops 2 | bytes 16 | tf_op jit(solution)/shard_map/psum | solution.py:54
  203.4 0.9 multiply_reduce_fusion
  204.3 30.1 %psum.23 = f32[]{:T(128)} all-reduce(f32[]{:T(128)} %multiply_reduce_fusion), channel_id=1, replica_groups=mesh['rep'=2,'sec'=8,'term'=2] {'sec','term'}, use_global_device_ids=true, to_apply=%region_16.17 | all-reduce | flops 1 | bytes 8 | tf_op jit(solution)/shard_map/psum | solution.py:59
  235.1 1.0 multiply_convert_fusion
  236.1 6.4 %all-gather.2.cloned.1.call-done = bf16[32,128,128]{2,1,0:T(8,128)(2,1)} async-done(((bf16[32,64,128]{2,1,0:T(8,128)(2,1)}), bf16[32,128,128]{2,1,0:T(8,128)(2,1)}) %all-gather.2.cloned.1.call-update) | async-done | bytes 1048592 | tf_op jit(solution)/shard_map/all_gather | solution.py:64
  242.6 2.4 fusion
  245.6 1.8 broadcast.174.clone
  247.5 4.6 %scatter_fusion.4 = bf16[64,128,128]{2,1,0:T(8,128)(2,1)} fusion(bf16[64,128,128]{2,1,0:T(8,128)(2,1)} %broadcast.174.clone, s32[32]{0:T(128)S(1)} %get-tuple-element.11, bf16[32,128,128]{2,1,0:T(8,128)(2,1)S(1)} %copy.13), kind=kCustom, calls=%fused_computation.8 | custom fusion | bytes 3145856 | tf_op jit(solution)/shard_map/scatter | solution.py:25
  252.1 6.0 %all-to-all-start.4 = ((bf16[8,8,128,128]{3,2,1,0:T(8,128)(2,1)}), bf16[8,8,128,128]{3,2,1,0:T(8,128)(2,1)}, u32[]{:S(2)}, u32[]{:S(2)}) async-start(bf16[8,8,128,128]{3,2,1,0:T(8,128)(2,1)} %bitcast.29), calls=%async_computation.5 | async-start | bytes 4194304 | tf_op jit(solution)/shard_map/all_to_all | solution.py:35
  258.1 1.9 fusion.1
  260.0 1.6 copy.14
  262.1 1.7 scatter_fusion.6
  263.8 43.0 %all-to-all-done.4 = bf16[8,8,128,128]{3,2,1,0:T(8,128)(2,1)} async-done(((bf16[8,8,128,128]{3,2,1,0:T(8,128)(2,1)}), bf16[8,8,128,128]{3,2,1,0:T(8,128)(2,1)}, u32[]{:S(2)}, u32[]{:S(2)}) %all-to-all-start.4) | async-done | bytes 2097184 | tf_op jit(solution)/shard_map/all_to_all | solution.py:35
  306.9 4.5 %all-to-all-start.5 = ((bf16[8,8,128,128]{3,2,1,0:T(8,128)(2,1)}), bf16[8,8,128,128]{3,2,1,0:T(8,128)(2,1)}, u32[]{:S(2)}, u32[]{:S(2)}) async-start(bf16[8,8,128,128]{3,2,1,0:T(8,128)(2,1)} %bitcast.89), calls=%async_computation.6 | async-start | bytes 4194304 | tf_op jit(solution)/shard_map/all_to_all | solution.py:35
  311.5 4.2 %fusion.25 = f32[8,8,128,128]{3,2,1,0:T(8,128)} fusion(bf16[8,8,128,128]{3,2,1,0:T(8,128)(2,1)} %all-to-all-done.4, bf16[8,8,128,128]{3,2,1,0:T(8,128)(2,1)S(1)} %bitcast.84), kind=kOutput, calls=%fused_computation.66 | convolution fusion | flops 268435456 | bytes 8388608 | tf_op jit(solution)/shard_map/scir,scrq->sciq/dot_general | solution.py:38
  315.9 8.8 %scatter_fusion.5 = f32[32,128,128]{2,1,0:T(8,128)S(1)} fusion(f32[32,128,128]{2,1,0:T(8,128)S(1)} %broadcast.166, s32[64]{0:T(128)S(1)} %fusion.16, f32[64,128,128]{2,1,0:T(8,128)} %bitcast.85), kind=kCustom, calls=%fused_computation.9 | custom fusion | flops 1048576 | bytes 12583168 | tf_op jit(solution)/shard_map/scatter-add | solution.py:40
  324.7 34.6 %all-to-all-done.5 = bf16[8,8,128,128]{3,2,1,0:T(8,128)(2,1)} async-done(((bf16[8,8,128,128]{3,2,1,0:T(8,128)(2,1)}), bf16[8,8,128,128]{3,2,1,0:T(8,128)(2,1)}, u32[]{:S(2)}, u32[]{:S(2)}) %all-to-all-start.5) | async-done | bytes 2097184 | tf_op jit(solution)/shard_map/all_to_all | solution.py:35
  359.3 4.8 %fusion.26 = f32[8,8,128,128]{3,2,1,0:T(8,128)} fusion(bf16[8,8,128,128]{3,2,1,0:T(8,128)(2,1)} %all-to-all-done.5, bf16[8,8,128,128]{3,2,1,0:T(8,128)(2,1)} %bitcast.82), kind=kOutput, calls=%fused_computation.67 | convolution fusion | flops 268435456 | bytes 8388608 | tf_op jit(solution)/shard_map/scir,scrq->sciq/dot_general | solution.py:38
  364.1 8.8 %scatter_fusion.7 = f32[32,128,128]{2,1,0:T(8,128)S(1)} fusion(f32[32,128,128]{2,1,0:T(8,128)S(1)} %scatter_fusion.5, s32[64]{0:T(128)S(1)} %fusion.18, f32[64,128,128]{2,1,0:T(8,128)} %bitcast.86), kind=kCustom, calls=%fused_computation.11 | custom fusion | flops 1048576 | bytes 12583168 | tf_op jit(solution)/shard_map/scatter-add | solution.py:40
  372.9 1.3 copy-done
  374.3 8.8 %reduce-scatter.5.cloned.1.call-done = f32[32,64,128]{2,1,0:T(8,128)} async-done(((f32[32,128,128]{2,1,0:T(8,128)}), f32[32,64,128]{2,1,0:T(8,128)}) %reduce-scatter.5.cloned.1.call-update) | async-done | bytes 1048592 | tf_op jit(solution)/shard_map/reduce_scatter | solution.py:68
  383.0 2.1 convert_element_type.45
  (55 shorter events, 7.1 us)
Async XLA Ops:
  11.1 13.7 %all-to-all-start = ((s32[8,1,8]{2,1,0:T(1,128)}), s32[8,1,8]{2,1,0:T(1,128)S(1)}, u32[]{:S(2)}, u32[]{:S(2)}) async-start(s32[8,1,8]{2,1,0:T(1,128)} %bitcast.5), calls=%async_computation | async-start | bytes 8192 | tf_op jit(solution)/shard_map/all_to_all | solution.py:36
  24.7 11.7 %all-to-all-start.2 = ((s32[8,1,8]{2,1,0:T(1,128)}), s32[8,1,8]{2,1,0:T(1,128)S(1)}, u32[]{:S(2)}, u32[]{:S(2)}) async-start(s32[8,1,8]{2,1,0:T(1,128)} %bitcast.19), calls=%async_computation.2 | async-start | bytes 8192 | tf_op jit(solution)/shard_map/all_to_all | solution.py:36
  36.5 6.2 %copy-start.5 = (bf16[32,128,128]{2,1,0:T(8,128)(2,1)S(1)}, bf16[32,128,128]{2,1,0:T(8,128)(2,1)}, u32[]{:S(2)}) copy-start(bf16[32,128,128]{2,1,0:T(8,128)(2,1)} %param.5) | copy-start | bytes 3145732
  36.5 6.2 %copy-start.7 = (bf16[2,32,128,128]{3,2,1,0:T(8,128)(2,1)S(1)}, bf16[2,32,128,128]{3,2,1,0:T(8,128)(2,1)}, u32[]{:S(2)}) copy-start(bf16[2,32,128,128]{3,2,1,0:T(8,128)(2,1)} %param.6) | copy-start | bytes 6291460
  36.5 52.9 %all-to-all-start.1 = ((bf16[8,8,128,128]{3,2,1,0:T(8,128)(2,1)}), bf16[8,8,128,128]{3,2,1,0:T(8,128)(2,1)}, u32[]{:S(2)}, u32[]{:S(2)}) async-start(bf16[8,8,128,128]{3,2,1,0:T(8,128)(2,1)} %bitcast.8), calls=%async_computation.1 | async-start | bytes 4194304 | tf_op jit(solution)/shard_map/all_to_all | solution.py:35
  44.1 1.9 copy-start.10
  89.4 4.6 %copy-start.11 = (bf16[2,32,128,128]{3,2,1,0:T(8,128)(2,1)S(1)}, bf16[2,32,128,128]{3,2,1,0:T(8,128)(2,1)}, u32[]{:S(2)}) copy-start(bf16[2,32,128,128]{3,2,1,0:T(8,128)(2,1)} %param.7) | copy-start | bytes 6291460
  89.4 52.1 %all-to-all-start.3 = ((bf16[8,8,128,128]{3,2,1,0:T(8,128)(2,1)}), bf16[8,8,128,128]{3,2,1,0:T(8,128)(2,1)}, u32[]{:S(2)}, u32[]{:S(2)}) async-start(bf16[8,8,128,128]{3,2,1,0:T(8,128)(2,1)} %bitcast.22), calls=%async_computation.3 | async-start | bytes 4194304 | tf_op jit(solution)/shard_map/all_to_all | solution.py:35
  93.9 71.4 %reduce-scatter.3.cloned.1.call-start = ((), (), s32[]{:S(2)}) async-start(), calls=%async_computation.8 | async-start | bytes 3145728 | tf_op jit(solution)/shard_map/reduce_scatter | solution.py:53
  99.9 4.2 %copy-start.2 = (bf16[64,128,128]{2,1,0:T(8,128)(2,1)}, bf16[64,128,128]{2,1,0:T(8,128)(2,1)S(1)}, u32[]{:S(2)}) copy-start(bf16[64,128,128]{2,1,0:T(8,128)(2,1)S(1)} %gather_fusion) | copy-start | bytes 6291460
  155.2 1.4 copy-start.1
  156.6 86.0 %all-gather.2.cloned.1.call-start = ((), (), s32[]{:S(2)}) async-start(), calls=%async_computation.9 | async-start | bytes 1572864 | tf_op jit(solution)/shard_map/all_gather | solution.py:64
  165.4 38.0 %copy-start.6 = (f32[32,64,128]{2,1,0:T(8,128)S(1)}, f32[32,64,128]{2,1,0:T(8,128)}, u32[]{:S(2)}) copy-start(f32[32,64,128]{2,1,0:T(8,128)} %reduce-scatter.3.cloned.1.call-done) | copy-start | bytes 3145732
  252.1 6.0 %copy-start.8 = (bf16[2,32,128,128]{3,2,1,0:T(8,128)(2,1)S(1)}, bf16[2,32,128,128]{3,2,1,0:T(8,128)(2,1)}, u32[]{:S(2)}) copy-start(bf16[2,32,128,128]{3,2,1,0:T(8,128)(2,1)} %param.6) | copy-start | bytes 6291460
  252.1 6.0 %copy-start.9 = (bf16[32,128,128]{2,1,0:T(8,128)(2,1)S(1)}, bf16[32,128,128]{2,1,0:T(8,128)(2,1)}, u32[]{:S(2)}) copy-start(bf16[32,128,128]{2,1,0:T(8,128)(2,1)} %all-gather.2.cloned.1.call-done) | copy-start | bytes 3145732
  252.1 54.8 %all-to-all-start.4 = ((bf16[8,8,128,128]{3,2,1,0:T(8,128)(2,1)}), bf16[8,8,128,128]{3,2,1,0:T(8,128)(2,1)}, u32[]{:S(2)}, u32[]{:S(2)}) async-start(bf16[8,8,128,128]{3,2,1,0:T(8,128)(2,1)} %bitcast.29), calls=%async_computation.5 | async-start | bytes 4194304 | tf_op jit(solution)/shard_map/all_to_all | solution.py:35
  263.8 43.1 %copy-start.4 = (bf16[64,128,128]{2,1,0:T(8,128)(2,1)}, bf16[64,128,128]{2,1,0:T(8,128)(2,1)S(1)}, u32[]{:S(2)}) copy-start(bf16[64,128,128]{2,1,0:T(8,128)(2,1)S(1)} %scatter_fusion.6) | copy-start | bytes 6291460
  306.9 4.6 %copy-start.3 = (bf16[64,128,128]{2,1,0:T(8,128)(2,1)S(1)}, bf16[64,128,128]{2,1,0:T(8,128)(2,1)}, u32[]{:S(2)}) copy-start(bf16[64,128,128]{2,1,0:T(8,128)(2,1)} %copy-done.2) | copy-start | bytes 6291460
  306.9 52.4 %all-to-all-start.5 = ((bf16[8,8,128,128]{3,2,1,0:T(8,128)(2,1)}), bf16[8,8,128,128]{3,2,1,0:T(8,128)(2,1)}, u32[]{:S(2)}, u32[]{:S(2)}) async-start(bf16[8,8,128,128]{3,2,1,0:T(8,128)(2,1)} %bitcast.89), calls=%async_computation.6 | async-start | bytes 4194304 | tf_op jit(solution)/shard_map/all_to_all | solution.py:35
  311.4 71.6 %reduce-scatter.5.cloned.1.call-start = ((), (), s32[]{:S(2)}) async-start(), calls=%async_computation.10 | async-start | bytes 3145728 | tf_op jit(solution)/shard_map/reduce_scatter | solution.py:68
  372.9 1.4 copy-start
Sparse Core Ops, SparseCore 0:
  156.7 8.6 reduce-scatter.2
  236.2 6.2 all-gather.1
  374.4 8.5 reduce-scatter.4
where the time goes:
time: 395 us; the launch traced here: 393 us
  waiting for transfers between devices  170 us (43%)
  blocking collectives  64.6 us (16%)
  other arithmetic  43.8 us (11%)
  local copies, waits for them, and re-layouts  39.8 us (10%)
  starting transfers between devices  31.9 us (8%)
  matrix products  25.8 us (7%)
  between operations  17.2 us (4%)
    all_to_all x4, waiting for transfers between devices, contribute(): lax.all_to_all(outgoing, 'sec', split_axis=0, concat_axis=0, tiled=True)  141 us
    scatter-add x4, other arithmetic, contribute(): totals.at[labels_in.reshape(-1)]  35.1 us
    psum x1, blocking collectives, per_device(): lax.psum((jnp.sum(own_rows * sigma_rows), jnp.sum(own_rows * own_rows)),...  34.5 us
    psum x1, blocking collectives, per_device(): lax.psum(jnp.sum(residual_rows * residual_rows), ('sec', 'term'))  30.1 us
    all_to_all x4, starting transfers between devices, contribute(): lax.all_to_all(outgoing, 'sec', split_axis=0, concat_axis=0, tiled=True)  21.2 us
    dot_general x4, matrix products, contribute(): jnp.einsum('scir,scrq->sciq', pieces, picked, preferred_element_type=jnp....  18.1 us
    scatter x4, local copies, waits for them, and re-layouts, contribute(): outgoing = jnp.zeros((owners * capacity,) + vector.shape[1:], jnp.bfloat1...  15.6 us
    all_to_all x2, starting transfers between devices, contribute(): lax.all_to_all(labels, 'sec', split_axis=0, concat_axis=0, tiled=True)  10.6 us
  transfers between devices with their start and end apart: 9, of which 8 were waited for; matrix products, arithmetic and copies ran while one was open for 15% of the time, Pallas kernels for 0%

commit v1 on v0

v1 whole, which is shorter than its diff:
```python
import functools

import jax
import jax.numpy as jnp
from jax import lax
from jax.experimental import pallas as pl
from jax.experimental.pallas import tpu as pltpu
from jax.sharding import PartitionSpec as P

BOTH = ("sec", "term")


def slot_codes(target_owner, target_local, owners, capacity):
    terms, blocks = target_local.shape
    owner = target_owner[:, :, 0]
    place = jnp.arange(blocks, dtype=jnp.int32)
    same = (owner[:, :, None] == owner[:, None, :]) & (place[None, :] < place[:, None])[None]
    position = jnp.sum(same.astype(jnp.int32), axis=2)
    hit = (
        owner[:, None, None, :] == jnp.arange(owners, dtype=jnp.int32)[None, :, None, None]
    ) & (position[:, None, None, :] == jnp.arange(capacity, dtype=jnp.int32)[None, None, :, None])
    code = place[None, :] * (2 * blocks) + target_local - blocks
    return blocks + jnp.sum(jnp.where(hit, code[:, None, None, :], 0), axis=3)


def apply_kernel(first, capacity, blocks, code_ref, left_ref, vector_ref, right_ref, *rest):
    total_in, total = (None, rest[0]) if first else rest
    step = pl.program_id(0)
    rows, width = left_ref.shape[2:]

    @pl.when(step == 0)
    def _():
        total[...] = jnp.zeros_like(total) if first else total_in[...]

    for term in range(2):
        moved, where = [], []
        for slot in range(capacity):
            code = code_ref[2 * step + term, slot]
            source, target = lax.div(code, 2 * blocks), lax.rem(code, 2 * blocks)
            block = vector_ref[0, :, source].reshape(2 * rows, width)
            product = jnp.dot(left_ref[term, slot], block, preferred_element_type=jnp.float32)
            moved.append(product.astype(jnp.bfloat16))
            where.append(target)
        for slot in range(capacity):
            target = where[slot]
            total[target] += jnp.dot(
                moved[slot],
                right_ref[term, jnp.minimum(target, blocks - 1)],
                preferred_element_type=jnp.float32,
            )


def apply_chunk(total, codes, left, vector, right):
    owners, _, blocks, rows, width = vector.shape
    capacity = left.shape[1]
    first = total is None
    spec_total = pl.BlockSpec((blocks + 1, rows, width), lambda s, c: (0, 0, 0))
    return pl.pallas_call(
        functools.partial(apply_kernel, first, capacity, blocks),
        out_shape=jax.ShapeDtypeStruct((blocks + 1, rows, width), jnp.float32),
        grid_spec=pltpu.PrefetchScalarGridSpec(
            num_scalar_prefetch=1,
            grid=(owners,),
            in_specs=[
                pl.BlockSpec((2, capacity, rows, width), lambda s, c: (s, 0, 0, 0)),
                pl.BlockSpec((1, 2, blocks, rows, width), lambda s, c: (s, 0, 0, 0, 0)),
                pl.BlockSpec((2, blocks, width, width), lambda s, c: (0, 0, 0, 0)),
            ]
            + ([] if first else [spec_total]),
            out_specs=spec_total,
        ),
        compiler_params=pltpu.CompilerParams(vmem_limit_bytes=32 * 2**20),
        cost_estimate=pl.CostEstimate(
            flops=owners * 2 * capacity * 2 * 2 * rows * width * width,
            bytes_accessed=left.size * 2 + vector.size * 2 + right.size * 2,
            transcendentals=0,
        ),
    )(codes, left, vector, right, *([] if first else [total]))


def per_device(wavefunction, left_operator, right_operator, target_owner, target_local):
    owners = lax.axis_size("sec")
    halves = lax.axis_size("term")
    me, half = lax.axis_index("sec"), lax.axis_index("term")
    terms, blocks, height, width = left_operator.shape
    rows = height // halves
    capacity = 2 * blocks // owners

    own_rows = lax.dynamic_slice_in_dim(wavefunction, half * rows, rows, 1)
    codes = slot_codes(target_owner, target_local, owners, capacity)
    sources = codes // (2 * blocks)

    moved_left = []
    for k in range(terms):
        pick = sources[k][:, None, :] * halves + jnp.arange(halves, dtype=jnp.int32)[None, :, None]
        pieces = left_operator[k].reshape(blocks * halves, rows, width)[pick.reshape(-1)]
        pieces = pieces.reshape(owners * halves, capacity, rows, width)
        moved_left.append(lax.all_to_all(pieces, BOTH, split_axis=0, concat_axis=0, tiled=True))
    all_codes = lax.all_gather(codes, BOTH, axis=0)
    my_codes = lax.dynamic_index_in_dim(all_codes, me, axis=3 - 1, keepdims=False)
    gathered = lax.all_gather(own_rows, BOTH, axis=0).reshape(owners, halves, blocks, rows, width)
    right = lax.all_gather(right_operator, "term", axis=1)

    def apply(vector):
        total = None
        for k in range(terms):
            total = apply_chunk(total, my_codes[:, k], moved_left[k], vector, right[k])
        return total[:blocks]

    sigma_rows = apply(gathered)
    wave = own_rows.astype(jnp.float32)
    cross, own = jnp.sum(wave * sigma_rows), jnp.sum(wave * wave)
    local = jnp.where(own > 0, cross / own, 0.0)
    about = jnp.sum(jnp.square(sigma_rows - local * wave))
    stats = lax.all_gather(jnp.stack([about, cross, own, local]), BOTH, axis=0)
    rayleigh = jnp.sum(stats[:, 1]) / jnp.sum(stats[:, 2])
    residual_sq = jnp.sum(stats[:, 0] + jnp.square(stats[:, 3] - rayleigh) * stats[:, 2])
    entries = blocks * owners * height * width
    factor = lax.rsqrt(residual_sq / entries + 1e-06)
    direction = ((sigma_rows - rayleigh * wave) * factor).astype(jnp.bfloat16)
    direction = lax.all_gather(direction, BOTH, axis=0).reshape(gathered.shape)
    sigma_two = apply(direction).astype(jnp.bfloat16)
    return (sigma_two, jnp.reshape(rayleigh, (1,)))


def solution(mesh):
    placed = (
        P(("rep", "sec"), None, None),
        P("term", ("rep", "sec"), None, None),
        P("term", ("rep", "sec"), None, None),
        P("term", ("rep", "sec"), None),
        P("term", ("rep", "sec")),
    )
    return jax.shard_map(
        per_device,
        mesh=mesh,
        in_specs=placed,
        out_specs=(P(("rep", "sec"), "term", None), P("rep")),
        check_vma=False,
    )
```

time: 395 us -> 348 us (0.88)
  blocking collectives: 64.6 us -> 113 us
  waiting for transfers between devices: 170 us -> 127 us
  other arithmetic: 43.8 us -> 8.91 us
  matrix products: 25.8 us -> 0 us
  Pallas kernels: 0 us -> 20.4 us
  starting transfers between devices: 31.9 us -> 22.5 us
  local copies, waits for them, and re-layouts: 39.8 us -> 35.7 us
    all_to_all x6 -> x2, waiting for transfers between devices: 146 us -> 54.4 us  [per_device(): lax.all_to_all(pieces, BOTH, split_axis=0, concat_axis=0, tiled=True)]
    all_gather x0 -> x1, blocking collectives: none -> 73.2 us  [per_device(): all_codes = lax.all_gather(codes, BOTH, axis=0)]
    all_gather x1 -> x3, waiting for transfers between devices: 6.43 us -> 72.3 us  [the longest x1 72.3 us: per_device(): direction = lax.all_gather(direction, BOTH, axis=0).reshape(gathered.shape)]
    psum x2 -> x0, blocking collectives: 64.6 us -> none  [the longest x1 34.5 us: per_device(): lax.psum((jnp.sum(own_rows * sigma_rows), jnp.sum(own_rows * own_rows)),...]
    unnamed x0 -> x1, blocking collectives: none -> 39.6 us
    scatter-add x4 -> x0, other arithmetic: 35.1 us -> none  [contribute(): totals.at[labels_in.reshape(-1)]]
    dot_general x8 -> x0, matrix products: 25.8 us -> none  [the longest x4 18.1 us: contribute(): jnp.einsum('scir,scrq->sciq', pieces, picked, preferred_element_type=jnp....]
    pallas_call x0 -> x4, Pallas kernels: none -> 20.4 us  [apply_chunk(): pl.pallas_call(functools.partial(apply_kernel, first, capacity, blocks),...]
  transfers between devices with their start and end apart: 9 -> 5, of which waited for: 8 -> 2; matrix products, arithmetic and copies ran while one was open for 15% -> 4% of each run, Pallas kernels for 0% -> 1%
where the time goes in v1:
time: 348 us; the launch traced here: 347 us
  waiting for transfers between devices  127 us (36%)
  blocking collectives  113 us (32%)
  local copies, waits for them, and re-layouts  35.7 us (10%)
  starting transfers between devices  22.5 us (6%)
  Pallas kernels  20.4 us (6%)
  between operations  19.7 us (6%)
  other arithmetic  8.91 us (3%)
    all_gather x1, blocking collectives, per_device(): all_codes = lax.all_gather(codes, BOTH, axis=0)  73.2 us
    all_gather x1, waiting for transfers between devices, per_device(): direction = lax.all_gather(direction, BOTH, axis=0).reshape(gathered.shape)  72.3 us
    all_to_all x2, waiting for transfers between devices, per_device(): lax.all_to_all(pieces, BOTH, split_axis=0, concat_axis=0, tiled=True)  54.4 us
    unnamed x1, blocking collectives  39.6 us
    unnamed x37, local copies, waits for them, and re-layouts  22.8 us
    all_to_all x2, starting transfers between devices, per_device(): lax.all_to_all(pieces, BOTH, split_axis=0, concat_axis=0, tiled=True)  22.3 us
    pallas_call x4, Pallas kernels, apply_chunk(): pl.pallas_call(functools.partial(apply_kernel, first, capacity, blocks),...  20.4 us
  transfers between devices with their start and end apart: 5, of which 2 were waited for; matrix products, arithmetic and copies ran while one was open for 4% of the time, Pallas kernels for 1%

profile of v1, /device:TPU:0, one launch (start us, length us, event | category | flops | bytes accessed | tf_op | source)
XLA Modules:
  0.0 347.3 jit_solution(5864574153370213656)
XLA Ops:
  7.2 0.0 all-gather.11.cloned.1.call-start
  7.2 0.7 all-gather.11.cloned.1.call-update
  7.9 0.0 all-gather.9.cloned.1.call-start
  8.0 0.4 copy-done.12
  8.4 0.8 constant_dynamic-slice_fusion.1
  9.3 0.2 convert_reduce_fusion
  9.5 0.4 select_reduce_fusion
  9.9 0.1 add.123
  10.0 1.7 fusion.19
  11.7 2.1 gather_fusion.1
  13.8 7.4 %all-to-all-start.1 = ((bf16[16,8,64,128]{3,2,1,0:T(8,128)(2,1)}), bf16[16,8,64,128]{3,2,1,0:T(8,128)(2,1)S(1)}, u32[]{:S(2)}, u32[]{:S(2)}) async-start(bf16[16,8,64,128]{3,2,1,0:T(8,128)(2,1)} %bitcast.40), calls=%async_computation.1 | async-start | bytes 4194304 | tf_op jit(solution)/shard_map/all_to_all | solution.py:98
  21.3 0.1 add.117
  21.4 2.1 gather_fusion
  23.5 54.4 %all-to-all-done.1.left_ref = bf16[16,8,64,128]{3,2,1,0:T(8,128)(2,1)S(1)} async-done(((bf16[16,8,64,128]{3,2,1,0:T(8,128)(2,1)}), bf16[16,8,64,128]{3,2,1,0:T(8,128)(2,1)S(1)}, u32[]{:S(2)}, u32[]{:S(2)}) %all-to-all-start.1) | async-done | bytes 2097184 | tf_op jit(solution)/shard_map/all_to_all | solution.py:98
  77.9 1.3 copy-done.5
  79.2 15.0 %all-to-all-start = ((bf16[16,8,64,128]{3,2,1,0:T(8,128)(2,1)}), bf16[16,8,64,128]{3,2,1,0:T(8,128)(2,1)S(1)}, u32[]{:S(2)}, u32[]{:S(2)}) async-start(bf16[16,8,64,128]{3,2,1,0:T(8,128)(2,1)} %bitcast.39), calls=%async_computation | async-start | bytes 4194304 | tf_op jit(solution)/shard_map/all_to_all | solution.py:98
  94.2 0.0 all-gather.13.cloned.1.call-start
  94.2 73.2 %all-gather = s32[32,8,8]{2,1,0:T(8,128)S(1)} all-gather(s32[2,8,8]{2,1,0:T(8,128)S(1)} %get-tuple-element.15), channel_id=2, replica_groups=mesh['rep'=2,'sec'=8,'term'=2] {'sec','term'}, dimensions={0}, use_global_device_ids=true | all-gather | bytes 8704 | tf_op jit(solution)/shard_map/all_gather | solution.py:99
  167.5 0.1 copy.27
  167.5 0.1 copy.23.code_ref
  167.6 0.1 copy.26.code_ref
  167.7 0.6 dynamic-slice
  168.9 0.0 all-gather.11.cloned.1.call-done
  169.0 4.7 %fusion.18 = (bf16[1,64,128,128]{3,2,1,0:T(8,128)(2,1)}, bf16[1,64,128,128]{3,2,1,0:T(8,128)(2,1)}) fusion(bf16[2,64,128,128]{3,2,1,0:T(8,128)(2,1)} %all-gather.11.cloned.1.call-done), kind=kLoop, calls=%fused_computation.54 | loop fusion | bytes 8388608 | tf_op jit(solution)/shard_map/slice | solution.py:107
  173.7 3.4 copy-done
  177.1 1.6 copy-done.6
  178.7 1.6 copy-done.8
  180.3 5.1 %shard_map.68.rest_0_ = f32[33,64,128]{2,1,0:T(8,128)S(1)} custom-call(s32[16,8]{1,0:T(8,128)S(1)} %copy.23.code_ref, bf16[16,8,64,128]{3,2,1,0:T(8,128)(2,1)S(1)} %copy-done.6, bf16[8,2,32,64,128]{4,3,2,1,0:T(8,128)(2,1)S(1)} %bitcast.29, bf16[2,32,128,128]{3,2,1,0:T(8,128)(2,1)S(1)} %bitcast.35), custom_call_target="tpu_custom_call" | custom-call | flops 536870912 | bytes 12582912 | tf_op jit(solution)/shard_map/pallas_call | solution.py:58
  185.4 1.1 copy-done.10
  186.4 3.4 copy-done.1
  189.8 1.6 copy-done.3
  191.4 1.2 copy-done.11
  192.7 5.1 %shard_map.69 = f32[33,64,128]{2,1,0:T(8,128)S(1)} custom-call(s32[16,8]{1,0:T(8,128)S(1)} %copy.26.code_ref, bf16[16,8,64,128]{3,2,1,0:T(8,128)(2,1)S(1)} %all-to-all-done.left_ref, bf16[8,2,32,64,128]{4,3,2,1,0:T(8,128)(2,1)S(1)} %bitcast.30, bf16[2,32,128,128]{3,2,1,0:T(8,128)(2,1)S(1)} %bitcast.33, f32[33,64,128]{2,1,0:T(8,128)S(1)} %copy-done.11), custom_call_target="tpu_custom_call" | custom-call | flops 536870912 | bytes 12582912 | tf_op jit(solution)/shard_map/pallas_call | solution.py:58
  197.8 1.0 fusion.1
  200.7 1.9 fusion.4
  202.6 2.0 maximum_dynamic-update-slice_fusion
  204.6 39.6 %all-reduce = f32[64]{0:T(128)S(1)} all-reduce(f32[64]{0:T(128)S(1)} %maximum_dynamic-update-slice_fusion), channel_id=5, replica_groups=mesh['rep'=2,'sec'=8,'term'=2] {'sec','term'}, use_global_device_ids=true, to_apply=%add | all-reduce | flops 64 | bytes 512
  244.2 0.1 reshape.170
  244.3 0.7 slice_reduce_fusion.1
  246.3 0.7 fusion.12
  247.7 2.0 fusion.7
  249.7 72.3 %all-gather.13.cloned.1.call-done = bf16[512,64,128]{2,1,0:T(8,128)(2,1)} async-done(((bf16[32,64,128]{2,1,0:T(8,128)(2,1)}), bf16[512,64,128]{2,1,0:T(8,128)(2,1)}) %all-gather.13.cloned.1.call-update) | async-done | bytes 8388624 | tf_op jit(solution)/shard_map/all_gather | solution.py:121
  322.0 3.4 copy-done.2
  325.4 1.6 copy-done.7
  327.0 1.6 copy-done.9
  328.6 5.1 %shard_map.70.rest_0_ = f32[33,64,128]{2,1,0:T(8,128)S(1)} custom-call(s32[16,8]{1,0:T(8,128)S(1)} %copy.23.code_ref, bf16[16,8,64,128]{3,2,1,0:T(8,128)(2,1)S(1)} %copy-done.7, bf16[8,2,32,64,128]{4,3,2,1,0:T(8,128)(2,1)S(1)} %bitcast.31, bf16[2,32,128,128]{3,2,1,0:T(8,128)(2,1)S(1)} %bitcast.36), custom_call_target="tpu_custom_call" | custom-call | flops 536870912 | bytes 12582912 | tf_op jit(solution)/shard_map/pallas_call | solution.py:58
  333.7 5.1 %shard_map.71 = f32[33,64,128]{2,1,0:T(8,128)S(1)} custom-call(s32[16,8]{1,0:T(8,128)S(1)} %copy.26.code_ref, bf16[16,8,64,128]{3,2,1,0:T(8,128)(2,1)S(1)} %all-to-all-done.left_ref, bf16[8,2,32,64,128]{4,3,2,1,0:T(8,128)(2,1)S(1)} %bitcast.32, bf16[2,32,128,128]{3,2,1,0:T(8,128)(2,1)S(1)} %bitcast.34, f32[33,64,128]{2,1,0:T(8,128)S(1)} %shard_map.70.rest_0_), custom_call_target="tpu_custom_call" | custom-call | flops 536870912 | bytes 12582912 | tf_op jit(solution)/shard_map/pallas_call | solution.py:58
  338.8 0.9 slice.105
  (41 shorter events, 0.2 us)
Async XLA Ops:
  7.2 1.2 copy-start.12
  7.2 2.1 copy-start.14
  7.2 2.3 copy-start.15
  7.2 161.8 %all-gather.11.cloned.1.call-start = ((), (), s32[]{:S(2)}) async-start(), calls=%async_computation.3 | async-start | bytes 6291456 | tf_op jit(solution)/shard_map/all_gather | solution.py:102
  7.9 165.8 %all-gather.9.cloned.1.call-start = ((), (), s32[]{:S(2)}) async-start(), calls=%async_computation.2 | async-start | bytes 8912896 | tf_op jit(solution)/shard_map/all_gather | solution.py:101
  13.8 64.0 %all-to-all-start.1 = ((bf16[16,8,64,128]{3,2,1,0:T(8,128)(2,1)}), bf16[16,8,64,128]{3,2,1,0:T(8,128)(2,1)S(1)}, u32[]{:S(2)}, u32[]{:S(2)}) async-start(bf16[16,8,64,128]{3,2,1,0:T(8,128)(2,1)} %bitcast.40), calls=%async_computation.1 | async-start | bytes 4194304 | tf_op jit(solution)/shard_map/all_to_all | solution.py:98
  77.9 1.3 copy-start.5
  79.2 88.5 %copy-start.16 = (u32[32]{0:T(128)S(1)}, u32[32]{0:T(128)}, u32[]{:S(2)}) copy-start(u32[32]{0:T(128)} %constant.52) | copy-start | bytes 388
  79.2 107.2 %all-to-all-start = ((bf16[16,8,64,128]{3,2,1,0:T(8,128)(2,1)}), bf16[16,8,64,128]{3,2,1,0:T(8,128)(2,1)S(1)}, u32[]{:S(2)}, u32[]{:S(2)}) async-start(bf16[16,8,64,128]{3,2,1,0:T(8,128)(2,1)} %bitcast.39), calls=%async_computation | async-start | bytes 4194304 | tf_op jit(solution)/shard_map/all_to_all | solution.py:98
  94.2 227.8 %all-gather.13.cloned.1.call-start = ((), (), s32[]{:S(2)}) async-start(), calls=%async_computation.4 | async-start | bytes 8912896 | tf_op jit(solution)/shard_map/all_gather | solution.py:121
  173.7 3.4 copy-start
  177.1 1.6 copy-start.6
  178.7 1.6 copy-start.8
  185.4 1.1 copy-start.10
  186.4 3.4 copy-start.1
  189.8 1.6 copy-start.3
  191.4 1.2 copy-start.11
  192.7 5.1 %copy-start.13 = (bf16[32,128,128]{2,1,0:T(8,128)(2,1)S(1)}, bf16[32,128,128]{2,1,0:T(8,128)(2,1)}, u32[]{:S(2)}) copy-start(bf16[32,128,128]{2,1,0:T(8,128)(2,1)} %param.5) | copy-start | bytes 3145732
  322.0 3.4 copy-start.2
  325.4 1.6 copy-start.7
  327.0 1.6 copy-start.9
  328.6 5.1 %copy-start.4 = (bf16[1,64,128,128]{3,2,1,0:T(8,128)(2,1)S(1)}, bf16[1,64,128,128]{3,2,1,0:T(8,128)(2,1)}, u32[]{:S(2)}) copy-start(bf16[1,64,128,128]{3,2,1,0:T(8,128)(2,1)} %get-tuple-element.7) | copy-start | bytes 6291460
Sparse Core Ops, SparseCore 0:
  9.6 16.3 all-gather.10
  28.7 127.9 all-gather.8
  249.8 72.1 all-gather.12

commit v2 on v1

--- a/solution.py
+++ b/solution.py
@@ -8,6 +8,63 @@
 from jax.sharding import PartitionSpec as P
 
 BOTH = ("sec", "term")
+VMEM_LIMIT = 32 * 2**20
+RING_BYTES = 24 * 2**20
+
+
+def ring_order(owners):
+    if owners % 2:
+        return list(range(owners))
+    return list(range(0, owners, 2)) + list(range(owners - 1, 0, -2))
+
+
+def ring_place(owner, owners):
+    if owners % 2:
+        return owner
+    return jnp.where(owner % 2 == 0, owner // 2, owners - 1 - owner // 2)
+
+
+def ring_owner(place, owners):
+    place = place % owners
+    if owners % 2:
+        return place
+    return jnp.where(place < owners // 2, 2 * place, 2 * (owners - 1 - place) + 1)
+
+
+def send(value, owners, halves, shifts, flip=0):
+    ring = ring_order(owners)
+    pairs = []
+    for place in range(owners):
+        for half in range(halves):
+            to = ring[(place + shifts[half]) % owners]
+            pairs.append((ring[place] * halves + half, to * halves + (half ^ flip)))
+    return lax.ppermute(value, BOTH, pairs)
+
+
+def swap(value, owners, halves):
+    return send(value, owners, halves, (0,) * halves, 1)
+
+
+def ring_gather(unit, owners, halves, half):
+    units = {0: unit}
+    reach = (owners - 1) // 2
+    for step in range(1, reach + 1):
+        units[step] = send(units[step - 1], owners, halves, (1,) * halves)
+        units[-step] = send(units[1 - step], owners, halves, (-1,) * halves)
+    if owners % 2 == 0:
+        last = jnp.where(half == 0, units[reach], units[-reach])
+        units[owners // 2] = send(last, owners, halves, (1, -1))
+    return units
+
+
+def spread(value, devices, me):
+    if devices & (devices - 1):
+        return lax.psum(value, BOTH)
+    step = 1
+    while step < devices:
+        value = value + lax.ppermute(value, BOTH, [(d, d ^ step) for d in range(devices)])
+        step *= 2
+    return value
 
 
 def slot_codes(target_owner, target_local, owners, capacity):
@@ -23,7 +80,226 @@
     return blocks + jnp.sum(jnp.where(hit, code[:, None, None, :], 0), axis=3)
 
 
-def apply_kernel(first, capacity, blocks, code_ref, left_ref, vector_ref, right_ref, *rest):
+def apply_kernel(
+    sources, second, first, last, capacity, blocks, terms, half_ref, codes_ref, scale_ref, *refs
+):
+    refs = list(refs)
+    pieces = [[refs.pop(0) for _ in range(6 if second else 4)] for _ in range(sources)]
+    rights = [refs.pop(0), refs.pop(0)]
+    total_in = None if first else refs.pop(0)
+    if last:
+        out, total = refs
+    else:
+        (total,) = refs
+    upper = half_ref[0] == 0
+    rows, width = pieces[0][0].shape[2:]
+
+    total[...] = jnp.zeros_like(total) if first else total_in[...]
+
+    for index, piece in enumerate(pieces):
+        for flip in range(2):
+
+            @pl.loop(0, terms)
+            def _(term):
+                moved, where = [], []
+                for slot in range(capacity):
+                    code = codes_ref[((index * 2 + flip) * terms + term) * capacity + slot]
+                    source, target = lax.div(code, 2 * blocks), lax.rem(code, 2 * blocks)
+                    near, far = piece[2][source], piece[3][source]
+                    if second:
+                        factor = scale_ref[0]
+                        shift = scale_ref[1 + 2 * index], scale_ref[2 + 2 * index]
+                        near = near.astype(jnp.float32) + shift[0] * piece[4][source].astype(
+                            jnp.float32
+                        )
+                        far = far.astype(jnp.float32) + shift[1] * piece[5][source].astype(
+                            jnp.float32
+                        )
+                        near = (near * factor).astype(jnp.bfloat16)
+                        far = (far * factor).astype(jnp.bfloat16)
+                    block = jnp.concatenate(
+                        [jnp.where(upper, near, far), jnp.where(upper, far, near)], axis=0
+                    )
+                    product = jnp.dot(
+                        piece[flip][term, slot], block, preferred_element_type=jnp.float32
+                    )
+                    moved.append(product.astype(jnp.bfloat16))
+                    where.append(target)
+                for slot in range(capacity):
+                    target = where[slot]
+                    total[target] += jnp.dot(
+                        moved[slot],
+                        rights[flip][term, jnp.minimum(target, blocks - 1)],
+                        preferred_element_type=jnp.float32,
+                    )
+
+    if last:
+        out[...] = total[:blocks].astype(out.dtype)
+
+
+def apply_group(half, codes, scale, pieces, rights, total, last):
+    terms, capacity, rows, width = pieces[0][0].shape
+    blocks = rights[0].shape[1]
+    first, second = total is None, len(pieces[0]) == 6
+    arrays = [array for piece in pieces for array in piece] + list(rights)
+    if not first:
+        arrays.append(total)
+    scalars = pl.BlockSpec(memory_space=pltpu.SMEM)
+    whole = pl.BlockSpec(memory_space=pltpu.VMEM)
+    total_shape = (blocks + 1, rows, width)
+    if last:
+        out_shape = jax.ShapeDtypeStruct((blocks, rows, width), jnp.bfloat16)
+        scratch = [pltpu.VMEM(total_shape, jnp.float32)]
+    else:
+        out_shape = jax.ShapeDtypeStruct(total_shape, jnp.float32)
+        scratch = []
+    return pl.pallas_call(
+        functools.partial(
+            apply_kernel, len(pieces), second, first, last, capacity, blocks, terms
+        ),
+        out_shape=out_shape,
+        in_specs=[scalars] * 3 + [whole] * len(arrays),
+        out_specs=whole,
+        scratch_shapes=scratch,
+        compiler_params=pltpu.CompilerParams(vmem_limit_bytes=VMEM_LIMIT),
+        cost_estimate=pl.CostEstimate(
+            flops=len(pieces) * 2 * terms * capacity * 2 * 2 * rows * width * width,
+            bytes_accessed=sum(array.size * array.dtype.itemsize for array in arrays),
+            transcendentals=0,
+        ),
+    )(half, codes, scale, *arrays)
+
+
+def residual_kernel(me_ref, total_ref, wave_ref, rest_ref, stats_ref):
+    blocks = wave_ref.shape[0]
+
+    def sums(block, carry):
+        cross, own = carry
+        wave = wave_ref[block].astype(jnp.float32)
+        return cross + wave * total_ref[block], own + wave * wave
+
+    zero = jnp.zeros(wave_ref.shape[1:], jnp.float32)
+    cross, own = lax.fori_loop(0, blocks, sums, (zero, zero), unroll=4)
+    cross, own = jnp.sum(cross, keepdims=True), jnp.sum(own, keepdims=True)
+    local = jnp.where(own > 0, cross / own, 0.0)
+
+    def rest(block, carry):
+        value = total_ref[block] - local * wave_ref[block].astype(jnp.float32)
+        rest_ref[block] = value.astype(jnp.bfloat16)
+        return carry + value * value
+
+    about = jnp.sum(lax.fori_loop(0, blocks, rest, zero, unroll=4), keepdims=True)
+    lane = lax.broadcasted_iota(jnp.int32, stats_ref.shape, 1)
+    row = lax.broadcasted_iota(jnp.int32, stats_ref.shape, 0)
+    values = jnp.where(lane == 0, about, jnp.where(lane == 1, cross, jnp.where(lane == 2, own, local)))
+    stats_ref[...] = jnp.where((row == me_ref[0]) & (lane < 4), values, 0.0)
+
+
+def local_residual(me, devices, total, wave):
+    scalars = pl.BlockSpec(memory_space=pltpu.SMEM)
+    whole = pl.BlockSpec(memory_space=pltpu.VMEM)
+    return pl.pallas_call(
+        residual_kernel,
+        out_shape=(
+            jax.ShapeDtypeStruct(wave.shape, jnp.bfloat16),
+            jax.ShapeDtypeStruct((devices, 128), jnp.float32),
+        ),
+        in_specs=[scalars, whole, whole],
+        out_specs=(whole, whole),
+        compiler_params=pltpu.CompilerParams(vmem_limit_bytes=VMEM_LIMIT),
+    )(me, total, wave)
+
+
+def per_device_ring(wavefunction, left_operator, right_operator, target_owner, target_local):
+    owners, halves = lax.axis_size("sec"), lax.axis_size("term")
+    devices = owners * halves
+    me, half = lax.axis_index("sec"), lax.axis_index("term")
+    terms, blocks, height, width = left_operator.shape
+    rows = height // halves
+    capacity = 2 * blocks // owners
+    place = ring_place(me, owners)
+    device = jnp.reshape(me * halves + half, (1,)).astype(jnp.int32)
+    half_scalar = jnp.reshape(half, (1,)).astype(jnp.int32)
+
+    own_rows = lax.dynamic_slice_in_dim(wavefunction, half * rows, rows, 1)
+    other_rows = lax.dynamic_slice_in_dim(wavefunction, (1 - half) * rows, rows, 1)
+    reach = (owners - 1) // 2
+    distances = [0] + [s for step in range(1, reach + 1) for s in (step, -step)]
+    if owners % 2 == 0:
+        distances.append(owners // 2)
+
+    codes = slot_codes(target_owner, target_local, owners, capacity)
+    sources = codes // (2 * blocks)
+    term_ids = jnp.arange(terms, dtype=jnp.int32)[:, None]
+    flat_left = left_operator.reshape(terms * blocks * halves, rows, width)
+    lefts = {}
+    for s in reversed(distances):
+        to = ring_owner(place + s, owners)
+        picked = lax.dynamic_index_in_dim(sources, to, axis=1, keepdims=False)
+        for flip in range(2):
+            pick = (term_ids * blocks + picked) * halves + (half ^ flip)
+            piece = flat_left[pick.reshape(-1)].reshape(terms, capacity, rows, width)
+            if s or flip:
+                piece = send(piece, owners, halves, (s,) * halves, flip)
+            lefts[s, flip] = piece
+
+    mine = jnp.arange(devices, dtype=jnp.int32) == device[0]
+    table = jnp.where(mine[:, None], codes.reshape(1, -1), 0)
+    table = spread(table, devices, device).reshape(devices, terms, owners, capacity)
+    table = lax.dynamic_index_in_dim(table, me, axis=2, keepdims=False)
+    rights = (right_operator, swap(right_operator, owners, halves))
+
+    near = ring_gather(own_rows, owners, halves, half)
+    far = {s: swap(unit, owners, halves) if s else other_rows for s, unit in near.items()}
+
+    groups = [[0]] + [[step, -step] for step in range(1, reach + 1)]
+    if owners % 2 == 0:
+        groups.append([owners // 2])
+
+    def origin(s, flip):
+        return ring_owner(place - s, owners) * halves + (half ^ flip)
+
+    group_codes = [
+        jnp.concatenate(
+            [
+                lax.dynamic_index_in_dim(table, origin(s, flip), 0, keepdims=False).reshape(-1)
+                for s in group
+                for flip in range(2)
+            ]
+        )
+        for group in groups
+    ]
+
+    total = None
+    no_scale = jnp.zeros((1,), jnp.float32)
+    for group, code in zip(groups, group_codes):
+        pieces = [(lefts[s, 0], lefts[s, 1], near[s], far[s]) for s in group]
+        total = apply_group(half_scalar, code, no_scale, pieces, rights, total, False)
+
+    rest, stats = local_residual(device, devices, total, own_rows)
+    near_rest = ring_gather(rest, owners, halves, half)
+    far_rest = {s: swap(unit, owners, halves) for s, unit in near_rest.items()}
+
+    stats = spread(stats, devices, device)
+    rayleigh = jnp.sum(stats[:, 1]) / jnp.sum(stats[:, 2])
+    offset = stats[:, 3] - rayleigh
+    residual_sq = jnp.sum(stats[:, 0] + jnp.square(offset) * stats[:, 2])
+    entries = blocks * owners * height * width
+    factor = lax.rsqrt(residual_sq / entries + 1e-06)
+
+    total = None
+    for group, code in zip(groups, group_codes):
+        pieces = [
+            (lefts[s, 0], lefts[s, 1], near_rest[s], far_rest[s], near[s], far[s]) for s in group
+        ]
+        scale = jnp.stack([factor] + [offset[origin(s, flip)] for s in group for flip in range(2)])
+        total = apply_group(
+            half_scalar, code, scale, pieces, rights, total, group is groups[-1]
+        )
+    return (total, jnp.reshape(rayleigh, (1,)))
+
+
+def stream_kernel(first, capacity, blocks, code_ref, left_ref, vector_ref, right_ref, *rest):
     total_in, total = (None, rest[0]) if first else rest
     step = pl.program_id(0)
     rows, width = left_ref.shape[2:]
@@ -50,13 +326,13 @@
             )
 
 
-def apply_chunk(total, codes, left, vector, right):
+def stream_chunk(total, codes, left, vector, right):
     owners, _, blocks, rows, width = vector.shape
     capacity = left.shape[1]
     first = total is None
     spec_total = pl.BlockSpec((blocks + 1, rows, width), lambda s, c: (0, 0, 0))
     return pl.pallas_call(
-        functools.partial(apply_kernel, first, capacity, blocks),
+        functools.partial(stream_kernel, first, capacity, blocks),
         out_shape=jax.ShapeDtypeStruct((blocks + 1, rows, width), jnp.float32),
         grid_spec=pltpu.PrefetchScalarGridSpec(
             num_scalar_prefetch=1,
@@ -78,7 +354,7 @@
     )(codes, left, vector, right, *([] if first else [total]))
 
 
-def per_device(wavefunction, left_operator, right_operator, target_owner, target_local):
+def per_device_streamed(wavefunction, left_operator, right_operator, target_owner, target_local):
     owners = lax.axis_size("sec")
     halves = lax.axis_size("term")
     me, half = lax.axis_index("sec"), lax.axis_index("term")
@@ -104,7 +380,7 @@
     def apply(vector):
         total = None
         for k in range(terms):
-            total = apply_chunk(total, my_codes[:, k], moved_left[k], vector, right[k])
+            total = stream_chunk(total, my_codes[:, k], moved_left[k], vector, right[k])
         return total[:blocks]
 
     sigma_rows = apply(gathered)
@@ -121,6 +397,13 @@
     direction = lax.all_gather(direction, BOTH, axis=0).reshape(gathered.shape)
     sigma_two = apply(direction).astype(jnp.bfloat16)
     return (sigma_two, jnp.reshape(rayleigh, (1,)))
+
+
+def per_device(wavefunction, *operands):
+    gathered_bytes = lax.axis_size("sec") * wavefunction.size * wavefunction.dtype.itemsize
+    if 2 * gathered_bytes > RING_BYTES:
+        return per_device_streamed(wavefunction, *operands)
+    return per_device_ring(wavefunction, *operands)
 
 
 def solution(mesh):

time: 348 us -> 298 us (0.86)
  blocking collectives: 113 us -> 0 us
  starting transfers between devices: 22.5 us -> 58.7 us
  Pallas kernels: 20.4 us -> 48.6 us
  between operations: 19.7 us -> 4.59 us
  local copies, waits for them, and re-layouts: 35.7 us -> 48.5 us
  other arithmetic: 8.91 us -> 17.4 us
  waiting for transfers between devices: 127 us -> 119 us
    ppermute x0 -> x53, waiting for transfers between devices: none -> 119 us  [the longest x45 95.4 us: send(): return lax.ppermute(value, BOTH, pairs)]
    all_gather x1 -> x0, blocking collectives: 73.2 us -> none  [per_device(): all_codes = lax.all_gather(codes, BOTH, axis=0)]
    all_gather x3 -> x0, waiting for transfers between devices: 72.3 us -> none  [the longest x1 72.3 us: per_device(): direction = lax.all_gather(direction, BOTH, axis=0).reshape(gathered.shape)]
    ppermute x0 -> x53, starting transfers between devices: none -> 58.7 us  [the longest x45 51 us: send(): return lax.ppermute(value, BOTH, pairs)]
    all_to_all x2 -> x0, waiting for transfers between devices: 54.4 us -> none  [per_device(): lax.all_to_all(pieces, BOTH, split_axis=0, concat_axis=0, tiled=True)]
    unnamed x1 -> x0, blocking collectives: 39.6 us -> none
    pallas_call x4 -> x11, Pallas kernels: 20.4 us -> 48.6 us  [the longest x10 47.9 us: apply_group(): pl.pallas_call(functools.partial(apply_kernel, len(pieces), second, first...]
    all_to_all x2 -> x0, starting transfers between devices: 22.3 us -> none  [per_device(): lax.all_to_all(pieces, BOTH, split_axis=0, concat_axis=0, tiled=True)]
  transfers between devices with their start and end apart: 5 -> 53, of which waited for: 2 -> 18; matrix products, arithmetic and copies ran while one was open for 4% -> 16% of each run, Pallas kernels for 1% -> 13%
where the time goes in v2:
time: 298 us; the launch traced here: 297 us
  waiting for transfers between devices  119 us (40%)
  starting transfers between devices  58.7 us (20%)
  Pallas kernels  48.6 us (16%)
  local copies, waits for them, and re-layouts  48.5 us (16%)
  other arithmetic  17.4 us (6%)
  between operations  4.59 us (2%)
    ppermute x45, waiting for transfers between devices, send(): return lax.ppermute(value, BOTH, pairs)  95.4 us
    ppermute x45, starting transfers between devices, send(): return lax.ppermute(value, BOTH, pairs)  51 us
    pallas_call x10, Pallas kernels, apply_group(): pl.pallas_call(functools.partial(apply_kernel, len(pieces), second, first...  47.9 us
    ppermute x8, waiting for transfers between devices, spread(): lax.ppermute(value, BOTH, [(d, d ^ step) for d in range(devices)])  23.9 us
    gather x16, local copies, waits for them, and re-layouts, per_device_ring(): piece = flat_left[pick.reshape(-1)].reshape(terms, capacity, rows, width)  19.9 us
    unnamed x78, local copies, waits for them, and re-layouts  14.9 us
    another operation x3, local copies, waits for them, and re-layouts, per_device_ring(): jnp.stack([factor] + [offset[origin(s, flip)] for s in group for flip in...  7.79 us
    ppermute x8, starting transfers between devices, spread(): lax.ppermute(value, BOTH, [(d, d ^ step) for d in range(devices)])  7.72 us
  transfers between devices with their start and end apart: 53, of which 18 were waited for; matrix products, arithmetic and copies ran while one was open for 16% of the time, Pallas kernels for 13%

profile of v2, /device:TPU:0, one launch (start us, length us, event | category | flops | bytes accessed | tf_op | source)
XLA Modules:
  0.0 297.1 jit_solution(12008764318519583860)
XLA Ops:
  0.7 2.2 constant_dynamic-slice_fusion.16
  2.9 3.0 %collective-permute-start.6 = (bf16[32,64,128]{2,1,0:T(8,128)(2,1)S(1)}, bf16[32,64,128]{2,1,0:T(8,128)(2,1)S(1)}, u32[]{:S(2)}, u32[]{:S(2)}) collective-permute-start(bf16[32,64,128]{2,1,0:T(8,128)(2,1)S(1)} %get-tuple-element.35.refs_2_.wave_ref.refs_4_), channel_id=1, source_target_pairs={{0,4},{1,5},{4,8},{5,9},{8,12},{9,13},{12,14},{13,15},{14,10},{15,... | collective-permute-start | bytes 1572872 | tf_op jit(solution)/shard_map/ppermute | solution.py:41
  8.7 2.0 collective-permute-start.1
  12.0 7.3 %collective-permute-done.1 = s32[16,128]{0,1:T(8,128)} collective-permute-done((s32[16,128]{0,1:T(8,128)S(1)}, s32[16,128]{0,1:T(8,128)}, u32[]{:S(2)}, u32[]{:S(2)}) %collective-permute-start.1) | collective-permute-done | bytes 8224 | tf_op jit(solution)/shard_map/ppermute | solution.py:65
  22.3 2.0 collective-permute-start.27
  25.5 3.8 %collective-permute-start.3 = (s32[16,128]{0,1:T(8,128)S(1)}, s32[16,128]{0,1:T(8,128)S(1)}, u32[]{:S(2)}, u32[]{:S(2)}) collective-permute-start(s32[16,128]{0,1:T(8,128)S(1)} %add.1002), channel_id=1, source_target_pairs={{0,8},{1,9},{2,10},{3,11},{4,12},{5,13},{6,14},{7,15},{8,0},{9,1},... | collective-permute-start | bytes 24584 | tf_op jit(solution)/shard_map/ppermute | solution.py:65
  34.9 3.3 %collective-permute-start.30 = (bf16[2,8,64,128]{3,2,1,0:T(8,128)(2,1)}, bf16[2,8,64,128]{3,2,1,0:T(8,128)(2,1)}, u32[]{:S(2)}, u32[]{:S(2)}) collective-permute-start(bf16[2,8,64,128]{3,2,1,0:T(8,128)(2,1)} %bitcast.98), channel_id=1, source_target_pairs={{0,2},{1,3},{4,0},{5,1},{8,4},{9,5},{12,8},{13,9},{14,12},{15,13},... | collective-permute-start | bytes 786440 | tf_op jit(solution)/shard_map/ppermute | solution.py:41
  40.1 2.7 collective-permute-start.31
  44.8 2.4 collective-permute-start.21
  47.6 1.6 collective-permute-start.10
  50.6 2.3 collective-permute-start.22
  54.9 1.9 collective-permute-done.21.refs_0_
  59.2 19.6 %collective-permute-done.22.refs_1_ = bf16[2,8,64,128]{3,2,1,0:T(8,128)(2,1)} collective-permute-done((bf16[2,8,64,128]{3,2,1,0:T(8,128)(2,1)}, bf16[2,8,64,128]{3,2,1,0:T(8,128)(2,1)}, u32[]{:S(2)}, u32[]{:S(2)}) %collective-permute-start.22) | collective-permute-done | bytes 262176 | tf_op jit(solution)/shard_map/ppermute | solution.py:41
  80.8 6.7 %collective-permute-start.15 = (bf16[2,8,64,128]{3,2,1,0:T(8,128)(2,1)}, bf16[2,8,64,128]{3,2,1,0:T(8,128)(2,1)}, u32[]{:S(2)}, u32[]{:S(2)}) collective-permute-start(bf16[2,8,64,128]{3,2,1,0:T(8,128)(2,1)} %bitcast.97), channel_id=1, source_target_pairs={{0,12},{1,13},{4,14},{5,15},{8,10},{9,11},{12,6},{13,7},{14,2},{15... | collective-permute-start | bytes 786440 | tf_op jit(solution)/shard_map/ppermute | solution.py:41
  87.6 2.0 collective-permute-start.11
  91.5 8.3 %collective-permute-done.25.refs_5_.refs_7_ = bf16[2,8,64,128]{3,2,1,0:T(8,128)(2,1)} collective-permute-done((bf16[2,8,64,128]{3,2,1,0:T(8,128)(2,1)}, bf16[2,8,64,128]{3,2,1,0:T(8,128)(2,1)}, u32[]{:S(2)}, u32[]{:S(2)}) %collective-permute-start.25) | collective-permute-done | bytes 262176 | tf_op jit(solution)/shard_map/ppermute | solution.py:41
  101.7 3.7 %collective-permute-start.18 = (bf16[2,8,64,128]{3,2,1,0:T(8,128)(2,1)}, bf16[2,8,64,128]{3,2,1,0:T(8,128)(2,1)S(1)}, u32[]{:S(2)}, u32[]{:S(2)}) collective-permute-start(bf16[2,8,64,128]{3,2,1,0:T(8,128)(2,1)} %bitcast.104), channel_id=1, source_target_pairs={{0,10},{1,11},{4,6},{5,7},{8,2},{9,3},{12,0},{13,1},{14,4},{15,5},... | collective-permute-start | bytes 786440 | tf_op jit(solution)/shard_map/ppermute | solution.py:41
  105.5 22.6 %collective-permute-done.16.refs_1_ = bf16[2,8,64,128]{3,2,1,0:T(8,128)(2,1)} collective-permute-done((bf16[2,8,64,128]{3,2,1,0:T(8,128)(2,1)}, bf16[2,8,64,128]{3,2,1,0:T(8,128)(2,1)}, u32[]{:S(2)}, u32[]{:S(2)}) %collective-permute-start.16) | collective-permute-done | bytes 262176 | tf_op jit(solution)/shard_map/ppermute | solution.py:41
  131.7 8.7 %collective-permute-done.19.refs_5_.refs_7_ = bf16[2,8,64,128]{3,2,1,0:T(8,128)(2,1)S(1)} collective-permute-done((bf16[2,8,64,128]{3,2,1,0:T(8,128)(2,1)}, bf16[2,8,64,128]{3,2,1,0:T(8,128)(2,1)S(1)}, u32[]{:S(2)}, u32[]{:S(2)}) %collective-permute-start.19) | collective-permute-done | bytes 262176 | tf_op jit(solution)/shard_map/ppermute | solution.py:41
  141.7 5.1 %collective-permute-start.26 = (bf16[32,64,128]{2,1,0:T(8,128)(2,1)}, bf16[32,64,128]{2,1,0:T(8,128)(2,1)}, u32[]{:S(2)}, u32[]{:S(2)}) collective-permute-start(bf16[32,64,128]{2,1,0:T(8,128)(2,1)} %collective-permute-done.10.refs_6_.refs_10_), channel_id=1, source_target_pairs={{0,1},{1,0},{4,5},{5,4},{8,9},{9,8},{12,13},{13,12},{14,15},{15,14... | collective-permute-start | bytes 1572872 | tf_op jit(solution)/shard_map/ppermute | solution.py:41
  152.1 1.7 collective-permute-done.12.refs_2_.refs_4_
  154.4 4.1 %collective-permute-start.5 = (bf16[2,8,64,128]{3,2,1,0:T(8,128)(2,1)}, bf16[2,8,64,128]{3,2,1,0:T(8,128)(2,1)S(1)}, u32[]{:S(2)}, u32[]{:S(2)}) collective-permute-start(bf16[2,8,64,128]{3,2,1,0:T(8,128)(2,1)} %bitcast.91), channel_id=1, source_target_pairs={{0,15},{1,14},{4,11},{5,10},{8,7},{9,6},{12,3},{13,2},{14,1},{15,0... | collective-permute-start | bytes 786440 | tf_op jit(solution)/shard_map/ppermute | solution.py:41
  158.7 1.6 copy-done.1
  162.2 3.0 %shard_map.68.refs_10_ = f32[33,64,128]{2,1,0:T(8,128)S(1)} custom-call(s32[1]{0:T(128)} %bitcast.half_ref, s32[32]{0:T(128)S(1)} %pad_add_fusion.4.codes_ref, f32[1]{0:T(128)} %constant.578.clone.1.scale_ref, bf16[2,8,64,128]{3,2,1,0:T(8,128)(2,1)S(1)} %bitcast.87, bf16[2,8,64,128]{3,2,1,0:T(8,128)(2,1)S(1)} %copy-done.11, ...), custom_call_target="tpu_custom_call" | custom-call | flops 134217728 | bytes 5767168 | tf_op jit(solution)/shard_map/pallas_call | solution.py:156
  165.3 5.1 %shard_map.69.refs_10_ = f32[33,64,128]{2,1,0:T(8,128)S(1)} custom-call(s32[1]{0:T(128)} %bitcast.half_ref, s32[64]{0:T(128)S(1)} %pad_add_fusion.3.codes_ref, f32[1]{0:T(128)} %constant.578.clone.1.scale_ref, bf16[2,8,64,128]{3,2,1,0:T(8,128)(2,1)} %collective-permute-done.27.refs_0_, bf16[2,8,64,128]{3,2,1,0:T(8,128)(2,1)} %collective-permute-done.28.refs_1_, ...), custom_call_target="tpu_custom_call" | custom-call | flops 268435456 | bytes 8421376 | tf_op jit(solution)/shard_map/pallas_call | solution.py:156
  170.4 5.3 %shard_map.70.refs_10_ = f32[33,64,128]{2,1,0:T(8,128)S(1)} custom-call(s32[1]{0:T(128)} %bitcast.half_ref, s32[64]{0:T(128)S(1)} %pad_add_fusion.2.codes_ref, f32[1]{0:T(128)} %constant.578.clone.1.scale_ref, bf16[2,8,64,128]{3,2,1,0:T(8,128)(2,1)} %collective-permute-done.21.refs_0_, bf16[2,8,64,128]{3,2,1,0:T(8,128)(2,1)} %collective-permute-done.22.refs_1_, ...), custom_call_target="tpu_custom_call" | custom-call | flops 268435456 | bytes 8421376 | tf_op jit(solution)/shard_map/pallas_call | solution.py:156
  175.8 4.9 %shard_map.71.refs_6_ = f32[33,64,128]{2,1,0:T(8,128)S(1)} custom-call(s32[1]{0:T(128)} %bitcast.half_ref, s32[64]{0:T(128)S(1)} %pad_add_fusion.1.codes_ref, f32[1]{0:T(128)} %constant.578.clone.1.scale_ref, bf16[2,8,64,128]{3,2,1,0:T(8,128)(2,1)} %collective-permute-done.15.refs_0_, bf16[2,8,64,128]{3,2,1,0:T(8,128)(2,1)} %collective-permute-done.16.refs_1_, ...), custom_call_target="tpu_custom_call" | custom-call | flops 268435456 | bytes 8421376 | tf_op jit(solution)/shard_map/pallas_call | solution.py:156
  180.8 3.5 %shard_map.72.total_ref = f32[33,64,128]{2,1,0:T(8,128)S(1)} custom-call(s32[1]{0:T(128)} %bitcast.half_ref, s32[32]{0:T(128)S(1)} %pad_add_fusion.codes_ref, f32[1]{0:T(128)} %constant.578.clone.1.scale_ref, bf16[2,8,64,128]{3,2,1,0:T(8,128)(2,1)S(1)} %collective-permute-done.4.refs_0_, bf16[2,8,64,128]{3,2,1,0:T(8,128)(2,1)S(1)} %collective-permute-done.5.refs_1_, ...), custom_call_target="tpu_custom_call" | custom-call | flops 134217728 | bytes 6848512 | tf_op jit(solution)/shard_map/pallas_call | solution.py:156
  185.1 2.1 collective-permute-start.41
  187.1 12.3 %collective-permute-done.38.refs_2_ = bf16[32,64,128]{2,1,0:T(8,128)(2,1)S(1)} collective-permute-done((bf16[32,64,128]{2,1,0:T(8,128)(2,1)S(1)}, bf16[32,64,128]{2,1,0:T(8,128)(2,1)S(1)}, u32[]{:S(2)}, u32[]{:S(2)}) %collective-permute-start.38) | collective-permute-done | bytes 524320 | tf_op jit(solution)/shard_map/ppermute | solution.py:41
  199.5 2.0 collective-permute-start.42
  201.5 11.7 %collective-permute-done.39.refs_2_ = bf16[32,64,128]{2,1,0:T(8,128)(2,1)} collective-permute-done((bf16[32,64,128]{2,1,0:T(8,128)(2,1)S(1)}, bf16[32,64,128]{2,1,0:T(8,128)(2,1)}, u32[]{:S(2)}, u32[]{:S(2)}) %collective-permute-start.39) | collective-permute-done | bytes 524320 | tf_op jit(solution)/shard_map/ppermute | solution.py:41
  213.4 1.7 collective-permute-start.43
  218.1 8.1 %collective-permute-done.40.refs_2_ = bf16[32,64,128]{2,1,0:T(8,128)(2,1)} collective-permute-done((bf16[32,64,128]{2,1,0:T(8,128)(2,1)}, bf16[32,64,128]{2,1,0:T(8,128)(2,1)}, u32[]{:S(2)}, u32[]{:S(2)}) %collective-permute-start.40) | collective-permute-done | bytes 524320 | tf_op jit(solution)/shard_map/ppermute | solution.py:41
  226.5 1.9 broadcast_select_fusion
  229.9 1.7 collective-permute-start.35
  231.6 6.4 %collective-permute-done.35 = f32[16,128]{1,0:T(8,128)S(1)} collective-permute-done((f32[16,128]{1,0:T(8,128)S(1)}, f32[16,128]{1,0:T(8,128)S(1)}, u32[]{:S(2)}, u32[]{:S(2)}) %collective-permute-start.35) | collective-permute-done | bytes 8224 | tf_op jit(solution)/shard_map/ppermute | solution.py:65
  238.0 3.6 %collective-permute-done.36 = f32[16,128]{1,0:T(8,128)S(1)} collective-permute-done((f32[16,128]{1,0:T(8,128)S(1)}, f32[16,128]{1,0:T(8,128)S(1)}, u32[]{:S(2)}, u32[]{:S(2)}) %collective-permute-start.36) | collective-permute-done | bytes 8224 | tf_op jit(solution)/shard_map/ppermute | solution.py:65
  241.7 4.5 %collective-permute-done.37 = f32[16,128]{1,0:T(8,128)S(1)} collective-permute-done((f32[16,128]{1,0:T(8,128)S(1)}, f32[16,128]{1,0:T(8,128)S(1)}, u32[]{:S(2)}, u32[]{:S(2)}) %collective-permute-start.37) | collective-permute-done | bytes 8224 | tf_op jit(solution)/shard_map/ppermute | solution.py:65
  253.6 2.7 stack.26.scale_ref
  256.3 2.6 stack.25.scale_ref
  258.9 2.5 stack.24.scale_ref
  264.1 1.6 copy-done.2
  269.7 3.4 %shard_map.74.refs_14_ = f32[33,64,128]{2,1,0:T(8,128)S(1)} custom-call(s32[1]{0:T(128)} %bitcast.half_ref, s32[32]{0:T(128)S(1)} %pad_add_fusion.4.codes_ref, f32[3]{0:T(128)S(1)} %pad_maximum_fusion.1.scale_ref, bf16[2,8,64,128]{3,2,1,0:T(8,128)(2,1)S(1)} %bitcast.88, bf16[2,8,64,128]{3,2,1,0:T(8,128)(2,1)S(1)} %copy-done.12, ...), custom_call_target="tpu_custom_call" | custom-call | flops 134217728 | bytes 6815744 | tf_op jit(solution)/shard_map/pallas_call | solution.py:156
  273.2 5.6 %shard_map.75.refs_14_ = f32[33,64,128]{2,1,0:T(8,128)S(1)} custom-call(s32[1]{0:T(128)} %bitcast.half_ref, s32[64]{0:T(128)S(1)} %pad_add_fusion.3.codes_ref, f32[5]{0:T(128)S(1)} %stack.26.scale_ref, bf16[2,8,64,128]{3,2,1,0:T(8,128)(2,1)} %collective-permute-done.27.refs_0_, bf16[2,8,64,128]{3,2,1,0:T(8,128)(2,1)} %collective-permute-done.28.refs_1_, ...), custom_call_target="tpu_custom_call" | custom-call | flops 268435456 | bytes 10518528 | tf_op jit(solution)/shard_map/pallas_call | solution.py:156
  278.8 6.4 %shard_map.76.refs_14_ = f32[33,64,128]{2,1,0:T(8,128)S(1)} custom-call(s32[1]{0:T(128)} %bitcast.half_ref, s32[64]{0:T(128)S(1)} %pad_add_fusion.2.codes_ref, f32[5]{0:T(128)S(1)} %stack.25.scale_ref, bf16[2,8,64,128]{3,2,1,0:T(8,128)(2,1)} %collective-permute-done.21.refs_0_, bf16[2,8,64,128]{3,2,1,0:T(8,128)(2,1)} %collective-permute-done.22.refs_1_, ...), custom_call_target="tpu_custom_call" | custom-call | flops 268435456 | bytes 10518528 | tf_op jit(solution)/shard_map/pallas_call | solution.py:156
  285.3 6.1 %shard_map.77.refs_8_ = f32[33,64,128]{2,1,0:T(8,128)S(1)} custom-call(s32[1]{0:T(128)} %bitcast.half_ref, s32[64]{0:T(128)S(1)} %pad_add_fusion.1.codes_ref, f32[5]{0:T(128)S(1)} %stack.24.scale_ref, bf16[2,8,64,128]{3,2,1,0:T(8,128)(2,1)} %collective-permute-done.15.refs_0_, bf16[2,8,64,128]{3,2,1,0:T(8,128)(2,1)} %collective-permute-done.16.refs_1_, ...), custom_call_target="tpu_custom_call" | custom-call | flops 268435456 | bytes 10518528 | tf_op jit(solution)/shard_map/pallas_call | solution.py:156
  291.4 4.6 %shard_map.78 = bf16[32,64,128]{2,1,0:T(8,128)(2,1)} custom-call(s32[1]{0:T(128)} %bitcast.half_ref, s32[32]{0:T(128)S(1)} %pad_add_fusion.codes_ref, f32[3]{0:T(128)S(1)} %pad_maximum_fusion.scale_ref, bf16[2,8,64,128]{3,2,1,0:T(8,128)(2,1)S(1)} %copy-done.20, bf16[2,8,64,128]{3,2,1,0:T(8,128)(2,1)S(1)} %copy-done.22, ...), custom_call_target="tpu_custom_call" | custom-call | flops 134217728 | bytes 7897088 | tf_op jit(solution)/shard_map/pallas_call | solution.py:156
  (243 shorter events, 60.2 us)
Async XLA Ops:
  2.9 44.3 %collective-permute-start.6 = (bf16[32,64,128]{2,1,0:T(8,128)(2,1)S(1)}, bf16[32,64,128]{2,1,0:T(8,128)(2,1)S(1)}, u32[]{:S(2)}, u32[]{:S(2)}) collective-permute-start(bf16[32,64,128]{2,1,0:T(8,128)(2,1)S(1)} %get-tuple-element.35.refs_2_.wave_ref.refs_4_), channel_id=1, source_target_pairs={{0,4},{1,5},{4,8},{5,9},{8,12},{9,13},{12,14},{13,15},{14,10},{15,... | collective-permute-start | bytes 1572872 | tf_op jit(solution)/shard_map/ppermute | solution.py:41
  5.9 41.7 %collective-permute-start.9 = (bf16[32,64,128]{2,1,0:T(8,128)(2,1)S(1)}, bf16[32,64,128]{2,1,0:T(8,128)(2,1)}, u32[]{:S(2)}, u32[]{:S(2)}) collective-permute-start(bf16[32,64,128]{2,1,0:T(8,128)(2,1)S(1)} %get-tuple-element.35.refs_2_.wave_ref.refs_4_), channel_id=1, source_target_pairs={{0,2},{1,3},{4,0},{5,1},{8,4},{9,5},{12,8},{13,9},{14,12},{15,13},... | collective-permute-start | bytes 1572872 | tf_op jit(solution)/shard_map/ppermute | solution.py:41
  8.7 10.6 %collective-permute-start.1 = (s32[16,128]{0,1:T(8,128)S(1)}, s32[16,128]{0,1:T(8,128)}, u32[]{:S(2)}, u32[]{:S(2)}) collective-permute-start(s32[16,128]{0,1:T(8,128)S(1)} %fusion), channel_id=1, source_target_pairs={{0,2},{1,3},{2,0},{3,1},{4,6},{5,7},{6,4},{7,5},{8,10},{9,11},{10,... | collective-permute-start | bytes 24584 | tf_op jit(solution)/shard_map/ppermute | solution.py:65
  12.0 22.9 %collective-permute-start.33 = (bf16[2,8,64,128]{3,2,1,0:T(8,128)(2,1)}, bf16[2,8,64,128]{3,2,1,0:T(8,128)(2,1)S(1)}, u32[]{:S(2)}, u32[]{:S(2)}) collective-permute-start(bf16[2,8,64,128]{3,2,1,0:T(8,128)(2,1)} %bitcast.92), channel_id=1, source_target_pairs={{0,1},{1,0},{4,5},{5,4},{8,9},{9,8},{12,13},{13,12},{14,15},{15,14... | collective-permute-start | bytes 786440 | tf_op jit(solution)/shard_map/ppermute | solution.py:41
  22.3 17.9 %collective-permute-start.27 = (bf16[2,8,64,128]{3,2,1,0:T(8,128)(2,1)}, bf16[2,8,64,128]{3,2,1,0:T(8,128)(2,1)}, u32[]{:S(2)}, u32[]{:S(2)}) collective-permute-start(bf16[2,8,64,128]{3,2,1,0:T(8,128)(2,1)} %bitcast.94), channel_id=1, source_target_pairs={{0,4},{1,5},{4,8},{5,9},{8,12},{9,13},{12,14},{13,15},{14,10},{15,... | collective-permute-start | bytes 786440 | tf_op jit(solution)/shard_map/ppermute | solution.py:41
  25.5 6.3 %collective-permute-start.3 = (s32[16,128]{0,1:T(8,128)S(1)}, s32[16,128]{0,1:T(8,128)S(1)}, u32[]{:S(2)}, u32[]{:S(2)}) collective-permute-start(s32[16,128]{0,1:T(8,128)S(1)} %add.1002), channel_id=1, source_target_pairs={{0,8},{1,9},{2,10},{3,11},{4,12},{5,13},{6,14},{7,15},{8,0},{9,1},... | collective-permute-start | bytes 24584 | tf_op jit(solution)/shard_map/ppermute | solution.py:65
  31.8 8.3 %collective-permute-start.28 = (bf16[2,8,64,128]{3,2,1,0:T(8,128)(2,1)}, bf16[2,8,64,128]{3,2,1,0:T(8,128)(2,1)}, u32[]{:S(2)}, u32[]{:S(2)}) collective-permute-start(bf16[2,8,64,128]{3,2,1,0:T(8,128)(2,1)} %bitcast.99), channel_id=1, source_target_pairs={{0,5},{1,4},{4,9},{5,8},{8,13},{9,12},{12,15},{13,14},{14,11},{15,... | collective-permute-start | bytes 786440 | tf_op jit(solution)/shard_map/ppermute | solution.py:41
  34.9 9.9 %collective-permute-start.30 = (bf16[2,8,64,128]{3,2,1,0:T(8,128)(2,1)}, bf16[2,8,64,128]{3,2,1,0:T(8,128)(2,1)}, u32[]{:S(2)}, u32[]{:S(2)}) collective-permute-start(bf16[2,8,64,128]{3,2,1,0:T(8,128)(2,1)} %bitcast.98), channel_id=1, source_target_pairs={{0,2},{1,3},{4,0},{5,1},{8,4},{9,5},{12,8},{13,9},{14,12},{15,13},... | collective-permute-start | bytes 786440 | tf_op jit(solution)/shard_map/ppermute | solution.py:41
  40.1 114.2 %collective-permute-start.14 = (bf16[2,32,128,128]{3,2,1,0:T(8,128)(2,1)}, bf16[2,32,128,128]{3,2,1,0:T(8,128)(2,1)}, u32[]{:S(2)}, u32[]{:S(2)}) collective-permute-start(bf16[2,32,128,128]{3,2,1,0:T(8,128)(2,1)} %refs_6_.3), channel_id=1, source_target_pairs={{0,1},{1,0},{4,5},{5,4},{8,9},{9,8},{12,13},{13,12},{14,15},{15,14... | collective-permute-start | bytes 6291464 | tf_op jit(solution)/shard_map/ppermute | solution.py:41
  40.1 10.5 %collective-permute-start.31 = (bf16[2,8,64,128]{3,2,1,0:T(8,128)(2,1)}, bf16[2,8,64,128]{3,2,1,0:T(8,128)(2,1)}, u32[]{:S(2)}, u32[]{:S(2)}) collective-permute-start(bf16[2,8,64,128]{3,2,1,0:T(8,128)(2,1)} %bitcast.93), channel_id=1, source_target_pairs={{0,3},{1,2},{4,1},{5,0},{8,5},{9,4},{12,9},{13,8},{14,13},{15,12},... | collective-permute-start | bytes 786440 | tf_op jit(solution)/shard_map/ppermute | solution.py:41
  44.8 11.9 %collective-permute-start.21 = (bf16[2,8,64,128]{3,2,1,0:T(8,128)(2,1)}, bf16[2,8,64,128]{3,2,1,0:T(8,128)(2,1)}, u32[]{:S(2)}, u32[]{:S(2)}) collective-permute-start(bf16[2,8,64,128]{3,2,1,0:T(8,128)(2,1)} %bitcast.95), channel_id=1, source_target_pairs={{0,8},{1,9},{4,12},{5,13},{8,14},{9,15},{12,10},{13,11},{14,6},{15... | collective-permute-start | bytes 786440 | tf_op jit(solution)/shard_map/ppermute | solution.py:41
  47.2 40.4 %collective-permute-start.7 = (bf16[32,64,128]{2,1,0:T(8,128)(2,1)S(1)}, bf16[32,64,128]{2,1,0:T(8,128)(2,1)}, u32[]{:S(2)}, u32[]{:S(2)}) collective-permute-start(bf16[32,64,128]{2,1,0:T(8,128)(2,1)S(1)} %collective-permute-done.6.refs_2_.refs_4_), channel_id=1, source_target_pairs={{0,4},{1,5},{4,8},{5,9},{8,12},{9,13},{12,14},{13,15},{14,10},{15,... | collective-permute-start | bytes 1572872 | tf_op jit(solution)/shard_map/ppermute | solution.py:41
  47.6 40.0 %collective-permute-start.10 = (bf16[32,64,128]{2,1,0:T(8,128)(2,1)}, bf16[32,64,128]{2,1,0:T(8,128)(2,1)}, u32[]{:S(2)}, u32[]{:S(2)}) collective-permute-start(bf16[32,64,128]{2,1,0:T(8,128)(2,1)} %collective-permute-done.9.refs_6_.refs_10_), channel_id=1, source_target_pairs={{0,2},{1,3},{4,0},{5,1},{8,4},{9,5},{12,8},{13,9},{14,12},{15,13},... | collective-permute-start | bytes 1572872 | tf_op jit(solution)/shard_map/ppermute | solution.py:41
  50.6 28.2 %collective-permute-start.22 = (bf16[2,8,64,128]{3,2,1,0:T(8,128)(2,1)}, bf16[2,8,64,128]{3,2,1,0:T(8,128)(2,1)}, u32[]{:S(2)}, u32[]{:S(2)}) collective-permute-start(bf16[2,8,64,128]{3,2,1,0:T(8,128)(2,1)} %bitcast.100), channel_id=1, source_target_pairs={{0,9},{1,8},{4,13},{5,12},{8,15},{9,14},{12,11},{13,10},{14,7},{15... | collective-permute-start | bytes 786440 | tf_op jit(solution)/shard_map/ppermute | solution.py:41
  56.7 24.1 %collective-permute-start.24 = (bf16[2,8,64,128]{3,2,1,0:T(8,128)(2,1)}, bf16[2,8,64,128]{3,2,1,0:T(8,128)(2,1)}, u32[]{:S(2)}, u32[]{:S(2)}) collective-permute-start(bf16[2,8,64,128]{3,2,1,0:T(8,128)(2,1)} %bitcast.101), channel_id=1, source_target_pairs={{0,6},{1,7},{4,2},{5,3},{8,0},{9,1},{12,4},{13,5},{14,8},{15,9},{1... | collective-permute-start | bytes 786440 | tf_op jit(solution)/shard_map/ppermute | solution.py:41
  78.9 21.0 %collective-permute-start.25 = (bf16[2,8,64,128]{3,2,1,0:T(8,128)(2,1)}, bf16[2,8,64,128]{3,2,1,0:T(8,128)(2,1)}, u32[]{:S(2)}, u32[]{:S(2)}) collective-permute-start(bf16[2,8,64,128]{3,2,1,0:T(8,128)(2,1)} %bitcast.96), channel_id=1, source_target_pairs={{0,7},{1,6},{4,3},{5,2},{8,1},{9,0},{12,5},{13,4},{14,9},{15,8},{1... | collective-permute-start | bytes 786440 | tf_op jit(solution)/shard_map/ppermute | solution.py:41
  80.8 20.9 %collective-permute-start.15 = (bf16[2,8,64,128]{3,2,1,0:T(8,128)(2,1)}, bf16[2,8,64,128]{3,2,1,0:T(8,128)(2,1)}, u32[]{:S(2)}, u32[]{:S(2)}) collective-permute-start(bf16[2,8,64,128]{3,2,1,0:T(8,128)(2,1)} %bitcast.97), channel_id=1, source_target_pairs={{0,12},{1,13},{4,14},{5,15},{8,10},{9,11},{12,6},{13,7},{14,2},{15... | collective-permute-start | bytes 786440 | tf_op jit(solution)/shard_map/ppermute | solution.py:41
  87.6 42.7 %collective-permute-start.8 = (bf16[32,64,128]{2,1,0:T(8,128)(2,1)}, bf16[32,64,128]{2,1,0:T(8,128)(2,1)S(1)}, u32[]{:S(2)}, u32[]{:S(2)}) collective-permute-start(bf16[32,64,128]{2,1,0:T(8,128)(2,1)} %collective-permute-done.7.refs_2_.refs_4_), channel_id=1, source_target_pairs={{0,4},{1,5},{4,8},{5,9},{8,12},{9,13},{12,14},{13,15},{14,10},{15,... | collective-permute-start | bytes 1572872 | tf_op jit(solution)/shard_map/ppermute | solution.py:41
  87.6 43.1 %collective-permute-start.11 = (bf16[32,64,128]{2,1,0:T(8,128)(2,1)}, bf16[32,64,128]{2,1,0:T(8,128)(2,1)}, u32[]{:S(2)}, u32[]{:S(2)}) collective-permute-start(bf16[32,64,128]{2,1,0:T(8,128)(2,1)} %collective-permute-done.10.refs_6_.refs_10_), channel_id=1, source_target_pairs={{0,2},{1,3},{4,0},{5,1},{8,4},{9,5},{12,8},{13,9},{14,12},{15,13},... | collective-permute-start | bytes 1572872 | tf_op jit(solution)/shard_map/ppermute | solution.py:41
  99.8 28.3 %collective-permute-start.16 = (bf16[2,8,64,128]{3,2,1,0:T(8,128)(2,1)}, bf16[2,8,64,128]{3,2,1,0:T(8,128)(2,1)}, u32[]{:S(2)}, u32[]{:S(2)}) collective-permute-start(bf16[2,8,64,128]{3,2,1,0:T(8,128)(2,1)} %bitcast.103), channel_id=1, source_target_pairs={{0,13},{1,12},{4,15},{5,14},{8,11},{9,10},{12,7},{13,6},{14,3},{15... | collective-permute-start | bytes 786440 | tf_op jit(solution)/shard_map/ppermute | solution.py:41
  101.7 28.5 %collective-permute-start.18 = (bf16[2,8,64,128]{3,2,1,0:T(8,128)(2,1)}, bf16[2,8,64,128]{3,2,1,0:T(8,128)(2,1)S(1)}, u32[]{:S(2)}, u32[]{:S(2)}) collective-permute-start(bf16[2,8,64,128]{3,2,1,0:T(8,128)(2,1)} %bitcast.104), channel_id=1, source_target_pairs={{0,10},{1,11},{4,6},{5,7},{8,2},{9,3},{12,0},{13,1},{14,4},{15,5},... | collective-permute-start | bytes 786440 | tf_op jit(solution)/shard_map/ppermute | solution.py:41
  128.1 13.6 %collective-permute-start.29 = (bf16[32,64,128]{2,1,0:T(8,128)(2,1)}, bf16[32,64,128]{2,1,0:T(8,128)(2,1)}, u32[]{:S(2)}, u32[]{:S(2)}) collective-permute-start(bf16[32,64,128]{2,1,0:T(8,128)(2,1)} %copy-done.5), channel_id=1, source_target_pairs={{0,1},{1,0},{4,5},{5,4},{8,9},{9,8},{12,13},{13,12},{14,15},{15,14... | collective-permute-start | bytes 1572872 | tf_op jit(solution)/shard_map/ppermute | solution.py:41
  130.2 10.2 %collective-permute-start.19 = (bf16[2,8,64,128]{3,2,1,0:T(8,128)(2,1)}, bf16[2,8,64,128]{3,2,1,0:T(8,128)(2,1)S(1)}, u32[]{:S(2)}, u32[]{:S(2)}) collective-permute-start(bf16[2,8,64,128]{3,2,1,0:T(8,128)(2,1)} %bitcast.102), channel_id=1, source_target_pairs={{0,11},{1,10},{4,7},{5,6},{8,3},{9,2},{12,1},{13,0},{14,5},{15,4},... | collective-permute-start | bytes 786440 | tf_op jit(solution)/shard_map/ppermute | solution.py:41
  130.2 20.1 %collective-permute-start.32 = (bf16[32,64,128]{2,1,0:T(8,128)(2,1)}, bf16[32,64,128]{2,1,0:T(8,128)(2,1)}, u32[]{:S(2)}, u32[]{:S(2)}) collective-permute-start(bf16[32,64,128]{2,1,0:T(8,128)(2,1)} %collective-permute-done.9.refs_6_.refs_10_), channel_id=1, source_target_pairs={{0,1},{1,0},{4,5},{5,4},{8,9},{9,8},{12,13},{13,12},{14,15},{15,14... | collective-permute-start | bytes 1572872 | tf_op jit(solution)/shard_map/ppermute | solution.py:41
  130.7 19.7 %collective-permute-start.23 = (bf16[32,64,128]{2,1,0:T(8,128)(2,1)}, bf16[32,64,128]{2,1,0:T(8,128)(2,1)}, u32[]{:S(2)}, u32[]{:S(2)}) collective-permute-start(bf16[32,64,128]{2,1,0:T(8,128)(2,1)} %collective-permute-done.7.refs_2_.refs_4_), channel_id=1, source_target_pairs={{0,1},{1,0},{4,5},{5,4},{8,9},{9,8},{12,13},{13,12},{14,15},{15,14... | collective-permute-start | bytes 1572872 | tf_op jit(solution)/shard_map/ppermute | solution.py:41
  141.1 12.7 %collective-permute-start.12 = (bf16[32,64,128]{2,1,0:T(8,128)(2,1)}, bf16[32,64,128]{2,1,0:T(8,128)(2,1)}, u32[]{:S(2)}, u32[]{:S(2)}) collective-permute-start(bf16[32,64,128]{2,1,0:T(8,128)(2,1)} %broadcast_select_fusion.1), channel_id=1, source_target_pairs={{0,4},{1,3},{4,8},{5,1},{8,12},{9,5},{12,14},{13,9},{14,10},{15,13... | collective-permute-start | bytes 1572872 | tf_op jit(solution)/shard_map/ppermute | solution.py:41
  141.7 12.2 %collective-permute-start.26 = (bf16[32,64,128]{2,1,0:T(8,128)(2,1)}, bf16[32,64,128]{2,1,0:T(8,128)(2,1)}, u32[]{:S(2)}, u32[]{:S(2)}) collective-permute-start(bf16[32,64,128]{2,1,0:T(8,128)(2,1)} %collective-permute-done.10.refs_6_.refs_10_), channel_id=1, source_target_pairs={{0,1},{1,0},{4,5},{5,4},{8,9},{9,8},{12,13},{13,12},{14,15},{15,14... | collective-permute-start | bytes 1572872 | tf_op jit(solution)/shard_map/ppermute | solution.py:41
  150.4 25.4 %collective-permute-start.17 = (bf16[32,64,128]{2,1,0:T(8,128)(2,1)S(1)}, bf16[32,64,128]{2,1,0:T(8,128)(2,1)}, u32[]{:S(2)}, u32[]{:S(2)}) collective-permute-start(bf16[32,64,128]{2,1,0:T(8,128)(2,1)S(1)} %collective-permute-done.8.refs_2_.refs_4_), channel_id=1, source_target_pairs={{0,1},{1,0},{4,5},{5,4},{8,9},{9,8},{12,13},{13,12},{14,15},{15,14... | collective-permute-start | bytes 1572872 | tf_op jit(solution)/shard_map/ppermute | solution.py:41
  150.4 25.4 %collective-permute-start.20 = (bf16[32,64,128]{2,1,0:T(8,128)(2,1)}, bf16[32,64,128]{2,1,0:T(8,128)(2,1)}, u32[]{:S(2)}, u32[]{:S(2)}) collective-permute-start(bf16[32,64,128]{2,1,0:T(8,128)(2,1)} %collective-permute-done.11.refs_6_.refs_10_), channel_id=1, source_target_pairs={{0,1},{1,0},{4,5},{5,4},{8,9},{9,8},{12,13},{13,12},{14,15},{15,14... | collective-permute-start | bytes 1572872 | tf_op jit(solution)/shard_map/ppermute | solution.py:41
  153.8 27.0 %collective-permute-start.13 = (bf16[32,64,128]{2,1,0:T(8,128)(2,1)}, bf16[32,64,128]{2,1,0:T(8,128)(2,1)S(1)}, u32[]{:S(2)}, u32[]{:S(2)}) collective-permute-start(bf16[32,64,128]{2,1,0:T(8,128)(2,1)} %collective-permute-done.12.refs_2_.refs_4_), channel_id=1, source_target_pairs={{0,1},{1,0},{4,5},{5,4},{8,9},{9,8},{12,13},{13,12},{14,15},{15,14... | collective-permute-start | bytes 1572872 | tf_op jit(solution)/shard_map/ppermute | solution.py:41
  153.9 26.8 %collective-permute-start.4 = (bf16[2,8,64,128]{3,2,1,0:T(8,128)(2,1)}, bf16[2,8,64,128]{3,2,1,0:T(8,128)(2,1)S(1)}, u32[]{:S(2)}, u32[]{:S(2)}) collective-permute-start(bf16[2,8,64,128]{3,2,1,0:T(8,128)(2,1)} %bitcast.90), channel_id=1, source_target_pairs={{0,14},{1,15},{4,10},{5,11},{8,6},{9,7},{12,2},{13,3},{14,0},{15,1... | collective-permute-start | bytes 786440 | tf_op jit(solution)/shard_map/ppermute | solution.py:41
  154.4 26.4 %collective-permute-start.5 = (bf16[2,8,64,128]{3,2,1,0:T(8,128)(2,1)}, bf16[2,8,64,128]{3,2,1,0:T(8,128)(2,1)S(1)}, u32[]{:S(2)}, u32[]{:S(2)}) collective-permute-start(bf16[2,8,64,128]{3,2,1,0:T(8,128)(2,1)} %bitcast.91), channel_id=1, source_target_pairs={{0,15},{1,14},{4,11},{5,10},{8,7},{9,6},{12,3},{13,2},{14,1},{15,0... | collective-permute-start | bytes 786440 | tf_op jit(solution)/shard_map/ppermute | solution.py:41
  185.0 14.4 %collective-permute-start.38 = (bf16[32,64,128]{2,1,0:T(8,128)(2,1)S(1)}, bf16[32,64,128]{2,1,0:T(8,128)(2,1)S(1)}, u32[]{:S(2)}, u32[]{:S(2)}) collective-permute-start(bf16[32,64,128]{2,1,0:T(8,128)(2,1)S(1)} %get-tuple-element.5.refs_2_), channel_id=1, source_target_pairs={{0,4},{1,5},{4,8},{5,9},{8,12},{9,13},{12,14},{13,15},{14,10},{15,... | collective-permute-start | bytes 1572872 | tf_op jit(solution)/shard_map/ppermute | solution.py:41
  185.1 14.4 %collective-permute-start.41 = (bf16[32,64,128]{2,1,0:T(8,128)(2,1)S(1)}, bf16[32,64,128]{2,1,0:T(8,128)(2,1)S(1)}, u32[]{:S(2)}, u32[]{:S(2)}) collective-permute-start(bf16[32,64,128]{2,1,0:T(8,128)(2,1)S(1)} %get-tuple-element.5.refs_2_), channel_id=1, source_target_pairs={{0,2},{1,3},{4,0},{5,1},{8,4},{9,5},{12,8},{13,9},{14,12},{15,13},... | collective-permute-start | bytes 1572872 | tf_op jit(solution)/shard_map/ppermute | solution.py:41
  199.4 13.7 %collective-permute-start.39 = (bf16[32,64,128]{2,1,0:T(8,128)(2,1)S(1)}, bf16[32,64,128]{2,1,0:T(8,128)(2,1)}, u32[]{:S(2)}, u32[]{:S(2)}) collective-permute-start(bf16[32,64,128]{2,1,0:T(8,128)(2,1)S(1)} %collective-permute-done.38.refs_2_), channel_id=1, source_target_pairs={{0,4},{1,5},{4,8},{5,9},{8,12},{9,13},{12,14},{13,15},{14,10},{15,... | collective-permute-start | bytes 1572872 | tf_op jit(solution)/shard_map/ppermute | solution.py:41
  199.5 14.0 %collective-permute-start.42 = (bf16[32,64,128]{2,1,0:T(8,128)(2,1)S(1)}, bf16[32,64,128]{2,1,0:T(8,128)(2,1)}, u32[]{:S(2)}, u32[]{:S(2)}) collective-permute-start(bf16[32,64,128]{2,1,0:T(8,128)(2,1)S(1)} %collective-permute-done.41.refs_8_), channel_id=1, source_target_pairs={{0,2},{1,3},{4,0},{5,1},{8,4},{9,5},{12,8},{13,9},{14,12},{15,13},... | collective-permute-start | bytes 1572872 | tf_op jit(solution)/shard_map/ppermute | solution.py:41
  213.2 13.0 %collective-permute-start.40 = (bf16[32,64,128]{2,1,0:T(8,128)(2,1)}, bf16[32,64,128]{2,1,0:T(8,128)(2,1)}, u32[]{:S(2)}, u32[]{:S(2)}) collective-permute-start(bf16[32,64,128]{2,1,0:T(8,128)(2,1)} %collective-permute-done.39.refs_2_), channel_id=1, source_target_pairs={{0,4},{1,5},{4,8},{5,9},{8,12},{9,13},{12,14},{13,15},{14,10},{15,... | collective-permute-start | bytes 1572872 | tf_op jit(solution)/shard_map/ppermute | solution.py:41
  213.4 13.1 %collective-permute-start.43 = (bf16[32,64,128]{2,1,0:T(8,128)(2,1)}, bf16[32,64,128]{2,1,0:T(8,128)(2,1)}, u32[]{:S(2)}, u32[]{:S(2)}) collective-permute-start(bf16[32,64,128]{2,1,0:T(8,128)(2,1)} %collective-permute-done.42.refs_8_), channel_id=1, source_target_pairs={{0,2},{1,3},{4,0},{5,1},{8,4},{9,5},{12,8},{13,9},{14,12},{15,13},... | collective-permute-start | bytes 1572872 | tf_op jit(solution)/shard_map/ppermute | solution.py:41
  215.2 31.0 %collective-permute-start.52 = (bf16[32,64,128]{2,1,0:T(8,128)(2,1)S(1)}, bf16[32,64,128]{2,1,0:T(8,128)(2,1)S(1)}, u32[]{:S(2)}, u32[]{:S(2)}) collective-permute-start(bf16[32,64,128]{2,1,0:T(8,128)(2,1)S(1)} %get-tuple-element.5.refs_2_), channel_id=1, source_target_pairs={{0,1},{1,0},{4,5},{5,4},{8,9},{9,8},{12,13},{13,12},{14,15},{15,14... | collective-permute-start | bytes 1572872 | tf_op jit(solution)/shard_map/ppermute | solution.py:41
  216.0 31.5 %collective-permute-start.50 = (bf16[32,64,128]{2,1,0:T(8,128)(2,1)S(1)}, bf16[32,64,128]{2,1,0:T(8,128)(2,1)S(1)}, u32[]{:S(2)}, u32[]{:S(2)}) collective-permute-start(bf16[32,64,128]{2,1,0:T(8,128)(2,1)S(1)} %collective-permute-done.38.refs_2_), channel_id=1, source_target_pairs={{0,1},{1,0},{4,5},{5,4},{8,9},{9,8},{12,13},{13,12},{14,15},{15,14... | collective-permute-start | bytes 1572872 | tf_op jit(solution)/shard_map/ppermute | solution.py:41
  217.3 31.0 %collective-permute-start.51 = (bf16[32,64,128]{2,1,0:T(8,128)(2,1)S(1)}, bf16[32,64,128]{2,1,0:T(8,128)(2,1)S(1)}, u32[]{:S(2)}, u32[]{:S(2)}) collective-permute-start(bf16[32,64,128]{2,1,0:T(8,128)(2,1)S(1)} %collective-permute-done.41.refs_8_), channel_id=1, source_target_pairs={{0,1},{1,0},{4,5},{5,4},{8,9},{9,8},{12,13},{13,12},{14,15},{15,14... | collective-permute-start | bytes 1572872 | tf_op jit(solution)/shard_map/ppermute | solution.py:41
  228.4 23.2 %collective-permute-start.44 = (bf16[32,64,128]{2,1,0:T(8,128)(2,1)}, bf16[32,64,128]{2,1,0:T(8,128)(2,1)}, u32[]{:S(2)}, u32[]{:S(2)}) collective-permute-start(bf16[32,64,128]{2,1,0:T(8,128)(2,1)} %broadcast_select_fusion), channel_id=1, source_target_pairs={{0,4},{1,3},{4,8},{5,1},{8,12},{9,5},{12,14},{13,9},{14,10},{15,13... | collective-permute-start | bytes 1572872 | tf_op jit(solution)/shard_map/ppermute | solution.py:41
  229.9 8.1 %collective-permute-start.35 = (f32[16,128]{1,0:T(8,128)S(1)}, f32[16,128]{1,0:T(8,128)S(1)}, u32[]{:S(2)}, u32[]{:S(2)}) collective-permute-start(f32[16,128]{1,0:T(8,128)S(1)} %add.1111), channel_id=1, source_target_pairs={{0,2},{1,3},{2,0},{3,1},{4,6},{5,7},{6,4},{7,5},{8,10},{9,11},{10,... | collective-permute-start | bytes 24584 | tf_op jit(solution)/shard_map/ppermute | solution.py:65
  246.2 32.6 %collective-permute-start.48 = (bf16[32,64,128]{2,1,0:T(8,128)(2,1)}, bf16[32,64,128]{2,1,0:T(8,128)(2,1)}, u32[]{:S(2)}, u32[]{:S(2)}) collective-permute-start(bf16[32,64,128]{2,1,0:T(8,128)(2,1)} %collective-permute-done.39.refs_2_), channel_id=1, source_target_pairs={{0,1},{1,0},{4,5},{5,4},{8,9},{9,8},{12,13},{13,12},{14,15},{15,14... | collective-permute-start | bytes 1572872 | tf_op jit(solution)/shard_map/ppermute | solution.py:41
  247.0 31.8 %collective-permute-start.49 = (bf16[32,64,128]{2,1,0:T(8,128)(2,1)}, bf16[32,64,128]{2,1,0:T(8,128)(2,1)}, u32[]{:S(2)}, u32[]{:S(2)}) collective-permute-start(bf16[32,64,128]{2,1,0:T(8,128)(2,1)} %collective-permute-done.42.refs_8_), channel_id=1, source_target_pairs={{0,1},{1,0},{4,5},{5,4},{8,9},{9,8},{12,13},{13,12},{14,15},{15,14... | collective-permute-start | bytes 1572872 | tf_op jit(solution)/shard_map/ppermute | solution.py:41
  248.3 36.9 %collective-permute-start.46 = (bf16[32,64,128]{2,1,0:T(8,128)(2,1)}, bf16[32,64,128]{2,1,0:T(8,128)(2,1)}, u32[]{:S(2)}, u32[]{:S(2)}) collective-permute-start(bf16[32,64,128]{2,1,0:T(8,128)(2,1)} %collective-permute-done.40.refs_2_), channel_id=1, source_target_pairs={{0,1},{1,0},{4,5},{5,4},{8,9},{9,8},{12,13},{13,12},{14,15},{15,14... | collective-permute-start | bytes 1572872 | tf_op jit(solution)/shard_map/ppermute | solution.py:41
  249.2 36.1 %collective-permute-start.47 = (bf16[32,64,128]{2,1,0:T(8,128)(2,1)}, bf16[32,64,128]{2,1,0:T(8,128)(2,1)}, u32[]{:S(2)}, u32[]{:S(2)}) collective-permute-start(bf16[32,64,128]{2,1,0:T(8,128)(2,1)} %collective-permute-done.43.refs_8_), channel_id=1, source_target_pairs={{0,1},{1,0},{4,5},{5,4},{8,9},{9,8},{12,13},{13,12},{14,15},{15,14... | collective-permute-start | bytes 1572872 | tf_op jit(solution)/shard_map/ppermute | solution.py:41
  251.6 39.8 %collective-permute-start.45 = (bf16[32,64,128]{2,1,0:T(8,128)(2,1)}, bf16[32,64,128]{2,1,0:T(8,128)(2,1)}, u32[]{:S(2)}, u32[]{:S(2)}) collective-permute-start(bf16[32,64,128]{2,1,0:T(8,128)(2,1)} %collective-permute-done.44.refs_2_), channel_id=1, source_target_pairs={{0,1},{1,0},{4,5},{5,4},{8,9},{9,8},{12,13},{13,12},{14,15},{15,14... | collective-permute-start | bytes 1572872 | tf_op jit(solution)/shard_map/ppermute | solution.py:41
  (44 other events, 354.7 us)

commit v3 on v1

--- a/solution.py
+++ b/solution.py
@@ -8,6 +8,358 @@
 from jax.sharding import PartitionSpec as P
 
 BOTH = ("sec", "term")
+VMEM_LIMIT = 32 * 2**20
+RING_BYTES = 24 * 2**20
+
+
+def ring_order(owners):
+    if owners % 2:
+        return list(range(owners))
+    return list(range(0, owners, 2)) + list(range(owners - 1, 0, -2))
+
+
+def ring_place(owner, owners):
+    if owners % 2:
+        return owner
+    return jnp.where(owner % 2 == 0, owner // 2, owners - 1 - owner // 2)
+
+
+def ring_owner(place, owners):
+    place = place % owners
+    if owners % 2:
+        return place
+    return jnp.where(place < owners // 2, 2 * place, 2 * (owners - 1 - place) + 1)
+
+
+def permute(value, owners, halves, target, flip=0):
+    pairs = [
+        (chip * halves + half, target(chip, half) * halves + (half ^ flip))
+        for chip in range(owners)
+        for half in range(halves)
+    ]
+    return lax.ppermute(value, BOTH, pairs)
+
+
+def swap(value, owners, halves):
+    return permute(value, owners, halves, lambda chip, half: chip, 1)
+
+
+def exchange(value, owners, halves, mask):
+    return permute(value, owners, halves, lambda chip, half: chip ^ mask)
+
+
+def ring_send(value, owners, halves, shifts):
+    ring = ring_order(owners)
+    place = {chip: index for index, chip in enumerate(ring)}
+    return permute(
+        value, owners, halves, lambda chip, half: ring[(place[chip] + shifts[half]) % owners]
+    )
+
+
+def ring_gather(unit, owners, halves, half):
+    units = {0: unit}
+    reach = (owners - 1) // 2
+    for step in range(1, reach + 1):
+        units[step] = ring_send(units[step - 1], owners, halves, (1,) * halves)
+        units[-step] = ring_send(units[1 - step], owners, halves, (-1,) * halves)
+    if owners % 2 == 0:
+        last = jnp.where(half == 0, units[reach], units[-reach])
+        units[owners // 2] = ring_send(last, owners, halves, (1, -1))
+    return units
+
+
+def mask_gather(unit, owners, halves):
+    units = {0: unit}
+    step = owners // 2
+    while step:
+        for mask in list(units):
+            units[mask | step] = exchange(units[mask], owners, halves, step)
+        step //= 2
+    return units
+
+
+def doubled(value, count, axes, stride):
+    step = 1
+    total = lax.axis_size("sec") * lax.axis_size("term")
+    while step < count:
+        value = value + lax.ppermute(
+            value, axes, [(d, d ^ (step * stride)) for d in range(total)]
+        )
+        step *= 2
+    return value
+
+
+def pack_kernel(capacity, blocks, terms, ids_ref, plan_ref, left_ref, other_ref, *refs):
+    pieces, codes, seen = refs[:-2], refs[-2], refs[-1]
+    owners = len(pieces)
+    me, half = ids_ref[0], ids_ref[1]
+    rows = other_ref.shape[2]
+    start = pl.multiple_of(half * rows, rows)
+
+    @pl.loop(0, owners)
+    def _(owner):
+        for index in range(2 * terms * capacity):
+            codes[owner, index] = blocks
+
+    for stream in range(2 * terms):
+
+        @pl.loop(0, owners)
+        def _(owner):
+            seen[owner] = 0
+
+        @pl.loop(0, blocks)
+        def _(block):
+            plan = plan_ref[stream, block]
+            owner, target = lax.div(plan, blocks), lax.rem(plan, blocks)
+            slot = seen[owner]
+            seen[owner] = slot + 1
+            codes[owner, stream * capacity + slot] = block * (2 * blocks) + target
+
+    for mask, piece in enumerate(pieces):
+        owner = me ^ mask
+        for stream in range(2 * terms):
+
+            @pl.loop(0, capacity, unroll=True)
+            def _(slot):
+                block = lax.div(codes[owner, stream * capacity + slot], 2 * blocks)
+                if stream < terms:
+                    value = left_ref[stream, block, pl.ds(start, rows), :]
+                else:
+                    value = other_ref[stream - terms, block]
+                value = pltpu.roll(value.astype(jnp.float32), half * rows, 1)
+                piece[stream, slot] = value.astype(jnp.bfloat16)
+
+
+def pack(ids, plan, left, other, owners, capacity):
+    terms, blocks, rows, width = other.shape
+    scalars = pl.BlockSpec(memory_space=pltpu.SMEM)
+    whole = pl.BlockSpec(memory_space=pltpu.VMEM)
+    piece = jax.ShapeDtypeStruct((2 * terms, capacity, rows, width), jnp.bfloat16)
+    *pieces, codes = pl.pallas_call(
+        functools.partial(pack_kernel, capacity, blocks, terms),
+        out_shape=[piece] * owners
+        + [jax.ShapeDtypeStruct((owners, 2 * terms * capacity), jnp.int32)],
+        in_specs=[scalars, scalars, whole, whole],
+        out_specs=[whole] * owners + [scalars],
+        scratch_shapes=[pltpu.SMEM((owners,), jnp.int32)],
+        compiler_params=pltpu.CompilerParams(vmem_limit_bytes=VMEM_LIMIT),
+    )(ids, plan, left, other)
+    return pieces, codes
+
+
+def add_products(piece, near, far, rights, total, code_of, blocks):
+    streams, capacity = piece.shape[:2]
+    terms = streams // 2
+    for side in range(2):
+        moved, where = [], []
+        for stream in range(terms * side, terms * side + terms):
+            for slot in range(capacity):
+                code = code_of(stream * capacity + slot)
+                source, target = lax.div(code, 2 * blocks), lax.rem(code, 2 * blocks)
+                block = jnp.concatenate([near[source], far[source]], axis=0)
+                product = jnp.dot(piece[stream, slot], block, preferred_element_type=jnp.float32)
+                moved.append(product.astype(jnp.bfloat16))
+                where.append((stream - terms * side, target))
+        for value, (term, target) in zip(moved, where):
+            total[target] += jnp.dot(
+                value,
+                rights[side][term, jnp.minimum(target, blocks - 1)],
+                preferred_element_type=jnp.float32,
+            )
+
+
+def apply_kernel(sources, first, choices, last, blocks, ids_ref, codes_ref, *refs):
+    refs = list(refs)
+    lefts = [refs.pop(0) for _ in range(choices or sources)]
+    vectors = [(refs.pop(0), refs.pop(0)) for _ in range(sources)]
+    rights = refs.pop(0), refs.pop(0)
+    total_in = None if first else refs.pop(0)
+    out = refs.pop(0) if last else None
+    total = refs.pop(0)
+    chosen = refs.pop(0) if choices else None
+
+    total[...] = jnp.zeros_like(total) if first else total_in[...]
+    for index, (near, far) in enumerate(vectors):
+        chip = ids_ref[2 * index]
+        if choices:
+            for choice, left in enumerate(lefts):
+
+                @pl.when(ids_ref[2 * index + 1] == choice)
+                def _():
+                    chosen[...] = left[...]
+
+            piece = chosen
+        else:
+            piece = lefts[index]
+        add_products(piece, near, far, rights, total, lambda at: codes_ref[chip, at], blocks)
+    if last:
+        out[...] = total[:blocks].astype(out.dtype)
+
+
+def apply_group(ids, codes, lefts, vectors, rights, total, choices, last):
+    streams, capacity, rows, width = lefts[0].shape
+    blocks = rights[0].shape[1]
+    first = total is None
+    arrays = list(lefts) + [unit for pair in vectors for unit in pair] + list(rights)
+    if not first:
+        arrays.append(total)
+    scalars = pl.BlockSpec(memory_space=pltpu.SMEM)
+    whole = pl.BlockSpec(memory_space=pltpu.VMEM)
+    total_shape = (blocks + 1, rows, width)
+    scratch = [pltpu.VMEM(lefts[0].shape, lefts[0].dtype)] if choices else []
+    aliases = {}
+    if last:
+        out_shape = jax.ShapeDtypeStruct((blocks, rows, width), jnp.bfloat16)
+        scratch = [pltpu.VMEM(total_shape, jnp.float32)] + scratch
+    else:
+        out_shape = jax.ShapeDtypeStruct(total_shape, jnp.float32)
+        if not first:
+            aliases = {len(arrays) + 1: 0}
+    return pl.pallas_call(
+        functools.partial(
+            apply_kernel, len(vectors), first, len(lefts) if choices else 0, last, blocks
+        ),
+        out_shape=out_shape,
+        in_specs=[scalars] * 2 + [whole] * len(arrays),
+        out_specs=whole,
+        scratch_shapes=scratch,
+        input_output_aliases=aliases,
+        compiler_params=pltpu.CompilerParams(vmem_limit_bytes=VMEM_LIMIT),
+        cost_estimate=pl.CostEstimate(
+            flops=len(vectors) * streams * capacity * 2 * 2 * rows * width * width,
+            bytes_accessed=2 * len(vectors) * (streams * capacity + 2 * blocks) * rows * width,
+            transcendentals=0,
+        ),
+    )(ids, codes, *arrays)
+
+
+def stats_kernel(ids_ref, total_ref, wave_ref, stats_ref):
+    blocks = wave_ref.shape[0]
+    zero = jnp.zeros(wave_ref.shape[1:], jnp.float32)
+
+    def sums(block, carry):
+        cross, own = carry
+        wave = wave_ref[block].astype(jnp.float32)
+        return cross + wave * total_ref[block], own + wave * wave
+
+    cross, own = lax.fori_loop(0, blocks, sums, (zero, zero), unroll=4)
+    cross, own = jnp.sum(cross, keepdims=True), jnp.sum(own, keepdims=True)
+    local = jnp.where(own > 0, cross / own, 0.0)
+
+    def squares(block, carry):
+        rest = total_ref[block] - local * wave_ref[block].astype(jnp.float32)
+        return carry + rest * rest
+
+    about = jnp.sum(lax.fori_loop(0, blocks, squares, zero, unroll=4), keepdims=True)
+    lane = lax.broadcasted_iota(jnp.int32, stats_ref.shape, 1)
+    row = lax.broadcasted_iota(jnp.int32, stats_ref.shape, 0)
+    values = jnp.where(lane == 0, about, jnp.where(lane == 1, cross, jnp.where(lane == 2, own, local)))
+    stats_ref[...] = jnp.where((row == ids_ref[2]) & (lane < 4), values, 0.0)
+
+
+def direction_kernel(entries, total_ref, wave_ref, stats_ref, out_ref, rayleigh_ref):
+    blocks = wave_ref.shape[0]
+    stats = stats_ref[...]
+    about, cross, own, local = (stats[:, lane : lane + 1] for lane in range(4))
+    rayleigh = jnp.sum(cross, keepdims=True) / jnp.sum(own, keepdims=True)
+    offset = local - rayleigh
+    residual_sq = jnp.sum(about + offset * offset * own, keepdims=True)
+    factor = lax.rsqrt(residual_sq / entries + 1e-06)
+    rayleigh_ref[...] = rayleigh
+
+    @pl.loop(0, blocks, unroll=4)
+    def _(block):
+        rest = total_ref[block] - rayleigh * wave_ref[block].astype(jnp.float32)
+        out_ref[block] = (rest * factor).astype(jnp.bfloat16)
+
+
+def new_direction(ids, total, wave, owners, halves, entries):
+    devices = owners * halves
+    scalars = pl.BlockSpec(memory_space=pltpu.SMEM)
+    whole = pl.BlockSpec(memory_space=pltpu.VMEM)
+    params = pltpu.CompilerParams(vmem_limit_bytes=VMEM_LIMIT)
+    stats = pl.pallas_call(
+        stats_kernel,
+        out_shape=jax.ShapeDtypeStruct((devices, 128), jnp.float32),
+        in_specs=[scalars, whole, whole],
+        out_specs=whole,
+        compiler_params=params,
+    )(ids, total, wave)
+    stats = doubled(stats, devices, BOTH, 1)
+    return pl.pallas_call(
+        functools.partial(direction_kernel, entries),
+        out_shape=(
+            jax.ShapeDtypeStruct(wave.shape, jnp.bfloat16),
+            jax.ShapeDtypeStruct((1, 1), jnp.float32),
+        ),
+        in_specs=[whole] * 3,
+        out_specs=(whole, whole),
+        compiler_params=params,
+    )(total, wave, stats)
+
+
+def per_device_ring(wavefunction, left_operator, right_operator, target_owner, target_local):
+    owners, halves = lax.axis_size("sec"), lax.axis_size("term")
+    me, half = lax.axis_index("sec"), lax.axis_index("term")
+    terms, blocks, height, width = left_operator.shape
+    rows = height // halves
+    capacity = 2 * blocks // owners
+    place = ring_place(me, owners)
+    ids = jnp.stack([me, half, me * halves + half]).astype(jnp.int32)
+
+    own_rows = lax.dynamic_slice_in_dim(wavefunction, half * rows, rows, 1)
+    other_rows = lax.dynamic_slice_in_dim(wavefunction, (1 - half) * rows, rows, 1)
+    near = mask_gather(own_rows, owners, halves)
+    far = {m: swap(unit, owners, halves) if m else other_rows for m, unit in near.items()}
+
+    plan = target_owner[:, :, 0] * blocks + target_local
+    plan = jnp.concatenate([plan, swap(plan, owners, halves)], axis=0)
+    other_left = swap(
+        lax.dynamic_slice_in_dim(left_operator, (1 - half) * rows, rows, 2), owners, halves
+    )
+    pieces, codes = pack(ids, plan, left_operator, other_left, owners, capacity)
+    lefts = [exchange(piece, owners, halves, m) if m else piece for m, piece in enumerate(pieces)]
+    codes = jnp.where(jnp.arange(owners)[:, None] == me, codes.reshape(1, -1), 0)
+    codes = doubled(codes, owners, BOTH, halves).reshape(owners, owners, -1)
+    codes = lax.dynamic_index_in_dim(codes, me, axis=1, keepdims=False)
+    rights = (right_operator, swap(right_operator, owners, halves))
+
+    order = [m for pair in zip(range(owners // 2), range(owners // 2, owners)) for m in pair]
+    total = None
+    for m in order:
+        total = apply_group(
+            jnp.stack([me ^ m, 0]).astype(jnp.int32),
+            codes,
+            [lefts[m]],
+            [(near[m], far[m])],
+            rights,
+            total,
+            False,
+            False,
+        )
+
+    entries = blocks * owners * height * width
+    direction, rayleigh = new_direction(ids, total, own_rows, owners, halves, entries)
+    near = ring_gather(direction, owners, halves, half)
+    far = {s: swap(unit, owners, halves) for s, unit in near.items()}
+    reach = (owners - 1) // 2
+    groups = [[0]] + [[step, -step] for step in range(1, reach + 1)]
+    if owners % 2 == 0:
+        groups.append([owners // 2])
+    total = None
+    for group in groups:
+        chips = [ring_owner(place - s, owners) for s in group]
+        total = apply_group(
+            jnp.stack([value for chip in chips for value in (chip, chip ^ me)]).astype(jnp.int32),
+            codes,
+            lefts,
+            [(near[s], far[s]) for s in group],
+            rights,
+            total,
+            True,
+            group is groups[-1],
+        )
+    return (total, rayleigh[0])
 
 
 def slot_codes(target_owner, target_local, owners, capacity):
@@ -23,7 +375,7 @@
     return blocks + jnp.sum(jnp.where(hit, code[:, None, None, :], 0), axis=3)
 
 
-def apply_kernel(first, capacity, blocks, code_ref, left_ref, vector_ref, right_ref, *rest):
+def stream_kernel(first, capacity, blocks, code_ref, left_ref, vector_ref, right_ref, *rest):
     total_in, total = (None, rest[0]) if first else rest
     step = pl.program_id(0)
     rows, width = left_ref.shape[2:]
@@ -50,13 +402,13 @@
             )
 
 
-def apply_chunk(total, codes, left, vector, right):
+def stream_chunk(total, codes, left, vector, right):
     owners, _, blocks, rows, width = vector.shape
     capacity = left.shape[1]
     first = total is None
     spec_total = pl.BlockSpec((blocks + 1, rows, width), lambda s, c: (0, 0, 0))
     return pl.pallas_call(
-        functools.partial(apply_kernel, first, capacity, blocks),
+        functools.partial(stream_kernel, first, capacity, blocks),
         out_shape=jax.ShapeDtypeStruct((blocks + 1, rows, width), jnp.float32),
         grid_spec=pltpu.PrefetchScalarGridSpec(
             num_scalar_prefetch=1,
@@ -78,7 +430,7 @@
     )(codes, left, vector, right, *([] if first else [total]))
 
 
-def per_device(wavefunction, left_operator, right_operator, target_owner, target_local):
+def per_device_streamed(wavefunction, left_operator, right_operator, target_owner, target_local):
     owners = lax.axis_size("sec")
     halves = lax.axis_size("term")
     me, half = lax.axis_index("sec"), lax.axis_index("term")
@@ -104,7 +456,7 @@
     def apply(vector):
         total = None
         for k in range(terms):
-            total = apply_chunk(total, my_codes[:, k], moved_left[k], vector, right[k])
+            total = stream_chunk(total, my_codes[:, k], moved_left[k], vector, right[k])
         return total[:blocks]
 
     sigma_rows = apply(gathered)
@@ -121,6 +473,13 @@
     direction = lax.all_gather(direction, BOTH, axis=0).reshape(gathered.shape)
     sigma_two = apply(direction).astype(jnp.bfloat16)
     return (sigma_two, jnp.reshape(rayleigh, (1,)))
+
+
+def per_device(wavefunction, *operands):
+    gathered_bytes = lax.axis_size("sec") * wavefunction.size * wavefunction.dtype.itemsize
+    if 2 * gathered_bytes > RING_BYTES:
+        return per_device_streamed(wavefunction, *operands)
+    return per_device_ring(wavefunction, *operands)
 
 
 def solution(mesh):

time: 348 us -> 252 us (0.72)
  blocking collectives: 113 us -> 0 us
  Pallas kernels: 20.4 us -> 53.1 us
  local copies, waits for them, and re-layouts: 35.7 us -> 14.7 us
  starting transfers between devices: 22.5 us -> 43.1 us
  between operations: 19.7 us -> 1 us
  waiting for transfers between devices: 127 us -> 137 us
  other arithmetic: 8.91 us -> 3.21 us
    ppermute x0 -> x46, waiting for transfers between devices: none -> 137 us  [the longest x39 92.7 us: permute(): return lax.ppermute(value, BOTH, pairs)]
    all_gather x1 -> x0, blocking collectives: 73.2 us -> none  [per_device(): all_codes = lax.all_gather(codes, BOTH, axis=0)]
    all_gather x3 -> x0, waiting for transfers between devices: 72.3 us -> none  [the longest x1 72.3 us: per_device(): direction = lax.all_gather(direction, BOTH, axis=0).reshape(gathered.shape)]
    all_to_all x2 -> x0, waiting for transfers between devices: 54.4 us -> none  [per_device(): lax.all_to_all(pieces, BOTH, split_axis=0, concat_axis=0, tiled=True)]
    ppermute x0 -> x46, starting transfers between devices: none -> 43.1 us  [the longest x39 32.7 us: permute(): return lax.ppermute(value, BOTH, pairs)]
    unnamed x1 -> x0, blocking collectives: 39.6 us -> none
    pallas_call x4 -> x16, Pallas kernels: 20.4 us -> 53.1 us  [the longest x13 45.5 us: apply_group(): pl.pallas_call(functools.partial(apply_kernel, len(vectors), first, len(l...]
    all_to_all x2 -> x0, starting transfers between devices: 22.3 us -> none  [per_device(): lax.all_to_all(pieces, BOTH, split_axis=0, concat_axis=0, tiled=True)]
  transfers between devices with their start and end apart: 5 -> 46, of which waited for: 2 -> 18; matrix products, arithmetic and copies ran while one was open for 4% -> 2% of each run, Pallas kernels for 1% -> 17%
where the time goes in v3:
time: 252 us
  waiting for transfers between devices  137 us (54%)
  Pallas kernels  53.1 us (21%)
  starting transfers between devices  43.1 us (17%)
  local copies, waits for them, and re-layouts  14.7 us (6%)
  other arithmetic  3.21 us (1%)
    ppermute x39, waiting for transfers between devices, permute(): return lax.ppermute(value, BOTH, pairs)  92.7 us
    pallas_call x13, Pallas kernels, apply_group(): pl.pallas_call(functools.partial(apply_kernel, len(vectors), first, len(l...  45.5 us
    ppermute x7, waiting for transfers between devices, doubled(): lax.ppermute(value, axes, [(d, d ^ step * stride) for d in range(total)])  43.9 us
    ppermute x39, starting transfers between devices, permute(): return lax.ppermute(value, BOTH, pairs)  32.7 us
    unnamed x48, local copies, waits for them, and re-layouts  11.2 us
    ppermute x7, starting transfers between devices, doubled(): lax.ppermute(value, axes, [(d, d ^ step * stride) for d in range(total)])  10.4 us
    pallas_call x1, Pallas kernels, pack(): pl.pallas_call(functools.partial(pack_kernel, capacity, blocks, terms), o...  5.29 us
  transfers between devices with their start and end apart: 46, of which 18 were waited for; matrix products, arithmetic and copies ran while one was open for 2% of the time, Pallas kernels for 17%

profile of v3, /device:TPU:0, one launch (start us, length us, event | category | flops | bytes accessed | tf_op | source)
XLA Modules:
  0.0 251.7 jit_solution(6525679080796568233)
XLA Ops:
  0.6 2.2 constant_dynamic-slice_fusion
  2.9 4.1 %collective-permute-start.12 = (bf16[32,64,128]{2,1,0:T(8,128)(2,1)S(1)}, bf16[32,64,128]{2,1,0:T(8,128)(2,1)}, u32[]{:S(2)}, u32[]{:S(2)}) collective-permute-start(bf16[32,64,128]{2,1,0:T(8,128)(2,1)S(1)} %get-tuple-element.25.refs_1_.wave_ref), channel_id=1, source_target_pairs={{0,8},{1,9},{2,10},{3,11},{4,12},{5,13},{6,14},{7,15},{8,0},{9,1},... | collective-permute-start | bytes 1572872 | tf_op jit(solution)/shard_map/ppermute | solution.py:40
  8.0 1.5 collective-permute-start.24
  9.6 1.6 collective-permute-start.17
  11.1 19.2 %collective-permute-done.12.refs_1_ = bf16[32,64,128]{2,1,0:T(8,128)(2,1)} collective-permute-done((bf16[32,64,128]{2,1,0:T(8,128)(2,1)S(1)}, bf16[32,64,128]{2,1,0:T(8,128)(2,1)}, u32[]{:S(2)}, u32[]{:S(2)}) %collective-permute-start.12) | collective-permute-done | bytes 524320 | tf_op jit(solution)/shard_map/ppermute | solution.py:40
  30.9 1.3 collective-permute-done
  35.8 1.6 copy-done.5
  37.4 5.3 %shard_map.68 = (bf16[4,8,64,128]{3,2,1,0:T(8,128)(2,1)S(1)}, bf16[4,8,64,128]{3,2,1,0:T(8,128)(2,1)S(1)}, bf16[4,8,64,128]{3,2,1,0:T(8,128)(2,1)S(1)}, bf16[4,8...) custom-call(s32[3]{0:T(128)S(1)} %pad_add_fusion.10.ids_ref, ...), custom_call_target="tpu_custom_call" | custom-call | tf_op jit(solution)/shard_map/pallas_call | solution.py:138
  49.4 2.7 %collective-permute-done.2 = s32[8,256]{1,0:T(8,128)S(1)} collective-permute-done((s32[8,256]{1,0:T(8,128)S(1)}, s32[8,256]{1,0:T(8,128)S(1)}, u32[]{:S(2)}, u32[]{:S(2)}) %collective-permute-start.2) | collective-permute-done | bytes 8224 | tf_op jit(solution)/shard_map/ppermute | solution.py:85
  53.1 2.0 collective-permute-start.3
  55.1 1.2 collective-permute-start.8
  56.4 1.5 collective-permute-start.5
  57.9 3.1 %collective-permute-start.9 = (bf16[4,8,64,128]{3,2,1,0:T(8,128)(2,1)}, bf16[4,8,64,128]{3,2,1,0:T(8,128)(2,1)}, u32[]{:S(2)}, u32[]{:S(2)}) collective-permute-start(bf16[4,8,64,128]{3,2,1,0:T(8,128)(2,1)} %copy-done.19), channel_id=1, source_target_pairs={{0,10},{1,11},{2,8},{3,9},{4,14},{5,15},{6,12},{7,13},{8,2},{9,3},... | collective-permute-start | bytes 1572872 | tf_op jit(solution)/shard_map/ppermute | solution.py:40
  61.1 6.2 %collective-permute-done.18.refs_1_ = bf16[32,64,128]{2,1,0:T(8,128)(2,1)} collective-permute-done((bf16[32,64,128]{2,1,0:T(8,128)(2,1)}, bf16[32,64,128]{2,1,0:T(8,128)(2,1)}, u32[]{:S(2)}, u32[]{:S(2)}) %collective-permute-start.18) | collective-permute-done | bytes 524320 | tf_op jit(solution)/shard_map/ppermute | solution.py:40
  67.3 4.8 %collective-permute-start.4 = (s32[8,256]{1,0:T(8,128)S(1)}, s32[8,256]{1,0:T(8,128)S(1)}, u32[]{:S(2)}, u32[]{:S(2)}) collective-permute-start(s32[8,256]{1,0:T(8,128)S(1)} %fusion.1), channel_id=1, source_target_pairs={{0,8},{1,9},{2,10},{3,11},{4,12},{5,13},{6,14},{7,15},{8,0},{9,1},... | collective-permute-start | bytes 24584 | tf_op jit(solution)/shard_map/ppermute | solution.py:85
  72.1 30.8 %collective-permute-done.4 = s32[8,256]{1,0:T(8,128)S(1)} collective-permute-done((s32[8,256]{1,0:T(8,128)S(1)}, s32[8,256]{1,0:T(8,128)S(1)}, u32[]{:S(2)}, u32[]{:S(2)}) %collective-permute-start.4) | collective-permute-done | bytes 8224 | tf_op jit(solution)/shard_map/ppermute | solution.py:85
  103.0 2.5 %collective-permute-start.10 = (bf16[4,8,64,128]{3,2,1,0:T(8,128)(2,1)}, bf16[4,8,64,128]{3,2,1,0:T(8,128)(2,1)}, u32[]{:S(2)}, u32[]{:S(2)}) collective-permute-start(bf16[4,8,64,128]{3,2,1,0:T(8,128)(2,1)} %copy-done.17), channel_id=1, source_target_pairs={{0,12},{1,13},{2,14},{3,15},{4,8},{5,9},{6,10},{7,11},{8,4},{9,5},... | collective-permute-start | bytes 1572872 | tf_op jit(solution)/shard_map/ppermute | solution.py:40
  105.6 1.4 collective-permute-start.14
  107.4 10.2 %collective-permute-done.6.refs_0_.refs_2_ = bf16[4,8,64,128]{3,2,1,0:T(8,128)(2,1)} collective-permute-done((bf16[4,8,64,128]{3,2,1,0:T(8,128)(2,1)}, bf16[4,8,64,128]{3,2,1,0:T(8,128)(2,1)}, u32[]{:S(2)}, u32[]{:S(2)}) %collective-permute-start.6) | collective-permute-done | bytes 524320 | tf_op jit(solution)/shard_map/ppermute | solution.py:40
  118.5 11.2 %collective-permute-done.10.refs_0_.refs_6_ = bf16[4,8,64,128]{3,2,1,0:T(8,128)(2,1)} collective-permute-done((bf16[4,8,64,128]{3,2,1,0:T(8,128)(2,1)}, bf16[4,8,64,128]{3,2,1,0:T(8,128)(2,1)}, u32[]{:S(2)}, u32[]{:S(2)}) %collective-permute-start.10) | collective-permute-done | bytes 524320 | tf_op jit(solution)/shard_map/ppermute | solution.py:40
  129.7 2.5 collective-permute-start.11
  135.1 2.4 shard_map.69.refs_5_
  137.5 2.7 %shard_map.70.refs_5_ = f32[33,64,128]{2,1,0:T(8,128)S(1)} custom-call(s32[2]{0:T(128)S(1)} %pad_add_fusion.2.ids_ref, s32[8,32]{1,0:T(8,128)S(1)} %bitcast.30, bf16[4,8,64,128]{3,2,1,0:T(8,128)(2,1)S(1)} %collective-permute-done.8.refs_0_.refs_4_, bf16[32,64,128]{2,1,0:T(8,128)(2,1)} %collective-permute-done.12.refs_1_, ...), custom_call_target="tpu_custom_call", output_to_operand_aliasing={{}: (7, {})} | custom-call | flops 134217728 | bytes 1572864 | tf_op jit(solution)/shard_map/pallas_call | solution.py:218
  140.2 3.0 %shard_map.71.refs_5_ = f32[33,64,128]{2,1,0:T(8,128)S(1)} custom-call(s32[2]{0:T(128)S(1)} %pad_add_fusion.3.ids_ref, s32[8,32]{1,0:T(8,128)S(1)} %bitcast.31, bf16[4,8,64,128]{3,2,1,0:T(8,128)(2,1)} %collective-permute-done.5.refs_0_.refs_1_, bf16[32,64,128]{2,1,0:T(8,128)(2,1)} %collective-permute-done.24.refs_1_, ...), custom_call_target="tpu_custom_call", output_to_operand_aliasing={{}: (7, {})} | custom-call | flops 134217728 | bytes 1572864 | tf_op jit(solution)/shard_map/pallas_call | solution.py:218
  143.1 3.0 %shard_map.72.refs_5_ = f32[33,64,128]{2,1,0:T(8,128)S(1)} custom-call(s32[2]{0:T(128)S(1)} %pad_add_fusion.4.ids_ref, s32[8,32]{1,0:T(8,128)S(1)} %bitcast.32, bf16[4,8,64,128]{3,2,1,0:T(8,128)(2,1)} %collective-permute-done.9.refs_0_.refs_5_, bf16[32,64,128]{2,1,0:T(8,128)(2,1)} %collective-permute-done.22.refs_1_, ...), custom_call_target="tpu_custom_call", output_to_operand_aliasing={{}: (7, {})} | custom-call | flops 134217728 | bytes 1572864 | tf_op jit(solution)/shard_map/pallas_call | solution.py:218
  146.1 3.0 %shard_map.73.refs_5_ = f32[33,64,128]{2,1,0:T(8,128)S(1)} custom-call(s32[2]{0:T(128)S(1)} %pad_add_fusion.5.ids_ref, s32[8,32]{1,0:T(8,128)S(1)} %bitcast.33, bf16[4,8,64,128]{3,2,1,0:T(8,128)(2,1)} %collective-permute-done.6.refs_0_.refs_2_, bf16[32,64,128]{2,1,0:T(8,128)(2,1)} %collective-permute-done.17.refs_1_, ...), custom_call_target="tpu_custom_call", output_to_operand_aliasing={{}: (7, {})} | custom-call | flops 134217728 | bytes 1572864 | tf_op jit(solution)/shard_map/pallas_call | solution.py:218
  149.1 3.0 %shard_map.74.refs_5_ = f32[33,64,128]{2,1,0:T(8,128)S(1)} custom-call(s32[2]{0:T(128)S(1)} %pad_add_fusion.6.ids_ref, s32[8,32]{1,0:T(8,128)S(1)} %bitcast.34, bf16[4,8,64,128]{3,2,1,0:T(8,128)(2,1)} %collective-permute-done.10.refs_0_.refs_6_, bf16[32,64,128]{2,1,0:T(8,128)(2,1)} %collective-permute-done.13.refs_1_, ...), custom_call_target="tpu_custom_call", output_to_operand_aliasing={{}: (7, {})} | custom-call | flops 134217728 | bytes 1572864 | tf_op jit(solution)/shard_map/pallas_call | solution.py:218
  152.1 3.0 %shard_map.75.refs_5_ = f32[33,64,128]{2,1,0:T(8,128)S(1)} custom-call(s32[2]{0:T(128)S(1)} %pad_add_fusion.7.ids_ref, s32[8,32]{1,0:T(8,128)S(1)} %bitcast.35, bf16[4,8,64,128]{3,2,1,0:T(8,128)(2,1)} %collective-permute-done.7.refs_0_.refs_3_, bf16[32,64,128]{2,1,0:T(8,128)(2,1)} %collective-permute-done.18.refs_1_, ...), custom_call_target="tpu_custom_call", output_to_operand_aliasing={{}: (7, {})} | custom-call | flops 134217728 | bytes 1572864 | tf_op jit(solution)/shard_map/pallas_call | solution.py:218
  155.1 6.9 %collective-permute-done.11.refs_0_.refs_7_ = bf16[4,8,64,128]{3,2,1,0:T(8,128)(2,1)} collective-permute-done((bf16[4,8,64,128]{3,2,1,0:T(8,128)(2,1)}, bf16[4,8,64,128]{3,2,1,0:T(8,128)(2,1)}, u32[]{:S(2)}, u32[]{:S(2)}) %collective-permute-start.11) | collective-permute-done | bytes 524320 | tf_op jit(solution)/shard_map/ppermute | solution.py:40
  162.0 3.0 %shard_map.76.total_ref = f32[33,64,128]{2,1,0:T(8,128)S(1)} custom-call(s32[2]{0:T(128)S(1)} %pad_add_fusion.8.ids_ref, s32[8,32]{1,0:T(8,128)S(1)} %bitcast.36, bf16[4,8,64,128]{3,2,1,0:T(8,128)(2,1)} %collective-permute-done.11.refs_0_.refs_7_, bf16[32,64,128]{2,1,0:T(8,128)(2,1)} %collective-permute-done.14.refs_1_, ...), custom_call_target="tpu_custom_call", output_to_operand_aliasing={{}: (7, {})} | custom-call | flops 134217728 | bytes 1572864 | tf_op jit(solution)/shard_map/pallas_call | solution.py:218
  165.0 1.2 shard_map.77
  166.2 1.2 collective-permute-done.27
  167.5 3.5 %collective-permute-done.28 = f32[16,128]{1,0:T(8,128)S(1)} collective-permute-done((f32[16,128]{1,0:T(8,128)S(1)}, f32[16,128]{1,0:T(8,128)S(1)}, u32[]{:S(2)}, u32[]{:S(2)}) %collective-permute-start.28) | collective-permute-done | bytes 8224 | tf_op jit(solution)/shard_map/ppermute | solution.py:85
  172.1 2.6 %collective-permute-done.29 = f32[16,128]{1,0:T(8,128)S(1)} collective-permute-done((f32[16,128]{1,0:T(8,128)S(1)}, f32[16,128]{1,0:T(8,128)S(1)}, u32[]{:S(2)}, u32[]{:S(2)}) %collective-permute-start.29) | collective-permute-done | bytes 8224 | tf_op jit(solution)/shard_map/ppermute | solution.py:85
  174.7 1.4 collective-permute-start.30
  176.1 3.2 %collective-permute-done.30 = f32[16,128]{1,0:T(8,128)S(1)} collective-permute-done((f32[16,128]{1,0:T(8,128)S(1)}, f32[16,128]{1,0:T(8,128)S(1)}, u32[]{:S(2)}, u32[]{:S(2)}) %collective-permute-start.30) | collective-permute-done | bytes 8224 | tf_op jit(solution)/shard_map/ppermute | solution.py:85
  182.4 10.1 %collective-permute-done.31.refs_8_ = bf16[32,64,128]{2,1,0:T(8,128)(2,1)S(1)} collective-permute-done((bf16[32,64,128]{2,1,0:T(8,128)(2,1)S(1)}, bf16[32,64,128]{2,1,0:T(8,128)(2,1)S(1)}, u32[]{:S(2)}, u32[]{:S(2)}) %collective-permute-start.31) | collective-permute-done | bytes 524320 | tf_op jit(solution)/shard_map/ppermute | solution.py:40
  194.5 9.8 %collective-permute-done.32.refs_8_ = bf16[32,64,128]{2,1,0:T(8,128)(2,1)} collective-permute-done((bf16[32,64,128]{2,1,0:T(8,128)(2,1)S(1)}, bf16[32,64,128]{2,1,0:T(8,128)(2,1)}, u32[]{:S(2)}, u32[]{:S(2)}) %collective-permute-start.32) | collective-permute-done | bytes 524320 | tf_op jit(solution)/shard_map/ppermute | solution.py:40
  204.3 1.1 collective-permute-start.33
  206.9 7.0 %collective-permute-done.33.refs_8_ = bf16[32,64,128]{2,1,0:T(8,128)(2,1)} collective-permute-done((bf16[32,64,128]{2,1,0:T(8,128)(2,1)}, bf16[32,64,128]{2,1,0:T(8,128)(2,1)}, u32[]{:S(2)}, u32[]{:S(2)}) %collective-permute-start.33) | collective-permute-done | bytes 524320 | tf_op jit(solution)/shard_map/ppermute | solution.py:40
  213.8 2.3 collective-permute-done.36.refs_10_
  216.2 1.9 broadcast_select_fusion
  219.9 7.6 %collective-permute-done.37.refs_8_ = bf16[32,64,128]{2,1,0:T(8,128)(2,1)} collective-permute-done((bf16[32,64,128]{2,1,0:T(8,128)(2,1)}, bf16[32,64,128]{2,1,0:T(8,128)(2,1)}, u32[]{:S(2)}, u32[]{:S(2)}) %collective-permute-start.37) | collective-permute-done | bytes 524320 | tf_op jit(solution)/shard_map/ppermute | solution.py:40
  228.9 3.7 %shard_map.79.refs_14_ = f32[33,64,128]{2,1,0:T(8,128)S(1)} custom-call(s32[2]{0:T(128)S(1)} %pad_add_fusion.14.ids_ref, s32[8,32]{1,0:T(8,128)S(1)} %bitcast.37, bf16[4,8,64,128]{3,2,1,0:T(8,128)(2,1)S(1)} %get-tuple-element.14.refs_0_, bf16[4,8,64,128]{3,2,1,0:T(8,128)(2,1)} %collective-permute-done.5.refs_0_.refs_1_, ...), custom_call_target="tpu_custom_call" | custom-call | flops 134217728 | bytes 1572864 | tf_op jit(solution)/shard_map/pallas_call | solution.py:218
  232.6 4.6 %shard_map.80.refs_14_ = f32[33,64,128]{2,1,0:T(8,128)S(1)} custom-call(s32[4]{0:T(128)S(1)} %pad_add_fusion.13.ids_ref, s32[8,32]{1,0:T(8,128)S(1)} %bitcast.38, bf16[4,8,64,128]{3,2,1,0:T(8,128)(2,1)S(1)} %get-tuple-element.14.refs_0_, bf16[4,8,64,128]{3,2,1,0:T(8,128)(2,1)} %collective-permute-done.5.refs_0_.refs_1_, ...), custom_call_target="tpu_custom_call", output_to_operand_aliasing={{}: (16, {})} | custom-call | flops 268435456 | bytes 3145728 | tf_op jit(solution)/shard_map/pallas_call | solution.py:218
  237.3 5.0 %shard_map.81.refs_14_ = f32[33,64,128]{2,1,0:T(8,128)S(1)} custom-call(s32[4]{0:T(128)S(1)} %pad_add_fusion.12.ids_ref, s32[8,32]{1,0:T(8,128)S(1)} %bitcast.39, bf16[4,8,64,128]{3,2,1,0:T(8,128)(2,1)S(1)} %get-tuple-element.14.refs_0_, bf16[4,8,64,128]{3,2,1,0:T(8,128)(2,1)} %collective-permute-done.5.refs_0_.refs_1_, ...), custom_call_target="tpu_custom_call", output_to_operand_aliasing={{}: (16, {})} | custom-call | flops 268435456 | bytes 3145728 | tf_op jit(solution)/shard_map/pallas_call | solution.py:218
  242.3 5.0 %shard_map.82.refs_12_ = f32[33,64,128]{2,1,0:T(8,128)S(1)} custom-call(s32[4]{0:T(128)S(1)} %pad_add_fusion.11.ids_ref, s32[8,32]{1,0:T(8,128)S(1)} %bitcast.40, bf16[4,8,64,128]{3,2,1,0:T(8,128)(2,1)S(1)} %get-tuple-element.14.refs_0_, bf16[4,8,64,128]{3,2,1,0:T(8,128)(2,1)} %collective-permute-done.5.refs_0_.refs_1_, ...), custom_call_target="tpu_custom_call", output_to_operand_aliasing={{}: (16, {})} | custom-call | flops 268435456 | bytes 3145728 | tf_op jit(solution)/shard_map/pallas_call | solution.py:218
  247.3 4.4 %shard_map.83 = bf16[32,64,128]{2,1,0:T(8,128)(2,1)} custom-call(s32[2]{0:T(128)S(1)} %pad_add_fusion.9.ids_ref, s32[8,32]{1,0:T(8,128)S(1)} %bitcast.41, bf16[4,8,64,128]{3,2,1,0:T(8,128)(2,1)S(1)} %get-tuple-element.14.refs_0_, bf16[4,8,64,128]{3,2,1,0:T(8,128)(2,1)} %collective-permute-done.5.refs_0_.refs_1_, ...), custom_call_target="tpu_custom_call" | custom-call | flops 134217728 | bytes 1572864 | tf_op jit(solution)/shard_map/pallas_call | solution.py:218
  (140 shorter events, 28.5 us)
Async XLA Ops:
  2.9 32.9 %copy-start.1 = (bf16[32,64,128]{2,1,0:T(8,128)(2,1)}, bf16[32,64,128]{2,1,0:T(8,128)(2,1)S(1)}, u32[]{:S(2)}) copy-start(bf16[32,64,128]{2,1,0:T(8,128)(2,1)S(1)} %get-tuple-element.25.refs_1_.wave_ref) | copy-start | bytes 1572868
  2.9 29.4 %copy-start = (bf16[2,32,128,128]{3,2,1,0:T(8,128)(2,1)S(1)}, bf16[2,32,128,128]{3,2,1,0:T(8,128)(2,1)}, u32[]{:S(2)}) copy-start(bf16[2,32,128,128]{3,2,1,0:T(8,128)(2,1)} %refs_10_.3) | copy-start | bytes 6291460
  2.9 27.5 %collective-permute-start.12 = (bf16[32,64,128]{2,1,0:T(8,128)(2,1)S(1)}, bf16[32,64,128]{2,1,0:T(8,128)(2,1)}, u32[]{:S(2)}, u32[]{:S(2)}) collective-permute-start(bf16[32,64,128]{2,1,0:T(8,128)(2,1)S(1)} %get-tuple-element.25.refs_1_.wave_ref), channel_id=1, source_target_pairs={{0,8},{1,9},{2,10},{3,11},{4,12},{5,13},{6,14},{7,15},{8,0},{9,1},... | collective-permute-start | bytes 1572872 | tf_op jit(solution)/shard_map/ppermute | solution.py:40
  8.0 26.4 %collective-permute-start.1 = (bf16[2,32,64,128]{3,2,1,0:T(8,128)(2,1)}, bf16[2,32,64,128]{3,2,1,0:T(8,128)(2,1)}, u32[]{:S(2)}, u32[]{:S(2)}) collective-permute-start(bf16[2,32,64,128]{3,2,1,0:T(8,128)(2,1)} %constant_dynamic-slice_fusion.3), channel_id=1, source_target_pairs={{0,1},{1,0},{2,3},{3,2},{4,5},{5,4},{6,7},{7,6},{8,9},{9,8},{10,11... | collective-permute-start | bytes 3145736 | tf_op jit(solution)/shard_map/ppermute | solution.py:40
  8.0 24.4 %collective-permute-start.24 = (bf16[32,64,128]{2,1,0:T(8,128)(2,1)S(1)}, bf16[32,64,128]{2,1,0:T(8,128)(2,1)}, u32[]{:S(2)}, u32[]{:S(2)}) collective-permute-start(bf16[32,64,128]{2,1,0:T(8,128)(2,1)S(1)} %get-tuple-element.25.refs_1_.wave_ref), channel_id=1, source_target_pairs={{0,2},{1,3},{2,0},{3,1},{4,6},{5,7},{6,4},{7,5},{8,10},{9,11},{10,... | collective-permute-start | bytes 1572872 | tf_op jit(solution)/shard_map/ppermute | solution.py:40
  9.6 24.2 %collective-permute-start.17 = (bf16[32,64,128]{2,1,0:T(8,128)(2,1)S(1)}, bf16[32,64,128]{2,1,0:T(8,128)(2,1)}, u32[]{:S(2)}, u32[]{:S(2)}) collective-permute-start(bf16[32,64,128]{2,1,0:T(8,128)(2,1)S(1)} %get-tuple-element.25.refs_1_.wave_ref), channel_id=1, source_target_pairs={{0,4},{1,5},{2,6},{3,7},{4,0},{5,1},{6,2},{7,3},{8,12},{9,13},{10,... | collective-permute-start | bytes 1572872 | tf_op jit(solution)/shard_map/ppermute | solution.py:40
  30.4 4.6 %collective-permute-start.26 = (bf16[32,64,128]{2,1,0:T(8,128)(2,1)}, bf16[32,64,128]{2,1,0:T(8,128)(2,1)S(1)}, u32[]{:S(2)}, u32[]{:S(2)}) collective-permute-start(bf16[32,64,128]{2,1,0:T(8,128)(2,1)} %collective-permute-done.12.refs_1_), channel_id=1, source_target_pairs={{0,1},{1,0},{2,3},{3,2},{4,5},{5,4},{6,7},{7,6},{8,9},{9,8},{10,11... | collective-permute-start | bytes 1572872 | tf_op jit(solution)/shard_map/ppermute | solution.py:40
  30.4 1.9 collective-permute-start
  32.2 100.0 %collective-permute-start.16 = (bf16[2,32,128,128]{3,2,1,0:T(8,128)(2,1)S(1)}, bf16[2,32,128,128]{3,2,1,0:T(8,128)(2,1)}, u32[]{:S(2)}, u32[]{:S(2)}) collective-permute-start(bf16[2,32,128,128]{3,2,1,0:T(8,128)(2,1)S(1)} %copy-done), channel_id=1, source_target_pairs={{0,1},{1,0},{2,3},{3,2},{4,5},{5,4},{6,7},{7,6},{8,9},{9,8},{10,11... | collective-permute-start | bytes 6291464 | tf_op jit(solution)/shard_map/ppermute | solution.py:40
  32.4 16.1 %collective-permute-start.25 = (bf16[32,64,128]{2,1,0:T(8,128)(2,1)}, bf16[32,64,128]{2,1,0:T(8,128)(2,1)}, u32[]{:S(2)}, u32[]{:S(2)}) collective-permute-start(bf16[32,64,128]{2,1,0:T(8,128)(2,1)} %collective-permute-done.24.refs_1_), channel_id=1, source_target_pairs={{0,1},{1,0},{2,3},{3,2},{4,5},{5,4},{6,7},{7,6},{8,9},{9,8},{10,11... | collective-permute-start | bytes 1572872 | tf_op jit(solution)/shard_map/ppermute | solution.py:40
  33.8 19.3 %collective-permute-start.22 = (bf16[32,64,128]{2,1,0:T(8,128)(2,1)}, bf16[32,64,128]{2,1,0:T(8,128)(2,1)}, u32[]{:S(2)}, u32[]{:S(2)}) collective-permute-start(bf16[32,64,128]{2,1,0:T(8,128)(2,1)} %collective-permute-done.12.refs_1_), channel_id=1, source_target_pairs={{0,2},{1,3},{2,0},{3,1},{4,6},{5,7},{6,4},{7,5},{8,10},{9,11},{10,... | collective-permute-start | bytes 1572872 | tf_op jit(solution)/shard_map/ppermute | solution.py:40
  34.4 21.9 %collective-permute-start.13 = (bf16[32,64,128]{2,1,0:T(8,128)(2,1)}, bf16[32,64,128]{2,1,0:T(8,128)(2,1)}, u32[]{:S(2)}, u32[]{:S(2)}) collective-permute-start(bf16[32,64,128]{2,1,0:T(8,128)(2,1)} %collective-permute-done.12.refs_1_), channel_id=1, source_target_pairs={{0,4},{1,5},{2,6},{3,7},{4,0},{5,1},{6,2},{7,3},{8,12},{9,13},{10,... | collective-permute-start | bytes 1572872 | tf_op jit(solution)/shard_map/ppermute | solution.py:40
  35.8 19.4 %collective-permute-start.21 = (bf16[32,64,128]{2,1,0:T(8,128)(2,1)}, bf16[32,64,128]{2,1,0:T(8,128)(2,1)}, u32[]{:S(2)}, u32[]{:S(2)}) collective-permute-start(bf16[32,64,128]{2,1,0:T(8,128)(2,1)} %collective-permute-done.17.refs_1_), channel_id=1, source_target_pairs={{0,1},{1,0},{2,3},{3,2},{4,5},{5,4},{6,7},{7,6},{8,9},{9,8},{10,11... | collective-permute-start | bytes 1572872 | tf_op jit(solution)/shard_map/ppermute | solution.py:40
  48.5 3.7 %collective-permute-start.2 = (s32[8,256]{1,0:T(8,128)S(1)}, s32[8,256]{1,0:T(8,128)S(1)}, u32[]{:S(2)}, u32[]{:S(2)}) collective-permute-start(s32[8,256]{1,0:T(8,128)S(1)} %broadcast_select_fusion.1), channel_id=1, source_target_pairs={{0,2},{1,3},{2,0},{3,1},{4,6},{5,7},{6,4},{7,5},{8,10},{9,11},{10,... | collective-permute-start | bytes 24584 | tf_op jit(solution)/shard_map/ppermute | solution.py:85
  52.1 15.2 %collective-permute-start.18 = (bf16[32,64,128]{2,1,0:T(8,128)(2,1)}, bf16[32,64,128]{2,1,0:T(8,128)(2,1)}, u32[]{:S(2)}, u32[]{:S(2)}) collective-permute-start(bf16[32,64,128]{2,1,0:T(8,128)(2,1)} %collective-permute-done.17.refs_1_), channel_id=1, source_target_pairs={{0,2},{1,3},{2,0},{3,1},{4,6},{5,7},{6,4},{7,5},{8,10},{9,11},{10,... | collective-permute-start | bytes 1572872 | tf_op jit(solution)/shard_map/ppermute | solution.py:40
  53.1 4.8 %collective-permute-start.3 = (s32[8,256]{1,0:T(8,128)S(1)}, s32[8,256]{1,0:T(8,128)S(1)}, u32[]{:S(2)}, u32[]{:S(2)}) collective-permute-start(s32[8,256]{1,0:T(8,128)S(1)} %fusion), channel_id=1, source_target_pairs={{0,4},{1,5},{2,6},{3,7},{4,0},{5,1},{6,2},{7,3},{8,12},{9,13},{10,... | collective-permute-start | bytes 24584 | tf_op jit(solution)/shard_map/ppermute | solution.py:85
  55.1 47.9 %collective-permute-start.8 = (bf16[4,8,64,128]{3,2,1,0:T(8,128)(2,1)}, bf16[4,8,64,128]{3,2,1,0:T(8,128)(2,1)S(1)}, u32[]{:S(2)}, u32[]{:S(2)}) collective-permute-start(bf16[4,8,64,128]{3,2,1,0:T(8,128)(2,1)} %copy-done.21), channel_id=1, source_target_pairs={{0,8},{1,9},{2,10},{3,11},{4,12},{5,13},{6,14},{7,15},{8,0},{9,1},... | collective-permute-start | bytes 1572872 | tf_op jit(solution)/shard_map/ppermute | solution.py:40
  56.4 46.6 %collective-permute-start.5 = (bf16[4,8,64,128]{3,2,1,0:T(8,128)(2,1)}, bf16[4,8,64,128]{3,2,1,0:T(8,128)(2,1)}, u32[]{:S(2)}, u32[]{:S(2)}) collective-permute-start(bf16[4,8,64,128]{3,2,1,0:T(8,128)(2,1)} %copy-done.20), channel_id=1, source_target_pairs={{0,2},{1,3},{2,0},{3,1},{4,6},{5,7},{6,4},{7,5},{8,10},{9,11},{10,... | collective-permute-start | bytes 1572872 | tf_op jit(solution)/shard_map/ppermute | solution.py:40
  57.9 47.7 %collective-permute-start.9 = (bf16[4,8,64,128]{3,2,1,0:T(8,128)(2,1)}, bf16[4,8,64,128]{3,2,1,0:T(8,128)(2,1)}, u32[]{:S(2)}, u32[]{:S(2)}) collective-permute-start(bf16[4,8,64,128]{3,2,1,0:T(8,128)(2,1)} %copy-done.19), channel_id=1, source_target_pairs={{0,10},{1,11},{2,8},{3,9},{4,14},{5,15},{6,12},{7,13},{8,2},{9,3},... | collective-permute-start | bytes 1572872 | tf_op jit(solution)/shard_map/ppermute | solution.py:40
  67.3 35.6 %collective-permute-start.4 = (s32[8,256]{1,0:T(8,128)S(1)}, s32[8,256]{1,0:T(8,128)S(1)}, u32[]{:S(2)}, u32[]{:S(2)}) collective-permute-start(s32[8,256]{1,0:T(8,128)S(1)} %fusion.1), channel_id=1, source_target_pairs={{0,8},{1,9},{2,10},{3,11},{4,12},{5,13},{6,14},{7,15},{8,0},{9,1},... | collective-permute-start | bytes 24584 | tf_op jit(solution)/shard_map/ppermute | solution.py:85
  102.9 4.4 %collective-permute-start.23 = (bf16[32,64,128]{2,1,0:T(8,128)(2,1)}, bf16[32,64,128]{2,1,0:T(8,128)(2,1)}, u32[]{:S(2)}, u32[]{:S(2)}) collective-permute-start(bf16[32,64,128]{2,1,0:T(8,128)(2,1)} %collective-permute-done.22.refs_1_), channel_id=1, source_target_pairs={{0,1},{1,0},{2,3},{3,2},{4,5},{5,4},{6,7},{7,6},{8,9},{9,8},{10,11... | collective-permute-start | bytes 1572872 | tf_op jit(solution)/shard_map/ppermute | solution.py:40
  103.0 14.6 %collective-permute-start.6 = (bf16[4,8,64,128]{3,2,1,0:T(8,128)(2,1)}, bf16[4,8,64,128]{3,2,1,0:T(8,128)(2,1)}, u32[]{:S(2)}, u32[]{:S(2)}) collective-permute-start(bf16[4,8,64,128]{3,2,1,0:T(8,128)(2,1)} %copy-done.18), channel_id=1, source_target_pairs={{0,4},{1,5},{2,6},{3,7},{4,0},{5,1},{6,2},{7,3},{8,12},{9,13},{10,... | collective-permute-start | bytes 1572872 | tf_op jit(solution)/shard_map/ppermute | solution.py:40
  103.0 26.7 %collective-permute-start.10 = (bf16[4,8,64,128]{3,2,1,0:T(8,128)(2,1)}, bf16[4,8,64,128]{3,2,1,0:T(8,128)(2,1)}, u32[]{:S(2)}, u32[]{:S(2)}) collective-permute-start(bf16[4,8,64,128]{3,2,1,0:T(8,128)(2,1)} %copy-done.17), channel_id=1, source_target_pairs={{0,12},{1,13},{2,14},{3,15},{4,8},{5,9},{6,10},{7,11},{8,4},{9,5},... | collective-permute-start | bytes 1572872 | tf_op jit(solution)/shard_map/ppermute | solution.py:40
  105.6 26.6 %collective-permute-start.14 = (bf16[32,64,128]{2,1,0:T(8,128)(2,1)}, bf16[32,64,128]{2,1,0:T(8,128)(2,1)}, u32[]{:S(2)}, u32[]{:S(2)}) collective-permute-start(bf16[32,64,128]{2,1,0:T(8,128)(2,1)} %collective-permute-done.13.refs_1_), channel_id=1, source_target_pairs={{0,2},{1,3},{2,0},{3,1},{4,6},{5,7},{6,4},{7,5},{8,10},{9,11},{10,... | collective-permute-start | bytes 1572872 | tf_op jit(solution)/shard_map/ppermute | solution.py:40
  107.3 41.8 %collective-permute-start.20 = (bf16[32,64,128]{2,1,0:T(8,128)(2,1)}, bf16[32,64,128]{2,1,0:T(8,128)(2,1)}, u32[]{:S(2)}, u32[]{:S(2)}) collective-permute-start(bf16[32,64,128]{2,1,0:T(8,128)(2,1)} %collective-permute-done.13.refs_1_), channel_id=1, source_target_pairs={{0,1},{1,0},{2,3},{3,2},{4,5},{5,4},{6,7},{7,6},{8,9},{9,8},{10,11... | collective-permute-start | bytes 1572872 | tf_op jit(solution)/shard_map/ppermute | solution.py:40
  117.6 34.5 %collective-permute-start.7 = (bf16[4,8,64,128]{3,2,1,0:T(8,128)(2,1)}, bf16[4,8,64,128]{3,2,1,0:T(8,128)(2,1)}, u32[]{:S(2)}, u32[]{:S(2)}) collective-permute-start(bf16[4,8,64,128]{3,2,1,0:T(8,128)(2,1)} %copy-done.16), channel_id=1, source_target_pairs={{0,6},{1,7},{2,4},{3,5},{4,2},{5,3},{6,0},{7,1},{8,14},{9,15},{10,... | collective-permute-start | bytes 1572872 | tf_op jit(solution)/shard_map/ppermute | solution.py:40
  129.7 32.3 %collective-permute-start.11 = (bf16[4,8,64,128]{3,2,1,0:T(8,128)(2,1)}, bf16[4,8,64,128]{3,2,1,0:T(8,128)(2,1)}, u32[]{:S(2)}, u32[]{:S(2)}) collective-permute-start(bf16[4,8,64,128]{3,2,1,0:T(8,128)(2,1)} %copy-done.15), channel_id=1, source_target_pairs={{0,14},{1,15},{2,12},{3,13},{4,10},{5,11},{6,8},{7,9},{8,6},{9,7},... | collective-permute-start | bytes 1572872 | tf_op jit(solution)/shard_map/ppermute | solution.py:40
  132.2 19.9 %collective-permute-start.19 = (bf16[32,64,128]{2,1,0:T(8,128)(2,1)}, bf16[32,64,128]{2,1,0:T(8,128)(2,1)}, u32[]{:S(2)}, u32[]{:S(2)}) collective-permute-start(bf16[32,64,128]{2,1,0:T(8,128)(2,1)} %collective-permute-done.18.refs_1_), channel_id=1, source_target_pairs={{0,1},{1,0},{2,3},{3,2},{4,5},{5,4},{6,7},{7,6},{8,9},{9,8},{10,11... | collective-permute-start | bytes 1572872 | tf_op jit(solution)/shard_map/ppermute | solution.py:40
  132.2 29.8 %collective-permute-start.15 = (bf16[32,64,128]{2,1,0:T(8,128)(2,1)}, bf16[32,64,128]{2,1,0:T(8,128)(2,1)}, u32[]{:S(2)}, u32[]{:S(2)}) collective-permute-start(bf16[32,64,128]{2,1,0:T(8,128)(2,1)} %collective-permute-done.14.refs_1_), channel_id=1, source_target_pairs={{0,1},{1,0},{2,3},{3,2},{4,5},{5,4},{6,7},{7,6},{8,9},{9,8},{10,11... | collective-permute-start | bytes 1572872 | tf_op jit(solution)/shard_map/ppermute | solution.py:40
  166.2 1.2 collective-permute-start.27
  167.4 3.7 %collective-permute-start.28 = (f32[16,128]{1,0:T(8,128)S(1)}, f32[16,128]{1,0:T(8,128)S(1)}, u32[]{:S(2)}, u32[]{:S(2)}) collective-permute-start(f32[16,128]{1,0:T(8,128)S(1)} %add.109), channel_id=1, source_target_pairs={{0,2},{1,3},{2,0},{3,1},{4,6},{5,7},{6,4},{7,5},{8,10},{9,11},{10,... | collective-permute-start | bytes 24584 | tf_op jit(solution)/shard_map/ppermute | solution.py:85
  171.1 3.7 %collective-permute-start.29 = (f32[16,128]{1,0:T(8,128)S(1)}, f32[16,128]{1,0:T(8,128)S(1)}, u32[]{:S(2)}, u32[]{:S(2)}) collective-permute-start(f32[16,128]{1,0:T(8,128)S(1)} %add.110), channel_id=1, source_target_pairs={{0,4},{1,5},{2,6},{3,7},{4,0},{5,1},{6,2},{7,3},{8,12},{9,13},{10,... | collective-permute-start | bytes 24584 | tf_op jit(solution)/shard_map/ppermute | solution.py:85
  174.7 4.5 %collective-permute-start.30 = (f32[16,128]{1,0:T(8,128)S(1)}, f32[16,128]{1,0:T(8,128)S(1)}, u32[]{:S(2)}, u32[]{:S(2)}) collective-permute-start(f32[16,128]{1,0:T(8,128)S(1)} %add.111), channel_id=1, source_target_pairs={{0,8},{1,9},{2,10},{3,11},{4,12},{5,13},{6,14},{7,15},{8,0},{9,1},... | collective-permute-start | bytes 24584 | tf_op jit(solution)/shard_map/ppermute | solution.py:85
  180.3 12.1 %collective-permute-start.31 = (bf16[32,64,128]{2,1,0:T(8,128)(2,1)S(1)}, bf16[32,64,128]{2,1,0:T(8,128)(2,1)S(1)}, u32[]{:S(2)}, u32[]{:S(2)}) collective-permute-start(bf16[32,64,128]{2,1,0:T(8,128)(2,1)S(1)} %get-tuple-element.22.refs_8_), channel_id=1, source_target_pairs={{0,4},{1,5},{2,0},{3,1},{4,8},{5,9},{6,2},{7,3},{8,12},{9,13},{10,... | collective-permute-start | bytes 1572872 | tf_op jit(solution)/shard_map/ppermute | solution.py:40
  181.4 12.1 %collective-permute-start.34 = (bf16[32,64,128]{2,1,0:T(8,128)(2,1)S(1)}, bf16[32,64,128]{2,1,0:T(8,128)(2,1)S(1)}, u32[]{:S(2)}, u32[]{:S(2)}) collective-permute-start(bf16[32,64,128]{2,1,0:T(8,128)(2,1)S(1)} %get-tuple-element.22.refs_8_), channel_id=1, source_target_pairs={{0,2},{1,3},{2,6},{3,7},{4,0},{5,1},{6,10},{7,11},{8,4},{9,5},{10,... | collective-permute-start | bytes 1572872 | tf_op jit(solution)/shard_map/ppermute | solution.py:40
  192.4 11.9 %collective-permute-start.32 = (bf16[32,64,128]{2,1,0:T(8,128)(2,1)S(1)}, bf16[32,64,128]{2,1,0:T(8,128)(2,1)}, u32[]{:S(2)}, u32[]{:S(2)}) collective-permute-start(bf16[32,64,128]{2,1,0:T(8,128)(2,1)S(1)} %collective-permute-done.31.refs_8_), channel_id=1, source_target_pairs={{0,4},{1,5},{2,0},{3,1},{4,8},{5,9},{6,2},{7,3},{8,12},{9,13},{10,... | collective-permute-start | bytes 1572872 | tf_op jit(solution)/shard_map/ppermute | solution.py:40
  193.5 11.9 %collective-permute-start.35 = (bf16[32,64,128]{2,1,0:T(8,128)(2,1)S(1)}, bf16[32,64,128]{2,1,0:T(8,128)(2,1)}, u32[]{:S(2)}, u32[]{:S(2)}) collective-permute-start(bf16[32,64,128]{2,1,0:T(8,128)(2,1)S(1)} %collective-permute-done.34.refs_10_), channel_id=1, source_target_pairs={{0,2},{1,3},{2,6},{3,7},{4,0},{5,1},{6,10},{7,11},{8,4},{9,5},{10,... | collective-permute-start | bytes 1572872 | tf_op jit(solution)/shard_map/ppermute | solution.py:40
  204.3 9.5 %collective-permute-start.33 = (bf16[32,64,128]{2,1,0:T(8,128)(2,1)}, bf16[32,64,128]{2,1,0:T(8,128)(2,1)}, u32[]{:S(2)}, u32[]{:S(2)}) collective-permute-start(bf16[32,64,128]{2,1,0:T(8,128)(2,1)} %collective-permute-done.32.refs_8_), channel_id=1, source_target_pairs={{0,4},{1,5},{2,0},{3,1},{4,8},{5,9},{6,2},{7,3},{8,12},{9,13},{10,... | collective-permute-start | bytes 1572872 | tf_op jit(solution)/shard_map/ppermute | solution.py:40
  205.4 10.8 %collective-permute-start.36 = (bf16[32,64,128]{2,1,0:T(8,128)(2,1)}, bf16[32,64,128]{2,1,0:T(8,128)(2,1)}, u32[]{:S(2)}, u32[]{:S(2)}) collective-permute-start(bf16[32,64,128]{2,1,0:T(8,128)(2,1)} %collective-permute-done.35.refs_10_), channel_id=1, source_target_pairs={{0,2},{1,3},{2,6},{3,7},{4,0},{5,1},{6,10},{7,11},{8,4},{9,5},{10,... | collective-permute-start | bytes 1572872 | tf_op jit(solution)/shard_map/ppermute | solution.py:40
  206.4 12.5 %collective-permute-start.45 = (bf16[32,64,128]{2,1,0:T(8,128)(2,1)}, bf16[32,64,128]{2,1,0:T(8,128)(2,1)}, u32[]{:S(2)}, u32[]{:S(2)}) collective-permute-start(bf16[32,64,128]{2,1,0:T(8,128)(2,1)} %copy-done.7), channel_id=1, source_target_pairs={{0,1},{1,0},{2,3},{3,2},{4,5},{5,4},{6,7},{7,6},{8,9},{9,8},{10,11... | collective-permute-start | bytes 1572872 | tf_op jit(solution)/shard_map/ppermute | solution.py:40
  206.4 13.0 %collective-permute-start.43 = (bf16[32,64,128]{2,1,0:T(8,128)(2,1)}, bf16[32,64,128]{2,1,0:T(8,128)(2,1)}, u32[]{:S(2)}, u32[]{:S(2)}) collective-permute-start(bf16[32,64,128]{2,1,0:T(8,128)(2,1)} %copy-done.9), channel_id=1, source_target_pairs={{0,1},{1,0},{2,3},{3,2},{4,5},{5,4},{6,7},{7,6},{8,9},{9,8},{10,11... | collective-permute-start | bytes 1572872 | tf_op jit(solution)/shard_map/ppermute | solution.py:40
  206.9 12.6 %collective-permute-start.44 = (bf16[32,64,128]{2,1,0:T(8,128)(2,1)}, bf16[32,64,128]{2,1,0:T(8,128)(2,1)}, u32[]{:S(2)}, u32[]{:S(2)}) collective-permute-start(bf16[32,64,128]{2,1,0:T(8,128)(2,1)} %copy-done.11), channel_id=1, source_target_pairs={{0,1},{1,0},{2,3},{3,2},{4,5},{5,4},{6,7},{7,6},{8,9},{9,8},{10,11... | collective-permute-start | bytes 1572872 | tf_op jit(solution)/shard_map/ppermute | solution.py:40
  218.1 9.5 %collective-permute-start.37 = (bf16[32,64,128]{2,1,0:T(8,128)(2,1)}, bf16[32,64,128]{2,1,0:T(8,128)(2,1)}, u32[]{:S(2)}, u32[]{:S(2)}) collective-permute-start(bf16[32,64,128]{2,1,0:T(8,128)(2,1)} %broadcast_select_fusion), channel_id=1, source_target_pairs={{0,4},{1,3},{2,0},{3,7},{4,8},{5,1},{6,2},{7,11},{8,12},{9,5},{10,... | collective-permute-start | bytes 1572872 | tf_op jit(solution)/shard_map/ppermute | solution.py:40
  218.8 18.4 %collective-permute-start.41 = (bf16[32,64,128]{2,1,0:T(8,128)(2,1)}, bf16[32,64,128]{2,1,0:T(8,128)(2,1)}, u32[]{:S(2)}, u32[]{:S(2)}) collective-permute-start(bf16[32,64,128]{2,1,0:T(8,128)(2,1)} %collective-permute-done.32.refs_8_), channel_id=1, source_target_pairs={{0,1},{1,0},{2,3},{3,2},{4,5},{5,4},{6,7},{7,6},{8,9},{9,8},{10,11... | collective-permute-start | bytes 1572872 | tf_op jit(solution)/shard_map/ppermute | solution.py:40
  218.8 18.4 %collective-permute-start.42 = (bf16[32,64,128]{2,1,0:T(8,128)(2,1)}, bf16[32,64,128]{2,1,0:T(8,128)(2,1)}, u32[]{:S(2)}, u32[]{:S(2)}) collective-permute-start(bf16[32,64,128]{2,1,0:T(8,128)(2,1)} %collective-permute-done.35.refs_10_), channel_id=1, source_target_pairs={{0,1},{1,0},{2,3},{3,2},{4,5},{5,4},{6,7},{7,6},{8,9},{9,8},{10,11... | collective-permute-start | bytes 1572872 | tf_op jit(solution)/shard_map/ppermute | solution.py:40
  219.4 22.9 %collective-permute-start.39 = (bf16[32,64,128]{2,1,0:T(8,128)(2,1)}, bf16[32,64,128]{2,1,0:T(8,128)(2,1)}, u32[]{:S(2)}, u32[]{:S(2)}) collective-permute-start(bf16[32,64,128]{2,1,0:T(8,128)(2,1)} %collective-permute-done.33.refs_8_), channel_id=1, source_target_pairs={{0,1},{1,0},{2,3},{3,2},{4,5},{5,4},{6,7},{7,6},{8,9},{9,8},{10,11... | collective-permute-start | bytes 1572872 | tf_op jit(solution)/shard_map/ppermute | solution.py:40
  219.4 22.8 %collective-permute-start.40 = (bf16[32,64,128]{2,1,0:T(8,128)(2,1)}, bf16[32,64,128]{2,1,0:T(8,128)(2,1)}, u32[]{:S(2)}, u32[]{:S(2)}) collective-permute-start(bf16[32,64,128]{2,1,0:T(8,128)(2,1)} %collective-permute-done.36.refs_10_), channel_id=1, source_target_pairs={{0,1},{1,0},{2,3},{3,2},{4,5},{5,4},{6,7},{7,6},{8,9},{9,8},{10,11... | collective-permute-start | bytes 1572872 | tf_op jit(solution)/shard_map/ppermute | solution.py:40
  227.6 19.7 %collective-permute-start.38 = (bf16[32,64,128]{2,1,0:T(8,128)(2,1)}, bf16[32,64,128]{2,1,0:T(8,128)(2,1)S(1)}, u32[]{:S(2)}, u32[]{:S(2)}) collective-permute-start(bf16[32,64,128]{2,1,0:T(8,128)(2,1)} %collective-permute-done.37.refs_8_), channel_id=1, source_target_pairs={{0,1},{1,0},{2,3},{3,2},{4,5},{5,4},{6,7},{7,6},{8,9},{9,8},{10,11... | collective-permute-start | bytes 1572872 | tf_op jit(solution)/shard_map/ppermute | solution.py:40
  (22 other events, 105.1 us)

commit v4 on v3

--- a/solution.py
+++ b/solution.py
@@ -8,7 +8,8 @@
 from jax.sharding import PartitionSpec as P
 
 BOTH = ("sec", "term")
-VMEM_LIMIT = 32 * 2**20
+VMEM_LIMIT = 20 * 2**20
+PART = 16
 RING_BYTES = 24 * 2**20
 
 
@@ -56,6 +57,28 @@
     )
 
 
+def select_kernel(half_ref, lower_ref, upper_ref, out_ref, sem):
+    for half, source in enumerate((lower_ref, upper_ref)):
+
+        @pl.when(half_ref[0] == half)
+        def _():
+            copy = pltpu.make_async_copy(source, out_ref, sem)
+            copy.start()
+            copy.wait()
+
+
+def select_half(half, lower, upper):
+    anywhere = pl.BlockSpec(memory_space=pl.ANY)
+    return pl.pallas_call(
+        select_kernel,
+        out_shape=jax.ShapeDtypeStruct(lower.shape, lower.dtype),
+        in_specs=[pl.BlockSpec(memory_space=pltpu.SMEM), anywhere, anywhere],
+        out_specs=anywhere,
+        scratch_shapes=[pltpu.SemaphoreType.DMA],
+        cost_estimate=busy(0.8),
+    )(jnp.reshape(half, (1,)).astype(jnp.int32), lower, upper)
+
+
 def ring_gather(unit, owners, halves, half):
     units = {0: unit}
     reach = (owners - 1) // 2
@@ -63,18 +86,40 @@
         units[step] = ring_send(units[step - 1], owners, halves, (1,) * halves)
         units[-step] = ring_send(units[1 - step], owners, halves, (-1,) * halves)
     if owners % 2 == 0:
-        last = jnp.where(half == 0, units[reach], units[-reach])
+        last = select_half(half, units[reach], units[-reach])
         units[owners // 2] = ring_send(last, owners, halves, (1, -1))
     return units
 
 
-def mask_gather(unit, owners, halves):
+def after_kernel(*refs):
+    del refs
+
+
+def after(value, *others):
+    anywhere = pl.BlockSpec(memory_space=pl.ANY)
+    return pl.pallas_call(
+        after_kernel,
+        out_shape=jax.ShapeDtypeStruct(value.shape, value.dtype),
+        in_specs=[anywhere] * (1 + len(others)),
+        out_specs=anywhere,
+        input_output_aliases={0: 0},
+        cost_estimate=busy(0.3),
+    )(value, *others)
+
+
+def mask_gather(unit, lefts, owners, halves):
     units = {0: unit}
     step = owners // 2
+    masks = []
     while step:
-        for mask in list(units):
+        masks.append(step)
+        units[step] = exchange(unit, owners, halves, step)
+        step //= 2
+    for mask in masks[:-1]:
+        units[mask] = after(units[mask], lefts[mask])
+    for step in masks[1:]:
+        for mask in [m for m in units if m >= 2 * step and m % (2 * step) == 0]:
             units[mask | step] = exchange(units[mask], owners, halves, step)
-        step //= 2
     return units
 
 
@@ -89,75 +134,104 @@
     return value
 
 
-def pack_kernel(capacity, blocks, terms, ids_ref, plan_ref, left_ref, other_ref, *refs):
-    pieces, codes, seen = refs[:-2], refs[-2], refs[-1]
-    owners = len(pieces)
+def pack_kernel(order, capacity, blocks, terms, ids_ref, plan_ref, other_plan_ref, *refs):
+    left_ref, other_ref, *pieces, codes, seen, built, sems = refs
+    owners = len(order)
     me, half = ids_ref[0], ids_ref[1]
-    rows = other_ref.shape[2]
+    rows, width = other_ref.shape[2:]
     start = pl.multiple_of(half * rows, rows)
+    parts = rows // PART
 
     @pl.loop(0, owners)
     def _(owner):
         for index in range(2 * terms * capacity):
-            codes[owner, index] = blocks
+            codes[0, owner, index] = 0
+            codes[1, owner, index] = blocks
 
     for stream in range(2 * terms):
+        plan = plan_ref if stream < terms else other_plan_ref
 
         @pl.loop(0, owners)
         def _(owner):
             seen[owner] = 0
 
-        @pl.loop(0, blocks)
+        @pl.loop(0, blocks, unroll=4)
         def _(block):
-            plan = plan_ref[stream, block]
-            owner, target = lax.div(plan, blocks), lax.rem(plan, blocks)
+            owner = plan[0, stream % terms, block]
             slot = seen[owner]
             seen[owner] = slot + 1
-            codes[owner, stream * capacity + slot] = block * (2 * blocks) + target
-
-    for mask, piece in enumerate(pieces):
+            codes[0, owner, stream * capacity + slot] = block
+            codes[1, owner, stream * capacity + slot] = plan[1, stream % terms, block]
+
+    lane = lax.broadcasted_iota(jnp.int32, (PART, width), 1)
+    row = lax.broadcasted_iota(jnp.int32, (PART, width), 0)
+    copies = []
+    for mask in order:
         owner = me ^ mask
+        labels = jnp.zeros((PART, width), jnp.int32)
         for stream in range(2 * terms):
-
-            @pl.loop(0, capacity, unroll=True)
-            def _(slot):
-                block = lax.div(codes[owner, stream * capacity + slot], 2 * blocks)
+            for slot in range(capacity):
+                at = stream * capacity + slot
+                block = codes[0, owner, at]
                 if stream < terms:
                     value = left_ref[stream, block, pl.ds(start, rows), :]
                 else:
                     value = other_ref[stream - terms, block]
                 value = pltpu.roll(value.astype(jnp.float32), half * rows, 1)
-                piece[stream, slot] = value.astype(jnp.bfloat16)
-
-
-def pack(ids, plan, left, other, owners, capacity):
+                built[mask, at * parts : (at + 1) * parts] = value.astype(jnp.bfloat16).reshape(
+                    parts, PART, width
+                )
+                label = jnp.where(row == 0, block, codes[1, owner, at])
+                labels = jnp.where(lane == at, label, labels)
+        built[mask, 2 * terms * capacity * parts] = labels.astype(jnp.float32).astype(jnp.bfloat16)
+        copies.append(pltpu.make_async_copy(built.at[mask], pieces[mask], sems.at[mask]))
+        copies[-1].start()
+    for copy in copies:
+        copy.wait()
+
+
+def pack(ids, plan, other_plan, left, other, order, capacity):
     terms, blocks, rows, width = other.shape
+    owners = len(order)
     scalars = pl.BlockSpec(memory_space=pltpu.SMEM)
     whole = pl.BlockSpec(memory_space=pltpu.VMEM)
-    piece = jax.ShapeDtypeStruct((2 * terms, capacity, rows, width), jnp.bfloat16)
-    *pieces, codes = pl.pallas_call(
-        functools.partial(pack_kernel, capacity, blocks, terms),
-        out_shape=[piece] * owners
-        + [jax.ShapeDtypeStruct((owners, 2 * terms * capacity), jnp.int32)],
-        in_specs=[scalars, scalars, whole, whole],
-        out_specs=[whole] * owners + [scalars],
-        scratch_shapes=[pltpu.SMEM((owners,), jnp.int32)],
+    anywhere = pl.BlockSpec(memory_space=pl.ANY)
+    shape = (2 * terms * capacity * rows // PART + 1, PART, width)
+    return pl.pallas_call(
+        functools.partial(pack_kernel, order, capacity, blocks, terms),
+        out_shape=[jax.ShapeDtypeStruct(shape, jnp.bfloat16)] * owners,
+        in_specs=[scalars] * 3 + [whole, whole],
+        out_specs=[anywhere] * owners,
+        scratch_shapes=[
+            pltpu.SMEM((2, owners, 2 * terms * capacity), jnp.int32),
+            pltpu.SMEM((owners,), jnp.int32),
+            pltpu.VMEM((owners,) + shape, jnp.bfloat16),
+            pltpu.SemaphoreType.DMA((owners,)),
+        ],
         compiler_params=pltpu.CompilerParams(vmem_limit_bytes=VMEM_LIMIT),
-    )(ids, plan, left, other)
-    return pieces, codes
-
-
-def add_products(piece, near, far, rights, total, code_of, blocks):
-    streams, capacity = piece.shape[:2]
+        cost_estimate=busy(5.0),
+    )(ids, plan, other_plan, left, other)
+
+
+def busy(microseconds):
+    return pl.CostEstimate(
+        flops=int(1.15e9 * microseconds), bytes_accessed=0, transcendentals=0
+    )
+
+
+def add_products(piece, labels, near, far, rights, total, streams, capacity):
     terms = streams // 2
+    blocks, rows, width = near.shape
+    parts = rows // PART
     for side in range(2):
         moved, where = [], []
         for stream in range(terms * side, terms * side + terms):
             for slot in range(capacity):
-                code = code_of(stream * capacity + slot)
-                source, target = lax.div(code, 2 * blocks), lax.rem(code, 2 * blocks)
+                at = stream * capacity + slot
+                source, target = labels[0, at], labels[1, at]
                 block = jnp.concatenate([near[source], far[source]], axis=0)
-                product = jnp.dot(piece[stream, slot], block, preferred_element_type=jnp.float32)
+                left = piece[at * parts : (at + 1) * parts].reshape(rows, width)
+                product = jnp.dot(left, block, preferred_element_type=jnp.float32)
                 moved.append(product.astype(jnp.bfloat16))
                 where.append((stream - terms * side, target))
         for value, (term, target) in zip(moved, where):
@@ -168,7 +242,7 @@
             )
 
 
-def apply_kernel(sources, first, choices, last, blocks, ids_ref, codes_ref, *refs):
+def apply_kernel(sources, first, choices, last, streams, capacity, ids_ref, *refs):
     refs = list(refs)
     lefts = [refs.pop(0) for _ in range(choices or sources)]
     vectors = [(refs.pop(0), refs.pop(0)) for _ in range(sources)]
@@ -176,37 +250,66 @@
     total_in = None if first else refs.pop(0)
     out = refs.pop(0) if last else None
     total = refs.pop(0)
-    chosen = refs.pop(0) if choices else None
+    spread_labels, labels, label_sems = refs.pop(0), refs.pop(0), refs.pop(0)
+    blocks = vectors[0][0].shape[0]
+
+    if choices:
+        chosen, chosen_sems = refs.pop(0), refs.pop(0)
+        for index in range(sources):
+            for choice, left in enumerate(lefts):
+
+                @pl.when(ids_ref[index] == choice)
+                def _():
+                    pltpu.make_async_copy(left, chosen.at[index], chosen_sems.at[index]).start()
 
     total[...] = jnp.zeros_like(total) if first else total_in[...]
-    for index, (near, far) in enumerate(vectors):
-        chip = ids_ref[2 * index]
+    pieces = []
+    for index in range(sources):
         if choices:
-            for choice, left in enumerate(lefts):
-
-                @pl.when(ids_ref[2 * index + 1] == choice)
-                def _():
-                    chosen[...] = left[...]
-
-            piece = chosen
+            pltpu.make_async_copy(lefts[0], chosen.at[index], chosen_sems.at[index]).wait()
+            piece = chosen.at[index]
         else:
             piece = lefts[index]
-        add_products(piece, near, far, rights, total, lambda at: codes_ref[chip, at], blocks)
+        pieces.append(piece)
+        values = piece[piece.shape[0] - 1].astype(jnp.float32).astype(jnp.int32)
+        spread_labels[index] = values[:8]
+        pltpu.make_async_copy(
+            spread_labels.at[index], labels.at[index], label_sems.at[index]
+        ).start()
+    for index, (near, far) in enumerate(vectors):
+        pltpu.make_async_copy(
+            spread_labels.at[index], labels.at[index], label_sems.at[index]
+        ).wait()
+        add_products(
+            pieces[index], labels.at[index], near, far, rights, total, streams, capacity
+        )
     if last:
         out[...] = total[:blocks].astype(out.dtype)
 
 
-def apply_group(ids, codes, lefts, vectors, rights, total, choices, last):
-    streams, capacity, rows, width = lefts[0].shape
-    blocks = rights[0].shape[1]
+def apply_group(ids, lefts, vectors, rights, total, choices, last):
+    blocks, rows, width = vectors[0][0].shape
+    streams = 2 * rights[0].shape[0]
+    capacity = (lefts[0].shape[0] - 1) * PART // (streams * rows)
+    sources = len(vectors)
     first = total is None
     arrays = list(lefts) + [unit for pair in vectors for unit in pair] + list(rights)
     if not first:
         arrays.append(total)
-    scalars = pl.BlockSpec(memory_space=pltpu.SMEM)
     whole = pl.BlockSpec(memory_space=pltpu.VMEM)
     total_shape = (blocks + 1, rows, width)
-    scratch = [pltpu.VMEM(lefts[0].shape, lefts[0].dtype)] if choices else []
+    scratch = [
+        pltpu.VMEM((sources, 8, width), jnp.int32),
+        pltpu.SMEM((sources, 8, width), jnp.int32),
+        pltpu.SemaphoreType.DMA((sources,)),
+    ]
+    specs = [whole] * len(arrays)
+    if choices:
+        scratch += [
+            pltpu.VMEM((sources,) + lefts[0].shape, lefts[0].dtype),
+            pltpu.SemaphoreType.DMA((sources,)),
+        ]
+        specs[: len(lefts)] = [pl.BlockSpec(memory_space=pl.ANY)] * len(lefts)
     aliases = {}
     if last:
         out_shape = jax.ShapeDtypeStruct((blocks, rows, width), jnp.bfloat16)
@@ -214,23 +317,19 @@
     else:
         out_shape = jax.ShapeDtypeStruct(total_shape, jnp.float32)
         if not first:
-            aliases = {len(arrays) + 1: 0}
+            aliases = {len(arrays): 0}
     return pl.pallas_call(
         functools.partial(
-            apply_kernel, len(vectors), first, len(lefts) if choices else 0, last, blocks
+            apply_kernel, sources, first, len(lefts) if choices else 0, last, streams, capacity
         ),
         out_shape=out_shape,
-        in_specs=[scalars] * 2 + [whole] * len(arrays),
+        in_specs=[pl.BlockSpec(memory_space=pltpu.SMEM)] + specs,
         out_specs=whole,
         scratch_shapes=scratch,
         input_output_aliases=aliases,
         compiler_params=pltpu.CompilerParams(vmem_limit_bytes=VMEM_LIMIT),
-        cost_estimate=pl.CostEstimate(
-            flops=len(vectors) * streams * capacity * 2 * 2 * rows * width * width,
-            bytes_accessed=2 * len(vectors) * (streams * capacity + 2 * blocks) * rows * width,
-            transcendentals=0,
-        ),
-    )(ids, codes, *arrays)
+        cost_estimate=busy(0.7 + 1.4 * sources),
+    )(ids, *arrays)
 
 
 def stats_kernel(ids_ref, total_ref, wave_ref, stats_ref):
@@ -309,33 +408,31 @@
 
     own_rows = lax.dynamic_slice_in_dim(wavefunction, half * rows, rows, 1)
     other_rows = lax.dynamic_slice_in_dim(wavefunction, (1 - half) * rows, rows, 1)
-    near = mask_gather(own_rows, owners, halves)
-    far = {m: swap(unit, owners, halves) if m else other_rows for m, unit in near.items()}
-
-    plan = target_owner[:, :, 0] * blocks + target_local
-    plan = jnp.concatenate([plan, swap(plan, owners, halves)], axis=0)
+    plan = jnp.stack([target_owner[:, :, 0], target_local])
     other_left = swap(
         lax.dynamic_slice_in_dim(left_operator, (1 - half) * rows, rows, 2), owners, halves
     )
-    pieces, codes = pack(ids, plan, left_operator, other_left, owners, capacity)
+    order = [m for pair in zip(range(owners // 2), range(owners // 2, owners)) for m in pair]
+    order = order[:-2] + order[-1:] + order[-2:-1]
+    pieces = pack(
+        ids,
+        plan,
+        swap(plan, owners, halves),
+        left_operator,
+        other_left,
+        order[1:] + order[:1],
+        capacity,
+    )
     lefts = [exchange(piece, owners, halves, m) if m else piece for m, piece in enumerate(pieces)]
-    codes = jnp.where(jnp.arange(owners)[:, None] == me, codes.reshape(1, -1), 0)
-    codes = doubled(codes, owners, BOTH, halves).reshape(owners, owners, -1)
-    codes = lax.dynamic_index_in_dim(codes, me, axis=1, keepdims=False)
     rights = (right_operator, swap(right_operator, owners, halves))
-
-    order = [m for pair in zip(range(owners // 2), range(owners // 2, owners)) for m in pair]
+    near = mask_gather(own_rows, lefts, owners, halves)
+    far = {m: swap(unit, owners, halves) if m else other_rows for m, unit in near.items()}
+
     total = None
+    no_choice = jnp.zeros((1,), jnp.int32)
     for m in order:
         total = apply_group(
-            jnp.stack([me ^ m, 0]).astype(jnp.int32),
-            codes,
-            [lefts[m]],
-            [(near[m], far[m])],
-            rights,
-            total,
-            False,
-            False,
+            no_choice, [lefts[m]], [(near[m], far[m])], rights, total, False, False
         )
 
     entries = blocks * owners * height * width
@@ -348,10 +445,9 @@
         groups.append([owners // 2])
     total = None
     for group in groups:
-        chips = [ring_owner(place - s, owners) for s in group]
+        choice = jnp.stack([ring_owner(place - s, owners) ^ me for s in group])
         total = apply_group(
-            jnp.stack([value for chip in chips for value in (chip, chip ^ me)]).astype(jnp.int32),
-            codes,
+            choice.astype(jnp.int32),
             lefts,
             [(near[s], far[s]) for s in group],
             rights,

time: 252 us -> 260 us (1.032)
  waiting for transfers between devices: 137 us -> 114 us
  Pallas kernels: 53.1 us -> 72.8 us
  starting transfers between devices: 43.1 us -> 53.6 us
  other arithmetic: 3.21 us -> 0.32 us
    ppermute x7 -> x4, waiting for transfers between devices: 43.9 us -> 8.08 us  [doubled(): lax.ppermute(value, axes, [(d, d ^ step * stride) for d in range(total)])]
    pallas_call x14 -> x17, Pallas kernels: 50.8 us -> 68.6 us  [the longest x13 47.8 us: apply_group(): pl.pallas_call(functools.partial(apply_kernel, sources, first, len(lefts)...]
    ppermute x39, waiting for transfers between devices: 92.7 us -> 106 us  [permute(): return lax.ppermute(value, BOTH, pairs)]
    ppermute x39, starting transfers between devices: 32.7 us -> 45.1 us  [permute(): return lax.ppermute(value, BOTH, pairs)]
    ppermute x7 -> x4, starting transfers between devices: 10.4 us -> 8.45 us  [doubled(): lax.ppermute(value, axes, [(d, d ^ step * stride) for d in range(total)])]
    unnamed x48 -> x52, local copies, waits for them, and re-layouts: 11.2 us -> 11.8 us
  transfers between devices with their start and end apart: 46 -> 43, of which waited for: 18 -> 16; matrix products, arithmetic and copies ran while one was open for 2% -> 1% of each run, Pallas kernels for 17% -> 24%
where the time goes in v4:
time: 260 us; the launch traced here: 259 us
  waiting for transfers between devices  114 us (44%)
  Pallas kernels  72.8 us (28%)
  starting transfers between devices  53.6 us (21%)
  local copies, waits for them, and re-layouts  16.5 us (6%)
    ppermute x39, waiting for transfers between devices, permute(): return lax.ppermute(value, BOTH, pairs)  106 us
    pallas_call x13, Pallas kernels, apply_group(): pl.pallas_call(functools.partial(apply_kernel, sources, first, len(lefts)...  47.8 us
    ppermute x39, starting transfers between devices, permute(): return lax.ppermute(value, BOTH, pairs)  45.1 us
    pallas_call x1, Pallas kernels, select_half(): pl.pallas_call(select_kernel, out_shape=jax.ShapeDtypeStruct(lower.shape,...  17 us
    unnamed x52, local copies, waits for them, and re-layouts  11.8 us
    ppermute x4, starting transfers between devices, doubled(): lax.ppermute(value, axes, [(d, d ^ step * stride) for d in range(total)])  8.45 us
    ppermute x4, waiting for transfers between devices, doubled(): lax.ppermute(value, axes, [(d, d ^ step * stride) for d in range(total)])  8.08 us
  transfers between devices with their start and end apart: 43, of which 16 were waited for; matrix products, arithmetic and copies ran while one was open for 1% of the time, Pallas kernels for 24%

profile of v4, /device:TPU:0, one launch (start us, length us, event | category | flops | bytes accessed | tf_op | source)
XLA Modules:
  0.0 259.0 jit_solution(1013605439395878399)
XLA Ops:
  0.6 2.4 constant_dynamic-slice_fusion.2
  3.6 2.3 constant_dynamic-slice_fusion
  5.9 4.0 %collective-permute-start.13 = (bf16[32,64,128]{2,1,0:T(8,128)(2,1)}, bf16[32,64,128]{2,1,0:T(8,128)(2,1)}, u32[]{:S(2)}, u32[]{:S(2)}) collective-permute-start(bf16[32,64,128]{2,1,0:T(8,128)(2,1)} %get-tuple-element.23.refs_1_.wave_ref), channel_id=1, source_target_pairs={{0,8},{1,9},{2,10},{3,11},{4,12},{5,13},{6,14},{7,15},{8,0},{9,1},... | collective-permute-start | bytes 1572872 | tf_op jit(solution)/shard_map/ppermute | solution.py:41
  9.9 1.5 collective-permute-start.21
  12.7 1.6 copy-done.12
  14.3 3.8 %shard_map.68 = (bf16[129,16,128]{2,1,0:T(8,128)(2,1)S(1)}, bf16[129,16,128]{2,1,0:T(8,128)(2,1)}, bf16[129,16,128]{2,1,0:T(8,128)(2,1)}, bf16[129,16,128]{2,1,0...) custom-call(s32[3]{0:T(128)S(1)} %pad_add_fusion.1.ids_ref, ...), custom_call_target="tpu_custom_call" | custom-call | flops 5750000128 | tf_op jit(solution)/shard_map/pallas_call | solution.py:200
  22.5 1.6 collective-permute-start.9
  24.1 21.5 %collective-permute-done.13.refs_0_ = bf16[32,64,128]{2,1,0:T(8,128)(2,1)} collective-permute-done((bf16[32,64,128]{2,1,0:T(8,128)(2,1)}, bf16[32,64,128]{2,1,0:T(8,128)(2,1)}, u32[]{:S(2)}, u32[]{:S(2)}) %collective-permute-start.13) | collective-permute-done | bytes 524320 | tf_op jit(solution)/shard_map/ppermute | solution.py:41
  45.5 1.9 collective-permute-start.2
  47.4 8.8 %collective-permute-done.5.refs_1_.refs_0_.refs_4_ = bf16[129,16,128]{2,1,0:T(8,128)(2,1)S(1)} collective-permute-done((bf16[129,16,128]{2,1,0:T(8,128)(2,1)S(1)}, bf16[129,16,128]{2,1,0:T(8,128)(2,1)S(1)}, u32[]{:S(2)}, u32[]{:S(2)}) %collective-permute-start.5) | collective-permute-done | bytes 528416 | tf_op jit(solution)/shard_map/ppermute | solution.py:41
  57.1 1.6 collective-permute-start.19
  59.8 3.6 %collective-permute-start.6 = (bf16[129,16,128]{2,1,0:T(8,128)(2,1)}, bf16[129,16,128]{2,1,0:T(8,128)(2,1)}, u32[]{:S(2)}, u32[]{:S(2)}) collective-permute-start(bf16[129,16,128]{2,1,0:T(8,128)(2,1)} %copy-done.19), channel_id=1, source_target_pairs={{0,10},{1,11},{2,8},{3,9},{4,14},{5,15},{6,12},{7,13},{8,2},{9,3},... | collective-permute-start | bytes 1585160 | tf_op jit(solution)/shard_map/ppermute | solution.py:41
  63.4 19.3 %collective-permute-done.3.refs_1_.refs_0_.refs_2_ = bf16[129,16,128]{2,1,0:T(8,128)(2,1)S(1)} collective-permute-done((bf16[129,16,128]{2,1,0:T(8,128)(2,1)}, bf16[129,16,128]{2,1,0:T(8,128)(2,1)S(1)}, u32[]{:S(2)}, u32[]{:S(2)}) %collective-permute-start.3) | collective-permute-done | bytes 528416 | tf_op jit(solution)/shard_map/ppermute | solution.py:41
  82.7 3.6 %collective-permute-start.7 = (bf16[129,16,128]{2,1,0:T(8,128)(2,1)}, bf16[129,16,128]{2,1,0:T(8,128)(2,1)}, u32[]{:S(2)}, u32[]{:S(2)}) collective-permute-start(bf16[129,16,128]{2,1,0:T(8,128)(2,1)} %copy-done.18), channel_id=1, source_target_pairs={{0,12},{1,13},{2,14},{3,15},{4,8},{5,9},{6,10},{7,11},{8,4},{9,5},... | collective-permute-start | bytes 1585160 | tf_op jit(solution)/shard_map/ppermute | solution.py:41
  86.5 6.0 %collective-permute-done.14.refs_1_ = bf16[32,64,128]{2,1,0:T(8,128)(2,1)} collective-permute-done((bf16[32,64,128]{2,1,0:T(8,128)(2,1)}, bf16[32,64,128]{2,1,0:T(8,128)(2,1)}, u32[]{:S(2)}, u32[]{:S(2)}) %collective-permute-start.14) | collective-permute-done | bytes 524320 | tf_op jit(solution)/shard_map/ppermute | solution.py:41
  95.9 3.2 %shard_map.71.refs_5_ = f32[33,64,128]{2,1,0:T(8,128)S(1)} custom-call(s32[1]{0:T(128)} %constant.94.clone.1.ids_ref, bf16[129,16,128]{2,1,0:T(8,128)(2,1)S(1)} %copy-done.6, bf16[32,64,128]{2,1,0:T(8,128)(2,1)} %get-tuple-element.23.refs_1_.wave_ref, bf16[32,64,128]{2,1,0:T(8,128)(2,1)S(1)} %copy-done.13, bf16[2,32,128,128]{3,2,1,0:T(8,128)(2,1)S(1)} %copy-done, ...), custom_call_target="tpu_custom_call" | custom-call | flops 2415000064 | tf_op jit(solution)/shard_map/pallas_call | solution.py:321
  100.0 3.2 %shard_map.72.refs_5_ = f32[33,64,128]{2,1,0:T(8,128)S(1)} custom-call(s32[1]{0:T(128)} %constant.94.clone.1.ids_ref, bf16[129,16,128]{2,1,0:T(8,128)(2,1)S(1)} %copy-done.2, bf16[32,64,128]{2,1,0:T(8,128)(2,1)} %shard_map.70.refs_1_, bf16[32,64,128]{2,1,0:T(8,128)(2,1)} %collective-permute-done.23.refs_2_, ...), custom_call_target="tpu_custom_call", output_to_operand_aliasing={{}: (6, {})} | custom-call | flops 2415000064 | tf_op jit(solution)/shard_map/pallas_call | solution.py:321
  103.3 3.0 %collective-permute-done.7.refs_0_.refs_6_ = bf16[129,16,128]{2,1,0:T(8,128)(2,1)} collective-permute-done((bf16[129,16,128]{2,1,0:T(8,128)(2,1)}, bf16[129,16,128]{2,1,0:T(8,128)(2,1)}, u32[]{:S(2)}, u32[]{:S(2)}) %collective-permute-start.7) | collective-permute-done | bytes 528416 | tf_op jit(solution)/shard_map/ppermute | solution.py:41
  106.3 3.4 %shard_map.73.refs_5_ = f32[33,64,128]{2,1,0:T(8,128)S(1)} custom-call(s32[1]{0:T(128)} %constant.94.clone.1.ids_ref, bf16[129,16,128]{2,1,0:T(8,128)(2,1)} %collective-permute-done.2.refs_0_.refs_1_, bf16[32,64,128]{2,1,0:T(8,128)(2,1)} %collective-permute-done.21.refs_1_, ...), custom_call_target="tpu_custom_call", output_to_operand_aliasing={{}: (6, {})} | custom-call | flops 2415000064 | tf_op jit(solution)/shard_map/pallas_call | solution.py:321
  109.7 13.6 %collective-permute-start.8 = (bf16[129,16,128]{2,1,0:T(8,128)(2,1)S(1)}, bf16[129,16,128]{2,1,0:T(8,128)(2,1)S(1)}, u32[]{:S(2)}, u32[]{:S(2)}) collective-permute-start(bf16[129,16,128]{2,1,0:T(8,128)(2,1)S(1)} %copy-done.17), channel_id=1, source_target_pairs={{0,14},{1,15},{2,12},{3,13},{4,10},{5,11},{6,8},{7,9},{8,6},{9,7},... | collective-permute-start | bytes 1585160 | tf_op jit(solution)/shard_map/ppermute | solution.py:41
  123.4 3.2 %shard_map.74.refs_5_ = f32[33,64,128]{2,1,0:T(8,128)S(1)} custom-call(s32[1]{0:T(128)} %constant.94.clone.1.ids_ref, bf16[129,16,128]{2,1,0:T(8,128)(2,1)} %collective-permute-done.6.refs_0_.refs_5_, bf16[32,64,128]{2,1,0:T(8,128)(2,1)} %collective-permute-done.19.refs_1_, ...), custom_call_target="tpu_custom_call", output_to_operand_aliasing={{}: (6, {})} | custom-call | flops 2415000064 | tf_op jit(solution)/shard_map/pallas_call | solution.py:321
  127.3 3.1 %shard_map.75.refs_5_ = f32[33,64,128]{2,1,0:T(8,128)S(1)} custom-call(s32[1]{0:T(128)} %constant.94.clone.1.ids_ref, bf16[129,16,128]{2,1,0:T(8,128)(2,1)S(1)} %copy-done.4, bf16[32,64,128]{2,1,0:T(8,128)(2,1)} %shard_map.69.refs_1_, bf16[32,64,128]{2,1,0:T(8,128)(2,1)S(1)} %collective-permute-done.18.refs_2_, ...), custom_call_target="tpu_custom_call", output_to_operand_aliasing={{}: (6, {})} | custom-call | flops 2415000064 | tf_op jit(solution)/shard_map/pallas_call | solution.py:321
  130.4 3.2 %shard_map.76.refs_5_ = f32[33,64,128]{2,1,0:T(8,128)S(1)} custom-call(s32[1]{0:T(128)} %constant.94.clone.1.ids_ref, bf16[129,16,128]{2,1,0:T(8,128)(2,1)} %collective-permute-done.7.refs_0_.refs_6_, bf16[32,64,128]{2,1,0:T(8,128)(2,1)} %collective-permute-done.14.refs_1_, ...), custom_call_target="tpu_custom_call", output_to_operand_aliasing={{}: (6, {})} | custom-call | flops 2415000064 | tf_op jit(solution)/shard_map/pallas_call | solution.py:321
  133.7 2.6 %collective-permute-done.8.refs_0_.refs_7_ = bf16[129,16,128]{2,1,0:T(8,128)(2,1)S(1)} collective-permute-done((bf16[129,16,128]{2,1,0:T(8,128)(2,1)S(1)}, bf16[129,16,128]{2,1,0:T(8,128)(2,1)S(1)}, u32[]{:S(2)}, u32[]{:S(2)}) %collective-permute-start.8) | collective-permute-done | bytes 528416 | tf_op jit(solution)/shard_map/ppermute | solution.py:41
  136.3 3.1 %shard_map.77.refs_5_ = f32[33,64,128]{2,1,0:T(8,128)S(1)} custom-call(s32[1]{0:T(128)} %constant.94.clone.1.ids_ref, bf16[129,16,128]{2,1,0:T(8,128)(2,1)S(1)} %collective-permute-done.8.refs_0_.refs_7_, bf16[32,64,128]{2,1,0:T(8,128)(2,1)S(1)} %collective-permute-done.15.refs_1_, ...), custom_call_target="tpu_custom_call", output_to_operand_aliasing={{}: (6, {})} | custom-call | flops 2415000064 | tf_op jit(solution)/shard_map/pallas_call | solution.py:321
  139.4 16.2 %collective-permute-done.4.refs_0_.refs_3_ = bf16[129,16,128]{2,1,0:T(8,128)(2,1)S(1)} collective-permute-done((bf16[129,16,128]{2,1,0:T(8,128)(2,1)S(1)}, bf16[129,16,128]{2,1,0:T(8,128)(2,1)S(1)}, u32[]{:S(2)}, u32[]{:S(2)}) %collective-permute-start.4) | collective-permute-done | bytes 528416 | tf_op jit(solution)/shard_map/ppermute | solution.py:41
  155.6 3.1 %shard_map.78.total_ref = f32[33,64,128]{2,1,0:T(8,128)S(1)} custom-call(s32[1]{0:T(128)} %constant.94.clone.1.ids_ref, bf16[129,16,128]{2,1,0:T(8,128)(2,1)S(1)} %collective-permute-done.4.refs_0_.refs_3_, bf16[32,64,128]{2,1,0:T(8,128)(2,1)S(1)} %collective-permute-done.10.refs_1_, ...), custom_call_target="tpu_custom_call", output_to_operand_aliasing={{}: (6, {})} | custom-call | flops 2415000064 | tf_op jit(solution)/shard_map/pallas_call | solution.py:321
  158.7 1.7 shard_map.79
  161.7 1.5 collective-permute-start.25
  163.2 2.1 collective-permute-done.25
  165.3 5.5 %collective-permute-start.26 = (f32[16,128]{1,0:T(8,128)S(1)}, f32[16,128]{1,0:T(8,128)S(1)}, u32[]{:S(2)}, u32[]{:S(2)}) collective-permute-start(f32[16,128]{1,0:T(8,128)S(1)} %add.89), channel_id=1, source_target_pairs={{0,4},{1,5},{2,6},{3,7},{4,0},{5,1},{6,2},{7,3},{8,12},{9,13},{10,... | collective-permute-start | bytes 24584 | tf_op jit(solution)/shard_map/ppermute | solution.py:130
  170.8 1.6 collective-permute-done.26
  172.4 1.4 collective-permute-start.27
  173.8 3.2 %collective-permute-done.27 = f32[16,128]{1,0:T(8,128)S(1)} collective-permute-done((f32[16,128]{1,0:T(8,128)S(1)}, f32[16,128]{1,0:T(8,128)S(1)}, u32[]{:S(2)}, u32[]{:S(2)}) %collective-permute-start.27) | collective-permute-done | bytes 8224 | tf_op jit(solution)/shard_map/ppermute | solution.py:130
  177.0 2.4 shard_map.80
  179.4 2.0 collective-permute-start.28
  181.4 9.4 %collective-permute-done.28.refs_8_ = bf16[32,64,128]{2,1,0:T(8,128)(2,1)S(1)} collective-permute-done((bf16[32,64,128]{2,1,0:T(8,128)(2,1)}, bf16[32,64,128]{2,1,0:T(8,128)(2,1)S(1)}, u32[]{:S(2)}, u32[]{:S(2)}) %collective-permute-start.28) | collective-permute-done | bytes 524320 | tf_op jit(solution)/shard_map/ppermute | solution.py:41
  191.7 2.0 collective-permute-start.29
  193.8 9.8 %collective-permute-done.29.refs_8_ = bf16[32,64,128]{2,1,0:T(8,128)(2,1)} collective-permute-done((bf16[32,64,128]{2,1,0:T(8,128)(2,1)S(1)}, bf16[32,64,128]{2,1,0:T(8,128)(2,1)}, u32[]{:S(2)}, u32[]{:S(2)}) %collective-permute-start.29) | collective-permute-done | bytes 524320 | tf_op jit(solution)/shard_map/ppermute | solution.py:41
  203.6 2.0 collective-permute-start.30
  206.6 6.5 %collective-permute-done.30.lower_ref.refs_8_ = bf16[32,64,128]{2,1,0:T(8,128)(2,1)} collective-permute-done((bf16[32,64,128]{2,1,0:T(8,128)(2,1)}, bf16[32,64,128]{2,1,0:T(8,128)(2,1)}, u32[]{:S(2)}, u32[]{:S(2)}) %collective-permute-start.30) | collective-permute-done | bytes 524320 | tf_op jit(solution)/shard_map/ppermute | solution.py:41
  213.1 2.0 collective-permute-done.33.upper_ref.refs_10_
  215.1 17.0 %shard_map.81 = bf16[32,64,128]{2,1,0:T(8,128)(2,1)} custom-call(s32[1]{0:T(128)} %bitcast.2.half_ref, bf16[32,64,128]{2,1,0:T(8,128)(2,1)} %collective-permute-done.30.lower_ref.refs_8_, bf16[32,64,128]{2,1,0:T(8,128)(2,1)} %collective-permute-done.33.upper_ref.refs_10_), custom_call_target="tpu_custom_call" | custom-call | flops 920000000 | tf_op jit(solution)/shard_map/pallas_call | solution.py:72
  235.8 3.5 %shard_map.82.refs_14_ = f32[33,64,128]{2,1,0:T(8,128)S(1)} custom-call(s32[1]{0:T(128)} %bitcast.12.ids_ref, bf16[129,16,128]{2,1,0:T(8,128)(2,1)S(1)} %copy-done.7, bf16[129,16,128]{2,1,0:T(8,128)(2,1)} %collective-permute-done.2.refs_0_.refs_1_, bf16[129,16,128]{2,1,0:T(8,128)(2,1)S(1)} %copy-done.4, bf16[129,16,128]{2,1,0:T(8,128)(2,1)S(1)} %copy-done.11, ...), custom_call_target="tpu_custom_call" | custom-call | flops 2415000064 | tf_op jit(solution)/shard_map/pallas_call | solution.py:321
  239.9 5.1 %shard_map.83.refs_14_ = f32[33,64,128]{2,1,0:T(8,128)S(1)} custom-call(s32[2]{0:T(128)S(1)} %pad_add_fusion.4.ids_ref, bf16[129,16,128]{2,1,0:T(8,128)(2,1)S(1)} %copy-done.7, bf16[129,16,128]{2,1,0:T(8,128)(2,1)} %collective-permute-done.2.refs_0_.refs_1_, bf16[129,16,128]{2,1,0:T(8,128)(2,1)S(1)} %copy-done.4, ...), custom_call_target="tpu_custom_call", output_to_operand_aliasing={{}: (15, {})} | custom-call | flops 4024999936 | tf_op jit(solution)/shard_map/pallas_call | solution.py:321
  245.2 4.6 %shard_map.84.refs_14_ = f32[33,64,128]{2,1,0:T(8,128)S(1)} custom-call(s32[2]{0:T(128)S(1)} %pad_add_fusion.3.ids_ref, bf16[129,16,128]{2,1,0:T(8,128)(2,1)S(1)} %copy-done.7, bf16[129,16,128]{2,1,0:T(8,128)(2,1)} %collective-permute-done.2.refs_0_.refs_1_, bf16[129,16,128]{2,1,0:T(8,128)(2,1)S(1)} %copy-done.4, ...), custom_call_target="tpu_custom_call", output_to_operand_aliasing={{}: (15, {})} | custom-call | flops 4024999936 | tf_op jit(solution)/shard_map/pallas_call | solution.py:321
  249.8 5.1 %shard_map.85.refs_12_ = f32[33,64,128]{2,1,0:T(8,128)S(1)} custom-call(s32[2]{0:T(128)S(1)} %pad_add_fusion.2.ids_ref, bf16[129,16,128]{2,1,0:T(8,128)(2,1)S(1)} %copy-done.7, bf16[129,16,128]{2,1,0:T(8,128)(2,1)} %collective-permute-done.2.refs_0_.refs_1_, bf16[129,16,128]{2,1,0:T(8,128)(2,1)S(1)} %copy-done.4, ...), custom_call_target="tpu_custom_call", output_to_operand_aliasing={{}: (15, {})} | custom-call | flops 4024999936 | tf_op jit(solution)/shard_map/pallas_call | solution.py:321
  254.9 3.9 %shard_map.86 = bf16[32,64,128]{2,1,0:T(8,128)(2,1)} custom-call(s32[1]{0:T(128)} %bitcast.ids_ref, bf16[129,16,128]{2,1,0:T(8,128)(2,1)S(1)} %copy-done.7, bf16[129,16,128]{2,1,0:T(8,128)(2,1)} %collective-permute-done.2.refs_0_.refs_1_, bf16[129,16,128]{2,1,0:T(8,128)(2,1)S(1)} %copy-done.4, bf16[129,16,128]{2,1,0:T(8,128)(2,1)S(1)} %copy-done.11, ...), custom_call_target="tpu_custom_call" | custom-call | flops 2415000064 | tf_op jit(solution)/shard_map/pallas_call | solution.py:321
  (120 shorter events, 20.5 us)
Async XLA Ops:
  3.1 8.4 %copy-start.24 = (s32[2,32]{1,0:T(2,128)S(1)}, s32[2,32]{1,0:T(2,128)}, u32[]{:S(2)}) copy-start(s32[2,32]{1,0:T(2,128)} %param.9) | copy-start | bytes 772
  3.1 8.4 %copy-start.25 = (s32[2,32,1]{1,2,0:T(1,128)S(1)}, s32[2,32,1]{1,2,0:T(1,128)}, u32[]{:S(2)}) copy-start(s32[2,32,1]{1,2,0:T(1,128)} %param.8) | copy-start | bytes 772
  3.1 9.6 %collective-permute-start.1 = (bf16[2,32,64,128]{3,2,1,0:T(8,128)(2,1)}, bf16[2,32,64,128]{3,2,1,0:T(8,128)(2,1)S(1)}, u32[]{:S(2)}, u32[]{:S(2)}) collective-permute-start(bf16[2,32,64,128]{3,2,1,0:T(8,128)(2,1)} %constant_dynamic-slice_fusion.2), channel_id=1, source_target_pairs={{0,1},{1,0},{2,3},{3,2},{4,5},{5,4},{6,7},{7,6},{8,9},{9,8},{10,11... | collective-permute-start | bytes 3145736 | tf_op jit(solution)/shard_map/ppermute | solution.py:41
  3.5 79.1 %collective-permute-start.12 = (bf16[2,32,128,128]{3,2,1,0:T(8,128)(2,1)S(1)}, bf16[2,32,128,128]{3,2,1,0:T(8,128)(2,1)}, u32[]{:S(2)}, u32[]{:S(2)}) collective-permute-start(bf16[2,32,128,128]{3,2,1,0:T(8,128)(2,1)S(1)} %copy-done), channel_id=1, source_target_pairs={{0,1},{1,0},{2,3},{3,2},{4,5},{5,4},{6,7},{7,6},{8,9},{9,8},{10,11... | collective-permute-start | bytes 6291464 | tf_op jit(solution)/shard_map/ppermute | solution.py:41
  5.9 39.6 %collective-permute-start.13 = (bf16[32,64,128]{2,1,0:T(8,128)(2,1)}, bf16[32,64,128]{2,1,0:T(8,128)(2,1)}, u32[]{:S(2)}, u32[]{:S(2)}) collective-permute-start(bf16[32,64,128]{2,1,0:T(8,128)(2,1)} %get-tuple-element.23.refs_1_.wave_ref), channel_id=1, source_target_pairs={{0,8},{1,9},{2,10},{3,11},{4,12},{5,13},{6,14},{7,15},{8,0},{9,1},... | collective-permute-start | bytes 1572872 | tf_op jit(solution)/shard_map/ppermute | solution.py:41
  9.9 14.1 %collective-permute-start.21 = (bf16[32,64,128]{2,1,0:T(8,128)(2,1)}, bf16[32,64,128]{2,1,0:T(8,128)(2,1)}, u32[]{:S(2)}, u32[]{:S(2)}) collective-permute-start(bf16[32,64,128]{2,1,0:T(8,128)(2,1)} %get-tuple-element.23.refs_1_.wave_ref), channel_id=1, source_target_pairs={{0,2},{1,3},{2,0},{3,1},{4,6},{5,7},{6,4},{7,5},{8,10},{9,11},{10,... | collective-permute-start | bytes 1572872 | tf_op jit(solution)/shard_map/ppermute | solution.py:41
  11.5 1.2 collective-permute-start
  22.1 34.1 %collective-permute-start.5 = (bf16[129,16,128]{2,1,0:T(8,128)(2,1)S(1)}, bf16[129,16,128]{2,1,0:T(8,128)(2,1)S(1)}, u32[]{:S(2)}, u32[]{:S(2)}) collective-permute-start(bf16[129,16,128]{2,1,0:T(8,128)(2,1)S(1)} %get-tuple-element.16), channel_id=1, source_target_pairs={{0,8},{1,9},{2,10},{3,11},{4,12},{5,13},{6,14},{7,15},{8,0},{9,1},... | collective-permute-start | bytes 1585160 | tf_op jit(solution)/shard_map/ppermute | solution.py:41
  22.5 34.6 %collective-permute-start.9 = (bf16[32,64,128]{2,1,0:T(8,128)(2,1)}, bf16[32,64,128]{2,1,0:T(8,128)(2,1)}, u32[]{:S(2)}, u32[]{:S(2)}) collective-permute-start(bf16[32,64,128]{2,1,0:T(8,128)(2,1)} %get-tuple-element.23.refs_1_.wave_ref), channel_id=1, source_target_pairs={{0,4},{1,5},{2,6},{3,7},{4,0},{5,1},{6,2},{7,3},{8,12},{9,13},{10,... | collective-permute-start | bytes 1572872 | tf_op jit(solution)/shard_map/ppermute | solution.py:41
  24.1 34.6 %collective-permute-start.22 = (bf16[32,64,128]{2,1,0:T(8,128)(2,1)}, bf16[32,64,128]{2,1,0:T(8,128)(2,1)}, u32[]{:S(2)}, u32[]{:S(2)}) collective-permute-start(bf16[32,64,128]{2,1,0:T(8,128)(2,1)} %collective-permute-done.21.refs_1_), channel_id=1, source_target_pairs={{0,1},{1,0},{2,3},{3,2},{4,5},{5,4},{6,7},{7,6},{8,9},{9,8},{10,11... | collective-permute-start | bytes 1572872 | tf_op jit(solution)/shard_map/ppermute | solution.py:41
  45.5 14.3 %collective-permute-start.2 = (bf16[129,16,128]{2,1,0:T(8,128)(2,1)}, bf16[129,16,128]{2,1,0:T(8,128)(2,1)}, u32[]{:S(2)}, u32[]{:S(2)}) collective-permute-start(bf16[129,16,128]{2,1,0:T(8,128)(2,1)} %get-tuple-element.13), channel_id=1, source_target_pairs={{0,2},{1,3},{2,0},{3,1},{4,6},{5,7},{6,4},{7,5},{8,10},{9,11},{10,... | collective-permute-start | bytes 1585160 | tf_op jit(solution)/shard_map/ppermute | solution.py:41
  56.2 26.5 %collective-permute-start.3 = (bf16[129,16,128]{2,1,0:T(8,128)(2,1)}, bf16[129,16,128]{2,1,0:T(8,128)(2,1)S(1)}, u32[]{:S(2)}, u32[]{:S(2)}) collective-permute-start(bf16[129,16,128]{2,1,0:T(8,128)(2,1)} %get-tuple-element.14), channel_id=1, source_target_pairs={{0,4},{1,5},{2,6},{3,7},{4,0},{5,1},{6,2},{7,3},{8,12},{9,13},{10,... | collective-permute-start | bytes 1585160 | tf_op jit(solution)/shard_map/ppermute | solution.py:41
  57.1 29.3 %collective-permute-start.19 = (bf16[32,64,128]{2,1,0:T(8,128)(2,1)}, bf16[32,64,128]{2,1,0:T(8,128)(2,1)}, u32[]{:S(2)}, u32[]{:S(2)}) collective-permute-start(bf16[32,64,128]{2,1,0:T(8,128)(2,1)} %shard_map.70.refs_1_), channel_id=1, source_target_pairs={{0,2},{1,3},{2,0},{3,1},{4,6},{5,7},{6,4},{7,5},{8,10},{9,11},{10,... | collective-permute-start | bytes 1572872 | tf_op jit(solution)/shard_map/ppermute | solution.py:41
  58.6 33.9 %collective-permute-start.14 = (bf16[32,64,128]{2,1,0:T(8,128)(2,1)}, bf16[32,64,128]{2,1,0:T(8,128)(2,1)}, u32[]{:S(2)}, u32[]{:S(2)}) collective-permute-start(bf16[32,64,128]{2,1,0:T(8,128)(2,1)} %shard_map.70.refs_1_), channel_id=1, source_target_pairs={{0,4},{1,5},{2,6},{3,7},{4,0},{5,1},{6,2},{7,3},{8,12},{9,13},{10,... | collective-permute-start | bytes 1572872 | tf_op jit(solution)/shard_map/ppermute | solution.py:41
  59.8 39.3 %collective-permute-start.6 = (bf16[129,16,128]{2,1,0:T(8,128)(2,1)}, bf16[129,16,128]{2,1,0:T(8,128)(2,1)}, u32[]{:S(2)}, u32[]{:S(2)}) collective-permute-start(bf16[129,16,128]{2,1,0:T(8,128)(2,1)} %copy-done.19), channel_id=1, source_target_pairs={{0,10},{1,11},{2,8},{3,9},{4,14},{5,15},{6,12},{7,13},{8,2},{9,3},... | collective-permute-start | bytes 1585160 | tf_op jit(solution)/shard_map/ppermute | solution.py:41
  82.7 16.5 %collective-permute-start.23 = (bf16[32,64,128]{2,1,0:T(8,128)(2,1)}, bf16[32,64,128]{2,1,0:T(8,128)(2,1)}, u32[]{:S(2)}, u32[]{:S(2)}) collective-permute-start(bf16[32,64,128]{2,1,0:T(8,128)(2,1)} %shard_map.70.refs_1_), channel_id=1, source_target_pairs={{0,1},{1,0},{2,3},{3,2},{4,5},{5,4},{6,7},{7,6},{8,9},{9,8},{10,11... | collective-permute-start | bytes 1572872 | tf_op jit(solution)/shard_map/ppermute | solution.py:41
  82.7 23.6 %collective-permute-start.7 = (bf16[129,16,128]{2,1,0:T(8,128)(2,1)}, bf16[129,16,128]{2,1,0:T(8,128)(2,1)}, u32[]{:S(2)}, u32[]{:S(2)}) collective-permute-start(bf16[129,16,128]{2,1,0:T(8,128)(2,1)} %copy-done.18), channel_id=1, source_target_pairs={{0,12},{1,13},{2,14},{3,15},{4,8},{5,9},{6,10},{7,11},{8,4},{9,5},... | collective-permute-start | bytes 1585160 | tf_op jit(solution)/shard_map/ppermute | solution.py:41
  86.3 23.4 %collective-permute-start.20 = (bf16[32,64,128]{2,1,0:T(8,128)(2,1)}, bf16[32,64,128]{2,1,0:T(8,128)(2,1)S(1)}, u32[]{:S(2)}, u32[]{:S(2)}) collective-permute-start(bf16[32,64,128]{2,1,0:T(8,128)(2,1)} %collective-permute-done.19.refs_1_), channel_id=1, source_target_pairs={{0,1},{1,0},{2,3},{3,2},{4,5},{5,4},{6,7},{7,6},{8,9},{9,8},{10,11... | collective-permute-start | bytes 1572872 | tf_op jit(solution)/shard_map/ppermute | solution.py:41
  92.5 30.8 %collective-permute-start.15 = (bf16[32,64,128]{2,1,0:T(8,128)(2,1)}, bf16[32,64,128]{2,1,0:T(8,128)(2,1)S(1)}, u32[]{:S(2)}, u32[]{:S(2)}) collective-permute-start(bf16[32,64,128]{2,1,0:T(8,128)(2,1)} %collective-permute-done.14.refs_1_), channel_id=1, source_target_pairs={{0,2},{1,3},{2,0},{3,1},{4,6},{5,7},{6,4},{7,5},{8,10},{9,11},{10,... | collective-permute-start | bytes 1572872 | tf_op jit(solution)/shard_map/ppermute | solution.py:41
  99.1 27.6 %collective-permute-start.18 = (bf16[32,64,128]{2,1,0:T(8,128)(2,1)}, bf16[32,64,128]{2,1,0:T(8,128)(2,1)S(1)}, u32[]{:S(2)}, u32[]{:S(2)}) collective-permute-start(bf16[32,64,128]{2,1,0:T(8,128)(2,1)} %shard_map.69.refs_1_), channel_id=1, source_target_pairs={{0,1},{1,0},{2,3},{3,2},{4,5},{5,4},{6,7},{7,6},{8,9},{9,8},{10,11... | collective-permute-start | bytes 1572872 | tf_op jit(solution)/shard_map/ppermute | solution.py:41
  99.2 27.6 %collective-permute-start.10 = (bf16[32,64,128]{2,1,0:T(8,128)(2,1)}, bf16[32,64,128]{2,1,0:T(8,128)(2,1)S(1)}, u32[]{:S(2)}, u32[]{:S(2)}) collective-permute-start(bf16[32,64,128]{2,1,0:T(8,128)(2,1)} %shard_map.69.refs_1_), channel_id=1, source_target_pairs={{0,2},{1,3},{2,0},{3,1},{4,6},{5,7},{6,4},{7,5},{8,10},{9,11},{10,... | collective-permute-start | bytes 1572872 | tf_op jit(solution)/shard_map/ppermute | solution.py:41
  106.3 24.1 %collective-permute-start.17 = (bf16[32,64,128]{2,1,0:T(8,128)(2,1)}, bf16[32,64,128]{2,1,0:T(8,128)(2,1)S(1)}, u32[]{:S(2)}, u32[]{:S(2)}) collective-permute-start(bf16[32,64,128]{2,1,0:T(8,128)(2,1)} %collective-permute-done.14.refs_1_), channel_id=1, source_target_pairs={{0,1},{1,0},{2,3},{3,2},{4,5},{5,4},{6,7},{7,6},{8,9},{9,8},{10,11... | collective-permute-start | bytes 1572872 | tf_op jit(solution)/shard_map/ppermute | solution.py:41
  109.7 17.0 %copy-start.15 = (bf16[129,16,128]{2,1,0:T(8,128)(2,1)S(1)}, bf16[129,16,128]{2,1,0:T(8,128)(2,1)}, u32[]{:S(2)}) copy-start(bf16[129,16,128]{2,1,0:T(8,128)(2,1)} %copy-done.14) | copy-start | bytes 1585156
  109.7 17.6 %copy-start.4 = (bf16[129,16,128]{2,1,0:T(8,128)(2,1)S(1)}, bf16[129,16,128]{2,1,0:T(8,128)(2,1)}, u32[]{:S(2)}) copy-start(bf16[129,16,128]{2,1,0:T(8,128)(2,1)} %copy-done.3) | copy-start | bytes 1585156
  109.7 26.6 %collective-permute-start.8 = (bf16[129,16,128]{2,1,0:T(8,128)(2,1)S(1)}, bf16[129,16,128]{2,1,0:T(8,128)(2,1)S(1)}, u32[]{:S(2)}, u32[]{:S(2)}) collective-permute-start(bf16[129,16,128]{2,1,0:T(8,128)(2,1)S(1)} %copy-done.17), channel_id=1, source_target_pairs={{0,14},{1,15},{2,12},{3,13},{4,10},{5,11},{6,8},{7,9},{8,6},{9,7},... | collective-permute-start | bytes 1585160 | tf_op jit(solution)/shard_map/ppermute | solution.py:41
  123.4 13.0 %collective-permute-start.16 = (bf16[32,64,128]{2,1,0:T(8,128)(2,1)S(1)}, bf16[32,64,128]{2,1,0:T(8,128)(2,1)S(1)}, u32[]{:S(2)}, u32[]{:S(2)}) collective-permute-start(bf16[32,64,128]{2,1,0:T(8,128)(2,1)S(1)} %collective-permute-done.15.refs_1_), channel_id=1, source_target_pairs={{0,1},{1,0},{2,3},{3,2},{4,5},{5,4},{6,7},{7,6},{8,9},{9,8},{10,11... | collective-permute-start | bytes 1572872 | tf_op jit(solution)/shard_map/ppermute | solution.py:41
  126.7 28.9 %collective-permute-start.4 = (bf16[129,16,128]{2,1,0:T(8,128)(2,1)S(1)}, bf16[129,16,128]{2,1,0:T(8,128)(2,1)S(1)}, u32[]{:S(2)}, u32[]{:S(2)}) collective-permute-start(bf16[129,16,128]{2,1,0:T(8,128)(2,1)S(1)} %copy-done.15), channel_id=1, source_target_pairs={{0,6},{1,7},{2,4},{3,5},{4,2},{5,3},{6,0},{7,1},{8,14},{9,15},{10,... | collective-permute-start | bytes 1585160 | tf_op jit(solution)/shard_map/ppermute | solution.py:41
  126.8 28.8 %collective-permute-start.11 = (bf16[32,64,128]{2,1,0:T(8,128)(2,1)S(1)}, bf16[32,64,128]{2,1,0:T(8,128)(2,1)S(1)}, u32[]{:S(2)}, u32[]{:S(2)}) collective-permute-start(bf16[32,64,128]{2,1,0:T(8,128)(2,1)S(1)} %collective-permute-done.10.refs_1_), channel_id=1, source_target_pairs={{0,1},{1,0},{2,3},{3,2},{4,5},{5,4},{6,7},{7,6},{8,9},{9,8},{10,11... | collective-permute-start | bytes 1572872 | tf_op jit(solution)/shard_map/ppermute | solution.py:41
  160.4 1.2 collective-permute-start.24
  161.7 3.7 %collective-permute-start.25 = (f32[16,128]{1,0:T(8,128)S(1)}, f32[16,128]{1,0:T(8,128)S(1)}, u32[]{:S(2)}, u32[]{:S(2)}) collective-permute-start(f32[16,128]{1,0:T(8,128)S(1)} %add.88), channel_id=1, source_target_pairs={{0,2},{1,3},{2,0},{3,1},{4,6},{5,7},{6,4},{7,5},{8,10},{9,11},{10,... | collective-permute-start | bytes 24584 | tf_op jit(solution)/shard_map/ppermute | solution.py:130
  165.3 7.1 %collective-permute-start.26 = (f32[16,128]{1,0:T(8,128)S(1)}, f32[16,128]{1,0:T(8,128)S(1)}, u32[]{:S(2)}, u32[]{:S(2)}) collective-permute-start(f32[16,128]{1,0:T(8,128)S(1)} %add.89), channel_id=1, source_target_pairs={{0,4},{1,5},{2,6},{3,7},{4,0},{5,1},{6,2},{7,3},{8,12},{9,13},{10,... | collective-permute-start | bytes 24584 | tf_op jit(solution)/shard_map/ppermute | solution.py:130
  172.4 4.5 %collective-permute-start.27 = (f32[16,128]{1,0:T(8,128)S(1)}, f32[16,128]{1,0:T(8,128)S(1)}, u32[]{:S(2)}, u32[]{:S(2)}) collective-permute-start(f32[16,128]{1,0:T(8,128)S(1)} %add.90), channel_id=1, source_target_pairs={{0,8},{1,9},{2,10},{3,11},{4,12},{5,13},{6,14},{7,15},{8,0},{9,1},... | collective-permute-start | bytes 24584 | tf_op jit(solution)/shard_map/ppermute | solution.py:130
  179.4 11.5 %collective-permute-start.28 = (bf16[32,64,128]{2,1,0:T(8,128)(2,1)}, bf16[32,64,128]{2,1,0:T(8,128)(2,1)S(1)}, u32[]{:S(2)}, u32[]{:S(2)}) collective-permute-start(bf16[32,64,128]{2,1,0:T(8,128)(2,1)} %get-tuple-element.20.refs_8_), channel_id=1, source_target_pairs={{0,4},{1,5},{2,0},{3,1},{4,8},{5,9},{6,2},{7,3},{8,12},{9,13},{10,... | collective-permute-start | bytes 1572872 | tf_op jit(solution)/shard_map/ppermute | solution.py:41
  181.4 12.3 %collective-permute-start.31 = (bf16[32,64,128]{2,1,0:T(8,128)(2,1)}, bf16[32,64,128]{2,1,0:T(8,128)(2,1)S(1)}, u32[]{:S(2)}, u32[]{:S(2)}) collective-permute-start(bf16[32,64,128]{2,1,0:T(8,128)(2,1)} %get-tuple-element.20.refs_8_), channel_id=1, source_target_pairs={{0,2},{1,3},{2,6},{3,7},{4,0},{5,1},{6,10},{7,11},{8,4},{9,5},{10,... | collective-permute-start | bytes 1572872 | tf_op jit(solution)/shard_map/ppermute | solution.py:41
  191.7 11.9 %collective-permute-start.29 = (bf16[32,64,128]{2,1,0:T(8,128)(2,1)S(1)}, bf16[32,64,128]{2,1,0:T(8,128)(2,1)}, u32[]{:S(2)}, u32[]{:S(2)}) collective-permute-start(bf16[32,64,128]{2,1,0:T(8,128)(2,1)S(1)} %collective-permute-done.28.refs_8_), channel_id=1, source_target_pairs={{0,4},{1,5},{2,0},{3,1},{4,8},{5,9},{6,2},{7,3},{8,12},{9,13},{10,... | collective-permute-start | bytes 1572872 | tf_op jit(solution)/shard_map/ppermute | solution.py:41
  193.7 9.9 %copy-start.22 = (bf16[32,64,128]{2,1,0:T(8,128)(2,1)}, bf16[32,64,128]{2,1,0:T(8,128)(2,1)S(1)}, u32[]{:S(2)}) copy-start(bf16[32,64,128]{2,1,0:T(8,128)(2,1)S(1)} %collective-permute-done.31.refs_10_) | copy-start | bytes 1572868
  193.8 11.9 %collective-permute-start.32 = (bf16[32,64,128]{2,1,0:T(8,128)(2,1)S(1)}, bf16[32,64,128]{2,1,0:T(8,128)(2,1)}, u32[]{:S(2)}, u32[]{:S(2)}) collective-permute-start(bf16[32,64,128]{2,1,0:T(8,128)(2,1)S(1)} %collective-permute-done.31.refs_10_), channel_id=1, source_target_pairs={{0,2},{1,3},{2,6},{3,7},{4,0},{5,1},{6,10},{7,11},{8,4},{9,5},{10,... | collective-permute-start | bytes 1572872 | tf_op jit(solution)/shard_map/ppermute | solution.py:41
  203.6 9.5 %collective-permute-start.30 = (bf16[32,64,128]{2,1,0:T(8,128)(2,1)}, bf16[32,64,128]{2,1,0:T(8,128)(2,1)}, u32[]{:S(2)}, u32[]{:S(2)}) collective-permute-start(bf16[32,64,128]{2,1,0:T(8,128)(2,1)} %collective-permute-done.29.refs_8_), channel_id=1, source_target_pairs={{0,4},{1,5},{2,0},{3,1},{4,8},{5,9},{6,2},{7,3},{8,12},{9,13},{10,... | collective-permute-start | bytes 1572872 | tf_op jit(solution)/shard_map/ppermute | solution.py:41
  205.6 9.5 %collective-permute-start.33 = (bf16[32,64,128]{2,1,0:T(8,128)(2,1)}, bf16[32,64,128]{2,1,0:T(8,128)(2,1)}, u32[]{:S(2)}, u32[]{:S(2)}) collective-permute-start(bf16[32,64,128]{2,1,0:T(8,128)(2,1)} %collective-permute-done.32.refs_10_), channel_id=1, source_target_pairs={{0,2},{1,3},{2,6},{3,7},{4,0},{5,1},{6,10},{7,11},{8,4},{9,5},{10,... | collective-permute-start | bytes 1572872 | tf_op jit(solution)/shard_map/ppermute | solution.py:41
  205.6 26.5 %collective-permute-start.42 = (bf16[32,64,128]{2,1,0:T(8,128)(2,1)}, bf16[32,64,128]{2,1,0:T(8,128)(2,1)}, u32[]{:S(2)}, u32[]{:S(2)}) collective-permute-start(bf16[32,64,128]{2,1,0:T(8,128)(2,1)} %get-tuple-element.20.refs_8_), channel_id=1, source_target_pairs={{0,1},{1,0},{2,3},{3,2},{4,5},{5,4},{6,7},{7,6},{8,9},{9,8},{10,11... | collective-permute-start | bytes 1572872 | tf_op jit(solution)/shard_map/ppermute | solution.py:41
  205.9 33.4 %collective-permute-start.40 = (bf16[32,64,128]{2,1,0:T(8,128)(2,1)}, bf16[32,64,128]{2,1,0:T(8,128)(2,1)}, u32[]{:S(2)}, u32[]{:S(2)}) collective-permute-start(bf16[32,64,128]{2,1,0:T(8,128)(2,1)} %copy-done.20), channel_id=1, source_target_pairs={{0,1},{1,0},{2,3},{3,2},{4,5},{5,4},{6,7},{7,6},{8,9},{9,8},{10,11... | collective-permute-start | bytes 1572872 | tf_op jit(solution)/shard_map/ppermute | solution.py:41
  206.2 33.2 %collective-permute-start.41 = (bf16[32,64,128]{2,1,0:T(8,128)(2,1)}, bf16[32,64,128]{2,1,0:T(8,128)(2,1)}, u32[]{:S(2)}, u32[]{:S(2)}) collective-permute-start(bf16[32,64,128]{2,1,0:T(8,128)(2,1)} %copy-done.22), channel_id=1, source_target_pairs={{0,1},{1,0},{2,3},{3,2},{4,5},{5,4},{6,7},{7,6},{8,9},{9,8},{10,11... | collective-permute-start | bytes 1572872 | tf_op jit(solution)/shard_map/ppermute | solution.py:41
  213.1 32.0 %collective-permute-start.38 = (bf16[32,64,128]{2,1,0:T(8,128)(2,1)}, bf16[32,64,128]{2,1,0:T(8,128)(2,1)}, u32[]{:S(2)}, u32[]{:S(2)}) collective-permute-start(bf16[32,64,128]{2,1,0:T(8,128)(2,1)} %collective-permute-done.29.refs_8_), channel_id=1, source_target_pairs={{0,1},{1,0},{2,3},{3,2},{4,5},{5,4},{6,7},{7,6},{8,9},{9,8},{10,11... | collective-permute-start | bytes 1572872 | tf_op jit(solution)/shard_map/ppermute | solution.py:41
  215.1 30.0 %collective-permute-start.39 = (bf16[32,64,128]{2,1,0:T(8,128)(2,1)}, bf16[32,64,128]{2,1,0:T(8,128)(2,1)}, u32[]{:S(2)}, u32[]{:S(2)}) collective-permute-start(bf16[32,64,128]{2,1,0:T(8,128)(2,1)} %collective-permute-done.32.refs_10_), channel_id=1, source_target_pairs={{0,1},{1,0},{2,3},{3,2},{4,5},{5,4},{6,7},{7,6},{8,9},{9,8},{10,11... | collective-permute-start | bytes 1572872 | tf_op jit(solution)/shard_map/ppermute | solution.py:41
  232.1 12.8 %collective-permute-start.34 = (bf16[32,64,128]{2,1,0:T(8,128)(2,1)}, bf16[32,64,128]{2,1,0:T(8,128)(2,1)S(1)}, u32[]{:S(2)}, u32[]{:S(2)}) collective-permute-start(bf16[32,64,128]{2,1,0:T(8,128)(2,1)} %shard_map.81), channel_id=1, source_target_pairs={{0,4},{1,3},{2,0},{3,7},{4,8},{5,1},{6,2},{7,11},{8,12},{9,5},{10,... | collective-permute-start | bytes 1572872 | tf_op jit(solution)/shard_map/ppermute | solution.py:41
  239.3 10.5 %collective-permute-start.36 = (bf16[32,64,128]{2,1,0:T(8,128)(2,1)}, bf16[32,64,128]{2,1,0:T(8,128)(2,1)S(1)}, u32[]{:S(2)}, u32[]{:S(2)}) collective-permute-start(bf16[32,64,128]{2,1,0:T(8,128)(2,1)} %collective-permute-done.30.lower_ref.refs_8_), channel_id=1, source_target_pairs={{0,1},{1,0},{2,3},{3,2},{4,5},{5,4},{6,7},{7,6},{8,9},{9,8},{10,11... | collective-permute-start | bytes 1572872 | tf_op jit(solution)/shard_map/ppermute | solution.py:41
  239.4 10.4 %collective-permute-start.37 = (bf16[32,64,128]{2,1,0:T(8,128)(2,1)}, bf16[32,64,128]{2,1,0:T(8,128)(2,1)S(1)}, u32[]{:S(2)}, u32[]{:S(2)}) collective-permute-start(bf16[32,64,128]{2,1,0:T(8,128)(2,1)} %collective-permute-done.33.upper_ref.refs_10_), channel_id=1, source_target_pairs={{0,1},{1,0},{2,3},{3,2},{4,5},{5,4},{6,7},{7,6},{8,9},{9,8},{10,11... | collective-permute-start | bytes 1572872 | tf_op jit(solution)/shard_map/ppermute | solution.py:41
  245.0 9.9 %collective-permute-start.35 = (bf16[32,64,128]{2,1,0:T(8,128)(2,1)S(1)}, bf16[32,64,128]{2,1,0:T(8,128)(2,1)S(1)}, u32[]{:S(2)}, u32[]{:S(2)}) collective-permute-start(bf16[32,64,128]{2,1,0:T(8,128)(2,1)S(1)} %collective-permute-done.34.refs_8_), channel_id=1, source_target_pairs={{0,1},{1,0},{2,3},{3,2},{4,5},{5,4},{6,7},{7,6},{8,9},{9,8},{10,11... | collective-permute-start | bytes 1572872 | tf_op jit(solution)/shard_map/ppermute | solution.py:41
  (21 other events, 44.1 us)

commit v5 on v4

--- a/solution.py
+++ b/solution.py
@@ -57,38 +57,21 @@
     )
 
 
-def select_kernel(half_ref, lower_ref, upper_ref, out_ref, sem):
-    for half, source in enumerate((lower_ref, upper_ref)):
-
-        @pl.when(half_ref[0] == half)
-        def _():
-            copy = pltpu.make_async_copy(source, out_ref, sem)
-            copy.start()
-            copy.wait()
-
-
-def select_half(half, lower, upper):
+def select_kernel(half_ref, lower_ref, upper_ref, *rest):
+    out_ref = rest[-1]
+    out_ref[...] = jnp.where(half_ref[0] == 0, lower_ref[...], upper_ref[...])
+
+
+def select_half(half, lower, upper, *others):
     anywhere = pl.BlockSpec(memory_space=pl.ANY)
+    whole = pl.BlockSpec(memory_space=pltpu.VMEM)
     return pl.pallas_call(
         select_kernel,
         out_shape=jax.ShapeDtypeStruct(lower.shape, lower.dtype),
-        in_specs=[pl.BlockSpec(memory_space=pltpu.SMEM), anywhere, anywhere],
-        out_specs=anywhere,
-        scratch_shapes=[pltpu.SemaphoreType.DMA],
+        in_specs=[pl.BlockSpec(memory_space=pltpu.SMEM), whole, whole] + [anywhere] * len(others),
+        out_specs=whole,
         cost_estimate=busy(0.8),
-    )(jnp.reshape(half, (1,)).astype(jnp.int32), lower, upper)
-
-
-def ring_gather(unit, owners, halves, half):
-    units = {0: unit}
-    reach = (owners - 1) // 2
-    for step in range(1, reach + 1):
-        units[step] = ring_send(units[step - 1], owners, halves, (1,) * halves)
-        units[-step] = ring_send(units[1 - step], owners, halves, (-1,) * halves)
-    if owners % 2 == 0:
-        last = select_half(half, units[reach], units[-reach])
-        units[owners // 2] = ring_send(last, owners, halves, (1, -1))
-    return units
+    )(jnp.reshape(half, (1,)).astype(jnp.int32), lower, upper, *others)
 
 
 def after_kernel(*refs):
@@ -116,7 +99,7 @@
         units[step] = exchange(unit, owners, halves, step)
         step //= 2
     for mask in masks[:-1]:
-        units[mask] = after(units[mask], lefts[mask])
+        units[mask] = after(units[mask], lefts[masks[0]])
     for step in masks[1:]:
         for mask in [m for m in units if m >= 2 * step and m % (2 * step) == 0]:
             units[mask | step] = exchange(units[mask], owners, halves, step)
@@ -135,7 +118,7 @@
 
 
 def pack_kernel(order, capacity, blocks, terms, ids_ref, plan_ref, other_plan_ref, *refs):
-    left_ref, other_ref, *pieces, codes, seen, built, sems = refs
+    left_ref, other_ref, _, *pieces, codes, seen, built, sems = refs
     owners = len(order)
     me, half = ids_ref[0], ids_ref[1]
     rows, width = other_ref.shape[2:]
@@ -190,7 +173,7 @@
         copy.wait()
 
 
-def pack(ids, plan, other_plan, left, other, order, capacity):
+def pack(ids, plan, other_plan, left, other, before, order, capacity):
     terms, blocks, rows, width = other.shape
     owners = len(order)
     scalars = pl.BlockSpec(memory_space=pltpu.SMEM)
@@ -200,7 +183,7 @@
     return pl.pallas_call(
         functools.partial(pack_kernel, order, capacity, blocks, terms),
         out_shape=[jax.ShapeDtypeStruct(shape, jnp.bfloat16)] * owners,
-        in_specs=[scalars] * 3 + [whole, whole],
+        in_specs=[scalars] * 3 + [whole, whole, anywhere],
         out_specs=[anywhere] * owners,
         scratch_shapes=[
             pltpu.SMEM((2, owners, 2 * terms * capacity), jnp.int32),
@@ -210,7 +193,7 @@
         ],
         compiler_params=pltpu.CompilerParams(vmem_limit_bytes=VMEM_LIMIT),
         cost_estimate=busy(5.0),
-    )(ids, plan, other_plan, left, other)
+    )(ids, plan, other_plan, left, other, before)
 
 
 def busy(microseconds):
@@ -412,19 +395,22 @@
     other_left = swap(
         lax.dynamic_slice_in_dim(left_operator, (1 - half) * rows, rows, 2), owners, halves
     )
-    order = [m for pair in zip(range(owners // 2), range(owners // 2, owners)) for m in pair]
-    order = order[:-2] + order[-1:] + order[-2:-1]
+    far_pieces = list(range(owners // 2, owners))
+    order = [0, far_pieces[0]]
+    for m in range(1, owners // 2):
+        order += [far_pieces[m], m]
+    rights = (right_operator, swap(right_operator, owners, halves))
     pieces = pack(
         ids,
         plan,
         swap(plan, owners, halves),
         left_operator,
         other_left,
+        rights[1],
         order[1:] + order[:1],
         capacity,
     )
     lefts = [exchange(piece, owners, halves, m) if m else piece for m, piece in enumerate(pieces)]
-    rights = (right_operator, swap(right_operator, owners, halves))
     near = mask_gather(own_rows, lefts, owners, halves)
     far = {m: swap(unit, owners, halves) if m else other_rows for m, unit in near.items()}
 
@@ -437,24 +423,28 @@
 
     entries = blocks * owners * height * width
     direction, rayleigh = new_direction(ids, total, own_rows, owners, halves, entries)
-    near = ring_gather(direction, owners, halves, half)
-    far = {s: swap(unit, owners, halves) for s, unit in near.items()}
     reach = (owners - 1) // 2
-    groups = [[0]] + [[step, -step] for step in range(1, reach + 1)]
-    if owners % 2 == 0:
-        groups.append([owners // 2])
+
+    def add_group(total, units, last):
+        choice = jnp.stack([ring_owner(place - s, owners) ^ me for s in units])
+        vectors = [
+            (unit, swap(unit, owners, halves)) for unit in units.values()
+        ]
+        return apply_group(choice.astype(jnp.int32), lefts, vectors, rights, total, True, last)
+
+    ahead = behind = direction
+    units = {0: direction}
     total = None
-    for group in groups:
-        choice = jnp.stack([ring_owner(place - s, owners) ^ me for s in group])
-        total = apply_group(
-            choice.astype(jnp.int32),
-            lefts,
-            [(near[s], far[s]) for s in group],
-            rights,
-            total,
-            True,
-            group is groups[-1],
-        )
+    for step in range(1, reach + 1):
+        ahead_next = ring_send(ahead, owners, halves, (1,) * halves)
+        behind_next = ring_send(behind, owners, halves, (-1,) * halves)
+        total = add_group(total, units, False)
+        ahead, behind = after(ahead_next, total), behind_next
+        units = {step: ahead, -step: behind}
+    last = select_half(half, ahead, behind)
+    last = ring_send(last, owners, halves, (1, -1))
+    total = add_group(total, units, False)
+    total = add_group(total, {owners // 2: after(last, total)}, True)
     return (total, rayleigh[0])
 
 

time: 260 us -> 264 us (1.015)
  local copies, waits for them, and re-layouts: 16.5 us -> 57.5 us
  Pallas kernels: 72.8 us -> 46.6 us
  starting transfers between devices: 53.6 us -> 38.7 us
  waiting for transfers between devices: 114 us -> 118 us
    unnamed x52 -> x122, local copies, waits for them, and re-layouts: 11.8 us -> 53.1 us
    pallas_call x1, Pallas kernels: 17 us -> 2.13 us  [select_half(): pl.pallas_call(select_kernel, out_shape=jax.ShapeDtypeStruct(lower.shape,...]
    ppermute x39, starting transfers between devices: 45.1 us -> 31 us  [permute(): return lax.ppermute(value, BOTH, pairs)]
    pallas_call x13, Pallas kernels: 47.8 us -> 36.6 us  [apply_group(): pl.pallas_call(functools.partial(apply_kernel, sources, first, len(lefts)...]
    ppermute x39, waiting for transfers between devices: 106 us -> 110 us  [permute(): return lax.ppermute(value, BOTH, pairs)]
  transfers between devices with their start and end apart: 43 -> 43, of which waited for: 16 -> 20; matrix products, arithmetic and copies ran while one was open for 1% -> 2% of each run, Pallas kernels for 24% -> 15%
where the time goes in v5:
time: 264 us; the launch traced here: 262 us
  waiting for transfers between devices  118 us (45%)
  local copies, waits for them, and re-layouts  57.5 us (22%)
  Pallas kernels  46.6 us (18%)
  starting transfers between devices  38.7 us (15%)
    ppermute x39, waiting for transfers between devices, permute(): return lax.ppermute(value, BOTH, pairs)  110 us
    unnamed x122, local copies, waits for them, and re-layouts  53.1 us
    pallas_call x13, Pallas kernels, apply_group(): pl.pallas_call(functools.partial(apply_kernel, sources, first, len(lefts)...  36.6 us
    ppermute x39, starting transfers between devices, permute(): return lax.ppermute(value, BOTH, pairs)  31 us
    ppermute x4, waiting for transfers between devices, doubled(): lax.ppermute(value, axes, [(d, d ^ step * stride) for d in range(total)])  7.9 us
    ppermute x4, starting transfers between devices, doubled(): lax.ppermute(value, axes, [(d, d ^ step * stride) for d in range(total)])  7.68 us
    pallas_call x1, Pallas kernels, pack(): pl.pallas_call(functools.partial(pack_kernel, order, capacity, blocks, te...  5.33 us
  transfers between devices with their start and end apart: 43, of which 20 were waited for; matrix products, arithmetic and copies ran while one was open for 2% of the time, Pallas kernels for 15%

profile of v5, /device:TPU:0, one launch (start us, length us, event | category | flops | bytes accessed | tf_op | source)
XLA Modules:
  0.0 262.4 jit_solution(8155258178690475901)
XLA Ops:
  1.2 2.3 constant_dynamic-slice_fusion.2
  4.0 2.1 constant_dynamic-slice_fusion
  6.1 2.5 collective-permute-start.19
  10.3 5.3 %shard_map.68 = (bf16[129,16,128]{2,1,0:T(8,128)(2,1)S(1)}, bf16[129,16,128]{2,1,0:T(8,128)(2,1)S(1)}, bf16[129,16,128]{2,1,0:T(8,128)(2,1)S(1)}, bf16[129,16,12...) custom-call(s32[3]{0:T(128)S(1)} %pad_add_fusion.1.ids_ref, ...), custom_call_target="tpu_custom_call" | custom-call | flops 5750000128 | tf_op jit(solution)/shard_map/pallas_call | solution.py:183
  18.1 2.6 collective-permute-start.6
  22.6 3.0 %collective-permute-start.7 = (bf16[129,16,128]{2,1,0:T(8,128)(2,1)}, bf16[129,16,128]{2,1,0:T(8,128)(2,1)S(1)}, u32[]{:S(2)}, u32[]{:S(2)}) collective-permute-start(bf16[129,16,128]{2,1,0:T(8,128)(2,1)} %get-tuple-element.17), channel_id=1, source_target_pairs={{0,10},{1,11},{2,8},{3,9},{4,14},{5,15},{6,12},{7,13},{8,2},{9,3},... | collective-permute-start | bytes 1585160 | tf_op jit(solution)/shard_map/ppermute | solution.py:41
  25.6 53.5 %collective-permute-done.13.refs_0_ = bf16[32,64,128]{2,1,0:T(8,128)(2,1)} collective-permute-done((bf16[32,64,128]{2,1,0:T(8,128)(2,1)S(1)}, bf16[32,64,128]{2,1,0:T(8,128)(2,1)}, u32[]{:S(2)}, u32[]{:S(2)}) %collective-permute-start.13) | collective-permute-done | bytes 524320 | tf_op jit(solution)/shard_map/ppermute | solution.py:41
  82.0 2.9 %collective-permute-start.8 = (bf16[129,16,128]{2,1,0:T(8,128)(2,1)}, bf16[129,16,128]{2,1,0:T(8,128)(2,1)}, u32[]{:S(2)}, u32[]{:S(2)}) collective-permute-start(bf16[129,16,128]{2,1,0:T(8,128)(2,1)} %copy-done.57), channel_id=1, source_target_pairs={{0,12},{1,13},{2,14},{3,15},{4,8},{5,9},{6,10},{7,11},{8,4},{9,5},... | collective-permute-start | bytes 1585160 | tf_op jit(solution)/shard_map/ppermute | solution.py:41
  84.9 5.9 %collective-permute-done.7.refs_0_.refs_5_ = bf16[129,16,128]{2,1,0:T(8,128)(2,1)S(1)} collective-permute-done((bf16[129,16,128]{2,1,0:T(8,128)(2,1)}, bf16[129,16,128]{2,1,0:T(8,128)(2,1)S(1)}, u32[]{:S(2)}, u32[]{:S(2)}) %collective-permute-start.7) | collective-permute-done | bytes 528416 | tf_op jit(solution)/shard_map/ppermute | solution.py:41
  91.6 9.8 %collective-permute-done.21.refs_1_ = bf16[32,64,128]{2,1,0:T(8,128)(2,1)} collective-permute-done((bf16[32,64,128]{2,1,0:T(8,128)(2,1)}, bf16[32,64,128]{2,1,0:T(8,128)(2,1)}, u32[]{:S(2)}, u32[]{:S(2)}) %collective-permute-start.21) | collective-permute-done | bytes 524320 | tf_op jit(solution)/shard_map/ppermute | solution.py:41
  101.4 11.0 %collective-permute-done.3.refs_0_.refs_1_ = bf16[129,16,128]{2,1,0:T(8,128)(2,1)S(1)} collective-permute-done((bf16[129,16,128]{2,1,0:T(8,128)(2,1)}, bf16[129,16,128]{2,1,0:T(8,128)(2,1)S(1)}, u32[]{:S(2)}, u32[]{:S(2)}) %collective-permute-start.3) | collective-permute-done | bytes 528416 | tf_op jit(solution)/shard_map/ppermute | solution.py:41
  114.4 1.6 copy-done.10
  116.0 1.6 copy-done.20
  121.1 1.6 copy-done.11
  122.7 1.6 copy-done.21
  124.3 2.6 shard_map.72.refs_5_
  127.4 1.6 copy-done.12
  130.1 2.5 shard_map.73.refs_5_
  132.6 4.1 %collective-permute-start.9 = (bf16[129,16,128]{2,1,0:T(8,128)(2,1)S(1)}, bf16[129,16,128]{2,1,0:T(8,128)(2,1)S(1)}, u32[]{:S(2)}, u32[]{:S(2)}) collective-permute-start(bf16[129,16,128]{2,1,0:T(8,128)(2,1)S(1)} %copy-done.55), channel_id=1, source_target_pairs={{0,14},{1,15},{2,12},{3,13},{4,10},{5,11},{6,8},{7,9},{8,6},{9,7},... | collective-permute-start | bytes 1585160 | tf_op jit(solution)/shard_map/ppermute | solution.py:41
  136.8 2.5 shard_map.74.refs_5_
  139.3 16.2 %collective-permute-done.11.refs_1_ = bf16[32,64,128]{2,1,0:T(8,128)(2,1)S(1)} collective-permute-done((bf16[32,64,128]{2,1,0:T(8,128)(2,1)}, bf16[32,64,128]{2,1,0:T(8,128)(2,1)S(1)}, u32[]{:S(2)}, u32[]{:S(2)}) %collective-permute-start.11) | collective-permute-done | bytes 524320 | tf_op jit(solution)/shard_map/ppermute | solution.py:41
  155.6 2.7 %shard_map.75.refs_5_ = f32[33,64,128]{2,1,0:T(8,128)S(1)} custom-call(s32[1]{0:T(128)} %constant.94.clone.1.ids_ref, bf16[129,16,128]{2,1,0:T(8,128)(2,1)} %collective-permute-done.8.refs_0_.refs_6_, bf16[32,64,128]{2,1,0:T(8,128)(2,1)} %collective-permute-done.14.refs_1_, ...), custom_call_target="tpu_custom_call", output_to_operand_aliasing={{}: (6, {})} | custom-call | flops 2415000064 | tf_op jit(solution)/shard_map/pallas_call | solution.py:304
  158.3 2.5 shard_map.76.refs_5_
  160.8 2.6 shard_map.77.refs_5_
  163.4 5.8 %collective-permute-done.5.refs_0_.refs_3_ = bf16[129,16,128]{2,1,0:T(8,128)(2,1)S(1)} collective-permute-done((bf16[129,16,128]{2,1,0:T(8,128)(2,1)S(1)}, bf16[129,16,128]{2,1,0:T(8,128)(2,1)S(1)}, u32[]{:S(2)}, u32[]{:S(2)}) %collective-permute-start.5) | collective-permute-done | bytes 528416 | tf_op jit(solution)/shard_map/ppermute | solution.py:41
  174.0 2.7 %collective-permute-done.25 = f32[16,128]{1,0:T(8,128)S(1)} collective-permute-done((f32[16,128]{1,0:T(8,128)S(1)}, f32[16,128]{1,0:T(8,128)S(1)}, u32[]{:S(2)}, u32[]{:S(2)}) %collective-permute-start.25) | collective-permute-done | bytes 8224 | tf_op jit(solution)/shard_map/ppermute | solution.py:113
  176.7 4.5 %collective-permute-start.26 = (f32[16,128]{1,0:T(8,128)S(1)}, f32[16,128]{1,0:T(8,128)S(1)}, u32[]{:S(2)}, u32[]{:S(2)}) collective-permute-start(f32[16,128]{1,0:T(8,128)S(1)} %add.89), channel_id=1, source_target_pairs={{0,4},{1,5},{2,6},{3,7},{4,0},{5,1},{6,2},{7,3},{8,12},{9,13},{10,... | collective-permute-start | bytes 24584 | tf_op jit(solution)/shard_map/ppermute | solution.py:113
  181.2 1.6 collective-permute-done.26
  182.9 2.1 collective-permute-start.27
  185.0 2.4 collective-permute-done.27
  188.8 2.0 collective-permute-start.28
  190.9 1.6 copy-done.14
  192.5 1.6 copy-done.22
  198.3 2.7 %shard_map.81.refs_1_.refs_14_ = f32[33,64,128]{2,1,0:T(8,128)S(1)} custom-call(s32[1]{0:T(128)} %bitcast.6.ids_ref, bf16[129,16,128]{2,1,0:T(8,128)(2,1)S(1)} %get-tuple-element.12.refs_0_, bf16[129,16,128]{2,1,0:T(8,128)(2,1)S(1)} %copy-done.33, bf16[129,16,128]{2,1,0:T(8,128)(2,1)} %collective-permute-done.4.refs_0_.refs_2_, ...), custom_call_target="tpu_custom_call" | custom-call | flops 2415000064 | tf_op jit(solution)/shard_map/pallas_call | solution.py:304
  203.5 1.7 collective-permute-done.32.refs_10_
  207.5 1.6 copy-done.15
  209.0 1.6 copy-done.23
  213.8 4.1 %shard_map.83.refs_1_.refs_14_ = f32[33,64,128]{2,1,0:T(8,128)S(1)} custom-call(s32[2]{0:T(128)S(1)} %pad_add_fusion.2.ids_ref, bf16[129,16,128]{2,1,0:T(8,128)(2,1)S(1)} %get-tuple-element.12.refs_0_, bf16[129,16,128]{2,1,0:T(8,128)(2,1)S(1)} %copy-done.34, ...), custom_call_target="tpu_custom_call", output_to_operand_aliasing={{}: (15, {})} | custom-call | flops 4024999936 | tf_op jit(solution)/shard_map/pallas_call | solution.py:304
  222.9 1.6 copy-done.16
  224.5 1.6 copy-done.24
  229.2 3.9 %shard_map.85.refs_1_.refs_14_ = f32[33,64,128]{2,1,0:T(8,128)S(1)} custom-call(s32[2]{0:T(128)S(1)} %pad_add_fusion.3.ids_ref, bf16[129,16,128]{2,1,0:T(8,128)(2,1)S(1)} %get-tuple-element.12.refs_0_, bf16[129,16,128]{2,1,0:T(8,128)(2,1)S(1)} %copy-done.35, ...), custom_call_target="tpu_custom_call", output_to_operand_aliasing={{}: (15, {})} | custom-call | flops 4024999936 | tf_op jit(solution)/shard_map/pallas_call | solution.py:304
  235.4 2.1 shard_map.87
  240.0 1.6 copy-done.25
  244.7 4.2 %shard_map.88.refs_1_.refs_12_ = f32[33,64,128]{2,1,0:T(8,128)S(1)} custom-call(s32[2]{0:T(128)S(1)} %pad_add_fusion.4.ids_ref, bf16[129,16,128]{2,1,0:T(8,128)(2,1)S(1)} %get-tuple-element.12.refs_0_, bf16[129,16,128]{2,1,0:T(8,128)(2,1)S(1)} %copy-done.36, ...), custom_call_target="tpu_custom_call", output_to_operand_aliasing={{}: (15, {})} | custom-call | flops 4024999936 | tf_op jit(solution)/shard_map/pallas_call | solution.py:304
  250.6 1.9 collective-permute-done.42.refs_9_
  252.5 1.6 copy-done.18
  254.1 1.6 copy-done.26
  258.8 3.5 %shard_map.90 = bf16[32,64,128]{2,1,0:T(8,128)(2,1)} custom-call(s32[1]{0:T(128)} %bitcast.ids_ref, bf16[129,16,128]{2,1,0:T(8,128)(2,1)S(1)} %get-tuple-element.12.refs_0_, bf16[129,16,128]{2,1,0:T(8,128)(2,1)S(1)} %copy-done.37, bf16[129,16,128]{2,1,0:T(8,128)(2,1)} %collective-permute-done.4.refs_0_.refs_2_, bf16[129,16,128]{2,1,0:T(8,128)(2,1)S(1)} %copy-done.49, ...), custom_call_target="tpu_custom_call" | custom-call | flops 2415000064 | tf_op jit(solution)/shard_map/pallas_call | solution.py:304
  (194 shorter events, 56.8 us)
Async XLA Ops:
  0.6 8.1 %collective-permute-start.2 = (bf16[2,32,128,128]{3,2,1,0:T(8,128)(2,1)}, bf16[2,32,128,128]{3,2,1,0:T(8,128)(2,1)S(1)}, u32[]{:S(2)}, u32[]{:S(2)}) collective-permute-start(bf16[2,32,128,128]{3,2,1,0:T(8,128)(2,1)} %refs_10_.3), channel_id=1, source_target_pairs={{0,1},{1,0},{2,3},{3,2},{4,5},{5,4},{6,7},{7,6},{8,9},{9,8},{10,11... | collective-permute-start | bytes 6291464 | tf_op jit(solution)/shard_map/ppermute | solution.py:41
  3.4 5.3 %collective-permute-start.1 = (bf16[2,32,64,128]{3,2,1,0:T(8,128)(2,1)}, bf16[2,32,64,128]{3,2,1,0:T(8,128)(2,1)}, u32[]{:S(2)}, u32[]{:S(2)}) collective-permute-start(bf16[2,32,64,128]{3,2,1,0:T(8,128)(2,1)} %constant_dynamic-slice_fusion.2), channel_id=1, source_target_pairs={{0,1},{1,0},{2,3},{3,2},{4,5},{5,4},{6,7},{7,6},{8,9},{9,8},{10,11... | collective-permute-start | bytes 3145736 | tf_op jit(solution)/shard_map/ppermute | solution.py:41
  3.5 5.2 %collective-permute-start = (s32[2,2,32]{2,1,0:T(2,128)S(1)}, s32[2,2,32]{2,1,0:T(2,128)S(1)}, u32[]{:S(2)}, u32[]{:S(2)}) collective-permute-start(s32[2,2,32]{2,1,0:T(2,128)S(1)} %pad_add_fusion.plan_ref), channel_id=1, source_target_pairs={{0,1},{1,0},{2,3},{3,2},{4,5},{5,4},{6,7},{7,6},{8,9},{9,8},{10,11... | collective-permute-start | bytes 1544 | tf_op jit(solution)/shard_map/ppermute | solution.py:41
  6.1 16.5 %collective-permute-start.19 = (bf16[32,64,128]{2,1,0:T(8,128)(2,1)S(1)}, bf16[32,64,128]{2,1,0:T(8,128)(2,1)}, u32[]{:S(2)}, u32[]{:S(2)}) collective-permute-start(bf16[32,64,128]{2,1,0:T(8,128)(2,1)S(1)} %get-tuple-element.23.refs_1_.wave_ref), channel_id=1, source_target_pairs={{0,2},{1,3},{2,0},{3,1},{4,6},{5,7},{6,4},{7,5},{8,10},{9,11},{10,... | collective-permute-start | bytes 1572872 | tf_op jit(solution)/shard_map/ppermute | solution.py:41
  18.1 61.0 %copy-start.56 = (bf16[129,16,128]{2,1,0:T(8,128)(2,1)}, bf16[129,16,128]{2,1,0:T(8,128)(2,1)S(1)}, u32[]{:S(2)}) copy-start(bf16[129,16,128]{2,1,0:T(8,128)(2,1)S(1)} %get-tuple-element.14) | copy-start | bytes 1585156
  18.1 61.0 %copy-start.57 = (bf16[129,16,128]{2,1,0:T(8,128)(2,1)}, bf16[129,16,128]{2,1,0:T(8,128)(2,1)S(1)}, u32[]{:S(2)}) copy-start(bf16[129,16,128]{2,1,0:T(8,128)(2,1)S(1)} %get-tuple-element.18) | copy-start | bytes 1585156
  18.1 61.0 %collective-permute-start.6 = (bf16[129,16,128]{2,1,0:T(8,128)(2,1)S(1)}, bf16[129,16,128]{2,1,0:T(8,128)(2,1)S(1)}, u32[]{:S(2)}, u32[]{:S(2)}) collective-permute-start(bf16[129,16,128]{2,1,0:T(8,128)(2,1)S(1)} %get-tuple-element.16), channel_id=1, source_target_pairs={{0,8},{1,9},{2,10},{3,11},{4,12},{5,13},{6,14},{7,15},{8,0},{9,1},... | collective-permute-start | bytes 1585160 | tf_op jit(solution)/shard_map/ppermute | solution.py:41
  20.7 58.4 %collective-permute-start.13 = (bf16[32,64,128]{2,1,0:T(8,128)(2,1)S(1)}, bf16[32,64,128]{2,1,0:T(8,128)(2,1)}, u32[]{:S(2)}, u32[]{:S(2)}) collective-permute-start(bf16[32,64,128]{2,1,0:T(8,128)(2,1)S(1)} %get-tuple-element.23.refs_1_.wave_ref), channel_id=1, source_target_pairs={{0,8},{1,9},{2,10},{3,11},{4,12},{5,13},{6,14},{7,15},{8,0},{9,1},... | collective-permute-start | bytes 1572872 | tf_op jit(solution)/shard_map/ppermute | solution.py:41
  21.0 60.9 %collective-permute-start.10 = (bf16[32,64,128]{2,1,0:T(8,128)(2,1)S(1)}, bf16[32,64,128]{2,1,0:T(8,128)(2,1)}, u32[]{:S(2)}, u32[]{:S(2)}) collective-permute-start(bf16[32,64,128]{2,1,0:T(8,128)(2,1)S(1)} %get-tuple-element.23.refs_1_.wave_ref), channel_id=1, source_target_pairs={{0,4},{1,5},{2,6},{3,7},{4,0},{5,1},{6,2},{7,3},{8,12},{9,13},{10,... | collective-permute-start | bytes 1572872 | tf_op jit(solution)/shard_map/ppermute | solution.py:41
  22.6 59.4 %collective-permute-start.20 = (bf16[32,64,128]{2,1,0:T(8,128)(2,1)}, bf16[32,64,128]{2,1,0:T(8,128)(2,1)}, u32[]{:S(2)}, u32[]{:S(2)}) collective-permute-start(bf16[32,64,128]{2,1,0:T(8,128)(2,1)} %collective-permute-done.19.refs_1_), channel_id=1, source_target_pairs={{0,1},{1,0},{2,3},{3,2},{4,5},{5,4},{6,7},{7,6},{8,9},{9,8},{10,11... | collective-permute-start | bytes 1572872 | tf_op jit(solution)/shard_map/ppermute | solution.py:41
  22.6 68.1 %collective-permute-start.7 = (bf16[129,16,128]{2,1,0:T(8,128)(2,1)}, bf16[129,16,128]{2,1,0:T(8,128)(2,1)S(1)}, u32[]{:S(2)}, u32[]{:S(2)}) collective-permute-start(bf16[129,16,128]{2,1,0:T(8,128)(2,1)} %get-tuple-element.17), channel_id=1, source_target_pairs={{0,10},{1,11},{2,8},{3,9},{4,14},{5,15},{6,12},{7,13},{8,2},{9,3},... | collective-permute-start | bytes 1585160 | tf_op jit(solution)/shard_map/ppermute | solution.py:41
  79.9 21.5 %collective-permute-start.21 = (bf16[32,64,128]{2,1,0:T(8,128)(2,1)}, bf16[32,64,128]{2,1,0:T(8,128)(2,1)}, u32[]{:S(2)}, u32[]{:S(2)}) collective-permute-start(bf16[32,64,128]{2,1,0:T(8,128)(2,1)} %shard_map.70.refs_1_), channel_id=1, source_target_pairs={{0,2},{1,3},{2,0},{3,1},{4,6},{5,7},{6,4},{7,5},{8,10},{9,11},{10,... | collective-permute-start | bytes 1572872 | tf_op jit(solution)/shard_map/ppermute | solution.py:41
  80.9 31.6 %collective-permute-start.3 = (bf16[129,16,128]{2,1,0:T(8,128)(2,1)}, bf16[129,16,128]{2,1,0:T(8,128)(2,1)S(1)}, u32[]{:S(2)}, u32[]{:S(2)}) collective-permute-start(bf16[129,16,128]{2,1,0:T(8,128)(2,1)} %copy-done.58), channel_id=1, source_target_pairs={{0,2},{1,3},{2,0},{3,1},{4,6},{5,7},{6,4},{7,5},{8,10},{9,11},{10,... | collective-permute-start | bytes 1585160 | tf_op jit(solution)/shard_map/ppermute | solution.py:41
  82.0 31.3 %collective-permute-start.14 = (bf16[32,64,128]{2,1,0:T(8,128)(2,1)}, bf16[32,64,128]{2,1,0:T(8,128)(2,1)}, u32[]{:S(2)}, u32[]{:S(2)}) collective-permute-start(bf16[32,64,128]{2,1,0:T(8,128)(2,1)} %shard_map.70.refs_1_), channel_id=1, source_target_pairs={{0,4},{1,5},{2,6},{3,7},{4,0},{5,1},{6,2},{7,3},{8,12},{9,13},{10,... | collective-permute-start | bytes 1572872 | tf_op jit(solution)/shard_map/ppermute | solution.py:41
  82.0 38.1 %collective-permute-start.8 = (bf16[129,16,128]{2,1,0:T(8,128)(2,1)}, bf16[129,16,128]{2,1,0:T(8,128)(2,1)}, u32[]{:S(2)}, u32[]{:S(2)}) collective-permute-start(bf16[129,16,128]{2,1,0:T(8,128)(2,1)} %copy-done.57), channel_id=1, source_target_pairs={{0,12},{1,13},{2,14},{3,15},{4,8},{5,9},{6,10},{7,11},{8,4},{9,5},... | collective-permute-start | bytes 1585160 | tf_op jit(solution)/shard_map/ppermute | solution.py:41
  91.6 29.4 %collective-permute-start.23 = (bf16[32,64,128]{2,1,0:T(8,128)(2,1)}, bf16[32,64,128]{2,1,0:T(8,128)(2,1)}, u32[]{:S(2)}, u32[]{:S(2)}) collective-permute-start(bf16[32,64,128]{2,1,0:T(8,128)(2,1)} %shard_map.70.refs_1_), channel_id=1, source_target_pairs={{0,1},{1,0},{2,3},{3,2},{4,5},{5,4},{6,7},{7,6},{8,9},{9,8},{10,11... | collective-permute-start | bytes 1572872 | tf_op jit(solution)/shard_map/ppermute | solution.py:41
  101.4 25.5 %collective-permute-start.22 = (bf16[32,64,128]{2,1,0:T(8,128)(2,1)}, bf16[32,64,128]{2,1,0:T(8,128)(2,1)}, u32[]{:S(2)}, u32[]{:S(2)}) collective-permute-start(bf16[32,64,128]{2,1,0:T(8,128)(2,1)} %collective-permute-done.21.refs_1_), channel_id=1, source_target_pairs={{0,1},{1,0},{2,3},{3,2},{4,5},{5,4},{6,7},{7,6},{8,9},{9,8},{10,11... | collective-permute-start | bytes 1572872 | tf_op jit(solution)/shard_map/ppermute | solution.py:41
  113.3 19.3 %collective-permute-start.4 = (bf16[129,16,128]{2,1,0:T(8,128)(2,1)}, bf16[129,16,128]{2,1,0:T(8,128)(2,1)}, u32[]{:S(2)}, u32[]{:S(2)}) collective-permute-start(bf16[129,16,128]{2,1,0:T(8,128)(2,1)} %copy-done.56), channel_id=1, source_target_pairs={{0,4},{1,5},{2,6},{3,7},{4,0},{5,1},{6,2},{7,3},{8,12},{9,13},{10,... | collective-permute-start | bytes 1585160 | tf_op jit(solution)/shard_map/ppermute | solution.py:41
  113.3 23.5 %collective-permute-start.15 = (bf16[32,64,128]{2,1,0:T(8,128)(2,1)}, bf16[32,64,128]{2,1,0:T(8,128)(2,1)}, u32[]{:S(2)}, u32[]{:S(2)}) collective-permute-start(bf16[32,64,128]{2,1,0:T(8,128)(2,1)} %collective-permute-done.14.refs_1_), channel_id=1, source_target_pairs={{0,2},{1,3},{2,0},{3,1},{4,6},{5,7},{6,4},{7,5},{8,10},{9,11},{10,... | collective-permute-start | bytes 1572872 | tf_op jit(solution)/shard_map/ppermute | solution.py:41
  120.1 35.4 %collective-permute-start.11 = (bf16[32,64,128]{2,1,0:T(8,128)(2,1)}, bf16[32,64,128]{2,1,0:T(8,128)(2,1)S(1)}, u32[]{:S(2)}, u32[]{:S(2)}) collective-permute-start(bf16[32,64,128]{2,1,0:T(8,128)(2,1)} %shard_map.69.refs_1_), channel_id=1, source_target_pairs={{0,2},{1,3},{2,0},{3,1},{4,6},{5,7},{6,4},{7,5},{8,10},{9,11},{10,... | collective-permute-start | bytes 1572872 | tf_op jit(solution)/shard_map/ppermute | solution.py:41
  121.0 34.5 %collective-permute-start.18 = (bf16[32,64,128]{2,1,0:T(8,128)(2,1)}, bf16[32,64,128]{2,1,0:T(8,128)(2,1)S(1)}, u32[]{:S(2)}, u32[]{:S(2)}) collective-permute-start(bf16[32,64,128]{2,1,0:T(8,128)(2,1)} %collective-permute-done.14.refs_1_), channel_id=1, source_target_pairs={{0,1},{1,0},{2,3},{3,2},{4,5},{5,4},{6,7},{7,6},{8,9},{9,8},{10,11... | collective-permute-start | bytes 1572872 | tf_op jit(solution)/shard_map/ppermute | solution.py:41
  124.3 8.3 %copy-start.55 = (bf16[129,16,128]{2,1,0:T(8,128)(2,1)S(1)}, bf16[129,16,128]{2,1,0:T(8,128)(2,1)}, u32[]{:S(2)}) copy-start(bf16[129,16,128]{2,1,0:T(8,128)(2,1)} %copy-done.54) | copy-start | bytes 1585156
  124.3 12.5 %copy-start.32 = (bf16[129,16,128]{2,1,0:T(8,128)(2,1)S(1)}, bf16[129,16,128]{2,1,0:T(8,128)(2,1)}, u32[]{:S(2)}) copy-start(bf16[129,16,128]{2,1,0:T(8,128)(2,1)} %copy-done.31) | copy-start | bytes 1585156
  126.9 31.4 %collective-permute-start.17 = (bf16[32,64,128]{2,1,0:T(8,128)(2,1)}, bf16[32,64,128]{2,1,0:T(8,128)(2,1)S(1)}, u32[]{:S(2)}, u32[]{:S(2)}) collective-permute-start(bf16[32,64,128]{2,1,0:T(8,128)(2,1)} %shard_map.69.refs_1_), channel_id=1, source_target_pairs={{0,1},{1,0},{2,3},{3,2},{4,5},{5,4},{6,7},{7,6},{8,9},{9,8},{10,11... | collective-permute-start | bytes 1572872 | tf_op jit(solution)/shard_map/ppermute | solution.py:41
  132.6 22.9 %copy-start.53 = (bf16[129,16,128]{2,1,0:T(8,128)(2,1)S(1)}, bf16[129,16,128]{2,1,0:T(8,128)(2,1)}, u32[]{:S(2)}) copy-start(bf16[129,16,128]{2,1,0:T(8,128)(2,1)} %copy-done.52) | copy-start | bytes 1585156
  132.6 28.2 %collective-permute-start.9 = (bf16[129,16,128]{2,1,0:T(8,128)(2,1)S(1)}, bf16[129,16,128]{2,1,0:T(8,128)(2,1)S(1)}, u32[]{:S(2)}, u32[]{:S(2)}) collective-permute-start(bf16[129,16,128]{2,1,0:T(8,128)(2,1)S(1)} %copy-done.55), channel_id=1, source_target_pairs={{0,14},{1,15},{2,12},{3,13},{4,10},{5,11},{6,8},{7,9},{8,6},{9,7},... | collective-permute-start | bytes 1585160 | tf_op jit(solution)/shard_map/ppermute | solution.py:41
  136.7 24.1 %collective-permute-start.16 = (bf16[32,64,128]{2,1,0:T(8,128)(2,1)}, bf16[32,64,128]{2,1,0:T(8,128)(2,1)S(1)}, u32[]{:S(2)}, u32[]{:S(2)}) collective-permute-start(bf16[32,64,128]{2,1,0:T(8,128)(2,1)} %collective-permute-done.15.refs_1_), channel_id=1, source_target_pairs={{0,1},{1,0},{2,3},{3,2},{4,5},{5,4},{6,7},{7,6},{8,9},{9,8},{10,11... | collective-permute-start | bytes 1572872 | tf_op jit(solution)/shard_map/ppermute | solution.py:41
  155.5 13.8 %collective-permute-start.5 = (bf16[129,16,128]{2,1,0:T(8,128)(2,1)S(1)}, bf16[129,16,128]{2,1,0:T(8,128)(2,1)S(1)}, u32[]{:S(2)}, u32[]{:S(2)}) collective-permute-start(bf16[129,16,128]{2,1,0:T(8,128)(2,1)S(1)} %copy-done.53), channel_id=1, source_target_pairs={{0,6},{1,7},{2,4},{3,5},{4,2},{5,3},{6,0},{7,1},{8,14},{9,15},{10,... | collective-permute-start | bytes 1585160 | tf_op jit(solution)/shard_map/ppermute | solution.py:41
  155.5 13.8 %collective-permute-start.12 = (bf16[32,64,128]{2,1,0:T(8,128)(2,1)S(1)}, bf16[32,64,128]{2,1,0:T(8,128)(2,1)S(1)}, u32[]{:S(2)}, u32[]{:S(2)}) collective-permute-start(bf16[32,64,128]{2,1,0:T(8,128)(2,1)S(1)} %collective-permute-done.11.refs_1_), channel_id=1, source_target_pairs={{0,1},{1,0},{2,3},{3,2},{4,5},{5,4},{6,7},{7,6},{8,9},{9,8},{10,11... | collective-permute-start | bytes 1572872 | tf_op jit(solution)/shard_map/ppermute | solution.py:41
  171.8 1.2 collective-permute-start.24
  173.0 3.7 %collective-permute-start.25 = (f32[16,128]{1,0:T(8,128)S(1)}, f32[16,128]{1,0:T(8,128)S(1)}, u32[]{:S(2)}, u32[]{:S(2)}) collective-permute-start(f32[16,128]{1,0:T(8,128)S(1)} %add.88), channel_id=1, source_target_pairs={{0,2},{1,3},{2,0},{3,1},{4,6},{5,7},{6,4},{7,5},{8,10},{9,11},{10,... | collective-permute-start | bytes 24584 | tf_op jit(solution)/shard_map/ppermute | solution.py:113
  176.7 6.2 %collective-permute-start.26 = (f32[16,128]{1,0:T(8,128)S(1)}, f32[16,128]{1,0:T(8,128)S(1)}, u32[]{:S(2)}, u32[]{:S(2)}) collective-permute-start(f32[16,128]{1,0:T(8,128)S(1)} %add.89), channel_id=1, source_target_pairs={{0,4},{1,5},{2,6},{3,7},{4,0},{5,1},{6,2},{7,3},{8,12},{9,13},{10,... | collective-permute-start | bytes 24584 | tf_op jit(solution)/shard_map/ppermute | solution.py:113
  182.9 4.5 %collective-permute-start.27 = (f32[16,128]{1,0:T(8,128)S(1)}, f32[16,128]{1,0:T(8,128)S(1)}, u32[]{:S(2)}, u32[]{:S(2)}) collective-permute-start(f32[16,128]{1,0:T(8,128)S(1)} %add.90), channel_id=1, source_target_pairs={{0,8},{1,9},{2,10},{3,11},{4,12},{5,13},{6,14},{7,15},{8,0},{9,1},... | collective-permute-start | bytes 24584 | tf_op jit(solution)/shard_map/ppermute | solution.py:113
  188.8 2.1 collective-permute-start.29
  188.8 14.7 %collective-permute-start.28 = (bf16[32,64,128]{2,1,0:T(8,128)(2,1)}, bf16[32,64,128]{2,1,0:T(8,128)(2,1)}, u32[]{:S(2)}, u32[]{:S(2)}) collective-permute-start(bf16[32,64,128]{2,1,0:T(8,128)(2,1)} %get-tuple-element.20.refs_8_), channel_id=1, source_target_pairs={{0,4},{1,5},{2,0},{3,1},{4,8},{5,9},{6,2},{7,3},{8,12},{9,13},{10,... | collective-permute-start | bytes 1572872 | tf_op jit(solution)/shard_map/ppermute | solution.py:41
  190.8 14.4 %collective-permute-start.32 = (bf16[32,64,128]{2,1,0:T(8,128)(2,1)}, bf16[32,64,128]{2,1,0:T(8,128)(2,1)}, u32[]{:S(2)}, u32[]{:S(2)}) collective-permute-start(bf16[32,64,128]{2,1,0:T(8,128)(2,1)} %get-tuple-element.20.refs_8_), channel_id=1, source_target_pairs={{0,2},{1,3},{2,6},{3,7},{4,0},{5,1},{6,10},{7,11},{8,4},{9,5},{10,... | collective-permute-start | bytes 1572872 | tf_op jit(solution)/shard_map/ppermute | solution.py:41
  203.5 3.8 %collective-permute-start.31 = (bf16[32,64,128]{2,1,0:T(8,128)(2,1)}, bf16[32,64,128]{2,1,0:T(8,128)(2,1)}, u32[]{:S(2)}, u32[]{:S(2)}) collective-permute-start(bf16[32,64,128]{2,1,0:T(8,128)(2,1)} %shard_map.82.refs_8_), channel_id=1, source_target_pairs={{0,1},{1,0},{2,3},{3,2},{4,5},{5,4},{6,7},{7,6},{8,9},{9,8},{10,11... | collective-permute-start | bytes 1572872 | tf_op jit(solution)/shard_map/ppermute | solution.py:41
  205.2 2.3 collective-permute-start.33
  205.2 14.7 %collective-permute-start.30 = (bf16[32,64,128]{2,1,0:T(8,128)(2,1)}, bf16[32,64,128]{2,1,0:T(8,128)(2,1)}, u32[]{:S(2)}, u32[]{:S(2)}) collective-permute-start(bf16[32,64,128]{2,1,0:T(8,128)(2,1)} %shard_map.82.refs_8_), channel_id=1, source_target_pairs={{0,4},{1,5},{2,0},{3,1},{4,8},{5,9},{6,2},{7,3},{8,12},{9,13},{10,... | collective-permute-start | bytes 1572872 | tf_op jit(solution)/shard_map/ppermute | solution.py:41
  206.0 14.2 %collective-permute-start.36 = (bf16[32,64,128]{2,1,0:T(8,128)(2,1)}, bf16[32,64,128]{2,1,0:T(8,128)(2,1)}, u32[]{:S(2)}, u32[]{:S(2)}) collective-permute-start(bf16[32,64,128]{2,1,0:T(8,128)(2,1)} %collective-permute-done.32.refs_10_), channel_id=1, source_target_pairs={{0,2},{1,3},{2,6},{3,7},{4,0},{5,1},{6,10},{7,11},{8,4},{9,5},{10,... | collective-permute-start | bytes 1572872 | tf_op jit(solution)/shard_map/ppermute | solution.py:41
  219.9 2.6 %collective-permute-start.35 = (bf16[32,64,128]{2,1,0:T(8,128)(2,1)}, bf16[32,64,128]{2,1,0:T(8,128)(2,1)}, u32[]{:S(2)}, u32[]{:S(2)}) collective-permute-start(bf16[32,64,128]{2,1,0:T(8,128)(2,1)} %shard_map.84.refs_8_), channel_id=1, source_target_pairs={{0,1},{1,0},{2,3},{3,2},{4,5},{5,4},{6,7},{7,6},{8,9},{9,8},{10,11... | collective-permute-start | bytes 1572872 | tf_op jit(solution)/shard_map/ppermute | solution.py:41
  220.2 2.6 collective-permute-start.37
  220.4 14.5 %collective-permute-start.34 = (bf16[32,64,128]{2,1,0:T(8,128)(2,1)}, bf16[32,64,128]{2,1,0:T(8,128)(2,1)}, u32[]{:S(2)}, u32[]{:S(2)}) collective-permute-start(bf16[32,64,128]{2,1,0:T(8,128)(2,1)} %shard_map.84.refs_8_), channel_id=1, source_target_pairs={{0,4},{1,5},{2,0},{3,1},{4,8},{5,9},{6,2},{7,3},{8,12},{9,13},{10,... | collective-permute-start | bytes 1572872 | tf_op jit(solution)/shard_map/ppermute | solution.py:41
  221.0 13.9 %collective-permute-start.38 = (bf16[32,64,128]{2,1,0:T(8,128)(2,1)}, bf16[32,64,128]{2,1,0:T(8,128)(2,1)}, u32[]{:S(2)}, u32[]{:S(2)}) collective-permute-start(bf16[32,64,128]{2,1,0:T(8,128)(2,1)} %collective-permute-done.36.refs_10_), channel_id=1, source_target_pairs={{0,2},{1,3},{2,6},{3,7},{4,0},{5,1},{6,10},{7,11},{8,4},{9,5},{10,... | collective-permute-start | bytes 1572872 | tf_op jit(solution)/shard_map/ppermute | solution.py:41
  234.9 3.5 %collective-permute-start.40 = (bf16[32,64,128]{2,1,0:T(8,128)(2,1)}, bf16[32,64,128]{2,1,0:T(8,128)(2,1)}, u32[]{:S(2)}, u32[]{:S(2)}) collective-permute-start(bf16[32,64,128]{2,1,0:T(8,128)(2,1)} %shard_map.86.lower_ref.refs_8_), channel_id=1, source_target_pairs={{0,1},{1,0},{2,3},{3,2},{4,5},{5,4},{6,7},{7,6},{8,9},{9,8},{10,11... | collective-permute-start | bytes 1572872 | tf_op jit(solution)/shard_map/ppermute | solution.py:41
  235.0 3.4 %collective-permute-start.41 = (bf16[32,64,128]{2,1,0:T(8,128)(2,1)}, bf16[32,64,128]{2,1,0:T(8,128)(2,1)}, u32[]{:S(2)}, u32[]{:S(2)}) collective-permute-start(bf16[32,64,128]{2,1,0:T(8,128)(2,1)} %collective-permute-done.38.upper_ref.refs_10_), channel_id=1, source_target_pairs={{0,1},{1,0},{2,3},{3,2},{4,5},{5,4},{6,7},{7,6},{8,9},{9,8},{10,11... | collective-permute-start | bytes 1572872 | tf_op jit(solution)/shard_map/ppermute | solution.py:41
  237.5 12.3 %collective-permute-start.39 = (bf16[32,64,128]{2,1,0:T(8,128)(2,1)}, bf16[32,64,128]{2,1,0:T(8,128)(2,1)}, u32[]{:S(2)}, u32[]{:S(2)}) collective-permute-start(bf16[32,64,128]{2,1,0:T(8,128)(2,1)} %shard_map.87), channel_id=1, source_target_pairs={{0,4},{1,3},{2,0},{3,7},{4,8},{5,1},{6,2},{7,11},{8,12},{9,5},{10,... | collective-permute-start | bytes 1572872 | tf_op jit(solution)/shard_map/ppermute | solution.py:41
  249.9 2.6 collective-permute-start.42
  (56 other events, 90.5 us)

commit v6 on v5

--- a/solution.py
+++ b/solution.py
@@ -8,7 +8,7 @@
 from jax.sharding import PartitionSpec as P
 
 BOTH = ("sec", "term")
-VMEM_LIMIT = 20 * 2**20
+VMEM_LIMIT = 24 * 2**20
 PART = 16
 RING_BYTES = 24 * 2**20
 
@@ -79,30 +79,25 @@
 
 
 def after(value, *others):
+    far_memory = pl.BlockSpec(memory_space=pltpu.HBM)
     anywhere = pl.BlockSpec(memory_space=pl.ANY)
     return pl.pallas_call(
         after_kernel,
         out_shape=jax.ShapeDtypeStruct(value.shape, value.dtype),
-        in_specs=[anywhere] * (1 + len(others)),
-        out_specs=anywhere,
+        in_specs=[far_memory] + [anywhere] * len(others),
+        out_specs=far_memory,
         input_output_aliases={0: 0},
         cost_estimate=busy(0.3),
     )(value, *others)
 
 
-def mask_gather(unit, lefts, owners, halves):
+def mask_gather(unit, owners, halves):
     units = {0: unit}
     step = owners // 2
-    masks = []
     while step:
-        masks.append(step)
-        units[step] = exchange(unit, owners, halves, step)
+        for mask in list(units):
+            units[mask | step] = exchange(units[mask], owners, halves, step)
         step //= 2
-    for mask in masks[:-1]:
-        units[mask] = after(units[mask], lefts[masks[0]])
-    for step in masks[1:]:
-        for mask in [m for m in units if m >= 2 * step and m % (2 * step) == 0]:
-            units[mask | step] = exchange(units[mask], owners, halves, step)
     return units
 
 
@@ -117,22 +112,26 @@
     return value
 
 
-def pack_kernel(order, capacity, blocks, terms, ids_ref, plan_ref, other_plan_ref, *refs):
-    left_ref, other_ref, _, *pieces, codes, seen, built, sems = refs
-    owners = len(order)
-    me, half = ids_ref[0], ids_ref[1]
-    rows, width = other_ref.shape[2:]
-    start = pl.multiple_of(half * rows, rows)
+def pack_kernel(capacity, own_left, half_ref, owner_ref, target_ref, left_ref, out_ref, *scratch):
+    codes, seen, left, built, in_sem, sems = scratch
+    terms, blocks, rows, width = left.shape
+    owners = out_ref.shape[0]
+    half = half_ref[0]
     parts = rows // PART
+    if own_left:
+        start = pl.multiple_of(half * rows, rows)
+        load = pltpu.make_async_copy(left_ref.at[:, :, pl.ds(start, rows), :], left, in_sem)
+    else:
+        load = pltpu.make_async_copy(left_ref, left, in_sem)
+    load.start()
 
     @pl.loop(0, owners)
     def _(owner):
-        for index in range(2 * terms * capacity):
+        for index in range(terms * capacity):
             codes[0, owner, index] = 0
             codes[1, owner, index] = blocks
 
-    for stream in range(2 * terms):
-        plan = plan_ref if stream < terms else other_plan_ref
+    for term in range(terms):
 
         @pl.loop(0, owners)
         def _(owner):
@@ -140,60 +139,58 @@
 
         @pl.loop(0, blocks, unroll=4)
         def _(block):
-            owner = plan[0, stream % terms, block]
+            owner = owner_ref[term, block]
             slot = seen[owner]
             seen[owner] = slot + 1
-            codes[0, owner, stream * capacity + slot] = block
-            codes[1, owner, stream * capacity + slot] = plan[1, stream % terms, block]
-
+            codes[0, owner, term * capacity + slot] = block
+            codes[1, owner, term * capacity + slot] = target_ref[term, block]
+
+    load.wait()
     lane = lax.broadcasted_iota(jnp.int32, (PART, width), 1)
     row = lax.broadcasted_iota(jnp.int32, (PART, width), 0)
-    copies = []
-    for mask in order:
-        owner = me ^ mask
+    copies = [
+        pltpu.make_async_copy(built.at[owner], out_ref.at[owner], sems.at[owner])
+        for owner in range(owners)
+    ]
+    for owner in range(owners):
         labels = jnp.zeros((PART, width), jnp.int32)
-        for stream in range(2 * terms):
-            for slot in range(capacity):
-                at = stream * capacity + slot
-                block = codes[0, owner, at]
-                if stream < terms:
-                    value = left_ref[stream, block, pl.ds(start, rows), :]
-                else:
-                    value = other_ref[stream - terms, block]
-                value = pltpu.roll(value.astype(jnp.float32), half * rows, 1)
-                built[mask, at * parts : (at + 1) * parts] = value.astype(jnp.bfloat16).reshape(
-                    parts, PART, width
-                )
-                label = jnp.where(row == 0, block, codes[1, owner, at])
-                labels = jnp.where(lane == at, label, labels)
-        built[mask, 2 * terms * capacity * parts] = labels.astype(jnp.float32).astype(jnp.bfloat16)
-        copies.append(pltpu.make_async_copy(built.at[mask], pieces[mask], sems.at[mask]))
-        copies[-1].start()
+        for at in range(terms * capacity):
+            block = codes[0, owner, at]
+            value = left[at // capacity, block]
+            value = pltpu.roll(value.astype(jnp.float32), half * rows, 1)
+            built[owner, at * parts : (at + 1) * parts] = value.astype(jnp.bfloat16).reshape(
+                parts, PART, width
+            )
+            labels = jnp.where(
+                lane == at, jnp.where(row == 0, block, codes[1, owner, at]), labels
+            )
+        built[owner, terms * capacity * parts] = labels.astype(jnp.float32).astype(jnp.bfloat16)
+        copies[owner].start()
     for copy in copies:
         copy.wait()
 
 
-def pack(ids, plan, other_plan, left, other, before, order, capacity):
-    terms, blocks, rows, width = other.shape
-    owners = len(order)
+def pack(half, target_owner, target_local, left, rows, owners, capacity):
+    terms, blocks, height, width = left.shape
     scalars = pl.BlockSpec(memory_space=pltpu.SMEM)
-    whole = pl.BlockSpec(memory_space=pltpu.VMEM)
-    anywhere = pl.BlockSpec(memory_space=pl.ANY)
-    shape = (2 * terms * capacity * rows // PART + 1, PART, width)
+    far_memory = pl.BlockSpec(memory_space=pltpu.HBM)
+    shape = (owners, terms * capacity * rows // PART + 1, PART, width)
     return pl.pallas_call(
-        functools.partial(pack_kernel, order, capacity, blocks, terms),
-        out_shape=[jax.ShapeDtypeStruct(shape, jnp.bfloat16)] * owners,
-        in_specs=[scalars] * 3 + [whole, whole, anywhere],
-        out_specs=[anywhere] * owners,
+        functools.partial(pack_kernel, capacity, height != rows),
+        out_shape=jax.ShapeDtypeStruct(shape, jnp.bfloat16),
+        in_specs=[scalars] * 3 + [far_memory],
+        out_specs=far_memory,
         scratch_shapes=[
-            pltpu.SMEM((2, owners, 2 * terms * capacity), jnp.int32),
+            pltpu.SMEM((2, owners, terms * capacity), jnp.int32),
             pltpu.SMEM((owners,), jnp.int32),
-            pltpu.VMEM((owners,) + shape, jnp.bfloat16),
+            pltpu.VMEM((terms, blocks, rows, width), jnp.bfloat16),
+            pltpu.VMEM(shape, jnp.bfloat16),
+            pltpu.SemaphoreType.DMA,
             pltpu.SemaphoreType.DMA((owners,)),
         ],
         compiler_params=pltpu.CompilerParams(vmem_limit_bytes=VMEM_LIMIT),
-        cost_estimate=busy(5.0),
-    )(ids, plan, other_plan, left, other, before)
+        cost_estimate=busy(3.0),
+    )(half, target_owner, target_local, left)
 
 
 def busy(microseconds):
@@ -202,97 +199,133 @@
     )
 
 
-def add_products(piece, labels, near, far, rights, total, streams, capacity):
-    terms = streams // 2
+def add_products(left, labels, near, far, right, total, terms, capacity):
     blocks, rows, width = near.shape
     parts = rows // PART
-    for side in range(2):
-        moved, where = [], []
-        for stream in range(terms * side, terms * side + terms):
-            for slot in range(capacity):
-                at = stream * capacity + slot
-                source, target = labels[0, at], labels[1, at]
-                block = jnp.concatenate([near[source], far[source]], axis=0)
-                left = piece[at * parts : (at + 1) * parts].reshape(rows, width)
-                product = jnp.dot(left, block, preferred_element_type=jnp.float32)
-                moved.append(product.astype(jnp.bfloat16))
-                where.append((stream - terms * side, target))
-        for value, (term, target) in zip(moved, where):
-            total[target] += jnp.dot(
-                value,
-                rights[side][term, jnp.minimum(target, blocks - 1)],
-                preferred_element_type=jnp.float32,
-            )
-
-
-def apply_kernel(sources, first, choices, last, streams, capacity, ids_ref, *refs):
+    moved, where = [], []
+    for at in range(terms * capacity):
+        block = jnp.concatenate([near[labels[0, at]], far[labels[0, at]]], axis=0)
+        piece = left[at * parts : (at + 1) * parts].reshape(rows, width)
+        product = jnp.dot(piece, block, preferred_element_type=jnp.float32)
+        moved.append(product.astype(jnp.bfloat16))
+        where.append(labels[1, at])
+    for at in range(terms * capacity):
+        target = where[at]
+        total[target] += jnp.dot(
+            moved[at],
+            right[at // capacity, jnp.minimum(target, blocks - 1)],
+            preferred_element_type=jnp.float32,
+        )
+
+
+def apply_kernel(sources, sides, first, last, chips_ref, *refs):
     refs = list(refs)
-    lefts = [refs.pop(0) for _ in range(choices or sources)]
+    lefts = [refs.pop(0) for _ in range(sides)]
+    rights = [refs.pop(0) for _ in range(sides)]
     vectors = [(refs.pop(0), refs.pop(0)) for _ in range(sources)]
-    rights = refs.pop(0), refs.pop(0)
     total_in = None if first else refs.pop(0)
     out = refs.pop(0) if last else None
     total = refs.pop(0)
-    spread_labels, labels, label_sems = refs.pop(0), refs.pop(0), refs.pop(0)
-    blocks = vectors[0][0].shape[0]
-
-    if choices:
-        chosen, chosen_sems = refs.pop(0), refs.pop(0)
-        for index in range(sources):
-            for choice, left in enumerate(lefts):
-
-                @pl.when(ids_ref[index] == choice)
-                def _():
-                    pltpu.make_async_copy(left, chosen.at[index], chosen_sems.at[index]).start()
-
+    left, right, vector, raw, spread, labels = refs[:6]
+    left_sems, right_sems, vector_sems, raw_sems, label_sem = refs[6:]
+    terms, blocks = right.shape[1:3]
+    rows = vector.shape[3]
+    parts = left.shape[1]
+    capacity = parts * PART // (terms * rows)
+    items = [(source, side) for source in range(sources) for side in range(sides)]
+
+    def label_copy(item):
+        source, side = items[item]
+        return pltpu.make_async_copy(
+            lefts[side].at[chips_ref[source], parts], raw.at[item], raw_sems.at[item]
+        )
+
+    def left_copy(item):
+        source, side = items[item]
+        return pltpu.make_async_copy(
+            lefts[side].at[chips_ref[source], pl.ds(0, parts)],
+            left.at[item % 2],
+            left_sems.at[item % 2],
+        )
+
+    def vector_copies(source):
+        return [
+            pltpu.make_async_copy(
+                vectors[source][part], vector.at[source % 2, part], vector_sems.at[source % 2, part]
+            )
+            for part in range(2)
+        ]
+
+    def right_copy(side):
+        return pltpu.make_async_copy(rights[side], right.at[side], right_sems.at[side])
+
+    for item in range(len(items)):
+        label_copy(item).start()
+    for copy in [left_copy(0), *vector_copies(0), right_copy(0)]:
+        copy.start()
+    for side in range(1, sides):
+        right_copy(side).start()
     total[...] = jnp.zeros_like(total) if first else total_in[...]
-    pieces = []
-    for index in range(sources):
-        if choices:
-            pltpu.make_async_copy(lefts[0], chosen.at[index], chosen_sems.at[index]).wait()
-            piece = chosen.at[index]
-        else:
-            piece = lefts[index]
-        pieces.append(piece)
-        values = piece[piece.shape[0] - 1].astype(jnp.float32).astype(jnp.int32)
-        spread_labels[index] = values[:8]
-        pltpu.make_async_copy(
-            spread_labels.at[index], labels.at[index], label_sems.at[index]
-        ).start()
-    for index, (near, far) in enumerate(vectors):
-        pltpu.make_async_copy(
-            spread_labels.at[index], labels.at[index], label_sems.at[index]
-        ).wait()
+    for item in range(len(items)):
+        label_copy(item).wait()
+    spread[...] = raw[:, :8].astype(jnp.float32).astype(jnp.int32)
+    label_move = pltpu.make_async_copy(spread, labels, label_sem)
+    label_move.start()
+    label_move.wait()
+
+    for item, (source, side) in enumerate(items):
+        if item + 1 < len(items):
+            left_copy(item + 1).start()
+        if side == 0:
+            for copy in vector_copies(source):
+                copy.wait()
+            if source + 1 < sources:
+                for copy in vector_copies(source + 1):
+                    copy.start()
+        if source == 0:
+            right_copy(side).wait()
+        left_copy(item).wait()
         add_products(
-            pieces[index], labels.at[index], near, far, rights, total, streams, capacity
+            left.at[item % 2],
+            labels.at[item],
+            vector.at[source % 2, 0],
+            vector.at[source % 2, 1],
+            right.at[side],
+            total,
+            terms,
+            capacity,
         )
     if last:
         out[...] = total[:blocks].astype(out.dtype)
 
 
-def apply_group(ids, lefts, vectors, rights, total, choices, last):
+def apply_group(chips, lefts, rights, vectors, total, last):
     blocks, rows, width = vectors[0][0].shape
-    streams = 2 * rights[0].shape[0]
-    capacity = (lefts[0].shape[0] - 1) * PART // (streams * rows)
-    sources = len(vectors)
+    terms = rights[0].shape[0]
+    parts = lefts[0].shape[1] - 1
+    sources, sides = len(vectors), len(lefts)
     first = total is None
-    arrays = list(lefts) + [unit for pair in vectors for unit in pair] + list(rights)
+    arrays = list(lefts) + list(rights) + [unit for pair in vectors for unit in pair]
+    whole = pl.BlockSpec(memory_space=pltpu.VMEM)
+    specs = [pl.BlockSpec(memory_space=pltpu.HBM)] * len(arrays)
     if not first:
         arrays.append(total)
-    whole = pl.BlockSpec(memory_space=pltpu.VMEM)
+        specs.append(whole)
     total_shape = (blocks + 1, rows, width)
+    items = sources * sides
     scratch = [
-        pltpu.VMEM((sources, 8, width), jnp.int32),
-        pltpu.SMEM((sources, 8, width), jnp.int32),
-        pltpu.SemaphoreType.DMA((sources,)),
+        pltpu.VMEM((2, parts, PART, width), jnp.bfloat16),
+        pltpu.VMEM((sides, terms, blocks, width, width), jnp.bfloat16),
+        pltpu.VMEM((2, 2, blocks, rows, width), jnp.bfloat16),
+        pltpu.VMEM((items, PART, width), jnp.bfloat16),
+        pltpu.VMEM((items, 8, width), jnp.int32),
+        pltpu.SMEM((items, 8, width), jnp.int32),
+        pltpu.SemaphoreType.DMA((2,)),
+        pltpu.SemaphoreType.DMA((sides,)),
+        pltpu.SemaphoreType.DMA((2, 2)),
+        pltpu.SemaphoreType.DMA((items,)),
+        pltpu.SemaphoreType.DMA,
     ]
-    specs = [whole] * len(arrays)
-    if choices:
-        scratch += [
-            pltpu.VMEM((sources,) + lefts[0].shape, lefts[0].dtype),
-            pltpu.SemaphoreType.DMA((sources,)),
-        ]
-        specs[: len(lefts)] = [pl.BlockSpec(memory_space=pl.ANY)] * len(lefts)
     aliases = {}
     if last:
         out_shape = jax.ShapeDtypeStruct((blocks, rows, width), jnp.bfloat16)
@@ -302,17 +335,15 @@
         if not first:
             aliases = {len(arrays): 0}
     return pl.pallas_call(
-        functools.partial(
-            apply_kernel, sources, first, len(lefts) if choices else 0, last, streams, capacity
-        ),
+        functools.partial(apply_kernel, sources, sides, first, last),
         out_shape=out_shape,
         in_specs=[pl.BlockSpec(memory_space=pltpu.SMEM)] + specs,
         out_specs=whole,
         scratch_shapes=scratch,
         input_output_aliases=aliases,
         compiler_params=pltpu.CompilerParams(vmem_limit_bytes=VMEM_LIMIT),
-        cost_estimate=busy(0.7 + 1.4 * sources),
-    )(ids, *arrays)
+        cost_estimate=busy(1.5 + 0.7 * items),
+    )(chips.astype(jnp.int32), *arrays)
 
 
 def stats_kernel(ids_ref, total_ref, wave_ref, stats_ref):
@@ -391,46 +422,37 @@
 
     own_rows = lax.dynamic_slice_in_dim(wavefunction, half * rows, rows, 1)
     other_rows = lax.dynamic_slice_in_dim(wavefunction, (1 - half) * rows, rows, 1)
+    half_scalar = jnp.reshape(half, (1,)).astype(jnp.int32)
+
+    def send_left(owner_of, target_of, left):
+        packed = pack(half_scalar, owner_of, target_of, left, rows, owners, capacity)
+        return lax.all_to_all(packed, "sec", split_axis=0, concat_axis=0, tiled=True)
+
     plan = jnp.stack([target_owner[:, :, 0], target_local])
+    lefts = [send_left(plan[0], plan[1], left_operator)]
     other_left = swap(
         lax.dynamic_slice_in_dim(left_operator, (1 - half) * rows, rows, 2), owners, halves
     )
-    far_pieces = list(range(owners // 2, owners))
-    order = [0, far_pieces[0]]
-    for m in range(1, owners // 2):
-        order += [far_pieces[m], m]
-    rights = (right_operator, swap(right_operator, owners, halves))
-    pieces = pack(
-        ids,
-        plan,
-        swap(plan, owners, halves),
-        left_operator,
-        other_left,
-        rights[1],
-        order[1:] + order[:1],
-        capacity,
-    )
-    lefts = [exchange(piece, owners, halves, m) if m else piece for m, piece in enumerate(pieces)]
-    near = mask_gather(own_rows, lefts, owners, halves)
+    other_plan = swap(plan, owners, halves)
+    lefts.append(send_left(other_plan[0], other_plan[1], other_left))
+    rights = [right_operator, swap(right_operator, owners, halves)]
+    near = mask_gather(own_rows, owners, halves)
     far = {m: swap(unit, owners, halves) if m else other_rows for m, unit in near.items()}
+    masks = jnp.array(list(near), jnp.int32)
+    vectors = [(near[m], far[m]) for m in near]
 
     total = None
-    no_choice = jnp.zeros((1,), jnp.int32)
-    for m in order:
-        total = apply_group(
-            no_choice, [lefts[m]], [(near[m], far[m])], rights, total, False, False
-        )
+    for left, right in zip(lefts, rights):
+        total = apply_group(me ^ masks, [left], [right], vectors, total, False)
 
     entries = blocks * owners * height * width
     direction, rayleigh = new_direction(ids, total, own_rows, owners, halves, entries)
     reach = (owners - 1) // 2
 
     def add_group(total, units, last):
-        choice = jnp.stack([ring_owner(place - s, owners) ^ me for s in units])
-        vectors = [
-            (unit, swap(unit, owners, halves)) for unit in units.values()
-        ]
-        return apply_group(choice.astype(jnp.int32), lefts, vectors, rights, total, True, last)
+        chips = jnp.stack([ring_owner(place - s, owners) for s in units])
+        vectors = [(unit, swap(unit, owners, halves)) for unit in units.values()]
+        return apply_group(chips, lefts, rights, vectors, total, last)
 
     ahead = behind = direction
     units = {0: direction}

time: 264 us -> 298 us (1.13)
  waiting for transfers between devices: 118 us -> 170 us
  local copies, waits for them, and re-layouts: 57.5 us -> 35.8 us
  Pallas kernels: 46.6 us -> 51.2 us
    all_to_all x0 -> x2, waiting for transfers between devices: none -> 40.8 us  [send_left(): lax.all_to_all(packed, 'sec', split_axis=0, concat_axis=0, tiled=True)]
    unnamed x122 -> x84, local copies, waits for them, and re-layouts: 53.1 us -> 34.4 us
    ppermute x39 -> x32, starting transfers between devices: 31 us -> 18 us  [permute(): return lax.ppermute(value, BOTH, pairs)]
    ppermute x39 -> x32, waiting for transfers between devices: 110 us -> 123 us  [permute(): return lax.ppermute(value, BOTH, pairs)]
    all_to_all x0 -> x2, starting transfers between devices: none -> 11.8 us  [send_left(): lax.all_to_all(packed, 'sec', split_axis=0, concat_axis=0, tiled=True)]
    pallas_call x14 -> x9, Pallas kernels: 41.9 us -> 46.5 us  [the longest x7 41 us: apply_group(): pl.pallas_call(functools.partial(apply_kernel, sources, sides, first, las...]
  transfers between devices with their start and end apart: 43 -> 38, of which waited for: 20 -> 23; matrix products, arithmetic and copies ran while one was open for 2% -> 1% of each run, Pallas kernels for 15% -> 11%
where the time goes in v6:
time: 298 us; the launch traced here: 296 us
  waiting for transfers between devices  170 us (57%)
  Pallas kernels  51.2 us (17%)
  starting transfers between devices  37.6 us (13%)
  local copies, waits for them, and re-layouts  35.8 us (12%)
    ppermute x32, waiting for transfers between devices, permute(): return lax.ppermute(value, BOTH, pairs)  123 us
    pallas_call x7, Pallas kernels, apply_group(): pl.pallas_call(functools.partial(apply_kernel, sources, sides, first, las...  41 us
    all_to_all x2, waiting for transfers between devices, send_left(): lax.all_to_all(packed, 'sec', split_axis=0, concat_axis=0, tiled=True)  40.8 us
    unnamed x84, local copies, waits for them, and re-layouts  34.4 us
    ppermute x32, starting transfers between devices, permute(): return lax.ppermute(value, BOTH, pairs)  18 us
    all_to_all x2, starting transfers between devices, send_left(): lax.all_to_all(packed, 'sec', split_axis=0, concat_axis=0, tiled=True)  11.8 us
    ppermute x4, starting transfers between devices, doubled(): lax.ppermute(value, axes, [(d, d ^ step * stride) for d in range(total)])  7.77 us
    ppermute x4, waiting for transfers between devices, doubled(): lax.ppermute(value, axes, [(d, d ^ step * stride) for d in range(total)])  6.71 us
  transfers between devices with their start and end apart: 38, of which 23 were waited for; matrix products, arithmetic and copies ran while one was open for 1% of the time, Pallas kernels for 11%

profile of v6, /device:TPU:0, one launch (start us, length us, event | category | flops | bytes accessed | tf_op | source)
XLA Modules:
  0.0 296.1 jit_solution(5205955219651046598)
XLA Ops:
  0.6 1.6 copy-done.14
  3.6 2.8 shard_map.77
  6.4 1.3 copy-done.13
  7.7 7.3 %all-to-all-start = ((bf16[8,65,16,128]{3,2,1,0:T(8,128)(2,1)}), bf16[8,65,16,128]{3,2,1,0:T(8,128)(2,1)S(1)}, u32[]{:S(2)}, u32[]{:S(2)}) async-start(bf16[8,65,16,128]{3,2,1,0:T(8,128)(2,1)} %copy-done.13), calls=%async_computation | async-start | bytes 4259840 | tf_op jit(solution)/shard_map/all_to_all | solution.py:429
  15.0 1.3 constant_dynamic-slice_fusion.2
  17.0 2.1 collective-permute-done
  19.1 2.7 shard_map.78
  21.8 1.3 copy-done.12
  23.1 40.8 %all-to-all-done.refs_0_ = bf16[8,65,16,128]{3,2,1,0:T(8,128)(2,1)S(1)} async-done(((bf16[8,65,16,128]{3,2,1,0:T(8,128)(2,1)}), bf16[8,65,16,128]{3,2,1,0:T(8,128)(2,1)S(1)}, u32[]{:S(2)}, u32[]{:S(2)}) %all-to-all-start) | async-done | bytes 2129952 | tf_op jit(solution)/shard_map/all_to_all | solution.py:429
  63.9 1.4 copy-done.8
  65.4 4.5 %all-to-all-start.1 = ((bf16[8,65,16,128]{3,2,1,0:T(8,128)(2,1)}), bf16[8,65,16,128]{3,2,1,0:T(8,128)(2,1)}, u32[]{:S(2)}, u32[]{:S(2)}) async-start(bf16[8,65,16,128]{3,2,1,0:T(8,128)(2,1)} %copy-done.12), calls=%async_computation.1 | async-start | bytes 4259840 | tf_op jit(solution)/shard_map/all_to_all | solution.py:429
  70.0 2.7 collective-permute-start.3
  72.7 1.5 collective-permute-start.5
  74.2 1.5 collective-permute-start.9
  75.7 65.0 %collective-permute-done.3.refs_4_ = bf16[32,64,128]{2,1,0:T(8,128)(2,1)S(1)} collective-permute-done((bf16[32,64,128]{2,1,0:T(8,128)(2,1)S(1)}, bf16[32,64,128]{2,1,0:T(8,128)(2,1)S(1)}, u32[]{:S(2)}, u32[]{:S(2)}) %collective-permute-start.3) | collective-permute-done | bytes 524320 | tf_op jit(solution)/shard_map/ppermute | solution.py:41
  140.7 1.4 collective-permute-start.11
  143.2 9.6 %collective-permute-done.7.refs_8_ = bf16[32,64,128]{2,1,0:T(8,128)(2,1)} collective-permute-done((bf16[32,64,128]{2,1,0:T(8,128)(2,1)S(1)}, bf16[32,64,128]{2,1,0:T(8,128)(2,1)}, u32[]{:S(2)}, u32[]{:S(2)}) %collective-permute-start.7) | collective-permute-done | bytes 524320 | tf_op jit(solution)/shard_map/ppermute | solution.py:41
  153.7 2.0 collective-permute-done.11.refs_12_
  156.4 8.2 %collective-permute-done.13.refs_14_ = bf16[32,64,128]{2,1,0:T(8,128)(2,1)} collective-permute-done((bf16[32,64,128]{2,1,0:T(8,128)(2,1)S(1)}, bf16[32,64,128]{2,1,0:T(8,128)(2,1)}, u32[]{:S(2)}, u32[]{:S(2)}) %collective-permute-start.13) | collective-permute-done | bytes 524320 | tf_op jit(solution)/shard_map/ppermute | solution.py:41
  164.7 1.6 collective-permute-start.15
  169.2 7.6 %collective-permute-done.15.refs_16_ = bf16[32,64,128]{2,1,0:T(8,128)(2,1)} collective-permute-done((bf16[32,64,128]{2,1,0:T(8,128)(2,1)}, bf16[32,64,128]{2,1,0:T(8,128)(2,1)}, u32[]{:S(2)}, u32[]{:S(2)}) %collective-permute-start.15) | collective-permute-done | bytes 524320 | tf_op jit(solution)/shard_map/ppermute | solution.py:41
  179.0 1.6 copy-done.9
  187.9 8.8 %shard_map.79.refs_18_ = f32[33,64,128]{2,1,0:T(8,128)S(1)} custom-call(s32[8]{0:T(128)S(1)} %broadcast_xor_fusion.chips_ref, bf16[8,65,16,128]{3,2,1,0:T(8,128)(2,1)S(1)} %copy-done.9, bf16[2,32,128,128]{3,2,1,0:T(8,128)(2,1)} %refs_2_.9, bf16[32,64,128]{2,1,0:T(8,128)(2,1)S(1)} %get-tuple-element.7.refs_2_.wave_ref, ...), custom_call_target="tpu_custom_call" | custom-call | flops 8165000192 | tf_op jit(solution)/shard_map/pallas_call | solution.py:337
  204.1 9.3 %shard_map.80.total_ref = f32[33,64,128]{2,1,0:T(8,128)S(1)} custom-call(s32[8]{0:T(128)S(1)} %broadcast_xor_fusion.chips_ref, bf16[8,65,16,128]{3,2,1,0:T(8,128)(2,1)} %all-to-all-done.1.refs_0_.refs_1_, bf16[2,32,128,128]{3,2,1,0:T(8,128)(2,1)} %collective-permute-done.2.refs_1_.refs_3_, ...), custom_call_target="tpu_custom_call", output_to_operand_aliasing={{}: (19, {})} | custom-call | flops 8165000192 | tf_op jit(solution)/shard_map/pallas_call | solution.py:337
  215.9 1.8 collective-permute-start.18
  217.6 1.9 collective-permute-done.18
  219.5 1.5 collective-permute-start.19
  221.0 2.2 collective-permute-done.19
  223.2 4.3 %collective-permute-start.20 = (f32[16,128]{1,0:T(8,128)S(1)}, f32[16,128]{1,0:T(8,128)S(1)}, u32[]{:S(2)}, u32[]{:S(2)}) collective-permute-start(f32[16,128]{1,0:T(8,128)S(1)} %add.90), channel_id=1, source_target_pairs={{0,8},{1,9},{2,10},{3,11},{4,12},{5,13},{6,14},{7,15},{8,0},{9,1},... | collective-permute-start | bytes 24584 | tf_op jit(solution)/shard_map/ppermute | solution.py:108
  227.5 1.6 collective-permute-done.20
  229.1 1.4 shard_map.82
  231.1 1.4 collective-permute-start.25
  232.6 1.6 copy-done.10
  234.2 3.3 %shard_map.83.refs_1_.refs_8_ = f32[33,64,128]{2,1,0:T(8,128)S(1)} custom-call(s32[1]{0:T(128)} %bitcast.9.chips_ref, bf16[8,65,16,128]{3,2,1,0:T(8,128)(2,1)S(1)} %copy-done.10, bf16[8,65,16,128]{3,2,1,0:T(8,128)(2,1)} %all-to-all-done.1.refs_0_.refs_1_, bf16[2,32,128,128]{3,2,1,0:T(8,128)(2,1)} %refs_2_.9, ...), custom_call_target="tpu_custom_call" | custom-call | flops 3335000064 | tf_op jit(solution)/shard_map/pallas_call | solution.py:337
  238.5 6.6 %collective-permute-done.21.refs_0_ = bf16[32,64,128]{2,1,0:T(8,128)(2,1)} collective-permute-done((bf16[32,64,128]{2,1,0:T(8,128)(2,1)}, bf16[32,64,128]{2,1,0:T(8,128)(2,1)}, u32[]{:S(2)}, u32[]{:S(2)}) %collective-permute-start.21) | collective-permute-done | bytes 524320 | tf_op jit(solution)/shard_map/ppermute | solution.py:41
  245.2 1.5 collective-permute-done.25.refs_6_
  246.6 1.7 collective-permute-start.23
  248.9 5.2 %shard_map.85.refs_1_.refs_8_ = f32[33,64,128]{2,1,0:T(8,128)S(1)} custom-call(s32[2]{0:T(128)S(1)} %pad_add_fusion.2.chips_ref, bf16[8,65,16,128]{3,2,1,0:T(8,128)(2,1)S(1)} %copy-done.11, bf16[8,65,16,128]{3,2,1,0:T(8,128)(2,1)} %all-to-all-done.1.refs_0_.refs_1_, bf16[2,32,128,128]{3,2,1,0:T(8,128)(2,1)} %refs_2_.9, ...), custom_call_target="tpu_custom_call", output_to_operand_aliasing={{}: (9, {})} | custom-call | flops 4944999936 | tf_op jit(solution)/shard_map/pallas_call | solution.py:337
  255.1 6.2 %collective-permute-done.23.refs_0_ = bf16[32,64,128]{2,1,0:T(8,128)(2,1)} collective-permute-done((bf16[32,64,128]{2,1,0:T(8,128)(2,1)}, bf16[32,64,128]{2,1,0:T(8,128)(2,1)}, u32[]{:S(2)}, u32[]{:S(2)}) %collective-permute-start.23) | collective-permute-done | bytes 524320 | tf_op jit(solution)/shard_map/ppermute | solution.py:41
  261.3 1.4 collective-permute-done.29.refs_6_
  263.5 1.2 collective-permute-start.31
  265.0 5.2 %shard_map.87.refs_1_.refs_8_ = f32[33,64,128]{2,1,0:T(8,128)S(1)} custom-call(s32[2]{0:T(128)S(1)} %pad_add_fusion.3.chips_ref, bf16[8,65,16,128]{3,2,1,0:T(8,128)(2,1)S(1)} %copy-done.11, bf16[8,65,16,128]{3,2,1,0:T(8,128)(2,1)} %all-to-all-done.1.refs_0_.refs_1_, bf16[2,32,128,128]{3,2,1,0:T(8,128)(2,1)} %refs_2_.9, ...), custom_call_target="tpu_custom_call", output_to_operand_aliasing={{}: (9, {})} | custom-call | flops 4944999936 | tf_op jit(solution)/shard_map/pallas_call | solution.py:337
  271.1 6.2 %collective-permute-done.27.refs_0_ = bf16[32,64,128]{2,1,0:T(8,128)(2,1)} collective-permute-done((bf16[32,64,128]{2,1,0:T(8,128)(2,1)}, bf16[32,64,128]{2,1,0:T(8,128)(2,1)}, u32[]{:S(2)}, u32[]{:S(2)}) %collective-permute-start.27) | collective-permute-done | bytes 524320 | tf_op jit(solution)/shard_map/ppermute | solution.py:41
  277.9 2.1 shard_map.89
  280.9 5.2 %shard_map.90.refs_1_.refs_6_ = f32[33,64,128]{2,1,0:T(8,128)S(1)} custom-call(s32[2]{0:T(128)S(1)} %pad_add_fusion.4.chips_ref, bf16[8,65,16,128]{3,2,1,0:T(8,128)(2,1)S(1)} %copy-done.11, bf16[8,65,16,128]{3,2,1,0:T(8,128)(2,1)} %all-to-all-done.1.refs_0_.refs_1_, bf16[2,32,128,128]{3,2,1,0:T(8,128)(2,1)} %refs_2_.9, ...), custom_call_target="tpu_custom_call", output_to_operand_aliasing={{}: (9, {})} | custom-call | flops 4944999936 | tf_op jit(solution)/shard_map/pallas_call | solution.py:337
  287.0 2.5 collective-permute-done.32.refs_0_
  289.5 2.2 collective-permute-done.35.refs_5_
  291.8 4.1 %shard_map.92 = bf16[32,64,128]{2,1,0:T(8,128)(2,1)} custom-call(s32[1]{0:T(128)} %bitcast.chips_ref, bf16[8,65,16,128]{3,2,1,0:T(8,128)(2,1)S(1)} %copy-done.11, bf16[8,65,16,128]{3,2,1,0:T(8,128)(2,1)} %all-to-all-done.1.refs_0_.refs_1_, bf16[2,32,128,128]{3,2,1,0:T(8,128)(2,1)} %refs_2_.9, ...), custom_call_target="tpu_custom_call" | custom-call | flops 3335000064 | tf_op jit(solution)/shard_map/pallas_call | solution.py:337
  (141 shorter events, 34.7 us)
Async XLA Ops:
  0.6 1.6 copy-start.14
  7.7 56.2 %all-to-all-start = ((bf16[8,65,16,128]{3,2,1,0:T(8,128)(2,1)}), bf16[8,65,16,128]{3,2,1,0:T(8,128)(2,1)S(1)}, u32[]{:S(2)}, u32[]{:S(2)}) async-start(bf16[8,65,16,128]{3,2,1,0:T(8,128)(2,1)} %copy-done.13), calls=%async_computation | async-start | bytes 4259840 | tf_op jit(solution)/shard_map/all_to_all | solution.py:429
  16.3 2.7 collective-permute-start.1
  16.4 2.6 collective-permute-start
  23.1 46.8 %copy-start.40 = (bf16[32,128,128]{2,1,0:T(8,128)(2,1)S(1)}, bf16[32,128,128]{2,1,0:T(8,128)(2,1)}, u32[]{:S(2)}) copy-start(bf16[32,128,128]{2,1,0:T(8,128)(2,1)} %param.6) | copy-start | bytes 3145732
  65.4 131.4 %all-to-all-start.1 = ((bf16[8,65,16,128]{3,2,1,0:T(8,128)(2,1)}), bf16[8,65,16,128]{3,2,1,0:T(8,128)(2,1)}, u32[]{:S(2)}, u32[]{:S(2)}) async-start(bf16[8,65,16,128]{3,2,1,0:T(8,128)(2,1)} %copy-done.12), calls=%async_computation.1 | async-start | bytes 4259840 | tf_op jit(solution)/shard_map/all_to_all | solution.py:429
  69.9 107.0 %copy-start.41 = (s32[8]{0:T(128)S(1)}, s32[8]{0:T(128)}, u32[]{:S(2)}) copy-start(s32[8]{0:T(128)} %constant.98.clone) | copy-start | bytes 100
  70.0 70.7 %collective-permute-start.3 = (bf16[32,64,128]{2,1,0:T(8,128)(2,1)S(1)}, bf16[32,64,128]{2,1,0:T(8,128)(2,1)S(1)}, u32[]{:S(2)}, u32[]{:S(2)}) collective-permute-start(bf16[32,64,128]{2,1,0:T(8,128)(2,1)S(1)} %get-tuple-element.7.refs_2_.wave_ref), channel_id=1, source_target_pairs={{0,8},{1,9},{2,10},{3,11},{4,12},{5,13},{6,14},{7,15},{8,0},{9,1},... | collective-permute-start | bytes 1572872 | tf_op jit(solution)/shard_map/ppermute | solution.py:41
  72.7 69.3 %collective-permute-start.5 = (bf16[32,64,128]{2,1,0:T(8,128)(2,1)S(1)}, bf16[32,64,128]{2,1,0:T(8,128)(2,1)S(1)}, u32[]{:S(2)}, u32[]{:S(2)}) collective-permute-start(bf16[32,64,128]{2,1,0:T(8,128)(2,1)S(1)} %get-tuple-element.7.refs_2_.wave_ref), channel_id=1, source_target_pairs={{0,4},{1,5},{2,6},{3,7},{4,0},{5,1},{6,2},{7,3},{8,12},{9,13},{10,... | collective-permute-start | bytes 1572872 | tf_op jit(solution)/shard_map/ppermute | solution.py:41
  74.2 68.5 %collective-permute-start.9 = (bf16[32,64,128]{2,1,0:T(8,128)(2,1)S(1)}, bf16[32,64,128]{2,1,0:T(8,128)(2,1)S(1)}, u32[]{:S(2)}, u32[]{:S(2)}) collective-permute-start(bf16[32,64,128]{2,1,0:T(8,128)(2,1)S(1)} %get-tuple-element.7.refs_2_.wave_ref), channel_id=1, source_target_pairs={{0,2},{1,3},{2,0},{3,1},{4,6},{5,7},{6,4},{7,5},{8,10},{9,11},{10,... | collective-permute-start | bytes 1572872 | tf_op jit(solution)/shard_map/ppermute | solution.py:41
  140.7 12.2 %collective-permute-start.7 = (bf16[32,64,128]{2,1,0:T(8,128)(2,1)S(1)}, bf16[32,64,128]{2,1,0:T(8,128)(2,1)}, u32[]{:S(2)}, u32[]{:S(2)}) collective-permute-start(bf16[32,64,128]{2,1,0:T(8,128)(2,1)S(1)} %collective-permute-done.3.refs_4_), channel_id=1, source_target_pairs={{0,4},{1,5},{2,6},{3,7},{4,0},{5,1},{6,2},{7,3},{8,12},{9,13},{10,... | collective-permute-start | bytes 1572872 | tf_op jit(solution)/shard_map/ppermute | solution.py:41
  140.7 15.0 %collective-permute-start.11 = (bf16[32,64,128]{2,1,0:T(8,128)(2,1)S(1)}, bf16[32,64,128]{2,1,0:T(8,128)(2,1)}, u32[]{:S(2)}, u32[]{:S(2)}) collective-permute-start(bf16[32,64,128]{2,1,0:T(8,128)(2,1)S(1)} %collective-permute-done.3.refs_4_), channel_id=1, source_target_pairs={{0,2},{1,3},{2,0},{3,1},{4,6},{5,7},{6,4},{7,5},{8,10},{9,11},{10,... | collective-permute-start | bytes 1572872 | tf_op jit(solution)/shard_map/ppermute | solution.py:41
  142.1 22.6 %collective-permute-start.13 = (bf16[32,64,128]{2,1,0:T(8,128)(2,1)S(1)}, bf16[32,64,128]{2,1,0:T(8,128)(2,1)}, u32[]{:S(2)}, u32[]{:S(2)}) collective-permute-start(bf16[32,64,128]{2,1,0:T(8,128)(2,1)S(1)} %collective-permute-done.5.refs_6_), channel_id=1, source_target_pairs={{0,2},{1,3},{2,0},{3,1},{4,6},{5,7},{6,4},{7,5},{8,10},{9,11},{10,... | collective-permute-start | bytes 1572872 | tf_op jit(solution)/shard_map/ppermute | solution.py:41
  142.7 54.0 %collective-permute-start.2 = (bf16[2,32,128,128]{3,2,1,0:T(8,128)(2,1)}, bf16[2,32,128,128]{3,2,1,0:T(8,128)(2,1)}, u32[]{:S(2)}, u32[]{:S(2)}) collective-permute-start(bf16[2,32,128,128]{3,2,1,0:T(8,128)(2,1)} %refs_2_.9), channel_id=1, source_target_pairs={{0,1},{1,0},{2,3},{3,2},{4,5},{5,4},{6,7},{7,6},{8,9},{9,8},{10,11... | collective-permute-start | bytes 6291464 | tf_op jit(solution)/shard_map/ppermute | solution.py:41
  142.7 23.5 %collective-permute-start.4 = (bf16[32,64,128]{2,1,0:T(8,128)(2,1)S(1)}, bf16[32,64,128]{2,1,0:T(8,128)(2,1)S(1)}, u32[]{:S(2)}, u32[]{:S(2)}) collective-permute-start(bf16[32,64,128]{2,1,0:T(8,128)(2,1)S(1)} %collective-permute-done.3.refs_4_), channel_id=1, source_target_pairs={{0,1},{1,0},{2,3},{3,2},{4,5},{5,4},{6,7},{7,6},{8,9},{9,8},{10,11... | collective-permute-start | bytes 1572872 | tf_op jit(solution)/shard_map/ppermute | solution.py:41
  152.8 14.2 %collective-permute-start.6 = (bf16[32,64,128]{2,1,0:T(8,128)(2,1)S(1)}, bf16[32,64,128]{2,1,0:T(8,128)(2,1)S(1)}, u32[]{:S(2)}, u32[]{:S(2)}) collective-permute-start(bf16[32,64,128]{2,1,0:T(8,128)(2,1)S(1)} %collective-permute-done.5.refs_6_), channel_id=1, source_target_pairs={{0,1},{1,0},{2,3},{3,2},{4,5},{5,4},{6,7},{7,6},{8,9},{9,8},{10,11... | collective-permute-start | bytes 1572872 | tf_op jit(solution)/shard_map/ppermute | solution.py:41
  155.7 12.7 %collective-permute-start.10 = (bf16[32,64,128]{2,1,0:T(8,128)(2,1)S(1)}, bf16[32,64,128]{2,1,0:T(8,128)(2,1)S(1)}, u32[]{:S(2)}, u32[]{:S(2)}) collective-permute-start(bf16[32,64,128]{2,1,0:T(8,128)(2,1)S(1)} %collective-permute-done.9.refs_10_), channel_id=1, source_target_pairs={{0,1},{1,0},{2,3},{3,2},{4,5},{5,4},{6,7},{7,6},{8,9},{9,8},{10,11... | collective-permute-start | bytes 1572872 | tf_op jit(solution)/shard_map/ppermute | solution.py:41
  164.7 12.1 %collective-permute-start.15 = (bf16[32,64,128]{2,1,0:T(8,128)(2,1)}, bf16[32,64,128]{2,1,0:T(8,128)(2,1)}, u32[]{:S(2)}, u32[]{:S(2)}) collective-permute-start(bf16[32,64,128]{2,1,0:T(8,128)(2,1)} %collective-permute-done.7.refs_8_), channel_id=1, source_target_pairs={{0,2},{1,3},{2,0},{3,1},{4,6},{5,7},{6,4},{7,5},{8,10},{9,11},{10,... | collective-permute-start | bytes 1572872 | tf_op jit(solution)/shard_map/ppermute | solution.py:41
  167.1 9.8 %collective-permute-start.8 = (bf16[32,64,128]{2,1,0:T(8,128)(2,1)}, bf16[32,64,128]{2,1,0:T(8,128)(2,1)}, u32[]{:S(2)}, u32[]{:S(2)}) collective-permute-start(bf16[32,64,128]{2,1,0:T(8,128)(2,1)} %collective-permute-done.7.refs_8_), channel_id=1, source_target_pairs={{0,1},{1,0},{2,3},{3,2},{4,5},{5,4},{6,7},{7,6},{8,9},{9,8},{10,11... | collective-permute-start | bytes 1572872 | tf_op jit(solution)/shard_map/ppermute | solution.py:41
  167.9 9.0 %collective-permute-start.12 = (bf16[32,64,128]{2,1,0:T(8,128)(2,1)}, bf16[32,64,128]{2,1,0:T(8,128)(2,1)S(1)}, u32[]{:S(2)}, u32[]{:S(2)}) collective-permute-start(bf16[32,64,128]{2,1,0:T(8,128)(2,1)} %collective-permute-done.11.refs_12_), channel_id=1, source_target_pairs={{0,1},{1,0},{2,3},{3,2},{4,5},{5,4},{6,7},{7,6},{8,9},{9,8},{10,11... | collective-permute-start | bytes 1572872 | tf_op jit(solution)/shard_map/ppermute | solution.py:41
  169.2 8.5 %collective-permute-start.14 = (bf16[32,64,128]{2,1,0:T(8,128)(2,1)}, bf16[32,64,128]{2,1,0:T(8,128)(2,1)S(1)}, u32[]{:S(2)}, u32[]{:S(2)}) collective-permute-start(bf16[32,64,128]{2,1,0:T(8,128)(2,1)} %collective-permute-done.13.refs_14_), channel_id=1, source_target_pairs={{0,1},{1,0},{2,3},{3,2},{4,5},{5,4},{6,7},{7,6},{8,9},{9,8},{10,11... | collective-permute-start | bytes 1572872 | tf_op jit(solution)/shard_map/ppermute | solution.py:41
  176.8 2.3 collective-permute-start.16
  179.0 1.6 copy-start.9
  214.6 1.2 collective-permute-start.17
  215.9 3.7 %collective-permute-start.18 = (f32[16,128]{1,0:T(8,128)S(1)}, f32[16,128]{1,0:T(8,128)S(1)}, u32[]{:S(2)}, u32[]{:S(2)}) collective-permute-start(f32[16,128]{1,0:T(8,128)S(1)} %add.88), channel_id=1, source_target_pairs={{0,2},{1,3},{2,0},{3,1},{4,6},{5,7},{6,4},{7,5},{8,10},{9,11},{10,... | collective-permute-start | bytes 24584 | tf_op jit(solution)/shard_map/ppermute | solution.py:108
  219.5 3.7 %collective-permute-start.19 = (f32[16,128]{1,0:T(8,128)S(1)}, f32[16,128]{1,0:T(8,128)S(1)}, u32[]{:S(2)}, u32[]{:S(2)}) collective-permute-start(f32[16,128]{1,0:T(8,128)S(1)} %add.89), channel_id=1, source_target_pairs={{0,4},{1,5},{2,6},{3,7},{4,0},{5,1},{6,2},{7,3},{8,12},{9,13},{10,... | collective-permute-start | bytes 24584 | tf_op jit(solution)/shard_map/ppermute | solution.py:108
  223.2 5.9 %collective-permute-start.20 = (f32[16,128]{1,0:T(8,128)S(1)}, f32[16,128]{1,0:T(8,128)S(1)}, u32[]{:S(2)}, u32[]{:S(2)}) collective-permute-start(f32[16,128]{1,0:T(8,128)S(1)} %add.90), channel_id=1, source_target_pairs={{0,8},{1,9},{2,10},{3,11},{4,12},{5,13},{6,14},{7,15},{8,0},{9,1},... | collective-permute-start | bytes 24584 | tf_op jit(solution)/shard_map/ppermute | solution.py:108
  230.5 2.1 collective-permute-start.22
  230.5 14.7 %collective-permute-start.21 = (bf16[32,64,128]{2,1,0:T(8,128)(2,1)}, bf16[32,64,128]{2,1,0:T(8,128)(2,1)}, u32[]{:S(2)}, u32[]{:S(2)}) collective-permute-start(bf16[32,64,128]{2,1,0:T(8,128)(2,1)} %get-tuple-element.4.refs_4_), channel_id=1, source_target_pairs={{0,4},{1,5},{2,0},{3,1},{4,8},{5,9},{6,2},{7,3},{8,12},{9,13},{10,... | collective-permute-start | bytes 1572872 | tf_op jit(solution)/shard_map/ppermute | solution.py:41
  231.1 15.5 %collective-permute-start.25 = (bf16[32,64,128]{2,1,0:T(8,128)(2,1)}, bf16[32,64,128]{2,1,0:T(8,128)(2,1)}, u32[]{:S(2)}, u32[]{:S(2)}) collective-permute-start(bf16[32,64,128]{2,1,0:T(8,128)(2,1)} %get-tuple-element.4.refs_4_), channel_id=1, source_target_pairs={{0,2},{1,3},{2,6},{3,7},{4,0},{5,1},{6,10},{7,11},{8,4},{9,5},{10,... | collective-permute-start | bytes 1572872 | tf_op jit(solution)/shard_map/ppermute | solution.py:41
  232.6 1.6 copy-start.10
  234.2 14.7 %copy-start.11 = (bf16[8,65,16,128]{3,2,1,0:T(8,128)(2,1)S(1)}, bf16[8,65,16,128]{3,2,1,0:T(8,128)(2,1)}, u32[]{:S(2)}) copy-start(bf16[8,65,16,128]{3,2,1,0:T(8,128)(2,1)} %copy-done.8) | copy-start | bytes 6389764
  245.1 3.7 %copy-start.1 = (f32[33,64,128]{2,1,0:T(8,128)S(1)}, f32[33,64,128]{2,1,0:T(8,128)}, u32[]{:S(2)}) copy-start(f32[33,64,128]{2,1,0:T(8,128)} %copy-done) | copy-start | bytes 3244036
  245.2 3.6 %collective-permute-start.24 = (bf16[32,64,128]{2,1,0:T(8,128)(2,1)}, bf16[32,64,128]{2,1,0:T(8,128)(2,1)}, u32[]{:S(2)}, u32[]{:S(2)}) collective-permute-start(bf16[32,64,128]{2,1,0:T(8,128)(2,1)} %shard_map.84.refs_4_), channel_id=1, source_target_pairs={{0,1},{1,0},{2,3},{3,2},{4,5},{5,4},{6,7},{7,6},{8,9},{9,8},{10,11... | collective-permute-start | bytes 1572872 | tf_op jit(solution)/shard_map/ppermute | solution.py:41
  246.6 2.3 collective-permute-start.26
  246.6 14.7 %collective-permute-start.23 = (bf16[32,64,128]{2,1,0:T(8,128)(2,1)}, bf16[32,64,128]{2,1,0:T(8,128)(2,1)}, u32[]{:S(2)}, u32[]{:S(2)}) collective-permute-start(bf16[32,64,128]{2,1,0:T(8,128)(2,1)} %shard_map.84.refs_4_), channel_id=1, source_target_pairs={{0,4},{1,5},{2,0},{3,1},{4,8},{5,9},{6,2},{7,3},{8,12},{9,13},{10,... | collective-permute-start | bytes 1572872 | tf_op jit(solution)/shard_map/ppermute | solution.py:41
  248.3 14.4 %collective-permute-start.29 = (bf16[32,64,128]{2,1,0:T(8,128)(2,1)}, bf16[32,64,128]{2,1,0:T(8,128)(2,1)}, u32[]{:S(2)}, u32[]{:S(2)}) collective-permute-start(bf16[32,64,128]{2,1,0:T(8,128)(2,1)} %collective-permute-done.25.refs_6_), channel_id=1, source_target_pairs={{0,2},{1,3},{2,6},{3,7},{4,0},{5,1},{6,10},{7,11},{8,4},{9,5},{10,... | collective-permute-start | bytes 1572872 | tf_op jit(solution)/shard_map/ppermute | solution.py:41
  261.3 3.7 %copy-start.3 = (f32[33,64,128]{2,1,0:T(8,128)S(1)}, f32[33,64,128]{2,1,0:T(8,128)}, u32[]{:S(2)}) copy-start(f32[33,64,128]{2,1,0:T(8,128)} %copy-done.2) | copy-start | bytes 3244036
  261.3 3.5 %collective-permute-start.28 = (bf16[32,64,128]{2,1,0:T(8,128)(2,1)}, bf16[32,64,128]{2,1,0:T(8,128)(2,1)}, u32[]{:S(2)}, u32[]{:S(2)}) collective-permute-start(bf16[32,64,128]{2,1,0:T(8,128)(2,1)} %shard_map.86.refs_4_), channel_id=1, source_target_pairs={{0,1},{1,0},{2,3},{3,2},{4,5},{5,4},{6,7},{7,6},{8,9},{9,8},{10,11... | collective-permute-start | bytes 1572872 | tf_op jit(solution)/shard_map/ppermute | solution.py:41
  262.7 2.3 collective-permute-start.30
  262.7 14.7 %collective-permute-start.27 = (bf16[32,64,128]{2,1,0:T(8,128)(2,1)}, bf16[32,64,128]{2,1,0:T(8,128)(2,1)}, u32[]{:S(2)}, u32[]{:S(2)}) collective-permute-start(bf16[32,64,128]{2,1,0:T(8,128)(2,1)} %shard_map.86.refs_4_), channel_id=1, source_target_pairs={{0,4},{1,5},{2,0},{3,1},{4,8},{5,9},{6,2},{7,3},{8,12},{9,13},{10,... | collective-permute-start | bytes 1572872 | tf_op jit(solution)/shard_map/ppermute | solution.py:41
  263.5 14.2 %collective-permute-start.31 = (bf16[32,64,128]{2,1,0:T(8,128)(2,1)}, bf16[32,64,128]{2,1,0:T(8,128)(2,1)}, u32[]{:S(2)}, u32[]{:S(2)}) collective-permute-start(bf16[32,64,128]{2,1,0:T(8,128)(2,1)} %collective-permute-done.29.refs_6_), channel_id=1, source_target_pairs={{0,2},{1,3},{2,6},{3,7},{4,0},{5,1},{6,10},{7,11},{8,4},{9,5},{10,... | collective-permute-start | bytes 1572872 | tf_op jit(solution)/shard_map/ppermute | solution.py:41
  277.4 3.5 %copy-start.5 = (f32[33,64,128]{2,1,0:T(8,128)S(1)}, f32[33,64,128]{2,1,0:T(8,128)}, u32[]{:S(2)}) copy-start(f32[33,64,128]{2,1,0:T(8,128)} %copy-done.4) | copy-start | bytes 3244036
  277.4 3.5 %collective-permute-start.33 = (bf16[32,64,128]{2,1,0:T(8,128)(2,1)}, bf16[32,64,128]{2,1,0:T(8,128)(2,1)}, u32[]{:S(2)}, u32[]{:S(2)}) collective-permute-start(bf16[32,64,128]{2,1,0:T(8,128)(2,1)} %shard_map.88.lower_ref.refs_4_), channel_id=1, source_target_pairs={{0,1},{1,0},{2,3},{3,2},{4,5},{5,4},{6,7},{7,6},{8,9},{9,8},{10,11... | collective-permute-start | bytes 1572872 | tf_op jit(solution)/shard_map/ppermute | solution.py:41
  277.7 3.2 %collective-permute-start.34 = (bf16[32,64,128]{2,1,0:T(8,128)(2,1)}, bf16[32,64,128]{2,1,0:T(8,128)(2,1)}, u32[]{:S(2)}, u32[]{:S(2)}) collective-permute-start(bf16[32,64,128]{2,1,0:T(8,128)(2,1)} %collective-permute-done.31.upper_ref.refs_6_), channel_id=1, source_target_pairs={{0,1},{1,0},{2,3},{3,2},{4,5},{5,4},{6,7},{7,6},{8,9},{9,8},{10,11... | collective-permute-start | bytes 1572872 | tf_op jit(solution)/shard_map/ppermute | solution.py:41
  280.0 9.5 %collective-permute-start.32 = (bf16[32,64,128]{2,1,0:T(8,128)(2,1)}, bf16[32,64,128]{2,1,0:T(8,128)(2,1)}, u32[]{:S(2)}, u32[]{:S(2)}) collective-permute-start(bf16[32,64,128]{2,1,0:T(8,128)(2,1)} %shard_map.89), channel_id=1, source_target_pairs={{0,4},{1,3},{2,0},{3,7},{4,8},{5,1},{6,2},{7,11},{8,12},{9,5},{10,... | collective-permute-start | bytes 1572872 | tf_op jit(solution)/shard_map/ppermute | solution.py:41
  289.5 2.3 copy-start.7
  289.5 2.3 collective-permute-start.35
  (32 other events, 32.5 us)

commit v7 on v5

--- a/solution.py
+++ b/solution.py
@@ -10,6 +10,9 @@
 BOTH = ("sec", "term")
 VMEM_LIMIT = 20 * 2**20
 PART = 16
+ORDER = [0, 4, 5, 1, 2, 6, 3, 7]
+WAITS = {4: 1, 2: 5, 6: 2}
+PIECE_WAITS = {6: 4, 7: 5}
 RING_BYTES = 24 * 2**20
 
 
@@ -98,22 +101,23 @@
         masks.append(step)
         units[step] = exchange(unit, owners, halves, step)
         step //= 2
-    for mask in masks[:-1]:
-        units[mask] = after(units[mask], lefts[masks[0]])
+    waits = dict(WAITS)
     for step in masks[1:]:
         for mask in [m for m in units if m >= 2 * step and m % (2 * step) == 0]:
+            if mask in waits:
+                units[mask] = after(units[mask], lefts[waits.pop(mask)])
             units[mask | step] = exchange(units[mask], owners, halves, step)
     return units
 
 
-def doubled(value, count, axes, stride):
+def spread(value, devices):
     step = 1
-    total = lax.axis_size("sec") * lax.axis_size("term")
-    while step < count:
-        value = value + lax.ppermute(
-            value, axes, [(d, d ^ (step * stride)) for d in range(total)]
-        )
-        step *= 2
+    while step < devices:
+        masks = [step] if 2 * step == devices else [step, 2 * step, 3 * step]
+        parts = [lax.ppermute(value, BOTH, [(d, d ^ m) for d in range(devices)]) for m in masks]
+        for part in parts:
+            value = value + part
+        step *= 4
     return value
 
 
@@ -225,94 +229,166 @@
             )
 
 
-def apply_kernel(sources, first, choices, last, streams, capacity, ids_ref, *refs):
+def read_labels(raw, spread_labels, labels, sem):
+    spread_labels[...] = raw[:8].astype(jnp.float32).astype(jnp.int32)
+    copy = pltpu.make_async_copy(spread_labels, labels, sem)
+    copy.start()
+    copy.wait()
+
+
+def first_kernel(first, streams, capacity, chip_ref, piece, near, far, own, other, *refs):
     refs = list(refs)
-    lefts = [refs.pop(0) for _ in range(choices or sources)]
+    total_in = None if first else refs.pop(0)
+    if not first:
+        refs.pop(0)
+    total, kept, spread_labels, labels, label_sem, kept_sem = refs
+    keep = pltpu.make_async_copy(piece, kept.at[chip_ref[0]], kept_sem)
+    keep.start()
+    total[...] = jnp.zeros_like(total) if first else total_in[...]
+    read_labels(piece.at[piece.shape[0] - 1], spread_labels, labels, label_sem)
+    add_products(piece, labels, near, far, (own, other), total, streams, capacity)
+    keep.wait()
+
+
+def first_group(chip, piece, near, far, rights, total, kept):
+    blocks, rows, width = near.shape
+    streams = 2 * rights[0].shape[0]
+    capacity = (piece.shape[0] - 1) * PART // (streams * rows)
+    first = total is None
+    whole = pl.BlockSpec(memory_space=pltpu.VMEM)
+    anywhere = pl.BlockSpec(memory_space=pl.ANY)
+    arrays, specs, aliases = [piece, near, far, *rights], [whole] * 5, {}
+    if not first:
+        arrays += [total, kept]
+        specs += [whole, anywhere]
+        aliases = {6: 0, 7: 1}
+    return pl.pallas_call(
+        functools.partial(first_kernel, first, streams, capacity),
+        out_shape=(
+            jax.ShapeDtypeStruct((blocks + 1, rows, width), jnp.float32),
+            jax.ShapeDtypeStruct((lax.axis_size("sec"),) + piece.shape, piece.dtype),
+        ),
+        in_specs=[pl.BlockSpec(memory_space=pltpu.SMEM)] + specs,
+        out_specs=(whole, anywhere),
+        scratch_shapes=[
+            pltpu.VMEM((8, width), jnp.int32),
+            pltpu.SMEM((8, width), jnp.int32),
+            pltpu.SemaphoreType.DMA,
+            pltpu.SemaphoreType.DMA,
+        ],
+        input_output_aliases=aliases,
+        compiler_params=pltpu.CompilerParams(vmem_limit_bytes=VMEM_LIMIT),
+        cost_estimate=busy(2.5),
+    )(jnp.reshape(chip, (1,)).astype(jnp.int32), *arrays)
+
+
+def second_kernel(sources, first, last, streams, capacity, chips_ref, kept, *refs):
+    refs = list(refs)
+    rights = [refs.pop(0), refs.pop(0)]
     vectors = [(refs.pop(0), refs.pop(0)) for _ in range(sources)]
-    rights = refs.pop(0), refs.pop(0)
     total_in = None if first else refs.pop(0)
-    out = refs.pop(0) if last else None
-    total = refs.pop(0)
-    spread_labels, labels, label_sems = refs.pop(0), refs.pop(0), refs.pop(0)
-    blocks = vectors[0][0].shape[0]
-
-    if choices:
-        chosen, chosen_sems = refs.pop(0), refs.pop(0)
-        for index in range(sources):
-            for choice, left in enumerate(lefts):
-
-                @pl.when(ids_ref[index] == choice)
-                def _():
-                    pltpu.make_async_copy(left, chosen.at[index], chosen_sems.at[index]).start()
-
+    if last:
+        out, total = refs.pop(0), refs.pop(0)
+    else:
+        total, token = refs.pop(0), refs.pop(0)
+        token[...] = jnp.zeros_like(token)
+    left, right, vector, spread_labels, labels = refs[:5]
+    left_sems, right_sems, vector_sems, label_sem = refs[5:]
+    blocks = vector.shape[2]
+
+    def left_copy(source):
+        return pltpu.make_async_copy(
+            kept.at[chips_ref[source]], left.at[source], left_sems.at[source]
+        )
+
+    def right_copy(side):
+        return pltpu.make_async_copy(rights[side], right.at[side], right_sems.at[side])
+
+    def vector_copy(source, part):
+        return pltpu.make_async_copy(
+            vectors[source][part], vector.at[source, part], vector_sems.at[source, part]
+        )
+
+    for source in range(sources):
+        left_copy(source).start()
+        for part in range(2):
+            vector_copy(source, part).start()
+    for side in range(2):
+        right_copy(side).start()
     total[...] = jnp.zeros_like(total) if first else total_in[...]
-    pieces = []
-    for index in range(sources):
-        if choices:
-            pltpu.make_async_copy(lefts[0], chosen.at[index], chosen_sems.at[index]).wait()
-            piece = chosen.at[index]
-        else:
-            piece = lefts[index]
-        pieces.append(piece)
-        values = piece[piece.shape[0] - 1].astype(jnp.float32).astype(jnp.int32)
-        spread_labels[index] = values[:8]
-        pltpu.make_async_copy(
-            spread_labels.at[index], labels.at[index], label_sems.at[index]
-        ).start()
-    for index, (near, far) in enumerate(vectors):
-        pltpu.make_async_copy(
-            spread_labels.at[index], labels.at[index], label_sems.at[index]
-        ).wait()
+    for source in range(sources):
+        left_copy(source).wait()
+        read_labels(
+            left.at[source, left.shape[1] - 1],
+            spread_labels.at[source],
+            labels.at[source],
+            label_sem,
+        )
+    for side in range(2):
+        right_copy(side).wait()
+    for source in range(sources):
+        for part in range(2):
+            vector_copy(source, part).wait()
         add_products(
-            pieces[index], labels.at[index], near, far, rights, total, streams, capacity
+            left.at[source],
+            labels.at[source],
+            vector.at[source, 0],
+            vector.at[source, 1],
+            (right.at[0], right.at[1]),
+            total,
+            streams,
+            capacity,
         )
     if last:
         out[...] = total[:blocks].astype(out.dtype)
 
 
-def apply_group(ids, lefts, vectors, rights, total, choices, last):
+def second_group(chips, kept, vectors, rights, total, last):
     blocks, rows, width = vectors[0][0].shape
     streams = 2 * rights[0].shape[0]
-    capacity = (lefts[0].shape[0] - 1) * PART // (streams * rows)
-    sources = len(vectors)
-    first = total is None
-    arrays = list(lefts) + [unit for pair in vectors for unit in pair] + list(rights)
+    capacity = (kept.shape[1] - 1) * PART // (streams * rows)
+    sources, first = len(vectors), total is None
+    arrays = [kept, *rights] + [unit for pair in vectors for unit in pair]
+    whole = pl.BlockSpec(memory_space=pltpu.VMEM)
+    specs = [pl.BlockSpec(memory_space=pl.ANY)] * len(arrays)
     if not first:
         arrays.append(total)
-    whole = pl.BlockSpec(memory_space=pltpu.VMEM)
+        specs.append(whole)
     total_shape = (blocks + 1, rows, width)
     scratch = [
+        pltpu.VMEM((sources,) + kept.shape[1:], kept.dtype),
+        pltpu.VMEM((2,) + rights[0].shape, rights[0].dtype),
+        pltpu.VMEM((sources, 2, blocks, rows, width), jnp.bfloat16),
         pltpu.VMEM((sources, 8, width), jnp.int32),
         pltpu.SMEM((sources, 8, width), jnp.int32),
         pltpu.SemaphoreType.DMA((sources,)),
+        pltpu.SemaphoreType.DMA((2,)),
+        pltpu.SemaphoreType.DMA((sources, 2)),
+        pltpu.SemaphoreType.DMA,
     ]
-    specs = [whole] * len(arrays)
-    if choices:
-        scratch += [
-            pltpu.VMEM((sources,) + lefts[0].shape, lefts[0].dtype),
-            pltpu.SemaphoreType.DMA((sources,)),
-        ]
-        specs[: len(lefts)] = [pl.BlockSpec(memory_space=pl.ANY)] * len(lefts)
     aliases = {}
     if last:
         out_shape = jax.ShapeDtypeStruct((blocks, rows, width), jnp.bfloat16)
+        out_specs = whole
         scratch = [pltpu.VMEM(total_shape, jnp.float32)] + scratch
     else:
-        out_shape = jax.ShapeDtypeStruct(total_shape, jnp.float32)
+        out_shape = (
+            jax.ShapeDtypeStruct(total_shape, jnp.float32),
+            jax.ShapeDtypeStruct((8, width), jnp.float32),
+        )
+        out_specs = (whole, whole)
         if not first:
             aliases = {len(arrays): 0}
     return pl.pallas_call(
-        functools.partial(
-            apply_kernel, sources, first, len(lefts) if choices else 0, last, streams, capacity
-        ),
+        functools.partial(second_kernel, sources, first, last, streams, capacity),
         out_shape=out_shape,
         in_specs=[pl.BlockSpec(memory_space=pltpu.SMEM)] + specs,
-        out_specs=whole,
+        out_specs=out_specs,
         scratch_shapes=scratch,
         input_output_aliases=aliases,
         compiler_params=pltpu.CompilerParams(vmem_limit_bytes=VMEM_LIMIT),
-        cost_estimate=busy(0.7 + 1.4 * sources),
-    )(ids, *arrays)
+        cost_estimate=busy(1.5 + 1.4 * sources),
+    )(chips.astype(jnp.int32), *arrays)
 
 
 def stats_kernel(ids_ref, total_ref, wave_ref, stats_ref):
@@ -367,7 +443,7 @@
         out_specs=whole,
         compiler_params=params,
     )(ids, total, wave)
-    stats = doubled(stats, devices, BOTH, 1)
+    stats = spread(stats, devices)
     return pl.pallas_call(
         functools.partial(direction_kernel, entries),
         out_shape=(
@@ -395,10 +471,7 @@
     other_left = swap(
         lax.dynamic_slice_in_dim(left_operator, (1 - half) * rows, rows, 2), owners, halves
     )
-    far_pieces = list(range(owners // 2, owners))
-    order = [0, far_pieces[0]]
-    for m in range(1, owners // 2):
-        order += [far_pieces[m], m]
+    order = [m for m in ORDER if m < owners] + list(range(len(ORDER), owners))
     rights = (right_operator, swap(right_operator, owners, halves))
     pieces = pack(
         ids,
@@ -406,31 +479,31 @@
         swap(plan, owners, halves),
         left_operator,
         other_left,
-        rights[1],
+        plan,
         order[1:] + order[:1],
         capacity,
     )
-    lefts = [exchange(piece, owners, halves, m) if m else piece for m, piece in enumerate(pieces)]
+    lefts = [pieces[0]]
+    for m in range(1, owners):
+        piece = pieces[m]
+        if m in PIECE_WAITS:
+            piece = after(piece, lefts[PIECE_WAITS[m]])
+        lefts.append(exchange(piece, owners, halves, m))
     near = mask_gather(own_rows, lefts, owners, halves)
     far = {m: swap(unit, owners, halves) if m else other_rows for m, unit in near.items()}
 
-    total = None
-    no_choice = jnp.zeros((1,), jnp.int32)
+    total = kept = None
     for m in order:
-        total = apply_group(
-            no_choice, [lefts[m]], [(near[m], far[m])], rights, total, False, False
-        )
+        total, kept = first_group(me ^ m, lefts[m], near[m], far[m], rights, total, kept)
 
     entries = blocks * owners * height * width
     direction, rayleigh = new_direction(ids, total, own_rows, owners, halves, entries)
     reach = (owners - 1) // 2
 
     def add_group(total, units, last):
-        choice = jnp.stack([ring_owner(place - s, owners) ^ me for s in units])
-        vectors = [
-            (unit, swap(unit, owners, halves)) for unit in units.values()
-        ]
-        return apply_group(choice.astype(jnp.int32), lefts, vectors, rights, total, True, last)
+        chips = jnp.stack([ring_owner(place - s, owners) for s in units])
+        vectors = [(unit, swap(unit, owners, halves)) for unit in units.values()]
+        return second_group(chips, kept, vectors, rights, total, last)
 
     ahead = behind = direction
     units = {0: direction}
@@ -438,13 +511,13 @@
     for step in range(1, reach + 1):
         ahead_next = ring_send(ahead, owners, halves, (1,) * halves)
         behind_next = ring_send(behind, owners, halves, (-1,) * halves)
-        total = add_group(total, units, False)
-        ahead, behind = after(ahead_next, total), behind_next
+        total, token = add_group(total, units, False)
+        ahead, behind = after(ahead_next, token), behind_next
         units = {step: ahead, -step: behind}
     last = select_half(half, ahead, behind)
     last = ring_send(last, owners, halves, (1, -1))
-    total = add_group(total, units, False)
-    total = add_group(total, {owners // 2: after(last, total)}, True)
+    total, token = add_group(total, units, False)
+    total = add_group(total, {owners // 2: after(last, token)}, True)
     return (total, rayleigh[0])
 
 

time: 264 us -> 252 us (0.955)
  waiting for transfers between devices: 118 us -> 94.7 us
  Pallas kernels: 46.6 us -> 53.8 us
  local copies, waits for them, and re-layouts: 57.5 us -> 64.2 us
    ppermute x39, waiting for transfers between devices: 110 us -> 89.7 us  [permute(): return lax.ppermute(value, BOTH, pairs)]
    pallas_call x13, Pallas kernels: 36.6 us -> 44.6 us  [the longest x8 26 us: first_group(): pl.pallas_call(functools.partial(first_kernel, first, streams, capacity),...]
    unnamed x122 -> x104, local copies, waits for them, and re-layouts: 53.1 us -> 59.7 us
    ppermute x4 -> x6, waiting for transfers between devices: 7.9 us -> 5.06 us  [spread(): lax.ppermute(value, BOTH, [(d, d ^ m) for d in range(devices)])]
    ppermute x4 -> x6, starting transfers between devices: 7.68 us -> 6.44 us  [spread(): lax.ppermute(value, BOTH, [(d, d ^ m) for d in range(devices)])]
  transfers between devices with their start and end apart: 43 -> 45, of which waited for: 20 -> 19; matrix products, arithmetic and copies ran while one was open for 2% -> 1% of each run, Pallas kernels for 15% -> 18%
where the time goes in v7:
time: 252 us; the launch traced here: 251 us
  waiting for transfers between devices  94.7 us (38%)
  local copies, waits for them, and re-layouts  64.2 us (25%)
  Pallas kernels  53.8 us (21%)
  starting transfers between devices  36.4 us (14%)
    ppermute x39, waiting for transfers between devices, permute(): return lax.ppermute(value, BOTH, pairs)  89.7 us
    unnamed x104, local copies, waits for them, and re-layouts  59.7 us
    ppermute x39, starting transfers between devices, permute(): return lax.ppermute(value, BOTH, pairs)  30 us
    pallas_call x8, Pallas kernels, first_group(): pl.pallas_call(functools.partial(first_kernel, first, streams, capacity),...  26 us
    pallas_call x5, Pallas kernels, second_group(): pl.pallas_call(functools.partial(second_kernel, sources, first, last, str...  18.6 us
    ppermute x6, starting transfers between devices, spread(): lax.ppermute(value, BOTH, [(d, d ^ m) for d in range(devices)])  6.44 us
    ppermute x6, waiting for transfers between devices, spread(): lax.ppermute(value, BOTH, [(d, d ^ m) for d in range(devices)])  5.06 us
  transfers between devices with their start and end apart: 45, of which 19 were waited for; matrix products, arithmetic and copies ran while one was open for 1% of the time, Pallas kernels for 18%

profile of v7, /device:TPU:0, one launch (start us, length us, event | category | flops | bytes accessed | tf_op | source)
XLA Modules:
  0.0 250.7 jit_solution(15849395458870356160)
XLA Ops:
  0.7 2.4 constant_dynamic-slice_fusion.2
  4.1 2.1 constant_dynamic-slice_fusion
  6.2 3.6 %collective-permute-start.4 = (bf16[32,64,128]{2,1,0:T(8,128)(2,1)S(1)}, bf16[32,64,128]{2,1,0:T(8,128)(2,1)}, u32[]{:S(2)}, u32[]{:S(2)}) collective-permute-start(bf16[32,64,128]{2,1,0:T(8,128)(2,1)S(1)} %get-tuple-element.71.near.wave_ref), channel_id=1, source_target_pairs={{0,8},{1,9},{2,10},{3,11},{4,12},{5,13},{6,14},{7,15},{8,0},{9,1},... | collective-permute-start | bytes 1572872 | tf_op jit(solution)/shard_map/ppermute | solution.py:44
  11.5 4.5 %shard_map.68 = (bf16[129,16,128]{2,1,0:T(8,128)(2,1)S(1)}, bf16[129,16,128]{2,1,0:T(8,128)(2,1)S(1)}, bf16[129,16,128]{2,1,0:T(8,128)(2,1)S(1)}, bf16[129,16,12...) custom-call(s32[3]{0:T(128)S(1)} %pad_add_fusion.1.ids_ref, ...), custom_call_target="tpu_custom_call" | custom-call | flops 5750000128 | tf_op jit(solution)/shard_map/pallas_call | solution.py:187
  23.7 10.2 %collective-permute-done.4.refs_0_ = bf16[32,64,128]{2,1,0:T(8,128)(2,1)} collective-permute-done((bf16[32,64,128]{2,1,0:T(8,128)(2,1)S(1)}, bf16[32,64,128]{2,1,0:T(8,128)(2,1)}, u32[]{:S(2)}, u32[]{:S(2)}) %collective-permute-start.4) | collective-permute-done | bytes 524320 | tf_op jit(solution)/shard_map/ppermute | solution.py:44
  35.7 2.9 %collective-permute-start.2 = (bf16[129,16,128]{2,1,0:T(8,128)(2,1)}, bf16[129,16,128]{2,1,0:T(8,128)(2,1)S(1)}, u32[]{:S(2)}, u32[]{:S(2)}) collective-permute-start(bf16[129,16,128]{2,1,0:T(8,128)(2,1)} %get-tuple-element.37), channel_id=1, source_target_pairs={{0,10},{1,11},{2,8},{3,9},{4,14},{5,15},{6,12},{7,13},{8,2},{9,3},... | collective-permute-start | bytes 1585160 | tf_op jit(solution)/shard_map/ppermute | solution.py:44
  38.6 6.9 %collective-permute-done.19.near = bf16[32,64,128]{2,1,0:T(8,128)(2,1)} collective-permute-done((bf16[32,64,128]{2,1,0:T(8,128)(2,1)S(1)}, bf16[32,64,128]{2,1,0:T(8,128)(2,1)}, u32[]{:S(2)}, u32[]{:S(2)}) %collective-permute-start.19) | collective-permute-done | bytes 524320 | tf_op jit(solution)/shard_map/ppermute | solution.py:44
  48.6 24.0 %collective-permute-done.15.refs_1_.piece = bf16[129,16,128]{2,1,0:T(8,128)(2,1)} collective-permute-done((bf16[129,16,128]{2,1,0:T(8,128)(2,1)}, bf16[129,16,128]{2,1,0:T(8,128)(2,1)}, u32[]{:S(2)}, u32[]{:S(2)}) %collective-permute-start.15) | collective-permute-done | bytes 528416 | tf_op jit(solution)/shard_map/ppermute | solution.py:44
  72.6 11.0 %collective-permute-done.2.refs_1_.piece = bf16[129,16,128]{2,1,0:T(8,128)(2,1)S(1)} collective-permute-done((bf16[129,16,128]{2,1,0:T(8,128)(2,1)}, bf16[129,16,128]{2,1,0:T(8,128)(2,1)S(1)}, u32[]{:S(2)}, u32[]{:S(2)}) %collective-permute-start.2) | collective-permute-done | bytes 528416 | tf_op jit(solution)/shard_map/ppermute | solution.py:44
  88.1 3.0 %shard_map.74 = (f32[33,64,128]{2,1,0:T(8,128)S(1)}, bf16[8,129,16,128]{3,2,1,0:T(8,128)(2,1)S(1)}) custom-call(s32[1]{0:T(128)} %bitcast.2.chip_ref, bf16[129,16,128]{2,1,0:T(8,128)(2,1)S(1)} %copy-done.49, bf16[32,64,128]{2,1,0:T(8,128)(2,1)S(1)} %copy-done.20, bf16[32,64,128]{2,1,0:T(8,128)(2,1)S(1)} %copy-done.28, ...), custom_call_target="tpu_custom_call" | custom-call | flops 2875000064 | tf_op jit(solution)/shard_map/pallas_call | solution.py:265
  91.1 2.0 copy-done
  95.4 2.7 %collective-permute-start.16 = (bf16[129,16,128]{2,1,0:T(8,128)(2,1)}, bf16[129,16,128]{2,1,0:T(8,128)(2,1)S(1)}, u32[]{:S(2)}, u32[]{:S(2)}) collective-permute-start(bf16[129,16,128]{2,1,0:T(8,128)(2,1)} %shard_map.73), channel_id=1, source_target_pairs={{0,12},{1,13},{2,14},{3,15},{4,8},{5,9},{6,10},{7,11},{8,4},{9,5},... | collective-permute-start | bytes 1585160 | tf_op jit(solution)/shard_map/ppermute | solution.py:44
  98.2 2.2 copy-done.1
  100.3 3.5 %shard_map.75 = (f32[33,64,128]{2,1,0:T(8,128)S(1)}, bf16[8,129,16,128]{3,2,1,0:T(8,128)(2,1)S(1)}) custom-call(s32[1]{0:T(128)} %bitcast.12.chip_ref, bf16[129,16,128]{2,1,0:T(8,128)(2,1)} %collective-permute-done.15.refs_1_.piece, bf16[32,64,128]{2,1,0:T(8,128)(2,1)} %shard_map.70.near, ...), custom_call_target="tpu_custom_call", output_to_operand_aliasing={{0}: (6, {}), {1}: (7, {})} | custom-call | flops 2875000064 | tf_op jit(solution)/shard_map/pallas_call | solution.py:265
  103.9 2.0 copy-done.2
  105.9 2.2 copy-done.3
  108.1 3.3 %shard_map.76 = (f32[33,64,128]{2,1,0:T(8,128)S(1)}, bf16[8,129,16,128]{3,2,1,0:T(8,128)(2,1)S(1)}) custom-call(s32[1]{0:T(128)} %bitcast.11.chip_ref, bf16[129,16,128]{2,1,0:T(8,128)(2,1)S(1)} %copy-done.18, bf16[32,64,128]{2,1,0:T(8,128)(2,1)} %collective-permute-done.21.near, ...), custom_call_target="tpu_custom_call", output_to_operand_aliasing={{0}: (6, {}), {1}: (7, {})} | custom-call | flops 2875000064 | tf_op jit(solution)/shard_map/pallas_call | solution.py:265
  112.1 3.3 %shard_map.77 = (f32[33,64,128]{2,1,0:T(8,128)S(1)}, bf16[8,129,16,128]{3,2,1,0:T(8,128)(2,1)S(1)}) custom-call(s32[1]{0:T(128)} %bitcast.10.chip_ref, bf16[129,16,128]{2,1,0:T(8,128)(2,1)S(1)} %copy-done.23, bf16[32,64,128]{2,1,0:T(8,128)(2,1)} %collective-permute-done.19.near, ...), custom_call_target="tpu_custom_call", output_to_operand_aliasing={{0}: (6, {}), {1}: (7, {})} | custom-call | flops 2875000064 | tf_op jit(solution)/shard_map/pallas_call | solution.py:265
  115.4 2.0 copy-done.4
  117.8 2.2 copy-done.5
  120.0 3.5 %shard_map.78 = (f32[33,64,128]{2,1,0:T(8,128)S(1)}, bf16[8,129,16,128]{3,2,1,0:T(8,128)(2,1)S(1)}) custom-call(s32[1]{0:T(128)} %bitcast.9.chip_ref, bf16[129,16,128]{2,1,0:T(8,128)(2,1)} %collective-permute-done.7.refs_1_.piece, bf16[32,64,128]{2,1,0:T(8,128)(2,1)} %shard_map.72.near, ...), custom_call_target="tpu_custom_call", output_to_operand_aliasing={{0}: (6, {}), {1}: (7, {})} | custom-call | flops 2875000064 | tf_op jit(solution)/shard_map/pallas_call | solution.py:265
  123.5 2.0 copy-done.6
  125.5 2.0 collective-permute-start.3
  127.6 21.2 %collective-permute-done.8.near = bf16[32,64,128]{2,1,0:T(8,128)(2,1)S(1)} collective-permute-done((bf16[32,64,128]{2,1,0:T(8,128)(2,1)}, bf16[32,64,128]{2,1,0:T(8,128)(2,1)S(1)}, u32[]{:S(2)}, u32[]{:S(2)}) %collective-permute-start.8) | collective-permute-done | bytes 524320 | tf_op jit(solution)/shard_map/ppermute | solution.py:44
  148.7 2.2 copy-done.7
  150.9 3.1 %shard_map.79 = (f32[33,64,128]{2,1,0:T(8,128)S(1)}, bf16[8,129,16,128]{3,2,1,0:T(8,128)(2,1)S(1)}) custom-call(s32[1]{0:T(128)} %bitcast.8.chip_ref, bf16[129,16,128]{2,1,0:T(8,128)(2,1)S(1)} %collective-permute-done.16.piece, bf16[32,64,128]{2,1,0:T(8,128)(2,1)} %shard_map.71.near, ...), custom_call_target="tpu_custom_call", output_to_operand_aliasing={{0}: (6, {}), {1}: (7, {})} | custom-call | flops 2875000064 | tf_op jit(solution)/shard_map/pallas_call | solution.py:265
  154.1 2.0 copy-done.8
  156.1 2.2 copy-done.9
  158.3 3.1 %shard_map.80 = (f32[33,64,128]{2,1,0:T(8,128)S(1)}, bf16[8,129,16,128]{3,2,1,0:T(8,128)(2,1)S(1)}) custom-call(s32[1]{0:T(128)} %bitcast.7.chip_ref, bf16[129,16,128]{2,1,0:T(8,128)(2,1)S(1)} %collective-permute-done.11.piece, bf16[32,64,128]{2,1,0:T(8,128)(2,1)} %collective-permute-done.13.near, ...), custom_call_target="tpu_custom_call", output_to_operand_aliasing={{0}: (6, {}), {1}: (7, {})} | custom-call | flops 2875000064 | tf_op jit(solution)/shard_map/pallas_call | solution.py:265
  161.5 3.0 %shard_map.81 = (f32[33,64,128]{2,1,0:T(8,128)S(1)}, bf16[8,129,16,128]{3,2,1,0:T(8,128)(2,1)S(1)}) custom-call(s32[1]{0:T(128)} %bitcast.1.chip_ref, bf16[129,16,128]{2,1,0:T(8,128)(2,1)S(1)} %collective-permute-done.3.piece, bf16[32,64,128]{2,1,0:T(8,128)(2,1)S(1)} %collective-permute-done.8.near, ...), custom_call_target="tpu_custom_call", output_to_operand_aliasing={{0}: (6, {}), {1}: (7, {})} | custom-call | flops 2875000064 | tf_op jit(solution)/shard_map/pallas_call | solution.py:265
  164.5 2.0 copy-done.10
  169.8 2.3 collective-permute-done.25
  173.9 2.7 %collective-permute-start.29 = (f32[16,128]{1,0:T(8,128)S(1)}, f32[16,128]{1,0:T(8,128)S(1)}, u32[]{:S(2)}, u32[]{:S(2)}) collective-permute-start(f32[16,128]{1,0:T(8,128)S(1)} %add_add_fusion.1), channel_id=1, source_target_pairs={{0,12},{1,13},{2,14},{3,15},{4,8},{5,9},{6,10},{7,11},{8,4},{9,5},... | collective-permute-start | bytes 24584 | tf_op jit(solution)/shard_map/ppermute | solution.py:117
  176.7 2.6 %collective-permute-done.29 = f32[16,128]{1,0:T(8,128)S(1)} collective-permute-done((f32[16,128]{1,0:T(8,128)S(1)}, f32[16,128]{1,0:T(8,128)S(1)}, u32[]{:S(2)}, u32[]{:S(2)}) %collective-permute-start.29) | collective-permute-done | bytes 8224 | tf_op jit(solution)/shard_map/ppermute | solution.py:117
  182.9 2.2 copy-done.11
  185.1 2.8 %shard_map.84 = (f32[33,64,128]{2,1,0:T(8,128)S(1)}, f32[8,128]{1,0:T(8,128)S(1)}) custom-call(s32[1]{0:T(128)} %bitcast.13.chips_ref, bf16[8,129,16,128]{3,2,1,0:T(8,128)(2,1)S(1)} %copy-done.11, bf16[2,32,128,128]{3,2,1,0:T(8,128)(2,1)S(1)} %copy-done.16, bf16[2,32,128,128]{3,2,1,0:T(8,128)(2,1)} %collective-permute-done.10.other.refs_1_, ...), custom_call_target="tpu_custom_call" | custom-call | flops 3335000064 | tf_op jit(solution)/shard_map/pallas_call | solution.py:382
  189.5 5.7 %collective-permute-done.30.refs_0_ = bf16[32,64,128]{2,1,0:T(8,128)(2,1)S(1)} collective-permute-done((bf16[32,64,128]{2,1,0:T(8,128)(2,1)}, bf16[32,64,128]{2,1,0:T(8,128)(2,1)S(1)}, u32[]{:S(2)}, u32[]{:S(2)}) %collective-permute-start.30) | collective-permute-done | bytes 524320 | tf_op jit(solution)/shard_map/ppermute | solution.py:44
  199.0 2.2 copy-done.12
  203.4 4.1 %shard_map.86 = (f32[33,64,128]{2,1,0:T(8,128)S(1)}, f32[8,128]{1,0:T(8,128)S(1)}) custom-call(s32[2]{0:T(128)S(1)} %pad_add_fusion.2.chips_ref, bf16[8,129,16,128]{3,2,1,0:T(8,128)(2,1)S(1)} %copy-done.12, bf16[2,32,128,128]{3,2,1,0:T(8,128)(2,1)S(1)} %copy-done.16, ...), custom_call_target="tpu_custom_call", output_to_operand_aliasing={{0}: (8, {})} | custom-call | flops 4944999936 | tf_op jit(solution)/shard_map/pallas_call | solution.py:382
  213.5 2.2 copy-done.13
  216.9 4.2 %shard_map.88 = (f32[33,64,128]{2,1,0:T(8,128)S(1)}, f32[8,128]{1,0:T(8,128)S(1)}) custom-call(s32[2]{0:T(128)S(1)} %pad_add_fusion.3.chips_ref, bf16[8,129,16,128]{3,2,1,0:T(8,128)(2,1)S(1)} %copy-done.13, bf16[2,32,128,128]{3,2,1,0:T(8,128)(2,1)S(1)} %copy-done.16, ...), custom_call_target="tpu_custom_call", output_to_operand_aliasing={{0}: (8, {})} | custom-call | flops 4944999936 | tf_op jit(solution)/shard_map/pallas_call | solution.py:382
  222.8 3.0 %collective-permute-done.36.refs_0_ = bf16[32,64,128]{2,1,0:T(8,128)(2,1)} collective-permute-done((bf16[32,64,128]{2,1,0:T(8,128)(2,1)}, bf16[32,64,128]{2,1,0:T(8,128)(2,1)}, u32[]{:S(2)}, u32[]{:S(2)}) %collective-permute-start.36) | collective-permute-done | bytes 524320 | tf_op jit(solution)/shard_map/ppermute | solution.py:44
  227.7 2.1 shard_map.90
  231.3 2.2 copy-done.14
  235.8 4.1 %shard_map.91 = (f32[33,64,128]{2,1,0:T(8,128)S(1)}, f32[8,128]{1,0:T(8,128)S(1)}) custom-call(s32[2]{0:T(128)S(1)} %pad_add_fusion.4.chips_ref, bf16[8,129,16,128]{3,2,1,0:T(8,128)(2,1)S(1)} %copy-done.14, bf16[2,32,128,128]{3,2,1,0:T(8,128)(2,1)S(1)} %copy-done.16, ...), custom_call_target="tpu_custom_call", output_to_operand_aliasing={{0}: (8, {})} | custom-call | flops 4944999936 | tf_op jit(solution)/shard_map/pallas_call | solution.py:382
  241.5 2.1 collective-permute-done.44.refs_3_
  243.6 2.2 copy-done.15
  247.0 3.5 %shard_map.93 = bf16[32,64,128]{2,1,0:T(8,128)(2,1)} custom-call(s32[1]{0:T(128)} %bitcast.chips_ref, bf16[8,129,16,128]{3,2,1,0:T(8,128)(2,1)S(1)} %copy-done.15, bf16[2,32,128,128]{3,2,1,0:T(8,128)(2,1)S(1)} %copy-done.16, bf16[2,32,128,128]{3,2,1,0:T(8,128)(2,1)} %collective-permute-done.10.other.refs_1_, bf16[32,64,128]{2,1,0:T(8,128)(2,1)} %shard_map.92.refs_2_, ...), custom_call_target="tpu_custom_call" | custom-call | flops 3335000064 | tf_op jit(solution)/shard_map/pallas_call | solution.py:382
  (181 shorter events, 56.9 us)
Async XLA Ops:
  3.1 6.8 %collective-permute-start.1 = (bf16[2,32,64,128]{3,2,1,0:T(8,128)(2,1)}, bf16[2,32,64,128]{3,2,1,0:T(8,128)(2,1)}, u32[]{:S(2)}, u32[]{:S(2)}) collective-permute-start(bf16[2,32,64,128]{3,2,1,0:T(8,128)(2,1)} %constant_dynamic-slice_fusion.2), channel_id=1, source_target_pairs={{0,1},{1,0},{2,3},{3,2},{4,5},{5,4},{6,7},{7,6},{8,9},{9,8},{10,11... | collective-permute-start | bytes 3145736 | tf_op jit(solution)/shard_map/ppermute | solution.py:44
  3.5 80.9 %collective-permute-start.10 = (bf16[2,32,128,128]{3,2,1,0:T(8,128)(2,1)S(1)}, bf16[2,32,128,128]{3,2,1,0:T(8,128)(2,1)}, u32[]{:S(2)}, u32[]{:S(2)}) collective-permute-start(bf16[2,32,128,128]{3,2,1,0:T(8,128)(2,1)S(1)} %copy-done.16), channel_id=1, source_target_pairs={{0,1},{1,0},{2,3},{3,2},{4,5},{5,4},{6,7},{7,6},{8,9},{9,8},{10,11... | collective-permute-start | bytes 6291464 | tf_op jit(solution)/shard_map/ppermute | solution.py:44
  3.6 6.3 %collective-permute-start = (s32[2,2,32]{2,1,0:T(2,128)S(1)}, s32[2,2,32]{2,1,0:T(2,128)S(1)}, u32[]{:S(2)}, u32[]{:S(2)}) collective-permute-start(s32[2,2,32]{2,1,0:T(2,128)S(1)} %pad_add_fusion.plan_ref.refs_2_), channel_id=1, source_target_pairs={{0,1},{1,0},{2,3},{3,2},{4,5},{5,4},{6,7},{7,6},{8,9},{9,8},{10,11... | collective-permute-start | bytes 1544 | tf_op jit(solution)/shard_map/ppermute | solution.py:44
  6.2 15.9 %copy-start.19 = (bf16[32,64,128]{2,1,0:T(8,128)(2,1)}, bf16[32,64,128]{2,1,0:T(8,128)(2,1)S(1)}, u32[]{:S(2)}) copy-start(bf16[32,64,128]{2,1,0:T(8,128)(2,1)S(1)} %get-tuple-element.71.near.wave_ref) | copy-start | bytes 1572868
  6.2 27.6 %collective-permute-start.4 = (bf16[32,64,128]{2,1,0:T(8,128)(2,1)S(1)}, bf16[32,64,128]{2,1,0:T(8,128)(2,1)}, u32[]{:S(2)}, u32[]{:S(2)}) collective-permute-start(bf16[32,64,128]{2,1,0:T(8,128)(2,1)S(1)} %get-tuple-element.71.near.wave_ref), channel_id=1, source_target_pairs={{0,8},{1,9},{2,10},{3,11},{4,12},{5,13},{6,14},{7,15},{8,0},{9,1},... | collective-permute-start | bytes 1572872 | tf_op jit(solution)/shard_map/ppermute | solution.py:44
  20.1 14.9 %collective-permute-start.5 = (bf16[129,16,128]{2,1,0:T(8,128)(2,1)S(1)}, bf16[129,16,128]{2,1,0:T(8,128)(2,1)S(1)}, u32[]{:S(2)}, u32[]{:S(2)}) collective-permute-start(bf16[129,16,128]{2,1,0:T(8,128)(2,1)S(1)} %get-tuple-element.38), channel_id=1, source_target_pairs={{0,2},{1,3},{2,0},{3,1},{4,6},{5,7},{6,4},{7,5},{8,10},{9,11},{10,... | collective-permute-start | bytes 1585160 | tf_op jit(solution)/shard_map/ppermute | solution.py:44
  21.6 23.9 %collective-permute-start.19 = (bf16[32,64,128]{2,1,0:T(8,128)(2,1)S(1)}, bf16[32,64,128]{2,1,0:T(8,128)(2,1)}, u32[]{:S(2)}, u32[]{:S(2)}) collective-permute-start(bf16[32,64,128]{2,1,0:T(8,128)(2,1)S(1)} %get-tuple-element.71.near.wave_ref), channel_id=1, source_target_pairs={{0,2},{1,3},{2,0},{3,1},{4,6},{5,7},{6,4},{7,5},{8,10},{9,11},{10,... | collective-permute-start | bytes 1572872 | tf_op jit(solution)/shard_map/ppermute | solution.py:44
  22.1 25.0 %collective-permute-start.12 = (bf16[32,64,128]{2,1,0:T(8,128)(2,1)S(1)}, bf16[32,64,128]{2,1,0:T(8,128)(2,1)}, u32[]{:S(2)}, u32[]{:S(2)}) collective-permute-start(bf16[32,64,128]{2,1,0:T(8,128)(2,1)S(1)} %get-tuple-element.71.near.wave_ref), channel_id=1, source_target_pairs={{0,4},{1,5},{2,6},{3,7},{4,0},{5,1},{6,2},{7,3},{8,12},{9,13},{10,... | collective-permute-start | bytes 1572872 | tf_op jit(solution)/shard_map/ppermute | solution.py:44
  33.8 38.8 %collective-permute-start.15 = (bf16[129,16,128]{2,1,0:T(8,128)(2,1)}, bf16[129,16,128]{2,1,0:T(8,128)(2,1)}, u32[]{:S(2)}, u32[]{:S(2)}) collective-permute-start(bf16[129,16,128]{2,1,0:T(8,128)(2,1)} %get-tuple-element.42), channel_id=1, source_target_pairs={{0,8},{1,9},{2,10},{3,11},{4,12},{5,13},{6,14},{7,15},{8,0},{9,1},... | collective-permute-start | bytes 1585160 | tf_op jit(solution)/shard_map/ppermute | solution.py:44
  35.7 47.9 %collective-permute-start.2 = (bf16[129,16,128]{2,1,0:T(8,128)(2,1)}, bf16[129,16,128]{2,1,0:T(8,128)(2,1)S(1)}, u32[]{:S(2)}, u32[]{:S(2)}) collective-permute-start(bf16[129,16,128]{2,1,0:T(8,128)(2,1)} %get-tuple-element.37), channel_id=1, source_target_pairs={{0,10},{1,11},{2,8},{3,9},{4,14},{5,15},{6,12},{7,13},{8,2},{9,3},... | collective-permute-start | bytes 1585160 | tf_op jit(solution)/shard_map/ppermute | solution.py:44
  45.5 38.9 %collective-permute-start.21 = (bf16[32,64,128]{2,1,0:T(8,128)(2,1)}, bf16[32,64,128]{2,1,0:T(8,128)(2,1)}, u32[]{:S(2)}, u32[]{:S(2)}) collective-permute-start(bf16[32,64,128]{2,1,0:T(8,128)(2,1)} %shard_map.70.near), channel_id=1, source_target_pairs={{0,2},{1,3},{2,0},{3,1},{4,6},{5,7},{6,4},{7,5},{8,10},{9,11},{10,... | collective-permute-start | bytes 1572872 | tf_op jit(solution)/shard_map/ppermute | solution.py:44
  47.0 46.1 %collective-permute-start.7 = (bf16[129,16,128]{2,1,0:T(8,128)(2,1)}, bf16[129,16,128]{2,1,0:T(8,128)(2,1)}, u32[]{:S(2)}, u32[]{:S(2)}) collective-permute-start(bf16[129,16,128]{2,1,0:T(8,128)(2,1)} %copy-done.31), channel_id=1, source_target_pairs={{0,4},{1,5},{2,6},{3,7},{4,0},{5,1},{6,2},{7,3},{8,12},{9,13},{10,... | collective-permute-start | bytes 1585160 | tf_op jit(solution)/shard_map/ppermute | solution.py:44
  72.6 21.5 %collective-permute-start.6 = (bf16[32,64,128]{2,1,0:T(8,128)(2,1)}, bf16[32,64,128]{2,1,0:T(8,128)(2,1)}, u32[]{:S(2)}, u32[]{:S(2)}) collective-permute-start(bf16[32,64,128]{2,1,0:T(8,128)(2,1)} %shard_map.70.near), channel_id=1, source_target_pairs={{0,4},{1,5},{2,6},{3,7},{4,0},{5,1},{6,2},{7,3},{8,12},{9,13},{10,... | collective-permute-start | bytes 1572872 | tf_op jit(solution)/shard_map/ppermute | solution.py:44
  83.6 11.8 %collective-permute-start.23 = (bf16[32,64,128]{2,1,0:T(8,128)(2,1)}, bf16[32,64,128]{2,1,0:T(8,128)(2,1)}, u32[]{:S(2)}, u32[]{:S(2)}) collective-permute-start(bf16[32,64,128]{2,1,0:T(8,128)(2,1)} %shard_map.70.near), channel_id=1, source_target_pairs={{0,1},{1,0},{2,3},{3,2},{4,5},{5,4},{6,7},{7,6},{8,9},{9,8},{10,11... | collective-permute-start | bytes 1572872 | tf_op jit(solution)/shard_map/ppermute | solution.py:44
  84.4 27.0 %collective-permute-start.20 = (bf16[32,64,128]{2,1,0:T(8,128)(2,1)}, bf16[32,64,128]{2,1,0:T(8,128)(2,1)}, u32[]{:S(2)}, u32[]{:S(2)}) collective-permute-start(bf16[32,64,128]{2,1,0:T(8,128)(2,1)} %collective-permute-done.19.near), channel_id=1, source_target_pairs={{0,1},{1,0},{2,3},{3,2},{4,5},{5,4},{6,7},{7,6},{8,9},{9,8},{10,11... | collective-permute-start | bytes 1572872 | tf_op jit(solution)/shard_map/ppermute | solution.py:44
  84.4 21.5 %collective-permute-start.22 = (bf16[32,64,128]{2,1,0:T(8,128)(2,1)}, bf16[32,64,128]{2,1,0:T(8,128)(2,1)}, u32[]{:S(2)}, u32[]{:S(2)}) collective-permute-start(bf16[32,64,128]{2,1,0:T(8,128)(2,1)} %collective-permute-done.21.near), channel_id=1, source_target_pairs={{0,1},{1,0},{2,3},{3,2},{4,5},{5,4},{6,7},{7,6},{8,9},{9,8},{10,11... | collective-permute-start | bytes 1572872 | tf_op jit(solution)/shard_map/ppermute | solution.py:44
  93.1 24.3 %collective-permute-start.18 = (bf16[32,64,128]{2,1,0:T(8,128)(2,1)}, bf16[32,64,128]{2,1,0:T(8,128)(2,1)}, u32[]{:S(2)}, u32[]{:S(2)}) collective-permute-start(bf16[32,64,128]{2,1,0:T(8,128)(2,1)} %shard_map.72.near), channel_id=1, source_target_pairs={{0,1},{1,0},{2,3},{3,2},{4,5},{5,4},{6,7},{7,6},{8,9},{9,8},{10,11... | collective-permute-start | bytes 1572872 | tf_op jit(solution)/shard_map/ppermute | solution.py:44
  94.0 23.4 %collective-permute-start.13 = (bf16[32,64,128]{2,1,0:T(8,128)(2,1)}, bf16[32,64,128]{2,1,0:T(8,128)(2,1)}, u32[]{:S(2)}, u32[]{:S(2)}) collective-permute-start(bf16[32,64,128]{2,1,0:T(8,128)(2,1)} %shard_map.72.near), channel_id=1, source_target_pairs={{0,2},{1,3},{2,0},{3,1},{4,6},{5,7},{6,4},{7,5},{8,10},{9,11},{10,... | collective-permute-start | bytes 1572872 | tf_op jit(solution)/shard_map/ppermute | solution.py:44
  95.4 30.1 %collective-permute-start.16 = (bf16[129,16,128]{2,1,0:T(8,128)(2,1)}, bf16[129,16,128]{2,1,0:T(8,128)(2,1)S(1)}, u32[]{:S(2)}, u32[]{:S(2)}) collective-permute-start(bf16[129,16,128]{2,1,0:T(8,128)(2,1)} %shard_map.73), channel_id=1, source_target_pairs={{0,12},{1,13},{2,14},{3,15},{4,8},{5,9},{6,10},{7,11},{8,4},{9,5},... | collective-permute-start | bytes 1585160 | tf_op jit(solution)/shard_map/ppermute | solution.py:44
  100.3 5.6 %copy-start.18 = (bf16[129,16,128]{2,1,0:T(8,128)(2,1)S(1)}, bf16[129,16,128]{2,1,0:T(8,128)(2,1)}, u32[]{:S(2)}) copy-start(bf16[129,16,128]{2,1,0:T(8,128)(2,1)} %copy-done.17) | copy-start | bytes 1585156
  105.9 42.8 %collective-permute-start.17 = (bf16[32,64,128]{2,1,0:T(8,128)(2,1)}, bf16[32,64,128]{2,1,0:T(8,128)(2,1)S(1)}, u32[]{:S(2)}, u32[]{:S(2)}) collective-permute-start(bf16[32,64,128]{2,1,0:T(8,128)(2,1)} %shard_map.71.near), channel_id=1, source_target_pairs={{0,1},{1,0},{2,3},{3,2},{4,5},{5,4},{6,7},{7,6},{8,9},{9,8},{10,11... | collective-permute-start | bytes 1572872 | tf_op jit(solution)/shard_map/ppermute | solution.py:44
  111.5 37.3 %collective-permute-start.8 = (bf16[32,64,128]{2,1,0:T(8,128)(2,1)}, bf16[32,64,128]{2,1,0:T(8,128)(2,1)S(1)}, u32[]{:S(2)}, u32[]{:S(2)}) collective-permute-start(bf16[32,64,128]{2,1,0:T(8,128)(2,1)} %shard_map.71.near), channel_id=1, source_target_pairs={{0,2},{1,3},{2,0},{3,1},{4,6},{5,7},{6,4},{7,5},{8,10},{9,11},{10,... | collective-permute-start | bytes 1572872 | tf_op jit(solution)/shard_map/ppermute | solution.py:44
  117.5 38.7 %collective-permute-start.11 = (bf16[129,16,128]{2,1,0:T(8,128)(2,1)S(1)}, bf16[129,16,128]{2,1,0:T(8,128)(2,1)S(1)}, u32[]{:S(2)}, u32[]{:S(2)}) collective-permute-start(bf16[129,16,128]{2,1,0:T(8,128)(2,1)S(1)} %copy-done.30), channel_id=1, source_target_pairs={{0,6},{1,7},{2,4},{3,5},{4,2},{5,3},{6,0},{7,1},{8,14},{9,15},{10,... | collective-permute-start | bytes 1585160 | tf_op jit(solution)/shard_map/ppermute | solution.py:44
  117.5 38.6 %collective-permute-start.14 = (bf16[32,64,128]{2,1,0:T(8,128)(2,1)}, bf16[32,64,128]{2,1,0:T(8,128)(2,1)S(1)}, u32[]{:S(2)}, u32[]{:S(2)}) collective-permute-start(bf16[32,64,128]{2,1,0:T(8,128)(2,1)} %collective-permute-done.13.near), channel_id=1, source_target_pairs={{0,1},{1,0},{2,3},{3,2},{4,5},{5,4},{6,7},{7,6},{8,9},{9,8},{10,11... | collective-permute-start | bytes 1572872 | tf_op jit(solution)/shard_map/ppermute | solution.py:44
  120.0 5.6 %copy-start.26 = (bf16[129,16,128]{2,1,0:T(8,128)(2,1)S(1)}, bf16[129,16,128]{2,1,0:T(8,128)(2,1)}, u32[]{:S(2)}) copy-start(bf16[129,16,128]{2,1,0:T(8,128)(2,1)} %shard_map.69) | copy-start | bytes 1585156
  125.5 35.9 %collective-permute-start.3 = (bf16[129,16,128]{2,1,0:T(8,128)(2,1)S(1)}, bf16[129,16,128]{2,1,0:T(8,128)(2,1)S(1)}, u32[]{:S(2)}, u32[]{:S(2)}) collective-permute-start(bf16[129,16,128]{2,1,0:T(8,128)(2,1)S(1)} %copy-done.26), channel_id=1, source_target_pairs={{0,14},{1,15},{2,12},{3,13},{4,10},{5,11},{6,8},{7,9},{8,6},{9,7},... | collective-permute-start | bytes 1585160 | tf_op jit(solution)/shard_map/ppermute | solution.py:44
  148.7 12.8 %collective-permute-start.9 = (bf16[32,64,128]{2,1,0:T(8,128)(2,1)S(1)}, bf16[32,64,128]{2,1,0:T(8,128)(2,1)S(1)}, u32[]{:S(2)}, u32[]{:S(2)}) collective-permute-start(bf16[32,64,128]{2,1,0:T(8,128)(2,1)S(1)} %collective-permute-done.8.near), channel_id=1, source_target_pairs={{0,1},{1,0},{2,3},{3,2},{4,5},{5,4},{6,7},{7,6},{8,9},{9,8},{10,11... | collective-permute-start | bytes 1572872 | tf_op jit(solution)/shard_map/ppermute | solution.py:44
  167.8 2.0 collective-permute-start.24
  168.4 3.7 %collective-permute-start.25 = (f32[16,128]{1,0:T(8,128)S(1)}, f32[16,128]{1,0:T(8,128)S(1)}, u32[]{:S(2)}, u32[]{:S(2)}) collective-permute-start(f32[16,128]{1,0:T(8,128)S(1)} %shard_map.82), channel_id=1, source_target_pairs={{0,2},{1,3},{2,0},{3,1},{4,6},{5,7},{6,4},{7,5},{8,10},{9,11},{10,... | collective-permute-start | bytes 24584 | tf_op jit(solution)/shard_map/ppermute | solution.py:117
  168.9 3.2 %collective-permute-start.26 = (f32[16,128]{1,0:T(8,128)S(1)}, f32[16,128]{1,0:T(8,128)S(1)}, u32[]{:S(2)}, u32[]{:S(2)}) collective-permute-start(f32[16,128]{1,0:T(8,128)S(1)} %shard_map.82), channel_id=1, source_target_pairs={{0,3},{1,2},{2,1},{3,0},{4,7},{5,6},{6,5},{7,4},{8,11},{9,10},{10,... | collective-permute-start | bytes 24584 | tf_op jit(solution)/shard_map/ppermute | solution.py:117
  172.1 4.5 %collective-permute-start.27 = (f32[16,128]{1,0:T(8,128)S(1)}, f32[16,128]{1,0:T(8,128)S(1)}, u32[]{:S(2)}, u32[]{:S(2)}) collective-permute-start(f32[16,128]{1,0:T(8,128)S(1)} %add_add_fusion.1), channel_id=1, source_target_pairs={{0,4},{1,5},{2,6},{3,7},{4,0},{5,1},{6,2},{7,3},{8,12},{9,13},{10,... | collective-permute-start | bytes 24584 | tf_op jit(solution)/shard_map/ppermute | solution.py:117
  172.1 4.6 %collective-permute-start.28 = (f32[16,128]{1,0:T(8,128)S(1)}, f32[16,128]{1,0:T(8,128)S(1)}, u32[]{:S(2)}, u32[]{:S(2)}) collective-permute-start(f32[16,128]{1,0:T(8,128)S(1)} %add_add_fusion.1), channel_id=1, source_target_pairs={{0,8},{1,9},{2,10},{3,11},{4,12},{5,13},{6,14},{7,15},{8,0},{9,1},... | collective-permute-start | bytes 24584 | tf_op jit(solution)/shard_map/ppermute | solution.py:117
  173.9 5.4 %collective-permute-start.29 = (f32[16,128]{1,0:T(8,128)S(1)}, f32[16,128]{1,0:T(8,128)S(1)}, u32[]{:S(2)}, u32[]{:S(2)}) collective-permute-start(f32[16,128]{1,0:T(8,128)S(1)} %add_add_fusion.1), channel_id=1, source_target_pairs={{0,12},{1,13},{2,14},{3,15},{4,8},{5,9},{6,10},{7,11},{8,4},{9,5},... | collective-permute-start | bytes 24584 | tf_op jit(solution)/shard_map/ppermute | solution.py:117
  180.7 2.3 collective-permute-start.31
  180.7 14.5 %collective-permute-start.30 = (bf16[32,64,128]{2,1,0:T(8,128)(2,1)}, bf16[32,64,128]{2,1,0:T(8,128)(2,1)S(1)}, u32[]{:S(2)}, u32[]{:S(2)}) collective-permute-start(bf16[32,64,128]{2,1,0:T(8,128)(2,1)} %get-tuple-element.60.refs_2_), channel_id=1, source_target_pairs={{0,4},{1,5},{2,0},{3,1},{4,8},{5,9},{6,2},{7,3},{8,12},{9,13},{10,... | collective-permute-start | bytes 1572872 | tf_op jit(solution)/shard_map/ppermute | solution.py:44
  180.7 15.3 %collective-permute-start.34 = (bf16[32,64,128]{2,1,0:T(8,128)(2,1)}, bf16[32,64,128]{2,1,0:T(8,128)(2,1)S(1)}, u32[]{:S(2)}, u32[]{:S(2)}) collective-permute-start(bf16[32,64,128]{2,1,0:T(8,128)(2,1)} %get-tuple-element.60.refs_2_), channel_id=1, source_target_pairs={{0,2},{1,3},{2,6},{3,7},{4,0},{5,1},{6,10},{7,11},{8,4},{9,5},{10,... | collective-permute-start | bytes 1572872 | tf_op jit(solution)/shard_map/ppermute | solution.py:44
  196.0 2.9 %collective-permute-start.33 = (bf16[32,64,128]{2,1,0:T(8,128)(2,1)}, bf16[32,64,128]{2,1,0:T(8,128)(2,1)}, u32[]{:S(2)}, u32[]{:S(2)}) collective-permute-start(bf16[32,64,128]{2,1,0:T(8,128)(2,1)} %shard_map.85.refs_2_), channel_id=1, source_target_pairs={{0,1},{1,0},{2,3},{3,2},{4,5},{5,4},{6,7},{7,6},{8,9},{9,8},{10,11... | collective-permute-start | bytes 1572872 | tf_op jit(solution)/shard_map/ppermute | solution.py:44
  196.0 2.9 %collective-permute-start.35 = (bf16[32,64,128]{2,1,0:T(8,128)(2,1)S(1)}, bf16[32,64,128]{2,1,0:T(8,128)(2,1)}, u32[]{:S(2)}, u32[]{:S(2)}) collective-permute-start(bf16[32,64,128]{2,1,0:T(8,128)(2,1)S(1)} %collective-permute-done.34.refs_4_), channel_id=1, source_target_pairs={{0,1},{1,0},{2,3},{3,2},{4,5},{5,4},{6,7},{7,6},{8,9},{9,8},{10,11... | collective-permute-start | bytes 1572872 | tf_op jit(solution)/shard_map/ppermute | solution.py:44
  196.5 14.1 %collective-permute-start.32 = (bf16[32,64,128]{2,1,0:T(8,128)(2,1)}, bf16[32,64,128]{2,1,0:T(8,128)(2,1)}, u32[]{:S(2)}, u32[]{:S(2)}) collective-permute-start(bf16[32,64,128]{2,1,0:T(8,128)(2,1)} %shard_map.85.refs_2_), channel_id=1, source_target_pairs={{0,4},{1,5},{2,0},{3,1},{4,8},{5,9},{6,2},{7,3},{8,12},{9,13},{10,... | collective-permute-start | bytes 1572872 | tf_op jit(solution)/shard_map/ppermute | solution.py:44
  197.0 14.1 %collective-permute-start.38 = (bf16[32,64,128]{2,1,0:T(8,128)(2,1)S(1)}, bf16[32,64,128]{2,1,0:T(8,128)(2,1)S(1)}, u32[]{:S(2)}, u32[]{:S(2)}) collective-permute-start(bf16[32,64,128]{2,1,0:T(8,128)(2,1)S(1)} %collective-permute-done.34.refs_4_), channel_id=1, source_target_pairs={{0,2},{1,3},{2,6},{3,7},{4,0},{5,1},{6,10},{7,11},{8,4},{9,5},{10,... | collective-permute-start | bytes 1572872 | tf_op jit(solution)/shard_map/ppermute | solution.py:44
  210.7 2.6 %collective-permute-start.37 = (bf16[32,64,128]{2,1,0:T(8,128)(2,1)}, bf16[32,64,128]{2,1,0:T(8,128)(2,1)}, u32[]{:S(2)}, u32[]{:S(2)}) collective-permute-start(bf16[32,64,128]{2,1,0:T(8,128)(2,1)} %shard_map.87.refs_2_), channel_id=1, source_target_pairs={{0,1},{1,0},{2,3},{3,2},{4,5},{5,4},{6,7},{7,6},{8,9},{9,8},{10,11... | collective-permute-start | bytes 1572872 | tf_op jit(solution)/shard_map/ppermute | solution.py:44
  211.1 2.4 collective-permute-start.39
  211.2 14.5 %collective-permute-start.36 = (bf16[32,64,128]{2,1,0:T(8,128)(2,1)}, bf16[32,64,128]{2,1,0:T(8,128)(2,1)}, u32[]{:S(2)}, u32[]{:S(2)}) collective-permute-start(bf16[32,64,128]{2,1,0:T(8,128)(2,1)} %shard_map.87.refs_2_), channel_id=1, source_target_pairs={{0,4},{1,5},{2,0},{3,1},{4,8},{5,9},{6,2},{7,3},{8,12},{9,13},{10,... | collective-permute-start | bytes 1572872 | tf_op jit(solution)/shard_map/ppermute | solution.py:44
  212.8 14.1 %collective-permute-start.40 = (bf16[32,64,128]{2,1,0:T(8,128)(2,1)S(1)}, bf16[32,64,128]{2,1,0:T(8,128)(2,1)S(1)}, u32[]{:S(2)}, u32[]{:S(2)}) collective-permute-start(bf16[32,64,128]{2,1,0:T(8,128)(2,1)S(1)} %collective-permute-done.38.refs_4_), channel_id=1, source_target_pairs={{0,2},{1,3},{2,6},{3,7},{4,0},{5,1},{6,10},{7,11},{8,4},{9,5},{10,... | collective-permute-start | bytes 1572872 | tf_op jit(solution)/shard_map/ppermute | solution.py:44
  225.7 5.5 %collective-permute-start.42 = (bf16[32,64,128]{2,1,0:T(8,128)(2,1)}, bf16[32,64,128]{2,1,0:T(8,128)(2,1)}, u32[]{:S(2)}, u32[]{:S(2)}) collective-permute-start(bf16[32,64,128]{2,1,0:T(8,128)(2,1)} %shard_map.89.lower_ref.refs_2_), channel_id=1, source_target_pairs={{0,1},{1,0},{2,3},{3,2},{4,5},{5,4},{6,7},{7,6},{8,9},{9,8},{10,11... | collective-permute-start | bytes 1572872 | tf_op jit(solution)/shard_map/ppermute | solution.py:44
  226.9 4.4 %collective-permute-start.43 = (bf16[32,64,128]{2,1,0:T(8,128)(2,1)S(1)}, bf16[32,64,128]{2,1,0:T(8,128)(2,1)S(1)}, u32[]{:S(2)}, u32[]{:S(2)}) collective-permute-start(bf16[32,64,128]{2,1,0:T(8,128)(2,1)S(1)} %collective-permute-done.40.upper_ref.refs_4_), channel_id=1, source_target_pairs={{0,1},{1,0},{2,3},{3,2},{4,5},{5,4},{6,7},{7,6},{8,9},{9,8},{10,11... | collective-permute-start | bytes 1572872 | tf_op jit(solution)/shard_map/ppermute | solution.py:44
  229.8 11.7 %collective-permute-start.41 = (bf16[32,64,128]{2,1,0:T(8,128)(2,1)}, bf16[32,64,128]{2,1,0:T(8,128)(2,1)}, u32[]{:S(2)}, u32[]{:S(2)}) collective-permute-start(bf16[32,64,128]{2,1,0:T(8,128)(2,1)} %shard_map.90), channel_id=1, source_target_pairs={{0,4},{1,3},{2,0},{3,7},{4,8},{5,1},{6,2},{7,11},{8,12},{9,5},{10,... | collective-permute-start | bytes 1572872 | tf_op jit(solution)/shard_map/ppermute | solution.py:44
  241.5 2.1 collective-permute-start.44
  (49 other events, 83.0 us)

commit v8 on v7

--- a/solution.py
+++ b/solution.py
@@ -8,7 +8,7 @@
 from jax.sharding import PartitionSpec as P
 
 BOTH = ("sec", "term")
-VMEM_LIMIT = 20 * 2**20
+VMEM_LIMIT = 60 * 2**20
 PART = 16
 ORDER = [0, 4, 5, 1, 2, 6, 3, 7]
 WAITS = {4: 1, 2: 5, 6: 2}

time: 252 us -> 252 us (level)
  local copies, waits for them, and re-layouts: 64.2 us -> 17.3 us
  Pallas kernels: 53.8 us -> 88.1 us
  waiting for transfers between devices: 94.7 us -> 103 us
  other arithmetic: 0.31 us -> 3.87 us
    unnamed x104 -> x66, local copies, waits for them, and re-layouts: 59.7 us -> 12.8 us
    pallas_call x8, Pallas kernels: 26 us -> 43.2 us  [first_group(): pl.pallas_call(functools.partial(first_kernel, first, streams, capacity),...]
    pallas_call x5, Pallas kernels: 18.6 us -> 31.7 us  [second_group(): pl.pallas_call(functools.partial(second_kernel, sources, first, last, str...]
    ppermute x39, waiting for transfers between devices: 89.7 us -> 96 us  [permute(): return lax.ppermute(value, BOTH, pairs)]
  transfers between devices with their start and end apart: 45 -> 45, of which waited for: 19 -> 16; matrix products, arithmetic and copies ran while one was open for 1% -> 2% of each run, Pallas kernels for 18% -> 29%
where the time goes in v8:
time: 252 us
  waiting for transfers between devices  103 us (41%)
  Pallas kernels  88.1 us (35%)
  starting transfers between devices  38.3 us (15%)
  local copies, waits for them, and re-layouts  17.3 us (7%)
  other arithmetic  3.87 us (2%)
    ppermute x39, waiting for transfers between devices, permute(): return lax.ppermute(value, BOTH, pairs)  96 us
    pallas_call x8, Pallas kernels, first_group(): pl.pallas_call(functools.partial(first_kernel, first, streams, capacity),...  43.2 us
    ppermute x39, starting transfers between devices, permute(): return lax.ppermute(value, BOTH, pairs)  32.1 us
    pallas_call x5, Pallas kernels, second_group(): pl.pallas_call(functools.partial(second_kernel, sources, first, last, str...  31.7 us
    unnamed x66, local copies, waits for them, and re-layouts  12.8 us
    ppermute x6, waiting for transfers between devices, spread(): lax.ppermute(value, BOTH, [(d, d ^ m) for d in range(devices)])  6.74 us
    ppermute x6, starting transfers between devices, spread(): lax.ppermute(value, BOTH, [(d, d ^ m) for d in range(devices)])  6.25 us
    pallas_call x1, Pallas kernels, pack(): pl.pallas_call(functools.partial(pack_kernel, order, capacity, blocks, te...  5.54 us
  transfers between devices with their start and end apart: 45, of which 16 were waited for; matrix products, arithmetic and copies ran while one was open for 2% of the time, Pallas kernels for 29%

profile of v8, /device:TPU:0, one launch (start us, length us, event | category | flops | bytes accessed | tf_op | source)
XLA Modules:
  0.0 251.5 jit_solution(18426974272345193201)
XLA Ops:
  0.7 2.4 constant_dynamic-slice_fusion.2
  4.2 2.1 constant_dynamic-slice_fusion
  6.2 3.6 %collective-permute-start.4 = (bf16[32,64,128]{2,1,0:T(8,128)(2,1)S(1)}, bf16[32,64,128]{2,1,0:T(8,128)(2,1)}, u32[]{:S(2)}, u32[]{:S(2)}) collective-permute-start(bf16[32,64,128]{2,1,0:T(8,128)(2,1)S(1)} %get-tuple-element.71.near.wave_ref), channel_id=1, source_target_pairs={{0,8},{1,9},{2,10},{3,11},{4,12},{5,13},{6,14},{7,15},{8,0},{9,1},... | collective-permute-start | bytes 1572872 | tf_op jit(solution)/shard_map/ppermute | solution.py:44
  11.1 5.5 %shard_map.68 = (bf16[129,16,128]{2,1,0:T(8,128)(2,1)}, bf16[129,16,128]{2,1,0:T(8,128)(2,1)}, bf16[129,16,128]{2,1,0:T(8,128)(2,1)}, bf16[129,16,128]{2,1,0:T(8...) custom-call(s32[3]{0:T(128)} %pad_add_fusion.1.ids_ref, ...), custom_call_target="tpu_custom_call" | custom-call | flops 5750000128 | tf_op jit(solution)/shard_map/pallas_call | solution.py:187
  16.6 1.6 collective-permute-start.5
  18.7 1.6 collective-permute-start.12
  20.3 13.6 %collective-permute-done.4.refs_0_ = bf16[32,64,128]{2,1,0:T(8,128)(2,1)} collective-permute-done((bf16[32,64,128]{2,1,0:T(8,128)(2,1)S(1)}, bf16[32,64,128]{2,1,0:T(8,128)(2,1)}, u32[]{:S(2)}, u32[]{:S(2)}) %collective-permute-start.4) | collective-permute-done | bytes 524320 | tf_op jit(solution)/shard_map/ppermute | solution.py:44
  34.7 3.9 %collective-permute-start.2 = (bf16[129,16,128]{2,1,0:T(8,128)(2,1)}, bf16[129,16,128]{2,1,0:T(8,128)(2,1)S(1)}, u32[]{:S(2)}, u32[]{:S(2)}) collective-permute-start(bf16[129,16,128]{2,1,0:T(8,128)(2,1)} %get-tuple-element.37), channel_id=1, source_target_pairs={{0,10},{1,11},{2,8},{3,9},{4,14},{5,15},{6,12},{7,13},{8,2},{9,3},... | collective-permute-start | bytes 1585160 | tf_op jit(solution)/shard_map/ppermute | solution.py:44
  38.6 3.7 %collective-permute-done.19.near = bf16[32,64,128]{2,1,0:T(8,128)(2,1)} collective-permute-done((bf16[32,64,128]{2,1,0:T(8,128)(2,1)S(1)}, bf16[32,64,128]{2,1,0:T(8,128)(2,1)}, u32[]{:S(2)}, u32[]{:S(2)}) %collective-permute-start.19) | collective-permute-done | bytes 524320 | tf_op jit(solution)/shard_map/ppermute | solution.py:44
  42.3 1.5 collective-permute-start.21
  43.9 1.6 collective-permute-start.7
  45.4 27.2 %collective-permute-done.15.refs_1_.piece = bf16[129,16,128]{2,1,0:T(8,128)(2,1)} collective-permute-done((bf16[129,16,128]{2,1,0:T(8,128)(2,1)}, bf16[129,16,128]{2,1,0:T(8,128)(2,1)}, u32[]{:S(2)}, u32[]{:S(2)}) %collective-permute-start.15) | collective-permute-done | bytes 528416 | tf_op jit(solution)/shard_map/ppermute | solution.py:44
  72.6 11.0 %collective-permute-done.2.refs_1_.piece = bf16[129,16,128]{2,1,0:T(8,128)(2,1)S(1)} collective-permute-done((bf16[129,16,128]{2,1,0:T(8,128)(2,1)}, bf16[129,16,128]{2,1,0:T(8,128)(2,1)S(1)}, u32[]{:S(2)}, u32[]{:S(2)}) %collective-permute-start.2) | collective-permute-done | bytes 528416 | tf_op jit(solution)/shard_map/ppermute | solution.py:44
  84.9 5.2 %shard_map.74 = (f32[33,64,128]{2,1,0:T(8,128)}, bf16[8,129,16,128]{3,2,1,0:T(8,128)(2,1)}) custom-call(s32[1]{0:T(128)} %bitcast.2.chip_ref, bf16[129,16,128]{2,1,0:T(8,128)(2,1)} %get-tuple-element.43.piece, bf16[32,64,128]{2,1,0:T(8,128)(2,1)} %copy-done.2, bf16[32,64,128]{2,1,0:T(8,128)(2,1)} %get-tuple-element.70.far, ...), custom_call_target="tpu_custom_call" | custom-call | flops 2875000064 | tf_op jit(solution)/shard_map/pallas_call | solution.py:265
  90.4 3.7 %collective-permute-done.6.refs_0_ = bf16[32,64,128]{2,1,0:T(8,128)(2,1)} collective-permute-done((bf16[32,64,128]{2,1,0:T(8,128)(2,1)}, bf16[32,64,128]{2,1,0:T(8,128)(2,1)}, u32[]{:S(2)}, u32[]{:S(2)}) %collective-permute-start.6) | collective-permute-done | bytes 524320 | tf_op jit(solution)/shard_map/ppermute | solution.py:44
  94.1 1.4 collective-permute-start.13
  95.5 1.2 collective-permute-start.16
  96.7 5.4 %shard_map.75 = (f32[33,64,128]{2,1,0:T(8,128)}, bf16[8,129,16,128]{3,2,1,0:T(8,128)(2,1)}) custom-call(s32[1]{0:T(128)} %bitcast.12.chip_ref, bf16[129,16,128]{2,1,0:T(8,128)(2,1)} %collective-permute-done.15.refs_1_.piece, bf16[32,64,128]{2,1,0:T(8,128)(2,1)} %shard_map.70.near, ...), custom_call_target="tpu_custom_call", output_to_operand_aliasing={{0}: (6, {}), {1}: (7, {})} | custom-call | flops 2875000064 | tf_op jit(solution)/shard_map/pallas_call | solution.py:265
  102.1 5.4 %shard_map.76 = (f32[33,64,128]{2,1,0:T(8,128)}, bf16[8,129,16,128]{3,2,1,0:T(8,128)(2,1)}) custom-call(s32[1]{0:T(128)} %bitcast.11.chip_ref, bf16[129,16,128]{2,1,0:T(8,128)(2,1)} %copy-done.1, bf16[32,64,128]{2,1,0:T(8,128)(2,1)} %collective-permute-done.21.near, ...), custom_call_target="tpu_custom_call", output_to_operand_aliasing={{0}: (6, {}), {1}: (7, {})} | custom-call | flops 2875000064 | tf_op jit(solution)/shard_map/pallas_call | solution.py:265
  108.4 5.4 %shard_map.77 = (f32[33,64,128]{2,1,0:T(8,128)}, bf16[8,129,16,128]{3,2,1,0:T(8,128)(2,1)}) custom-call(s32[1]{0:T(128)} %bitcast.10.chip_ref, bf16[129,16,128]{2,1,0:T(8,128)(2,1)} %copy-done.3, bf16[32,64,128]{2,1,0:T(8,128)(2,1)} %collective-permute-done.19.near, bf16[32,64,128]{2,1,0:T(8,128)(2,1)} %copy-done.13, ...), custom_call_target="tpu_custom_call", output_to_operand_aliasing={{0}: (6, {}), {1}: (7, {})} | custom-call | flops 2875000064 | tf_op jit(solution)/shard_map/pallas_call | solution.py:265
  115.1 5.4 %shard_map.78 = (f32[33,64,128]{2,1,0:T(8,128)}, bf16[8,129,16,128]{3,2,1,0:T(8,128)(2,1)}) custom-call(s32[1]{0:T(128)} %bitcast.9.chip_ref, bf16[129,16,128]{2,1,0:T(8,128)(2,1)} %copy-done.4, bf16[32,64,128]{2,1,0:T(8,128)(2,1)} %shard_map.72.near, bf16[32,64,128]{2,1,0:T(8,128)(2,1)} %copy-done.12, ...), custom_call_target="tpu_custom_call", output_to_operand_aliasing={{0}: (6, {}), {1}: (7, {})} | custom-call | flops 2875000064 | tf_op jit(solution)/shard_map/pallas_call | solution.py:265
  120.6 3.2 %collective-permute-start.3 = (bf16[129,16,128]{2,1,0:T(8,128)(2,1)S(1)}, bf16[129,16,128]{2,1,0:T(8,128)(2,1)S(1)}, u32[]{:S(2)}, u32[]{:S(2)}) collective-permute-start(bf16[129,16,128]{2,1,0:T(8,128)(2,1)S(1)} %copy-done.9), channel_id=1, source_target_pairs={{0,14},{1,15},{2,12},{3,13},{4,10},{5,11},{6,8},{7,9},{8,6},{9,7},... | collective-permute-start | bytes 1585160 | tf_op jit(solution)/shard_map/ppermute | solution.py:44
  123.8 21.0 %collective-permute-done.8.near = bf16[32,64,128]{2,1,0:T(8,128)(2,1)S(1)} collective-permute-done((bf16[32,64,128]{2,1,0:T(8,128)(2,1)}, bf16[32,64,128]{2,1,0:T(8,128)(2,1)S(1)}, u32[]{:S(2)}, u32[]{:S(2)}) %collective-permute-start.8) | collective-permute-done | bytes 524320 | tf_op jit(solution)/shard_map/ppermute | solution.py:44
  144.8 5.6 %shard_map.79 = (f32[33,64,128]{2,1,0:T(8,128)}, bf16[8,129,16,128]{3,2,1,0:T(8,128)(2,1)}) custom-call(s32[1]{0:T(128)} %bitcast.8.chip_ref, bf16[129,16,128]{2,1,0:T(8,128)(2,1)} %copy-done.5, bf16[32,64,128]{2,1,0:T(8,128)(2,1)} %shard_map.71.near, ...), custom_call_target="tpu_custom_call", output_to_operand_aliasing={{0}: (6, {}), {1}: (7, {})} | custom-call | flops 2875000064 | tf_op jit(solution)/shard_map/pallas_call | solution.py:265
  151.3 5.4 %shard_map.80 = (f32[33,64,128]{2,1,0:T(8,128)}, bf16[8,129,16,128]{3,2,1,0:T(8,128)(2,1)}) custom-call(s32[1]{0:T(128)} %bitcast.7.chip_ref, bf16[129,16,128]{2,1,0:T(8,128)(2,1)} %copy-done.6, bf16[32,64,128]{2,1,0:T(8,128)(2,1)} %copy-done.10, bf16[32,64,128]{2,1,0:T(8,128)(2,1)} %collective-permute-done.14.far, ...), custom_call_target="tpu_custom_call", output_to_operand_aliasing={{0}: (6, {}), {1}: (7, {})} | custom-call | flops 2875000064 | tf_op jit(solution)/shard_map/pallas_call | solution.py:265
  157.6 5.4 %shard_map.81 = (f32[33,64,128]{2,1,0:T(8,128)}, bf16[8,129,16,128]{3,2,1,0:T(8,128)(2,1)}) custom-call(s32[1]{0:T(128)} %bitcast.1.chip_ref, bf16[129,16,128]{2,1,0:T(8,128)(2,1)} %copy-done.7, bf16[32,64,128]{2,1,0:T(8,128)(2,1)} %copy-done.11, bf16[32,64,128]{2,1,0:T(8,128)(2,1)} %collective-permute-done.9.far, ...), custom_call_target="tpu_custom_call", output_to_operand_aliasing={{0}: (6, {}), {1}: (7, {})} | custom-call | flops 2875000064 | tf_op jit(solution)/shard_map/pallas_call | solution.py:265
  162.9 2.6 %shard_map.82 = f32[16,128]{1,0:T(8,128)} custom-call(s32[3]{0:T(128)} %pad_add_fusion.1.ids_ref, f32[33,64,128]{2,1,0:T(8,128)} %get-tuple-element.59.total_ref, bf16[32,64,128]{2,1,0:T(8,128)(2,1)} %copy-done.2), custom_call_target="tpu_custom_call" | custom-call | tf_op jit(solution)/shard_map/pallas_call | solution.py:439
  166.5 0.9 collective-permute-start.26
  167.4 2.3 collective-permute-done.25
  170.6 3.3 %collective-permute-start.28 = (f32[16,128]{1,0:T(8,128)S(1)}, f32[16,128]{1,0:T(8,128)S(1)}, u32[]{:S(2)}, u32[]{:S(2)}) collective-permute-start(f32[16,128]{1,0:T(8,128)S(1)} %add_add_fusion.1), channel_id=1, source_target_pairs={{0,8},{1,9},{2,10},{3,11},{4,12},{5,13},{6,14},{7,15},{8,0},{9,1},... | collective-permute-start | bytes 24584 | tf_op jit(solution)/shard_map/ppermute | solution.py:117
  173.8 1.1 collective-permute-start.29
  175.5 3.7 %collective-permute-done.29 = f32[16,128]{1,0:T(8,128)S(1)} collective-permute-done((f32[16,128]{1,0:T(8,128)S(1)}, f32[16,128]{1,0:T(8,128)S(1)}, u32[]{:S(2)}, u32[]{:S(2)}) %collective-permute-start.29) | collective-permute-done | bytes 8224 | tf_op jit(solution)/shard_map/ppermute | solution.py:117
  179.9 2.8 %shard_map.83 = (bf16[32,64,128]{2,1,0:T(8,128)(2,1)}, f32[1,1]{1,0:T(1,128)}) custom-call(f32[33,64,128]{2,1,0:T(8,128)} %get-tuple-element.59.total_ref, bf16[32,64,128]{2,1,0:T(8,128)(2,1)} %copy-done.2, f32[16,128]{1,0:T(8,128)} %add_add_fusion.stats_ref), custom_call_target="tpu_custom_call" | custom-call | tf_op jit(solution)/shard_map/pallas_call | solution.py:447
  182.7 2.0 collective-permute-start.34
  184.8 0.9 copy-done.27
  185.6 4.6 %shard_map.84 = (f32[33,64,128]{2,1,0:T(8,128)}, f32[8,128]{1,0:T(8,128)}) custom-call(s32[1]{0:T(128)} %bitcast.13.chips_ref, bf16[8,129,16,128]{3,2,1,0:T(8,128)(2,1)} %get-tuple-element.58.kept, bf16[2,32,128,128]{3,2,1,0:T(8,128)(2,1)} %refs_0_.11, bf16[2,32,128,128]{3,2,1,0:T(8,128)(2,1)} %collective-permute-done.10.other.refs_1_, ...), custom_call_target="tpu_custom_call" | custom-call | flops 3335000064 | tf_op jit(solution)/shard_map/pallas_call | solution.py:382
  190.2 7.0 %collective-permute-done.30.refs_0_ = bf16[32,64,128]{2,1,0:T(8,128)(2,1)S(1)} collective-permute-done((bf16[32,64,128]{2,1,0:T(8,128)(2,1)}, bf16[32,64,128]{2,1,0:T(8,128)(2,1)S(1)}, u32[]{:S(2)}, u32[]{:S(2)}) %collective-permute-start.30) | collective-permute-done | bytes 524320 | tf_op jit(solution)/shard_map/ppermute | solution.py:44
  198.8 1.7 collective-permute-start.38
  202.2 7.2 %shard_map.86 = (f32[33,64,128]{2,1,0:T(8,128)}, f32[8,128]{1,0:T(8,128)}) custom-call(s32[2]{0:T(128)} %pad_add_fusion.2.chips_ref, bf16[8,129,16,128]{3,2,1,0:T(8,128)(2,1)} %get-tuple-element.58.kept, bf16[2,32,128,128]{3,2,1,0:T(8,128)(2,1)} %refs_0_.11, ...), custom_call_target="tpu_custom_call", output_to_operand_aliasing={{0}: (8, {})} | custom-call | flops 4944999936 | tf_op jit(solution)/shard_map/pallas_call | solution.py:382
  209.4 3.3 %collective-permute-done.32.refs_0_ = bf16[32,64,128]{2,1,0:T(8,128)(2,1)S(1)} collective-permute-done((bf16[32,64,128]{2,1,0:T(8,128)(2,1)}, bf16[32,64,128]{2,1,0:T(8,128)(2,1)S(1)}, u32[]{:S(2)}, u32[]{:S(2)}) %collective-permute-start.32) | collective-permute-done | bytes 524320 | tf_op jit(solution)/shard_map/ppermute | solution.py:44
  214.2 1.7 collective-permute-start.40
  217.6 7.2 %shard_map.88 = (f32[33,64,128]{2,1,0:T(8,128)}, f32[8,128]{1,0:T(8,128)}) custom-call(s32[2]{0:T(128)} %pad_add_fusion.3.chips_ref, bf16[8,129,16,128]{3,2,1,0:T(8,128)(2,1)} %get-tuple-element.58.kept, bf16[2,32,128,128]{3,2,1,0:T(8,128)(2,1)} %refs_0_.11, ...), custom_call_target="tpu_custom_call", output_to_operand_aliasing={{0}: (8, {})} | custom-call | flops 4944999936 | tf_op jit(solution)/shard_map/pallas_call | solution.py:382
  224.8 3.3 %collective-permute-done.36.refs_0_ = bf16[32,64,128]{2,1,0:T(8,128)(2,1)S(1)} collective-permute-done((bf16[32,64,128]{2,1,0:T(8,128)(2,1)}, bf16[32,64,128]{2,1,0:T(8,128)(2,1)S(1)}, u32[]{:S(2)}, u32[]{:S(2)}) %collective-permute-start.36) | collective-permute-done | bytes 524320 | tf_op jit(solution)/shard_map/ppermute | solution.py:44
  229.7 2.2 shard_map.90
  233.8 7.2 %shard_map.91 = (f32[33,64,128]{2,1,0:T(8,128)}, f32[8,128]{1,0:T(8,128)}) custom-call(s32[2]{0:T(128)} %pad_add_fusion.4.chips_ref, bf16[8,129,16,128]{3,2,1,0:T(8,128)(2,1)} %get-tuple-element.58.kept, bf16[2,32,128,128]{3,2,1,0:T(8,128)(2,1)} %refs_0_.11, ...), custom_call_target="tpu_custom_call", output_to_operand_aliasing={{0}: (8, {})} | custom-call | flops 4944999936 | tf_op jit(solution)/shard_map/pallas_call | solution.py:382
  242.1 1.1 collective-permute-start.44
  243.2 1.7 collective-permute-done.44.refs_3_
  245.8 5.6 %shard_map.93 = bf16[32,64,128]{2,1,0:T(8,128)(2,1)} custom-call(s32[1]{0:T(128)} %bitcast.chips_ref, bf16[8,129,16,128]{3,2,1,0:T(8,128)(2,1)} %get-tuple-element.58.kept, bf16[2,32,128,128]{3,2,1,0:T(8,128)(2,1)} %refs_0_.11, bf16[2,32,128,128]{3,2,1,0:T(8,128)(2,1)} %collective-permute-done.10.other.refs_1_, bf16[32,64,128]{2,1,0:T(8,128)(2,1)} %shard_map.92.refs_2_, ...), custom_call_target="tpu_custom_call" | custom-call | flops 3335000064 | tf_op jit(solution)/shard_map/pallas_call | solution.py:382
  (143 shorter events, 23.8 us)
Async XLA Ops:
  3.1 7.4 %collective-permute-start.1 = (bf16[2,32,64,128]{3,2,1,0:T(8,128)(2,1)}, bf16[2,32,64,128]{3,2,1,0:T(8,128)(2,1)}, u32[]{:S(2)}, u32[]{:S(2)}) collective-permute-start(bf16[2,32,64,128]{3,2,1,0:T(8,128)(2,1)} %constant_dynamic-slice_fusion.2), channel_id=1, source_target_pairs={{0,1},{1,0},{2,3},{3,2},{4,5},{5,4},{6,7},{7,6},{8,9},{9,8},{10,11... | collective-permute-start | bytes 3145736 | tf_op jit(solution)/shard_map/ppermute | solution.py:44
  3.6 80.9 %collective-permute-start.10 = (bf16[2,32,128,128]{3,2,1,0:T(8,128)(2,1)S(1)}, bf16[2,32,128,128]{3,2,1,0:T(8,128)(2,1)}, u32[]{:S(2)}, u32[]{:S(2)}) collective-permute-start(bf16[2,32,128,128]{3,2,1,0:T(8,128)(2,1)S(1)} %copy-done), channel_id=1, source_target_pairs={{0,1},{1,0},{2,3},{3,2},{4,5},{5,4},{6,7},{7,6},{8,9},{9,8},{10,11... | collective-permute-start | bytes 6291464 | tf_op jit(solution)/shard_map/ppermute | solution.py:44
  3.6 6.8 %collective-permute-start = (s32[2,2,32]{2,1,0:T(2,128)S(1)}, s32[2,2,32]{2,1,0:T(2,128)S(1)}, u32[]{:S(2)}, u32[]{:S(2)}) collective-permute-start(s32[2,2,32]{2,1,0:T(2,128)S(1)} %pad_add_fusion.plan_ref.refs_2_), channel_id=1, source_target_pairs={{0,1},{1,0},{2,3},{3,2},{4,5},{5,4},{6,7},{7,6},{8,9},{9,8},{10,11... | collective-permute-start | bytes 1544 | tf_op jit(solution)/shard_map/ppermute | solution.py:44
  6.2 12.5 %copy-start.2 = (bf16[32,64,128]{2,1,0:T(8,128)(2,1)}, bf16[32,64,128]{2,1,0:T(8,128)(2,1)S(1)}, u32[]{:S(2)}) copy-start(bf16[32,64,128]{2,1,0:T(8,128)(2,1)S(1)} %get-tuple-element.71.near.wave_ref) | copy-start | bytes 1572868
  6.2 27.6 %collective-permute-start.4 = (bf16[32,64,128]{2,1,0:T(8,128)(2,1)S(1)}, bf16[32,64,128]{2,1,0:T(8,128)(2,1)}, u32[]{:S(2)}, u32[]{:S(2)}) collective-permute-start(bf16[32,64,128]{2,1,0:T(8,128)(2,1)S(1)} %get-tuple-element.71.near.wave_ref), channel_id=1, source_target_pairs={{0,8},{1,9},{2,10},{3,11},{4,12},{5,13},{6,14},{7,15},{8,0},{9,1},... | collective-permute-start | bytes 1572872 | tf_op jit(solution)/shard_map/ppermute | solution.py:44
  16.6 17.3 %collective-permute-start.5 = (bf16[129,16,128]{2,1,0:T(8,128)(2,1)}, bf16[129,16,128]{2,1,0:T(8,128)(2,1)S(1)}, u32[]{:S(2)}, u32[]{:S(2)}) collective-permute-start(bf16[129,16,128]{2,1,0:T(8,128)(2,1)} %get-tuple-element.38), channel_id=1, source_target_pairs={{0,2},{1,3},{2,0},{3,1},{4,6},{5,7},{6,4},{7,5},{8,10},{9,11},{10,... | collective-permute-start | bytes 1585160 | tf_op jit(solution)/shard_map/ppermute | solution.py:44
  18.2 24.1 %collective-permute-start.19 = (bf16[32,64,128]{2,1,0:T(8,128)(2,1)S(1)}, bf16[32,64,128]{2,1,0:T(8,128)(2,1)}, u32[]{:S(2)}, u32[]{:S(2)}) collective-permute-start(bf16[32,64,128]{2,1,0:T(8,128)(2,1)S(1)} %get-tuple-element.71.near.wave_ref), channel_id=1, source_target_pairs={{0,2},{1,3},{2,0},{3,1},{4,6},{5,7},{6,4},{7,5},{8,10},{9,11},{10,... | collective-permute-start | bytes 1572872 | tf_op jit(solution)/shard_map/ppermute | solution.py:44
  18.7 25.2 %collective-permute-start.12 = (bf16[32,64,128]{2,1,0:T(8,128)(2,1)S(1)}, bf16[32,64,128]{2,1,0:T(8,128)(2,1)}, u32[]{:S(2)}, u32[]{:S(2)}) collective-permute-start(bf16[32,64,128]{2,1,0:T(8,128)(2,1)S(1)} %get-tuple-element.71.near.wave_ref), channel_id=1, source_target_pairs={{0,4},{1,5},{2,6},{3,7},{4,0},{5,1},{6,2},{7,3},{8,12},{9,13},{10,... | collective-permute-start | bytes 1572872 | tf_op jit(solution)/shard_map/ppermute | solution.py:44
  33.9 38.8 %collective-permute-start.15 = (bf16[129,16,128]{2,1,0:T(8,128)(2,1)}, bf16[129,16,128]{2,1,0:T(8,128)(2,1)}, u32[]{:S(2)}, u32[]{:S(2)}) collective-permute-start(bf16[129,16,128]{2,1,0:T(8,128)(2,1)} %get-tuple-element.42), channel_id=1, source_target_pairs={{0,8},{1,9},{2,10},{3,11},{4,12},{5,13},{6,14},{7,15},{8,0},{9,1},... | collective-permute-start | bytes 1585160 | tf_op jit(solution)/shard_map/ppermute | solution.py:44
  34.7 49.0 %collective-permute-start.2 = (bf16[129,16,128]{2,1,0:T(8,128)(2,1)}, bf16[129,16,128]{2,1,0:T(8,128)(2,1)S(1)}, u32[]{:S(2)}, u32[]{:S(2)}) collective-permute-start(bf16[129,16,128]{2,1,0:T(8,128)(2,1)} %get-tuple-element.37), channel_id=1, source_target_pairs={{0,10},{1,11},{2,8},{3,9},{4,14},{5,15},{6,12},{7,13},{8,2},{9,3},... | collective-permute-start | bytes 1585160 | tf_op jit(solution)/shard_map/ppermute | solution.py:44
  42.3 42.1 %collective-permute-start.21 = (bf16[32,64,128]{2,1,0:T(8,128)(2,1)}, bf16[32,64,128]{2,1,0:T(8,128)(2,1)}, u32[]{:S(2)}, u32[]{:S(2)}) collective-permute-start(bf16[32,64,128]{2,1,0:T(8,128)(2,1)} %shard_map.70.near), channel_id=1, source_target_pairs={{0,2},{1,3},{2,0},{3,1},{4,6},{5,7},{6,4},{7,5},{8,10},{9,11},{10,... | collective-permute-start | bytes 1572872 | tf_op jit(solution)/shard_map/ppermute | solution.py:44
  43.9 46.3 %collective-permute-start.7 = (bf16[129,16,128]{2,1,0:T(8,128)(2,1)}, bf16[129,16,128]{2,1,0:T(8,128)(2,1)S(1)}, u32[]{:S(2)}, u32[]{:S(2)}) collective-permute-start(bf16[129,16,128]{2,1,0:T(8,128)(2,1)} %get-tuple-element.39), channel_id=1, source_target_pairs={{0,4},{1,5},{2,6},{3,7},{4,0},{5,1},{6,2},{7,3},{8,12},{9,13},{10,... | collective-permute-start | bytes 1585160 | tf_op jit(solution)/shard_map/ppermute | solution.py:44
  72.6 21.5 %collective-permute-start.6 = (bf16[32,64,128]{2,1,0:T(8,128)(2,1)}, bf16[32,64,128]{2,1,0:T(8,128)(2,1)}, u32[]{:S(2)}, u32[]{:S(2)}) collective-permute-start(bf16[32,64,128]{2,1,0:T(8,128)(2,1)} %shard_map.70.near), channel_id=1, source_target_pairs={{0,4},{1,5},{2,6},{3,7},{4,0},{5,1},{6,2},{7,3},{8,12},{9,13},{10,... | collective-permute-start | bytes 1572872 | tf_op jit(solution)/shard_map/ppermute | solution.py:44
  83.6 11.8 %collective-permute-start.23 = (bf16[32,64,128]{2,1,0:T(8,128)(2,1)}, bf16[32,64,128]{2,1,0:T(8,128)(2,1)}, u32[]{:S(2)}, u32[]{:S(2)}) collective-permute-start(bf16[32,64,128]{2,1,0:T(8,128)(2,1)} %shard_map.70.near), channel_id=1, source_target_pairs={{0,1},{1,0},{2,3},{3,2},{4,5},{5,4},{6,7},{7,6},{8,9},{9,8},{10,11... | collective-permute-start | bytes 1572872 | tf_op jit(solution)/shard_map/ppermute | solution.py:44
  84.4 23.1 %collective-permute-start.20 = (bf16[32,64,128]{2,1,0:T(8,128)(2,1)}, bf16[32,64,128]{2,1,0:T(8,128)(2,1)S(1)}, u32[]{:S(2)}, u32[]{:S(2)}) collective-permute-start(bf16[32,64,128]{2,1,0:T(8,128)(2,1)} %collective-permute-done.19.near), channel_id=1, source_target_pairs={{0,1},{1,0},{2,3},{3,2},{4,5},{5,4},{6,7},{7,6},{8,9},{9,8},{10,11... | collective-permute-start | bytes 1572872 | tf_op jit(solution)/shard_map/ppermute | solution.py:44
  84.4 17.6 %collective-permute-start.22 = (bf16[32,64,128]{2,1,0:T(8,128)(2,1)}, bf16[32,64,128]{2,1,0:T(8,128)(2,1)}, u32[]{:S(2)}, u32[]{:S(2)}) collective-permute-start(bf16[32,64,128]{2,1,0:T(8,128)(2,1)} %collective-permute-done.21.near), channel_id=1, source_target_pairs={{0,1},{1,0},{2,3},{3,2},{4,5},{5,4},{6,7},{7,6},{8,9},{9,8},{10,11... | collective-permute-start | bytes 1572872 | tf_op jit(solution)/shard_map/ppermute | solution.py:44
  84.9 10.5 %copy-start.8 = (bf16[129,16,128]{2,1,0:T(8,128)(2,1)S(1)}, bf16[129,16,128]{2,1,0:T(8,128)(2,1)}, u32[]{:S(2)}) copy-start(bf16[129,16,128]{2,1,0:T(8,128)(2,1)} %shard_map.73) | copy-start | bytes 1585156
  90.2 23.5 %collective-permute-start.18 = (bf16[32,64,128]{2,1,0:T(8,128)(2,1)}, bf16[32,64,128]{2,1,0:T(8,128)(2,1)S(1)}, u32[]{:S(2)}, u32[]{:S(2)}) collective-permute-start(bf16[32,64,128]{2,1,0:T(8,128)(2,1)} %shard_map.72.near), channel_id=1, source_target_pairs={{0,1},{1,0},{2,3},{3,2},{4,5},{5,4},{6,7},{7,6},{8,9},{9,8},{10,11... | collective-permute-start | bytes 1572872 | tf_op jit(solution)/shard_map/ppermute | solution.py:44
  94.1 20.5 %collective-permute-start.13 = (bf16[32,64,128]{2,1,0:T(8,128)(2,1)}, bf16[32,64,128]{2,1,0:T(8,128)(2,1)S(1)}, u32[]{:S(2)}, u32[]{:S(2)}) collective-permute-start(bf16[32,64,128]{2,1,0:T(8,128)(2,1)} %shard_map.72.near), channel_id=1, source_target_pairs={{0,2},{1,3},{2,0},{3,1},{4,6},{5,7},{6,4},{7,5},{8,10},{9,11},{10,... | collective-permute-start | bytes 1572872 | tf_op jit(solution)/shard_map/ppermute | solution.py:44
  95.5 25.1 %collective-permute-start.16 = (bf16[129,16,128]{2,1,0:T(8,128)(2,1)S(1)}, bf16[129,16,128]{2,1,0:T(8,128)(2,1)S(1)}, u32[]{:S(2)}, u32[]{:S(2)}) collective-permute-start(bf16[129,16,128]{2,1,0:T(8,128)(2,1)S(1)} %copy-done.8), channel_id=1, source_target_pairs={{0,12},{1,13},{2,14},{3,15},{4,8},{5,9},{6,10},{7,11},{8,4},{9,5},... | collective-permute-start | bytes 1585160 | tf_op jit(solution)/shard_map/ppermute | solution.py:44
  102.1 42.7 %collective-permute-start.17 = (bf16[32,64,128]{2,1,0:T(8,128)(2,1)}, bf16[32,64,128]{2,1,0:T(8,128)(2,1)}, u32[]{:S(2)}, u32[]{:S(2)}) collective-permute-start(bf16[32,64,128]{2,1,0:T(8,128)(2,1)} %shard_map.71.near), channel_id=1, source_target_pairs={{0,1},{1,0},{2,3},{3,2},{4,5},{5,4},{6,7},{7,6},{8,9},{9,8},{10,11... | collective-permute-start | bytes 1572872 | tf_op jit(solution)/shard_map/ppermute | solution.py:44
  107.6 37.2 %collective-permute-start.8 = (bf16[32,64,128]{2,1,0:T(8,128)(2,1)}, bf16[32,64,128]{2,1,0:T(8,128)(2,1)S(1)}, u32[]{:S(2)}, u32[]{:S(2)}) collective-permute-start(bf16[32,64,128]{2,1,0:T(8,128)(2,1)} %shard_map.71.near), channel_id=1, source_target_pairs={{0,2},{1,3},{2,0},{3,1},{4,6},{5,7},{6,4},{7,5},{8,10},{9,11},{10,... | collective-permute-start | bytes 1572872 | tf_op jit(solution)/shard_map/ppermute | solution.py:44
  114.5 35.9 %collective-permute-start.11 = (bf16[129,16,128]{2,1,0:T(8,128)(2,1)}, bf16[129,16,128]{2,1,0:T(8,128)(2,1)S(1)}, u32[]{:S(2)}, u32[]{:S(2)}) collective-permute-start(bf16[129,16,128]{2,1,0:T(8,128)(2,1)} %get-tuple-element.40), channel_id=1, source_target_pairs={{0,6},{1,7},{2,4},{3,5},{4,2},{5,3},{6,0},{7,1},{8,14},{9,15},{10,... | collective-permute-start | bytes 1585160 | tf_op jit(solution)/shard_map/ppermute | solution.py:44
  114.6 35.9 %collective-permute-start.14 = (bf16[32,64,128]{2,1,0:T(8,128)(2,1)S(1)}, bf16[32,64,128]{2,1,0:T(8,128)(2,1)}, u32[]{:S(2)}, u32[]{:S(2)}) collective-permute-start(bf16[32,64,128]{2,1,0:T(8,128)(2,1)S(1)} %collective-permute-done.13.near), channel_id=1, source_target_pairs={{0,1},{1,0},{2,3},{3,2},{4,5},{5,4},{6,7},{7,6},{8,9},{9,8},{10,11... | collective-permute-start | bytes 1572872 | tf_op jit(solution)/shard_map/ppermute | solution.py:44
  120.6 24.2 %copy-start.5 = (bf16[129,16,128]{2,1,0:T(8,128)(2,1)}, bf16[129,16,128]{2,1,0:T(8,128)(2,1)S(1)}, u32[]{:S(2)}) copy-start(bf16[129,16,128]{2,1,0:T(8,128)(2,1)S(1)} %collective-permute-done.16.piece) | copy-start | bytes 1585156
  120.6 36.1 %collective-permute-start.3 = (bf16[129,16,128]{2,1,0:T(8,128)(2,1)S(1)}, bf16[129,16,128]{2,1,0:T(8,128)(2,1)S(1)}, u32[]{:S(2)}, u32[]{:S(2)}) collective-permute-start(bf16[129,16,128]{2,1,0:T(8,128)(2,1)S(1)} %copy-done.9), channel_id=1, source_target_pairs={{0,14},{1,15},{2,12},{3,13},{4,10},{5,11},{6,8},{7,9},{8,6},{9,7},... | collective-permute-start | bytes 1585160 | tf_op jit(solution)/shard_map/ppermute | solution.py:44
  144.8 11.9 %collective-permute-start.9 = (bf16[32,64,128]{2,1,0:T(8,128)(2,1)S(1)}, bf16[32,64,128]{2,1,0:T(8,128)(2,1)}, u32[]{:S(2)}, u32[]{:S(2)}) collective-permute-start(bf16[32,64,128]{2,1,0:T(8,128)(2,1)S(1)} %collective-permute-done.8.near), channel_id=1, source_target_pairs={{0,1},{1,0},{2,3},{3,2},{4,5},{5,4},{6,7},{7,6},{8,9},{9,8},{10,11... | collective-permute-start | bytes 1572872 | tf_op jit(solution)/shard_map/ppermute | solution.py:44
  165.6 1.9 collective-permute-start.24
  165.9 3.9 %collective-permute-start.25 = (f32[16,128]{1,0:T(8,128)}, f32[16,128]{1,0:T(8,128)S(1)}, u32[]{:S(2)}, u32[]{:S(2)}) collective-permute-start(f32[16,128]{1,0:T(8,128)} %shard_map.82), channel_id=1, source_target_pairs={{0,2},{1,3},{2,0},{3,1},{4,6},{5,7},{6,4},{7,5},{8,10},{9,11},{10,... | collective-permute-start | bytes 24584 | tf_op jit(solution)/shard_map/ppermute | solution.py:117
  166.5 3.3 %collective-permute-start.26 = (f32[16,128]{1,0:T(8,128)}, f32[16,128]{1,0:T(8,128)S(1)}, u32[]{:S(2)}, u32[]{:S(2)}) collective-permute-start(f32[16,128]{1,0:T(8,128)} %shard_map.82), channel_id=1, source_target_pairs={{0,3},{1,2},{2,1},{3,0},{4,7},{5,6},{6,5},{7,4},{8,11},{9,10},{10,... | collective-permute-start | bytes 24584 | tf_op jit(solution)/shard_map/ppermute | solution.py:117
  170.6 4.4 %collective-permute-start.27 = (f32[16,128]{1,0:T(8,128)S(1)}, f32[16,128]{1,0:T(8,128)S(1)}, u32[]{:S(2)}, u32[]{:S(2)}) collective-permute-start(f32[16,128]{1,0:T(8,128)S(1)} %add_add_fusion.1), channel_id=1, source_target_pairs={{0,4},{1,5},{2,6},{3,7},{4,0},{5,1},{6,2},{7,3},{8,12},{9,13},{10,... | collective-permute-start | bytes 24584 | tf_op jit(solution)/shard_map/ppermute | solution.py:117
  170.6 5.0 %collective-permute-start.28 = (f32[16,128]{1,0:T(8,128)S(1)}, f32[16,128]{1,0:T(8,128)S(1)}, u32[]{:S(2)}, u32[]{:S(2)}) collective-permute-start(f32[16,128]{1,0:T(8,128)S(1)} %add_add_fusion.1), channel_id=1, source_target_pairs={{0,8},{1,9},{2,10},{3,11},{4,12},{5,13},{6,14},{7,15},{8,0},{9,1},... | collective-permute-start | bytes 24584 | tf_op jit(solution)/shard_map/ppermute | solution.py:117
  173.8 5.4 %collective-permute-start.29 = (f32[16,128]{1,0:T(8,128)S(1)}, f32[16,128]{1,0:T(8,128)S(1)}, u32[]{:S(2)}, u32[]{:S(2)}) collective-permute-start(f32[16,128]{1,0:T(8,128)S(1)} %add_add_fusion.1), channel_id=1, source_target_pairs={{0,12},{1,13},{2,14},{3,15},{4,8},{5,9},{6,10},{7,11},{8,4},{9,5},... | collective-permute-start | bytes 24584 | tf_op jit(solution)/shard_map/ppermute | solution.py:117
  182.6 2.1 collective-permute-start.31
  182.7 14.5 %collective-permute-start.30 = (bf16[32,64,128]{2,1,0:T(8,128)(2,1)}, bf16[32,64,128]{2,1,0:T(8,128)(2,1)S(1)}, u32[]{:S(2)}, u32[]{:S(2)}) collective-permute-start(bf16[32,64,128]{2,1,0:T(8,128)(2,1)} %get-tuple-element.60.refs_2_), channel_id=1, source_target_pairs={{0,4},{1,5},{2,0},{3,1},{4,8},{5,9},{6,2},{7,3},{8,12},{9,13},{10,... | collective-permute-start | bytes 1572872 | tf_op jit(solution)/shard_map/ppermute | solution.py:44
  182.7 15.3 %collective-permute-start.34 = (bf16[32,64,128]{2,1,0:T(8,128)(2,1)}, bf16[32,64,128]{2,1,0:T(8,128)(2,1)S(1)}, u32[]{:S(2)}, u32[]{:S(2)}) collective-permute-start(bf16[32,64,128]{2,1,0:T(8,128)(2,1)} %get-tuple-element.60.refs_2_), channel_id=1, source_target_pairs={{0,2},{1,3},{2,6},{3,7},{4,0},{5,1},{6,10},{7,11},{8,4},{9,5},{10,... | collective-permute-start | bytes 1572872 | tf_op jit(solution)/shard_map/ppermute | solution.py:44
  198.0 3.2 %collective-permute-start.33 = (bf16[32,64,128]{2,1,0:T(8,128)(2,1)}, bf16[32,64,128]{2,1,0:T(8,128)(2,1)S(1)}, u32[]{:S(2)}, u32[]{:S(2)}) collective-permute-start(bf16[32,64,128]{2,1,0:T(8,128)(2,1)} %shard_map.85.refs_2_), channel_id=1, source_target_pairs={{0,1},{1,0},{2,3},{3,2},{4,5},{5,4},{6,7},{7,6},{8,9},{9,8},{10,11... | collective-permute-start | bytes 1572872 | tf_op jit(solution)/shard_map/ppermute | solution.py:44
  198.0 3.2 %collective-permute-start.35 = (bf16[32,64,128]{2,1,0:T(8,128)(2,1)S(1)}, bf16[32,64,128]{2,1,0:T(8,128)(2,1)S(1)}, u32[]{:S(2)}, u32[]{:S(2)}) collective-permute-start(bf16[32,64,128]{2,1,0:T(8,128)(2,1)S(1)} %collective-permute-done.34.refs_4_), channel_id=1, source_target_pairs={{0,1},{1,0},{2,3},{3,2},{4,5},{5,4},{6,7},{7,6},{8,9},{9,8},{10,11... | collective-permute-start | bytes 1572872 | tf_op jit(solution)/shard_map/ppermute | solution.py:44
  198.5 14.1 %collective-permute-start.32 = (bf16[32,64,128]{2,1,0:T(8,128)(2,1)}, bf16[32,64,128]{2,1,0:T(8,128)(2,1)S(1)}, u32[]{:S(2)}, u32[]{:S(2)}) collective-permute-start(bf16[32,64,128]{2,1,0:T(8,128)(2,1)} %shard_map.85.refs_2_), channel_id=1, source_target_pairs={{0,4},{1,5},{2,0},{3,1},{4,8},{5,9},{6,2},{7,3},{8,12},{9,13},{10,... | collective-permute-start | bytes 1572872 | tf_op jit(solution)/shard_map/ppermute | solution.py:44
  198.8 14.7 %collective-permute-start.38 = (bf16[32,64,128]{2,1,0:T(8,128)(2,1)S(1)}, bf16[32,64,128]{2,1,0:T(8,128)(2,1)S(1)}, u32[]{:S(2)}, u32[]{:S(2)}) collective-permute-start(bf16[32,64,128]{2,1,0:T(8,128)(2,1)S(1)} %collective-permute-done.34.refs_4_), channel_id=1, source_target_pairs={{0,2},{1,3},{2,6},{3,7},{4,0},{5,1},{6,10},{7,11},{8,4},{9,5},{10,... | collective-permute-start | bytes 1572872 | tf_op jit(solution)/shard_map/ppermute | solution.py:44
  213.4 3.2 %collective-permute-start.37 = (bf16[32,64,128]{2,1,0:T(8,128)(2,1)}, bf16[32,64,128]{2,1,0:T(8,128)(2,1)S(1)}, u32[]{:S(2)}, u32[]{:S(2)}) collective-permute-start(bf16[32,64,128]{2,1,0:T(8,128)(2,1)} %shard_map.87.refs_2_), channel_id=1, source_target_pairs={{0,1},{1,0},{2,3},{3,2},{4,5},{5,4},{6,7},{7,6},{8,9},{9,8},{10,11... | collective-permute-start | bytes 1572872 | tf_op jit(solution)/shard_map/ppermute | solution.py:44
  213.4 3.2 %collective-permute-start.39 = (bf16[32,64,128]{2,1,0:T(8,128)(2,1)S(1)}, bf16[32,64,128]{2,1,0:T(8,128)(2,1)S(1)}, u32[]{:S(2)}, u32[]{:S(2)}) collective-permute-start(bf16[32,64,128]{2,1,0:T(8,128)(2,1)S(1)} %collective-permute-done.38.refs_4_), channel_id=1, source_target_pairs={{0,1},{1,0},{2,3},{3,2},{4,5},{5,4},{6,7},{7,6},{8,9},{9,8},{10,11... | collective-permute-start | bytes 1572872 | tf_op jit(solution)/shard_map/ppermute | solution.py:44
  214.0 14.1 %collective-permute-start.36 = (bf16[32,64,128]{2,1,0:T(8,128)(2,1)}, bf16[32,64,128]{2,1,0:T(8,128)(2,1)S(1)}, u32[]{:S(2)}, u32[]{:S(2)}) collective-permute-start(bf16[32,64,128]{2,1,0:T(8,128)(2,1)} %shard_map.87.refs_2_), channel_id=1, source_target_pairs={{0,4},{1,5},{2,0},{3,1},{4,8},{5,9},{6,2},{7,3},{8,12},{9,13},{10,... | collective-permute-start | bytes 1572872 | tf_op jit(solution)/shard_map/ppermute | solution.py:44
  214.2 14.7 %collective-permute-start.40 = (bf16[32,64,128]{2,1,0:T(8,128)(2,1)S(1)}, bf16[32,64,128]{2,1,0:T(8,128)(2,1)S(1)}, u32[]{:S(2)}, u32[]{:S(2)}) collective-permute-start(bf16[32,64,128]{2,1,0:T(8,128)(2,1)S(1)} %collective-permute-done.38.refs_4_), channel_id=1, source_target_pairs={{0,2},{1,3},{2,6},{3,7},{4,0},{5,1},{6,10},{7,11},{8,4},{9,5},{10,... | collective-permute-start | bytes 1572872 | tf_op jit(solution)/shard_map/ppermute | solution.py:44
  228.9 4.0 %collective-permute-start.42 = (bf16[32,64,128]{2,1,0:T(8,128)(2,1)}, bf16[32,64,128]{2,1,0:T(8,128)(2,1)S(1)}, u32[]{:S(2)}, u32[]{:S(2)}) collective-permute-start(bf16[32,64,128]{2,1,0:T(8,128)(2,1)} %shard_map.89.lower_ref.refs_2_), channel_id=1, source_target_pairs={{0,1},{1,0},{2,3},{3,2},{4,5},{5,4},{6,7},{7,6},{8,9},{9,8},{10,11... | collective-permute-start | bytes 1572872 | tf_op jit(solution)/shard_map/ppermute | solution.py:44
  228.9 3.9 %collective-permute-start.43 = (bf16[32,64,128]{2,1,0:T(8,128)(2,1)S(1)}, bf16[32,64,128]{2,1,0:T(8,128)(2,1)S(1)}, u32[]{:S(2)}, u32[]{:S(2)}) collective-permute-start(bf16[32,64,128]{2,1,0:T(8,128)(2,1)S(1)} %collective-permute-done.40.upper_ref.refs_4_), channel_id=1, source_target_pairs={{0,1},{1,0},{2,3},{3,2},{4,5},{5,4},{6,7},{7,6},{8,9},{9,8},{10,11... | collective-permute-start | bytes 1572872 | tf_op jit(solution)/shard_map/ppermute | solution.py:44
  231.9 9.4 %collective-permute-start.41 = (bf16[32,64,128]{2,1,0:T(8,128)(2,1)}, bf16[32,64,128]{2,1,0:T(8,128)(2,1)S(1)}, u32[]{:S(2)}, u32[]{:S(2)}) collective-permute-start(bf16[32,64,128]{2,1,0:T(8,128)(2,1)} %shard_map.90), channel_id=1, source_target_pairs={{0,4},{1,3},{2,0},{3,7},{4,8},{5,1},{6,2},{7,11},{8,12},{9,5},{10,... | collective-permute-start | bytes 1572872 | tf_op jit(solution)/shard_map/ppermute | solution.py:44
  242.1 2.8 %collective-permute-start.44 = (bf16[32,64,128]{2,1,0:T(8,128)(2,1)}, bf16[32,64,128]{2,1,0:T(8,128)(2,1)S(1)}, u32[]{:S(2)}, u32[]{:S(2)}) collective-permute-start(bf16[32,64,128]{2,1,0:T(8,128)(2,1)} %shard_map.92.refs_2_), channel_id=1, source_target_pairs={{0,1},{1,0},{2,3},{3,2},{4,5},{5,4},{6,7},{7,6},{8,9},{9,8},{10,11... | collective-permute-start | bytes 1572872 | tf_op jit(solution)/shard_map/ppermute | solution.py:44
  (30 other events, 60.9 us)

commit v9 on v5

--- a/solution.py
+++ b/solution.py
@@ -8,8 +8,11 @@
 from jax.sharding import PartitionSpec as P
 
 BOTH = ("sec", "term")
-VMEM_LIMIT = 20 * 2**20
+VMEM_LIMIT = 60 * 2**20
 PART = 16
+ORDER = [0, 4, 5, 1, 2, 6, 3, 7]
+WAITS = {4: 1, 2: 5, 6: 2}
+PIECE_WAITS = {6: 4, 7: 5}
 RING_BYTES = 24 * 2**20
 
 
@@ -98,22 +101,23 @@
         masks.append(step)
         units[step] = exchange(unit, owners, halves, step)
         step //= 2
-    for mask in masks[:-1]:
-        units[mask] = after(units[mask], lefts[masks[0]])
+    waits = dict(WAITS)
     for step in masks[1:]:
         for mask in [m for m in units if m >= 2 * step and m % (2 * step) == 0]:
+            if mask in waits:
+                units[mask] = after(units[mask], lefts[waits.pop(mask)])
             units[mask | step] = exchange(units[mask], owners, halves, step)
     return units
 
 
-def doubled(value, count, axes, stride):
+def spread(value, devices):
     step = 1
-    total = lax.axis_size("sec") * lax.axis_size("term")
-    while step < count:
-        value = value + lax.ppermute(
-            value, axes, [(d, d ^ (step * stride)) for d in range(total)]
-        )
-        step *= 2
+    while step < devices:
+        masks = [step] if 2 * step == devices else [step, 2 * step, 3 * step]
+        parts = [lax.ppermute(value, BOTH, [(d, d ^ m) for d in range(devices)]) for m in masks]
+        for part in parts:
+            value = value + part
+        step *= 4
     return value
 
 
@@ -160,10 +164,7 @@
                     value = left_ref[stream, block, pl.ds(start, rows), :]
                 else:
                     value = other_ref[stream - terms, block]
-                value = pltpu.roll(value.astype(jnp.float32), half * rows, 1)
-                built[mask, at * parts : (at + 1) * parts] = value.astype(jnp.bfloat16).reshape(
-                    parts, PART, width
-                )
+                built[mask, at * parts : (at + 1) * parts] = value.reshape(parts, PART, width)
                 label = jnp.where(row == 0, block, codes[1, owner, at])
                 labels = jnp.where(lane == at, label, labels)
         built[mask, 2 * terms * capacity * parts] = labels.astype(jnp.float32).astype(jnp.bfloat16)
@@ -202,141 +203,206 @@
     )
 
 
-def add_products(piece, labels, near, far, rights, total, streams, capacity):
-    terms = streams // 2
-    blocks, rows, width = near.shape
+def add_products(left, labels, vector, right, total, side, terms, capacity):
+    blocks, rows, width = vector.shape[1:]
     parts = rows // PART
-    for side in range(2):
-        moved, where = [], []
-        for stream in range(terms * side, terms * side + terms):
-            for slot in range(capacity):
-                at = stream * capacity + slot
-                source, target = labels[0, at], labels[1, at]
-                block = jnp.concatenate([near[source], far[source]], axis=0)
-                left = piece[at * parts : (at + 1) * parts].reshape(rows, width)
-                product = jnp.dot(left, block, preferred_element_type=jnp.float32)
-                moved.append(product.astype(jnp.bfloat16))
-                where.append((stream - terms * side, target))
-        for value, (term, target) in zip(moved, where):
-            total[target] += jnp.dot(
-                value,
-                rights[side][term, jnp.minimum(target, blocks - 1)],
-                preferred_element_type=jnp.float32,
-            )
-
-
-def apply_kernel(sources, first, choices, last, streams, capacity, ids_ref, *refs):
-    refs = list(refs)
-    lefts = [refs.pop(0) for _ in range(choices or sources)]
-    vectors = [(refs.pop(0), refs.pop(0)) for _ in range(sources)]
-    rights = refs.pop(0), refs.pop(0)
-    total_in = None if first else refs.pop(0)
-    out = refs.pop(0) if last else None
-    total = refs.pop(0)
-    spread_labels, labels, label_sems = refs.pop(0), refs.pop(0), refs.pop(0)
-    blocks = vectors[0][0].shape[0]
-
-    if choices:
-        chosen, chosen_sems = refs.pop(0), refs.pop(0)
-        for index in range(sources):
-            for choice, left in enumerate(lefts):
-
-                @pl.when(ids_ref[index] == choice)
-                def _():
-                    pltpu.make_async_copy(left, chosen.at[index], chosen_sems.at[index]).start()
-
-    total[...] = jnp.zeros_like(total) if first else total_in[...]
-    pieces = []
-    for index in range(sources):
-        if choices:
-            pltpu.make_async_copy(lefts[0], chosen.at[index], chosen_sems.at[index]).wait()
-            piece = chosen.at[index]
-        else:
-            piece = lefts[index]
-        pieces.append(piece)
-        values = piece[piece.shape[0] - 1].astype(jnp.float32).astype(jnp.int32)
-        spread_labels[index] = values[:8]
-        pltpu.make_async_copy(
-            spread_labels.at[index], labels.at[index], label_sems.at[index]
-        ).start()
-    for index, (near, far) in enumerate(vectors):
-        pltpu.make_async_copy(
-            spread_labels.at[index], labels.at[index], label_sems.at[index]
-        ).wait()
-        add_products(
-            pieces[index], labels.at[index], near, far, rights, total, streams, capacity
+    moved, where = [], []
+    for slot in range(terms * capacity):
+        at = side * terms * capacity + slot
+        block = vector[:, labels[0, at]].reshape(2 * rows, width)
+        piece = left[at * parts : (at + 1) * parts].reshape(rows, width)
+        product = jnp.dot(piece, block, preferred_element_type=jnp.float32)
+        moved.append(product.astype(jnp.bfloat16))
+        where.append(labels[1, at])
+    for slot in range(terms * capacity):
+        target = where[slot]
+        total[target] += jnp.dot(
+            moved[slot],
+            right[slot // capacity, jnp.minimum(target, blocks - 1)],
+            preferred_element_type=jnp.float32,
         )
-    if last:
-        out[...] = total[:blocks].astype(out.dtype)
-
-
-def apply_group(ids, lefts, vectors, rights, total, choices, last):
-    blocks, rows, width = vectors[0][0].shape
-    streams = 2 * rights[0].shape[0]
-    capacity = (lefts[0].shape[0] - 1) * PART // (streams * rows)
-    sources = len(vectors)
-    first = total is None
-    arrays = list(lefts) + [unit for pair in vectors for unit in pair] + list(rights)
-    if not first:
-        arrays.append(total)
-    whole = pl.BlockSpec(memory_space=pltpu.VMEM)
-    total_shape = (blocks + 1, rows, width)
-    scratch = [
-        pltpu.VMEM((sources, 8, width), jnp.int32),
-        pltpu.SMEM((sources, 8, width), jnp.int32),
-        pltpu.SemaphoreType.DMA((sources,)),
-    ]
-    specs = [whole] * len(arrays)
-    if choices:
-        scratch += [
-            pltpu.VMEM((sources,) + lefts[0].shape, lefts[0].dtype),
-            pltpu.SemaphoreType.DMA((sources,)),
-        ]
-        specs[: len(lefts)] = [pl.BlockSpec(memory_space=pl.ANY)] * len(lefts)
-    aliases = {}
-    if last:
-        out_shape = jax.ShapeDtypeStruct((blocks, rows, width), jnp.bfloat16)
-        scratch = [pltpu.VMEM(total_shape, jnp.float32)] + scratch
-    else:
-        out_shape = jax.ShapeDtypeStruct(total_shape, jnp.float32)
-        if not first:
-            aliases = {len(arrays): 0}
-    return pl.pallas_call(
-        functools.partial(
-            apply_kernel, sources, first, len(lefts) if choices else 0, last, streams, capacity
-        ),
-        out_shape=out_shape,
-        in_specs=[pl.BlockSpec(memory_space=pltpu.SMEM)] + specs,
-        out_specs=whole,
-        scratch_shapes=scratch,
-        input_output_aliases=aliases,
-        compiler_params=pltpu.CompilerParams(vmem_limit_bytes=VMEM_LIMIT),
-        cost_estimate=busy(0.7 + 1.4 * sources),
-    )(ids, *arrays)
-
-
-def stats_kernel(ids_ref, total_ref, wave_ref, stats_ref):
+
+
+def local_stats(total, wave_ref, device, stats_ref):
     blocks = wave_ref.shape[0]
     zero = jnp.zeros(wave_ref.shape[1:], jnp.float32)
 
     def sums(block, carry):
         cross, own = carry
         wave = wave_ref[block].astype(jnp.float32)
-        return cross + wave * total_ref[block], own + wave * wave
+        return cross + wave * total[block], own + wave * wave
 
     cross, own = lax.fori_loop(0, blocks, sums, (zero, zero), unroll=4)
     cross, own = jnp.sum(cross, keepdims=True), jnp.sum(own, keepdims=True)
     local = jnp.where(own > 0, cross / own, 0.0)
 
     def squares(block, carry):
-        rest = total_ref[block] - local * wave_ref[block].astype(jnp.float32)
+        rest = total[block] - local * wave_ref[block].astype(jnp.float32)
         return carry + rest * rest
 
     about = jnp.sum(lax.fori_loop(0, blocks, squares, zero, unroll=4), keepdims=True)
     lane = lax.broadcasted_iota(jnp.int32, stats_ref.shape, 1)
     row = lax.broadcasted_iota(jnp.int32, stats_ref.shape, 0)
     values = jnp.where(lane == 0, about, jnp.where(lane == 1, cross, jnp.where(lane == 2, own, local)))
-    stats_ref[...] = jnp.where((row == ids_ref[2]) & (lane < 4), values, 0.0)
+    stats_ref[...] = jnp.where((row == device) & (lane < 4), values, 0.0)
+
+
+def apply_kernel(sources, choices, first, end, terms, capacity, ids_ref, *refs):
+    refs = list(refs)
+
+    def take(count):
+        taken, refs[:count] = refs[:count], []
+        return taken
+
+    lefts = take(choices or sources)
+    rights = take(2)
+    vectors = [take(2) for _ in range(sources)]
+    (wave_in,) = take(1) if end == "stats" else (None,)
+    (total_in,) = (None,) if first else take(1)
+    (total_out,) = (None,) if end == "result" else take(1)
+    (last_out,) = take(1)
+    total, left, right, vector, raw, spread_labels, labels = take(7)
+    left_sems, right_sems, vector_sems, raw_sems, label_sem, total_sem = take(6)
+    (wave, wave_sem) = take(2) if end == "stats" else (None, None)
+    half = ids_ref[0]
+    blocks = vector.shape[2]
+    parts = left.shape[1]
+
+    def left_copies(source, piece):
+        return [
+            pltpu.make_async_copy(piece.at[parts], raw.at[source], raw_sems.at[source]),
+            pltpu.make_async_copy(
+                piece.at[pl.ds(0, parts)], left.at[source], left_sems.at[source]
+            ),
+        ]
+
+    def vector_copies(source):
+        return [
+            pltpu.make_async_copy(
+                vectors[source][part],
+                vector.at[source, half if part == 0 else 1 - half],
+                vector_sems.at[source, part],
+            )
+            for part in range(2)
+        ]
+
+    def right_copy(side):
+        return pltpu.make_async_copy(rights[side], right.at[side], right_sems.at[side])
+
+    for source in range(sources):
+        if choices:
+            for choice, piece in enumerate(lefts):
+
+                @pl.when(ids_ref[2 + source] == choice)
+                def _():
+                    for copy in left_copies(source, piece):
+                        copy.start()
+
+        else:
+            for copy in left_copies(source, lefts[source]):
+                copy.start()
+    for copy in [*vector_copies(0), right_copy(0)]:
+        copy.start()
+    for source in range(1, sources):
+        for copy in vector_copies(source):
+            copy.start()
+    right_copy(1).start()
+    if first:
+        total[...] = jnp.zeros_like(total)
+    else:
+        load_total = pltpu.make_async_copy(total_in, total, total_sem)
+        load_total.start()
+    if end == "stats":
+        load_wave = pltpu.make_async_copy(wave_in, wave, wave_sem)
+        load_wave.start()
+    if end == "go on":
+        last_out[...] = jnp.zeros_like(last_out)
+
+    for source in range(sources):
+        left_copies(source, lefts[0])[0].wait()
+    spread_labels[...] = raw[:, :8].astype(jnp.float32).astype(jnp.int32)
+    move_labels = pltpu.make_async_copy(spread_labels, labels, label_sem)
+    move_labels.start()
+    move_labels.wait()
+    if not first:
+        load_total.wait()
+    for side in range(2):
+        right_copy(side).wait()
+        for source in range(sources):
+            if side == 0:
+                left_copies(source, lefts[0])[1].wait()
+                for copy in vector_copies(source):
+                    copy.wait()
+            add_products(
+                left.at[source],
+                labels.at[source],
+                vector.at[source],
+                right.at[side],
+                total,
+                side,
+                terms,
+                capacity,
+            )
+    if end == "result":
+        last_out[...] = total[:blocks].astype(last_out.dtype)
+    else:
+        store_total = pltpu.make_async_copy(total, total_out, total_sem)
+        store_total.start()
+        if end == "stats":
+            load_wave.wait()
+            local_stats(total, wave, ids_ref[1], last_out)
+        store_total.wait()
+
+
+def apply_group(ids, lefts, rights, vectors, total, end, wave=None):
+    blocks, rows, width = vectors[0][0].shape
+    terms = rights[0].shape[0]
+    parts = lefts[0].shape[0] - 1
+    capacity = parts * PART // (2 * terms * rows)
+    sources, first = len(vectors), total is None
+    arrays = [*lefts, *rights] + [unit for pair in vectors for unit in pair]
+    arrays += [wave] if end == "stats" else []
+    arrays += [] if first else [total]
+    whole = pl.BlockSpec(memory_space=pltpu.VMEM)
+    anywhere = pl.BlockSpec(memory_space=pl.ANY)
+    total_shape = (blocks + 1, rows, width)
+    scratch = [
+        pltpu.VMEM(total_shape, jnp.float32),
+        pltpu.VMEM((sources, parts, PART, width), jnp.bfloat16),
+        pltpu.VMEM((2,) + rights[0].shape, jnp.bfloat16),
+        pltpu.VMEM((sources, 2, blocks, rows, width), jnp.bfloat16),
+        pltpu.VMEM((sources, PART, width), jnp.bfloat16),
+        pltpu.VMEM((sources, 8, width), jnp.int32),
+        pltpu.SMEM((sources, 8, width), jnp.int32),
+        pltpu.SemaphoreType.DMA((sources,)),
+        pltpu.SemaphoreType.DMA((2,)),
+        pltpu.SemaphoreType.DMA((sources, 2)),
+        pltpu.SemaphoreType.DMA((sources,)),
+        pltpu.SemaphoreType.DMA,
+        pltpu.SemaphoreType.DMA,
+    ]
+    if end == "stats":
+        scratch += [pltpu.VMEM(wave.shape, wave.dtype), pltpu.SemaphoreType.DMA]
+    devices = lax.axis_size("sec") * lax.axis_size("term")
+    total_out = jax.ShapeDtypeStruct(total_shape, jnp.float32)
+    out_shape, out_specs = {
+        "go on": ((total_out, jax.ShapeDtypeStruct((8, width), jnp.float32)), (anywhere, whole)),
+        "stats": (
+            (total_out, jax.ShapeDtypeStruct((devices, 128), jnp.float32)),
+            (anywhere, whole),
+        ),
+        "result": (jax.ShapeDtypeStruct((blocks, rows, width), jnp.bfloat16), whole),
+    }[end]
+    choices = len(lefts) if ids.shape[0] > 2 else 0
+    return pl.pallas_call(
+        functools.partial(apply_kernel, sources, choices, first, end, terms, capacity),
+        out_shape=out_shape,
+        in_specs=[pl.BlockSpec(memory_space=pltpu.SMEM)] + [anywhere] * len(arrays),
+        out_specs=out_specs,
+        scratch_shapes=scratch,
+        compiler_params=pltpu.CompilerParams(vmem_limit_bytes=VMEM_LIMIT),
+        cost_estimate=busy(2.0 + 1.4 * sources),
+    )(ids, *arrays)
 
 
 def direction_kernel(entries, total_ref, wave_ref, stats_ref, out_ref, rayleigh_ref):
@@ -355,19 +421,8 @@
         out_ref[block] = (rest * factor).astype(jnp.bfloat16)
 
 
-def new_direction(ids, total, wave, owners, halves, entries):
-    devices = owners * halves
-    scalars = pl.BlockSpec(memory_space=pltpu.SMEM)
+def new_direction(total, wave, stats, entries):
     whole = pl.BlockSpec(memory_space=pltpu.VMEM)
-    params = pltpu.CompilerParams(vmem_limit_bytes=VMEM_LIMIT)
-    stats = pl.pallas_call(
-        stats_kernel,
-        out_shape=jax.ShapeDtypeStruct((devices, 128), jnp.float32),
-        in_specs=[scalars, whole, whole],
-        out_specs=whole,
-        compiler_params=params,
-    )(ids, total, wave)
-    stats = doubled(stats, devices, BOTH, 1)
     return pl.pallas_call(
         functools.partial(direction_kernel, entries),
         out_shape=(
@@ -376,7 +431,8 @@
         ),
         in_specs=[whole] * 3,
         out_specs=(whole, whole),
-        compiler_params=params,
+        compiler_params=pltpu.CompilerParams(vmem_limit_bytes=VMEM_LIMIT),
+        cost_estimate=busy(2.0),
     )(total, wave, stats)
 
 
@@ -387,7 +443,7 @@
     rows = height // halves
     capacity = 2 * blocks // owners
     place = ring_place(me, owners)
-    ids = jnp.stack([me, half, me * halves + half]).astype(jnp.int32)
+    ids = jnp.stack([me, half]).astype(jnp.int32)
 
     own_rows = lax.dynamic_slice_in_dim(wavefunction, half * rows, rows, 1)
     other_rows = lax.dynamic_slice_in_dim(wavefunction, (1 - half) * rows, rows, 1)
@@ -395,10 +451,7 @@
     other_left = swap(
         lax.dynamic_slice_in_dim(left_operator, (1 - half) * rows, rows, 2), owners, halves
     )
-    far_pieces = list(range(owners // 2, owners))
-    order = [0, far_pieces[0]]
-    for m in range(1, owners // 2):
-        order += [far_pieces[m], m]
+    order = [m for m in ORDER if m < owners] + list(range(len(ORDER), owners))
     rights = (right_operator, swap(right_operator, owners, halves))
     pieces = pack(
         ids,
@@ -406,31 +459,44 @@
         swap(plan, owners, halves),
         left_operator,
         other_left,
-        rights[1],
+        plan,
         order[1:] + order[:1],
         capacity,
     )
-    lefts = [exchange(piece, owners, halves, m) if m else piece for m, piece in enumerate(pieces)]
+    lefts = [pieces[0]]
+    for m in range(1, owners):
+        piece = pieces[m]
+        if m in PIECE_WAITS:
+            piece = after(piece, lefts[PIECE_WAITS[m]])
+        lefts.append(exchange(piece, owners, halves, m))
     near = mask_gather(own_rows, lefts, owners, halves)
     far = {m: swap(unit, owners, halves) if m else other_rows for m, unit in near.items()}
 
+    here = [half, me * halves + half]
+    no_choice = jnp.stack(here).astype(jnp.int32)
     total = None
-    no_choice = jnp.zeros((1,), jnp.int32)
-    for m in order:
-        total = apply_group(
-            no_choice, [lefts[m]], [(near[m], far[m])], rights, total, False, False
+    for at in range(0, owners, 2):
+        group = order[at : at + 2]
+        total, stats = apply_group(
+            no_choice,
+            [lefts[m] for m in group],
+            rights,
+            [(near[m], far[m]) for m in group],
+            total,
+            "go on" if at + 2 < owners else "stats",
+            own_rows,
         )
 
     entries = blocks * owners * height * width
-    direction, rayleigh = new_direction(ids, total, own_rows, owners, halves, entries)
+    stats = spread(stats, owners * halves)
+    direction, rayleigh = new_direction(total, own_rows, stats, entries)
     reach = (owners - 1) // 2
 
     def add_group(total, units, last):
-        choice = jnp.stack([ring_owner(place - s, owners) ^ me for s in units])
-        vectors = [
-            (unit, swap(unit, owners, halves)) for unit in units.values()
-        ]
-        return apply_group(choice.astype(jnp.int32), lefts, vectors, rights, total, True, last)
+        choices = [me ^ ring_owner(place - s, owners) for s in units]
+        vectors = [(unit, swap(unit, owners, halves)) for unit in units.values()]
+        ids = jnp.stack(here + choices).astype(jnp.int32)
+        return apply_group(ids, lefts, rights, vectors, total, "result" if last else "go on")
 
     ahead = behind = direction
     units = {0: direction}
@@ -438,13 +504,13 @@
     for step in range(1, reach + 1):
         ahead_next = ring_send(ahead, owners, halves, (1,) * halves)
         behind_next = ring_send(behind, owners, halves, (-1,) * halves)
-        total = add_group(total, units, False)
-        ahead, behind = after(ahead_next, total), behind_next
+        total, token = add_group(total, units, False)
+        ahead, behind = after(ahead_next, token), behind_next
         units = {step: ahead, -step: behind}
     last = select_half(half, ahead, behind)
     last = ring_send(last, owners, halves, (1, -1))
-    total = add_group(total, units, False)
-    total = add_group(total, {owners // 2: after(last, total)}, True)
+    total, token = add_group(total, units, False)
+    total = add_group(total, {owners // 2: after(last, token)}, True)
     return (total, rayleigh[0])
 
 

time: 264 us -> 260 us (0.985)
  local copies, waits for them, and re-layouts: 57.5 us -> 12.9 us
  Pallas kernels: 46.6 us -> 72.1 us
  waiting for transfers between devices: 118 us -> 129 us
  other arithmetic: 0.32 us -> 5.56 us
    unnamed x122 -> x74, local copies, waits for them, and re-layouts: 53.1 us -> 10.6 us
    pallas_call x14 -> x9, Pallas kernels: 37.8 us -> 61.7 us  [apply_group(): pl.pallas_call(functools.partial(apply_kernel, sources, choices, first, e...]
    ppermute x39, waiting for transfers between devices: 110 us -> 123 us  [permute(): return lax.ppermute(value, BOTH, pairs)]
    another operation x4 -> x7, other arithmetic: 0.3 us -> 4.25 us  [the longest x5 3.08 us: add_group(): ids = jnp.stack(here + choices).astype(jnp.int32)]
    ppermute x4 -> x6, waiting for transfers between devices: 7.9 us -> 5.94 us  [spread(): lax.ppermute(value, BOTH, [(d, d ^ m) for d in range(devices)])]
    ppermute x4 -> x6, starting transfers between devices: 7.68 us -> 6.38 us  [spread(): lax.ppermute(value, BOTH, [(d, d ^ m) for d in range(devices)])]
  transfers between devices with their start and end apart: 43 -> 45, of which waited for: 20 -> 17; matrix products, arithmetic and copies ran while one was open for 2% -> 2% of each run, Pallas kernels for 15% -> 22%
where the time goes in v9:
time: 260 us; the launch traced here: 259 us
  waiting for transfers between devices  129 us (50%)
  Pallas kernels  72.1 us (28%)
  starting transfers between devices  38.1 us (15%)
  local copies, waits for them, and re-layouts  12.9 us (5%)
  other arithmetic  5.56 us (2%)
    ppermute x39, waiting for transfers between devices, permute(): return lax.ppermute(value, BOTH, pairs)  123 us
    pallas_call x9, Pallas kernels, apply_group(): pl.pallas_call(functools.partial(apply_kernel, sources, choices, first, e...  61.7 us
    ppermute x39, starting transfers between devices, permute(): return lax.ppermute(value, BOTH, pairs)  31.7 us
    unnamed x74, local copies, waits for them, and re-layouts  10.6 us
    ppermute x6, starting transfers between devices, spread(): lax.ppermute(value, BOTH, [(d, d ^ m) for d in range(devices)])  6.38 us
    ppermute x6, waiting for transfers between devices, spread(): lax.ppermute(value, BOTH, [(d, d ^ m) for d in range(devices)])  5.94 us
    pallas_call x1, Pallas kernels, pack(): pl.pallas_call(functools.partial(pack_kernel, order, capacity, blocks, te...  5.46 us
  transfers between devices with their start and end apart: 45, of which 17 were waited for; matrix products, arithmetic and copies ran while one was open for 2% of the time, Pallas kernels for 22%

profile of v9, /device:TPU:0, one launch (start us, length us, event | category | flops | bytes accessed | tf_op | source)
XLA Modules:
  0.0 259.2 jit_solution(8320341838724127894)
XLA Ops:
  0.7 1.3 constant_dynamic-slice_fusion.2
  3.7 1.1 collective-permute-done.other_plan_ref
  5.4 1.0 copy-done.15
  6.3 5.5 %shard_map.68 = (bf16[129,16,128]{2,1,0:T(8,128)(2,1)}, bf16[129,16,128]{2,1,0:T(8,128)(2,1)}, bf16[129,16,128]{2,1,0:T(8,128)(2,1)}, bf16[129,16,128]{2,1,0:T(8...) custom-call(s32[2]{0:T(128)} %pad_add_fusion.3.ids_ref, ...), custom_call_target="tpu_custom_call" | custom-call | flops 5750000128 | tf_op jit(solution)/shard_map/pallas_call | solution.py:184
  11.8 2.9 %collective-permute-start.2 = (bf16[129,16,128]{2,1,0:T(8,128)(2,1)}, bf16[129,16,128]{2,1,0:T(8,128)(2,1)S(1)}, u32[]{:S(2)}, u32[]{:S(2)}) collective-permute-start(bf16[129,16,128]{2,1,0:T(8,128)(2,1)} %get-tuple-element.26), channel_id=1, source_target_pairs={{0,2},{1,3},{2,0},{3,1},{4,6},{5,7},{6,4},{7,5},{8,10},{9,11},{10,... | collective-permute-start | bytes 1585160 | tf_op jit(solution)/shard_map/ppermute | solution.py:44
  14.7 1.0 constant_dynamic-slice_fusion
  15.8 2.6 collective-permute-start.13
  18.9 1.6 collective-permute-start.10
  20.5 21.5 %collective-permute-done.13.refs_0_ = bf16[32,64,128]{2,1,0:T(8,128)(2,1)S(1)} collective-permute-done((bf16[32,64,128]{2,1,0:T(8,128)(2,1)}, bf16[32,64,128]{2,1,0:T(8,128)(2,1)S(1)}, u32[]{:S(2)}, u32[]{:S(2)}) %collective-permute-start.13) | collective-permute-done | bytes 524320 | tf_op jit(solution)/shard_map/ppermute | solution.py:44
  41.9 2.8 %collective-permute-start.6 = (bf16[129,16,128]{2,1,0:T(8,128)(2,1)}, bf16[129,16,128]{2,1,0:T(8,128)(2,1)S(1)}, u32[]{:S(2)}, u32[]{:S(2)}) collective-permute-start(bf16[129,16,128]{2,1,0:T(8,128)(2,1)} %get-tuple-element.30), channel_id=1, source_target_pairs={{0,10},{1,11},{2,8},{3,9},{4,14},{5,15},{6,12},{7,13},{8,2},{9,3},... | collective-permute-start | bytes 1585160 | tf_op jit(solution)/shard_map/ppermute | solution.py:44
  44.8 2.0 collective-permute-start.3
  47.5 33.1 %collective-permute-done.5.refs_1_.refs_4_ = bf16[129,16,128]{2,1,0:T(8,128)(2,1)S(1)} collective-permute-done((bf16[129,16,128]{2,1,0:T(8,128)(2,1)}, bf16[129,16,128]{2,1,0:T(8,128)(2,1)S(1)}, u32[]{:S(2)}, u32[]{:S(2)}) %collective-permute-start.5) | collective-permute-done | bytes 528416 | tf_op jit(solution)/shard_map/ppermute | solution.py:44
  80.6 9.6 %collective-permute-done.6.refs_1_.refs_0_.refs_5_ = bf16[129,16,128]{2,1,0:T(8,128)(2,1)S(1)} collective-permute-done((bf16[129,16,128]{2,1,0:T(8,128)(2,1)}, bf16[129,16,128]{2,1,0:T(8,128)(2,1)S(1)}, u32[]{:S(2)}, u32[]{:S(2)}) %collective-permute-start.6) | collective-permute-done | bytes 528416 | tf_op jit(solution)/shard_map/ppermute | solution.py:44
  90.2 1.3 collective-permute-start.19
  92.4 1.0 copy-done.8
  94.2 4.8 %collective-permute-start.7 = (bf16[129,16,128]{2,1,0:T(8,128)(2,1)S(1)}, bf16[129,16,128]{2,1,0:T(8,128)(2,1)S(1)}, u32[]{:S(2)}, u32[]{:S(2)}) collective-permute-start(bf16[129,16,128]{2,1,0:T(8,128)(2,1)S(1)} %copy-done.6), channel_id=1, source_target_pairs={{0,12},{1,13},{2,14},{3,15},{4,8},{5,9},{6,10},{7,11},{8,4},{9,5},... | collective-permute-start | bytes 1585160 | tf_op jit(solution)/shard_map/ppermute | solution.py:44
  99.6 5.7 %collective-permute-done.19.refs_4_ = bf16[32,64,128]{2,1,0:T(8,128)(2,1)} collective-permute-done((bf16[32,64,128]{2,1,0:T(8,128)(2,1)}, bf16[32,64,128]{2,1,0:T(8,128)(2,1)}, u32[]{:S(2)}, u32[]{:S(2)}) %collective-permute-start.19) | collective-permute-done | bytes 524320 | tf_op jit(solution)/shard_map/ppermute | solution.py:44
  105.8 6.7 %shard_map.74 = (f32[33,64,128]{2,1,0:T(8,128)}, f32[8,128]{1,0:T(8,128)}) custom-call(s32[2]{0:T(128)} %pad_add_fusion.4.ids_ref, bf16[129,16,128]{2,1,0:T(8,128)(2,1)} %get-tuple-element.25.refs_0_, bf16[129,16,128]{2,1,0:T(8,128)(2,1)} %copy-done.3, bf16[2,32,128,128]{3,2,1,0:T(8,128)(2,1)} %refs_8_.9, ...), custom_call_target="tpu_custom_call" | custom-call | flops 5520000000 | tf_op jit(solution)/shard_map/pallas_call | solution.py:397
  112.5 4.0 %collective-permute-done.11.refs_4_ = bf16[32,64,128]{2,1,0:T(8,128)(2,1)} collective-permute-done((bf16[32,64,128]{2,1,0:T(8,128)(2,1)S(1)}, bf16[32,64,128]{2,1,0:T(8,128)(2,1)}, u32[]{:S(2)}, u32[]{:S(2)}) %collective-permute-start.11) | collective-permute-done | bytes 524320 | tf_op jit(solution)/shard_map/ppermute | solution.py:44
  116.6 1.9 collective-permute-start.8
  118.5 31.4 %collective-permute-done.15.refs_6_ = bf16[32,64,128]{2,1,0:T(8,128)(2,1)} collective-permute-done((bf16[32,64,128]{2,1,0:T(8,128)(2,1)}, bf16[32,64,128]{2,1,0:T(8,128)(2,1)}, u32[]{:S(2)}, u32[]{:S(2)}) %collective-permute-start.15) | collective-permute-done | bytes 524320 | tf_op jit(solution)/shard_map/ppermute | solution.py:44
  150.0 7.4 %shard_map.75 = (f32[33,64,128]{2,1,0:T(8,128)}, f32[8,128]{1,0:T(8,128)}) custom-call(s32[2]{0:T(128)} %pad_add_fusion.4.ids_ref, bf16[129,16,128]{2,1,0:T(8,128)(2,1)} %copy-done, bf16[129,16,128]{2,1,0:T(8,128)(2,1)} %copy-done.2, bf16[2,32,128,128]{3,2,1,0:T(8,128)(2,1)} %refs_8_.9, bf16[2,32,128,128]{3,2,1,0:T(8,128)(2,1)} %collective-permute-done.9.refs_3_.refs_9_, ...), custom_call_target="tpu_custom_call" | custom-call | flops 5520000000 | tf_op jit(solution)/shard_map/pallas_call | solution.py:397
  157.4 7.3 %shard_map.76 = (f32[33,64,128]{2,1,0:T(8,128)}, f32[8,128]{1,0:T(8,128)}) custom-call(s32[2]{0:T(128)} %pad_add_fusion.4.ids_ref, bf16[129,16,128]{2,1,0:T(8,128)(2,1)} %copy-done.4, bf16[129,16,128]{2,1,0:T(8,128)(2,1)} %copy-done.16, bf16[2,32,128,128]{3,2,1,0:T(8,128)(2,1)} %refs_8_.9, bf16[2,32,128,128]{3,2,1,0:T(8,128)(2,1)} %collective-permute-done.9.refs_3_.refs_9_, ...), custom_call_target="tpu_custom_call" | custom-call | flops 5520000000 | tf_op jit(solution)/shard_map/pallas_call | solution.py:397
  165.9 7.4 %shard_map.77 = (f32[33,64,128]{2,1,0:T(8,128)}, f32[16,128]{1,0:T(8,128)}) custom-call(s32[2]{0:T(128)} %pad_add_fusion.4.ids_ref, bf16[129,16,128]{2,1,0:T(8,128)(2,1)} %copy-done.17, bf16[129,16,128]{2,1,0:T(8,128)(2,1)} %copy-done.18, bf16[2,32,128,128]{3,2,1,0:T(8,128)(2,1)} %refs_8_.9, ...), custom_call_target="tpu_custom_call" | custom-call | flops 5520000000 | tf_op jit(solution)/shard_map/pallas_call | solution.py:397
  173.8 1.3 collective-permute-start.25
  175.3 2.4 collective-permute-done.25
  179.2 1.7 collective-permute-start.28
  180.8 2.7 %collective-permute-start.29 = (f32[16,128]{1,0:T(8,128)S(1)}, f32[16,128]{1,0:T(8,128)S(1)}, u32[]{:S(2)}, u32[]{:S(2)}) collective-permute-start(f32[16,128]{1,0:T(8,128)S(1)} %add_add_fusion.1), channel_id=1, source_target_pairs={{0,12},{1,13},{2,14},{3,15},{4,8},{5,9},{6,10},{7,11},{8,4},{9,5},... | collective-permute-start | bytes 24584 | tf_op jit(solution)/shard_map/ppermute | solution.py:117
  183.7 2.6 collective-permute-done.29
  186.9 2.8 %shard_map.78 = (bf16[32,64,128]{2,1,0:T(8,128)(2,1)}, f32[1,1]{1,0:T(1,128)}) custom-call(f32[33,64,128]{2,1,0:T(8,128)} %get-tuple-element.36.total_ref, bf16[32,64,128]{2,1,0:T(8,128)(2,1)} %get-tuple-element.49.refs_4_.refs_8_.wave_ref, f32[16,128]{1,0:T(8,128)} %add_add_fusion.stats_ref), custom_call_target="tpu_custom_call" | custom-call | flops 2300000000 | tf_op jit(solution)/shard_map/pallas_call | solution.py:426
  189.7 2.0 collective-permute-start.34
  193.1 5.5 %shard_map.79 = (f32[33,64,128]{2,1,0:T(8,128)}, f32[8,128]{1,0:T(8,128)}) custom-call(s32[3]{0:T(128)} %pad_add_fusion.5.ids_ref, bf16[129,16,128]{2,1,0:T(8,128)(2,1)} %get-tuple-element.25.refs_0_, bf16[129,16,128]{2,1,0:T(8,128)(2,1)} %copy-done.2, bf16[129,16,128]{2,1,0:T(8,128)(2,1)} %copy-done.4, bf16[129,16,128]{2,1,0:T(8,128)(2,1)} %copy-done.17, ...), custom_call_target="tpu_custom_call" | custom-call | flops 3910000128 | tf_op jit(solution)/shard_map/pallas_call | solution.py:397
  198.6 5.7 %collective-permute-done.30.refs_0_ = bf16[32,64,128]{2,1,0:T(8,128)(2,1)} collective-permute-done((bf16[32,64,128]{2,1,0:T(8,128)(2,1)}, bf16[32,64,128]{2,1,0:T(8,128)(2,1)}, u32[]{:S(2)}, u32[]{:S(2)}) %collective-permute-start.30) | collective-permute-done | bytes 524320 | tf_op jit(solution)/shard_map/ppermute | solution.py:44
  204.8 1.2 collective-permute-start.32
  208.5 7.3 %shard_map.81 = (f32[33,64,128]{2,1,0:T(8,128)}, f32[8,128]{1,0:T(8,128)}) custom-call(s32[4]{0:T(128)} %pad_add_fusion.6.ids_ref, bf16[129,16,128]{2,1,0:T(8,128)(2,1)} %get-tuple-element.25.refs_0_, bf16[129,16,128]{2,1,0:T(8,128)(2,1)} %copy-done.2, bf16[129,16,128]{2,1,0:T(8,128)(2,1)} %copy-done.4, bf16[129,16,128]{2,1,0:T(8,128)(2,1)} %copy-done.17, ...), custom_call_target="tpu_custom_call" | custom-call | flops 5520000000 | tf_op jit(solution)/shard_map/pallas_call | solution.py:397
  215.9 3.2 %collective-permute-done.32.refs_0_ = bf16[32,64,128]{2,1,0:T(8,128)(2,1)} collective-permute-done((bf16[32,64,128]{2,1,0:T(8,128)(2,1)}, bf16[32,64,128]{2,1,0:T(8,128)(2,1)}, u32[]{:S(2)}, u32[]{:S(2)}) %collective-permute-start.32) | collective-permute-done | bytes 524320 | tf_op jit(solution)/shard_map/ppermute | solution.py:44
  219.1 1.7 collective-permute-done.38.refs_12_
  220.8 1.7 collective-permute-start.36
  224.4 7.4 %shard_map.83 = (f32[33,64,128]{2,1,0:T(8,128)}, f32[8,128]{1,0:T(8,128)}) custom-call(s32[4]{0:T(128)} %pad_add_fusion.8.ids_ref, bf16[129,16,128]{2,1,0:T(8,128)(2,1)} %get-tuple-element.25.refs_0_, bf16[129,16,128]{2,1,0:T(8,128)(2,1)} %copy-done.2, bf16[129,16,128]{2,1,0:T(8,128)(2,1)} %copy-done.4, bf16[129,16,128]{2,1,0:T(8,128)(2,1)} %copy-done.17, ...), custom_call_target="tpu_custom_call" | custom-call | flops 5520000000 | tf_op jit(solution)/shard_map/pallas_call | solution.py:397
  231.8 3.6 %collective-permute-done.36.refs_0_ = bf16[32,64,128]{2,1,0:T(8,128)(2,1)S(1)} collective-permute-done((bf16[32,64,128]{2,1,0:T(8,128)(2,1)}, bf16[32,64,128]{2,1,0:T(8,128)(2,1)S(1)}, u32[]{:S(2)}, u32[]{:S(2)}) %collective-permute-start.36) | collective-permute-done | bytes 524320 | tf_op jit(solution)/shard_map/ppermute | solution.py:44
  236.1 1.0 collective-permute-done.40.upper_ref.refs_12_
  237.1 0.8 copy-done.23
  238.0 2.1 shard_map.85
  242.5 7.3 %shard_map.86 = (f32[33,64,128]{2,1,0:T(8,128)}, f32[8,128]{1,0:T(8,128)}) custom-call(s32[4]{0:T(128)} %pad_add_fusion.9.ids_ref, bf16[129,16,128]{2,1,0:T(8,128)(2,1)} %get-tuple-element.25.refs_0_, bf16[129,16,128]{2,1,0:T(8,128)(2,1)} %copy-done.2, bf16[129,16,128]{2,1,0:T(8,128)(2,1)} %copy-done.4, bf16[129,16,128]{2,1,0:T(8,128)(2,1)} %copy-done.17, ...), custom_call_target="tpu_custom_call" | custom-call | flops 5520000000 | tf_op jit(solution)/shard_map/pallas_call | solution.py:397
  249.8 0.8 copy-done.35
  251.3 1.5 collective-permute-done.44.refs_11_
  252.8 0.8 copy-done.32
  253.6 5.4 %shard_map.88 = bf16[32,64,128]{2,1,0:T(8,128)(2,1)} custom-call(s32[3]{0:T(128)} %pad_add_fusion.1.ids_ref, bf16[129,16,128]{2,1,0:T(8,128)(2,1)} %get-tuple-element.25.refs_0_, bf16[129,16,128]{2,1,0:T(8,128)(2,1)} %copy-done.2, bf16[129,16,128]{2,1,0:T(8,128)(2,1)} %copy-done.4, bf16[129,16,128]{2,1,0:T(8,128)(2,1)} %copy-done.17, ...), custom_call_target="tpu_custom_call" | custom-call | flops 3910000128 | tf_op jit(solution)/shard_map/pallas_call | solution.py:397
  (149 shorter events, 20.3 us)
Async XLA Ops:
  2.0 2.8 %collective-permute-start.1 = (bf16[2,32,64,128]{3,2,1,0:T(8,128)(2,1)S(1)}, bf16[2,32,64,128]{3,2,1,0:T(8,128)(2,1)S(1)}, u32[]{:S(2)}, u32[]{:S(2)}) collective-permute-start(bf16[2,32,64,128]{3,2,1,0:T(8,128)(2,1)S(1)} %constant_dynamic-slice_fusion.2), channel_id=1, source_target_pairs={{0,1},{1,0},{2,3},{3,2},{4,5},{5,4},{6,7},{7,6},{8,9},{9,8},{10,11... | collective-permute-start | bytes 3145736 | tf_op jit(solution)/shard_map/ppermute | solution.py:44
  2.5 2.3 collective-permute-start
  2.6 91.5 %collective-permute-start.9 = (bf16[2,32,128,128]{3,2,1,0:T(8,128)(2,1)}, bf16[2,32,128,128]{3,2,1,0:T(8,128)(2,1)}, u32[]{:S(2)}, u32[]{:S(2)}) collective-permute-start(bf16[2,32,128,128]{3,2,1,0:T(8,128)(2,1)} %refs_8_.9), channel_id=1, source_target_pairs={{0,1},{1,0},{2,3},{3,2},{4,5},{5,4},{6,7},{7,6},{8,9},{9,8},{10,11... | collective-permute-start | bytes 6291464 | tf_op jit(solution)/shard_map/ppermute | solution.py:44
  11.8 33.0 %collective-permute-start.2 = (bf16[129,16,128]{2,1,0:T(8,128)(2,1)}, bf16[129,16,128]{2,1,0:T(8,128)(2,1)S(1)}, u32[]{:S(2)}, u32[]{:S(2)}) collective-permute-start(bf16[129,16,128]{2,1,0:T(8,128)(2,1)} %get-tuple-element.26), channel_id=1, source_target_pairs={{0,2},{1,3},{2,0},{3,1},{4,6},{5,7},{6,4},{7,5},{8,10},{9,11},{10,... | collective-permute-start | bytes 1585160 | tf_op jit(solution)/shard_map/ppermute | solution.py:44
  15.8 26.1 %collective-permute-start.13 = (bf16[32,64,128]{2,1,0:T(8,128)(2,1)}, bf16[32,64,128]{2,1,0:T(8,128)(2,1)S(1)}, u32[]{:S(2)}, u32[]{:S(2)}) collective-permute-start(bf16[32,64,128]{2,1,0:T(8,128)(2,1)} %get-tuple-element.49.refs_4_.refs_8_.wave_ref), channel_id=1, source_target_pairs={{0,8},{1,9},{2,10},{3,11},{4,12},{5,13},{6,14},{7,15},{8,0},{9,1},... | collective-permute-start | bytes 1572872 | tf_op jit(solution)/shard_map/ppermute | solution.py:44
  18.4 23.6 %collective-permute-start.21 = (bf16[32,64,128]{2,1,0:T(8,128)(2,1)}, bf16[32,64,128]{2,1,0:T(8,128)(2,1)S(1)}, u32[]{:S(2)}, u32[]{:S(2)}) collective-permute-start(bf16[32,64,128]{2,1,0:T(8,128)(2,1)} %get-tuple-element.49.refs_4_.refs_8_.wave_ref), channel_id=1, source_target_pairs={{0,2},{1,3},{2,0},{3,1},{4,6},{5,7},{6,4},{7,5},{8,10},{9,11},{10,... | collective-permute-start | bytes 1572872 | tf_op jit(solution)/shard_map/ppermute | solution.py:44
  18.9 27.8 %collective-permute-start.10 = (bf16[32,64,128]{2,1,0:T(8,128)(2,1)}, bf16[32,64,128]{2,1,0:T(8,128)(2,1)S(1)}, u32[]{:S(2)}, u32[]{:S(2)}) collective-permute-start(bf16[32,64,128]{2,1,0:T(8,128)(2,1)} %get-tuple-element.49.refs_4_.refs_8_.wave_ref), channel_id=1, source_target_pairs={{0,4},{1,5},{2,6},{3,7},{4,0},{5,1},{6,2},{7,3},{8,12},{9,13},{10,... | collective-permute-start | bytes 1572872 | tf_op jit(solution)/shard_map/ppermute | solution.py:44
  41.9 38.7 %collective-permute-start.5 = (bf16[129,16,128]{2,1,0:T(8,128)(2,1)}, bf16[129,16,128]{2,1,0:T(8,128)(2,1)S(1)}, u32[]{:S(2)}, u32[]{:S(2)}) collective-permute-start(bf16[129,16,128]{2,1,0:T(8,128)(2,1)} %get-tuple-element.29), channel_id=1, source_target_pairs={{0,8},{1,9},{2,10},{3,11},{4,12},{5,13},{6,14},{7,15},{8,0},{9,1},... | collective-permute-start | bytes 1585160 | tf_op jit(solution)/shard_map/ppermute | solution.py:44
  41.9 48.2 %collective-permute-start.6 = (bf16[129,16,128]{2,1,0:T(8,128)(2,1)}, bf16[129,16,128]{2,1,0:T(8,128)(2,1)S(1)}, u32[]{:S(2)}, u32[]{:S(2)}) collective-permute-start(bf16[129,16,128]{2,1,0:T(8,128)(2,1)} %get-tuple-element.30), channel_id=1, source_target_pairs={{0,10},{1,11},{2,8},{3,9},{4,14},{5,15},{6,12},{7,13},{8,2},{9,3},... | collective-permute-start | bytes 1585160 | tf_op jit(solution)/shard_map/ppermute | solution.py:44
  44.8 45.4 %collective-permute-start.3 = (bf16[129,16,128]{2,1,0:T(8,128)(2,1)}, bf16[129,16,128]{2,1,0:T(8,128)(2,1)S(1)}, u32[]{:S(2)}, u32[]{:S(2)}) collective-permute-start(bf16[129,16,128]{2,1,0:T(8,128)(2,1)} %get-tuple-element.27), channel_id=1, source_target_pairs={{0,4},{1,5},{2,6},{3,7},{4,0},{5,1},{6,2},{7,3},{8,12},{9,13},{10,... | collective-permute-start | bytes 1585160 | tf_op jit(solution)/shard_map/ppermute | solution.py:44
  46.7 44.8 %copy-start.7 = (bf16[32,64,128]{2,1,0:T(8,128)(2,1)}, bf16[32,64,128]{2,1,0:T(8,128)(2,1)S(1)}, u32[]{:S(2)}) copy-start(bf16[32,64,128]{2,1,0:T(8,128)(2,1)S(1)} %collective-permute-done.10.refs_0_) | copy-start | bytes 1572868
  46.7 44.8 %collective-permute-start.14 = (bf16[32,64,128]{2,1,0:T(8,128)(2,1)}, bf16[32,64,128]{2,1,0:T(8,128)(2,1)S(1)}, u32[]{:S(2)}, u32[]{:S(2)}) collective-permute-start(bf16[32,64,128]{2,1,0:T(8,128)(2,1)} %shard_map.72.refs_6_), channel_id=1, source_target_pairs={{0,4},{1,5},{2,6},{3,7},{4,0},{5,1},{6,2},{7,3},{8,12},{9,13},{10,... | collective-permute-start | bytes 1572872 | tf_op jit(solution)/shard_map/ppermute | solution.py:44
  80.6 11.8 %collective-permute-start.22 = (bf16[32,64,128]{2,1,0:T(8,128)(2,1)}, bf16[32,64,128]{2,1,0:T(8,128)(2,1)S(1)}, u32[]{:S(2)}, u32[]{:S(2)}) collective-permute-start(bf16[32,64,128]{2,1,0:T(8,128)(2,1)} %copy-done.21), channel_id=1, source_target_pairs={{0,1},{1,0},{2,3},{3,2},{4,5},{5,4},{6,7},{7,6},{8,9},{9,8},{10,11... | collective-permute-start | bytes 1572872 | tf_op jit(solution)/shard_map/ppermute | solution.py:44
  90.2 8.8 %collective-permute-start.23 = (bf16[32,64,128]{2,1,0:T(8,128)(2,1)}, bf16[32,64,128]{2,1,0:T(8,128)(2,1)}, u32[]{:S(2)}, u32[]{:S(2)}) collective-permute-start(bf16[32,64,128]{2,1,0:T(8,128)(2,1)} %shard_map.72.refs_6_), channel_id=1, source_target_pairs={{0,1},{1,0},{2,3},{3,2},{4,5},{5,4},{6,7},{7,6},{8,9},{9,8},{10,11... | collective-permute-start | bytes 1572872 | tf_op jit(solution)/shard_map/ppermute | solution.py:44
  90.2 15.1 %collective-permute-start.19 = (bf16[32,64,128]{2,1,0:T(8,128)(2,1)}, bf16[32,64,128]{2,1,0:T(8,128)(2,1)}, u32[]{:S(2)}, u32[]{:S(2)}) collective-permute-start(bf16[32,64,128]{2,1,0:T(8,128)(2,1)} %shard_map.72.refs_6_), channel_id=1, source_target_pairs={{0,2},{1,3},{2,0},{3,1},{4,6},{5,7},{6,4},{7,5},{8,10},{9,11},{10,... | collective-permute-start | bytes 1572872 | tf_op jit(solution)/shard_map/ppermute | solution.py:44
  91.5 13.8 %collective-permute-start.17 = (bf16[32,64,128]{2,1,0:T(8,128)(2,1)}, bf16[32,64,128]{2,1,0:T(8,128)(2,1)}, u32[]{:S(2)}, u32[]{:S(2)}) collective-permute-start(bf16[32,64,128]{2,1,0:T(8,128)(2,1)} %shard_map.71.refs_4_), channel_id=1, source_target_pairs={{0,1},{1,0},{2,3},{3,2},{4,5},{5,4},{6,7},{7,6},{8,9},{9,8},{10,11... | collective-permute-start | bytes 1572872 | tf_op jit(solution)/shard_map/ppermute | solution.py:44
  92.4 12.9 %copy-start.10 = (bf16[32,64,128]{2,1,0:T(8,128)(2,1)S(1)}, bf16[32,64,128]{2,1,0:T(8,128)(2,1)}, u32[]{:S(2)}) copy-start(bf16[32,64,128]{2,1,0:T(8,128)(2,1)} %shard_map.73.refs_6_) | copy-start | bytes 1572868
  93.4 23.1 %collective-permute-start.11 = (bf16[32,64,128]{2,1,0:T(8,128)(2,1)S(1)}, bf16[32,64,128]{2,1,0:T(8,128)(2,1)}, u32[]{:S(2)}, u32[]{:S(2)}) collective-permute-start(bf16[32,64,128]{2,1,0:T(8,128)(2,1)S(1)} %copy-done.8), channel_id=1, source_target_pairs={{0,2},{1,3},{2,0},{3,1},{4,6},{5,7},{6,4},{7,5},{8,10},{9,11},{10,... | collective-permute-start | bytes 1572872 | tf_op jit(solution)/shard_map/ppermute | solution.py:44
  94.2 22.4 %collective-permute-start.7 = (bf16[129,16,128]{2,1,0:T(8,128)(2,1)S(1)}, bf16[129,16,128]{2,1,0:T(8,128)(2,1)S(1)}, u32[]{:S(2)}, u32[]{:S(2)}) collective-permute-start(bf16[129,16,128]{2,1,0:T(8,128)(2,1)S(1)} %copy-done.6), channel_id=1, source_target_pairs={{0,12},{1,13},{2,14},{3,15},{4,8},{5,9},{6,10},{7,11},{8,4},{9,5},... | collective-permute-start | bytes 1585160 | tf_op jit(solution)/shard_map/ppermute | solution.py:44
  99.0 51.0 %collective-permute-start.15 = (bf16[32,64,128]{2,1,0:T(8,128)(2,1)}, bf16[32,64,128]{2,1,0:T(8,128)(2,1)}, u32[]{:S(2)}, u32[]{:S(2)}) collective-permute-start(bf16[32,64,128]{2,1,0:T(8,128)(2,1)} %shard_map.73.refs_6_), channel_id=1, source_target_pairs={{0,2},{1,3},{2,0},{3,1},{4,6},{5,7},{6,4},{7,5},{8,10},{9,11},{10,... | collective-permute-start | bytes 1572872 | tf_op jit(solution)/shard_map/ppermute | solution.py:44
  105.3 13.2 %collective-permute-start.20 = (bf16[32,64,128]{2,1,0:T(8,128)(2,1)}, bf16[32,64,128]{2,1,0:T(8,128)(2,1)}, u32[]{:S(2)}, u32[]{:S(2)}) collective-permute-start(bf16[32,64,128]{2,1,0:T(8,128)(2,1)} %collective-permute-done.19.refs_4_), channel_id=1, source_target_pairs={{0,1},{1,0},{2,3},{3,2},{4,5},{5,4},{6,7},{7,6},{8,9},{9,8},{10,11... | collective-permute-start | bytes 1572872 | tf_op jit(solution)/shard_map/ppermute | solution.py:44
  105.3 52.1 %collective-permute-start.18 = (bf16[32,64,128]{2,1,0:T(8,128)(2,1)S(1)}, bf16[32,64,128]{2,1,0:T(8,128)(2,1)}, u32[]{:S(2)}, u32[]{:S(2)}) collective-permute-start(bf16[32,64,128]{2,1,0:T(8,128)(2,1)S(1)} %copy-done.10), channel_id=1, source_target_pairs={{0,1},{1,0},{2,3},{3,2},{4,5},{5,4},{6,7},{7,6},{8,9},{9,8},{10,11... | collective-permute-start | bytes 1572872 | tf_op jit(solution)/shard_map/ppermute | solution.py:44
  116.5 48.2 %collective-permute-start.4 = (bf16[129,16,128]{2,1,0:T(8,128)(2,1)S(1)}, bf16[129,16,128]{2,1,0:T(8,128)(2,1)S(1)}, u32[]{:S(2)}, u32[]{:S(2)}) collective-permute-start(bf16[129,16,128]{2,1,0:T(8,128)(2,1)S(1)} %copy-done.19), channel_id=1, source_target_pairs={{0,6},{1,7},{2,4},{3,5},{4,2},{5,3},{6,0},{7,1},{8,14},{9,15},{10,... | collective-permute-start | bytes 1585160 | tf_op jit(solution)/shard_map/ppermute | solution.py:44
  116.6 40.8 %copy-start.16 = (bf16[129,16,128]{2,1,0:T(8,128)(2,1)}, bf16[129,16,128]{2,1,0:T(8,128)(2,1)S(1)}, u32[]{:S(2)}) copy-start(bf16[129,16,128]{2,1,0:T(8,128)(2,1)S(1)} %collective-permute-done.7.refs_1_.refs_6_) | copy-start | bytes 1585156
  116.6 48.2 %collective-permute-start.8 = (bf16[129,16,128]{2,1,0:T(8,128)(2,1)S(1)}, bf16[129,16,128]{2,1,0:T(8,128)(2,1)S(1)}, u32[]{:S(2)}, u32[]{:S(2)}) collective-permute-start(bf16[129,16,128]{2,1,0:T(8,128)(2,1)S(1)} %copy-done.5), channel_id=1, source_target_pairs={{0,14},{1,15},{2,12},{3,13},{4,10},{5,11},{6,8},{7,9},{8,6},{9,7},... | collective-permute-start | bytes 1585160 | tf_op jit(solution)/shard_map/ppermute | solution.py:44
  118.5 46.2 %collective-permute-start.12 = (bf16[32,64,128]{2,1,0:T(8,128)(2,1)}, bf16[32,64,128]{2,1,0:T(8,128)(2,1)S(1)}, u32[]{:S(2)}, u32[]{:S(2)}) collective-permute-start(bf16[32,64,128]{2,1,0:T(8,128)(2,1)} %collective-permute-done.11.refs_4_), channel_id=1, source_target_pairs={{0,1},{1,0},{2,3},{3,2},{4,5},{5,4},{6,7},{7,6},{8,9},{9,8},{10,11... | collective-permute-start | bytes 1572872 | tf_op jit(solution)/shard_map/ppermute | solution.py:44
  150.0 14.8 %collective-permute-start.16 = (bf16[32,64,128]{2,1,0:T(8,128)(2,1)}, bf16[32,64,128]{2,1,0:T(8,128)(2,1)}, u32[]{:S(2)}, u32[]{:S(2)}) collective-permute-start(bf16[32,64,128]{2,1,0:T(8,128)(2,1)} %collective-permute-done.15.refs_6_), channel_id=1, source_target_pairs={{0,1},{1,0},{2,3},{3,2},{4,5},{5,4},{6,7},{7,6},{8,9},{9,8},{10,11... | collective-permute-start | bytes 1572872 | tf_op jit(solution)/shard_map/ppermute | solution.py:44
  173.3 2.0 collective-permute-start.24
  173.8 3.9 %collective-permute-start.25 = (f32[16,128]{1,0:T(8,128)}, f32[16,128]{1,0:T(8,128)S(1)}, u32[]{:S(2)}, u32[]{:S(2)}) collective-permute-start(f32[16,128]{1,0:T(8,128)} %get-tuple-element.37), channel_id=1, source_target_pairs={{0,2},{1,3},{2,0},{3,1},{4,6},{5,7},{6,4},{7,5},{8,10},{9,11},{10,... | collective-permute-start | bytes 24584 | tf_op jit(solution)/shard_map/ppermute | solution.py:117
  175.1 3.4 %collective-permute-start.26 = (f32[16,128]{1,0:T(8,128)}, f32[16,128]{1,0:T(8,128)S(1)}, u32[]{:S(2)}, u32[]{:S(2)}) collective-permute-start(f32[16,128]{1,0:T(8,128)} %get-tuple-element.37), channel_id=1, source_target_pairs={{0,3},{1,2},{2,1},{3,0},{4,7},{5,6},{6,5},{7,4},{8,11},{9,10},{10,... | collective-permute-start | bytes 24584 | tf_op jit(solution)/shard_map/ppermute | solution.py:117
  179.2 4.4 %collective-permute-start.27 = (f32[16,128]{1,0:T(8,128)S(1)}, f32[16,128]{1,0:T(8,128)S(1)}, u32[]{:S(2)}, u32[]{:S(2)}) collective-permute-start(f32[16,128]{1,0:T(8,128)S(1)} %add_add_fusion.1), channel_id=1, source_target_pairs={{0,4},{1,5},{2,6},{3,7},{4,0},{5,1},{6,2},{7,3},{8,12},{9,13},{10,... | collective-permute-start | bytes 24584 | tf_op jit(solution)/shard_map/ppermute | solution.py:117
  179.2 4.5 %collective-permute-start.28 = (f32[16,128]{1,0:T(8,128)S(1)}, f32[16,128]{1,0:T(8,128)S(1)}, u32[]{:S(2)}, u32[]{:S(2)}) collective-permute-start(f32[16,128]{1,0:T(8,128)S(1)} %add_add_fusion.1), channel_id=1, source_target_pairs={{0,8},{1,9},{2,10},{3,11},{4,12},{5,13},{6,14},{7,15},{8,0},{9,1},... | collective-permute-start | bytes 24584 | tf_op jit(solution)/shard_map/ppermute | solution.py:117
  180.8 5.4 %collective-permute-start.29 = (f32[16,128]{1,0:T(8,128)S(1)}, f32[16,128]{1,0:T(8,128)S(1)}, u32[]{:S(2)}, u32[]{:S(2)}) collective-permute-start(f32[16,128]{1,0:T(8,128)S(1)} %add_add_fusion.1), channel_id=1, source_target_pairs={{0,12},{1,13},{2,14},{3,15},{4,8},{5,9},{6,10},{7,11},{8,4},{9,5},... | collective-permute-start | bytes 24584 | tf_op jit(solution)/shard_map/ppermute | solution.py:117
  189.7 2.6 %collective-permute-start.31 = (bf16[32,64,128]{2,1,0:T(8,128)(2,1)}, bf16[32,64,128]{2,1,0:T(8,128)(2,1)S(1)}, u32[]{:S(2)}, u32[]{:S(2)}) collective-permute-start(bf16[32,64,128]{2,1,0:T(8,128)(2,1)} %get-tuple-element.38.refs_10_), channel_id=1, source_target_pairs={{0,1},{1,0},{2,3},{3,2},{4,5},{5,4},{6,7},{7,6},{8,9},{9,8},{10,11... | collective-permute-start | bytes 1572872 | tf_op jit(solution)/shard_map/ppermute | solution.py:44
  189.7 14.7 %collective-permute-start.30 = (bf16[32,64,128]{2,1,0:T(8,128)(2,1)}, bf16[32,64,128]{2,1,0:T(8,128)(2,1)}, u32[]{:S(2)}, u32[]{:S(2)}) collective-permute-start(bf16[32,64,128]{2,1,0:T(8,128)(2,1)} %get-tuple-element.38.refs_10_), channel_id=1, source_target_pairs={{0,4},{1,5},{2,0},{3,1},{4,8},{5,9},{6,2},{7,3},{8,12},{9,13},{10,... | collective-permute-start | bytes 1572872 | tf_op jit(solution)/shard_map/ppermute | solution.py:44
  189.7 14.7 %collective-permute-start.34 = (bf16[32,64,128]{2,1,0:T(8,128)(2,1)}, bf16[32,64,128]{2,1,0:T(8,128)(2,1)S(1)}, u32[]{:S(2)}, u32[]{:S(2)}) collective-permute-start(bf16[32,64,128]{2,1,0:T(8,128)(2,1)} %get-tuple-element.38.refs_10_), channel_id=1, source_target_pairs={{0,2},{1,3},{2,6},{3,7},{4,0},{5,1},{6,10},{7,11},{8,4},{9,5},{10,... | collective-permute-start | bytes 1572872 | tf_op jit(solution)/shard_map/ppermute | solution.py:44
  204.3 3.2 %collective-permute-start.33 = (bf16[32,64,128]{2,1,0:T(8,128)(2,1)}, bf16[32,64,128]{2,1,0:T(8,128)(2,1)S(1)}, u32[]{:S(2)}, u32[]{:S(2)}) collective-permute-start(bf16[32,64,128]{2,1,0:T(8,128)(2,1)} %shard_map.80.refs_10_), channel_id=1, source_target_pairs={{0,1},{1,0},{2,3},{3,2},{4,5},{5,4},{6,7},{7,6},{8,9},{9,8},{10,11... | collective-permute-start | bytes 1572872 | tf_op jit(solution)/shard_map/ppermute | solution.py:44
  204.3 3.2 %collective-permute-start.35 = (bf16[32,64,128]{2,1,0:T(8,128)(2,1)S(1)}, bf16[32,64,128]{2,1,0:T(8,128)(2,1)S(1)}, u32[]{:S(2)}, u32[]{:S(2)}) collective-permute-start(bf16[32,64,128]{2,1,0:T(8,128)(2,1)S(1)} %collective-permute-done.34.refs_12_), channel_id=1, source_target_pairs={{0,1},{1,0},{2,3},{3,2},{4,5},{5,4},{6,7},{7,6},{8,9},{9,8},{10,11... | collective-permute-start | bytes 1572872 | tf_op jit(solution)/shard_map/ppermute | solution.py:44
  204.8 14.3 %collective-permute-start.32 = (bf16[32,64,128]{2,1,0:T(8,128)(2,1)}, bf16[32,64,128]{2,1,0:T(8,128)(2,1)}, u32[]{:S(2)}, u32[]{:S(2)}) collective-permute-start(bf16[32,64,128]{2,1,0:T(8,128)(2,1)} %shard_map.80.refs_10_), channel_id=1, source_target_pairs={{0,4},{1,5},{2,0},{3,1},{4,8},{5,9},{6,2},{7,3},{8,12},{9,13},{10,... | collective-permute-start | bytes 1572872 | tf_op jit(solution)/shard_map/ppermute | solution.py:44
  206.7 14.1 %collective-permute-start.38 = (bf16[32,64,128]{2,1,0:T(8,128)(2,1)S(1)}, bf16[32,64,128]{2,1,0:T(8,128)(2,1)S(1)}, u32[]{:S(2)}, u32[]{:S(2)}) collective-permute-start(bf16[32,64,128]{2,1,0:T(8,128)(2,1)S(1)} %collective-permute-done.34.refs_12_), channel_id=1, source_target_pairs={{0,2},{1,3},{2,6},{3,7},{4,0},{5,1},{6,10},{7,11},{8,4},{9,5},{10,... | collective-permute-start | bytes 1572872 | tf_op jit(solution)/shard_map/ppermute | solution.py:44
  219.1 4.3 %collective-permute-start.37 = (bf16[32,64,128]{2,1,0:T(8,128)(2,1)}, bf16[32,64,128]{2,1,0:T(8,128)(2,1)S(1)}, u32[]{:S(2)}, u32[]{:S(2)}) collective-permute-start(bf16[32,64,128]{2,1,0:T(8,128)(2,1)} %shard_map.82.refs_10_), channel_id=1, source_target_pairs={{0,1},{1,0},{2,3},{3,2},{4,5},{5,4},{6,7},{7,6},{8,9},{9,8},{10,11... | collective-permute-start | bytes 1572872 | tf_op jit(solution)/shard_map/ppermute | solution.py:44
  220.8 2.6 %collective-permute-start.39 = (bf16[32,64,128]{2,1,0:T(8,128)(2,1)S(1)}, bf16[32,64,128]{2,1,0:T(8,128)(2,1)S(1)}, u32[]{:S(2)}, u32[]{:S(2)}) collective-permute-start(bf16[32,64,128]{2,1,0:T(8,128)(2,1)S(1)} %collective-permute-done.38.refs_12_), channel_id=1, source_target_pairs={{0,1},{1,0},{2,3},{3,2},{4,5},{5,4},{6,7},{7,6},{8,9},{9,8},{10,11... | collective-permute-start | bytes 1572872 | tf_op jit(solution)/shard_map/ppermute | solution.py:44
  220.8 14.5 %collective-permute-start.36 = (bf16[32,64,128]{2,1,0:T(8,128)(2,1)}, bf16[32,64,128]{2,1,0:T(8,128)(2,1)S(1)}, u32[]{:S(2)}, u32[]{:S(2)}) collective-permute-start(bf16[32,64,128]{2,1,0:T(8,128)(2,1)} %shard_map.82.refs_10_), channel_id=1, source_target_pairs={{0,4},{1,5},{2,0},{3,1},{4,8},{5,9},{6,2},{7,3},{8,12},{9,13},{10,... | collective-permute-start | bytes 1572872 | tf_op jit(solution)/shard_map/ppermute | solution.py:44
  223.1 14.1 %collective-permute-start.40 = (bf16[32,64,128]{2,1,0:T(8,128)(2,1)S(1)}, bf16[32,64,128]{2,1,0:T(8,128)(2,1)S(1)}, u32[]{:S(2)}, u32[]{:S(2)}) collective-permute-start(bf16[32,64,128]{2,1,0:T(8,128)(2,1)S(1)} %collective-permute-done.38.refs_12_), channel_id=1, source_target_pairs={{0,2},{1,3},{2,6},{3,7},{4,0},{5,1},{6,10},{7,11},{8,4},{9,5},{10,... | collective-permute-start | bytes 1572872 | tf_op jit(solution)/shard_map/ppermute | solution.py:44
  236.1 5.3 %collective-permute-start.42 = (bf16[32,64,128]{2,1,0:T(8,128)(2,1)}, bf16[32,64,128]{2,1,0:T(8,128)(2,1)S(1)}, u32[]{:S(2)}, u32[]{:S(2)}) collective-permute-start(bf16[32,64,128]{2,1,0:T(8,128)(2,1)} %shard_map.84.lower_ref.refs_10_), channel_id=1, source_target_pairs={{0,1},{1,0},{2,3},{3,2},{4,5},{5,4},{6,7},{7,6},{8,9},{9,8},{10,11... | collective-permute-start | bytes 1572872 | tf_op jit(solution)/shard_map/ppermute | solution.py:44
  237.1 4.3 %collective-permute-start.43 = (bf16[32,64,128]{2,1,0:T(8,128)(2,1)S(1)}, bf16[32,64,128]{2,1,0:T(8,128)(2,1)S(1)}, u32[]{:S(2)}, u32[]{:S(2)}) collective-permute-start(bf16[32,64,128]{2,1,0:T(8,128)(2,1)S(1)} %collective-permute-done.40.upper_ref.refs_12_), channel_id=1, source_target_pairs={{0,1},{1,0},{2,3},{3,2},{4,5},{5,4},{6,7},{7,6},{8,9},{9,8},{10,11... | collective-permute-start | bytes 1572872 | tf_op jit(solution)/shard_map/ppermute | solution.py:44
  240.1 9.7 %collective-permute-start.41 = (bf16[32,64,128]{2,1,0:T(8,128)(2,1)}, bf16[32,64,128]{2,1,0:T(8,128)(2,1)S(1)}, u32[]{:S(2)}, u32[]{:S(2)}) collective-permute-start(bf16[32,64,128]{2,1,0:T(8,128)(2,1)} %shard_map.85), channel_id=1, source_target_pairs={{0,4},{1,3},{2,0},{3,7},{4,8},{5,1},{6,2},{7,11},{8,12},{9,5},{10,... | collective-permute-start | bytes 1572872 | tf_op jit(solution)/shard_map/ppermute | solution.py:44
  250.7 2.1 collective-permute-start.44
  (34 other events, 99.1 us)

commit v10 on v9

--- a/solution.py
+++ b/solution.py
@@ -223,7 +223,7 @@
         )
 
 
-def local_stats(total, wave_ref, device, stats_ref):
+def local_residual(total, wave_ref, device, rest_ref, stats_ref):
     blocks = wave_ref.shape[0]
     zero = jnp.zeros(wave_ref.shape[1:], jnp.float32)
 
@@ -238,6 +238,7 @@
 
     def squares(block, carry):
         rest = total[block] - local * wave_ref[block].astype(jnp.float32)
+        rest_ref[block] = rest.astype(rest_ref.dtype)
         return carry + rest * rest
 
     about = jnp.sum(lax.fori_loop(0, blocks, squares, zero, unroll=4), keepdims=True)
@@ -247,6 +248,18 @@
     stats_ref[...] = jnp.where((row == device) & (lane < 4), values, 0.0)
 
 
+def form_direction(vector, wave, scale, chip):
+    factor = scale[0, 1]
+    for part in range(2):
+        shift = scale[2 * chip + part, 0]
+
+        @pl.loop(0, vector.shape[1], unroll=4)
+        def _(block):
+            rest = vector[part, block].astype(jnp.float32)
+            rest = rest + shift * wave[part, block].astype(jnp.float32)
+            vector[part, block] = (rest * factor).astype(vector.dtype)
+
+
 def apply_kernel(sources, choices, first, end, terms, capacity, ids_ref, *refs):
     refs = list(refs)
 
@@ -254,16 +267,18 @@
         taken, refs[:count] = refs[:count], []
         return taken
 
+    (scale,) = take(1) if choices else (None,)
     lefts = take(choices or sources)
     rights = take(2)
     vectors = [take(2) for _ in range(sources)]
+    waves = [take(2) for _ in range(choices)]
     (wave_in,) = take(1) if end == "stats" else (None,)
     (total_in,) = (None,) if first else take(1)
     (total_out,) = (None,) if end == "result" else take(1)
     (last_out,) = take(1)
     total, left, right, vector, raw, spread_labels, labels = take(7)
     left_sems, right_sems, vector_sems, raw_sems, label_sem, total_sem = take(6)
-    (wave, wave_sem) = take(2) if end == "stats" else (None, None)
+    wave, wave_sems = take(2) if choices or end == "stats" else (None, None)
     half = ids_ref[0]
     blocks = vector.shape[2]
     parts = left.shape[1]
@@ -286,6 +301,16 @@
             for part in range(2)
         ]
 
+    def wave_copies(source, pair):
+        return [
+            pltpu.make_async_copy(
+                pair[part],
+                wave.at[source, half if part == 0 else 1 - half],
+                wave_sems.at[source, part],
+            )
+            for part in range(2)
+        ]
+
     def right_copy(side):
         return pltpu.make_async_copy(rights[side], right.at[side], right_sems.at[side])
 
@@ -295,7 +320,7 @@
 
                 @pl.when(ids_ref[2 + source] == choice)
                 def _():
-                    for copy in left_copies(source, piece):
+                    for copy in left_copies(source, piece) + wave_copies(source, waves[choice]):
                         copy.start()
 
         else:
@@ -313,7 +338,7 @@
         load_total = pltpu.make_async_copy(total_in, total, total_sem)
         load_total.start()
     if end == "stats":
-        load_wave = pltpu.make_async_copy(wave_in, wave, wave_sem)
+        load_wave = pltpu.make_async_copy(wave_in, wave.at[0, 0], wave_sems.at[0, 0])
         load_wave.start()
     if end == "go on":
         last_out[...] = jnp.zeros_like(last_out)
@@ -333,6 +358,11 @@
                 left_copies(source, lefts[0])[1].wait()
                 for copy in vector_copies(source):
                     copy.wait()
+                if choices:
+                    for copy in wave_copies(source, waves[0]):
+                        copy.wait()
+                    chip = lax.div(ids_ref[1], 2) ^ ids_ref[2 + source]
+                    form_direction(vector.at[source], wave.at[source], scale, chip)
             add_products(
                 left.at[source],
                 labels.at[source],
@@ -345,22 +375,22 @@
             )
     if end == "result":
         last_out[...] = total[:blocks].astype(last_out.dtype)
+    elif end == "stats":
+        load_wave.wait()
+        local_residual(total, wave.at[0, 0], ids_ref[1], total_out, last_out)
     else:
         store_total = pltpu.make_async_copy(total, total_out, total_sem)
         store_total.start()
-        if end == "stats":
-            load_wave.wait()
-            local_stats(total, wave, ids_ref[1], last_out)
         store_total.wait()
 
 
-def apply_group(ids, lefts, rights, vectors, total, end, wave=None):
+def apply_group(ids, lefts, rights, vectors, total, end, wave=None, waves=(), scale=None):
     blocks, rows, width = vectors[0][0].shape
     terms = rights[0].shape[0]
     parts = lefts[0].shape[0] - 1
     capacity = parts * PART // (2 * terms * rows)
     sources, first = len(vectors), total is None
-    arrays = [*lefts, *rights] + [unit for pair in vectors for unit in pair]
+    arrays = [*lefts, *rights] + [unit for pair in [*vectors, *waves] for unit in pair]
     arrays += [wave] if end == "stats" else []
     arrays += [] if first else [total]
     whole = pl.BlockSpec(memory_space=pltpu.VMEM)
@@ -381,59 +411,61 @@
         pltpu.SemaphoreType.DMA,
         pltpu.SemaphoreType.DMA,
     ]
-    if end == "stats":
-        scratch += [pltpu.VMEM(wave.shape, wave.dtype), pltpu.SemaphoreType.DMA]
+    if waves or end == "stats":
+        scratch += [
+            pltpu.VMEM((sources, 2, blocks, rows, width), jnp.bfloat16),
+            pltpu.SemaphoreType.DMA((sources, 2)),
+        ]
     devices = lax.axis_size("sec") * lax.axis_size("term")
     total_out = jax.ShapeDtypeStruct(total_shape, jnp.float32)
     out_shape, out_specs = {
         "go on": ((total_out, jax.ShapeDtypeStruct((8, width), jnp.float32)), (anywhere, whole)),
         "stats": (
-            (total_out, jax.ShapeDtypeStruct((devices, 128), jnp.float32)),
-            (anywhere, whole),
+            (
+                jax.ShapeDtypeStruct((blocks, rows, width), jnp.bfloat16),
+                jax.ShapeDtypeStruct((devices, 128), jnp.float32),
+            ),
+            (whole, whole),
         ),
         "result": (jax.ShapeDtypeStruct((blocks, rows, width), jnp.bfloat16), whole),
     }[end]
-    choices = len(lefts) if ids.shape[0] > 2 else 0
+    choices = len(waves)
+    scalars = [ids] if scale is None else [ids, scale]
     return pl.pallas_call(
         functools.partial(apply_kernel, sources, choices, first, end, terms, capacity),
         out_shape=out_shape,
-        in_specs=[pl.BlockSpec(memory_space=pltpu.SMEM)] + [anywhere] * len(arrays),
+        in_specs=[pl.BlockSpec(memory_space=pltpu.SMEM)] * len(scalars) + [anywhere] * len(arrays),
         out_specs=out_specs,
         scratch_shapes=scratch,
         compiler_params=pltpu.CompilerParams(vmem_limit_bytes=VMEM_LIMIT),
-        cost_estimate=busy(2.0 + 1.4 * sources),
-    )(ids, *arrays)
-
-
-def direction_kernel(entries, total_ref, wave_ref, stats_ref, out_ref, rayleigh_ref):
-    blocks = wave_ref.shape[0]
+        cost_estimate=busy(3.5 + (2.7 if waves else 1.8) * sources),
+    )(*scalars, *arrays)
+
+
+def scale_kernel(entries, stats_ref, scale_ref, rayleigh_ref):
     stats = stats_ref[...]
     about, cross, own, local = (stats[:, lane : lane + 1] for lane in range(4))
     rayleigh = jnp.sum(cross, keepdims=True) / jnp.sum(own, keepdims=True)
     offset = local - rayleigh
     residual_sq = jnp.sum(about + offset * offset * own, keepdims=True)
     factor = lax.rsqrt(residual_sq / entries + 1e-06)
+    lane = lax.broadcasted_iota(jnp.int32, scale_ref.shape, 1)
+    scale_ref[...] = jnp.where(lane == 0, offset, factor)
     rayleigh_ref[...] = rayleigh
 
-    @pl.loop(0, blocks, unroll=4)
-    def _(block):
-        rest = total_ref[block] - rayleigh * wave_ref[block].astype(jnp.float32)
-        out_ref[block] = (rest * factor).astype(jnp.bfloat16)
-
-
-def new_direction(total, wave, stats, entries):
+
+def scales(stats, entries):
     whole = pl.BlockSpec(memory_space=pltpu.VMEM)
     return pl.pallas_call(
-        functools.partial(direction_kernel, entries),
+        functools.partial(scale_kernel, entries),
         out_shape=(
-            jax.ShapeDtypeStruct(wave.shape, jnp.bfloat16),
+            jax.ShapeDtypeStruct(stats.shape, jnp.float32),
             jax.ShapeDtypeStruct((1, 1), jnp.float32),
         ),
-        in_specs=[whole] * 3,
+        in_specs=[whole],
         out_specs=(whole, whole),
-        compiler_params=pltpu.CompilerParams(vmem_limit_bytes=VMEM_LIMIT),
-        cost_estimate=busy(2.0),
-    )(total, wave, stats)
+        cost_estimate=busy(0.7),
+    )(stats)
 
 
 def per_device_ring(wavefunction, left_operator, right_operator, target_owner, target_local):
@@ -487,30 +519,34 @@
             own_rows,
         )
 
+    rest = total
     entries = blocks * owners * height * width
-    stats = spread(stats, owners * halves)
-    direction, rayleigh = new_direction(total, own_rows, stats, entries)
+    scale, rayleigh = scales(spread(stats, owners * halves), entries)
     reach = (owners - 1) // 2
-
-    def add_group(total, units, last):
+    waves = [(near[m], far[m]) for m in range(owners)]
+
+    def add_group(total, units, end):
         choices = [me ^ ring_owner(place - s, owners) for s in units]
         vectors = [(unit, swap(unit, owners, halves)) for unit in units.values()]
         ids = jnp.stack(here + choices).astype(jnp.int32)
-        return apply_group(ids, lefts, rights, vectors, total, "result" if last else "go on")
-
-    ahead = behind = direction
-    units = {0: direction}
-    total = None
+        return apply_group(
+            ids, lefts, rights, vectors, total, end, waves=waves, scale=scale
+        )
+
+    total = token = None
+    ready = [{0: rest}]
+    ahead = behind = rest
     for step in range(1, reach + 1):
-        ahead_next = ring_send(ahead, owners, halves, (1,) * halves)
-        behind_next = ring_send(behind, owners, halves, (-1,) * halves)
-        total, token = add_group(total, units, False)
-        ahead, behind = after(ahead_next, token), behind_next
-        units = {step: ahead, -step: behind}
-    last = select_half(half, ahead, behind)
-    last = ring_send(last, owners, halves, (1, -1))
-    total, token = add_group(total, units, False)
-    total = add_group(total, {owners // 2: after(last, token)}, True)
+        ahead = ring_send(ahead, owners, halves, (1,) * halves)
+        behind = ring_send(behind, owners, halves, (-1,) * halves)
+        if step > 1:
+            total, token = add_group(total, ready.pop(0), "go on")
+            ahead = after(ahead, token)
+        ready.append({step: ahead, -step: behind})
+    last = ring_send(select_half(half, ahead, behind), owners, halves, (1, -1))
+    total, token = add_group(total, ready.pop(0), "go on")
+    last = after(last, token)
+    total = add_group(total, {**ready.pop(0), owners // 2: last}, "result")
     return (total, rayleigh[0])
 
 

time: 260 us -> 238 us (0.915)
  waiting for transfers between devices: 129 us -> 112 us
    ppermute x39, waiting for transfers between devices: 123 us -> 97.2 us  [permute(): return lax.ppermute(value, BOTH, pairs)]
    ppermute x6, waiting for transfers between devices: 5.94 us -> 14.8 us  [spread(): lax.ppermute(value, BOTH, [(d, d ^ m) for d in range(devices)])]
    unnamed x74 -> x72, local copies, waits for them, and re-layouts: 10.6 us -> 7.66 us
    pallas_call x9 -> x8, Pallas kernels: 61.7 us -> 63.2 us  [apply_group(): pl.pallas_call(functools.partial(apply_kernel, sources, choices, first, e...]
  transfers between devices with their start and end apart: 45 -> 45, of which waited for: 17 -> 14; matrix products, arithmetic and copies ran while one was open for 2% -> 3% of each run, Pallas kernels for 22% -> 23%
where the time goes in v10:
time: 238 us; the launch traced here: 237 us
  waiting for transfers between devices  112 us (47%)
  Pallas kernels  72.5 us (30%)
  starting transfers between devices  35.8 us (15%)
  local copies, waits for them, and re-layouts  10.8 us (5%)
  other arithmetic  4.41 us (2%)
    ppermute x39, waiting for transfers between devices, permute(): return lax.ppermute(value, BOTH, pairs)  97.2 us
    pallas_call x8, Pallas kernels, apply_group(): pl.pallas_call(functools.partial(apply_kernel, sources, choices, first, e...  63.2 us
    ppermute x39, starting transfers between devices, permute(): return lax.ppermute(value, BOTH, pairs)  31.1 us
    ppermute x6, waiting for transfers between devices, spread(): lax.ppermute(value, BOTH, [(d, d ^ m) for d in range(devices)])  14.8 us
    unnamed x72, local copies, waits for them, and re-layouts  7.66 us
    pallas_call x1, Pallas kernels, pack(): pl.pallas_call(functools.partial(pack_kernel, order, capacity, blocks, te...  5.45 us
  transfers between devices with their start and end apart: 45, of which 14 were waited for; matrix products, arithmetic and copies ran while one was open for 3% of the time, Pallas kernels for 23%

profile of v10, /device:TPU:0, one launch (start us, length us, event | category | flops | bytes accessed | tf_op | source)
XLA Modules:
  0.0 236.9 jit_solution(2539736196617004996)
XLA Ops:
  0.6 1.4 constant_dynamic-slice_fusion.2
  2.7 1.1 constant_dynamic-slice_fusion
  3.7 4.0 %collective-permute-start.9 = (bf16[32,64,128]{2,1,0:T(8,128)(2,1)}, bf16[32,64,128]{2,1,0:T(8,128)(2,1)S(1)}, u32[]{:S(2)}, u32[]{:S(2)}) collective-permute-start(bf16[32,64,128]{2,1,0:T(8,128)(2,1)} %get-tuple-element.45.refs_4_.refs_8_.refs_13_.refs_15_.refs_17_), channel_id=1, source_target_pairs={{0,8},{1,9},{2,10},{3,11},{4,12},{5,13},{6,14},{7,15},{8,0},{9,1},... | collective-permute-start | bytes 1572872 | tf_op jit(solution)/shard_map/ppermute | solution.py:44
  7.8 1.5 collective-permute-start.21
  11.1 1.0 copy-done.15
  12.1 5.5 %shard_map.68 = (bf16[129,16,128]{2,1,0:T(8,128)(2,1)}, bf16[129,16,128]{2,1,0:T(8,128)(2,1)}, bf16[129,16,128]{2,1,0:T(8,128)(2,1)}, bf16[129,16,128]{2,1,0:T(8...) custom-call(s32[2]{0:T(128)} %pad_add_fusion.2.ids_ref, ...), custom_call_target="tpu_custom_call" | custom-call | flops 5750000128 | tf_op jit(solution)/shard_map/pallas_call | solution.py:184
  18.1 1.6 collective-permute-start.6
  19.7 11.8 %collective-permute-done.9.refs_0_ = bf16[32,64,128]{2,1,0:T(8,128)(2,1)S(1)} collective-permute-done((bf16[32,64,128]{2,1,0:T(8,128)(2,1)}, bf16[32,64,128]{2,1,0:T(8,128)(2,1)S(1)}, u32[]{:S(2)}, u32[]{:S(2)}) %collective-permute-start.9) | collective-permute-done | bytes 524320 | tf_op jit(solution)/shard_map/ppermute | solution.py:44
  31.5 3.9 %collective-permute-start.3 = (bf16[129,16,128]{2,1,0:T(8,128)(2,1)}, bf16[129,16,128]{2,1,0:T(8,128)(2,1)S(1)}, u32[]{:S(2)}, u32[]{:S(2)}) collective-permute-start(bf16[129,16,128]{2,1,0:T(8,128)(2,1)} %get-tuple-element.25), channel_id=1, source_target_pairs={{0,10},{1,11},{2,8},{3,9},{4,14},{5,15},{6,12},{7,13},{8,2},{9,3},... | collective-permute-start | bytes 1585160 | tf_op jit(solution)/shard_map/ppermute | solution.py:44
  35.4 1.2 collective-permute-start.12
  36.6 7.5 %collective-permute-done.6.refs_0_ = bf16[32,64,128]{2,1,0:T(8,128)(2,1)S(1)} collective-permute-done((bf16[32,64,128]{2,1,0:T(8,128)(2,1)}, bf16[32,64,128]{2,1,0:T(8,128)(2,1)S(1)}, u32[]{:S(2)}, u32[]{:S(2)}) %collective-permute-start.6) | collective-permute-done | bytes 524320 | tf_op jit(solution)/shard_map/ppermute | solution.py:44
  44.1 26.1 %collective-permute-done.15.refs_1_.refs_5_ = bf16[129,16,128]{2,1,0:T(8,128)(2,1)S(1)} collective-permute-done((bf16[129,16,128]{2,1,0:T(8,128)(2,1)}, bf16[129,16,128]{2,1,0:T(8,128)(2,1)S(1)}, u32[]{:S(2)}, u32[]{:S(2)}) %collective-permute-start.15) | collective-permute-done | bytes 528416 | tf_op jit(solution)/shard_map/ppermute | solution.py:44
  70.3 10.5 %collective-permute-done.3.refs_1_.refs_0_.refs_6_ = bf16[129,16,128]{2,1,0:T(8,128)(2,1)S(1)} collective-permute-done((bf16[129,16,128]{2,1,0:T(8,128)(2,1)}, bf16[129,16,128]{2,1,0:T(8,128)(2,1)S(1)}, u32[]{:S(2)}, u32[]{:S(2)}) %collective-permute-start.3) | collective-permute-done | bytes 528416 | tf_op jit(solution)/shard_map/ppermute | solution.py:44
  80.8 0.8 collective-permute-start.19
  82.3 5.0 %collective-permute-done.11.refs_0_ = bf16[32,64,128]{2,1,0:T(8,128)(2,1)S(1)} collective-permute-done((bf16[32,64,128]{2,1,0:T(8,128)(2,1)}, bf16[32,64,128]{2,1,0:T(8,128)(2,1)S(1)}, u32[]{:S(2)}, u32[]{:S(2)}) %collective-permute-start.11) | collective-permute-done | bytes 524320 | tf_op jit(solution)/shard_map/ppermute | solution.py:44
  87.3 0.8 copy-done.9
  88.1 1.6 collective-permute-start.7
  89.7 3.4 %collective-permute-start.16 = (bf16[129,16,128]{2,1,0:T(8,128)(2,1)S(1)}, bf16[129,16,128]{2,1,0:T(8,128)(2,1)S(1)}, u32[]{:S(2)}, u32[]{:S(2)}) collective-permute-start(bf16[129,16,128]{2,1,0:T(8,128)(2,1)S(1)} %copy-done.5), channel_id=1, source_target_pairs={{0,12},{1,13},{2,14},{3,15},{4,8},{5,9},{6,10},{7,11},{8,4},{9,5},... | collective-permute-start | bytes 1585160 | tf_op jit(solution)/shard_map/ppermute | solution.py:44
  93.1 2.8 %collective-permute-done.19.refs_4_.refs_23_.refs_25_.refs_27_ = bf16[32,64,128]{2,1,0:T(8,128)(2,1)} collective-permute-done((bf16[32,64,128]{2,1,0:T(8,128)(2,1)}, bf16[32,64,128]{2,1,0:T(8,128)(2,1)}, u32[]{:S(2)}, u32[]{:S(2)}) %collective-permute-start.19) | collective-permute-done | bytes 524320 | tf_op jit(solution)/shard_map/ppermute | solution.py:44
  95.8 6.7 %shard_map.74 = (f32[33,64,128]{2,1,0:T(8,128)}, f32[8,128]{1,0:T(8,128)}) custom-call(s32[2]{0:T(128)} %pad_add_fusion.1.ids_ref, bf16[129,16,128]{2,1,0:T(8,128)(2,1)} %get-tuple-element.30.refs_0_.refs_1_, bf16[129,16,128]{2,1,0:T(8,128)(2,1)} %copy-done.3, bf16[2,32,128,128]{3,2,1,0:T(8,128)(2,1)} %refs_9_.7, ...), custom_call_target="tpu_custom_call" | custom-call | flops 8165000192 | tf_op jit(solution)/shard_map/pallas_call | solution.py:434
  103.9 7.5 %shard_map.75 = (f32[33,64,128]{2,1,0:T(8,128)}, f32[8,128]{1,0:T(8,128)}) custom-call(s32[2]{0:T(128)} %pad_add_fusion.1.ids_ref, bf16[129,16,128]{2,1,0:T(8,128)(2,1)} %copy-done, bf16[129,16,128]{2,1,0:T(8,128)(2,1)} %copy-done.2, bf16[2,32,128,128]{3,2,1,0:T(8,128)(2,1)} %refs_9_.7, bf16[2,32,128,128]{3,2,1,0:T(8,128)(2,1)} %collective-permute-done.5.refs_3_.refs_10_, ...), custom_call_target="tpu_custom_call" | custom-call | flops 8165000192 | tf_op jit(solution)/shard_map/pallas_call | solution.py:434
  111.5 1.9 collective-permute-start.4
  113.5 15.0 %collective-permute-done.13.refs_6_.refs_27_.refs_29_.refs_31_ = bf16[32,64,128]{2,1,0:T(8,128)(2,1)} collective-permute-done((bf16[32,64,128]{2,1,0:T(8,128)(2,1)S(1)}, bf16[32,64,128]{2,1,0:T(8,128)(2,1)}, u32[]{:S(2)}, u32[]{:S(2)}) %collective-permute-start.13) | collective-permute-done | bytes 524320 | tf_op jit(solution)/shard_map/ppermute | solution.py:44
  128.5 7.4 %shard_map.76 = (f32[33,64,128]{2,1,0:T(8,128)}, f32[8,128]{1,0:T(8,128)}) custom-call(s32[2]{0:T(128)} %pad_add_fusion.1.ids_ref, bf16[129,16,128]{2,1,0:T(8,128)(2,1)} %copy-done.4, bf16[129,16,128]{2,1,0:T(8,128)(2,1)} %copy-done.16, bf16[2,32,128,128]{3,2,1,0:T(8,128)(2,1)} %refs_9_.7, bf16[2,32,128,128]{3,2,1,0:T(8,128)(2,1)} %collective-permute-done.5.refs_3_.refs_10_, ...), custom_call_target="tpu_custom_call" | custom-call | flops 8165000192 | tf_op jit(solution)/shard_map/pallas_call | solution.py:434
  135.9 8.1 %collective-permute-done.4.refs_1_.refs_8_ = bf16[129,16,128]{2,1,0:T(8,128)(2,1)S(1)} collective-permute-done((bf16[129,16,128]{2,1,0:T(8,128)(2,1)S(1)}, bf16[129,16,128]{2,1,0:T(8,128)(2,1)S(1)}, u32[]{:S(2)}, u32[]{:S(2)}) %collective-permute-start.4) | collective-permute-done | bytes 528416 | tf_op jit(solution)/shard_map/ppermute | solution.py:44
  144.0 0.8 copy-done.18
  145.0 7.1 %shard_map.77 = (bf16[32,64,128]{2,1,0:T(8,128)(2,1)}, f32[16,128]{1,0:T(8,128)}) custom-call(s32[2]{0:T(128)} %pad_add_fusion.1.ids_ref, bf16[129,16,128]{2,1,0:T(8,128)(2,1)} %copy-done.17, bf16[129,16,128]{2,1,0:T(8,128)(2,1)} %copy-done.18, bf16[2,32,128,128]{3,2,1,0:T(8,128)(2,1)} %refs_9_.7, ...), custom_call_target="tpu_custom_call" | custom-call | flops 8165000192 | tf_op jit(solution)/shard_map/pallas_call | solution.py:434
  152.2 1.5 collective-permute-start.25
  155.1 2.9 %collective-permute-start.30 = (bf16[32,64,128]{2,1,0:T(8,128)(2,1)}, bf16[32,64,128]{2,1,0:T(8,128)(2,1)S(1)}, u32[]{:S(2)}, u32[]{:S(2)}) collective-permute-start(bf16[32,64,128]{2,1,0:T(8,128)(2,1)} %get-tuple-element.36.refs_11_), channel_id=1, source_target_pairs={{0,4},{1,5},{2,0},{3,1},{4,8},{5,9},{6,2},{7,3},{8,12},{9,13},{10,... | collective-permute-start | bytes 1572872 | tf_op jit(solution)/shard_map/ppermute | solution.py:44
  158.7 2.0 collective-permute-start.27
  161.9 10.4 %collective-permute-done.27 = f32[16,128]{1,0:T(8,128)S(1)} collective-permute-done((f32[16,128]{1,0:T(8,128)S(1)}, f32[16,128]{1,0:T(8,128)S(1)}, u32[]{:S(2)}, u32[]{:S(2)}) %collective-permute-start.27) | collective-permute-done | bytes 8224 | tf_op jit(solution)/shard_map/ppermute | solution.py:117
  173.2 4.5 %collective-permute-done.29 = f32[16,128]{1,0:T(8,128)S(1)} collective-permute-done((f32[16,128]{1,0:T(8,128)S(1)}, f32[16,128]{1,0:T(8,128)S(1)}, u32[]{:S(2)}, u32[]{:S(2)}) %collective-permute-start.29) | collective-permute-done | bytes 8224 | tf_op jit(solution)/shard_map/ppermute | solution.py:117
  178.3 1.7 shard_map.78
  180.5 1.7 collective-permute-start.38
  182.2 0.8 copy-done.30
  183.0 6.1 %shard_map.79 = (f32[33,64,128]{2,1,0:T(8,128)}, f32[8,128]{1,0:T(8,128)}) custom-call(s32[3]{0:T(128)} %pad_add_fusion.3.ids_ref, f32[16,128]{1,0:T(8,128)} %get-tuple-element.35.refs_0_, bf16[129,16,128]{2,1,0:T(8,128)(2,1)} %get-tuple-element.30.refs_0_.refs_1_, bf16[129,16,128]{2,1,0:T(8,128)(2,1)} %copy-done.2, bf16[129,16,128]{2,1,0:T(8,128)(2,1)} %copy-done.4, ...), custom_call_target="tpu_custom_call" | custom-call | flops 7129999872 | tf_op jit(solution)/shard_map/pallas_call | solution.py:434
  189.1 5.1 %collective-permute-done.31.refs_0_ = bf16[32,64,128]{2,1,0:T(8,128)(2,1)S(1)} collective-permute-done((bf16[32,64,128]{2,1,0:T(8,128)(2,1)S(1)}, bf16[32,64,128]{2,1,0:T(8,128)(2,1)S(1)}, u32[]{:S(2)}, u32[]{:S(2)}) %collective-permute-start.31) | collective-permute-done | bytes 524320 | tf_op jit(solution)/shard_map/ppermute | solution.py:44
  194.3 0.8 copy-done.34
  195.7 1.7 collective-permute-start.39
  197.4 9.1 %shard_map.81 = (f32[33,64,128]{2,1,0:T(8,128)}, f32[8,128]{1,0:T(8,128)}) custom-call(s32[4]{0:T(128)} %pad_add_fusion.4.ids_ref, f32[16,128]{1,0:T(8,128)} %get-tuple-element.35.refs_0_, bf16[129,16,128]{2,1,0:T(8,128)(2,1)} %get-tuple-element.30.refs_0_.refs_1_, bf16[129,16,128]{2,1,0:T(8,128)(2,1)} %copy-done.2, bf16[129,16,128]{2,1,0:T(8,128)(2,1)} %copy-done.4, ...), custom_call_target="tpu_custom_call" | custom-call | flops 10234999808 | tf_op jit(solution)/shard_map/pallas_call | solution.py:434
  206.5 3.3 %collective-permute-done.33.refs_0_ = bf16[32,64,128]{2,1,0:T(8,128)(2,1)} collective-permute-done((bf16[32,64,128]{2,1,0:T(8,128)(2,1)}, bf16[32,64,128]{2,1,0:T(8,128)(2,1)}, u32[]{:S(2)}, u32[]{:S(2)}) %collective-permute-start.33) | collective-permute-done | bytes 524320 | tf_op jit(solution)/shard_map/ppermute | solution.py:44
  209.8 0.8 copy-done.24
  210.6 2.1 shard_map.83
  213.6 0.8 copy-done.32
  214.4 9.0 %shard_map.84 = (f32[33,64,128]{2,1,0:T(8,128)}, f32[8,128]{1,0:T(8,128)}) custom-call(s32[4]{0:T(128)} %pad_add_fusion.6.ids_ref, f32[16,128]{1,0:T(8,128)} %get-tuple-element.35.refs_0_, bf16[129,16,128]{2,1,0:T(8,128)(2,1)} %get-tuple-element.30.refs_0_.refs_1_, bf16[129,16,128]{2,1,0:T(8,128)(2,1)} %copy-done.2, bf16[129,16,128]{2,1,0:T(8,128)(2,1)} %copy-done.4, ...), custom_call_target="tpu_custom_call" | custom-call | flops 10234999808 | tf_op jit(solution)/shard_map/pallas_call | solution.py:434
  224.3 1.3 collective-permute-done.44.refs_16_
  225.6 0.8 copy-done.29
  226.4 10.3 %shard_map.86 = bf16[32,64,128]{2,1,0:T(8,128)(2,1)} custom-call(s32[5]{0:T(128)} %stack.71.ids_ref, f32[16,128]{1,0:T(8,128)} %get-tuple-element.35.refs_0_, bf16[129,16,128]{2,1,0:T(8,128)(2,1)} %get-tuple-element.30.refs_0_.refs_1_, bf16[129,16,128]{2,1,0:T(8,128)(2,1)} %copy-done.2, bf16[129,16,128]{2,1,0:T(8,128)(2,1)} %copy-done.4, ...), custom_call_target="tpu_custom_call" | custom-call | flops 13340000256 | tf_op jit(solution)/shard_map/pallas_call | solution.py:434
  (144 shorter events, 13.1 us)
Async XLA Ops:
  2.1 8.5 %collective-permute-start.1 = (bf16[2,32,64,128]{3,2,1,0:T(8,128)(2,1)S(1)}, bf16[2,32,64,128]{3,2,1,0:T(8,128)(2,1)S(1)}, u32[]{:S(2)}, u32[]{:S(2)}) collective-permute-start(bf16[2,32,64,128]{3,2,1,0:T(8,128)(2,1)S(1)} %constant_dynamic-slice_fusion.2), channel_id=1, source_target_pairs={{0,1},{1,0},{2,3},{3,2},{4,5},{5,4},{6,7},{7,6},{8,9},{9,8},{10,11... | collective-permute-start | bytes 3145736 | tf_op jit(solution)/shard_map/ppermute | solution.py:44
  2.6 85.5 %collective-permute-start.5 = (bf16[2,32,128,128]{3,2,1,0:T(8,128)(2,1)}, bf16[2,32,128,128]{3,2,1,0:T(8,128)(2,1)}, u32[]{:S(2)}, u32[]{:S(2)}) collective-permute-start(bf16[2,32,128,128]{3,2,1,0:T(8,128)(2,1)} %refs_9_.7), channel_id=1, source_target_pairs={{0,1},{1,0},{2,3},{3,2},{4,5},{5,4},{6,7},{7,6},{8,9},{9,8},{10,11... | collective-permute-start | bytes 6291464 | tf_op jit(solution)/shard_map/ppermute | solution.py:44
  3.7 27.7 %collective-permute-start.9 = (bf16[32,64,128]{2,1,0:T(8,128)(2,1)}, bf16[32,64,128]{2,1,0:T(8,128)(2,1)S(1)}, u32[]{:S(2)}, u32[]{:S(2)}) collective-permute-start(bf16[32,64,128]{2,1,0:T(8,128)(2,1)} %get-tuple-element.45.refs_4_.refs_8_.refs_13_.refs_15_.refs_17_), channel_id=1, source_target_pairs={{0,8},{1,9},{2,10},{3,11},{4,12},{5,13},{6,14},{7,15},{8,0},{9,1},... | collective-permute-start | bytes 1572872 | tf_op jit(solution)/shard_map/ppermute | solution.py:44
  7.8 23.7 %collective-permute-start.21 = (bf16[32,64,128]{2,1,0:T(8,128)(2,1)}, bf16[32,64,128]{2,1,0:T(8,128)(2,1)}, u32[]{:S(2)}, u32[]{:S(2)}) collective-permute-start(bf16[32,64,128]{2,1,0:T(8,128)(2,1)} %get-tuple-element.45.refs_4_.refs_8_.refs_13_.refs_15_.refs_17_), channel_id=1, source_target_pairs={{0,2},{1,3},{2,0},{3,1},{4,6},{5,7},{6,4},{7,5},{8,10},{9,11},{10,... | collective-permute-start | bytes 1572872 | tf_op jit(solution)/shard_map/ppermute | solution.py:44
  9.3 1.2 collective-permute-start
  17.5 17.9 %collective-permute-start.10 = (bf16[129,16,128]{2,1,0:T(8,128)(2,1)}, bf16[129,16,128]{2,1,0:T(8,128)(2,1)S(1)}, u32[]{:S(2)}, u32[]{:S(2)}) collective-permute-start(bf16[129,16,128]{2,1,0:T(8,128)(2,1)} %get-tuple-element.26), channel_id=1, source_target_pairs={{0,2},{1,3},{2,0},{3,1},{4,6},{5,7},{6,4},{7,5},{8,10},{9,11},{10,... | collective-permute-start | bytes 1585160 | tf_op jit(solution)/shard_map/ppermute | solution.py:44
  18.1 26.0 %collective-permute-start.6 = (bf16[32,64,128]{2,1,0:T(8,128)(2,1)}, bf16[32,64,128]{2,1,0:T(8,128)(2,1)S(1)}, u32[]{:S(2)}, u32[]{:S(2)}) collective-permute-start(bf16[32,64,128]{2,1,0:T(8,128)(2,1)} %get-tuple-element.45.refs_4_.refs_8_.refs_13_.refs_15_.refs_17_), channel_id=1, source_target_pairs={{0,4},{1,5},{2,6},{3,7},{4,0},{5,1},{6,2},{7,3},{8,12},{9,13},{10,... | collective-permute-start | bytes 1572872 | tf_op jit(solution)/shard_map/ppermute | solution.py:44
  31.5 38.8 %collective-permute-start.15 = (bf16[129,16,128]{2,1,0:T(8,128)(2,1)}, bf16[129,16,128]{2,1,0:T(8,128)(2,1)S(1)}, u32[]{:S(2)}, u32[]{:S(2)}) collective-permute-start(bf16[129,16,128]{2,1,0:T(8,128)(2,1)} %get-tuple-element.29), channel_id=1, source_target_pairs={{0,8},{1,9},{2,10},{3,11},{4,12},{5,13},{6,14},{7,15},{8,0},{9,1},... | collective-permute-start | bytes 1585160 | tf_op jit(solution)/shard_map/ppermute | solution.py:44
  31.5 49.3 %collective-permute-start.3 = (bf16[129,16,128]{2,1,0:T(8,128)(2,1)}, bf16[129,16,128]{2,1,0:T(8,128)(2,1)S(1)}, u32[]{:S(2)}, u32[]{:S(2)}) collective-permute-start(bf16[129,16,128]{2,1,0:T(8,128)(2,1)} %get-tuple-element.25), channel_id=1, source_target_pairs={{0,10},{1,11},{2,8},{3,9},{4,14},{5,15},{6,12},{7,13},{8,2},{9,3},... | collective-permute-start | bytes 1585160 | tf_op jit(solution)/shard_map/ppermute | solution.py:44
  35.4 46.8 %collective-permute-start.12 = (bf16[129,16,128]{2,1,0:T(8,128)(2,1)}, bf16[129,16,128]{2,1,0:T(8,128)(2,1)S(1)}, u32[]{:S(2)}, u32[]{:S(2)}) collective-permute-start(bf16[129,16,128]{2,1,0:T(8,128)(2,1)} %get-tuple-element.27), channel_id=1, source_target_pairs={{0,4},{1,5},{2,6},{3,7},{4,0},{5,1},{6,2},{7,3},{8,12},{9,13},{10,... | collective-permute-start | bytes 1585160 | tf_op jit(solution)/shard_map/ppermute | solution.py:44
  44.1 38.0 %copy-start.7 = (bf16[32,64,128]{2,1,0:T(8,128)(2,1)}, bf16[32,64,128]{2,1,0:T(8,128)(2,1)S(1)}, u32[]{:S(2)}) copy-start(bf16[32,64,128]{2,1,0:T(8,128)(2,1)S(1)} %collective-permute-done.6.refs_0_) | copy-start | bytes 1572868
  44.1 43.2 %collective-permute-start.11 = (bf16[32,64,128]{2,1,0:T(8,128)(2,1)}, bf16[32,64,128]{2,1,0:T(8,128)(2,1)S(1)}, u32[]{:S(2)}, u32[]{:S(2)}) collective-permute-start(bf16[32,64,128]{2,1,0:T(8,128)(2,1)} %shard_map.71.refs_6_.refs_21_.refs_23_.refs_25_), channel_id=1, source_target_pairs={{0,4},{1,5},{2,6},{3,7},{4,0},{5,1},{6,2},{7,3},{8,12},{9,13},{10,... | collective-permute-start | bytes 1572872 | tf_op jit(solution)/shard_map/ppermute | solution.py:44
  70.3 11.9 %copy-start.3 = (bf16[129,16,128]{2,1,0:T(8,128)(2,1)}, bf16[129,16,128]{2,1,0:T(8,128)(2,1)S(1)}, u32[]{:S(2)}) copy-start(bf16[129,16,128]{2,1,0:T(8,128)(2,1)S(1)} %collective-permute-done.15.refs_1_.refs_5_) | copy-start | bytes 1585156
  70.3 19.4 %collective-permute-start.23 = (bf16[32,64,128]{2,1,0:T(8,128)(2,1)}, bf16[32,64,128]{2,1,0:T(8,128)(2,1)S(1)}, u32[]{:S(2)}, u32[]{:S(2)}) collective-permute-start(bf16[32,64,128]{2,1,0:T(8,128)(2,1)} %shard_map.71.refs_6_.refs_21_.refs_23_.refs_25_), channel_id=1, source_target_pairs={{0,1},{1,0},{2,3},{3,2},{4,5},{5,4},{6,7},{7,6},{8,9},{9,8},{10,11... | collective-permute-start | bytes 1572872 | tf_op jit(solution)/shard_map/ppermute | solution.py:44
  80.8 15.0 %collective-permute-start.19 = (bf16[32,64,128]{2,1,0:T(8,128)(2,1)}, bf16[32,64,128]{2,1,0:T(8,128)(2,1)}, u32[]{:S(2)}, u32[]{:S(2)}) collective-permute-start(bf16[32,64,128]{2,1,0:T(8,128)(2,1)} %shard_map.71.refs_6_.refs_21_.refs_23_.refs_25_), channel_id=1, source_target_pairs={{0,2},{1,3},{2,0},{3,1},{4,6},{5,7},{6,4},{7,5},{8,10},{9,11},{10,... | collective-permute-start | bytes 1572872 | tf_op jit(solution)/shard_map/ppermute | solution.py:44
  82.2 20.3 %collective-permute-start.22 = (bf16[32,64,128]{2,1,0:T(8,128)(2,1)}, bf16[32,64,128]{2,1,0:T(8,128)(2,1)S(1)}, u32[]{:S(2)}, u32[]{:S(2)}) collective-permute-start(bf16[32,64,128]{2,1,0:T(8,128)(2,1)} %collective-permute-done.21.refs_6_.refs_15_.refs_17_.refs_19_), channel_id=1, source_target_pairs={{0,1},{1,0},{2,3},{3,2},{4,5},{5,4},{6,7},{7,6},{8,9},{9,8},{10,11... | collective-permute-start | bytes 1572872 | tf_op jit(solution)/shard_map/ppermute | solution.py:44
  87.3 24.1 %collective-permute-start.17 = (bf16[32,64,128]{2,1,0:T(8,128)(2,1)S(1)}, bf16[32,64,128]{2,1,0:T(8,128)(2,1)}, u32[]{:S(2)}, u32[]{:S(2)}) collective-permute-start(bf16[32,64,128]{2,1,0:T(8,128)(2,1)S(1)} %copy-done.8), channel_id=1, source_target_pairs={{0,1},{1,0},{2,3},{3,2},{4,5},{5,4},{6,7},{7,6},{8,9},{9,8},{10,11... | collective-permute-start | bytes 1572872 | tf_op jit(solution)/shard_map/ppermute | solution.py:44
  88.1 23.4 %collective-permute-start.7 = (bf16[32,64,128]{2,1,0:T(8,128)(2,1)S(1)}, bf16[32,64,128]{2,1,0:T(8,128)(2,1)}, u32[]{:S(2)}, u32[]{:S(2)}) collective-permute-start(bf16[32,64,128]{2,1,0:T(8,128)(2,1)S(1)} %copy-done.8), channel_id=1, source_target_pairs={{0,2},{1,3},{2,0},{3,1},{4,6},{5,7},{6,4},{7,5},{8,10},{9,11},{10,... | collective-permute-start | bytes 1572872 | tf_op jit(solution)/shard_map/ppermute | solution.py:44
  89.7 23.8 %collective-permute-start.16 = (bf16[129,16,128]{2,1,0:T(8,128)(2,1)S(1)}, bf16[129,16,128]{2,1,0:T(8,128)(2,1)S(1)}, u32[]{:S(2)}, u32[]{:S(2)}) collective-permute-start(bf16[129,16,128]{2,1,0:T(8,128)(2,1)S(1)} %copy-done.5), channel_id=1, source_target_pairs={{0,12},{1,13},{2,14},{3,15},{4,8},{5,9},{6,10},{7,11},{8,4},{9,5},... | collective-permute-start | bytes 1585160 | tf_op jit(solution)/shard_map/ppermute | solution.py:44
  95.8 7.3 %collective-permute-start.20 = (bf16[32,64,128]{2,1,0:T(8,128)(2,1)}, bf16[32,64,128]{2,1,0:T(8,128)(2,1)S(1)}, u32[]{:S(2)}, u32[]{:S(2)}) collective-permute-start(bf16[32,64,128]{2,1,0:T(8,128)(2,1)} %collective-permute-done.19.refs_4_.refs_23_.refs_25_.refs_27_), channel_id=1, source_target_pairs={{0,1},{1,0},{2,3},{3,2},{4,5},{5,4},{6,7},{7,6},{8,9},{9,8},{10,11... | collective-permute-start | bytes 1572872 | tf_op jit(solution)/shard_map/ppermute | solution.py:44
  102.6 25.9 %collective-permute-start.18 = (bf16[32,64,128]{2,1,0:T(8,128)(2,1)S(1)}, bf16[32,64,128]{2,1,0:T(8,128)(2,1)}, u32[]{:S(2)}, u32[]{:S(2)}) collective-permute-start(bf16[32,64,128]{2,1,0:T(8,128)(2,1)S(1)} %copy-done.10), channel_id=1, source_target_pairs={{0,1},{1,0},{2,3},{3,2},{4,5},{5,4},{6,7},{7,6},{8,9},{9,8},{10,11... | collective-permute-start | bytes 1572872 | tf_op jit(solution)/shard_map/ppermute | solution.py:44
  103.1 25.4 %collective-permute-start.13 = (bf16[32,64,128]{2,1,0:T(8,128)(2,1)S(1)}, bf16[32,64,128]{2,1,0:T(8,128)(2,1)}, u32[]{:S(2)}, u32[]{:S(2)}) collective-permute-start(bf16[32,64,128]{2,1,0:T(8,128)(2,1)S(1)} %copy-done.10), channel_id=1, source_target_pairs={{0,2},{1,3},{2,0},{3,1},{4,6},{5,7},{6,4},{7,5},{8,10},{9,11},{10,... | collective-permute-start | bytes 1572872 | tf_op jit(solution)/shard_map/ppermute | solution.py:44
  111.4 24.4 %collective-permute-start.2 = (bf16[129,16,128]{2,1,0:T(8,128)(2,1)S(1)}, bf16[129,16,128]{2,1,0:T(8,128)(2,1)S(1)}, u32[]{:S(2)}, u32[]{:S(2)}) collective-permute-start(bf16[129,16,128]{2,1,0:T(8,128)(2,1)S(1)} %copy-done.19), channel_id=1, source_target_pairs={{0,6},{1,7},{2,4},{3,5},{4,2},{5,3},{6,0},{7,1},{8,14},{9,15},{10,... | collective-permute-start | bytes 1585160 | tf_op jit(solution)/shard_map/ppermute | solution.py:44
  111.5 32.5 %collective-permute-start.4 = (bf16[129,16,128]{2,1,0:T(8,128)(2,1)S(1)}, bf16[129,16,128]{2,1,0:T(8,128)(2,1)S(1)}, u32[]{:S(2)}, u32[]{:S(2)}) collective-permute-start(bf16[129,16,128]{2,1,0:T(8,128)(2,1)S(1)} %copy-done.6), channel_id=1, source_target_pairs={{0,14},{1,15},{2,12},{3,13},{4,10},{5,11},{6,8},{7,9},{8,6},{9,7},... | collective-permute-start | bytes 1585160 | tf_op jit(solution)/shard_map/ppermute | solution.py:44
  113.5 15.0 %copy-start.16 = (bf16[129,16,128]{2,1,0:T(8,128)(2,1)}, bf16[129,16,128]{2,1,0:T(8,128)(2,1)S(1)}, u32[]{:S(2)}) copy-start(bf16[129,16,128]{2,1,0:T(8,128)(2,1)S(1)} %collective-permute-done.16.refs_1_.refs_7_) | copy-start | bytes 1585156
  113.5 30.5 %collective-permute-start.8 = (bf16[32,64,128]{2,1,0:T(8,128)(2,1)}, bf16[32,64,128]{2,1,0:T(8,128)(2,1)S(1)}, u32[]{:S(2)}, u32[]{:S(2)}) collective-permute-start(bf16[32,64,128]{2,1,0:T(8,128)(2,1)} %collective-permute-done.7.refs_4_.refs_19_.refs_21_.refs_23_), channel_id=1, source_target_pairs={{0,1},{1,0},{2,3},{3,2},{4,5},{5,4},{6,7},{7,6},{8,9},{9,8},{10,11... | collective-permute-start | bytes 1572872 | tf_op jit(solution)/shard_map/ppermute | solution.py:44
  128.5 15.5 %collective-permute-start.14 = (bf16[32,64,128]{2,1,0:T(8,128)(2,1)}, bf16[32,64,128]{2,1,0:T(8,128)(2,1)}, u32[]{:S(2)}, u32[]{:S(2)}) collective-permute-start(bf16[32,64,128]{2,1,0:T(8,128)(2,1)} %collective-permute-done.13.refs_6_.refs_27_.refs_29_.refs_31_), channel_id=1, source_target_pairs={{0,1},{1,0},{2,3},{3,2},{4,5},{5,4},{6,7},{7,6},{8,9},{9,8},{10,11... | collective-permute-start | bytes 1572872 | tf_op jit(solution)/shard_map/ppermute | solution.py:44
  152.1 5.9 %collective-permute-start.24 = (f32[16,128]{1,0:T(8,128)}, f32[16,128]{1,0:T(8,128)S(1)}, u32[]{:S(2)}, u32[]{:S(2)}) collective-permute-start(f32[16,128]{1,0:T(8,128)} %get-tuple-element.34), channel_id=1, source_target_pairs={{0,1},{1,0},{2,3},{3,2},{4,5},{5,4},{6,7},{7,6},{8,9},{9,8},{10,11... | collective-permute-start | bytes 24584 | tf_op jit(solution)/shard_map/ppermute | solution.py:117
  152.2 5.8 %collective-permute-start.25 = (f32[16,128]{1,0:T(8,128)}, f32[16,128]{1,0:T(8,128)S(1)}, u32[]{:S(2)}, u32[]{:S(2)}) collective-permute-start(f32[16,128]{1,0:T(8,128)} %get-tuple-element.34), channel_id=1, source_target_pairs={{0,2},{1,3},{2,0},{3,1},{4,6},{5,7},{6,4},{7,5},{8,10},{9,11},{10,... | collective-permute-start | bytes 24584 | tf_op jit(solution)/shard_map/ppermute | solution.py:117
  153.7 4.3 %collective-permute-start.26 = (f32[16,128]{1,0:T(8,128)}, f32[16,128]{1,0:T(8,128)S(1)}, u32[]{:S(2)}, u32[]{:S(2)}) collective-permute-start(f32[16,128]{1,0:T(8,128)} %get-tuple-element.34), channel_id=1, source_target_pairs={{0,3},{1,2},{2,1},{3,0},{4,7},{5,6},{6,5},{7,4},{8,11},{9,10},{10,... | collective-permute-start | bytes 24584 | tf_op jit(solution)/shard_map/ppermute | solution.py:117
  154.8 27.5 %collective-permute-start.32 = (bf16[32,64,128]{2,1,0:T(8,128)(2,1)}, bf16[32,64,128]{2,1,0:T(8,128)(2,1)S(1)}, u32[]{:S(2)}, u32[]{:S(2)}) collective-permute-start(bf16[32,64,128]{2,1,0:T(8,128)(2,1)} %get-tuple-element.36.refs_11_), channel_id=1, source_target_pairs={{0,1},{1,0},{2,3},{3,2},{4,5},{5,4},{6,7},{7,6},{8,9},{9,8},{10,11... | collective-permute-start | bytes 1572872 | tf_op jit(solution)/shard_map/ppermute | solution.py:44
  155.1 24.9 %collective-permute-start.30 = (bf16[32,64,128]{2,1,0:T(8,128)(2,1)}, bf16[32,64,128]{2,1,0:T(8,128)(2,1)S(1)}, u32[]{:S(2)}, u32[]{:S(2)}) collective-permute-start(bf16[32,64,128]{2,1,0:T(8,128)(2,1)} %get-tuple-element.36.refs_11_), channel_id=1, source_target_pairs={{0,4},{1,5},{2,0},{3,1},{4,8},{5,9},{6,2},{7,3},{8,12},{9,13},{10,... | collective-permute-start | bytes 1572872 | tf_op jit(solution)/shard_map/ppermute | solution.py:44
  158.0 22.0 %collective-permute-start.35 = (bf16[32,64,128]{2,1,0:T(8,128)(2,1)}, bf16[32,64,128]{2,1,0:T(8,128)(2,1)S(1)}, u32[]{:S(2)}, u32[]{:S(2)}) collective-permute-start(bf16[32,64,128]{2,1,0:T(8,128)(2,1)} %get-tuple-element.36.refs_11_), channel_id=1, source_target_pairs={{0,2},{1,3},{2,6},{3,7},{4,0},{5,1},{6,10},{7,11},{8,4},{9,5},{10,... | collective-permute-start | bytes 1572872 | tf_op jit(solution)/shard_map/ppermute | solution.py:44
  158.7 13.5 %collective-permute-start.27 = (f32[16,128]{1,0:T(8,128)S(1)}, f32[16,128]{1,0:T(8,128)S(1)}, u32[]{:S(2)}, u32[]{:S(2)}) collective-permute-start(f32[16,128]{1,0:T(8,128)S(1)} %add_add_fusion.1), channel_id=1, source_target_pairs={{0,4},{1,5},{2,6},{3,7},{4,0},{5,1},{6,2},{7,3},{8,12},{9,13},{10,... | collective-permute-start | bytes 24584 | tf_op jit(solution)/shard_map/ppermute | solution.py:117
  161.4 11.8 %collective-permute-start.28 = (f32[16,128]{1,0:T(8,128)S(1)}, f32[16,128]{1,0:T(8,128)S(1)}, u32[]{:S(2)}, u32[]{:S(2)}) collective-permute-start(f32[16,128]{1,0:T(8,128)S(1)} %add_add_fusion.1), channel_id=1, source_target_pairs={{0,8},{1,9},{2,10},{3,11},{4,12},{5,13},{6,14},{7,15},{8,0},{9,1},... | collective-permute-start | bytes 24584 | tf_op jit(solution)/shard_map/ppermute | solution.py:117
  172.2 5.4 %collective-permute-start.29 = (f32[16,128]{1,0:T(8,128)S(1)}, f32[16,128]{1,0:T(8,128)S(1)}, u32[]{:S(2)}, u32[]{:S(2)}) collective-permute-start(f32[16,128]{1,0:T(8,128)S(1)} %add_add_fusion.1), channel_id=1, source_target_pairs={{0,12},{1,13},{2,14},{3,15},{4,8},{5,9},{6,10},{7,11},{8,4},{9,5},... | collective-permute-start | bytes 24584 | tf_op jit(solution)/shard_map/ppermute | solution.py:117
  179.9 15.7 %collective-permute-start.34 = (bf16[32,64,128]{2,1,0:T(8,128)(2,1)S(1)}, bf16[32,64,128]{2,1,0:T(8,128)(2,1)S(1)}, u32[]{:S(2)}, u32[]{:S(2)}) collective-permute-start(bf16[32,64,128]{2,1,0:T(8,128)(2,1)S(1)} %collective-permute-done.30.refs_11_), channel_id=1, source_target_pairs={{0,1},{1,0},{2,3},{3,2},{4,5},{5,4},{6,7},{7,6},{8,9},{9,8},{10,11... | collective-permute-start | bytes 1572872 | tf_op jit(solution)/shard_map/ppermute | solution.py:44
  180.0 14.3 %collective-permute-start.31 = (bf16[32,64,128]{2,1,0:T(8,128)(2,1)S(1)}, bf16[32,64,128]{2,1,0:T(8,128)(2,1)S(1)}, u32[]{:S(2)}, u32[]{:S(2)}) collective-permute-start(bf16[32,64,128]{2,1,0:T(8,128)(2,1)S(1)} %collective-permute-done.30.refs_11_), channel_id=1, source_target_pairs={{0,4},{1,5},{2,0},{3,1},{4,8},{5,9},{6,2},{7,3},{8,12},{9,13},{10,... | collective-permute-start | bytes 1572872 | tf_op jit(solution)/shard_map/ppermute | solution.py:44
  180.0 17.3 %collective-permute-start.36 = (bf16[32,64,128]{2,1,0:T(8,128)(2,1)S(1)}, bf16[32,64,128]{2,1,0:T(8,128)(2,1)}, u32[]{:S(2)}, u32[]{:S(2)}) collective-permute-start(bf16[32,64,128]{2,1,0:T(8,128)(2,1)S(1)} %collective-permute-done.35.refs_13_), channel_id=1, source_target_pairs={{0,1},{1,0},{2,3},{3,2},{4,5},{5,4},{6,7},{7,6},{8,9},{9,8},{10,11... | collective-permute-start | bytes 1572872 | tf_op jit(solution)/shard_map/ppermute | solution.py:44
  180.5 14.8 %collective-permute-start.38 = (bf16[32,64,128]{2,1,0:T(8,128)(2,1)S(1)}, bf16[32,64,128]{2,1,0:T(8,128)(2,1)S(1)}, u32[]{:S(2)}, u32[]{:S(2)}) collective-permute-start(bf16[32,64,128]{2,1,0:T(8,128)(2,1)S(1)} %collective-permute-done.35.refs_13_), channel_id=1, source_target_pairs={{0,2},{1,3},{2,6},{3,7},{4,0},{5,1},{6,10},{7,11},{8,4},{9,5},{10,... | collective-permute-start | bytes 1572872 | tf_op jit(solution)/shard_map/ppermute | solution.py:44
  195.1 18.5 %collective-permute-start.42 = (bf16[32,64,128]{2,1,0:T(8,128)(2,1)}, bf16[32,64,128]{2,1,0:T(8,128)(2,1)S(1)}, u32[]{:S(2)}, u32[]{:S(2)}) collective-permute-start(bf16[32,64,128]{2,1,0:T(8,128)(2,1)} %shard_map.80.refs_11_), channel_id=1, source_target_pairs={{0,1},{1,0},{2,3},{3,2},{4,5},{5,4},{6,7},{7,6},{8,9},{9,8},{10,11... | collective-permute-start | bytes 1572872 | tf_op jit(solution)/shard_map/ppermute | solution.py:44
  195.1 14.7 %collective-permute-start.33 = (bf16[32,64,128]{2,1,0:T(8,128)(2,1)}, bf16[32,64,128]{2,1,0:T(8,128)(2,1)}, u32[]{:S(2)}, u32[]{:S(2)}) collective-permute-start(bf16[32,64,128]{2,1,0:T(8,128)(2,1)} %shard_map.80.refs_11_), channel_id=1, source_target_pairs={{0,4},{1,5},{2,0},{3,1},{4,8},{5,9},{6,2},{7,3},{8,12},{9,13},{10,... | collective-permute-start | bytes 1572872 | tf_op jit(solution)/shard_map/ppermute | solution.py:44
  195.4 18.2 %collective-permute-start.43 = (bf16[32,64,128]{2,1,0:T(8,128)(2,1)S(1)}, bf16[32,64,128]{2,1,0:T(8,128)(2,1)}, u32[]{:S(2)}, u32[]{:S(2)}) collective-permute-start(bf16[32,64,128]{2,1,0:T(8,128)(2,1)S(1)} %collective-permute-done.38.refs_13_), channel_id=1, source_target_pairs={{0,1},{1,0},{2,3},{3,2},{4,5},{5,4},{6,7},{7,6},{8,9},{9,8},{10,11... | collective-permute-start | bytes 1572872 | tf_op jit(solution)/shard_map/ppermute | solution.py:44
  195.7 14.1 %collective-permute-start.39 = (bf16[32,64,128]{2,1,0:T(8,128)(2,1)S(1)}, bf16[32,64,128]{2,1,0:T(8,128)(2,1)S(1)}, u32[]{:S(2)}, u32[]{:S(2)}) collective-permute-start(bf16[32,64,128]{2,1,0:T(8,128)(2,1)S(1)} %collective-permute-done.38.refs_13_), channel_id=1, source_target_pairs={{0,2},{1,3},{2,6},{3,7},{4,0},{5,1},{6,10},{7,11},{8,4},{9,5},{10,... | collective-permute-start | bytes 1572872 | tf_op jit(solution)/shard_map/ppermute | solution.py:44
  209.7 14.5 %collective-permute-start.37 = (bf16[32,64,128]{2,1,0:T(8,128)(2,1)}, bf16[32,64,128]{2,1,0:T(8,128)(2,1)S(1)}, u32[]{:S(2)}, u32[]{:S(2)}) collective-permute-start(bf16[32,64,128]{2,1,0:T(8,128)(2,1)} %shard_map.82.lower_ref.refs_11_), channel_id=1, source_target_pairs={{0,1},{1,0},{2,3},{3,2},{4,5},{5,4},{6,7},{7,6},{8,9},{9,8},{10,11... | collective-permute-start | bytes 1572872 | tf_op jit(solution)/shard_map/ppermute | solution.py:44
  212.7 10.7 %collective-permute-start.41 = (bf16[32,64,128]{2,1,0:T(8,128)(2,1)}, bf16[32,64,128]{2,1,0:T(8,128)(2,1)}, u32[]{:S(2)}, u32[]{:S(2)}) collective-permute-start(bf16[32,64,128]{2,1,0:T(8,128)(2,1)} %shard_map.83), channel_id=1, source_target_pairs={{0,4},{1,3},{2,0},{3,7},{4,8},{5,1},{6,2},{7,11},{8,12},{9,5},{10,... | collective-permute-start | bytes 1572872 | tf_op jit(solution)/shard_map/ppermute | solution.py:44
  213.0 11.3 %collective-permute-start.40 = (bf16[32,64,128]{2,1,0:T(8,128)(2,1)}, bf16[32,64,128]{2,1,0:T(8,128)(2,1)S(1)}, u32[]{:S(2)}, u32[]{:S(2)}) collective-permute-start(bf16[32,64,128]{2,1,0:T(8,128)(2,1)} %copy-done.24), channel_id=1, source_target_pairs={{0,1},{1,0},{2,3},{3,2},{4,5},{5,4},{6,7},{7,6},{8,9},{9,8},{10,11... | collective-permute-start | bytes 1572872 | tf_op jit(solution)/shard_map/ppermute | solution.py:44
  223.4 2.2 collective-permute-start.44
  (33 other events, 123.4 us)

commit v11 on v10

--- a/solution.py
+++ b/solution.py
@@ -112,13 +112,15 @@
 
 def spread(value, devices):
     step = 1
+    values = []
     while step < devices:
         masks = [step] if 2 * step == devices else [step, 2 * step, 3 * step]
         parts = [lax.ppermute(value, BOTH, [(d, d ^ m) for d in range(devices)]) for m in masks]
         for part in parts:
             value = value + part
+        values.append(value)
         step *= 4
-    return value
+    return values
 
 
 def pack_kernel(order, capacity, blocks, terms, ids_ref, plan_ref, other_plan_ref, *refs):
@@ -519,9 +521,10 @@
             own_rows,
         )
 
-    rest = total
+    stats = spread(stats, owners * halves)
+    rest = after(total, stats[0])
     entries = blocks * owners * height * width
-    scale, rayleigh = scales(spread(stats, owners * halves), entries)
+    scale, rayleigh = scales(stats[-1], entries)
     reach = (owners - 1) // 2
     waves = [(near[m], far[m]) for m in range(owners)]
 

time: 238 us -> 239 us (level)
    ppermute x6, starting transfers between devices: 4.75 us -> 7.94 us  [spread(): lax.ppermute(value, BOTH, [(d, d ^ m) for d in range(devices)])]
    ppermute x6, waiting for transfers between devices: 14.8 us -> 12.4 us  [spread(): lax.ppermute(value, BOTH, [(d, d ^ m) for d in range(devices)])]
    unnamed x72 -> x76, local copies, waits for them, and re-layouts: 7.66 us -> 8.45 us
  transfers between devices with their start and end apart: 45 -> 45, of which waited for: 14 -> 17; matrix products, arithmetic and copies ran while one was open for 3% -> 3% of each run, Pallas kernels for 23% -> 23%
where the time goes in v11:
time: 239 us; the launch traced here: 238 us
  waiting for transfers between devices  110 us (46%)
  Pallas kernels  72.4 us (30%)
  starting transfers between devices  37.8 us (16%)
  local copies, waits for them, and re-layouts  11.6 us (5%)
  other arithmetic  5.09 us (2%)
    ppermute x39, waiting for transfers between devices, permute(): return lax.ppermute(value, BOTH, pairs)  97.3 us
    pallas_call x8, Pallas kernels, apply_group(): pl.pallas_call(functools.partial(apply_kernel, sources, choices, first, e...  63.1 us
    ppermute x39, starting transfers between devices, permute(): return lax.ppermute(value, BOTH, pairs)  29.8 us
    ppermute x6, waiting for transfers between devices, spread(): lax.ppermute(value, BOTH, [(d, d ^ m) for d in range(devices)])  12.4 us
    unnamed x76, local copies, waits for them, and re-layouts  8.45 us
    ppermute x6, starting transfers between devices, spread(): lax.ppermute(value, BOTH, [(d, d ^ m) for d in range(devices)])  7.94 us
    pallas_call x1, Pallas kernels, pack(): pl.pallas_call(functools.partial(pack_kernel, order, capacity, blocks, te...  5.48 us
  transfers between devices with their start and end apart: 45, of which 17 were waited for; matrix products, arithmetic and copies ran while one was open for 3% of the time, Pallas kernels for 23%

profile of v11, /device:TPU:0, one launch (start us, length us, event | category | flops | bytes accessed | tf_op | source)
XLA Modules:
  0.0 237.8 jit_solution(9311339144974601163)
XLA Ops:
  0.6 1.4 constant_dynamic-slice_fusion.2
  2.7 1.1 constant_dynamic-slice_fusion
  3.7 4.0 %collective-permute-start.9 = (bf16[32,64,128]{2,1,0:T(8,128)(2,1)}, bf16[32,64,128]{2,1,0:T(8,128)(2,1)S(1)}, u32[]{:S(2)}, u32[]{:S(2)}) collective-permute-start(bf16[32,64,128]{2,1,0:T(8,128)(2,1)} %get-tuple-element.45.refs_4_.refs_8_.refs_13_.refs_15_.refs_17_), channel_id=1, source_target_pairs={{0,8},{1,9},{2,10},{3,11},{4,12},{5,13},{6,14},{7,15},{8,0},{9,1},... | collective-permute-start | bytes 1572872 | tf_op jit(solution)/shard_map/ppermute | solution.py:44
  7.8 1.5 collective-permute-start.21
  11.1 1.0 copy-done.16
  12.1 5.5 %shard_map.68 = (bf16[129,16,128]{2,1,0:T(8,128)(2,1)}, bf16[129,16,128]{2,1,0:T(8,128)(2,1)}, bf16[129,16,128]{2,1,0:T(8,128)(2,1)}, bf16[129,16,128]{2,1,0:T(8...) custom-call(s32[2]{0:T(128)} %pad_add_fusion.2.ids_ref, ...), custom_call_target="tpu_custom_call" | custom-call | flops 5750000128 | tf_op jit(solution)/shard_map/pallas_call | solution.py:186
  18.1 1.6 collective-permute-start.6
  19.7 11.8 %collective-permute-done.9.refs_0_ = bf16[32,64,128]{2,1,0:T(8,128)(2,1)S(1)} collective-permute-done((bf16[32,64,128]{2,1,0:T(8,128)(2,1)}, bf16[32,64,128]{2,1,0:T(8,128)(2,1)S(1)}, u32[]{:S(2)}, u32[]{:S(2)}) %collective-permute-start.9) | collective-permute-done | bytes 524320 | tf_op jit(solution)/shard_map/ppermute | solution.py:44
  31.5 3.9 %collective-permute-start.3 = (bf16[129,16,128]{2,1,0:T(8,128)(2,1)}, bf16[129,16,128]{2,1,0:T(8,128)(2,1)S(1)}, u32[]{:S(2)}, u32[]{:S(2)}) collective-permute-start(bf16[129,16,128]{2,1,0:T(8,128)(2,1)} %get-tuple-element.25), channel_id=1, source_target_pairs={{0,10},{1,11},{2,8},{3,9},{4,14},{5,15},{6,12},{7,13},{8,2},{9,3},... | collective-permute-start | bytes 1585160 | tf_op jit(solution)/shard_map/ppermute | solution.py:44
  35.4 1.2 collective-permute-start.12
  36.6 7.5 %collective-permute-done.6.refs_0_ = bf16[32,64,128]{2,1,0:T(8,128)(2,1)S(1)} collective-permute-done((bf16[32,64,128]{2,1,0:T(8,128)(2,1)}, bf16[32,64,128]{2,1,0:T(8,128)(2,1)S(1)}, u32[]{:S(2)}, u32[]{:S(2)}) %collective-permute-start.6) | collective-permute-done | bytes 524320 | tf_op jit(solution)/shard_map/ppermute | solution.py:44
  44.1 26.1 %collective-permute-done.15.refs_1_.refs_5_ = bf16[129,16,128]{2,1,0:T(8,128)(2,1)S(1)} collective-permute-done((bf16[129,16,128]{2,1,0:T(8,128)(2,1)}, bf16[129,16,128]{2,1,0:T(8,128)(2,1)S(1)}, u32[]{:S(2)}, u32[]{:S(2)}) %collective-permute-start.15) | collective-permute-done | bytes 528416 | tf_op jit(solution)/shard_map/ppermute | solution.py:44
  70.3 10.5 %collective-permute-done.3.refs_1_.refs_0_.refs_6_ = bf16[129,16,128]{2,1,0:T(8,128)(2,1)S(1)} collective-permute-done((bf16[129,16,128]{2,1,0:T(8,128)(2,1)}, bf16[129,16,128]{2,1,0:T(8,128)(2,1)S(1)}, u32[]{:S(2)}, u32[]{:S(2)}) %collective-permute-start.3) | collective-permute-done | bytes 528416 | tf_op jit(solution)/shard_map/ppermute | solution.py:44
  82.3 5.0 %collective-permute-done.11.refs_0_ = bf16[32,64,128]{2,1,0:T(8,128)(2,1)S(1)} collective-permute-done((bf16[32,64,128]{2,1,0:T(8,128)(2,1)}, bf16[32,64,128]{2,1,0:T(8,128)(2,1)S(1)}, u32[]{:S(2)}, u32[]{:S(2)}) %collective-permute-start.11) | collective-permute-done | bytes 524320 | tf_op jit(solution)/shard_map/ppermute | solution.py:44
  88.2 1.6 collective-permute-start.7
  89.7 3.4 %collective-permute-start.16 = (bf16[129,16,128]{2,1,0:T(8,128)(2,1)S(1)}, bf16[129,16,128]{2,1,0:T(8,128)(2,1)S(1)}, u32[]{:S(2)}, u32[]{:S(2)}) collective-permute-start(bf16[129,16,128]{2,1,0:T(8,128)(2,1)S(1)} %copy-done.5), channel_id=1, source_target_pairs={{0,12},{1,13},{2,14},{3,15},{4,8},{5,9},{6,10},{7,11},{8,4},{9,5},... | collective-permute-start | bytes 1585160 | tf_op jit(solution)/shard_map/ppermute | solution.py:44
  93.1 2.7 %collective-permute-done.19.refs_4_.refs_23_.refs_25_.refs_27_ = bf16[32,64,128]{2,1,0:T(8,128)(2,1)} collective-permute-done((bf16[32,64,128]{2,1,0:T(8,128)(2,1)}, bf16[32,64,128]{2,1,0:T(8,128)(2,1)}, u32[]{:S(2)}, u32[]{:S(2)}) %collective-permute-start.19) | collective-permute-done | bytes 524320 | tf_op jit(solution)/shard_map/ppermute | solution.py:44
  95.8 6.8 %shard_map.74 = (f32[33,64,128]{2,1,0:T(8,128)}, f32[8,128]{1,0:T(8,128)}) custom-call(s32[2]{0:T(128)} %pad_add_fusion.1.ids_ref, bf16[129,16,128]{2,1,0:T(8,128)(2,1)} %get-tuple-element.30.refs_0_.refs_1_, bf16[129,16,128]{2,1,0:T(8,128)(2,1)} %copy-done.3, bf16[2,32,128,128]{3,2,1,0:T(8,128)(2,1)} %refs_9_.7, ...), custom_call_target="tpu_custom_call" | custom-call | flops 8165000192 | tf_op jit(solution)/shard_map/pallas_call | solution.py:436
  104.0 7.5 %shard_map.75 = (f32[33,64,128]{2,1,0:T(8,128)}, f32[8,128]{1,0:T(8,128)}) custom-call(s32[2]{0:T(128)} %pad_add_fusion.1.ids_ref, bf16[129,16,128]{2,1,0:T(8,128)(2,1)} %copy-done, bf16[129,16,128]{2,1,0:T(8,128)(2,1)} %copy-done.2, bf16[2,32,128,128]{3,2,1,0:T(8,128)(2,1)} %refs_9_.7, bf16[2,32,128,128]{3,2,1,0:T(8,128)(2,1)} %collective-permute-done.5.refs_3_.refs_10_, ...), custom_call_target="tpu_custom_call" | custom-call | flops 8165000192 | tf_op jit(solution)/shard_map/pallas_call | solution.py:436
  111.6 2.0 collective-permute-start.4
  113.6 14.9 %collective-permute-done.13.refs_6_.refs_27_.refs_29_.refs_31_ = bf16[32,64,128]{2,1,0:T(8,128)(2,1)} collective-permute-done((bf16[32,64,128]{2,1,0:T(8,128)(2,1)S(1)}, bf16[32,64,128]{2,1,0:T(8,128)(2,1)}, u32[]{:S(2)}, u32[]{:S(2)}) %collective-permute-start.13) | collective-permute-done | bytes 524320 | tf_op jit(solution)/shard_map/ppermute | solution.py:44
  128.5 7.4 %shard_map.76 = (f32[33,64,128]{2,1,0:T(8,128)}, f32[8,128]{1,0:T(8,128)}) custom-call(s32[2]{0:T(128)} %pad_add_fusion.1.ids_ref, bf16[129,16,128]{2,1,0:T(8,128)(2,1)} %copy-done.4, bf16[129,16,128]{2,1,0:T(8,128)(2,1)} %copy-done.17, bf16[2,32,128,128]{3,2,1,0:T(8,128)(2,1)} %refs_9_.7, bf16[2,32,128,128]{3,2,1,0:T(8,128)(2,1)} %collective-permute-done.5.refs_3_.refs_10_, ...), custom_call_target="tpu_custom_call" | custom-call | flops 8165000192 | tf_op jit(solution)/shard_map/pallas_call | solution.py:436
  135.9 8.2 %collective-permute-done.4.refs_1_.refs_8_ = bf16[129,16,128]{2,1,0:T(8,128)(2,1)S(1)} collective-permute-done((bf16[129,16,128]{2,1,0:T(8,128)(2,1)S(1)}, bf16[129,16,128]{2,1,0:T(8,128)(2,1)S(1)}, u32[]{:S(2)}, u32[]{:S(2)}) %collective-permute-start.4) | collective-permute-done | bytes 528416 | tf_op jit(solution)/shard_map/ppermute | solution.py:44
  145.1 7.1 %shard_map.77 = (bf16[32,64,128]{2,1,0:T(8,128)(2,1)}, f32[16,128]{1,0:T(8,128)}) custom-call(s32[2]{0:T(128)} %pad_add_fusion.1.ids_ref, bf16[129,16,128]{2,1,0:T(8,128)(2,1)} %copy-done.18, bf16[129,16,128]{2,1,0:T(8,128)(2,1)} %copy-done.19, bf16[2,32,128,128]{3,2,1,0:T(8,128)(2,1)} %refs_9_.7, ...), custom_call_target="tpu_custom_call" | custom-call | flops 8165000192 | tf_op jit(solution)/shard_map/pallas_call | solution.py:436
  152.3 1.5 collective-permute-start.25
  154.8 1.4 collective-permute-done.25
  156.2 0.9 collective-permute-done.26
  157.8 2.9 %collective-permute-start.27 = (f32[16,128]{1,0:T(8,128)S(1)}, f32[16,128]{1,0:T(8,128)S(1)}, u32[]{:S(2)}, u32[]{:S(2)}) collective-permute-start(f32[16,128]{1,0:T(8,128)S(1)} %add_add_fusion.1.refs_1_), channel_id=1, source_target_pairs={{0,4},{1,5},{2,6},{3,7},{4,0},{5,1},{6,2},{7,3},{8,12},{9,13},{10,... | collective-permute-start | bytes 24584 | tf_op jit(solution)/shard_map/ppermute | solution.py:118
  161.5 1.3 collective-permute-start.35
  163.4 1.2 collective-permute-start.28
  164.6 1.9 collective-permute-start.29
  167.1 9.2 %collective-permute-done.28 = f32[16,128]{1,0:T(8,128)S(1)} collective-permute-done((f32[16,128]{1,0:T(8,128)}, f32[16,128]{1,0:T(8,128)S(1)}, u32[]{:S(2)}, u32[]{:S(2)}) %collective-permute-start.28) | collective-permute-done | bytes 8224 | tf_op jit(solution)/shard_map/ppermute | solution.py:118
  176.4 0.9 collective-permute-done.29
  177.2 1.3 add_add_fusion.stats_ref
  178.5 1.7 shard_map.78
  180.9 1.5 collective-permute-start.38
  182.5 0.8 copy-done.31
  183.3 6.1 %shard_map.80 = (f32[33,64,128]{2,1,0:T(8,128)}, f32[8,128]{1,0:T(8,128)}) custom-call(s32[3]{0:T(128)} %pad_add_fusion.3.ids_ref, f32[16,128]{1,0:T(8,128)} %get-tuple-element.35.refs_0_, bf16[129,16,128]{2,1,0:T(8,128)(2,1)} %get-tuple-element.30.refs_0_.refs_1_, bf16[129,16,128]{2,1,0:T(8,128)(2,1)} %copy-done.2, bf16[129,16,128]{2,1,0:T(8,128)(2,1)} %copy-done.4, ...), custom_call_target="tpu_custom_call" | custom-call | flops 7129999872 | tf_op jit(solution)/shard_map/pallas_call | solution.py:436
  189.4 5.2 %collective-permute-done.31.refs_0_ = bf16[32,64,128]{2,1,0:T(8,128)(2,1)S(1)} collective-permute-done((bf16[32,64,128]{2,1,0:T(8,128)(2,1)S(1)}, bf16[32,64,128]{2,1,0:T(8,128)(2,1)S(1)}, u32[]{:S(2)}, u32[]{:S(2)}) %collective-permute-start.31) | collective-permute-done | bytes 524320 | tf_op jit(solution)/shard_map/ppermute | solution.py:44
  196.1 1.6 collective-permute-start.39
  197.6 9.1 %shard_map.82 = (f32[33,64,128]{2,1,0:T(8,128)}, f32[8,128]{1,0:T(8,128)}) custom-call(s32[4]{0:T(128)} %pad_add_fusion.4.ids_ref, f32[16,128]{1,0:T(8,128)} %get-tuple-element.35.refs_0_, bf16[129,16,128]{2,1,0:T(8,128)(2,1)} %get-tuple-element.30.refs_0_.refs_1_, bf16[129,16,128]{2,1,0:T(8,128)(2,1)} %copy-done.2, bf16[129,16,128]{2,1,0:T(8,128)(2,1)} %copy-done.4, ...), custom_call_target="tpu_custom_call" | custom-call | flops 10234999808 | tf_op jit(solution)/shard_map/pallas_call | solution.py:436
  206.7 3.3 %collective-permute-done.33.refs_0_ = bf16[32,64,128]{2,1,0:T(8,128)(2,1)} collective-permute-done((bf16[32,64,128]{2,1,0:T(8,128)(2,1)}, bf16[32,64,128]{2,1,0:T(8,128)(2,1)}, u32[]{:S(2)}, u32[]{:S(2)}) %collective-permute-start.33) | collective-permute-done | bytes 524320 | tf_op jit(solution)/shard_map/ppermute | solution.py:44
  210.2 0.8 copy-done.25
  211.0 2.1 shard_map.84
  213.8 0.8 copy-done.33
  214.6 9.0 %shard_map.85 = (f32[33,64,128]{2,1,0:T(8,128)}, f32[8,128]{1,0:T(8,128)}) custom-call(s32[4]{0:T(128)} %pad_add_fusion.6.ids_ref, f32[16,128]{1,0:T(8,128)} %get-tuple-element.35.refs_0_, bf16[129,16,128]{2,1,0:T(8,128)(2,1)} %get-tuple-element.30.refs_0_.refs_1_, bf16[129,16,128]{2,1,0:T(8,128)(2,1)} %copy-done.2, bf16[129,16,128]{2,1,0:T(8,128)(2,1)} %copy-done.4, ...), custom_call_target="tpu_custom_call" | custom-call | flops 10234999808 | tf_op jit(solution)/shard_map/pallas_call | solution.py:436
  225.3 1.3 collective-permute-done.44.refs_16_
  227.4 10.3 %shard_map.87 = bf16[32,64,128]{2,1,0:T(8,128)(2,1)} custom-call(s32[5]{0:T(128)} %stack.71.ids_ref, f32[16,128]{1,0:T(8,128)} %get-tuple-element.35.refs_0_, bf16[129,16,128]{2,1,0:T(8,128)(2,1)} %get-tuple-element.30.refs_0_.refs_1_, bf16[129,16,128]{2,1,0:T(8,128)(2,1)} %copy-done.2, bf16[129,16,128]{2,1,0:T(8,128)(2,1)} %copy-done.4, ...), custom_call_target="tpu_custom_call" | custom-call | flops 13340000256 | tf_op jit(solution)/shard_map/pallas_call | solution.py:436
  (149 shorter events, 17.1 us)
Async XLA Ops:
  2.1 8.5 %collective-permute-start.1 = (bf16[2,32,64,128]{3,2,1,0:T(8,128)(2,1)S(1)}, bf16[2,32,64,128]{3,2,1,0:T(8,128)(2,1)S(1)}, u32[]{:S(2)}, u32[]{:S(2)}) collective-permute-start(bf16[2,32,64,128]{3,2,1,0:T(8,128)(2,1)S(1)} %constant_dynamic-slice_fusion.2), channel_id=1, source_target_pairs={{0,1},{1,0},{2,3},{3,2},{4,5},{5,4},{6,7},{7,6},{8,9},{9,8},{10,11... | collective-permute-start | bytes 3145736 | tf_op jit(solution)/shard_map/ppermute | solution.py:44
  2.6 85.6 %collective-permute-start.5 = (bf16[2,32,128,128]{3,2,1,0:T(8,128)(2,1)}, bf16[2,32,128,128]{3,2,1,0:T(8,128)(2,1)}, u32[]{:S(2)}, u32[]{:S(2)}) collective-permute-start(bf16[2,32,128,128]{3,2,1,0:T(8,128)(2,1)} %refs_9_.7), channel_id=1, source_target_pairs={{0,1},{1,0},{2,3},{3,2},{4,5},{5,4},{6,7},{7,6},{8,9},{9,8},{10,11... | collective-permute-start | bytes 6291464 | tf_op jit(solution)/shard_map/ppermute | solution.py:44
  3.7 27.7 %collective-permute-start.9 = (bf16[32,64,128]{2,1,0:T(8,128)(2,1)}, bf16[32,64,128]{2,1,0:T(8,128)(2,1)S(1)}, u32[]{:S(2)}, u32[]{:S(2)}) collective-permute-start(bf16[32,64,128]{2,1,0:T(8,128)(2,1)} %get-tuple-element.45.refs_4_.refs_8_.refs_13_.refs_15_.refs_17_), channel_id=1, source_target_pairs={{0,8},{1,9},{2,10},{3,11},{4,12},{5,13},{6,14},{7,15},{8,0},{9,1},... | collective-permute-start | bytes 1572872 | tf_op jit(solution)/shard_map/ppermute | solution.py:44
  7.8 23.7 %collective-permute-start.21 = (bf16[32,64,128]{2,1,0:T(8,128)(2,1)}, bf16[32,64,128]{2,1,0:T(8,128)(2,1)}, u32[]{:S(2)}, u32[]{:S(2)}) collective-permute-start(bf16[32,64,128]{2,1,0:T(8,128)(2,1)} %get-tuple-element.45.refs_4_.refs_8_.refs_13_.refs_15_.refs_17_), channel_id=1, source_target_pairs={{0,2},{1,3},{2,0},{3,1},{4,6},{5,7},{6,4},{7,5},{8,10},{9,11},{10,... | collective-permute-start | bytes 1572872 | tf_op jit(solution)/shard_map/ppermute | solution.py:44
  9.3 1.2 collective-permute-start
  17.6 17.8 %collective-permute-start.10 = (bf16[129,16,128]{2,1,0:T(8,128)(2,1)}, bf16[129,16,128]{2,1,0:T(8,128)(2,1)S(1)}, u32[]{:S(2)}, u32[]{:S(2)}) collective-permute-start(bf16[129,16,128]{2,1,0:T(8,128)(2,1)} %get-tuple-element.26), channel_id=1, source_target_pairs={{0,2},{1,3},{2,0},{3,1},{4,6},{5,7},{6,4},{7,5},{8,10},{9,11},{10,... | collective-permute-start | bytes 1585160 | tf_op jit(solution)/shard_map/ppermute | solution.py:44
  18.1 26.0 %collective-permute-start.6 = (bf16[32,64,128]{2,1,0:T(8,128)(2,1)}, bf16[32,64,128]{2,1,0:T(8,128)(2,1)S(1)}, u32[]{:S(2)}, u32[]{:S(2)}) collective-permute-start(bf16[32,64,128]{2,1,0:T(8,128)(2,1)} %get-tuple-element.45.refs_4_.refs_8_.refs_13_.refs_15_.refs_17_), channel_id=1, source_target_pairs={{0,4},{1,5},{2,6},{3,7},{4,0},{5,1},{6,2},{7,3},{8,12},{9,13},{10,... | collective-permute-start | bytes 1572872 | tf_op jit(solution)/shard_map/ppermute | solution.py:44
  31.5 38.8 %collective-permute-start.15 = (bf16[129,16,128]{2,1,0:T(8,128)(2,1)}, bf16[129,16,128]{2,1,0:T(8,128)(2,1)S(1)}, u32[]{:S(2)}, u32[]{:S(2)}) collective-permute-start(bf16[129,16,128]{2,1,0:T(8,128)(2,1)} %get-tuple-element.29), channel_id=1, source_target_pairs={{0,8},{1,9},{2,10},{3,11},{4,12},{5,13},{6,14},{7,15},{8,0},{9,1},... | collective-permute-start | bytes 1585160 | tf_op jit(solution)/shard_map/ppermute | solution.py:44
  31.5 49.3 %collective-permute-start.3 = (bf16[129,16,128]{2,1,0:T(8,128)(2,1)}, bf16[129,16,128]{2,1,0:T(8,128)(2,1)S(1)}, u32[]{:S(2)}, u32[]{:S(2)}) collective-permute-start(bf16[129,16,128]{2,1,0:T(8,128)(2,1)} %get-tuple-element.25), channel_id=1, source_target_pairs={{0,10},{1,11},{2,8},{3,9},{4,14},{5,15},{6,12},{7,13},{8,2},{9,3},... | collective-permute-start | bytes 1585160 | tf_op jit(solution)/shard_map/ppermute | solution.py:44
  35.4 46.8 %collective-permute-start.12 = (bf16[129,16,128]{2,1,0:T(8,128)(2,1)}, bf16[129,16,128]{2,1,0:T(8,128)(2,1)S(1)}, u32[]{:S(2)}, u32[]{:S(2)}) collective-permute-start(bf16[129,16,128]{2,1,0:T(8,128)(2,1)} %get-tuple-element.27), channel_id=1, source_target_pairs={{0,4},{1,5},{2,6},{3,7},{4,0},{5,1},{6,2},{7,3},{8,12},{9,13},{10,... | collective-permute-start | bytes 1585160 | tf_op jit(solution)/shard_map/ppermute | solution.py:44
  44.1 38.0 %copy-start.7 = (bf16[32,64,128]{2,1,0:T(8,128)(2,1)}, bf16[32,64,128]{2,1,0:T(8,128)(2,1)S(1)}, u32[]{:S(2)}) copy-start(bf16[32,64,128]{2,1,0:T(8,128)(2,1)S(1)} %collective-permute-done.6.refs_0_) | copy-start | bytes 1572868
  44.1 43.2 %collective-permute-start.11 = (bf16[32,64,128]{2,1,0:T(8,128)(2,1)}, bf16[32,64,128]{2,1,0:T(8,128)(2,1)S(1)}, u32[]{:S(2)}, u32[]{:S(2)}) collective-permute-start(bf16[32,64,128]{2,1,0:T(8,128)(2,1)} %shard_map.71.refs_6_.refs_21_.refs_23_.refs_25_), channel_id=1, source_target_pairs={{0,4},{1,5},{2,6},{3,7},{4,0},{5,1},{6,2},{7,3},{8,12},{9,13},{10,... | collective-permute-start | bytes 1572872 | tf_op jit(solution)/shard_map/ppermute | solution.py:44
  70.3 11.9 %copy-start.3 = (bf16[129,16,128]{2,1,0:T(8,128)(2,1)}, bf16[129,16,128]{2,1,0:T(8,128)(2,1)S(1)}, u32[]{:S(2)}) copy-start(bf16[129,16,128]{2,1,0:T(8,128)(2,1)S(1)} %collective-permute-done.15.refs_1_.refs_5_) | copy-start | bytes 1585156
  70.3 19.5 %collective-permute-start.23 = (bf16[32,64,128]{2,1,0:T(8,128)(2,1)}, bf16[32,64,128]{2,1,0:T(8,128)(2,1)S(1)}, u32[]{:S(2)}, u32[]{:S(2)}) collective-permute-start(bf16[32,64,128]{2,1,0:T(8,128)(2,1)} %shard_map.71.refs_6_.refs_21_.refs_23_.refs_25_), channel_id=1, source_target_pairs={{0,1},{1,0},{2,3},{3,2},{4,5},{5,4},{6,7},{7,6},{8,9},{9,8},{10,11... | collective-permute-start | bytes 1572872 | tf_op jit(solution)/shard_map/ppermute | solution.py:44
  80.8 15.0 %collective-permute-start.19 = (bf16[32,64,128]{2,1,0:T(8,128)(2,1)}, bf16[32,64,128]{2,1,0:T(8,128)(2,1)}, u32[]{:S(2)}, u32[]{:S(2)}) collective-permute-start(bf16[32,64,128]{2,1,0:T(8,128)(2,1)} %shard_map.71.refs_6_.refs_21_.refs_23_.refs_25_), channel_id=1, source_target_pairs={{0,2},{1,3},{2,0},{3,1},{4,6},{5,7},{6,4},{7,5},{8,10},{9,11},{10,... | collective-permute-start | bytes 1572872 | tf_op jit(solution)/shard_map/ppermute | solution.py:44
  82.2 20.3 %collective-permute-start.22 = (bf16[32,64,128]{2,1,0:T(8,128)(2,1)}, bf16[32,64,128]{2,1,0:T(8,128)(2,1)S(1)}, u32[]{:S(2)}, u32[]{:S(2)}) collective-permute-start(bf16[32,64,128]{2,1,0:T(8,128)(2,1)} %collective-permute-done.21.refs_6_.refs_15_.refs_17_.refs_19_), channel_id=1, source_target_pairs={{0,1},{1,0},{2,3},{3,2},{4,5},{5,4},{6,7},{7,6},{8,9},{9,8},{10,11... | collective-permute-start | bytes 1572872 | tf_op jit(solution)/shard_map/ppermute | solution.py:44
  87.3 24.1 %collective-permute-start.17 = (bf16[32,64,128]{2,1,0:T(8,128)(2,1)S(1)}, bf16[32,64,128]{2,1,0:T(8,128)(2,1)}, u32[]{:S(2)}, u32[]{:S(2)}) collective-permute-start(bf16[32,64,128]{2,1,0:T(8,128)(2,1)S(1)} %copy-done.8), channel_id=1, source_target_pairs={{0,1},{1,0},{2,3},{3,2},{4,5},{5,4},{6,7},{7,6},{8,9},{9,8},{10,11... | collective-permute-start | bytes 1572872 | tf_op jit(solution)/shard_map/ppermute | solution.py:44
  88.2 23.4 %collective-permute-start.7 = (bf16[32,64,128]{2,1,0:T(8,128)(2,1)S(1)}, bf16[32,64,128]{2,1,0:T(8,128)(2,1)}, u32[]{:S(2)}, u32[]{:S(2)}) collective-permute-start(bf16[32,64,128]{2,1,0:T(8,128)(2,1)S(1)} %copy-done.8), channel_id=1, source_target_pairs={{0,2},{1,3},{2,0},{3,1},{4,6},{5,7},{6,4},{7,5},{8,10},{9,11},{10,... | collective-permute-start | bytes 1572872 | tf_op jit(solution)/shard_map/ppermute | solution.py:44
  89.7 23.8 %collective-permute-start.16 = (bf16[129,16,128]{2,1,0:T(8,128)(2,1)S(1)}, bf16[129,16,128]{2,1,0:T(8,128)(2,1)S(1)}, u32[]{:S(2)}, u32[]{:S(2)}) collective-permute-start(bf16[129,16,128]{2,1,0:T(8,128)(2,1)S(1)} %copy-done.5), channel_id=1, source_target_pairs={{0,12},{1,13},{2,14},{3,15},{4,8},{5,9},{6,10},{7,11},{8,4},{9,5},... | collective-permute-start | bytes 1585160 | tf_op jit(solution)/shard_map/ppermute | solution.py:44
  95.8 7.4 %collective-permute-start.20 = (bf16[32,64,128]{2,1,0:T(8,128)(2,1)}, bf16[32,64,128]{2,1,0:T(8,128)(2,1)S(1)}, u32[]{:S(2)}, u32[]{:S(2)}) collective-permute-start(bf16[32,64,128]{2,1,0:T(8,128)(2,1)} %collective-permute-done.19.refs_4_.refs_23_.refs_25_.refs_27_), channel_id=1, source_target_pairs={{0,1},{1,0},{2,3},{3,2},{4,5},{5,4},{6,7},{7,6},{8,9},{9,8},{10,11... | collective-permute-start | bytes 1572872 | tf_op jit(solution)/shard_map/ppermute | solution.py:44
  102.6 25.9 %collective-permute-start.18 = (bf16[32,64,128]{2,1,0:T(8,128)(2,1)S(1)}, bf16[32,64,128]{2,1,0:T(8,128)(2,1)}, u32[]{:S(2)}, u32[]{:S(2)}) collective-permute-start(bf16[32,64,128]{2,1,0:T(8,128)(2,1)S(1)} %copy-done.10), channel_id=1, source_target_pairs={{0,1},{1,0},{2,3},{3,2},{4,5},{5,4},{6,7},{7,6},{8,9},{9,8},{10,11... | collective-permute-start | bytes 1572872 | tf_op jit(solution)/shard_map/ppermute | solution.py:44
  103.2 25.4 %collective-permute-start.13 = (bf16[32,64,128]{2,1,0:T(8,128)(2,1)S(1)}, bf16[32,64,128]{2,1,0:T(8,128)(2,1)}, u32[]{:S(2)}, u32[]{:S(2)}) collective-permute-start(bf16[32,64,128]{2,1,0:T(8,128)(2,1)S(1)} %copy-done.10), channel_id=1, source_target_pairs={{0,2},{1,3},{2,0},{3,1},{4,6},{5,7},{6,4},{7,5},{8,10},{9,11},{10,... | collective-permute-start | bytes 1572872 | tf_op jit(solution)/shard_map/ppermute | solution.py:44
  111.5 24.4 %collective-permute-start.2 = (bf16[129,16,128]{2,1,0:T(8,128)(2,1)S(1)}, bf16[129,16,128]{2,1,0:T(8,128)(2,1)S(1)}, u32[]{:S(2)}, u32[]{:S(2)}) collective-permute-start(bf16[129,16,128]{2,1,0:T(8,128)(2,1)S(1)} %copy-done.20), channel_id=1, source_target_pairs={{0,6},{1,7},{2,4},{3,5},{4,2},{5,3},{6,0},{7,1},{8,14},{9,15},{10,... | collective-permute-start | bytes 1585160 | tf_op jit(solution)/shard_map/ppermute | solution.py:44
  111.6 32.6 %collective-permute-start.4 = (bf16[129,16,128]{2,1,0:T(8,128)(2,1)S(1)}, bf16[129,16,128]{2,1,0:T(8,128)(2,1)S(1)}, u32[]{:S(2)}, u32[]{:S(2)}) collective-permute-start(bf16[129,16,128]{2,1,0:T(8,128)(2,1)S(1)} %copy-done.6), channel_id=1, source_target_pairs={{0,14},{1,15},{2,12},{3,13},{4,10},{5,11},{6,8},{7,9},{8,6},{9,7},... | collective-permute-start | bytes 1585160 | tf_op jit(solution)/shard_map/ppermute | solution.py:44
  113.6 14.9 %copy-start.17 = (bf16[129,16,128]{2,1,0:T(8,128)(2,1)}, bf16[129,16,128]{2,1,0:T(8,128)(2,1)S(1)}, u32[]{:S(2)}) copy-start(bf16[129,16,128]{2,1,0:T(8,128)(2,1)S(1)} %collective-permute-done.16.refs_1_.refs_7_) | copy-start | bytes 1585156
  113.6 30.6 %collective-permute-start.8 = (bf16[32,64,128]{2,1,0:T(8,128)(2,1)}, bf16[32,64,128]{2,1,0:T(8,128)(2,1)S(1)}, u32[]{:S(2)}, u32[]{:S(2)}) collective-permute-start(bf16[32,64,128]{2,1,0:T(8,128)(2,1)} %collective-permute-done.7.refs_4_.refs_19_.refs_21_.refs_23_), channel_id=1, source_target_pairs={{0,1},{1,0},{2,3},{3,2},{4,5},{5,4},{6,7},{7,6},{8,9},{9,8},{10,11... | collective-permute-start | bytes 1572872 | tf_op jit(solution)/shard_map/ppermute | solution.py:44
  128.5 15.6 %collective-permute-start.14 = (bf16[32,64,128]{2,1,0:T(8,128)(2,1)}, bf16[32,64,128]{2,1,0:T(8,128)(2,1)}, u32[]{:S(2)}, u32[]{:S(2)}) collective-permute-start(bf16[32,64,128]{2,1,0:T(8,128)(2,1)} %collective-permute-done.13.refs_6_.refs_27_.refs_29_.refs_31_), channel_id=1, source_target_pairs={{0,1},{1,0},{2,3},{3,2},{4,5},{5,4},{6,7},{7,6},{8,9},{9,8},{10,11... | collective-permute-start | bytes 1572872 | tf_op jit(solution)/shard_map/ppermute | solution.py:44
  152.2 2.6 %collective-permute-start.24 = (f32[16,128]{1,0:T(8,128)}, f32[16,128]{1,0:T(8,128)S(1)}, u32[]{:S(2)}, u32[]{:S(2)}) collective-permute-start(f32[16,128]{1,0:T(8,128)} %get-tuple-element.34), channel_id=1, source_target_pairs={{0,1},{1,0},{2,3},{3,2},{4,5},{5,4},{6,7},{7,6},{8,9},{9,8},{10,11... | collective-permute-start | bytes 24584 | tf_op jit(solution)/shard_map/ppermute | solution.py:118
  152.3 3.9 %collective-permute-start.25 = (f32[16,128]{1,0:T(8,128)}, f32[16,128]{1,0:T(8,128)S(1)}, u32[]{:S(2)}, u32[]{:S(2)}) collective-permute-start(f32[16,128]{1,0:T(8,128)} %get-tuple-element.34), channel_id=1, source_target_pairs={{0,2},{1,3},{2,0},{3,1},{4,6},{5,7},{6,4},{7,5},{8,10},{9,11},{10,... | collective-permute-start | bytes 24584 | tf_op jit(solution)/shard_map/ppermute | solution.py:118
  153.8 3.3 %collective-permute-start.26 = (f32[16,128]{1,0:T(8,128)}, f32[16,128]{1,0:T(8,128)S(1)}, u32[]{:S(2)}, u32[]{:S(2)}) collective-permute-start(f32[16,128]{1,0:T(8,128)} %get-tuple-element.34), channel_id=1, source_target_pairs={{0,3},{1,2},{2,1},{3,0},{4,7},{5,6},{6,5},{7,4},{8,11},{9,10},{10,... | collective-permute-start | bytes 24584 | tf_op jit(solution)/shard_map/ppermute | solution.py:118
  157.8 6.8 %collective-permute-start.27 = (f32[16,128]{1,0:T(8,128)S(1)}, f32[16,128]{1,0:T(8,128)S(1)}, u32[]{:S(2)}, u32[]{:S(2)}) collective-permute-start(f32[16,128]{1,0:T(8,128)S(1)} %add_add_fusion.1.refs_1_), channel_id=1, source_target_pairs={{0,4},{1,5},{2,6},{3,7},{4,0},{5,1},{6,2},{7,3},{8,12},{9,13},{10,... | collective-permute-start | bytes 24584 | tf_op jit(solution)/shard_map/ppermute | solution.py:118
  160.7 21.8 %collective-permute-start.32 = (bf16[32,64,128]{2,1,0:T(8,128)(2,1)}, bf16[32,64,128]{2,1,0:T(8,128)(2,1)S(1)}, u32[]{:S(2)}, u32[]{:S(2)}) collective-permute-start(bf16[32,64,128]{2,1,0:T(8,128)(2,1)} %shard_map.79.refs_11_), channel_id=1, source_target_pairs={{0,1},{1,0},{2,3},{3,2},{4,5},{5,4},{6,7},{7,6},{8,9},{9,8},{10,11... | collective-permute-start | bytes 1572872 | tf_op jit(solution)/shard_map/ppermute | solution.py:44
  160.7 19.5 %collective-permute-start.30 = (bf16[32,64,128]{2,1,0:T(8,128)(2,1)}, bf16[32,64,128]{2,1,0:T(8,128)(2,1)S(1)}, u32[]{:S(2)}, u32[]{:S(2)}) collective-permute-start(bf16[32,64,128]{2,1,0:T(8,128)(2,1)} %shard_map.79.refs_11_), channel_id=1, source_target_pairs={{0,4},{1,5},{2,0},{3,1},{4,8},{5,9},{6,2},{7,3},{8,12},{9,13},{10,... | collective-permute-start | bytes 1572872 | tf_op jit(solution)/shard_map/ppermute | solution.py:44
  161.5 19.3 %collective-permute-start.35 = (bf16[32,64,128]{2,1,0:T(8,128)(2,1)}, bf16[32,64,128]{2,1,0:T(8,128)(2,1)S(1)}, u32[]{:S(2)}, u32[]{:S(2)}) collective-permute-start(bf16[32,64,128]{2,1,0:T(8,128)(2,1)} %shard_map.79.refs_11_), channel_id=1, source_target_pairs={{0,2},{1,3},{2,6},{3,7},{4,0},{5,1},{6,10},{7,11},{8,4},{9,5},{10,... | collective-permute-start | bytes 1572872 | tf_op jit(solution)/shard_map/ppermute | solution.py:44
  163.4 13.0 %collective-permute-start.28 = (f32[16,128]{1,0:T(8,128)}, f32[16,128]{1,0:T(8,128)S(1)}, u32[]{:S(2)}, u32[]{:S(2)}) collective-permute-start(f32[16,128]{1,0:T(8,128)} %copy-done.12), channel_id=1, source_target_pairs={{0,8},{1,9},{2,10},{3,11},{4,12},{5,13},{6,14},{7,15},{8,0},{9,1},... | collective-permute-start | bytes 24584 | tf_op jit(solution)/shard_map/ppermute | solution.py:118
  164.6 12.6 %collective-permute-start.29 = (f32[16,128]{1,0:T(8,128)}, f32[16,128]{1,0:T(8,128)S(1)}, u32[]{:S(2)}, u32[]{:S(2)}) collective-permute-start(f32[16,128]{1,0:T(8,128)} %copy-done.12), channel_id=1, source_target_pairs={{0,12},{1,13},{2,14},{3,15},{4,8},{5,9},{6,10},{7,11},{8,4},{9,5},... | collective-permute-start | bytes 24584 | tf_op jit(solution)/shard_map/ppermute | solution.py:118
  180.2 15.9 %collective-permute-start.34 = (bf16[32,64,128]{2,1,0:T(8,128)(2,1)S(1)}, bf16[32,64,128]{2,1,0:T(8,128)(2,1)S(1)}, u32[]{:S(2)}, u32[]{:S(2)}) collective-permute-start(bf16[32,64,128]{2,1,0:T(8,128)(2,1)S(1)} %collective-permute-done.30.refs_11_), channel_id=1, source_target_pairs={{0,1},{1,0},{2,3},{3,2},{4,5},{5,4},{6,7},{7,6},{8,9},{9,8},{10,11... | collective-permute-start | bytes 1572872 | tf_op jit(solution)/shard_map/ppermute | solution.py:44
  180.2 14.3 %collective-permute-start.31 = (bf16[32,64,128]{2,1,0:T(8,128)(2,1)S(1)}, bf16[32,64,128]{2,1,0:T(8,128)(2,1)S(1)}, u32[]{:S(2)}, u32[]{:S(2)}) collective-permute-start(bf16[32,64,128]{2,1,0:T(8,128)(2,1)S(1)} %collective-permute-done.30.refs_11_), channel_id=1, source_target_pairs={{0,4},{1,5},{2,0},{3,1},{4,8},{5,9},{6,2},{7,3},{8,12},{9,13},{10,... | collective-permute-start | bytes 1572872 | tf_op jit(solution)/shard_map/ppermute | solution.py:44
  180.8 16.9 %collective-permute-start.36 = (bf16[32,64,128]{2,1,0:T(8,128)(2,1)S(1)}, bf16[32,64,128]{2,1,0:T(8,128)(2,1)}, u32[]{:S(2)}, u32[]{:S(2)}) collective-permute-start(bf16[32,64,128]{2,1,0:T(8,128)(2,1)S(1)} %collective-permute-done.35.refs_13_), channel_id=1, source_target_pairs={{0,1},{1,0},{2,3},{3,2},{4,5},{5,4},{6,7},{7,6},{8,9},{9,8},{10,11... | collective-permute-start | bytes 1572872 | tf_op jit(solution)/shard_map/ppermute | solution.py:44
  180.9 14.9 %collective-permute-start.38 = (bf16[32,64,128]{2,1,0:T(8,128)(2,1)S(1)}, bf16[32,64,128]{2,1,0:T(8,128)(2,1)S(1)}, u32[]{:S(2)}, u32[]{:S(2)}) collective-permute-start(bf16[32,64,128]{2,1,0:T(8,128)(2,1)S(1)} %collective-permute-done.35.refs_13_), channel_id=1, source_target_pairs={{0,2},{1,3},{2,6},{3,7},{4,0},{5,1},{6,10},{7,11},{8,4},{9,5},{10,... | collective-permute-start | bytes 1572872 | tf_op jit(solution)/shard_map/ppermute | solution.py:44
  195.3 18.5 %collective-permute-start.42 = (bf16[32,64,128]{2,1,0:T(8,128)(2,1)}, bf16[32,64,128]{2,1,0:T(8,128)(2,1)S(1)}, u32[]{:S(2)}, u32[]{:S(2)}) collective-permute-start(bf16[32,64,128]{2,1,0:T(8,128)(2,1)} %shard_map.81.refs_11_), channel_id=1, source_target_pairs={{0,1},{1,0},{2,3},{3,2},{4,5},{5,4},{6,7},{7,6},{8,9},{9,8},{10,11... | collective-permute-start | bytes 1572872 | tf_op jit(solution)/shard_map/ppermute | solution.py:44
  195.3 14.7 %collective-permute-start.33 = (bf16[32,64,128]{2,1,0:T(8,128)(2,1)}, bf16[32,64,128]{2,1,0:T(8,128)(2,1)}, u32[]{:S(2)}, u32[]{:S(2)}) collective-permute-start(bf16[32,64,128]{2,1,0:T(8,128)(2,1)} %shard_map.81.refs_11_), channel_id=1, source_target_pairs={{0,4},{1,5},{2,0},{3,1},{4,8},{5,9},{6,2},{7,3},{8,12},{9,13},{10,... | collective-permute-start | bytes 1572872 | tf_op jit(solution)/shard_map/ppermute | solution.py:44
  195.8 18.0 %collective-permute-start.43 = (bf16[32,64,128]{2,1,0:T(8,128)(2,1)S(1)}, bf16[32,64,128]{2,1,0:T(8,128)(2,1)}, u32[]{:S(2)}, u32[]{:S(2)}) collective-permute-start(bf16[32,64,128]{2,1,0:T(8,128)(2,1)S(1)} %collective-permute-done.38.refs_13_), channel_id=1, source_target_pairs={{0,1},{1,0},{2,3},{3,2},{4,5},{5,4},{6,7},{7,6},{8,9},{9,8},{10,11... | collective-permute-start | bytes 1572872 | tf_op jit(solution)/shard_map/ppermute | solution.py:44
  196.1 14.1 %collective-permute-start.39 = (bf16[32,64,128]{2,1,0:T(8,128)(2,1)S(1)}, bf16[32,64,128]{2,1,0:T(8,128)(2,1)S(1)}, u32[]{:S(2)}, u32[]{:S(2)}) collective-permute-start(bf16[32,64,128]{2,1,0:T(8,128)(2,1)S(1)} %collective-permute-done.38.refs_13_), channel_id=1, source_target_pairs={{0,2},{1,3},{2,6},{3,7},{4,0},{5,1},{6,10},{7,11},{8,4},{9,5},{10,... | collective-permute-start | bytes 1572872 | tf_op jit(solution)/shard_map/ppermute | solution.py:44
  210.0 15.2 %collective-permute-start.37 = (bf16[32,64,128]{2,1,0:T(8,128)(2,1)}, bf16[32,64,128]{2,1,0:T(8,128)(2,1)S(1)}, u32[]{:S(2)}, u32[]{:S(2)}) collective-permute-start(bf16[32,64,128]{2,1,0:T(8,128)(2,1)} %shard_map.83.lower_ref.refs_11_), channel_id=1, source_target_pairs={{0,1},{1,0},{2,3},{3,2},{4,5},{5,4},{6,7},{7,6},{8,9},{9,8},{10,11... | collective-permute-start | bytes 1572872 | tf_op jit(solution)/shard_map/ppermute | solution.py:44
  213.1 10.5 %collective-permute-start.41 = (bf16[32,64,128]{2,1,0:T(8,128)(2,1)}, bf16[32,64,128]{2,1,0:T(8,128)(2,1)S(1)}, u32[]{:S(2)}, u32[]{:S(2)}) collective-permute-start(bf16[32,64,128]{2,1,0:T(8,128)(2,1)} %shard_map.84), channel_id=1, source_target_pairs={{0,4},{1,3},{2,0},{3,7},{4,8},{5,1},{6,2},{7,11},{8,12},{9,5},{10,... | collective-permute-start | bytes 1572872 | tf_op jit(solution)/shard_map/ppermute | solution.py:44
  213.4 11.8 %collective-permute-start.40 = (bf16[32,64,128]{2,1,0:T(8,128)(2,1)}, bf16[32,64,128]{2,1,0:T(8,128)(2,1)S(1)}, u32[]{:S(2)}, u32[]{:S(2)}) collective-permute-start(bf16[32,64,128]{2,1,0:T(8,128)(2,1)} %copy-done.25), channel_id=1, source_target_pairs={{0,1},{1,0},{2,3},{3,2},{4,5},{5,4},{6,7},{7,6},{8,9},{9,8},{10,11... | collective-permute-start | bytes 1572872 | tf_op jit(solution)/shard_map/ppermute | solution.py:44
  224.5 2.1 collective-permute-start.44
  (35 other events, 126.3 us)

commit v12 on v11

--- a/solution.py
+++ b/solution.py
@@ -217,11 +217,8 @@
         moved.append(product.astype(jnp.bfloat16))
         where.append(labels[1, at])
     for slot in range(terms * capacity):
-        target = where[slot]
-        total[target] += jnp.dot(
-            moved[slot],
-            right[slot // capacity, jnp.minimum(target, blocks - 1)],
-            preferred_element_type=jnp.float32,
+        total[where[slot]] += jnp.dot(
+            moved[slot], right[slot], preferred_element_type=jnp.float32
         )
 
 
@@ -313,8 +310,18 @@
             for part in range(2)
         ]
 
-    def right_copy(side):
-        return pltpu.make_async_copy(rights[side], right.at[side], right_sems.at[side])
+    def load_right(source, side):
+        for slot in range(terms * capacity):
+            target = jnp.minimum(labels[source, 1, side * terms * capacity + slot], blocks - 1)
+            pltpu.make_async_copy(
+                rights[side].at[slot // capacity, target],
+                right.at[source, side, slot],
+                right_sems.at[source, side],
+            ).start()
+
+    def wait_right(source, side):
+        whole = right.at[source, side]
+        pltpu.make_async_copy(whole, whole, right_sems.at[source, side]).wait()
 
     for source in range(sources):
         if choices:
@@ -328,12 +335,9 @@
         else:
             for copy in left_copies(source, lefts[source]):
                 copy.start()
-    for copy in [*vector_copies(0), right_copy(0)]:
-        copy.start()
-    for source in range(1, sources):
+    for source in range(sources):
         for copy in vector_copies(source):
             copy.start()
-    right_copy(1).start()
     if first:
         total[...] = jnp.zeros_like(total)
     else:
@@ -351,11 +355,13 @@
     move_labels = pltpu.make_async_copy(spread_labels, labels, label_sem)
     move_labels.start()
     move_labels.wait()
+    for source in range(sources):
+        for side in range(2):
+            load_right(source, side)
     if not first:
         load_total.wait()
-    for side in range(2):
-        right_copy(side).wait()
-        for source in range(sources):
+    for source in range(sources):
+        for side in range(2):
             if side == 0:
                 left_copies(source, lefts[0])[1].wait()
                 for copy in vector_copies(source):
@@ -365,11 +371,12 @@
                         copy.wait()
                     chip = lax.div(ids_ref[1], 2) ^ ids_ref[2 + source]
                     form_direction(vector.at[source], wave.at[source], scale, chip)
+            wait_right(source, side)
             add_products(
                 left.at[source],
                 labels.at[source],
                 vector.at[source],
-                right.at[side],
+                right.at[source, side],
                 total,
                 side,
                 terms,
@@ -401,13 +408,13 @@
     scratch = [
         pltpu.VMEM(total_shape, jnp.float32),
         pltpu.VMEM((sources, parts, PART, width), jnp.bfloat16),
-        pltpu.VMEM((2,) + rights[0].shape, jnp.bfloat16),
+        pltpu.VMEM((sources, 2, terms * capacity, width, width), jnp.bfloat16),
         pltpu.VMEM((sources, 2, blocks, rows, width), jnp.bfloat16),
         pltpu.VMEM((sources, PART, width), jnp.bfloat16),
         pltpu.VMEM((sources, 8, width), jnp.int32),
         pltpu.SMEM((sources, 8, width), jnp.int32),
         pltpu.SemaphoreType.DMA((sources,)),
-        pltpu.SemaphoreType.DMA((2,)),
+        pltpu.SemaphoreType.DMA((sources, 2)),
         pltpu.SemaphoreType.DMA((sources, 2)),
         pltpu.SemaphoreType.DMA((sources,)),
         pltpu.SemaphoreType.DMA,
@@ -537,19 +544,22 @@
         )
 
     total = token = None
-    ready = [{0: rest}]
+    units = {0: rest}
+    waiting = {}
     ahead = behind = rest
     for step in range(1, reach + 1):
         ahead = ring_send(ahead, owners, halves, (1,) * halves)
         behind = ring_send(behind, owners, halves, (-1,) * halves)
-        if step > 1:
-            total, token = add_group(total, ready.pop(0), "go on")
+        if step == reach:
+            total, token = add_group(total, waiting, "go on")
+            waiting = {}
             ahead = after(ahead, token)
-        ready.append({step: ahead, -step: behind})
+        waiting.update(units)
+        units = {step: ahead, -step: behind}
     last = ring_send(select_half(half, ahead, behind), owners, halves, (1, -1))
-    total, token = add_group(total, ready.pop(0), "go on")
+    total, token = add_group(total, waiting, "go on")
     last = after(last, token)
-    total = add_group(total, {**ready.pop(0), owners // 2: last}, "result")
+    total = add_group(total, {**units, owners // 2: last}, "result")
     return (total, rayleigh[0])
 
 

time: 239 us -> 233 us (0.975)
  Pallas kernels: 72.4 us -> 67.6 us
  local copies, waits for them, and re-layouts: 11.6 us -> 8.29 us
    ppermute x39, waiting for transfers between devices: 97.3 us -> 108 us  [permute(): return lax.ppermute(value, BOTH, pairs)]
    ppermute x6, waiting for transfers between devices: 12.4 us -> 3.67 us  [spread(): lax.ppermute(value, BOTH, [(d, d ^ m) for d in range(devices)])]
    pallas_call x8 -> x7, Pallas kernels: 63.1 us -> 58.4 us  [apply_group(): pl.pallas_call(functools.partial(apply_kernel, sources, choices, first, e...]
    unnamed x76 -> x66, local copies, waits for them, and re-layouts: 8.45 us -> 4.56 us
    ppermute x39, starting transfers between devices: 29.8 us -> 33 us  [permute(): return lax.ppermute(value, BOTH, pairs)]
  transfers between devices with their start and end apart: 45 -> 45, of which waited for: 17 -> 18; matrix products, arithmetic and copies ran while one was open for 3% -> 2% of each run, Pallas kernels for 23% -> 22%
where the time goes in v12:
time: 233 us; the launch traced here: 232 us
  waiting for transfers between devices  111 us (48%)
  Pallas kernels  67.6 us (29%)
  starting transfers between devices  39.7 us (17%)
  local copies, waits for them, and re-layouts  8.29 us (4%)
  other arithmetic  3.73 us (2%)
    ppermute x39, waiting for transfers between devices, permute(): return lax.ppermute(value, BOTH, pairs)  108 us
    pallas_call x7, Pallas kernels, apply_group(): pl.pallas_call(functools.partial(apply_kernel, sources, choices, first, e...  58.4 us
    ppermute x39, starting transfers between devices, permute(): return lax.ppermute(value, BOTH, pairs)  33 us
    ppermute x6, starting transfers between devices, spread(): lax.ppermute(value, BOTH, [(d, d ^ m) for d in range(devices)])  6.7 us
    pallas_call x1, Pallas kernels, pack(): pl.pallas_call(functools.partial(pack_kernel, order, capacity, blocks, te...  5.41 us
  transfers between devices with their start and end apart: 45, of which 18 were waited for; matrix products, arithmetic and copies ran while one was open for 2% of the time, Pallas kernels for 22%

profile of v12, /device:TPU:0, one launch (start us, length us, event | category | flops | bytes accessed | tf_op | source)
XLA Modules:
  0.0 231.8 jit_solution(15800666236176476692)
XLA Ops:
  0.6 1.4 constant_dynamic-slice_fusion.2
  2.7 1.1 constant_dynamic-slice_fusion
  3.8 4.0 %collective-permute-start.9 = (bf16[32,64,128]{2,1,0:T(8,128)(2,1)}, bf16[32,64,128]{2,1,0:T(8,128)(2,1)S(1)}, u32[]{:S(2)}, u32[]{:S(2)}) collective-permute-start(bf16[32,64,128]{2,1,0:T(8,128)(2,1)} %get-tuple-element.41.refs_4_.refs_8_.refs_17_.refs_15_), channel_id=1, source_target_pairs={{0,8},{1,9},{2,10},{3,11},{4,12},{5,13},{6,14},{7,15},{8,0},{9,1},... | collective-permute-start | bytes 1572872 | tf_op jit(solution)/shard_map/ppermute | solution.py:44
  7.8 1.5 collective-permute-start.21
  11.1 5.4 %shard_map.68 = (bf16[129,16,128]{2,1,0:T(8,128)(2,1)}, bf16[129,16,128]{2,1,0:T(8,128)(2,1)}, bf16[129,16,128]{2,1,0:T(8,128)(2,1)}, bf16[129,16,128]{2,1,0:T(8...) custom-call(s32[2]{0:T(128)} %pad_add_fusion.2.ids_ref, ...), custom_call_target="tpu_custom_call" | custom-call | flops 5750000128 | tf_op jit(solution)/shard_map/pallas_call | solution.py:186
  17.1 1.6 collective-permute-start.6
  18.7 12.8 %collective-permute-done.9.refs_0_ = bf16[32,64,128]{2,1,0:T(8,128)(2,1)S(1)} collective-permute-done((bf16[32,64,128]{2,1,0:T(8,128)(2,1)}, bf16[32,64,128]{2,1,0:T(8,128)(2,1)S(1)}, u32[]{:S(2)}, u32[]{:S(2)}) %collective-permute-start.9) | collective-permute-done | bytes 524320 | tf_op jit(solution)/shard_map/ppermute | solution.py:44
  31.5 3.9 %collective-permute-start.3 = (bf16[129,16,128]{2,1,0:T(8,128)(2,1)}, bf16[129,16,128]{2,1,0:T(8,128)(2,1)S(1)}, u32[]{:S(2)}, u32[]{:S(2)}) collective-permute-start(bf16[129,16,128]{2,1,0:T(8,128)(2,1)} %get-tuple-element.23), channel_id=1, source_target_pairs={{0,10},{1,11},{2,8},{3,9},{4,14},{5,15},{6,12},{7,13},{8,2},{9,3},... | collective-permute-start | bytes 1585160 | tf_op jit(solution)/shard_map/ppermute | solution.py:44
  35.4 1.2 collective-permute-start.12
  36.6 7.0 %collective-permute-done.6.refs_0_ = bf16[32,64,128]{2,1,0:T(8,128)(2,1)S(1)} collective-permute-done((bf16[32,64,128]{2,1,0:T(8,128)(2,1)}, bf16[32,64,128]{2,1,0:T(8,128)(2,1)S(1)}, u32[]{:S(2)}, u32[]{:S(2)}) %collective-permute-start.6) | collective-permute-done | bytes 524320 | tf_op jit(solution)/shard_map/ppermute | solution.py:44
  43.6 26.6 %collective-permute-done.15.refs_1_.refs_5_ = bf16[129,16,128]{2,1,0:T(8,128)(2,1)S(1)} collective-permute-done((bf16[129,16,128]{2,1,0:T(8,128)(2,1)}, bf16[129,16,128]{2,1,0:T(8,128)(2,1)S(1)}, u32[]{:S(2)}, u32[]{:S(2)}) %collective-permute-start.15) | collective-permute-done | bytes 528416 | tf_op jit(solution)/shard_map/ppermute | solution.py:44
  70.3 10.5 %collective-permute-done.3.refs_1_.refs_0_.refs_6_ = bf16[129,16,128]{2,1,0:T(8,128)(2,1)S(1)} collective-permute-done((bf16[129,16,128]{2,1,0:T(8,128)(2,1)}, bf16[129,16,128]{2,1,0:T(8,128)(2,1)S(1)}, u32[]{:S(2)}, u32[]{:S(2)}) %collective-permute-start.3) | collective-permute-done | bytes 528416 | tf_op jit(solution)/shard_map/ppermute | solution.py:44
  80.8 0.8 collective-permute-start.19
  82.3 4.0 %collective-permute-done.11.refs_0_ = bf16[32,64,128]{2,1,0:T(8,128)(2,1)S(1)} collective-permute-done((bf16[32,64,128]{2,1,0:T(8,128)(2,1)}, bf16[32,64,128]{2,1,0:T(8,128)(2,1)S(1)}, u32[]{:S(2)}, u32[]{:S(2)}) %collective-permute-start.11) | collective-permute-done | bytes 524320 | tf_op jit(solution)/shard_map/ppermute | solution.py:44
  86.3 0.8 copy-done.10
  87.2 1.6 collective-permute-start.7
  88.7 3.3 %collective-permute-start.16 = (bf16[129,16,128]{2,1,0:T(8,128)(2,1)S(1)}, bf16[129,16,128]{2,1,0:T(8,128)(2,1)S(1)}, u32[]{:S(2)}, u32[]{:S(2)}) collective-permute-start(bf16[129,16,128]{2,1,0:T(8,128)(2,1)S(1)} %copy-done.5), channel_id=1, source_target_pairs={{0,12},{1,13},{2,14},{3,15},{4,8},{5,9},{6,10},{7,11},{8,4},{9,5},... | collective-permute-start | bytes 1585160 | tf_op jit(solution)/shard_map/ppermute | solution.py:44
  92.0 4.0 %collective-permute-done.19.refs_4_.refs_27_.refs_25_ = bf16[32,64,128]{2,1,0:T(8,128)(2,1)} collective-permute-done((bf16[32,64,128]{2,1,0:T(8,128)(2,1)}, bf16[32,64,128]{2,1,0:T(8,128)(2,1)}, u32[]{:S(2)}, u32[]{:S(2)}) %collective-permute-start.19) | collective-permute-done | bytes 524320 | tf_op jit(solution)/shard_map/ppermute | solution.py:44
  96.0 7.6 %shard_map.74 = (f32[33,64,128]{2,1,0:T(8,128)}, f32[8,128]{1,0:T(8,128)}) custom-call(s32[2]{0:T(128)} %pad_add_fusion.1.ids_ref, bf16[129,16,128]{2,1,0:T(8,128)(2,1)} %get-tuple-element.28.refs_0_.refs_1_, bf16[129,16,128]{2,1,0:T(8,128)(2,1)} %copy-done.3, bf16[2,32,128,128]{3,2,1,0:T(8,128)(2,1)} %refs_9_.5, ...), custom_call_target="tpu_custom_call" | custom-call | flops 8165000192 | tf_op jit(solution)/shard_map/pallas_call | solution.py:443
  105.1 7.5 %shard_map.75 = (f32[33,64,128]{2,1,0:T(8,128)}, f32[8,128]{1,0:T(8,128)}) custom-call(s32[2]{0:T(128)} %pad_add_fusion.1.ids_ref, bf16[129,16,128]{2,1,0:T(8,128)(2,1)} %copy-done, bf16[129,16,128]{2,1,0:T(8,128)(2,1)} %copy-done.2, bf16[2,32,128,128]{3,2,1,0:T(8,128)(2,1)} %refs_9_.5, bf16[2,32,128,128]{3,2,1,0:T(8,128)(2,1)} %collective-permute-done.5.refs_3_.refs_10_, ...), custom_call_target="tpu_custom_call" | custom-call | flops 8165000192 | tf_op jit(solution)/shard_map/pallas_call | solution.py:443
  112.8 1.7 collective-permute-start.4
  114.4 15.2 %collective-permute-done.13.refs_6_.refs_31_.refs_29_ = bf16[32,64,128]{2,1,0:T(8,128)(2,1)} collective-permute-done((bf16[32,64,128]{2,1,0:T(8,128)(2,1)S(1)}, bf16[32,64,128]{2,1,0:T(8,128)(2,1)}, u32[]{:S(2)}, u32[]{:S(2)}) %collective-permute-start.13) | collective-permute-done | bytes 524320 | tf_op jit(solution)/shard_map/ppermute | solution.py:44
  129.7 7.3 %shard_map.76 = (f32[33,64,128]{2,1,0:T(8,128)}, f32[8,128]{1,0:T(8,128)}) custom-call(s32[2]{0:T(128)} %pad_add_fusion.1.ids_ref, bf16[129,16,128]{2,1,0:T(8,128)(2,1)} %copy-done.4, bf16[129,16,128]{2,1,0:T(8,128)(2,1)} %copy-done.16, bf16[2,32,128,128]{3,2,1,0:T(8,128)(2,1)} %refs_9_.5, bf16[2,32,128,128]{3,2,1,0:T(8,128)(2,1)} %collective-permute-done.5.refs_3_.refs_10_, ...), custom_call_target="tpu_custom_call" | custom-call | flops 8165000192 | tf_op jit(solution)/shard_map/pallas_call | solution.py:443
  137.0 8.0 %collective-permute-done.4.refs_1_.refs_8_ = bf16[129,16,128]{2,1,0:T(8,128)(2,1)S(1)} collective-permute-done((bf16[129,16,128]{2,1,0:T(8,128)(2,1)S(1)}, bf16[129,16,128]{2,1,0:T(8,128)(2,1)S(1)}, u32[]{:S(2)}, u32[]{:S(2)}) %collective-permute-start.4) | collective-permute-done | bytes 528416 | tf_op jit(solution)/shard_map/ppermute | solution.py:44
  145.1 0.8 copy-done.18
  146.0 7.2 %shard_map.77 = (bf16[32,64,128]{2,1,0:T(8,128)(2,1)}, f32[16,128]{1,0:T(8,128)}) custom-call(s32[2]{0:T(128)} %pad_add_fusion.1.ids_ref, bf16[129,16,128]{2,1,0:T(8,128)(2,1)} %copy-done.17, bf16[129,16,128]{2,1,0:T(8,128)(2,1)} %copy-done.18, bf16[2,32,128,128]{3,2,1,0:T(8,128)(2,1)} %refs_9_.5, ...), custom_call_target="tpu_custom_call" | custom-call | flops 8165000192 | tf_op jit(solution)/shard_map/pallas_call | solution.py:443
  153.3 2.1 collective-permute-start.25
  155.5 1.8 collective-permute-done.25
  157.3 1.4 collective-permute-done.26
  158.7 1.3 add_add_fusion.1.refs_1_
  160.0 2.9 %collective-permute-start.30 = (bf16[32,64,128]{2,1,0:T(8,128)(2,1)}, bf16[32,64,128]{2,1,0:T(8,128)(2,1)S(1)}, u32[]{:S(2)}, u32[]{:S(2)}) collective-permute-start(bf16[32,64,128]{2,1,0:T(8,128)(2,1)} %shard_map.79.refs_11_), channel_id=1, source_target_pairs={{0,4},{1,5},{2,0},{3,1},{4,8},{5,9},{6,2},{7,3},{8,12},{9,13},{10,... | collective-permute-start | bytes 1572872 | tf_op jit(solution)/shard_map/ppermute | solution.py:44
  163.0 2.0 collective-permute-start.27
  165.5 1.9 collective-permute-start.29
  167.4 7.7 %collective-permute-done.30.refs_13_ = bf16[32,64,128]{2,1,0:T(8,128)(2,1)S(1)} collective-permute-done((bf16[32,64,128]{2,1,0:T(8,128)(2,1)}, bf16[32,64,128]{2,1,0:T(8,128)(2,1)S(1)}, u32[]{:S(2)}, u32[]{:S(2)}) %collective-permute-start.30) | collective-permute-done | bytes 524320 | tf_op jit(solution)/shard_map/ppermute | solution.py:44
  175.1 2.4 %collective-permute-start.31 = (bf16[32,64,128]{2,1,0:T(8,128)(2,1)S(1)}, bf16[32,64,128]{2,1,0:T(8,128)(2,1)S(1)}, u32[]{:S(2)}, u32[]{:S(2)}) collective-permute-start(bf16[32,64,128]{2,1,0:T(8,128)(2,1)S(1)} %collective-permute-done.30.refs_13_), channel_id=1, source_target_pairs={{0,4},{1,5},{2,0},{3,1},{4,8},{5,9},{6,2},{7,3},{8,12},{9,13},{10,... | collective-permute-start | bytes 1572872 | tf_op jit(solution)/shard_map/ppermute | solution.py:44
  180.3 1.7 shard_map.78
  182.0 5.9 %collective-permute-done.31.refs_11_ = bf16[32,64,128]{2,1,0:T(8,128)(2,1)S(1)} collective-permute-done((bf16[32,64,128]{2,1,0:T(8,128)(2,1)S(1)}, bf16[32,64,128]{2,1,0:T(8,128)(2,1)S(1)}, u32[]{:S(2)}, u32[]{:S(2)}) %collective-permute-start.31) | collective-permute-done | bytes 524320 | tf_op jit(solution)/shard_map/ppermute | solution.py:44
  188.0 2.4 %collective-permute-start.32 = (bf16[32,64,128]{2,1,0:T(8,128)(2,1)S(1)}, bf16[32,64,128]{2,1,0:T(8,128)(2,1)}, u32[]{:S(2)}, u32[]{:S(2)}) collective-permute-start(bf16[32,64,128]{2,1,0:T(8,128)(2,1)S(1)} %collective-permute-done.31.refs_11_), channel_id=1, source_target_pairs={{0,4},{1,5},{2,0},{3,1},{4,8},{5,9},{6,2},{7,3},{8,12},{9,13},{10,... | collective-permute-start | bytes 1572872 | tf_op jit(solution)/shard_map/ppermute | solution.py:44
  190.4 1.4 collective-permute-done.38.refs_13_
  192.6 10.4 %shard_map.80 = (f32[33,64,128]{2,1,0:T(8,128)}, f32[8,128]{1,0:T(8,128)}) custom-call(s32[5]{0:T(128)} %stack.75.ids_ref, f32[16,128]{1,0:T(8,128)} %get-tuple-element.33.refs_0_, bf16[129,16,128]{2,1,0:T(8,128)(2,1)} %get-tuple-element.28.refs_0_.refs_1_, bf16[129,16,128]{2,1,0:T(8,128)(2,1)} %copy-done.2, bf16[129,16,128]{2,1,0:T(8,128)(2,1)} %copy-done.4, ...), custom_call_target="tpu_custom_call" | custom-call | flops 13340000256 | tf_op jit(solution)/shard_map/pallas_call | solution.py:443
  203.6 2.5 %collective-permute-done.39.upper_ref.refs_13_ = bf16[32,64,128]{2,1,0:T(8,128)(2,1)S(1)} collective-permute-done((bf16[32,64,128]{2,1,0:T(8,128)(2,1)S(1)}, bf16[32,64,128]{2,1,0:T(8,128)(2,1)S(1)}, u32[]{:S(2)}, u32[]{:S(2)}) %collective-permute-start.39) | collective-permute-done | bytes 524320 | tf_op jit(solution)/shard_map/ppermute | solution.py:44
  206.1 0.8 copy-done.28
  206.9 2.1 shard_map.82
  209.1 1.1 collective-permute-start.41
  210.2 8.2 %shard_map.83 = (f32[33,64,128]{2,1,0:T(8,128)}, f32[8,128]{1,0:T(8,128)}) custom-call(s32[4]{0:T(128)} %pad_add_fusion.3.ids_ref, f32[16,128]{1,0:T(8,128)} %get-tuple-element.33.refs_0_, bf16[129,16,128]{2,1,0:T(8,128)(2,1)} %get-tuple-element.28.refs_0_.refs_1_, bf16[129,16,128]{2,1,0:T(8,128)(2,1)} %copy-done.2, bf16[129,16,128]{2,1,0:T(8,128)(2,1)} %copy-done.4, ...), custom_call_target="tpu_custom_call" | custom-call | flops 10234999808 | tf_op jit(solution)/shard_map/pallas_call | solution.py:443
  219.6 1.1 collective-permute-done.44.refs_16_
  220.7 0.8 copy-done.31
  221.5 10.2 %shard_map.85 = bf16[32,64,128]{2,1,0:T(8,128)(2,1)} custom-call(s32[5]{0:T(128)} %stack.66.ids_ref, f32[16,128]{1,0:T(8,128)} %get-tuple-element.33.refs_0_, bf16[129,16,128]{2,1,0:T(8,128)(2,1)} %get-tuple-element.28.refs_0_.refs_1_, bf16[129,16,128]{2,1,0:T(8,128)(2,1)} %copy-done.2, bf16[129,16,128]{2,1,0:T(8,128)(2,1)} %copy-done.4, ...), custom_call_target="tpu_custom_call" | custom-call | flops 13340000256 | tf_op jit(solution)/shard_map/pallas_call | solution.py:443
  (136 shorter events, 11.6 us)
Async XLA Ops:
  2.1 8.5 %collective-permute-start.1 = (bf16[2,32,64,128]{3,2,1,0:T(8,128)(2,1)S(1)}, bf16[2,32,64,128]{3,2,1,0:T(8,128)(2,1)}, u32[]{:S(2)}, u32[]{:S(2)}) collective-permute-start(bf16[2,32,64,128]{3,2,1,0:T(8,128)(2,1)S(1)} %constant_dynamic-slice_fusion.2), channel_id=1, source_target_pairs={{0,1},{1,0},{2,3},{3,2},{4,5},{5,4},{6,7},{7,6},{8,9},{9,8},{10,11... | collective-permute-start | bytes 3145736 | tf_op jit(solution)/shard_map/ppermute | solution.py:44
  2.6 84.6 %collective-permute-start.5 = (bf16[2,32,128,128]{3,2,1,0:T(8,128)(2,1)}, bf16[2,32,128,128]{3,2,1,0:T(8,128)(2,1)}, u32[]{:S(2)}, u32[]{:S(2)}) collective-permute-start(bf16[2,32,128,128]{3,2,1,0:T(8,128)(2,1)} %refs_9_.5), channel_id=1, source_target_pairs={{0,1},{1,0},{2,3},{3,2},{4,5},{5,4},{6,7},{7,6},{8,9},{9,8},{10,11... | collective-permute-start | bytes 6291464 | tf_op jit(solution)/shard_map/ppermute | solution.py:44
  3.8 27.7 %collective-permute-start.9 = (bf16[32,64,128]{2,1,0:T(8,128)(2,1)}, bf16[32,64,128]{2,1,0:T(8,128)(2,1)S(1)}, u32[]{:S(2)}, u32[]{:S(2)}) collective-permute-start(bf16[32,64,128]{2,1,0:T(8,128)(2,1)} %get-tuple-element.41.refs_4_.refs_8_.refs_17_.refs_15_), channel_id=1, source_target_pairs={{0,8},{1,9},{2,10},{3,11},{4,12},{5,13},{6,14},{7,15},{8,0},{9,1},... | collective-permute-start | bytes 1572872 | tf_op jit(solution)/shard_map/ppermute | solution.py:44
  7.8 23.7 %collective-permute-start.21 = (bf16[32,64,128]{2,1,0:T(8,128)(2,1)}, bf16[32,64,128]{2,1,0:T(8,128)(2,1)}, u32[]{:S(2)}, u32[]{:S(2)}) collective-permute-start(bf16[32,64,128]{2,1,0:T(8,128)(2,1)} %get-tuple-element.41.refs_4_.refs_8_.refs_17_.refs_15_), channel_id=1, source_target_pairs={{0,2},{1,3},{2,0},{3,1},{4,6},{5,7},{6,4},{7,5},{8,10},{9,11},{10,... | collective-permute-start | bytes 1572872 | tf_op jit(solution)/shard_map/ppermute | solution.py:44
  9.3 1.2 collective-permute-start
  16.6 18.9 %collective-permute-start.10 = (bf16[129,16,128]{2,1,0:T(8,128)(2,1)}, bf16[129,16,128]{2,1,0:T(8,128)(2,1)S(1)}, u32[]{:S(2)}, u32[]{:S(2)}) collective-permute-start(bf16[129,16,128]{2,1,0:T(8,128)(2,1)} %get-tuple-element.24), channel_id=1, source_target_pairs={{0,2},{1,3},{2,0},{3,1},{4,6},{5,7},{6,4},{7,5},{8,10},{9,11},{10,... | collective-permute-start | bytes 1585160 | tf_op jit(solution)/shard_map/ppermute | solution.py:44
  17.1 26.5 %collective-permute-start.6 = (bf16[32,64,128]{2,1,0:T(8,128)(2,1)}, bf16[32,64,128]{2,1,0:T(8,128)(2,1)S(1)}, u32[]{:S(2)}, u32[]{:S(2)}) collective-permute-start(bf16[32,64,128]{2,1,0:T(8,128)(2,1)} %get-tuple-element.41.refs_4_.refs_8_.refs_17_.refs_15_), channel_id=1, source_target_pairs={{0,4},{1,5},{2,6},{3,7},{4,0},{5,1},{6,2},{7,3},{8,12},{9,13},{10,... | collective-permute-start | bytes 1572872 | tf_op jit(solution)/shard_map/ppermute | solution.py:44
  31.5 38.8 %collective-permute-start.15 = (bf16[129,16,128]{2,1,0:T(8,128)(2,1)}, bf16[129,16,128]{2,1,0:T(8,128)(2,1)S(1)}, u32[]{:S(2)}, u32[]{:S(2)}) collective-permute-start(bf16[129,16,128]{2,1,0:T(8,128)(2,1)} %get-tuple-element.27), channel_id=1, source_target_pairs={{0,8},{1,9},{2,10},{3,11},{4,12},{5,13},{6,14},{7,15},{8,0},{9,1},... | collective-permute-start | bytes 1585160 | tf_op jit(solution)/shard_map/ppermute | solution.py:44
  31.5 49.3 %collective-permute-start.3 = (bf16[129,16,128]{2,1,0:T(8,128)(2,1)}, bf16[129,16,128]{2,1,0:T(8,128)(2,1)S(1)}, u32[]{:S(2)}, u32[]{:S(2)}) collective-permute-start(bf16[129,16,128]{2,1,0:T(8,128)(2,1)} %get-tuple-element.23), channel_id=1, source_target_pairs={{0,10},{1,11},{2,8},{3,9},{4,14},{5,15},{6,12},{7,13},{8,2},{9,3},... | collective-permute-start | bytes 1585160 | tf_op jit(solution)/shard_map/ppermute | solution.py:44
  35.4 46.8 %collective-permute-start.12 = (bf16[129,16,128]{2,1,0:T(8,128)(2,1)}, bf16[129,16,128]{2,1,0:T(8,128)(2,1)S(1)}, u32[]{:S(2)}, u32[]{:S(2)}) collective-permute-start(bf16[129,16,128]{2,1,0:T(8,128)(2,1)} %get-tuple-element.25), channel_id=1, source_target_pairs={{0,4},{1,5},{2,6},{3,7},{4,0},{5,1},{6,2},{7,3},{8,12},{9,13},{10,... | collective-permute-start | bytes 1585160 | tf_op jit(solution)/shard_map/ppermute | solution.py:44
  43.6 38.5 %copy-start.8 = (bf16[32,64,128]{2,1,0:T(8,128)(2,1)}, bf16[32,64,128]{2,1,0:T(8,128)(2,1)S(1)}, u32[]{:S(2)}) copy-start(bf16[32,64,128]{2,1,0:T(8,128)(2,1)S(1)} %collective-permute-done.6.refs_0_) | copy-start | bytes 1572868
  43.6 42.7 %collective-permute-start.11 = (bf16[32,64,128]{2,1,0:T(8,128)(2,1)}, bf16[32,64,128]{2,1,0:T(8,128)(2,1)S(1)}, u32[]{:S(2)}, u32[]{:S(2)}) collective-permute-start(bf16[32,64,128]{2,1,0:T(8,128)(2,1)} %shard_map.71.refs_6_.refs_25_.refs_23_), channel_id=1, source_target_pairs={{0,4},{1,5},{2,6},{3,7},{4,0},{5,1},{6,2},{7,3},{8,12},{9,13},{10,... | collective-permute-start | bytes 1572872 | tf_op jit(solution)/shard_map/ppermute | solution.py:44
  70.3 18.5 %collective-permute-start.23 = (bf16[32,64,128]{2,1,0:T(8,128)(2,1)}, bf16[32,64,128]{2,1,0:T(8,128)(2,1)}, u32[]{:S(2)}, u32[]{:S(2)}) collective-permute-start(bf16[32,64,128]{2,1,0:T(8,128)(2,1)} %shard_map.71.refs_6_.refs_25_.refs_23_), channel_id=1, source_target_pairs={{0,1},{1,0},{2,3},{3,2},{4,5},{5,4},{6,7},{7,6},{8,9},{9,8},{10,11... | collective-permute-start | bytes 1572872 | tf_op jit(solution)/shard_map/ppermute | solution.py:44
  80.8 15.2 %collective-permute-start.19 = (bf16[32,64,128]{2,1,0:T(8,128)(2,1)}, bf16[32,64,128]{2,1,0:T(8,128)(2,1)}, u32[]{:S(2)}, u32[]{:S(2)}) collective-permute-start(bf16[32,64,128]{2,1,0:T(8,128)(2,1)} %shard_map.71.refs_6_.refs_25_.refs_23_), channel_id=1, source_target_pairs={{0,2},{1,3},{2,0},{3,1},{4,6},{5,7},{6,4},{7,5},{8,10},{9,11},{10,... | collective-permute-start | bytes 1572872 | tf_op jit(solution)/shard_map/ppermute | solution.py:44
  82.2 21.4 %collective-permute-start.22 = (bf16[32,64,128]{2,1,0:T(8,128)(2,1)}, bf16[32,64,128]{2,1,0:T(8,128)(2,1)S(1)}, u32[]{:S(2)}, u32[]{:S(2)}) collective-permute-start(bf16[32,64,128]{2,1,0:T(8,128)(2,1)} %collective-permute-done.21.refs_6_.refs_19_.refs_17_), channel_id=1, source_target_pairs={{0,1},{1,0},{2,3},{3,2},{4,5},{5,4},{6,7},{7,6},{8,9},{9,8},{10,11... | collective-permute-start | bytes 1572872 | tf_op jit(solution)/shard_map/ppermute | solution.py:44
  86.3 26.3 %collective-permute-start.17 = (bf16[32,64,128]{2,1,0:T(8,128)(2,1)S(1)}, bf16[32,64,128]{2,1,0:T(8,128)(2,1)}, u32[]{:S(2)}, u32[]{:S(2)}) collective-permute-start(bf16[32,64,128]{2,1,0:T(8,128)(2,1)S(1)} %copy-done.9), channel_id=1, source_target_pairs={{0,1},{1,0},{2,3},{3,2},{4,5},{5,4},{6,7},{7,6},{8,9},{9,8},{10,11... | collective-permute-start | bytes 1572872 | tf_op jit(solution)/shard_map/ppermute | solution.py:44
  87.2 25.6 %collective-permute-start.7 = (bf16[32,64,128]{2,1,0:T(8,128)(2,1)S(1)}, bf16[32,64,128]{2,1,0:T(8,128)(2,1)}, u32[]{:S(2)}, u32[]{:S(2)}) collective-permute-start(bf16[32,64,128]{2,1,0:T(8,128)(2,1)S(1)} %copy-done.9), channel_id=1, source_target_pairs={{0,2},{1,3},{2,0},{3,1},{4,6},{5,7},{6,4},{7,5},{8,10},{9,11},{10,... | collective-permute-start | bytes 1572872 | tf_op jit(solution)/shard_map/ppermute | solution.py:44
  88.7 25.7 %collective-permute-start.16 = (bf16[129,16,128]{2,1,0:T(8,128)(2,1)S(1)}, bf16[129,16,128]{2,1,0:T(8,128)(2,1)S(1)}, u32[]{:S(2)}, u32[]{:S(2)}) collective-permute-start(bf16[129,16,128]{2,1,0:T(8,128)(2,1)S(1)} %copy-done.5), channel_id=1, source_target_pairs={{0,12},{1,13},{2,14},{3,15},{4,8},{5,9},{6,10},{7,11},{8,4},{9,5},... | collective-permute-start | bytes 1585160 | tf_op jit(solution)/shard_map/ppermute | solution.py:44
  96.0 8.3 %collective-permute-start.20 = (bf16[32,64,128]{2,1,0:T(8,128)(2,1)}, bf16[32,64,128]{2,1,0:T(8,128)(2,1)S(1)}, u32[]{:S(2)}, u32[]{:S(2)}) collective-permute-start(bf16[32,64,128]{2,1,0:T(8,128)(2,1)} %collective-permute-done.19.refs_4_.refs_27_.refs_25_), channel_id=1, source_target_pairs={{0,1},{1,0},{2,3},{3,2},{4,5},{5,4},{6,7},{7,6},{8,9},{9,8},{10,11... | collective-permute-start | bytes 1572872 | tf_op jit(solution)/shard_map/ppermute | solution.py:44
  103.7 26.0 %collective-permute-start.18 = (bf16[32,64,128]{2,1,0:T(8,128)(2,1)S(1)}, bf16[32,64,128]{2,1,0:T(8,128)(2,1)}, u32[]{:S(2)}, u32[]{:S(2)}) collective-permute-start(bf16[32,64,128]{2,1,0:T(8,128)(2,1)S(1)} %copy-done.11), channel_id=1, source_target_pairs={{0,1},{1,0},{2,3},{3,2},{4,5},{5,4},{6,7},{7,6},{8,9},{9,8},{10,11... | collective-permute-start | bytes 1572872 | tf_op jit(solution)/shard_map/ppermute | solution.py:44
  104.3 25.4 %collective-permute-start.13 = (bf16[32,64,128]{2,1,0:T(8,128)(2,1)S(1)}, bf16[32,64,128]{2,1,0:T(8,128)(2,1)}, u32[]{:S(2)}, u32[]{:S(2)}) collective-permute-start(bf16[32,64,128]{2,1,0:T(8,128)(2,1)S(1)} %copy-done.11), channel_id=1, source_target_pairs={{0,2},{1,3},{2,0},{3,1},{4,6},{5,7},{6,4},{7,5},{8,10},{9,11},{10,... | collective-permute-start | bytes 1572872 | tf_op jit(solution)/shard_map/ppermute | solution.py:44
  112.7 24.4 %collective-permute-start.2 = (bf16[129,16,128]{2,1,0:T(8,128)(2,1)}, bf16[129,16,128]{2,1,0:T(8,128)(2,1)S(1)}, u32[]{:S(2)}, u32[]{:S(2)}) collective-permute-start(bf16[129,16,128]{2,1,0:T(8,128)(2,1)} %get-tuple-element.21), channel_id=1, source_target_pairs={{0,6},{1,7},{2,4},{3,5},{4,2},{5,3},{6,0},{7,1},{8,14},{9,15},{10,... | collective-permute-start | bytes 1585160 | tf_op jit(solution)/shard_map/ppermute | solution.py:44
  112.8 32.3 %collective-permute-start.4 = (bf16[129,16,128]{2,1,0:T(8,128)(2,1)S(1)}, bf16[129,16,128]{2,1,0:T(8,128)(2,1)S(1)}, u32[]{:S(2)}, u32[]{:S(2)}) collective-permute-start(bf16[129,16,128]{2,1,0:T(8,128)(2,1)S(1)} %copy-done.6), channel_id=1, source_target_pairs={{0,14},{1,15},{2,12},{3,13},{4,10},{5,11},{6,8},{7,9},{8,6},{9,7},... | collective-permute-start | bytes 1585160 | tf_op jit(solution)/shard_map/ppermute | solution.py:44
  114.4 15.3 %copy-start.16 = (bf16[129,16,128]{2,1,0:T(8,128)(2,1)}, bf16[129,16,128]{2,1,0:T(8,128)(2,1)S(1)}, u32[]{:S(2)}) copy-start(bf16[129,16,128]{2,1,0:T(8,128)(2,1)S(1)} %collective-permute-done.16.refs_1_.refs_7_) | copy-start | bytes 1585156
  114.4 30.6 %collective-permute-start.8 = (bf16[32,64,128]{2,1,0:T(8,128)(2,1)}, bf16[32,64,128]{2,1,0:T(8,128)(2,1)S(1)}, u32[]{:S(2)}, u32[]{:S(2)}) collective-permute-start(bf16[32,64,128]{2,1,0:T(8,128)(2,1)} %collective-permute-done.7.refs_4_.refs_23_.refs_21_), channel_id=1, source_target_pairs={{0,1},{1,0},{2,3},{3,2},{4,5},{5,4},{6,7},{7,6},{8,9},{9,8},{10,11... | collective-permute-start | bytes 1572872 | tf_op jit(solution)/shard_map/ppermute | solution.py:44
  129.7 15.4 %collective-permute-start.14 = (bf16[32,64,128]{2,1,0:T(8,128)(2,1)}, bf16[32,64,128]{2,1,0:T(8,128)(2,1)}, u32[]{:S(2)}, u32[]{:S(2)}) collective-permute-start(bf16[32,64,128]{2,1,0:T(8,128)(2,1)} %collective-permute-done.13.refs_6_.refs_31_.refs_29_), channel_id=1, source_target_pairs={{0,1},{1,0},{2,3},{3,2},{4,5},{5,4},{6,7},{7,6},{8,9},{9,8},{10,11... | collective-permute-start | bytes 1572872 | tf_op jit(solution)/shard_map/ppermute | solution.py:44
  153.2 2.3 collective-permute-start.24
  153.3 4.0 %collective-permute-start.25 = (f32[16,128]{1,0:T(8,128)}, f32[16,128]{1,0:T(8,128)S(1)}, u32[]{:S(2)}, u32[]{:S(2)}) collective-permute-start(f32[16,128]{1,0:T(8,128)} %get-tuple-element.32), channel_id=1, source_target_pairs={{0,2},{1,3},{2,0},{3,1},{4,6},{5,7},{6,4},{7,5},{8,10},{9,11},{10,... | collective-permute-start | bytes 24584 | tf_op jit(solution)/shard_map/ppermute | solution.py:118
  155.4 3.3 %collective-permute-start.26 = (f32[16,128]{1,0:T(8,128)}, f32[16,128]{1,0:T(8,128)S(1)}, u32[]{:S(2)}, u32[]{:S(2)}) collective-permute-start(f32[16,128]{1,0:T(8,128)} %get-tuple-element.32), channel_id=1, source_target_pairs={{0,3},{1,2},{2,1},{3,0},{4,7},{5,6},{6,5},{7,4},{8,11},{9,10},{10,... | collective-permute-start | bytes 24584 | tf_op jit(solution)/shard_map/ppermute | solution.py:118
  160.0 15.0 %collective-permute-start.30 = (bf16[32,64,128]{2,1,0:T(8,128)(2,1)}, bf16[32,64,128]{2,1,0:T(8,128)(2,1)S(1)}, u32[]{:S(2)}, u32[]{:S(2)}) collective-permute-start(bf16[32,64,128]{2,1,0:T(8,128)(2,1)} %shard_map.79.refs_11_), channel_id=1, source_target_pairs={{0,4},{1,5},{2,0},{3,1},{4,8},{5,9},{6,2},{7,3},{8,12},{9,13},{10,... | collective-permute-start | bytes 1572872 | tf_op jit(solution)/shard_map/ppermute | solution.py:44
  163.0 14.5 %collective-permute-start.35 = (bf16[32,64,128]{2,1,0:T(8,128)(2,1)}, bf16[32,64,128]{2,1,0:T(8,128)(2,1)S(1)}, u32[]{:S(2)}, u32[]{:S(2)}) collective-permute-start(bf16[32,64,128]{2,1,0:T(8,128)(2,1)} %shard_map.79.refs_11_), channel_id=1, source_target_pairs={{0,2},{1,3},{2,6},{3,7},{4,0},{5,1},{6,10},{7,11},{8,4},{9,5},{10,... | collective-permute-start | bytes 1572872 | tf_op jit(solution)/shard_map/ppermute | solution.py:44
  163.0 14.5 %collective-permute-start.27 = (f32[16,128]{1,0:T(8,128)S(1)}, f32[16,128]{1,0:T(8,128)S(1)}, u32[]{:S(2)}, u32[]{:S(2)}) collective-permute-start(f32[16,128]{1,0:T(8,128)S(1)} %copy-done.12), channel_id=1, source_target_pairs={{0,4},{1,5},{2,6},{3,7},{4,0},{5,1},{6,2},{7,3},{8,12},{9,13},{10,... | collective-permute-start | bytes 24584 | tf_op jit(solution)/shard_map/ppermute | solution.py:118
  165.0 13.0 %collective-permute-start.28 = (f32[16,128]{1,0:T(8,128)S(1)}, f32[16,128]{1,0:T(8,128)S(1)}, u32[]{:S(2)}, u32[]{:S(2)}) collective-permute-start(f32[16,128]{1,0:T(8,128)S(1)} %copy-done.12), channel_id=1, source_target_pairs={{0,8},{1,9},{2,10},{3,11},{4,12},{5,13},{6,14},{7,15},{8,0},{9,1},... | collective-permute-start | bytes 24584 | tf_op jit(solution)/shard_map/ppermute | solution.py:118
  165.5 12.6 %collective-permute-start.29 = (f32[16,128]{1,0:T(8,128)S(1)}, f32[16,128]{1,0:T(8,128)S(1)}, u32[]{:S(2)}, u32[]{:S(2)}) collective-permute-start(f32[16,128]{1,0:T(8,128)S(1)} %copy-done.12), channel_id=1, source_target_pairs={{0,12},{1,13},{2,14},{3,15},{4,8},{5,9},{6,10},{7,11},{8,4},{9,5},... | collective-permute-start | bytes 24584 | tf_op jit(solution)/shard_map/ppermute | solution.py:118
  175.1 12.9 %collective-permute-start.31 = (bf16[32,64,128]{2,1,0:T(8,128)(2,1)S(1)}, bf16[32,64,128]{2,1,0:T(8,128)(2,1)S(1)}, u32[]{:S(2)}, u32[]{:S(2)}) collective-permute-start(bf16[32,64,128]{2,1,0:T(8,128)(2,1)S(1)} %collective-permute-done.30.refs_13_), channel_id=1, source_target_pairs={{0,4},{1,5},{2,0},{3,1},{4,8},{5,9},{6,2},{7,3},{8,12},{9,13},{10,... | collective-permute-start | bytes 1572872 | tf_op jit(solution)/shard_map/ppermute | solution.py:44
  177.4 10.5 %collective-permute-start.33 = (bf16[32,64,128]{2,1,0:T(8,128)(2,1)}, bf16[32,64,128]{2,1,0:T(8,128)(2,1)S(1)}, u32[]{:S(2)}, u32[]{:S(2)}) collective-permute-start(bf16[32,64,128]{2,1,0:T(8,128)(2,1)} %shard_map.79.refs_11_), channel_id=1, source_target_pairs={{0,1},{1,0},{2,3},{3,2},{4,5},{5,4},{6,7},{7,6},{8,9},{9,8},{10,11... | collective-permute-start | bytes 1572872 | tf_op jit(solution)/shard_map/ppermute | solution.py:44
  177.5 14.3 %collective-permute-start.38 = (bf16[32,64,128]{2,1,0:T(8,128)(2,1)S(1)}, bf16[32,64,128]{2,1,0:T(8,128)(2,1)S(1)}, u32[]{:S(2)}, u32[]{:S(2)}) collective-permute-start(bf16[32,64,128]{2,1,0:T(8,128)(2,1)S(1)} %collective-permute-done.35.refs_15_), channel_id=1, source_target_pairs={{0,2},{1,3},{2,6},{3,7},{4,0},{5,1},{6,10},{7,11},{8,4},{9,5},{10,... | collective-permute-start | bytes 1572872 | tf_op jit(solution)/shard_map/ppermute | solution.py:44
  178.0 13.8 %collective-permute-start.34 = (bf16[32,64,128]{2,1,0:T(8,128)(2,1)S(1)}, bf16[32,64,128]{2,1,0:T(8,128)(2,1)S(1)}, u32[]{:S(2)}, u32[]{:S(2)}) collective-permute-start(bf16[32,64,128]{2,1,0:T(8,128)(2,1)S(1)} %collective-permute-done.30.refs_13_), channel_id=1, source_target_pairs={{0,1},{1,0},{2,3},{3,2},{4,5},{5,4},{6,7},{7,6},{8,9},{9,8},{10,11... | collective-permute-start | bytes 1572872 | tf_op jit(solution)/shard_map/ppermute | solution.py:44
  178.0 14.3 %collective-permute-start.36 = (bf16[32,64,128]{2,1,0:T(8,128)(2,1)S(1)}, bf16[32,64,128]{2,1,0:T(8,128)(2,1)}, u32[]{:S(2)}, u32[]{:S(2)}) collective-permute-start(bf16[32,64,128]{2,1,0:T(8,128)(2,1)S(1)} %collective-permute-done.35.refs_15_), channel_id=1, source_target_pairs={{0,1},{1,0},{2,3},{3,2},{4,5},{5,4},{6,7},{7,6},{8,9},{9,8},{10,11... | collective-permute-start | bytes 1572872 | tf_op jit(solution)/shard_map/ppermute | solution.py:44
  188.0 15.1 %copy-start.22 = (bf16[32,64,128]{2,1,0:T(8,128)(2,1)}, bf16[32,64,128]{2,1,0:T(8,128)(2,1)S(1)}, u32[]{:S(2)}) copy-start(bf16[32,64,128]{2,1,0:T(8,128)(2,1)S(1)} %collective-permute-done.31.refs_11_) | copy-start | bytes 1572868
  188.0 22.2 %collective-permute-start.42 = (bf16[32,64,128]{2,1,0:T(8,128)(2,1)S(1)}, bf16[32,64,128]{2,1,0:T(8,128)(2,1)}, u32[]{:S(2)}, u32[]{:S(2)}) collective-permute-start(bf16[32,64,128]{2,1,0:T(8,128)(2,1)S(1)} %collective-permute-done.31.refs_11_), channel_id=1, source_target_pairs={{0,1},{1,0},{2,3},{3,2},{4,5},{5,4},{6,7},{7,6},{8,9},{9,8},{10,11... | collective-permute-start | bytes 1572872 | tf_op jit(solution)/shard_map/ppermute | solution.py:44
  188.0 15.1 %collective-permute-start.32 = (bf16[32,64,128]{2,1,0:T(8,128)(2,1)S(1)}, bf16[32,64,128]{2,1,0:T(8,128)(2,1)}, u32[]{:S(2)}, u32[]{:S(2)}) collective-permute-start(bf16[32,64,128]{2,1,0:T(8,128)(2,1)S(1)} %collective-permute-done.31.refs_11_), channel_id=1, source_target_pairs={{0,4},{1,5},{2,0},{3,1},{4,8},{5,9},{6,2},{7,3},{8,12},{9,13},{10,... | collective-permute-start | bytes 1572872 | tf_op jit(solution)/shard_map/ppermute | solution.py:44
  191.8 18.4 %collective-permute-start.43 = (bf16[32,64,128]{2,1,0:T(8,128)(2,1)S(1)}, bf16[32,64,128]{2,1,0:T(8,128)(2,1)}, u32[]{:S(2)}, u32[]{:S(2)}) collective-permute-start(bf16[32,64,128]{2,1,0:T(8,128)(2,1)S(1)} %collective-permute-done.38.refs_13_), channel_id=1, source_target_pairs={{0,1},{1,0},{2,3},{3,2},{4,5},{5,4},{6,7},{7,6},{8,9},{9,8},{10,11... | collective-permute-start | bytes 1572872 | tf_op jit(solution)/shard_map/ppermute | solution.py:44
  191.8 14.3 %collective-permute-start.39 = (bf16[32,64,128]{2,1,0:T(8,128)(2,1)S(1)}, bf16[32,64,128]{2,1,0:T(8,128)(2,1)S(1)}, u32[]{:S(2)}, u32[]{:S(2)}) collective-permute-start(bf16[32,64,128]{2,1,0:T(8,128)(2,1)S(1)} %collective-permute-done.38.refs_13_), channel_id=1, source_target_pairs={{0,2},{1,3},{2,6},{3,7},{4,0},{5,1},{6,10},{7,11},{8,4},{9,5},{10,... | collective-permute-start | bytes 1572872 | tf_op jit(solution)/shard_map/ppermute | solution.py:44
  203.1 16.4 %collective-permute-start.37 = (bf16[32,64,128]{2,1,0:T(8,128)(2,1)}, bf16[32,64,128]{2,1,0:T(8,128)(2,1)S(1)}, u32[]{:S(2)}, u32[]{:S(2)}) collective-permute-start(bf16[32,64,128]{2,1,0:T(8,128)(2,1)} %shard_map.81.lower_ref.refs_11_), channel_id=1, source_target_pairs={{0,1},{1,0},{2,3},{3,2},{4,5},{5,4},{6,7},{7,6},{8,9},{9,8},{10,11... | collective-permute-start | bytes 1572872 | tf_op jit(solution)/shard_map/ppermute | solution.py:44
  209.1 9.5 %collective-permute-start.41 = (bf16[32,64,128]{2,1,0:T(8,128)(2,1)}, bf16[32,64,128]{2,1,0:T(8,128)(2,1)}, u32[]{:S(2)}, u32[]{:S(2)}) collective-permute-start(bf16[32,64,128]{2,1,0:T(8,128)(2,1)} %shard_map.82), channel_id=1, source_target_pairs={{0,4},{1,3},{2,0},{3,7},{4,8},{5,1},{6,2},{7,11},{8,12},{9,5},{10,... | collective-permute-start | bytes 1572872 | tf_op jit(solution)/shard_map/ppermute | solution.py:44
  210.2 9.4 %collective-permute-start.40 = (bf16[32,64,128]{2,1,0:T(8,128)(2,1)}, bf16[32,64,128]{2,1,0:T(8,128)(2,1)S(1)}, u32[]{:S(2)}, u32[]{:S(2)}) collective-permute-start(bf16[32,64,128]{2,1,0:T(8,128)(2,1)} %copy-done.28), channel_id=1, source_target_pairs={{0,1},{1,0},{2,3},{3,2},{4,5},{5,4},{6,7},{7,6},{8,9},{9,8},{10,11... | collective-permute-start | bytes 1572872 | tf_op jit(solution)/shard_map/ppermute | solution.py:44
  218.6 2.1 collective-permute-start.44
  (30 other events, 115.7 us)

commit v13 on v12

--- a/solution.py
+++ b/solution.py
@@ -110,17 +110,17 @@
     return units
 
 
-def spread(value, devices):
+def spread(value, devices, before):
     step = 1
-    values = []
     while step < devices:
+        if step > 1:
+            value = after(value, before)
         masks = [step] if 2 * step == devices else [step, 2 * step, 3 * step]
         parts = [lax.ppermute(value, BOTH, [(d, d ^ m) for d in range(devices)]) for m in masks]
         for part in parts:
             value = value + part
-        values.append(value)
         step *= 4
-    return values
+    return value
 
 
 def pack_kernel(order, capacity, blocks, terms, ids_ref, plan_ref, other_plan_ref, *refs):
@@ -447,7 +447,7 @@
         out_specs=out_specs,
         scratch_shapes=scratch,
         compiler_params=pltpu.CompilerParams(vmem_limit_bytes=VMEM_LIMIT),
-        cost_estimate=busy(3.5 + (2.7 if waves else 1.8) * sources),
+        cost_estimate=busy(0.5 if waves else 3.5 + 1.8 * sources),
     )(*scalars, *arrays)
 
 
@@ -528,10 +528,11 @@
             own_rows,
         )
 
-    stats = spread(stats, owners * halves)
-    rest = after(total, stats[0])
+    rest = total
+    ahead = ring_send(rest, owners, halves, (1,) * halves)
+    behind = ring_send(rest, owners, halves, (-1,) * halves)
     entries = blocks * owners * height * width
-    scale, rayleigh = scales(stats[-1], entries)
+    scale, rayleigh = scales(spread(stats, owners * halves, ahead), entries)
     reach = (owners - 1) // 2
     waves = [(near[m], far[m]) for m in range(owners)]
 
@@ -543,23 +544,19 @@
             ids, lefts, rights, vectors, total, end, waves=waves, scale=scale
         )
 
-    total = token = None
-    units = {0: rest}
-    waiting = {}
-    ahead = behind = rest
-    for step in range(1, reach + 1):
+    total, token = None, None
+    units, waiting = {1: ahead, -1: behind}, {0: rest}
+    for step in range(2, reach + 1):
         ahead = ring_send(ahead, owners, halves, (1,) * halves)
         behind = ring_send(behind, owners, halves, (-1,) * halves)
-        if step == reach:
-            total, token = add_group(total, waiting, "go on")
-            waiting = {}
-            ahead = after(ahead, token)
-        waiting.update(units)
+        total, token = add_group(total, waiting, "go on")
+        ahead = after(ahead, token)
+        waiting = units if step == 2 else {}
         units = {step: ahead, -step: behind}
+        waiting = {**waiting, **units}
     last = ring_send(select_half(half, ahead, behind), owners, halves, (1, -1))
     total, token = add_group(total, waiting, "go on")
-    last = after(last, token)
-    total = add_group(total, {**units, owners // 2: last}, "result")
+    total = add_group(total, {owners // 2: after(last, token)}, "result")
     return (total, rayleigh[0])
 
 
@@ -677,8 +674,9 @@
 
 
 def per_device(wavefunction, *operands):
-    gathered_bytes = lax.axis_size("sec") * wavefunction.size * wavefunction.dtype.itemsize
-    if 2 * gathered_bytes > RING_BYTES:
+    owners = lax.axis_size("sec")
+    gathered_bytes = owners * wavefunction.size * wavefunction.dtype.itemsize
+    if owners < 8 or owners & (owners - 1) or 2 * gathered_bytes > RING_BYTES:
         return per_device_streamed(wavefunction, *operands)
     return per_device_ring(wavefunction, *operands)
 

time: 233 us -> 243 us (1.043)
  Pallas kernels: 67.6 us -> 72.9 us
  local copies, waits for them, and re-layouts: 8.29 us -> 13.1 us
  starting transfers between devices: 39.7 us -> 36.5 us
    ppermute x6, waiting for transfers between devices: 3.67 us -> 12.7 us  [spread(): lax.ppermute(value, BOTH, [(d, d ^ m) for d in range(devices)])]
    ppermute x39, waiting for transfers between devices: 108 us -> 98.5 us  [permute(): return lax.ppermute(value, BOTH, pairs)]
    pallas_call x7 -> x8, Pallas kernels: 58.4 us -> 63.6 us  [apply_group(): pl.pallas_call(functools.partial(apply_kernel, sources, choices, first, e...]
    unnamed x66 -> x58, local copies, waits for them, and re-layouts: 4.56 us -> 7.77 us
    ppermute x39, starting transfers between devices: 33 us -> 30.5 us  [permute(): return lax.ppermute(value, BOTH, pairs)]
  transfers between devices with their start and end apart: 45 -> 45, of which waited for: 18 -> 13; matrix products, arithmetic and copies ran while one was open for 2% -> 4% of each run, Pallas kernels for 22% -> 25%
where the time goes in v13:
time: 243 us; the launch traced here: 241 us
  waiting for transfers between devices  111 us (46%)
  Pallas kernels  72.9 us (30%)
  starting transfers between devices  36.5 us (15%)
  local copies, waits for them, and re-layouts  13.1 us (5%)
  other arithmetic  5.78 us (2%)
    ppermute x39, waiting for transfers between devices, permute(): return lax.ppermute(value, BOTH, pairs)  98.5 us
    pallas_call x8, Pallas kernels, apply_group(): pl.pallas_call(functools.partial(apply_kernel, sources, choices, first, e...  63.6 us
    ppermute x39, starting transfers between devices, permute(): return lax.ppermute(value, BOTH, pairs)  30.5 us
    ppermute x6, waiting for transfers between devices, spread(): lax.ppermute(value, BOTH, [(d, d ^ m) for d in range(devices)])  12.7 us
    unnamed x58, local copies, waits for them, and re-layouts  7.77 us
    ppermute x6, starting transfers between devices, spread(): lax.ppermute(value, BOTH, [(d, d ^ m) for d in range(devices)])  6.03 us
    pallas_call x1, Pallas kernels, pack(): pl.pallas_call(functools.partial(pack_kernel, order, capacity, blocks, te...  5.46 us
  transfers between devices with their start and end apart: 45, of which 13 were waited for; matrix products, arithmetic and copies ran while one was open for 4% of the time, Pallas kernels for 25%

profile of v13, /device:TPU:0, one launch (start us, length us, event | category | flops | bytes accessed | tf_op | source)
XLA Modules:
  0.0 240.8 jit_solution(3219513092237772196)
XLA Ops:
  0.6 2.4 %constant_dynamic-slice_fusion.2 = bf16[2,32,64,128]{3,2,1,0:T(8,128)(2,1)} fusion(bf16[2,32,128,128]{3,2,1,0:T(8,128)(2,1)} %refs_0_.1, s32[]{:T(128)S(6)} %select_n.83), kind=kLoop, calls=%fused_computation.5 | loop fusion | bytes 2097156 | tf_op jit(solution)/shard_map/dynamic_slice | solution.py:493
  3.6 2.2 constant_dynamic-slice_fusion
  5.9 4.0 %collective-permute-start.9 = (bf16[32,64,128]{2,1,0:T(8,128)(2,1)}, bf16[32,64,128]{2,1,0:T(8,128)(2,1)S(1)}, u32[]{:S(2)}, u32[]{:S(2)}) collective-permute-start(bf16[32,64,128]{2,1,0:T(8,128)(2,1)} %get-tuple-element.45.refs_4_.refs_8_.refs_13_.refs_19_.refs_15_), channel_id=1, source_target_pairs={{0,8},{1,9},{2,10},{3,11},{4,12},{5,13},{6,14},{7,15},{8,0},{9,1},... | collective-permute-start | bytes 1572872 | tf_op jit(solution)/shard_map/ppermute | solution.py:44
  9.9 1.5 collective-permute-start.21
  13.2 5.5 %shard_map.68 = (bf16[129,16,128]{2,1,0:T(8,128)(2,1)}, bf16[129,16,128]{2,1,0:T(8,128)(2,1)}, bf16[129,16,128]{2,1,0:T(8,128)(2,1)}, bf16[129,16,128]{2,1,0:T(8...) custom-call(s32[2]{0:T(128)} %pad_add_fusion.4.ids_ref, ...), custom_call_target="tpu_custom_call" | custom-call | flops 5750000128 | tf_op jit(solution)/shard_map/pallas_call | solution.py:186
  19.3 1.6 collective-permute-start.6
  20.8 12.7 %collective-permute-done.9.refs_0_ = bf16[32,64,128]{2,1,0:T(8,128)(2,1)S(1)} collective-permute-done((bf16[32,64,128]{2,1,0:T(8,128)(2,1)}, bf16[32,64,128]{2,1,0:T(8,128)(2,1)S(1)}, u32[]{:S(2)}, u32[]{:S(2)}) %collective-permute-start.9) | collective-permute-done | bytes 524320 | tf_op jit(solution)/shard_map/ppermute | solution.py:44
  33.6 0.8 copy-done.3
  34.4 3.1 %collective-permute-start.3 = (bf16[129,16,128]{2,1,0:T(8,128)(2,1)}, bf16[129,16,128]{2,1,0:T(8,128)(2,1)S(1)}, u32[]{:S(2)}, u32[]{:S(2)}) collective-permute-start(bf16[129,16,128]{2,1,0:T(8,128)(2,1)} %get-tuple-element.25), channel_id=1, source_target_pairs={{0,10},{1,11},{2,8},{3,9},{4,14},{5,15},{6,12},{7,13},{8,2},{9,3},... | collective-permute-start | bytes 1585160 | tf_op jit(solution)/shard_map/ppermute | solution.py:44
  37.5 1.9 collective-permute-start.12
  39.5 6.2 %collective-permute-done.6.refs_0_ = bf16[32,64,128]{2,1,0:T(8,128)(2,1)} collective-permute-done((bf16[32,64,128]{2,1,0:T(8,128)(2,1)}, bf16[32,64,128]{2,1,0:T(8,128)(2,1)}, u32[]{:S(2)}, u32[]{:S(2)}) %collective-permute-start.6) | collective-permute-done | bytes 524320 | tf_op jit(solution)/shard_map/ppermute | solution.py:44
  45.7 26.8 %collective-permute-done.15.refs_1_.refs_5_ = bf16[129,16,128]{2,1,0:T(8,128)(2,1)} collective-permute-done((bf16[129,16,128]{2,1,0:T(8,128)(2,1)}, bf16[129,16,128]{2,1,0:T(8,128)(2,1)}, u32[]{:S(2)}, u32[]{:S(2)}) %collective-permute-start.15) | collective-permute-done | bytes 528416 | tf_op jit(solution)/shard_map/ppermute | solution.py:44
  72.5 10.4 %collective-permute-done.3.refs_1_.refs_0_.refs_6_ = bf16[129,16,128]{2,1,0:T(8,128)(2,1)S(1)} collective-permute-done((bf16[129,16,128]{2,1,0:T(8,128)(2,1)}, bf16[129,16,128]{2,1,0:T(8,128)(2,1)S(1)}, u32[]{:S(2)}, u32[]{:S(2)}) %collective-permute-start.3) | collective-permute-done | bytes 528416 | tf_op jit(solution)/shard_map/ppermute | solution.py:44
  84.4 4.1 %collective-permute-done.11.refs_0_ = bf16[32,64,128]{2,1,0:T(8,128)(2,1)S(1)} collective-permute-done((bf16[32,64,128]{2,1,0:T(8,128)(2,1)}, bf16[32,64,128]{2,1,0:T(8,128)(2,1)S(1)}, u32[]{:S(2)}, u32[]{:S(2)}) %collective-permute-start.11) | collective-permute-done | bytes 524320 | tf_op jit(solution)/shard_map/ppermute | solution.py:44
  88.5 0.8 copy-done.4
  89.3 1.6 collective-permute-start.7
  90.8 2.4 collective-permute-start.16
  93.2 4.9 %collective-permute-done.19.refs_4_.refs_23_.refs_29_.refs_25_ = bf16[32,64,128]{2,1,0:T(8,128)(2,1)} collective-permute-done((bf16[32,64,128]{2,1,0:T(8,128)(2,1)}, bf16[32,64,128]{2,1,0:T(8,128)(2,1)}, u32[]{:S(2)}, u32[]{:S(2)}) %collective-permute-start.19) | collective-permute-done | bytes 524320 | tf_op jit(solution)/shard_map/ppermute | solution.py:44
  98.1 7.7 %shard_map.74 = (f32[33,64,128]{2,1,0:T(8,128)}, f32[8,128]{1,0:T(8,128)}) custom-call(s32[2]{0:T(128)} %pad_add_fusion.3.ids_ref, bf16[129,16,128]{2,1,0:T(8,128)(2,1)} %get-tuple-element.30.refs_0_.refs_1_, bf16[129,16,128]{2,1,0:T(8,128)(2,1)} %collective-permute-done.15.refs_1_.refs_5_, bf16[2,32,128,128]{3,2,1,0:T(8,128)(2,1)} %refs_9_.7, ...), custom_call_target="tpu_custom_call" | custom-call | flops 8165000192 | tf_op jit(solution)/shard_map/pallas_call | solution.py:443
  106.4 1.0 collective-permute-start.13
  107.4 7.6 %shard_map.75 = (f32[33,64,128]{2,1,0:T(8,128)}, f32[8,128]{1,0:T(8,128)}) custom-call(s32[2]{0:T(128)} %pad_add_fusion.3.ids_ref, bf16[129,16,128]{2,1,0:T(8,128)(2,1)} %copy-done.1, bf16[129,16,128]{2,1,0:T(8,128)(2,1)} %copy-done.2, bf16[2,32,128,128]{3,2,1,0:T(8,128)(2,1)} %refs_9_.7, bf16[2,32,128,128]{3,2,1,0:T(8,128)(2,1)} %collective-permute-done.5.refs_3_.refs_10_, ...), custom_call_target="tpu_custom_call" | custom-call | flops 8165000192 | tf_op jit(solution)/shard_map/pallas_call | solution.py:443
  115.2 1.5 collective-permute-start.4
  116.7 15.0 %collective-permute-done.13.refs_6_.refs_27_.refs_33_.refs_29_ = bf16[32,64,128]{2,1,0:T(8,128)(2,1)} collective-permute-done((bf16[32,64,128]{2,1,0:T(8,128)(2,1)S(1)}, bf16[32,64,128]{2,1,0:T(8,128)(2,1)}, u32[]{:S(2)}, u32[]{:S(2)}) %collective-permute-start.13) | collective-permute-done | bytes 524320 | tf_op jit(solution)/shard_map/ppermute | solution.py:44
  131.7 7.5 %shard_map.76 = (f32[33,64,128]{2,1,0:T(8,128)}, f32[8,128]{1,0:T(8,128)}) custom-call(s32[2]{0:T(128)} %pad_add_fusion.3.ids_ref, bf16[129,16,128]{2,1,0:T(8,128)(2,1)} %collective-permute-done.12.refs_1_.refs_0_.refs_3_, bf16[129,16,128]{2,1,0:T(8,128)(2,1)} %copy-done.6, bf16[2,32,128,128]{3,2,1,0:T(8,128)(2,1)} %refs_9_.7, ...), custom_call_target="tpu_custom_call" | custom-call | flops 8165000192 | tf_op jit(solution)/shard_map/pallas_call | solution.py:443
  139.3 8.0 %collective-permute-done.4.refs_1_.refs_8_ = bf16[129,16,128]{2,1,0:T(8,128)(2,1)S(1)} collective-permute-done((bf16[129,16,128]{2,1,0:T(8,128)(2,1)}, bf16[129,16,128]{2,1,0:T(8,128)(2,1)S(1)}, u32[]{:S(2)}, u32[]{:S(2)}) %collective-permute-start.4) | collective-permute-done | bytes 528416 | tf_op jit(solution)/shard_map/ppermute | solution.py:44
  148.3 7.3 %shard_map.77 = (bf16[32,64,128]{2,1,0:T(8,128)(2,1)}, f32[16,128]{1,0:T(8,128)}) custom-call(s32[2]{0:T(128)} %pad_add_fusion.3.ids_ref, bf16[129,16,128]{2,1,0:T(8,128)(2,1)} %copy-done.7, bf16[129,16,128]{2,1,0:T(8,128)(2,1)} %copy-done.8, bf16[2,32,128,128]{3,2,1,0:T(8,128)(2,1)} %refs_9_.7, ...), custom_call_target="tpu_custom_call" | custom-call | flops 8165000192 | tf_op jit(solution)/shard_map/pallas_call | solution.py:443
  155.6 2.7 %collective-permute-start.27 = (bf16[32,64,128]{2,1,0:T(8,128)(2,1)}, bf16[32,64,128]{2,1,0:T(8,128)(2,1)S(1)}, u32[]{:S(2)}, u32[]{:S(2)}) collective-permute-start(bf16[32,64,128]{2,1,0:T(8,128)(2,1)} %get-tuple-element.35.refs_11_), channel_id=1, source_target_pairs={{0,4},{1,5},{2,0},{3,1},{4,8},{5,9},{6,2},{7,3},{8,12},{9,13},{10,... | collective-permute-start | bytes 1572872 | tf_op jit(solution)/shard_map/ppermute | solution.py:44
  158.3 1.4 collective-permute-start.25
  160.5 8.6 %collective-permute-done.27.refs_1_.refs_11_ = bf16[32,64,128]{2,1,0:T(8,128)(2,1)S(1)} collective-permute-done((bf16[32,64,128]{2,1,0:T(8,128)(2,1)}, bf16[32,64,128]{2,1,0:T(8,128)(2,1)S(1)}, u32[]{:S(2)}, u32[]{:S(2)}) %collective-permute-start.27) | collective-permute-done | bytes 524320 | tf_op jit(solution)/shard_map/ppermute | solution.py:44
  169.1 2.2 collective-permute-start.31
  171.3 1.3 add_add_fusion.1.refs_0_
  172.9 1.7 collective-permute-start.28
  174.6 1.2 collective-permute-start.29
  175.9 8.9 %collective-permute-done.28 = f32[16,128]{1,0:T(8,128)S(1)} collective-permute-done((f32[16,128]{1,0:T(8,128)}, f32[16,128]{1,0:T(8,128)S(1)}, u32[]{:S(2)}, u32[]{:S(2)}) %collective-permute-start.28) | collective-permute-done | bytes 8224 | tf_op jit(solution)/shard_map/ppermute | solution.py:119
  184.8 1.2 collective-permute-start.30
  186.6 3.8 %collective-permute-done.30 = f32[16,128]{1,0:T(8,128)S(1)} collective-permute-done((f32[16,128]{1,0:T(8,128)}, f32[16,128]{1,0:T(8,128)S(1)}, u32[]{:S(2)}, u32[]{:S(2)}) %collective-permute-start.30) | collective-permute-done | bytes 8224 | tf_op jit(solution)/shard_map/ppermute | solution.py:119
  190.4 1.3 add_add_fusion.stats_ref
  191.7 1.7 shard_map.79
  193.4 0.8 copy-done.20
  194.2 6.2 %shard_map.80 = (f32[33,64,128]{2,1,0:T(8,128)}, f32[8,128]{1,0:T(8,128)}) custom-call(s32[3]{0:T(128)} %pad_add_fusion.5.ids_ref, f32[16,128]{1,0:T(8,128)} %get-tuple-element.36.refs_0_, bf16[129,16,128]{2,1,0:T(8,128)(2,1)} %get-tuple-element.30.refs_0_.refs_1_, bf16[129,16,128]{2,1,0:T(8,128)(2,1)} %copy-done.2, ...), custom_call_target="tpu_custom_call" | custom-call | flops 575000000 | tf_op jit(solution)/shard_map/pallas_call | solution.py:443
  201.1 2.0 collective-permute-start.40
  204.8 13.2 %shard_map.82 = (f32[33,64,128]{2,1,0:T(8,128)}, f32[8,128]{1,0:T(8,128)}) custom-call(s32[6]{0:T(128)} %stack.81.ids_ref, f32[16,128]{1,0:T(8,128)} %get-tuple-element.36.refs_0_, bf16[129,16,128]{2,1,0:T(8,128)(2,1)} %get-tuple-element.30.refs_0_.refs_1_, bf16[129,16,128]{2,1,0:T(8,128)(2,1)} %copy-done.2, ...), custom_call_target="tpu_custom_call" | custom-call | flops 575000000 | tf_op jit(solution)/shard_map/pallas_call | solution.py:443
  218.9 2.1 shard_map.84
  221.7 0.8 copy-done.21
  222.7 8.6 %shard_map.85 = (f32[33,64,128]{2,1,0:T(8,128)}, f32[8,128]{1,0:T(8,128)}) custom-call(s32[4]{0:T(128)} %pad_add_fusion.6.ids_ref, f32[16,128]{1,0:T(8,128)} %get-tuple-element.36.refs_0_, bf16[129,16,128]{2,1,0:T(8,128)(2,1)} %get-tuple-element.30.refs_0_.refs_1_, bf16[129,16,128]{2,1,0:T(8,128)(2,1)} %copy-done.2, ...), custom_call_target="tpu_custom_call" | custom-call | flops 575000000 | tf_op jit(solution)/shard_map/pallas_call | solution.py:443
  233.2 1.1 collective-permute-done.44.refs_12_
  234.3 0.8 copy-done.24
  235.1 5.5 %shard_map.87 = bf16[32,64,128]{2,1,0:T(8,128)(2,1)} custom-call(s32[3]{0:T(128)} %pad_add_fusion.1.ids_ref, f32[16,128]{1,0:T(8,128)} %get-tuple-element.36.refs_0_, bf16[129,16,128]{2,1,0:T(8,128)(2,1)} %get-tuple-element.30.refs_0_.refs_1_, bf16[129,16,128]{2,1,0:T(8,128)(2,1)} %copy-done.2, ...), custom_call_target="tpu_custom_call" | custom-call | flops 575000000 | tf_op jit(solution)/shard_map/pallas_call | solution.py:443
  (131 shorter events, 13.6 us)
Async XLA Ops:
  3.1 9.6 %collective-permute-start.1 = (bf16[2,32,64,128]{3,2,1,0:T(8,128)(2,1)}, bf16[2,32,64,128]{3,2,1,0:T(8,128)(2,1)}, u32[]{:S(2)}, u32[]{:S(2)}) collective-permute-start(bf16[2,32,64,128]{3,2,1,0:T(8,128)(2,1)} %constant_dynamic-slice_fusion.2), channel_id=1, source_target_pairs={{0,1},{1,0},{2,3},{3,2},{4,5},{5,4},{6,7},{7,6},{8,9},{9,8},{10,11... | collective-permute-start | bytes 3145736 | tf_op jit(solution)/shard_map/ppermute | solution.py:44
  3.5 85.7 %collective-permute-start.5 = (bf16[2,32,128,128]{3,2,1,0:T(8,128)(2,1)S(1)}, bf16[2,32,128,128]{3,2,1,0:T(8,128)(2,1)}, u32[]{:S(2)}, u32[]{:S(2)}) collective-permute-start(bf16[2,32,128,128]{3,2,1,0:T(8,128)(2,1)S(1)} %copy-done), channel_id=1, source_target_pairs={{0,1},{1,0},{2,3},{3,2},{4,5},{5,4},{6,7},{7,6},{8,9},{9,8},{10,11... | collective-permute-start | bytes 6291464 | tf_op jit(solution)/shard_map/ppermute | solution.py:44
  5.9 27.7 %collective-permute-start.9 = (bf16[32,64,128]{2,1,0:T(8,128)(2,1)}, bf16[32,64,128]{2,1,0:T(8,128)(2,1)S(1)}, u32[]{:S(2)}, u32[]{:S(2)}) collective-permute-start(bf16[32,64,128]{2,1,0:T(8,128)(2,1)} %get-tuple-element.45.refs_4_.refs_8_.refs_13_.refs_19_.refs_15_), channel_id=1, source_target_pairs={{0,8},{1,9},{2,10},{3,11},{4,12},{5,13},{6,14},{7,15},{8,0},{9,1},... | collective-permute-start | bytes 1572872 | tf_op jit(solution)/shard_map/ppermute | solution.py:44
  9.9 23.7 %collective-permute-start.21 = (bf16[32,64,128]{2,1,0:T(8,128)(2,1)}, bf16[32,64,128]{2,1,0:T(8,128)(2,1)}, u32[]{:S(2)}, u32[]{:S(2)}) collective-permute-start(bf16[32,64,128]{2,1,0:T(8,128)(2,1)} %get-tuple-element.45.refs_4_.refs_8_.refs_13_.refs_19_.refs_15_), channel_id=1, source_target_pairs={{0,2},{1,3},{2,0},{3,1},{4,6},{5,7},{6,4},{7,5},{8,10},{9,11},{10,... | collective-permute-start | bytes 1572872 | tf_op jit(solution)/shard_map/ppermute | solution.py:44
  11.4 1.2 collective-permute-start
  18.7 18.8 %collective-permute-start.10 = (bf16[129,16,128]{2,1,0:T(8,128)(2,1)}, bf16[129,16,128]{2,1,0:T(8,128)(2,1)S(1)}, u32[]{:S(2)}, u32[]{:S(2)}) collective-permute-start(bf16[129,16,128]{2,1,0:T(8,128)(2,1)} %get-tuple-element.26), channel_id=1, source_target_pairs={{0,2},{1,3},{2,0},{3,1},{4,6},{5,7},{6,4},{7,5},{8,10},{9,11},{10,... | collective-permute-start | bytes 1585160 | tf_op jit(solution)/shard_map/ppermute | solution.py:44
  19.3 26.4 %collective-permute-start.6 = (bf16[32,64,128]{2,1,0:T(8,128)(2,1)}, bf16[32,64,128]{2,1,0:T(8,128)(2,1)}, u32[]{:S(2)}, u32[]{:S(2)}) collective-permute-start(bf16[32,64,128]{2,1,0:T(8,128)(2,1)} %get-tuple-element.45.refs_4_.refs_8_.refs_13_.refs_19_.refs_15_), channel_id=1, source_target_pairs={{0,4},{1,5},{2,6},{3,7},{4,0},{5,1},{6,2},{7,3},{8,12},{9,13},{10,... | collective-permute-start | bytes 1572872 | tf_op jit(solution)/shard_map/ppermute | solution.py:44
  33.6 38.9 %collective-permute-start.15 = (bf16[129,16,128]{2,1,0:T(8,128)(2,1)}, bf16[129,16,128]{2,1,0:T(8,128)(2,1)}, u32[]{:S(2)}, u32[]{:S(2)}) collective-permute-start(bf16[129,16,128]{2,1,0:T(8,128)(2,1)} %get-tuple-element.29), channel_id=1, source_target_pairs={{0,8},{1,9},{2,10},{3,11},{4,12},{5,13},{6,14},{7,15},{8,0},{9,1},... | collective-permute-start | bytes 1585160 | tf_op jit(solution)/shard_map/ppermute | solution.py:44
  34.4 48.5 %collective-permute-start.3 = (bf16[129,16,128]{2,1,0:T(8,128)(2,1)}, bf16[129,16,128]{2,1,0:T(8,128)(2,1)S(1)}, u32[]{:S(2)}, u32[]{:S(2)}) collective-permute-start(bf16[129,16,128]{2,1,0:T(8,128)(2,1)} %get-tuple-element.25), channel_id=1, source_target_pairs={{0,10},{1,11},{2,8},{3,9},{4,14},{5,15},{6,12},{7,13},{8,2},{9,3},... | collective-permute-start | bytes 1585160 | tf_op jit(solution)/shard_map/ppermute | solution.py:44
  37.5 46.7 %collective-permute-start.12 = (bf16[129,16,128]{2,1,0:T(8,128)(2,1)}, bf16[129,16,128]{2,1,0:T(8,128)(2,1)}, u32[]{:S(2)}, u32[]{:S(2)}) collective-permute-start(bf16[129,16,128]{2,1,0:T(8,128)(2,1)} %get-tuple-element.27), channel_id=1, source_target_pairs={{0,4},{1,5},{2,6},{3,7},{4,0},{5,1},{6,2},{7,3},{8,12},{9,13},{10,... | collective-permute-start | bytes 1585160 | tf_op jit(solution)/shard_map/ppermute | solution.py:44
  45.7 42.8 %collective-permute-start.11 = (bf16[32,64,128]{2,1,0:T(8,128)(2,1)}, bf16[32,64,128]{2,1,0:T(8,128)(2,1)S(1)}, u32[]{:S(2)}, u32[]{:S(2)}) collective-permute-start(bf16[32,64,128]{2,1,0:T(8,128)(2,1)} %shard_map.71.refs_6_.refs_21_.refs_27_.refs_23_), channel_id=1, source_target_pairs={{0,4},{1,5},{2,6},{3,7},{4,0},{5,1},{6,2},{7,3},{8,12},{9,13},{10,... | collective-permute-start | bytes 1572872 | tf_op jit(solution)/shard_map/ppermute | solution.py:44
  72.5 18.4 %collective-permute-start.23 = (bf16[32,64,128]{2,1,0:T(8,128)(2,1)}, bf16[32,64,128]{2,1,0:T(8,128)(2,1)}, u32[]{:S(2)}, u32[]{:S(2)}) collective-permute-start(bf16[32,64,128]{2,1,0:T(8,128)(2,1)} %shard_map.71.refs_6_.refs_21_.refs_27_.refs_23_), channel_id=1, source_target_pairs={{0,1},{1,0},{2,3},{3,2},{4,5},{5,4},{6,7},{7,6},{8,9},{9,8},{10,11... | collective-permute-start | bytes 1572872 | tf_op jit(solution)/shard_map/ppermute | solution.py:44
  82.9 15.2 %collective-permute-start.19 = (bf16[32,64,128]{2,1,0:T(8,128)(2,1)}, bf16[32,64,128]{2,1,0:T(8,128)(2,1)}, u32[]{:S(2)}, u32[]{:S(2)}) collective-permute-start(bf16[32,64,128]{2,1,0:T(8,128)(2,1)} %shard_map.71.refs_6_.refs_21_.refs_27_.refs_23_), channel_id=1, source_target_pairs={{0,2},{1,3},{2,0},{3,1},{4,6},{5,7},{6,4},{7,5},{8,10},{9,11},{10,... | collective-permute-start | bytes 1572872 | tf_op jit(solution)/shard_map/ppermute | solution.py:44
  84.3 21.5 %collective-permute-start.22 = (bf16[32,64,128]{2,1,0:T(8,128)(2,1)}, bf16[32,64,128]{2,1,0:T(8,128)(2,1)S(1)}, u32[]{:S(2)}, u32[]{:S(2)}) collective-permute-start(bf16[32,64,128]{2,1,0:T(8,128)(2,1)} %collective-permute-done.21.refs_6_.refs_15_.refs_21_.refs_17_), channel_id=1, source_target_pairs={{0,1},{1,0},{2,3},{3,2},{4,5},{5,4},{6,7},{7,6},{8,9},{9,8},{10,11... | collective-permute-start | bytes 1572872 | tf_op jit(solution)/shard_map/ppermute | solution.py:44
  88.5 26.6 %collective-permute-start.17 = (bf16[32,64,128]{2,1,0:T(8,128)(2,1)}, bf16[32,64,128]{2,1,0:T(8,128)(2,1)}, u32[]{:S(2)}, u32[]{:S(2)}) collective-permute-start(bf16[32,64,128]{2,1,0:T(8,128)(2,1)} %shard_map.70.refs_4_.refs_17_.refs_23_.refs_19_), channel_id=1, source_target_pairs={{0,1},{1,0},{2,3},{3,2},{4,5},{5,4},{6,7},{7,6},{8,9},{9,8},{10,11... | collective-permute-start | bytes 1572872 | tf_op jit(solution)/shard_map/ppermute | solution.py:44
  89.3 25.9 %collective-permute-start.7 = (bf16[32,64,128]{2,1,0:T(8,128)(2,1)}, bf16[32,64,128]{2,1,0:T(8,128)(2,1)S(1)}, u32[]{:S(2)}, u32[]{:S(2)}) collective-permute-start(bf16[32,64,128]{2,1,0:T(8,128)(2,1)} %shard_map.70.refs_4_.refs_17_.refs_23_.refs_19_), channel_id=1, source_target_pairs={{0,2},{1,3},{2,0},{3,1},{4,6},{5,7},{6,4},{7,5},{8,10},{9,11},{10,... | collective-permute-start | bytes 1572872 | tf_op jit(solution)/shard_map/ppermute | solution.py:44
  90.8 25.8 %collective-permute-start.16 = (bf16[129,16,128]{2,1,0:T(8,128)(2,1)}, bf16[129,16,128]{2,1,0:T(8,128)(2,1)S(1)}, u32[]{:S(2)}, u32[]{:S(2)}) collective-permute-start(bf16[129,16,128]{2,1,0:T(8,128)(2,1)} %shard_map.73), channel_id=1, source_target_pairs={{0,12},{1,13},{2,14},{3,15},{4,8},{5,9},{6,10},{7,11},{8,4},{9,5},... | collective-permute-start | bytes 1585160 | tf_op jit(solution)/shard_map/ppermute | solution.py:44
  98.1 8.3 %collective-permute-start.20 = (bf16[32,64,128]{2,1,0:T(8,128)(2,1)}, bf16[32,64,128]{2,1,0:T(8,128)(2,1)S(1)}, u32[]{:S(2)}, u32[]{:S(2)}) collective-permute-start(bf16[32,64,128]{2,1,0:T(8,128)(2,1)} %collective-permute-done.19.refs_4_.refs_23_.refs_29_.refs_25_), channel_id=1, source_target_pairs={{0,1},{1,0},{2,3},{3,2},{4,5},{5,4},{6,7},{7,6},{8,9},{9,8},{10,11... | collective-permute-start | bytes 1572872 | tf_op jit(solution)/shard_map/ppermute | solution.py:44
  105.8 25.9 %collective-permute-start.18 = (bf16[32,64,128]{2,1,0:T(8,128)(2,1)S(1)}, bf16[32,64,128]{2,1,0:T(8,128)(2,1)}, u32[]{:S(2)}, u32[]{:S(2)}) collective-permute-start(bf16[32,64,128]{2,1,0:T(8,128)(2,1)S(1)} %copy-done.5), channel_id=1, source_target_pairs={{0,1},{1,0},{2,3},{3,2},{4,5},{5,4},{6,7},{7,6},{8,9},{9,8},{10,11... | collective-permute-start | bytes 1572872 | tf_op jit(solution)/shard_map/ppermute | solution.py:44
  106.4 25.4 %collective-permute-start.13 = (bf16[32,64,128]{2,1,0:T(8,128)(2,1)S(1)}, bf16[32,64,128]{2,1,0:T(8,128)(2,1)}, u32[]{:S(2)}, u32[]{:S(2)}) collective-permute-start(bf16[32,64,128]{2,1,0:T(8,128)(2,1)S(1)} %copy-done.5), channel_id=1, source_target_pairs={{0,2},{1,3},{2,0},{3,1},{4,6},{5,7},{6,4},{7,5},{8,10},{9,11},{10,... | collective-permute-start | bytes 1572872 | tf_op jit(solution)/shard_map/ppermute | solution.py:44
  115.1 24.2 %collective-permute-start.2 = (bf16[129,16,128]{2,1,0:T(8,128)(2,1)}, bf16[129,16,128]{2,1,0:T(8,128)(2,1)S(1)}, u32[]{:S(2)}, u32[]{:S(2)}) collective-permute-start(bf16[129,16,128]{2,1,0:T(8,128)(2,1)} %get-tuple-element.23), channel_id=1, source_target_pairs={{0,6},{1,7},{2,4},{3,5},{4,2},{5,3},{6,0},{7,1},{8,14},{9,15},{10,... | collective-permute-start | bytes 1585160 | tf_op jit(solution)/shard_map/ppermute | solution.py:44
  115.2 24.1 %copy-start.10 = (bf16[32,64,128]{2,1,0:T(8,128)(2,1)}, bf16[32,64,128]{2,1,0:T(8,128)(2,1)S(1)}, u32[]{:S(2)}) copy-start(bf16[32,64,128]{2,1,0:T(8,128)(2,1)S(1)} %collective-permute-done.7.refs_4_.refs_19_.refs_25_.refs_21_) | copy-start | bytes 1572868
  115.2 32.2 %collective-permute-start.4 = (bf16[129,16,128]{2,1,0:T(8,128)(2,1)}, bf16[129,16,128]{2,1,0:T(8,128)(2,1)S(1)}, u32[]{:S(2)}, u32[]{:S(2)}) collective-permute-start(bf16[129,16,128]{2,1,0:T(8,128)(2,1)} %shard_map.69), channel_id=1, source_target_pairs={{0,14},{1,15},{2,12},{3,13},{4,10},{5,11},{6,8},{7,9},{8,6},{9,7},... | collective-permute-start | bytes 1585160 | tf_op jit(solution)/shard_map/ppermute | solution.py:44
  116.7 15.1 %copy-start.6 = (bf16[129,16,128]{2,1,0:T(8,128)(2,1)}, bf16[129,16,128]{2,1,0:T(8,128)(2,1)S(1)}, u32[]{:S(2)}) copy-start(bf16[129,16,128]{2,1,0:T(8,128)(2,1)S(1)} %collective-permute-done.16.refs_1_.refs_7_) | copy-start | bytes 1585156
  116.7 30.7 %collective-permute-start.8 = (bf16[32,64,128]{2,1,0:T(8,128)(2,1)S(1)}, bf16[32,64,128]{2,1,0:T(8,128)(2,1)S(1)}, u32[]{:S(2)}, u32[]{:S(2)}) collective-permute-start(bf16[32,64,128]{2,1,0:T(8,128)(2,1)S(1)} %collective-permute-done.7.refs_4_.refs_19_.refs_25_.refs_21_), channel_id=1, source_target_pairs={{0,1},{1,0},{2,3},{3,2},{4,5},{5,4},{6,7},{7,6},{8,9},{9,8},{10,11... | collective-permute-start | bytes 1572872 | tf_op jit(solution)/shard_map/ppermute | solution.py:44
  131.7 15.6 %collective-permute-start.14 = (bf16[32,64,128]{2,1,0:T(8,128)(2,1)}, bf16[32,64,128]{2,1,0:T(8,128)(2,1)}, u32[]{:S(2)}, u32[]{:S(2)}) collective-permute-start(bf16[32,64,128]{2,1,0:T(8,128)(2,1)} %collective-permute-done.13.refs_6_.refs_27_.refs_33_.refs_29_), channel_id=1, source_target_pairs={{0,1},{1,0},{2,3},{3,2},{4,5},{5,4},{6,7},{7,6},{8,9},{9,8},{10,11... | collective-permute-start | bytes 1572872 | tf_op jit(solution)/shard_map/ppermute | solution.py:44
  155.6 13.5 %collective-permute-start.27 = (bf16[32,64,128]{2,1,0:T(8,128)(2,1)}, bf16[32,64,128]{2,1,0:T(8,128)(2,1)S(1)}, u32[]{:S(2)}, u32[]{:S(2)}) collective-permute-start(bf16[32,64,128]{2,1,0:T(8,128)(2,1)} %get-tuple-element.35.refs_11_), channel_id=1, source_target_pairs={{0,4},{1,5},{2,0},{3,1},{4,8},{5,9},{6,2},{7,3},{8,12},{9,13},{10,... | collective-permute-start | bytes 1572872 | tf_op jit(solution)/shard_map/ppermute | solution.py:44
  158.3 14.2 %collective-permute-start.35 = (bf16[32,64,128]{2,1,0:T(8,128)(2,1)}, bf16[32,64,128]{2,1,0:T(8,128)(2,1)S(1)}, u32[]{:S(2)}, u32[]{:S(2)}) collective-permute-start(bf16[32,64,128]{2,1,0:T(8,128)(2,1)} %get-tuple-element.35.refs_11_), channel_id=1, source_target_pairs={{0,2},{1,3},{2,6},{3,7},{4,0},{5,1},{6,10},{7,11},{8,4},{9,5},{10,... | collective-permute-start | bytes 1572872 | tf_op jit(solution)/shard_map/ppermute | solution.py:44
  158.3 1.9 collective-permute-start.24
  158.3 12.9 %collective-permute-start.25 = (f32[16,128]{1,0:T(8,128)}, f32[16,128]{1,0:T(8,128)S(1)}, u32[]{:S(2)}, u32[]{:S(2)}) collective-permute-start(f32[16,128]{1,0:T(8,128)} %get-tuple-element.34), channel_id=1, source_target_pairs={{0,2},{1,3},{2,0},{3,1},{4,6},{5,7},{6,4},{7,5},{8,10},{9,11},{10,... | collective-permute-start | bytes 24584 | tf_op jit(solution)/shard_map/ppermute | solution.py:119
  159.8 11.5 %collective-permute-start.26 = (f32[16,128]{1,0:T(8,128)}, f32[16,128]{1,0:T(8,128)S(1)}, u32[]{:S(2)}, u32[]{:S(2)}) collective-permute-start(f32[16,128]{1,0:T(8,128)} %get-tuple-element.34), channel_id=1, source_target_pairs={{0,3},{1,2},{2,1},{3,0},{4,7},{5,6},{6,5},{7,4},{8,11},{9,10},{10,... | collective-permute-start | bytes 24584 | tf_op jit(solution)/shard_map/ppermute | solution.py:119
  160.2 33.2 %collective-permute-start.32 = (bf16[32,64,128]{2,1,0:T(8,128)(2,1)}, bf16[32,64,128]{2,1,0:T(8,128)(2,1)S(1)}, u32[]{:S(2)}, u32[]{:S(2)}) collective-permute-start(bf16[32,64,128]{2,1,0:T(8,128)(2,1)} %get-tuple-element.35.refs_11_), channel_id=1, source_target_pairs={{0,1},{1,0},{2,3},{3,2},{4,5},{5,4},{6,7},{7,6},{8,9},{9,8},{10,11... | collective-permute-start | bytes 1572872 | tf_op jit(solution)/shard_map/ppermute | solution.py:44
  169.1 31.4 %collective-permute-start.31 = (bf16[32,64,128]{2,1,0:T(8,128)(2,1)S(1)}, bf16[32,64,128]{2,1,0:T(8,128)(2,1)}, u32[]{:S(2)}, u32[]{:S(2)}) collective-permute-start(bf16[32,64,128]{2,1,0:T(8,128)(2,1)S(1)} %collective-permute-done.27.refs_1_.refs_11_), channel_id=1, source_target_pairs={{0,4},{1,5},{2,0},{3,1},{4,8},{5,9},{6,2},{7,3},{8,12},{9,13},{10,... | collective-permute-start | bytes 1572872 | tf_op jit(solution)/shard_map/ppermute | solution.py:44
  172.6 20.8 %copy-start.14 = (bf16[32,64,128]{2,1,0:T(8,128)(2,1)}, bf16[32,64,128]{2,1,0:T(8,128)(2,1)S(1)}, u32[]{:S(2)}) copy-start(bf16[32,64,128]{2,1,0:T(8,128)(2,1)S(1)} %collective-permute-done.35.refs_13_) | copy-start | bytes 1572868
  172.6 28.4 %collective-permute-start.38 = (bf16[32,64,128]{2,1,0:T(8,128)(2,1)S(1)}, bf16[32,64,128]{2,1,0:T(8,128)(2,1)S(1)}, u32[]{:S(2)}, u32[]{:S(2)}) collective-permute-start(bf16[32,64,128]{2,1,0:T(8,128)(2,1)S(1)} %collective-permute-done.35.refs_13_), channel_id=1, source_target_pairs={{0,2},{1,3},{2,6},{3,7},{4,0},{5,1},{6,10},{7,11},{8,4},{9,5},{10,... | collective-permute-start | bytes 1572872 | tf_op jit(solution)/shard_map/ppermute | solution.py:44
  172.9 11.9 %collective-permute-start.28 = (f32[16,128]{1,0:T(8,128)}, f32[16,128]{1,0:T(8,128)S(1)}, u32[]{:S(2)}, u32[]{:S(2)}) collective-permute-start(f32[16,128]{1,0:T(8,128)} %shard_map.78), channel_id=1, source_target_pairs={{0,4},{1,5},{2,6},{3,7},{4,0},{5,1},{6,2},{7,3},{8,12},{9,13},{10,... | collective-permute-start | bytes 24584 | tf_op jit(solution)/shard_map/ppermute | solution.py:119
  174.6 11.3 %collective-permute-start.29 = (f32[16,128]{1,0:T(8,128)}, f32[16,128]{1,0:T(8,128)S(1)}, u32[]{:S(2)}, u32[]{:S(2)}) collective-permute-start(f32[16,128]{1,0:T(8,128)} %shard_map.78), channel_id=1, source_target_pairs={{0,8},{1,9},{2,10},{3,11},{4,12},{5,13},{6,14},{7,15},{8,0},{9,1},... | collective-permute-start | bytes 24584 | tf_op jit(solution)/shard_map/ppermute | solution.py:119
  184.8 5.7 %collective-permute-start.30 = (f32[16,128]{1,0:T(8,128)}, f32[16,128]{1,0:T(8,128)S(1)}, u32[]{:S(2)}, u32[]{:S(2)}) collective-permute-start(f32[16,128]{1,0:T(8,128)} %shard_map.78), channel_id=1, source_target_pairs={{0,12},{1,13},{2,14},{3,15},{4,8},{5,9},{6,10},{7,11},{8,4},{9,5},... | collective-permute-start | bytes 24584 | tf_op jit(solution)/shard_map/ppermute | solution.py:119
  186.0 15.2 %collective-permute-start.34 = (bf16[32,64,128]{2,1,0:T(8,128)(2,1)}, bf16[32,64,128]{2,1,0:T(8,128)(2,1)S(1)}, u32[]{:S(2)}, u32[]{:S(2)}) collective-permute-start(bf16[32,64,128]{2,1,0:T(8,128)(2,1)} %copy-done.13), channel_id=1, source_target_pairs={{0,1},{1,0},{2,3},{3,2},{4,5},{5,4},{6,7},{7,6},{8,9},{9,8},{10,11... | collective-permute-start | bytes 1572872 | tf_op jit(solution)/shard_map/ppermute | solution.py:44
  190.4 13.4 %collective-permute-start.36 = (bf16[32,64,128]{2,1,0:T(8,128)(2,1)S(1)}, bf16[32,64,128]{2,1,0:T(8,128)(2,1)S(1)}, u32[]{:S(2)}, u32[]{:S(2)}) collective-permute-start(bf16[32,64,128]{2,1,0:T(8,128)(2,1)S(1)} %collective-permute-done.35.refs_13_), channel_id=1, source_target_pairs={{0,1},{1,0},{2,3},{3,2},{4,5},{5,4},{6,7},{7,6},{8,9},{9,8},{10,11... | collective-permute-start | bytes 1572872 | tf_op jit(solution)/shard_map/ppermute | solution.py:44
  200.5 3.4 %collective-permute-start.37 = (bf16[32,64,128]{2,1,0:T(8,128)(2,1)}, bf16[32,64,128]{2,1,0:T(8,128)(2,1)S(1)}, u32[]{:S(2)}, u32[]{:S(2)}) collective-permute-start(bf16[32,64,128]{2,1,0:T(8,128)(2,1)} %shard_map.81.refs_15_), channel_id=1, source_target_pairs={{0,1},{1,0},{2,3},{3,2},{4,5},{5,4},{6,7},{7,6},{8,9},{9,8},{10,11... | collective-permute-start | bytes 1572872 | tf_op jit(solution)/shard_map/ppermute | solution.py:44
  201.0 2.8 %collective-permute-start.39 = (bf16[32,64,128]{2,1,0:T(8,128)(2,1)S(1)}, bf16[32,64,128]{2,1,0:T(8,128)(2,1)}, u32[]{:S(2)}, u32[]{:S(2)}) collective-permute-start(bf16[32,64,128]{2,1,0:T(8,128)(2,1)S(1)} %collective-permute-done.38.refs_17_), channel_id=1, source_target_pairs={{0,1},{1,0},{2,3},{3,2},{4,5},{5,4},{6,7},{7,6},{8,9},{9,8},{10,11... | collective-permute-start | bytes 1572872 | tf_op jit(solution)/shard_map/ppermute | solution.py:44
  201.1 16.9 %collective-permute-start.33 = (bf16[32,64,128]{2,1,0:T(8,128)(2,1)}, bf16[32,64,128]{2,1,0:T(8,128)(2,1)}, u32[]{:S(2)}, u32[]{:S(2)}) collective-permute-start(bf16[32,64,128]{2,1,0:T(8,128)(2,1)} %shard_map.81.refs_15_), channel_id=1, source_target_pairs={{0,4},{1,5},{2,0},{3,1},{4,8},{5,9},{6,2},{7,3},{8,12},{9,13},{10,... | collective-permute-start | bytes 1572872 | tf_op jit(solution)/shard_map/ppermute | solution.py:44
  201.1 17.0 %collective-permute-start.40 = (bf16[32,64,128]{2,1,0:T(8,128)(2,1)S(1)}, bf16[32,64,128]{2,1,0:T(8,128)(2,1)S(1)}, u32[]{:S(2)}, u32[]{:S(2)}) collective-permute-start(bf16[32,64,128]{2,1,0:T(8,128)(2,1)S(1)} %collective-permute-done.38.refs_17_), channel_id=1, source_target_pairs={{0,2},{1,3},{2,6},{3,7},{4,0},{5,1},{6,10},{7,11},{8,4},{9,5},{10,... | collective-permute-start | bytes 1572872 | tf_op jit(solution)/shard_map/ppermute | solution.py:44
  218.0 3.7 %collective-permute-start.42 = (bf16[32,64,128]{2,1,0:T(8,128)(2,1)}, bf16[32,64,128]{2,1,0:T(8,128)(2,1)S(1)}, u32[]{:S(2)}, u32[]{:S(2)}) collective-permute-start(bf16[32,64,128]{2,1,0:T(8,128)(2,1)} %shard_map.83.lower_ref.refs_11_), channel_id=1, source_target_pairs={{0,1},{1,0},{2,3},{3,2},{4,5},{5,4},{6,7},{7,6},{8,9},{9,8},{10,11... | collective-permute-start | bytes 1572872 | tf_op jit(solution)/shard_map/ppermute | solution.py:44
  218.1 3.6 %collective-permute-start.43 = (bf16[32,64,128]{2,1,0:T(8,128)(2,1)S(1)}, bf16[32,64,128]{2,1,0:T(8,128)(2,1)S(1)}, u32[]{:S(2)}, u32[]{:S(2)}) collective-permute-start(bf16[32,64,128]{2,1,0:T(8,128)(2,1)S(1)} %collective-permute-done.40.upper_ref.refs_13_), channel_id=1, source_target_pairs={{0,1},{1,0},{2,3},{3,2},{4,5},{5,4},{6,7},{7,6},{8,9},{9,8},{10,11... | collective-permute-start | bytes 1572872 | tf_op jit(solution)/shard_map/ppermute | solution.py:44
  221.0 10.3 %collective-permute-start.41 = (bf16[32,64,128]{2,1,0:T(8,128)(2,1)}, bf16[32,64,128]{2,1,0:T(8,128)(2,1)S(1)}, u32[]{:S(2)}, u32[]{:S(2)}) collective-permute-start(bf16[32,64,128]{2,1,0:T(8,128)(2,1)} %shard_map.84), channel_id=1, source_target_pairs={{0,4},{1,3},{2,0},{3,7},{4,8},{5,1},{6,2},{7,11},{8,12},{9,5},{10,... | collective-permute-start | bytes 1572872 | tf_op jit(solution)/shard_map/ppermute | solution.py:44
  232.1 2.2 collective-permute-start.44
  (26 other events, 62.6 us)

commit v14 on v13

--- a/solution.py
+++ b/solution.py
@@ -110,17 +110,17 @@
     return units
 
 
-def spread(value, devices, before):
+def spread(value, devices):
     step = 1
+    values = []
     while step < devices:
-        if step > 1:
-            value = after(value, before)
         masks = [step] if 2 * step == devices else [step, 2 * step, 3 * step]
         parts = [lax.ppermute(value, BOTH, [(d, d ^ m) for d in range(devices)]) for m in masks]
         for part in parts:
             value = value + part
+        values.append(value)
         step *= 4
-    return value
+    return values
 
 
 def pack_kernel(order, capacity, blocks, terms, ids_ref, plan_ref, other_plan_ref, *refs):
@@ -528,11 +528,12 @@
             own_rows,
         )
 
-    rest = total
+    stats = spread(stats, owners * halves)
+    rest = after(total, stats[0])
     ahead = ring_send(rest, owners, halves, (1,) * halves)
     behind = ring_send(rest, owners, halves, (-1,) * halves)
     entries = blocks * owners * height * width
-    scale, rayleigh = scales(spread(stats, owners * halves, ahead), entries)
+    scale, rayleigh = scales(stats[-1], entries)
     reach = (owners - 1) // 2
     waves = [(near[m], far[m]) for m in range(owners)]
 

time: 243 us -> 248 us (1.021)
  waiting for transfers between devices: 111 us -> 119 us
    ppermute x6, waiting for transfers between devices: 12.7 us -> 17.4 us  [spread(): lax.ppermute(value, BOTH, [(d, d ^ m) for d in range(devices)])]
    ppermute x39, waiting for transfers between devices: 98.5 us -> 102 us  [permute(): return lax.ppermute(value, BOTH, pairs)]
    unnamed x58 -> x60, local copies, waits for them, and re-layouts: 7.77 us -> 8.12 us
  transfers between devices with their start and end apart: 45 -> 45, of which waited for: 13 -> 15; matrix products, arithmetic and copies ran while one was open for 4% -> 3% of each run, Pallas kernels for 25% -> 24%
where the time goes in v14:
time: 248 us; the launch traced here: 247 us
  waiting for transfers between devices  119 us (48%)
  Pallas kernels  72.3 us (29%)
  starting transfers between devices  35.9 us (14%)
  local copies, waits for them, and re-layouts  13.4 us (5%)
  other arithmetic  4.8 us (2%)
    ppermute x39, waiting for transfers between devices, permute(): return lax.ppermute(value, BOTH, pairs)  102 us
    pallas_call x8, Pallas kernels, apply_group(): pl.pallas_call(functools.partial(apply_kernel, sources, choices, first, e...  63 us
    ppermute x39, starting transfers between devices, permute(): return lax.ppermute(value, BOTH, pairs)  30.1 us
    ppermute x6, waiting for transfers between devices, spread(): lax.ppermute(value, BOTH, [(d, d ^ m) for d in range(devices)])  17.4 us
    unnamed x60, local copies, waits for them, and re-layouts  8.12 us
    ppermute x6, starting transfers between devices, spread(): lax.ppermute(value, BOTH, [(d, d ^ m) for d in range(devices)])  5.8 us
    pallas_call x1, Pallas kernels, pack(): pl.pallas_call(functools.partial(pack_kernel, order, capacity, blocks, te...  5.43 us
  transfers between devices with their start and end apart: 45, of which 15 were waited for; matrix products, arithmetic and copies ran while one was open for 3% of the time, Pallas kernels for 24%

profile of v14, /device:TPU:0, one launch (start us, length us, event | category | flops | bytes accessed | tf_op | source)
XLA Modules:
  0.0 246.7 jit_solution(2621431773504528840)
XLA Ops:
  0.6 2.4 constant_dynamic-slice_fusion.2
  3.6 2.2 constant_dynamic-slice_fusion
  5.9 4.0 %collective-permute-start.9 = (bf16[32,64,128]{2,1,0:T(8,128)(2,1)}, bf16[32,64,128]{2,1,0:T(8,128)(2,1)S(1)}, u32[]{:S(2)}, u32[]{:S(2)}) collective-permute-start(bf16[32,64,128]{2,1,0:T(8,128)(2,1)} %get-tuple-element.45.refs_4_.refs_8_.refs_13_.refs_19_.refs_15_), channel_id=1, source_target_pairs={{0,8},{1,9},{2,10},{3,11},{4,12},{5,13},{6,14},{7,15},{8,0},{9,1},... | collective-permute-start | bytes 1572872 | tf_op jit(solution)/shard_map/ppermute | solution.py:44
  9.9 1.5 collective-permute-start.21
  13.2 5.4 %shard_map.68 = (bf16[129,16,128]{2,1,0:T(8,128)(2,1)}, bf16[129,16,128]{2,1,0:T(8,128)(2,1)}, bf16[129,16,128]{2,1,0:T(8,128)(2,1)}, bf16[129,16,128]{2,1,0:T(8...) custom-call(s32[2]{0:T(128)} %pad_add_fusion.4.ids_ref, ...), custom_call_target="tpu_custom_call" | custom-call | flops 5750000128 | tf_op jit(solution)/shard_map/pallas_call | solution.py:186
  19.2 1.6 collective-permute-start.6
  20.8 12.8 %collective-permute-done.9.refs_0_ = bf16[32,64,128]{2,1,0:T(8,128)(2,1)S(1)} collective-permute-done((bf16[32,64,128]{2,1,0:T(8,128)(2,1)}, bf16[32,64,128]{2,1,0:T(8,128)(2,1)S(1)}, u32[]{:S(2)}, u32[]{:S(2)}) %collective-permute-start.9) | collective-permute-done | bytes 524320 | tf_op jit(solution)/shard_map/ppermute | solution.py:44
  33.6 0.8 copy-done.3
  34.4 3.1 %collective-permute-start.3 = (bf16[129,16,128]{2,1,0:T(8,128)(2,1)}, bf16[129,16,128]{2,1,0:T(8,128)(2,1)S(1)}, u32[]{:S(2)}, u32[]{:S(2)}) collective-permute-start(bf16[129,16,128]{2,1,0:T(8,128)(2,1)} %get-tuple-element.25), channel_id=1, source_target_pairs={{0,10},{1,11},{2,8},{3,9},{4,14},{5,15},{6,12},{7,13},{8,2},{9,3},... | collective-permute-start | bytes 1585160 | tf_op jit(solution)/shard_map/ppermute | solution.py:44
  37.5 1.9 collective-permute-start.12
  39.5 6.2 %collective-permute-done.6.refs_0_ = bf16[32,64,128]{2,1,0:T(8,128)(2,1)} collective-permute-done((bf16[32,64,128]{2,1,0:T(8,128)(2,1)}, bf16[32,64,128]{2,1,0:T(8,128)(2,1)}, u32[]{:S(2)}, u32[]{:S(2)}) %collective-permute-start.6) | collective-permute-done | bytes 524320 | tf_op jit(solution)/shard_map/ppermute | solution.py:44
  45.7 26.8 %collective-permute-done.15.refs_1_.refs_5_ = bf16[129,16,128]{2,1,0:T(8,128)(2,1)} collective-permute-done((bf16[129,16,128]{2,1,0:T(8,128)(2,1)}, bf16[129,16,128]{2,1,0:T(8,128)(2,1)}, u32[]{:S(2)}, u32[]{:S(2)}) %collective-permute-start.15) | collective-permute-done | bytes 528416 | tf_op jit(solution)/shard_map/ppermute | solution.py:44
  72.5 10.4 %collective-permute-done.3.refs_1_.refs_0_.refs_6_ = bf16[129,16,128]{2,1,0:T(8,128)(2,1)S(1)} collective-permute-done((bf16[129,16,128]{2,1,0:T(8,128)(2,1)}, bf16[129,16,128]{2,1,0:T(8,128)(2,1)S(1)}, u32[]{:S(2)}, u32[]{:S(2)}) %collective-permute-start.3) | collective-permute-done | bytes 528416 | tf_op jit(solution)/shard_map/ppermute | solution.py:44
  84.4 4.1 %collective-permute-done.11.refs_0_ = bf16[32,64,128]{2,1,0:T(8,128)(2,1)S(1)} collective-permute-done((bf16[32,64,128]{2,1,0:T(8,128)(2,1)}, bf16[32,64,128]{2,1,0:T(8,128)(2,1)S(1)}, u32[]{:S(2)}, u32[]{:S(2)}) %collective-permute-start.11) | collective-permute-done | bytes 524320 | tf_op jit(solution)/shard_map/ppermute | solution.py:44
  88.5 0.8 copy-done.4
  89.3 1.6 collective-permute-start.7
  90.8 2.4 collective-permute-start.16
  93.2 4.9 %collective-permute-done.19.refs_4_.refs_23_.refs_29_.refs_25_ = bf16[32,64,128]{2,1,0:T(8,128)(2,1)} collective-permute-done((bf16[32,64,128]{2,1,0:T(8,128)(2,1)}, bf16[32,64,128]{2,1,0:T(8,128)(2,1)}, u32[]{:S(2)}, u32[]{:S(2)}) %collective-permute-start.19) | collective-permute-done | bytes 524320 | tf_op jit(solution)/shard_map/ppermute | solution.py:44
  98.1 7.7 %shard_map.74 = (f32[33,64,128]{2,1,0:T(8,128)}, f32[8,128]{1,0:T(8,128)}) custom-call(s32[2]{0:T(128)} %pad_add_fusion.3.ids_ref, bf16[129,16,128]{2,1,0:T(8,128)(2,1)} %get-tuple-element.30.refs_0_.refs_1_, bf16[129,16,128]{2,1,0:T(8,128)(2,1)} %collective-permute-done.15.refs_1_.refs_5_, bf16[2,32,128,128]{3,2,1,0:T(8,128)(2,1)} %refs_9_.7, ...), custom_call_target="tpu_custom_call" | custom-call | flops 8165000192 | tf_op jit(solution)/shard_map/pallas_call | solution.py:443
  107.4 7.6 %shard_map.75 = (f32[33,64,128]{2,1,0:T(8,128)}, f32[8,128]{1,0:T(8,128)}) custom-call(s32[2]{0:T(128)} %pad_add_fusion.3.ids_ref, bf16[129,16,128]{2,1,0:T(8,128)(2,1)} %copy-done.1, bf16[129,16,128]{2,1,0:T(8,128)(2,1)} %copy-done.2, bf16[2,32,128,128]{3,2,1,0:T(8,128)(2,1)} %refs_9_.7, bf16[2,32,128,128]{3,2,1,0:T(8,128)(2,1)} %collective-permute-done.5.refs_3_.refs_10_, ...), custom_call_target="tpu_custom_call" | custom-call | flops 8165000192 | tf_op jit(solution)/shard_map/pallas_call | solution.py:443
  115.1 1.6 collective-permute-start.4
  116.7 15.2 %collective-permute-done.13.refs_6_.refs_27_.refs_33_.refs_29_ = bf16[32,64,128]{2,1,0:T(8,128)(2,1)} collective-permute-done((bf16[32,64,128]{2,1,0:T(8,128)(2,1)S(1)}, bf16[32,64,128]{2,1,0:T(8,128)(2,1)}, u32[]{:S(2)}, u32[]{:S(2)}) %collective-permute-start.13) | collective-permute-done | bytes 524320 | tf_op jit(solution)/shard_map/ppermute | solution.py:44
  131.9 7.4 %shard_map.76 = (f32[33,64,128]{2,1,0:T(8,128)}, f32[8,128]{1,0:T(8,128)}) custom-call(s32[2]{0:T(128)} %pad_add_fusion.3.ids_ref, bf16[129,16,128]{2,1,0:T(8,128)(2,1)} %collective-permute-done.12.refs_1_.refs_0_.refs_3_, bf16[129,16,128]{2,1,0:T(8,128)(2,1)} %copy-done.6, bf16[2,32,128,128]{3,2,1,0:T(8,128)(2,1)} %refs_9_.7, ...), custom_call_target="tpu_custom_call" | custom-call | flops 8165000192 | tf_op jit(solution)/shard_map/pallas_call | solution.py:443
  139.3 7.7 %collective-permute-done.4.refs_1_.refs_8_ = bf16[129,16,128]{2,1,0:T(8,128)(2,1)S(1)} collective-permute-done((bf16[129,16,128]{2,1,0:T(8,128)(2,1)}, bf16[129,16,128]{2,1,0:T(8,128)(2,1)S(1)}, u32[]{:S(2)}, u32[]{:S(2)}) %collective-permute-start.4) | collective-permute-done | bytes 528416 | tf_op jit(solution)/shard_map/ppermute | solution.py:44
  147.9 7.3 %shard_map.77 = (bf16[32,64,128]{2,1,0:T(8,128)(2,1)}, f32[16,128]{1,0:T(8,128)}) custom-call(s32[2]{0:T(128)} %pad_add_fusion.3.ids_ref, bf16[129,16,128]{2,1,0:T(8,128)(2,1)} %copy-done.7, bf16[129,16,128]{2,1,0:T(8,128)(2,1)} %copy-done.8, bf16[2,32,128,128]{3,2,1,0:T(8,128)(2,1)} %refs_9_.7, ...), custom_call_target="tpu_custom_call" | custom-call | flops 8165000192 | tf_op jit(solution)/shard_map/pallas_call | solution.py:443
  155.3 1.8 collective-permute-start.25
  157.2 2.0 collective-permute-done.25
  159.2 1.2 collective-permute-done.26
  160.4 1.3 add_add_fusion.1.refs_1_
  161.7 3.0 %collective-permute-start.30 = (bf16[32,64,128]{2,1,0:T(8,128)(2,1)}, bf16[32,64,128]{2,1,0:T(8,128)(2,1)S(1)}, u32[]{:S(2)}, u32[]{:S(2)}) collective-permute-start(bf16[32,64,128]{2,1,0:T(8,128)(2,1)} %shard_map.79.refs_11_), channel_id=1, source_target_pairs={{0,4},{1,5},{2,0},{3,1},{4,8},{5,9},{6,2},{7,3},{8,12},{9,13},{10,... | collective-permute-start | bytes 1572872 | tf_op jit(solution)/shard_map/ppermute | solution.py:44
  164.7 11.8 %collective-permute-done.30.refs_11_ = bf16[32,64,128]{2,1,0:T(8,128)(2,1)S(1)} collective-permute-done((bf16[32,64,128]{2,1,0:T(8,128)(2,1)}, bf16[32,64,128]{2,1,0:T(8,128)(2,1)S(1)}, u32[]{:S(2)}, u32[]{:S(2)}) %collective-permute-start.30) | collective-permute-done | bytes 524320 | tf_op jit(solution)/shard_map/ppermute | solution.py:44
  176.5 2.4 collective-permute-start.31
  179.0 2.0 collective-permute-start.27
  181.0 0.9 collective-permute-start.28
  181.8 10.2 %collective-permute-done.27 = f32[16,128]{1,0:T(8,128)S(1)} collective-permute-done((f32[16,128]{1,0:T(8,128)S(1)}, f32[16,128]{1,0:T(8,128)S(1)}, u32[]{:S(2)}, u32[]{:S(2)}) %collective-permute-start.27) | collective-permute-done | bytes 8224 | tf_op jit(solution)/shard_map/ppermute | solution.py:118
  192.1 0.9 collective-permute-start.29
  193.6 3.9 %collective-permute-done.29 = f32[16,128]{1,0:T(8,128)S(1)} collective-permute-done((f32[16,128]{1,0:T(8,128)S(1)}, f32[16,128]{1,0:T(8,128)S(1)}, u32[]{:S(2)}, u32[]{:S(2)}) %collective-permute-start.29) | collective-permute-done | bytes 8224 | tf_op jit(solution)/shard_map/ppermute | solution.py:118
  198.1 1.7 shard_map.78
  199.9 0.8 copy-done.20
  200.6 6.2 %shard_map.80 = (f32[33,64,128]{2,1,0:T(8,128)}, f32[8,128]{1,0:T(8,128)}) custom-call(s32[3]{0:T(128)} %pad_add_fusion.5.ids_ref, f32[16,128]{1,0:T(8,128)} %get-tuple-element.35.refs_0_, bf16[129,16,128]{2,1,0:T(8,128)(2,1)} %get-tuple-element.30.refs_0_.refs_1_, bf16[129,16,128]{2,1,0:T(8,128)(2,1)} %copy-done.2, ...), custom_call_target="tpu_custom_call" | custom-call | flops 575000000 | tf_op jit(solution)/shard_map/pallas_call | solution.py:443
  207.6 2.0 collective-permute-start.40
  211.2 12.8 %shard_map.82 = (f32[33,64,128]{2,1,0:T(8,128)}, f32[8,128]{1,0:T(8,128)}) custom-call(s32[6]{0:T(128)} %stack.81.ids_ref, f32[16,128]{1,0:T(8,128)} %get-tuple-element.35.refs_0_, bf16[129,16,128]{2,1,0:T(8,128)(2,1)} %get-tuple-element.30.refs_0_.refs_1_, bf16[129,16,128]{2,1,0:T(8,128)(2,1)} %copy-done.2, ...), custom_call_target="tpu_custom_call" | custom-call | flops 575000000 | tf_op jit(solution)/shard_map/pallas_call | solution.py:443
  224.9 2.1 shard_map.84
  228.6 8.6 %shard_map.85 = (f32[33,64,128]{2,1,0:T(8,128)}, f32[8,128]{1,0:T(8,128)}) custom-call(s32[4]{0:T(128)} %pad_add_fusion.6.ids_ref, f32[16,128]{1,0:T(8,128)} %get-tuple-element.35.refs_0_, bf16[129,16,128]{2,1,0:T(8,128)(2,1)} %get-tuple-element.30.refs_0_.refs_1_, bf16[129,16,128]{2,1,0:T(8,128)(2,1)} %copy-done.2, ...), custom_call_target="tpu_custom_call" | custom-call | flops 575000000 | tf_op jit(solution)/shard_map/pallas_call | solution.py:443
  237.1 0.8 copy-done.23
  239.1 1.2 collective-permute-done.44.refs_12_
  240.2 0.8 copy-done.24
  241.0 5.5 %shard_map.87 = bf16[32,64,128]{2,1,0:T(8,128)(2,1)} custom-call(s32[3]{0:T(128)} %pad_add_fusion.1.ids_ref, f32[16,128]{1,0:T(8,128)} %get-tuple-element.35.refs_0_, bf16[129,16,128]{2,1,0:T(8,128)(2,1)} %get-tuple-element.30.refs_0_.refs_1_, bf16[129,16,128]{2,1,0:T(8,128)(2,1)} %copy-done.2, ...), custom_call_target="tpu_custom_call" | custom-call | flops 575000000 | tf_op jit(solution)/shard_map/pallas_call | solution.py:443
  (133 shorter events, 14.1 us)
Async XLA Ops:
  3.1 9.6 %collective-permute-start.1 = (bf16[2,32,64,128]{3,2,1,0:T(8,128)(2,1)}, bf16[2,32,64,128]{3,2,1,0:T(8,128)(2,1)}, u32[]{:S(2)}, u32[]{:S(2)}) collective-permute-start(bf16[2,32,64,128]{3,2,1,0:T(8,128)(2,1)} %constant_dynamic-slice_fusion.2), channel_id=1, source_target_pairs={{0,1},{1,0},{2,3},{3,2},{4,5},{5,4},{6,7},{7,6},{8,9},{9,8},{10,11... | collective-permute-start | bytes 3145736 | tf_op jit(solution)/shard_map/ppermute | solution.py:44
  3.5 85.7 %collective-permute-start.5 = (bf16[2,32,128,128]{3,2,1,0:T(8,128)(2,1)S(1)}, bf16[2,32,128,128]{3,2,1,0:T(8,128)(2,1)}, u32[]{:S(2)}, u32[]{:S(2)}) collective-permute-start(bf16[2,32,128,128]{3,2,1,0:T(8,128)(2,1)S(1)} %copy-done), channel_id=1, source_target_pairs={{0,1},{1,0},{2,3},{3,2},{4,5},{5,4},{6,7},{7,6},{8,9},{9,8},{10,11... | collective-permute-start | bytes 6291464 | tf_op jit(solution)/shard_map/ppermute | solution.py:44
  5.9 27.7 %collective-permute-start.9 = (bf16[32,64,128]{2,1,0:T(8,128)(2,1)}, bf16[32,64,128]{2,1,0:T(8,128)(2,1)S(1)}, u32[]{:S(2)}, u32[]{:S(2)}) collective-permute-start(bf16[32,64,128]{2,1,0:T(8,128)(2,1)} %get-tuple-element.45.refs_4_.refs_8_.refs_13_.refs_19_.refs_15_), channel_id=1, source_target_pairs={{0,8},{1,9},{2,10},{3,11},{4,12},{5,13},{6,14},{7,15},{8,0},{9,1},... | collective-permute-start | bytes 1572872 | tf_op jit(solution)/shard_map/ppermute | solution.py:44
  9.9 23.7 %collective-permute-start.21 = (bf16[32,64,128]{2,1,0:T(8,128)(2,1)}, bf16[32,64,128]{2,1,0:T(8,128)(2,1)}, u32[]{:S(2)}, u32[]{:S(2)}) collective-permute-start(bf16[32,64,128]{2,1,0:T(8,128)(2,1)} %get-tuple-element.45.refs_4_.refs_8_.refs_13_.refs_19_.refs_15_), channel_id=1, source_target_pairs={{0,2},{1,3},{2,0},{3,1},{4,6},{5,7},{6,4},{7,5},{8,10},{9,11},{10,... | collective-permute-start | bytes 1572872 | tf_op jit(solution)/shard_map/ppermute | solution.py:44
  11.4 1.2 collective-permute-start
  18.7 18.9 %collective-permute-start.10 = (bf16[129,16,128]{2,1,0:T(8,128)(2,1)}, bf16[129,16,128]{2,1,0:T(8,128)(2,1)S(1)}, u32[]{:S(2)}, u32[]{:S(2)}) collective-permute-start(bf16[129,16,128]{2,1,0:T(8,128)(2,1)} %get-tuple-element.26), channel_id=1, source_target_pairs={{0,2},{1,3},{2,0},{3,1},{4,6},{5,7},{6,4},{7,5},{8,10},{9,11},{10,... | collective-permute-start | bytes 1585160 | tf_op jit(solution)/shard_map/ppermute | solution.py:44
  19.2 26.4 %collective-permute-start.6 = (bf16[32,64,128]{2,1,0:T(8,128)(2,1)}, bf16[32,64,128]{2,1,0:T(8,128)(2,1)}, u32[]{:S(2)}, u32[]{:S(2)}) collective-permute-start(bf16[32,64,128]{2,1,0:T(8,128)(2,1)} %get-tuple-element.45.refs_4_.refs_8_.refs_13_.refs_19_.refs_15_), channel_id=1, source_target_pairs={{0,4},{1,5},{2,6},{3,7},{4,0},{5,1},{6,2},{7,3},{8,12},{9,13},{10,... | collective-permute-start | bytes 1572872 | tf_op jit(solution)/shard_map/ppermute | solution.py:44
  33.6 38.9 %collective-permute-start.15 = (bf16[129,16,128]{2,1,0:T(8,128)(2,1)}, bf16[129,16,128]{2,1,0:T(8,128)(2,1)}, u32[]{:S(2)}, u32[]{:S(2)}) collective-permute-start(bf16[129,16,128]{2,1,0:T(8,128)(2,1)} %get-tuple-element.29), channel_id=1, source_target_pairs={{0,8},{1,9},{2,10},{3,11},{4,12},{5,13},{6,14},{7,15},{8,0},{9,1},... | collective-permute-start | bytes 1585160 | tf_op jit(solution)/shard_map/ppermute | solution.py:44
  34.4 48.5 %collective-permute-start.3 = (bf16[129,16,128]{2,1,0:T(8,128)(2,1)}, bf16[129,16,128]{2,1,0:T(8,128)(2,1)S(1)}, u32[]{:S(2)}, u32[]{:S(2)}) collective-permute-start(bf16[129,16,128]{2,1,0:T(8,128)(2,1)} %get-tuple-element.25), channel_id=1, source_target_pairs={{0,10},{1,11},{2,8},{3,9},{4,14},{5,15},{6,12},{7,13},{8,2},{9,3},... | collective-permute-start | bytes 1585160 | tf_op jit(solution)/shard_map/ppermute | solution.py:44
  37.5 46.7 %collective-permute-start.12 = (bf16[129,16,128]{2,1,0:T(8,128)(2,1)}, bf16[129,16,128]{2,1,0:T(8,128)(2,1)}, u32[]{:S(2)}, u32[]{:S(2)}) collective-permute-start(bf16[129,16,128]{2,1,0:T(8,128)(2,1)} %get-tuple-element.27), channel_id=1, source_target_pairs={{0,4},{1,5},{2,6},{3,7},{4,0},{5,1},{6,2},{7,3},{8,12},{9,13},{10,... | collective-permute-start | bytes 1585160 | tf_op jit(solution)/shard_map/ppermute | solution.py:44
  45.7 42.8 %collective-permute-start.11 = (bf16[32,64,128]{2,1,0:T(8,128)(2,1)}, bf16[32,64,128]{2,1,0:T(8,128)(2,1)S(1)}, u32[]{:S(2)}, u32[]{:S(2)}) collective-permute-start(bf16[32,64,128]{2,1,0:T(8,128)(2,1)} %shard_map.71.refs_6_.refs_21_.refs_27_.refs_23_), channel_id=1, source_target_pairs={{0,4},{1,5},{2,6},{3,7},{4,0},{5,1},{6,2},{7,3},{8,12},{9,13},{10,... | collective-permute-start | bytes 1572872 | tf_op jit(solution)/shard_map/ppermute | solution.py:44
  72.5 18.3 %collective-permute-start.23 = (bf16[32,64,128]{2,1,0:T(8,128)(2,1)}, bf16[32,64,128]{2,1,0:T(8,128)(2,1)}, u32[]{:S(2)}, u32[]{:S(2)}) collective-permute-start(bf16[32,64,128]{2,1,0:T(8,128)(2,1)} %shard_map.71.refs_6_.refs_21_.refs_27_.refs_23_), channel_id=1, source_target_pairs={{0,1},{1,0},{2,3},{3,2},{4,5},{5,4},{6,7},{7,6},{8,9},{9,8},{10,11... | collective-permute-start | bytes 1572872 | tf_op jit(solution)/shard_map/ppermute | solution.py:44
  82.9 15.2 %collective-permute-start.19 = (bf16[32,64,128]{2,1,0:T(8,128)(2,1)}, bf16[32,64,128]{2,1,0:T(8,128)(2,1)}, u32[]{:S(2)}, u32[]{:S(2)}) collective-permute-start(bf16[32,64,128]{2,1,0:T(8,128)(2,1)} %shard_map.71.refs_6_.refs_21_.refs_27_.refs_23_), channel_id=1, source_target_pairs={{0,2},{1,3},{2,0},{3,1},{4,6},{5,7},{6,4},{7,5},{8,10},{9,11},{10,... | collective-permute-start | bytes 1572872 | tf_op jit(solution)/shard_map/ppermute | solution.py:44
  84.3 21.6 %collective-permute-start.22 = (bf16[32,64,128]{2,1,0:T(8,128)(2,1)}, bf16[32,64,128]{2,1,0:T(8,128)(2,1)S(1)}, u32[]{:S(2)}, u32[]{:S(2)}) collective-permute-start(bf16[32,64,128]{2,1,0:T(8,128)(2,1)} %collective-permute-done.21.refs_6_.refs_15_.refs_21_.refs_17_), channel_id=1, source_target_pairs={{0,1},{1,0},{2,3},{3,2},{4,5},{5,4},{6,7},{7,6},{8,9},{9,8},{10,11... | collective-permute-start | bytes 1572872 | tf_op jit(solution)/shard_map/ppermute | solution.py:44
  88.4 26.5 %collective-permute-start.17 = (bf16[32,64,128]{2,1,0:T(8,128)(2,1)}, bf16[32,64,128]{2,1,0:T(8,128)(2,1)}, u32[]{:S(2)}, u32[]{:S(2)}) collective-permute-start(bf16[32,64,128]{2,1,0:T(8,128)(2,1)} %shard_map.70.refs_4_.refs_17_.refs_23_.refs_19_), channel_id=1, source_target_pairs={{0,1},{1,0},{2,3},{3,2},{4,5},{5,4},{6,7},{7,6},{8,9},{9,8},{10,11... | collective-permute-start | bytes 1572872 | tf_op jit(solution)/shard_map/ppermute | solution.py:44
  89.3 25.8 %collective-permute-start.7 = (bf16[32,64,128]{2,1,0:T(8,128)(2,1)}, bf16[32,64,128]{2,1,0:T(8,128)(2,1)S(1)}, u32[]{:S(2)}, u32[]{:S(2)}) collective-permute-start(bf16[32,64,128]{2,1,0:T(8,128)(2,1)} %shard_map.70.refs_4_.refs_17_.refs_23_.refs_19_), channel_id=1, source_target_pairs={{0,2},{1,3},{2,0},{3,1},{4,6},{5,7},{6,4},{7,5},{8,10},{9,11},{10,... | collective-permute-start | bytes 1572872 | tf_op jit(solution)/shard_map/ppermute | solution.py:44
  90.8 25.8 %collective-permute-start.16 = (bf16[129,16,128]{2,1,0:T(8,128)(2,1)}, bf16[129,16,128]{2,1,0:T(8,128)(2,1)S(1)}, u32[]{:S(2)}, u32[]{:S(2)}) collective-permute-start(bf16[129,16,128]{2,1,0:T(8,128)(2,1)} %shard_map.73), channel_id=1, source_target_pairs={{0,12},{1,13},{2,14},{3,15},{4,8},{5,9},{6,10},{7,11},{8,4},{9,5},... | collective-permute-start | bytes 1585160 | tf_op jit(solution)/shard_map/ppermute | solution.py:44
  98.1 8.4 %collective-permute-start.20 = (bf16[32,64,128]{2,1,0:T(8,128)(2,1)}, bf16[32,64,128]{2,1,0:T(8,128)(2,1)S(1)}, u32[]{:S(2)}, u32[]{:S(2)}) collective-permute-start(bf16[32,64,128]{2,1,0:T(8,128)(2,1)} %collective-permute-done.19.refs_4_.refs_23_.refs_29_.refs_25_), channel_id=1, source_target_pairs={{0,1},{1,0},{2,3},{3,2},{4,5},{5,4},{6,7},{7,6},{8,9},{9,8},{10,11... | collective-permute-start | bytes 1572872 | tf_op jit(solution)/shard_map/ppermute | solution.py:44
  105.9 26.0 %collective-permute-start.18 = (bf16[32,64,128]{2,1,0:T(8,128)(2,1)S(1)}, bf16[32,64,128]{2,1,0:T(8,128)(2,1)}, u32[]{:S(2)}, u32[]{:S(2)}) collective-permute-start(bf16[32,64,128]{2,1,0:T(8,128)(2,1)S(1)} %copy-done.5), channel_id=1, source_target_pairs={{0,1},{1,0},{2,3},{3,2},{4,5},{5,4},{6,7},{7,6},{8,9},{9,8},{10,11... | collective-permute-start | bytes 1572872 | tf_op jit(solution)/shard_map/ppermute | solution.py:44
  106.5 25.4 %collective-permute-start.13 = (bf16[32,64,128]{2,1,0:T(8,128)(2,1)S(1)}, bf16[32,64,128]{2,1,0:T(8,128)(2,1)}, u32[]{:S(2)}, u32[]{:S(2)}) collective-permute-start(bf16[32,64,128]{2,1,0:T(8,128)(2,1)S(1)} %copy-done.5), channel_id=1, source_target_pairs={{0,2},{1,3},{2,0},{3,1},{4,6},{5,7},{6,4},{7,5},{8,10},{9,11},{10,... | collective-permute-start | bytes 1572872 | tf_op jit(solution)/shard_map/ppermute | solution.py:44
  115.0 24.3 %collective-permute-start.2 = (bf16[129,16,128]{2,1,0:T(8,128)(2,1)}, bf16[129,16,128]{2,1,0:T(8,128)(2,1)S(1)}, u32[]{:S(2)}, u32[]{:S(2)}) collective-permute-start(bf16[129,16,128]{2,1,0:T(8,128)(2,1)} %get-tuple-element.23), channel_id=1, source_target_pairs={{0,6},{1,7},{2,4},{3,5},{4,2},{5,3},{6,0},{7,1},{8,14},{9,15},{10,... | collective-permute-start | bytes 1585160 | tf_op jit(solution)/shard_map/ppermute | solution.py:44
  115.0 24.2 %copy-start.10 = (bf16[32,64,128]{2,1,0:T(8,128)(2,1)}, bf16[32,64,128]{2,1,0:T(8,128)(2,1)S(1)}, u32[]{:S(2)}) copy-start(bf16[32,64,128]{2,1,0:T(8,128)(2,1)S(1)} %collective-permute-done.7.refs_4_.refs_19_.refs_25_.refs_21_) | copy-start | bytes 1572868
  115.1 31.9 %collective-permute-start.4 = (bf16[129,16,128]{2,1,0:T(8,128)(2,1)}, bf16[129,16,128]{2,1,0:T(8,128)(2,1)S(1)}, u32[]{:S(2)}, u32[]{:S(2)}) collective-permute-start(bf16[129,16,128]{2,1,0:T(8,128)(2,1)} %shard_map.69), channel_id=1, source_target_pairs={{0,14},{1,15},{2,12},{3,13},{4,10},{5,11},{6,8},{7,9},{8,6},{9,7},... | collective-permute-start | bytes 1585160 | tf_op jit(solution)/shard_map/ppermute | solution.py:44
  116.7 30.3 %collective-permute-start.8 = (bf16[32,64,128]{2,1,0:T(8,128)(2,1)S(1)}, bf16[32,64,128]{2,1,0:T(8,128)(2,1)S(1)}, u32[]{:S(2)}, u32[]{:S(2)}) collective-permute-start(bf16[32,64,128]{2,1,0:T(8,128)(2,1)S(1)} %collective-permute-done.7.refs_4_.refs_19_.refs_25_.refs_21_), channel_id=1, source_target_pairs={{0,1},{1,0},{2,3},{3,2},{4,5},{5,4},{6,7},{7,6},{8,9},{9,8},{10,11... | collective-permute-start | bytes 1572872 | tf_op jit(solution)/shard_map/ppermute | solution.py:44
  131.9 15.1 %collective-permute-start.14 = (bf16[32,64,128]{2,1,0:T(8,128)(2,1)}, bf16[32,64,128]{2,1,0:T(8,128)(2,1)}, u32[]{:S(2)}, u32[]{:S(2)}) collective-permute-start(bf16[32,64,128]{2,1,0:T(8,128)(2,1)} %collective-permute-done.13.refs_6_.refs_27_.refs_33_.refs_29_), channel_id=1, source_target_pairs={{0,1},{1,0},{2,3},{3,2},{4,5},{5,4},{6,7},{7,6},{8,9},{9,8},{10,11... | collective-permute-start | bytes 1572872 | tf_op jit(solution)/shard_map/ppermute | solution.py:44
  155.2 2.0 collective-permute-start.24
  155.3 3.9 %collective-permute-start.25 = (f32[16,128]{1,0:T(8,128)}, f32[16,128]{1,0:T(8,128)S(1)}, u32[]{:S(2)}, u32[]{:S(2)}) collective-permute-start(f32[16,128]{1,0:T(8,128)} %get-tuple-element.34), channel_id=1, source_target_pairs={{0,2},{1,3},{2,0},{3,1},{4,6},{5,7},{6,4},{7,5},{8,10},{9,11},{10,... | collective-permute-start | bytes 24584 | tf_op jit(solution)/shard_map/ppermute | solution.py:118
  157.2 3.3 %collective-permute-start.26 = (f32[16,128]{1,0:T(8,128)}, f32[16,128]{1,0:T(8,128)S(1)}, u32[]{:S(2)}, u32[]{:S(2)}) collective-permute-start(f32[16,128]{1,0:T(8,128)} %get-tuple-element.34), channel_id=1, source_target_pairs={{0,3},{1,2},{2,1},{3,0},{4,7},{5,6},{6,5},{7,4},{8,11},{9,10},{10,... | collective-permute-start | bytes 24584 | tf_op jit(solution)/shard_map/ppermute | solution.py:118
  161.7 14.8 %collective-permute-start.30 = (bf16[32,64,128]{2,1,0:T(8,128)(2,1)}, bf16[32,64,128]{2,1,0:T(8,128)(2,1)S(1)}, u32[]{:S(2)}, u32[]{:S(2)}) collective-permute-start(bf16[32,64,128]{2,1,0:T(8,128)(2,1)} %shard_map.79.refs_11_), channel_id=1, source_target_pairs={{0,4},{1,5},{2,0},{3,1},{4,8},{5,9},{6,2},{7,3},{8,12},{9,13},{10,... | collective-permute-start | bytes 1572872 | tf_op jit(solution)/shard_map/ppermute | solution.py:44
  164.7 14.2 %collective-permute-start.35 = (bf16[32,64,128]{2,1,0:T(8,128)(2,1)}, bf16[32,64,128]{2,1,0:T(8,128)(2,1)S(1)}, u32[]{:S(2)}, u32[]{:S(2)}) collective-permute-start(bf16[32,64,128]{2,1,0:T(8,128)(2,1)} %shard_map.79.refs_11_), channel_id=1, source_target_pairs={{0,2},{1,3},{2,6},{3,7},{4,0},{5,1},{6,10},{7,11},{8,4},{9,5},{10,... | collective-permute-start | bytes 1572872 | tf_op jit(solution)/shard_map/ppermute | solution.py:44
  164.7 35.1 %collective-permute-start.32 = (bf16[32,64,128]{2,1,0:T(8,128)(2,1)}, bf16[32,64,128]{2,1,0:T(8,128)(2,1)S(1)}, u32[]{:S(2)}, u32[]{:S(2)}) collective-permute-start(bf16[32,64,128]{2,1,0:T(8,128)(2,1)} %shard_map.79.refs_11_), channel_id=1, source_target_pairs={{0,1},{1,0},{2,3},{3,2},{4,5},{5,4},{6,7},{7,6},{8,9},{9,8},{10,11... | collective-permute-start | bytes 1572872 | tf_op jit(solution)/shard_map/ppermute | solution.py:44
  176.5 23.3 %copy-start.13 = (bf16[32,64,128]{2,1,0:T(8,128)(2,1)}, bf16[32,64,128]{2,1,0:T(8,128)(2,1)S(1)}, u32[]{:S(2)}) copy-start(bf16[32,64,128]{2,1,0:T(8,128)(2,1)S(1)} %collective-permute-done.30.refs_11_) | copy-start | bytes 1572868
  176.5 30.3 %collective-permute-start.31 = (bf16[32,64,128]{2,1,0:T(8,128)(2,1)S(1)}, bf16[32,64,128]{2,1,0:T(8,128)(2,1)}, u32[]{:S(2)}, u32[]{:S(2)}) collective-permute-start(bf16[32,64,128]{2,1,0:T(8,128)(2,1)S(1)} %collective-permute-done.30.refs_11_), channel_id=1, source_target_pairs={{0,4},{1,5},{2,0},{3,1},{4,8},{5,9},{6,2},{7,3},{8,12},{9,13},{10,... | collective-permute-start | bytes 1572872 | tf_op jit(solution)/shard_map/ppermute | solution.py:44
  178.9 20.9 %copy-start.14 = (bf16[32,64,128]{2,1,0:T(8,128)(2,1)}, bf16[32,64,128]{2,1,0:T(8,128)(2,1)S(1)}, u32[]{:S(2)}) copy-start(bf16[32,64,128]{2,1,0:T(8,128)(2,1)S(1)} %collective-permute-done.35.refs_13_) | copy-start | bytes 1572868
  178.9 28.6 %collective-permute-start.38 = (bf16[32,64,128]{2,1,0:T(8,128)(2,1)S(1)}, bf16[32,64,128]{2,1,0:T(8,128)(2,1)S(1)}, u32[]{:S(2)}, u32[]{:S(2)}) collective-permute-start(bf16[32,64,128]{2,1,0:T(8,128)(2,1)S(1)} %collective-permute-done.35.refs_13_), channel_id=1, source_target_pairs={{0,2},{1,3},{2,6},{3,7},{4,0},{5,1},{6,10},{7,11},{8,4},{9,5},{10,... | collective-permute-start | bytes 1572872 | tf_op jit(solution)/shard_map/ppermute | solution.py:44
  179.0 13.1 %collective-permute-start.27 = (f32[16,128]{1,0:T(8,128)S(1)}, f32[16,128]{1,0:T(8,128)S(1)}, u32[]{:S(2)}, u32[]{:S(2)}) collective-permute-start(f32[16,128]{1,0:T(8,128)S(1)} %copy-done.25), channel_id=1, source_target_pairs={{0,4},{1,5},{2,6},{3,7},{4,0},{5,1},{6,2},{7,3},{8,12},{9,13},{10,... | collective-permute-start | bytes 24584 | tf_op jit(solution)/shard_map/ppermute | solution.py:118
  181.0 12.1 %collective-permute-start.28 = (f32[16,128]{1,0:T(8,128)S(1)}, f32[16,128]{1,0:T(8,128)S(1)}, u32[]{:S(2)}, u32[]{:S(2)}) collective-permute-start(f32[16,128]{1,0:T(8,128)S(1)} %copy-done.25), channel_id=1, source_target_pairs={{0,8},{1,9},{2,10},{3,11},{4,12},{5,13},{6,14},{7,15},{8,0},{9,1},... | collective-permute-start | bytes 24584 | tf_op jit(solution)/shard_map/ppermute | solution.py:118
  192.1 5.4 %collective-permute-start.29 = (f32[16,128]{1,0:T(8,128)S(1)}, f32[16,128]{1,0:T(8,128)S(1)}, u32[]{:S(2)}, u32[]{:S(2)}) collective-permute-start(f32[16,128]{1,0:T(8,128)S(1)} %copy-done.25), channel_id=1, source_target_pairs={{0,12},{1,13},{2,14},{3,15},{4,8},{5,9},{6,10},{7,11},{8,4},{9,5},... | collective-permute-start | bytes 24584 | tf_op jit(solution)/shard_map/ppermute | solution.py:118
  193.0 14.6 %collective-permute-start.34 = (bf16[32,64,128]{2,1,0:T(8,128)(2,1)S(1)}, bf16[32,64,128]{2,1,0:T(8,128)(2,1)S(1)}, u32[]{:S(2)}, u32[]{:S(2)}) collective-permute-start(bf16[32,64,128]{2,1,0:T(8,128)(2,1)S(1)} %collective-permute-done.30.refs_11_), channel_id=1, source_target_pairs={{0,1},{1,0},{2,3},{3,2},{4,5},{5,4},{6,7},{7,6},{8,9},{9,8},{10,11... | collective-permute-start | bytes 1572872 | tf_op jit(solution)/shard_map/ppermute | solution.py:44
  199.8 10.4 %collective-permute-start.36 = (bf16[32,64,128]{2,1,0:T(8,128)(2,1)S(1)}, bf16[32,64,128]{2,1,0:T(8,128)(2,1)S(1)}, u32[]{:S(2)}, u32[]{:S(2)}) collective-permute-start(bf16[32,64,128]{2,1,0:T(8,128)(2,1)S(1)} %collective-permute-done.35.refs_13_), channel_id=1, source_target_pairs={{0,1},{1,0},{2,3},{3,2},{4,5},{5,4},{6,7},{7,6},{8,9},{9,8},{10,11... | collective-permute-start | bytes 1572872 | tf_op jit(solution)/shard_map/ppermute | solution.py:44
  206.9 3.3 %collective-permute-start.37 = (bf16[32,64,128]{2,1,0:T(8,128)(2,1)}, bf16[32,64,128]{2,1,0:T(8,128)(2,1)S(1)}, u32[]{:S(2)}, u32[]{:S(2)}) collective-permute-start(bf16[32,64,128]{2,1,0:T(8,128)(2,1)} %shard_map.81.refs_15_), channel_id=1, source_target_pairs={{0,1},{1,0},{2,3},{3,2},{4,5},{5,4},{6,7},{7,6},{8,9},{9,8},{10,11... | collective-permute-start | bytes 1572872 | tf_op jit(solution)/shard_map/ppermute | solution.py:44
  207.5 2.7 %collective-permute-start.39 = (bf16[32,64,128]{2,1,0:T(8,128)(2,1)S(1)}, bf16[32,64,128]{2,1,0:T(8,128)(2,1)}, u32[]{:S(2)}, u32[]{:S(2)}) collective-permute-start(bf16[32,64,128]{2,1,0:T(8,128)(2,1)S(1)} %collective-permute-done.38.refs_17_), channel_id=1, source_target_pairs={{0,1},{1,0},{2,3},{3,2},{4,5},{5,4},{6,7},{7,6},{8,9},{9,8},{10,11... | collective-permute-start | bytes 1572872 | tf_op jit(solution)/shard_map/ppermute | solution.py:44
  207.6 16.4 %collective-permute-start.33 = (bf16[32,64,128]{2,1,0:T(8,128)(2,1)}, bf16[32,64,128]{2,1,0:T(8,128)(2,1)}, u32[]{:S(2)}, u32[]{:S(2)}) collective-permute-start(bf16[32,64,128]{2,1,0:T(8,128)(2,1)} %shard_map.81.refs_15_), channel_id=1, source_target_pairs={{0,4},{1,5},{2,0},{3,1},{4,8},{5,9},{6,2},{7,3},{8,12},{9,13},{10,... | collective-permute-start | bytes 1572872 | tf_op jit(solution)/shard_map/ppermute | solution.py:44
  207.6 16.5 %collective-permute-start.40 = (bf16[32,64,128]{2,1,0:T(8,128)(2,1)S(1)}, bf16[32,64,128]{2,1,0:T(8,128)(2,1)S(1)}, u32[]{:S(2)}, u32[]{:S(2)}) collective-permute-start(bf16[32,64,128]{2,1,0:T(8,128)(2,1)S(1)} %collective-permute-done.38.refs_17_), channel_id=1, source_target_pairs={{0,2},{1,3},{2,6},{3,7},{4,0},{5,1},{6,10},{7,11},{8,4},{9,5},{10,... | collective-permute-start | bytes 1572872 | tf_op jit(solution)/shard_map/ppermute | solution.py:44
  224.0 3.6 %collective-permute-start.42 = (bf16[32,64,128]{2,1,0:T(8,128)(2,1)}, bf16[32,64,128]{2,1,0:T(8,128)(2,1)S(1)}, u32[]{:S(2)}, u32[]{:S(2)}) collective-permute-start(bf16[32,64,128]{2,1,0:T(8,128)(2,1)} %shard_map.83.lower_ref.refs_11_), channel_id=1, source_target_pairs={{0,1},{1,0},{2,3},{3,2},{4,5},{5,4},{6,7},{7,6},{8,9},{9,8},{10,11... | collective-permute-start | bytes 1572872 | tf_op jit(solution)/shard_map/ppermute | solution.py:44
  224.1 3.5 %collective-permute-start.43 = (bf16[32,64,128]{2,1,0:T(8,128)(2,1)S(1)}, bf16[32,64,128]{2,1,0:T(8,128)(2,1)S(1)}, u32[]{:S(2)}, u32[]{:S(2)}) collective-permute-start(bf16[32,64,128]{2,1,0:T(8,128)(2,1)S(1)} %collective-permute-done.40.upper_ref.refs_13_), channel_id=1, source_target_pairs={{0,1},{1,0},{2,3},{3,2},{4,5},{5,4},{6,7},{7,6},{8,9},{9,8},{10,11... | collective-permute-start | bytes 1572872 | tf_op jit(solution)/shard_map/ppermute | solution.py:44
  227.0 10.1 %collective-permute-start.41 = (bf16[32,64,128]{2,1,0:T(8,128)(2,1)}, bf16[32,64,128]{2,1,0:T(8,128)(2,1)S(1)}, u32[]{:S(2)}, u32[]{:S(2)}) collective-permute-start(bf16[32,64,128]{2,1,0:T(8,128)(2,1)} %shard_map.84), channel_id=1, source_target_pairs={{0,4},{1,3},{2,0},{3,7},{4,8},{5,1},{6,2},{7,11},{8,12},{9,5},{10,... | collective-permute-start | bytes 1572872 | tf_op jit(solution)/shard_map/ppermute | solution.py:44
  237.9 2.3 collective-permute-start.44
  (27 other events, 90.0 us)

commit v15 on v9

--- a/solution.py
+++ b/solution.py
@@ -215,11 +215,8 @@
         moved.append(product.astype(jnp.bfloat16))
         where.append(labels[1, at])
     for slot in range(terms * capacity):
-        target = where[slot]
-        total[target] += jnp.dot(
-            moved[slot],
-            right[slot // capacity, jnp.minimum(target, blocks - 1)],
-            preferred_element_type=jnp.float32,
+        total[where[slot]] += jnp.dot(
+            moved[slot], right[slot], preferred_element_type=jnp.float32
         )
 
 
@@ -263,7 +260,7 @@
     (last_out,) = take(1)
     total, left, right, vector, raw, spread_labels, labels = take(7)
     left_sems, right_sems, vector_sems, raw_sems, label_sem, total_sem = take(6)
-    (wave, wave_sem) = take(2) if end == "stats" else (None, None)
+    wave, wave_sem = take(2) if end == "stats" else (None, None)
     half = ids_ref[0]
     blocks = vector.shape[2]
     parts = left.shape[1]
@@ -286,8 +283,18 @@
             for part in range(2)
         ]
 
-    def right_copy(side):
-        return pltpu.make_async_copy(rights[side], right.at[side], right_sems.at[side])
+    def load_right(source, side):
+        for slot in range(terms * capacity):
+            target = jnp.minimum(labels[source, 1, side * terms * capacity + slot], blocks - 1)
+            pltpu.make_async_copy(
+                rights[side].at[slot // capacity, target],
+                right.at[source, side, slot],
+                right_sems.at[source, side],
+            ).start()
+
+    def wait_right(source, side):
+        whole = right.at[source, side]
+        pltpu.make_async_copy(whole, whole, right_sems.at[source, side]).wait()
 
     for source in range(sources):
         if choices:
@@ -301,12 +308,9 @@
         else:
             for copy in left_copies(source, lefts[source]):
                 copy.start()
-    for copy in [*vector_copies(0), right_copy(0)]:
-        copy.start()
-    for source in range(1, sources):
+    for source in range(sources):
         for copy in vector_copies(source):
             copy.start()
-    right_copy(1).start()
     if first:
         total[...] = jnp.zeros_like(total)
     else:
@@ -324,20 +328,23 @@
     move_labels = pltpu.make_async_copy(spread_labels, labels, label_sem)
     move_labels.start()
     move_labels.wait()
+    for source in range(sources):
+        for side in range(2):
+            load_right(source, side)
     if not first:
         load_total.wait()
-    for side in range(2):
-        right_copy(side).wait()
-        for source in range(sources):
+    for source in range(sources):
+        for side in range(2):
             if side == 0:
                 left_copies(source, lefts[0])[1].wait()
                 for copy in vector_copies(source):
                     copy.wait()
+            wait_right(source, side)
             add_products(
                 left.at[source],
                 labels.at[source],
                 vector.at[source],
-                right.at[side],
+                right.at[source, side],
                 total,
                 side,
                 terms,
@@ -345,12 +352,13 @@
             )
     if end == "result":
         last_out[...] = total[:blocks].astype(last_out.dtype)
+    elif end == "stats":
+        load_wave.wait()
+        local_stats(total, wave, ids_ref[1], last_out)
+        total_out[...] = total[:blocks]
     else:
         store_total = pltpu.make_async_copy(total, total_out, total_sem)
         store_total.start()
-        if end == "stats":
-            load_wave.wait()
-            local_stats(total, wave, ids_ref[1], last_out)
         store_total.wait()
 
 
@@ -369,13 +377,13 @@
     scratch = [
         pltpu.VMEM(total_shape, jnp.float32),
         pltpu.VMEM((sources, parts, PART, width), jnp.bfloat16),
-        pltpu.VMEM((2,) + rights[0].shape, jnp.bfloat16),
+        pltpu.VMEM((sources, 2, terms * capacity, width, width), jnp.bfloat16),
         pltpu.VMEM((sources, 2, blocks, rows, width), jnp.bfloat16),
         pltpu.VMEM((sources, PART, width), jnp.bfloat16),
         pltpu.VMEM((sources, 8, width), jnp.int32),
         pltpu.SMEM((sources, 8, width), jnp.int32),
         pltpu.SemaphoreType.DMA((sources,)),
-        pltpu.SemaphoreType.DMA((2,)),
+        pltpu.SemaphoreType.DMA((sources, 2)),
         pltpu.SemaphoreType.DMA((sources, 2)),
         pltpu.SemaphoreType.DMA((sources,)),
         pltpu.SemaphoreType.DMA,
@@ -388,8 +396,11 @@
     out_shape, out_specs = {
         "go on": ((total_out, jax.ShapeDtypeStruct((8, width), jnp.float32)), (anywhere, whole)),
         "stats": (
-            (total_out, jax.ShapeDtypeStruct((devices, 128), jnp.float32)),
-            (anywhere, whole),
+            (
+                jax.ShapeDtypeStruct((blocks, rows, width), jnp.float32),
+                jax.ShapeDtypeStruct((devices, 128), jnp.float32),
+            ),
+            (whole, whole),
         ),
         "result": (jax.ShapeDtypeStruct((blocks, rows, width), jnp.bfloat16), whole),
     }[end]
@@ -401,7 +412,7 @@
         out_specs=out_specs,
         scratch_shapes=scratch,
         compiler_params=pltpu.CompilerParams(vmem_limit_bytes=VMEM_LIMIT),
-        cost_estimate=busy(2.0 + 1.4 * sources),
+        cost_estimate=busy(3.5 + 1.8 * sources),
     )(ids, *arrays)
 
 
@@ -431,7 +442,7 @@
         ),
         in_specs=[whole] * 3,
         out_specs=(whole, whole),
-        compiler_params=pltpu.CompilerParams(vmem_limit_bytes=VMEM_LIMIT),
+        compiler_params=pltpu.CompilerParams(vmem_limit_bytes=8 * 2**20),
         cost_estimate=busy(2.0),
     )(total, wave, stats)
 
@@ -492,25 +503,24 @@
     direction, rayleigh = new_direction(total, own_rows, stats, entries)
     reach = (owners - 1) // 2
 
-    def add_group(total, units, last):
+    def add_group(total, units, end):
         choices = [me ^ ring_owner(place - s, owners) for s in units]
         vectors = [(unit, swap(unit, owners, halves)) for unit in units.values()]
         ids = jnp.stack(here + choices).astype(jnp.int32)
-        return apply_group(ids, lefts, rights, vectors, total, "result" if last else "go on")
-
+        return apply_group(ids, lefts, rights, vectors, total, end)
+
+    total, waiting = None, {0: direction}
     ahead = behind = direction
-    units = {0: direction}
-    total = None
     for step in range(1, reach + 1):
-        ahead_next = ring_send(ahead, owners, halves, (1,) * halves)
-        behind_next = ring_send(behind, owners, halves, (-1,) * halves)
-        total, token = add_group(total, units, False)
-        ahead, behind = after(ahead_next, token), behind_next
-        units = {step: ahead, -step: behind}
-    last = select_half(half, ahead, behind)
-    last = ring_send(last, owners, halves, (1, -1))
-    total, token = add_group(total, units, False)
-    total = add_group(total, {owners // 2: after(last, token)}, True)
+        ahead = ring_send(ahead, owners, halves, (1,) * halves)
+        behind = ring_send(behind, owners, halves, (-1,) * halves)
+        if step > 1:
+            total, token = add_group(total, waiting, "go on")
+            ahead, waiting = after(ahead, token), {}
+        waiting.update({step: ahead, -step: behind})
+    last = ring_send(select_half(half, ahead, behind), owners, halves, (1, -1))
+    total, token = add_group(total, waiting, "go on")
+    total = add_group(total, {owners // 2: after(last, token)}, "result")
     return (total, rayleigh[0])
 
 
@@ -628,8 +638,9 @@
 
 
 def per_device(wavefunction, *operands):
-    gathered_bytes = lax.axis_size("sec") * wavefunction.size * wavefunction.dtype.itemsize
-    if 2 * gathered_bytes > RING_BYTES:
+    owners = lax.axis_size("sec")
+    gathered_bytes = owners * wavefunction.size * wavefunction.dtype.itemsize
+    if owners < 8 or owners & (owners - 1) or 2 * gathered_bytes > RING_BYTES:
         return per_device_streamed(wavefunction, *operands)
     return per_device_ring(wavefunction, *operands)
 

time: 260 us -> 237 us (0.912)
  waiting for transfers between devices: 129 us -> 115 us
  Pallas kernels: 72.1 us -> 64.4 us
    ppermute x39, waiting for transfers between devices: 123 us -> 109 us  [permute(): return lax.ppermute(value, BOTH, pairs)]
    pallas_call x9 -> x8, Pallas kernels: 61.7 us -> 55.8 us  [apply_group(): pl.pallas_call(functools.partial(apply_kernel, sources, choices, first, e...]
    unnamed x74 -> x78, local copies, waits for them, and re-layouts: 10.6 us -> 10.7 us
  transfers between devices with their start and end apart: 45 -> 45, of which waited for: 17 -> 20; matrix products, arithmetic and copies ran while one was open for 2% -> 2% of each run, Pallas kernels for 22% -> 22%
where the time goes in v15:
time: 237 us; the launch traced here: 236 us
  waiting for transfers between devices  115 us (49%)
  Pallas kernels  64.4 us (27%)
  starting transfers between devices  37.5 us (16%)
  local copies, waits for them, and re-layouts  13.6 us (6%)
  other arithmetic  3.88 us (2%)
    ppermute x39, waiting for transfers between devices, permute(): return lax.ppermute(value, BOTH, pairs)  109 us
    pallas_call x8, Pallas kernels, apply_group(): pl.pallas_call(functools.partial(apply_kernel, sources, choices, first, e...  55.8 us
    ppermute x39, starting transfers between devices, permute(): return lax.ppermute(value, BOTH, pairs)  29.9 us
    unnamed x78, local copies, waits for them, and re-layouts  10.7 us
    ppermute x6, starting transfers between devices, spread(): lax.ppermute(value, BOTH, [(d, d ^ m) for d in range(devices)])  7.62 us
    ppermute x6, waiting for transfers between devices, spread(): lax.ppermute(value, BOTH, [(d, d ^ m) for d in range(devices)])  6.3 us
    pallas_call x1, Pallas kernels, pack(): pl.pallas_call(functools.partial(pack_kernel, order, capacity, blocks, te...  5.44 us
  transfers between devices with their start and end apart: 45, of which 20 were waited for; matrix products, arithmetic and copies ran while one was open for 2% of the time, Pallas kernels for 22%

profile of v15, /device:TPU:0, one launch (start us, length us, event | category | flops | bytes accessed | tf_op | source)
XLA Modules:
  0.0 235.8 jit_solution(13498819095174336977)
XLA Ops:
  0.6 1.4 constant_dynamic-slice_fusion.2
  3.5 4.0 %collective-permute-start.13 = (bf16[32,64,128]{2,1,0:T(8,128)(2,1)S(1)}, bf16[32,64,128]{2,1,0:T(8,128)(2,1)S(1)}, u32[]{:S(2)}, u32[]{:S(2)}) collective-permute-start(bf16[32,64,128]{2,1,0:T(8,128)(2,1)S(1)} %get-tuple-element.45.refs_4_.refs_8_.wave_ref), channel_id=1, source_target_pairs={{0,8},{1,9},{2,10},{3,11},{4,12},{5,13},{6,14},{7,15},{8,0},{9,1},... | collective-permute-start | bytes 1572872 | tf_op jit(solution)/shard_map/ppermute | solution.py:44
  7.6 1.5 collective-permute-start.21
  10.9 5.4 %shard_map.68 = (bf16[129,16,128]{2,1,0:T(8,128)(2,1)}, bf16[129,16,128]{2,1,0:T(8,128)(2,1)}, bf16[129,16,128]{2,1,0:T(8,128)(2,1)}, bf16[129,16,128]{2,1,0:T(8...) custom-call(s32[2]{0:T(128)} %pad_add_fusion.2.ids_ref, ...), custom_call_target="tpu_custom_call" | custom-call | flops 5750000128 | tf_op jit(solution)/shard_map/pallas_call | solution.py:184
  16.9 1.6 collective-permute-start.10
  18.5 12.6 %collective-permute-done.13.refs_0_ = bf16[32,64,128]{2,1,0:T(8,128)(2,1)S(1)} collective-permute-done((bf16[32,64,128]{2,1,0:T(8,128)(2,1)S(1)}, bf16[32,64,128]{2,1,0:T(8,128)(2,1)S(1)}, u32[]{:S(2)}, u32[]{:S(2)}) %collective-permute-start.13) | collective-permute-done | bytes 524320 | tf_op jit(solution)/shard_map/ppermute | solution.py:44
  31.9 3.9 %collective-permute-start.6 = (bf16[129,16,128]{2,1,0:T(8,128)(2,1)}, bf16[129,16,128]{2,1,0:T(8,128)(2,1)S(1)}, u32[]{:S(2)}, u32[]{:S(2)}) collective-permute-start(bf16[129,16,128]{2,1,0:T(8,128)(2,1)} %get-tuple-element.28), channel_id=1, source_target_pairs={{0,10},{1,11},{2,8},{3,9},{4,14},{5,15},{6,12},{7,13},{8,2},{9,3},... | collective-permute-start | bytes 1585160 | tf_op jit(solution)/shard_map/ppermute | solution.py:44
  35.8 1.2 collective-permute-start.3
  37.0 6.3 %collective-permute-done.10.refs_0_ = bf16[32,64,128]{2,1,0:T(8,128)(2,1)} collective-permute-done((bf16[32,64,128]{2,1,0:T(8,128)(2,1)S(1)}, bf16[32,64,128]{2,1,0:T(8,128)(2,1)}, u32[]{:S(2)}, u32[]{:S(2)}) %collective-permute-start.10) | collective-permute-done | bytes 524320 | tf_op jit(solution)/shard_map/ppermute | solution.py:44
  43.3 26.5 %collective-permute-done.5.refs_1_.refs_4_ = bf16[129,16,128]{2,1,0:T(8,128)(2,1)S(1)} collective-permute-done((bf16[129,16,128]{2,1,0:T(8,128)(2,1)}, bf16[129,16,128]{2,1,0:T(8,128)(2,1)S(1)}, u32[]{:S(2)}, u32[]{:S(2)}) %collective-permute-start.5) | collective-permute-done | bytes 528416 | tf_op jit(solution)/shard_map/ppermute | solution.py:44
  69.9 10.5 %collective-permute-done.6.refs_1_.refs_0_.refs_5_ = bf16[129,16,128]{2,1,0:T(8,128)(2,1)S(1)} collective-permute-done((bf16[129,16,128]{2,1,0:T(8,128)(2,1)}, bf16[129,16,128]{2,1,0:T(8,128)(2,1)S(1)}, u32[]{:S(2)}, u32[]{:S(2)}) %collective-permute-start.6) | collective-permute-done | bytes 528416 | tf_op jit(solution)/shard_map/ppermute | solution.py:44
  81.8 1.0 copy-done.27
  82.8 3.1 %collective-permute-done.14.refs_0_ = bf16[32,64,128]{2,1,0:T(8,128)(2,1)S(1)} collective-permute-done((bf16[32,64,128]{2,1,0:T(8,128)(2,1)}, bf16[32,64,128]{2,1,0:T(8,128)(2,1)S(1)}, u32[]{:S(2)}, u32[]{:S(2)}) %collective-permute-start.14) | collective-permute-done | bytes 524320 | tf_op jit(solution)/shard_map/ppermute | solution.py:44
  86.7 1.6 collective-permute-start.11
  88.3 3.5 %collective-permute-start.7 = (bf16[129,16,128]{2,1,0:T(8,128)(2,1)S(1)}, bf16[129,16,128]{2,1,0:T(8,128)(2,1)S(1)}, u32[]{:S(2)}, u32[]{:S(2)}) collective-permute-start(bf16[129,16,128]{2,1,0:T(8,128)(2,1)S(1)} %copy-done.9), channel_id=1, source_target_pairs={{0,12},{1,13},{2,14},{3,15},{4,8},{5,9},{6,10},{7,11},{8,4},{9,5},... | collective-permute-start | bytes 1585160 | tf_op jit(solution)/shard_map/ppermute | solution.py:44
  91.8 3.7 %collective-permute-done.19.refs_4_ = bf16[32,64,128]{2,1,0:T(8,128)(2,1)S(1)} collective-permute-done((bf16[32,64,128]{2,1,0:T(8,128)(2,1)}, bf16[32,64,128]{2,1,0:T(8,128)(2,1)S(1)}, u32[]{:S(2)}, u32[]{:S(2)}) %collective-permute-start.19) | collective-permute-done | bytes 524320 | tf_op jit(solution)/shard_map/ppermute | solution.py:44
  95.5 7.4 %shard_map.74 = (f32[33,64,128]{2,1,0:T(8,128)}, f32[8,128]{1,0:T(8,128)}) custom-call(s32[2]{0:T(128)} %pad_add_fusion.3.ids_ref, bf16[129,16,128]{2,1,0:T(8,128)(2,1)} %get-tuple-element.23.refs_0_, bf16[129,16,128]{2,1,0:T(8,128)(2,1)} %copy-done.7, bf16[2,32,128,128]{3,2,1,0:T(8,128)(2,1)} %refs_8_.7, ...), custom_call_target="tpu_custom_call" | custom-call | flops 8165000192 | tf_op jit(solution)/shard_map/pallas_call | solution.py:408
  103.5 1.0 collective-permute-start.15
  104.5 7.4 %shard_map.75 = (f32[33,64,128]{2,1,0:T(8,128)}, f32[8,128]{1,0:T(8,128)}) custom-call(s32[2]{0:T(128)} %pad_add_fusion.3.ids_ref, bf16[129,16,128]{2,1,0:T(8,128)(2,1)} %copy-done.4, bf16[129,16,128]{2,1,0:T(8,128)(2,1)} %copy-done.6, bf16[2,32,128,128]{3,2,1,0:T(8,128)(2,1)} %refs_8_.7, bf16[2,32,128,128]{3,2,1,0:T(8,128)(2,1)} %collective-permute-done.9.refs_3_.refs_9_, ...), custom_call_target="tpu_custom_call" | custom-call | flops 8165000192 | tf_op jit(solution)/shard_map/pallas_call | solution.py:408
  112.0 1.6 collective-permute-start.8
  113.6 15.2 %collective-permute-done.15.refs_6_ = bf16[32,64,128]{2,1,0:T(8,128)(2,1)} collective-permute-done((bf16[32,64,128]{2,1,0:T(8,128)(2,1)S(1)}, bf16[32,64,128]{2,1,0:T(8,128)(2,1)}, u32[]{:S(2)}, u32[]{:S(2)}) %collective-permute-start.15) | collective-permute-done | bytes 524320 | tf_op jit(solution)/shard_map/ppermute | solution.py:44
  128.9 7.2 %shard_map.76 = (f32[33,64,128]{2,1,0:T(8,128)}, f32[8,128]{1,0:T(8,128)}) custom-call(s32[2]{0:T(128)} %pad_add_fusion.3.ids_ref, bf16[129,16,128]{2,1,0:T(8,128)(2,1)} %copy-done.8, bf16[129,16,128]{2,1,0:T(8,128)(2,1)} %copy-done.17, bf16[2,32,128,128]{3,2,1,0:T(8,128)(2,1)} %refs_8_.7, bf16[2,32,128,128]{3,2,1,0:T(8,128)(2,1)} %collective-permute-done.9.refs_3_.refs_9_, ...), custom_call_target="tpu_custom_call" | custom-call | flops 8165000192 | tf_op jit(solution)/shard_map/pallas_call | solution.py:408
  136.1 7.9 %collective-permute-done.8.refs_1_.refs_7_ = bf16[129,16,128]{2,1,0:T(8,128)(2,1)S(1)} collective-permute-done((bf16[129,16,128]{2,1,0:T(8,128)(2,1)S(1)}, bf16[129,16,128]{2,1,0:T(8,128)(2,1)S(1)}, u32[]{:S(2)}, u32[]{:S(2)}) %collective-permute-start.8) | collective-permute-done | bytes 528416 | tf_op jit(solution)/shard_map/ppermute | solution.py:44
  145.0 7.3 %shard_map.77 = (f32[32,64,128]{2,1,0:T(8,128)}, f32[16,128]{1,0:T(8,128)}) custom-call(s32[2]{0:T(128)} %pad_add_fusion.3.ids_ref, bf16[129,16,128]{2,1,0:T(8,128)(2,1)} %copy-done.18, bf16[129,16,128]{2,1,0:T(8,128)(2,1)} %copy-done.19, bf16[2,32,128,128]{3,2,1,0:T(8,128)(2,1)} %refs_8_.7, ...), custom_call_target="tpu_custom_call" | custom-call | flops 8165000192 | tf_op jit(solution)/shard_map/pallas_call | solution.py:408
  152.4 2.0 collective-permute-start.25
  154.5 1.8 collective-permute-done.25
  156.3 1.4 collective-permute-done.26
  158.4 3.1 %collective-permute-start.27 = (f32[16,128]{1,0:T(8,128)S(1)}, f32[16,128]{1,0:T(8,128)S(1)}, u32[]{:S(2)}, u32[]{:S(2)}) collective-permute-start(f32[16,128]{1,0:T(8,128)S(1)} %add_add_fusion.1), channel_id=1, source_target_pairs={{0,4},{1,5},{2,6},{3,7},{4,0},{5,1},{6,2},{7,3},{8,12},{9,13},{10,... | collective-permute-start | bytes 24584 | tf_op jit(solution)/shard_map/ppermute | solution.py:117
  161.5 2.4 %collective-permute-start.29 = (f32[16,128]{1,0:T(8,128)S(1)}, f32[16,128]{1,0:T(8,128)S(1)}, u32[]{:S(2)}, u32[]{:S(2)}) collective-permute-start(f32[16,128]{1,0:T(8,128)S(1)} %add_add_fusion.1), channel_id=1, source_target_pairs={{0,12},{1,13},{2,14},{3,15},{4,8},{5,9},{6,10},{7,11},{8,4},{9,5},... | collective-permute-start | bytes 24584 | tf_op jit(solution)/shard_map/ppermute | solution.py:117
  163.9 2.2 collective-permute-done.28
  166.1 0.9 collective-permute-done.29
  167.0 1.2 copy-done.3
  168.2 1.1 shard_map.78
  169.3 2.0 collective-permute-start.34
  171.3 10.5 %collective-permute-done.30.refs_12_ = bf16[32,64,128]{2,1,0:T(8,128)(2,1)S(1)} collective-permute-done((bf16[32,64,128]{2,1,0:T(8,128)(2,1)S(1)}, bf16[32,64,128]{2,1,0:T(8,128)(2,1)S(1)}, u32[]{:S(2)}, u32[]{:S(2)}) %collective-permute-start.30) | collective-permute-done | bytes 524320 | tf_op jit(solution)/shard_map/ppermute | solution.py:44
  183.0 1.0 collective-permute-start.31
  184.0 1.0 collective-permute-start.38
  186.8 7.8 %shard_map.79 = (f32[33,64,128]{2,1,0:T(8,128)}, f32[8,128]{1,0:T(8,128)}) custom-call(s32[5]{0:T(128)} %stack.78.ids_ref, bf16[129,16,128]{2,1,0:T(8,128)(2,1)} %get-tuple-element.23.refs_0_, bf16[129,16,128]{2,1,0:T(8,128)(2,1)} %copy-done.6, bf16[129,16,128]{2,1,0:T(8,128)(2,1)} %copy-done.8, bf16[129,16,128]{2,1,0:T(8,128)(2,1)} %copy-done.18, ...), custom_call_target="tpu_custom_call" | custom-call | flops 10234999808 | tf_op jit(solution)/shard_map/pallas_call | solution.py:408
  194.6 2.4 %collective-permute-done.31.refs_0_ = bf16[32,64,128]{2,1,0:T(8,128)(2,1)} collective-permute-done((bf16[32,64,128]{2,1,0:T(8,128)(2,1)S(1)}, bf16[32,64,128]{2,1,0:T(8,128)(2,1)}, u32[]{:S(2)}, u32[]{:S(2)}) %collective-permute-start.31) | collective-permute-done | bytes 524320 | tf_op jit(solution)/shard_map/ppermute | solution.py:44
  197.0 1.1 collective-permute-done.38.refs_12_
  198.7 1.7 collective-permute-start.36
  201.7 6.8 %shard_map.81 = (f32[33,64,128]{2,1,0:T(8,128)}, f32[8,128]{1,0:T(8,128)}) custom-call(s32[4]{0:T(128)} %pad_add_fusion.4.ids_ref, bf16[129,16,128]{2,1,0:T(8,128)(2,1)} %get-tuple-element.23.refs_0_, bf16[129,16,128]{2,1,0:T(8,128)(2,1)} %copy-done.6, bf16[129,16,128]{2,1,0:T(8,128)(2,1)} %copy-done.8, bf16[129,16,128]{2,1,0:T(8,128)(2,1)} %copy-done.18, ...), custom_call_target="tpu_custom_call" | custom-call | flops 8165000192 | tf_op jit(solution)/shard_map/pallas_call | solution.py:408
  208.5 4.9 %collective-permute-done.36.refs_0_ = bf16[32,64,128]{2,1,0:T(8,128)(2,1)} collective-permute-done((bf16[32,64,128]{2,1,0:T(8,128)(2,1)}, bf16[32,64,128]{2,1,0:T(8,128)(2,1)}, u32[]{:S(2)}, u32[]{:S(2)}) %collective-permute-start.36) | collective-permute-done | bytes 524320 | tf_op jit(solution)/shard_map/ppermute | solution.py:44
  213.4 1.4 collective-permute-done.40.upper_ref.refs_12_
  215.6 2.1 shard_map.83
  219.4 7.0 %shard_map.84 = (f32[33,64,128]{2,1,0:T(8,128)}, f32[8,128]{1,0:T(8,128)}) custom-call(s32[4]{0:T(128)} %pad_add_fusion.6.ids_ref, bf16[129,16,128]{2,1,0:T(8,128)(2,1)} %get-tuple-element.23.refs_0_, bf16[129,16,128]{2,1,0:T(8,128)(2,1)} %copy-done.6, bf16[129,16,128]{2,1,0:T(8,128)(2,1)} %copy-done.8, bf16[129,16,128]{2,1,0:T(8,128)(2,1)} %copy-done.18, ...), custom_call_target="tpu_custom_call" | custom-call | flops 8165000192 | tf_op jit(solution)/shard_map/pallas_call | solution.py:408
  228.5 1.5 collective-permute-done.44.refs_11_
  230.8 4.9 %shard_map.86 = bf16[32,64,128]{2,1,0:T(8,128)(2,1)} custom-call(s32[3]{0:T(128)} %pad_add_fusion.1.ids_ref, bf16[129,16,128]{2,1,0:T(8,128)(2,1)} %get-tuple-element.23.refs_0_, bf16[129,16,128]{2,1,0:T(8,128)(2,1)} %copy-done.6, bf16[129,16,128]{2,1,0:T(8,128)(2,1)} %copy-done.8, bf16[129,16,128]{2,1,0:T(8,128)(2,1)} %copy-done.18, ...), custom_call_target="tpu_custom_call" | custom-call | flops 6095000064 | tf_op jit(solution)/shard_map/pallas_call | solution.py:408
  (150 shorter events, 19.6 us)
Async XLA Ops:
  2.1 8.3 %collective-permute-start.1 = (bf16[2,32,64,128]{3,2,1,0:T(8,128)(2,1)S(1)}, bf16[2,32,64,128]{3,2,1,0:T(8,128)(2,1)}, u32[]{:S(2)}, u32[]{:S(2)}) collective-permute-start(bf16[2,32,64,128]{3,2,1,0:T(8,128)(2,1)S(1)} %constant_dynamic-slice_fusion.2), channel_id=1, source_target_pairs={{0,1},{1,0},{2,3},{3,2},{4,5},{5,4},{6,7},{7,6},{8,9},{9,8},{10,11... | collective-permute-start | bytes 3145736 | tf_op jit(solution)/shard_map/ppermute | solution.py:44
  2.6 84.1 %collective-permute-start.9 = (bf16[2,32,128,128]{3,2,1,0:T(8,128)(2,1)}, bf16[2,32,128,128]{3,2,1,0:T(8,128)(2,1)}, u32[]{:S(2)}, u32[]{:S(2)}) collective-permute-start(bf16[2,32,128,128]{3,2,1,0:T(8,128)(2,1)} %refs_8_.7), channel_id=1, source_target_pairs={{0,1},{1,0},{2,3},{3,2},{4,5},{5,4},{6,7},{7,6},{8,9},{9,8},{10,11... | collective-permute-start | bytes 6291464 | tf_op jit(solution)/shard_map/ppermute | solution.py:44
  3.5 27.5 %collective-permute-start.13 = (bf16[32,64,128]{2,1,0:T(8,128)(2,1)S(1)}, bf16[32,64,128]{2,1,0:T(8,128)(2,1)S(1)}, u32[]{:S(2)}, u32[]{:S(2)}) collective-permute-start(bf16[32,64,128]{2,1,0:T(8,128)(2,1)S(1)} %get-tuple-element.45.refs_4_.refs_8_.wave_ref), channel_id=1, source_target_pairs={{0,8},{1,9},{2,10},{3,11},{4,12},{5,13},{6,14},{7,15},{8,0},{9,1},... | collective-permute-start | bytes 1572872 | tf_op jit(solution)/shard_map/ppermute | solution.py:44
  7.6 23.5 %collective-permute-start.21 = (bf16[32,64,128]{2,1,0:T(8,128)(2,1)S(1)}, bf16[32,64,128]{2,1,0:T(8,128)(2,1)S(1)}, u32[]{:S(2)}, u32[]{:S(2)}) collective-permute-start(bf16[32,64,128]{2,1,0:T(8,128)(2,1)S(1)} %get-tuple-element.45.refs_4_.refs_8_.wave_ref), channel_id=1, source_target_pairs={{0,2},{1,3},{2,0},{3,1},{4,6},{5,7},{6,4},{7,5},{8,10},{9,11},{10,... | collective-permute-start | bytes 1572872 | tf_op jit(solution)/shard_map/ppermute | solution.py:44
  9.1 1.2 collective-permute-start
  16.4 19.4 %collective-permute-start.2 = (bf16[129,16,128]{2,1,0:T(8,128)(2,1)}, bf16[129,16,128]{2,1,0:T(8,128)(2,1)S(1)}, u32[]{:S(2)}, u32[]{:S(2)}) collective-permute-start(bf16[129,16,128]{2,1,0:T(8,128)(2,1)} %get-tuple-element.24), channel_id=1, source_target_pairs={{0,2},{1,3},{2,0},{3,1},{4,6},{5,7},{6,4},{7,5},{8,10},{9,11},{10,... | collective-permute-start | bytes 1585160 | tf_op jit(solution)/shard_map/ppermute | solution.py:44
  16.9 26.4 %collective-permute-start.10 = (bf16[32,64,128]{2,1,0:T(8,128)(2,1)S(1)}, bf16[32,64,128]{2,1,0:T(8,128)(2,1)}, u32[]{:S(2)}, u32[]{:S(2)}) collective-permute-start(bf16[32,64,128]{2,1,0:T(8,128)(2,1)S(1)} %get-tuple-element.45.refs_4_.refs_8_.wave_ref), channel_id=1, source_target_pairs={{0,4},{1,5},{2,6},{3,7},{4,0},{5,1},{6,2},{7,3},{8,12},{9,13},{10,... | collective-permute-start | bytes 1572872 | tf_op jit(solution)/shard_map/ppermute | solution.py:44
  31.1 38.8 %collective-permute-start.5 = (bf16[129,16,128]{2,1,0:T(8,128)(2,1)}, bf16[129,16,128]{2,1,0:T(8,128)(2,1)S(1)}, u32[]{:S(2)}, u32[]{:S(2)}) collective-permute-start(bf16[129,16,128]{2,1,0:T(8,128)(2,1)} %get-tuple-element.27), channel_id=1, source_target_pairs={{0,8},{1,9},{2,10},{3,11},{4,12},{5,13},{6,14},{7,15},{8,0},{9,1},... | collective-permute-start | bytes 1585160 | tf_op jit(solution)/shard_map/ppermute | solution.py:44
  31.9 48.5 %collective-permute-start.6 = (bf16[129,16,128]{2,1,0:T(8,128)(2,1)}, bf16[129,16,128]{2,1,0:T(8,128)(2,1)S(1)}, u32[]{:S(2)}, u32[]{:S(2)}) collective-permute-start(bf16[129,16,128]{2,1,0:T(8,128)(2,1)} %get-tuple-element.28), channel_id=1, source_target_pairs={{0,10},{1,11},{2,8},{3,9},{4,14},{5,15},{6,12},{7,13},{8,2},{9,3},... | collective-permute-start | bytes 1585160 | tf_op jit(solution)/shard_map/ppermute | solution.py:44
  35.8 46.0 %collective-permute-start.3 = (bf16[129,16,128]{2,1,0:T(8,128)(2,1)}, bf16[129,16,128]{2,1,0:T(8,128)(2,1)S(1)}, u32[]{:S(2)}, u32[]{:S(2)}) collective-permute-start(bf16[129,16,128]{2,1,0:T(8,128)(2,1)} %get-tuple-element.25), channel_id=1, source_target_pairs={{0,4},{1,5},{2,6},{3,7},{4,0},{5,1},{6,2},{7,3},{8,12},{9,13},{10,... | collective-permute-start | bytes 1585160 | tf_op jit(solution)/shard_map/ppermute | solution.py:44
  43.3 42.6 %collective-permute-start.14 = (bf16[32,64,128]{2,1,0:T(8,128)(2,1)}, bf16[32,64,128]{2,1,0:T(8,128)(2,1)S(1)}, u32[]{:S(2)}, u32[]{:S(2)}) collective-permute-start(bf16[32,64,128]{2,1,0:T(8,128)(2,1)} %shard_map.72.refs_6_), channel_id=1, source_target_pairs={{0,4},{1,5},{2,6},{3,7},{4,0},{5,1},{6,2},{7,3},{8,12},{9,13},{10,... | collective-permute-start | bytes 1572872 | tf_op jit(solution)/shard_map/ppermute | solution.py:44
  69.9 18.4 %collective-permute-start.23 = (bf16[32,64,128]{2,1,0:T(8,128)(2,1)}, bf16[32,64,128]{2,1,0:T(8,128)(2,1)}, u32[]{:S(2)}, u32[]{:S(2)}) collective-permute-start(bf16[32,64,128]{2,1,0:T(8,128)(2,1)} %shard_map.72.refs_6_), channel_id=1, source_target_pairs={{0,1},{1,0},{2,3},{3,2},{4,5},{5,4},{6,7},{7,6},{8,9},{9,8},{10,11... | collective-permute-start | bytes 1572872 | tf_op jit(solution)/shard_map/ppermute | solution.py:44
  80.4 15.1 %collective-permute-start.19 = (bf16[32,64,128]{2,1,0:T(8,128)(2,1)}, bf16[32,64,128]{2,1,0:T(8,128)(2,1)S(1)}, u32[]{:S(2)}, u32[]{:S(2)}) collective-permute-start(bf16[32,64,128]{2,1,0:T(8,128)(2,1)} %shard_map.72.refs_6_), channel_id=1, source_target_pairs={{0,2},{1,3},{2,0},{3,1},{4,6},{5,7},{6,4},{7,5},{8,10},{9,11},{10,... | collective-permute-start | bytes 1572872 | tf_op jit(solution)/shard_map/ppermute | solution.py:44
  82.8 20.1 %collective-permute-start.22 = (bf16[32,64,128]{2,1,0:T(8,128)(2,1)S(1)}, bf16[32,64,128]{2,1,0:T(8,128)(2,1)}, u32[]{:S(2)}, u32[]{:S(2)}) collective-permute-start(bf16[32,64,128]{2,1,0:T(8,128)(2,1)S(1)} %copy-done.27), channel_id=1, source_target_pairs={{0,1},{1,0},{2,3},{3,2},{4,5},{5,4},{6,7},{7,6},{8,9},{9,8},{10,11... | collective-permute-start | bytes 1572872 | tf_op jit(solution)/shard_map/ppermute | solution.py:44
  85.9 26.0 %collective-permute-start.17 = (bf16[32,64,128]{2,1,0:T(8,128)(2,1)}, bf16[32,64,128]{2,1,0:T(8,128)(2,1)}, u32[]{:S(2)}, u32[]{:S(2)}) collective-permute-start(bf16[32,64,128]{2,1,0:T(8,128)(2,1)} %shard_map.71.refs_4_), channel_id=1, source_target_pairs={{0,1},{1,0},{2,3},{3,2},{4,5},{5,4},{6,7},{7,6},{8,9},{9,8},{10,11... | collective-permute-start | bytes 1572872 | tf_op jit(solution)/shard_map/ppermute | solution.py:44
  86.7 25.3 %collective-permute-start.11 = (bf16[32,64,128]{2,1,0:T(8,128)(2,1)}, bf16[32,64,128]{2,1,0:T(8,128)(2,1)}, u32[]{:S(2)}, u32[]{:S(2)}) collective-permute-start(bf16[32,64,128]{2,1,0:T(8,128)(2,1)} %shard_map.71.refs_4_), channel_id=1, source_target_pairs={{0,2},{1,3},{2,0},{3,1},{4,6},{5,7},{6,4},{7,5},{8,10},{9,11},{10,... | collective-permute-start | bytes 1572872 | tf_op jit(solution)/shard_map/ppermute | solution.py:44
  88.3 25.3 %collective-permute-start.7 = (bf16[129,16,128]{2,1,0:T(8,128)(2,1)S(1)}, bf16[129,16,128]{2,1,0:T(8,128)(2,1)S(1)}, u32[]{:S(2)}, u32[]{:S(2)}) collective-permute-start(bf16[129,16,128]{2,1,0:T(8,128)(2,1)S(1)} %copy-done.9), channel_id=1, source_target_pairs={{0,12},{1,13},{2,14},{3,15},{4,8},{5,9},{6,10},{7,11},{8,4},{9,5},... | collective-permute-start | bytes 1585160 | tf_op jit(solution)/shard_map/ppermute | solution.py:44
  95.5 8.0 %collective-permute-start.20 = (bf16[32,64,128]{2,1,0:T(8,128)(2,1)S(1)}, bf16[32,64,128]{2,1,0:T(8,128)(2,1)S(1)}, u32[]{:S(2)}, u32[]{:S(2)}) collective-permute-start(bf16[32,64,128]{2,1,0:T(8,128)(2,1)S(1)} %collective-permute-done.19.refs_4_), channel_id=1, source_target_pairs={{0,1},{1,0},{2,3},{3,2},{4,5},{5,4},{6,7},{7,6},{8,9},{9,8},{10,11... | collective-permute-start | bytes 1572872 | tf_op jit(solution)/shard_map/ppermute | solution.py:44
  102.9 26.0 %collective-permute-start.18 = (bf16[32,64,128]{2,1,0:T(8,128)(2,1)S(1)}, bf16[32,64,128]{2,1,0:T(8,128)(2,1)}, u32[]{:S(2)}, u32[]{:S(2)}) collective-permute-start(bf16[32,64,128]{2,1,0:T(8,128)(2,1)S(1)} %copy-done.13), channel_id=1, source_target_pairs={{0,1},{1,0},{2,3},{3,2},{4,5},{5,4},{6,7},{7,6},{8,9},{9,8},{10,11... | collective-permute-start | bytes 1572872 | tf_op jit(solution)/shard_map/ppermute | solution.py:44
  103.5 25.4 %collective-permute-start.15 = (bf16[32,64,128]{2,1,0:T(8,128)(2,1)S(1)}, bf16[32,64,128]{2,1,0:T(8,128)(2,1)}, u32[]{:S(2)}, u32[]{:S(2)}) collective-permute-start(bf16[32,64,128]{2,1,0:T(8,128)(2,1)S(1)} %copy-done.13), channel_id=1, source_target_pairs={{0,2},{1,3},{2,0},{3,1},{4,6},{5,7},{6,4},{7,5},{8,10},{9,11},{10,... | collective-permute-start | bytes 1572872 | tf_op jit(solution)/shard_map/ppermute | solution.py:44
  111.9 24.2 %collective-permute-start.4 = (bf16[129,16,128]{2,1,0:T(8,128)(2,1)S(1)}, bf16[129,16,128]{2,1,0:T(8,128)(2,1)S(1)}, u32[]{:S(2)}, u32[]{:S(2)}) collective-permute-start(bf16[129,16,128]{2,1,0:T(8,128)(2,1)S(1)} %copy-done.20), channel_id=1, source_target_pairs={{0,6},{1,7},{2,4},{3,5},{4,2},{5,3},{6,0},{7,1},{8,14},{9,15},{10,... | collective-permute-start | bytes 1585160 | tf_op jit(solution)/shard_map/ppermute | solution.py:44
  112.0 32.0 %collective-permute-start.8 = (bf16[129,16,128]{2,1,0:T(8,128)(2,1)S(1)}, bf16[129,16,128]{2,1,0:T(8,128)(2,1)S(1)}, u32[]{:S(2)}, u32[]{:S(2)}) collective-permute-start(bf16[129,16,128]{2,1,0:T(8,128)(2,1)S(1)} %copy-done.10), channel_id=1, source_target_pairs={{0,14},{1,15},{2,12},{3,13},{4,10},{5,11},{6,8},{7,9},{8,6},{9,7},... | collective-permute-start | bytes 1585160 | tf_op jit(solution)/shard_map/ppermute | solution.py:44
  113.6 15.3 %copy-start.17 = (bf16[129,16,128]{2,1,0:T(8,128)(2,1)}, bf16[129,16,128]{2,1,0:T(8,128)(2,1)S(1)}, u32[]{:S(2)}) copy-start(bf16[129,16,128]{2,1,0:T(8,128)(2,1)S(1)} %collective-permute-done.7.refs_1_.refs_6_) | copy-start | bytes 1585156
  113.6 30.4 %collective-permute-start.12 = (bf16[32,64,128]{2,1,0:T(8,128)(2,1)}, bf16[32,64,128]{2,1,0:T(8,128)(2,1)S(1)}, u32[]{:S(2)}, u32[]{:S(2)}) collective-permute-start(bf16[32,64,128]{2,1,0:T(8,128)(2,1)} %collective-permute-done.11.refs_4_), channel_id=1, source_target_pairs={{0,1},{1,0},{2,3},{3,2},{4,5},{5,4},{6,7},{7,6},{8,9},{9,8},{10,11... | collective-permute-start | bytes 1572872 | tf_op jit(solution)/shard_map/ppermute | solution.py:44
  128.8 15.2 %collective-permute-start.16 = (bf16[32,64,128]{2,1,0:T(8,128)(2,1)}, bf16[32,64,128]{2,1,0:T(8,128)(2,1)}, u32[]{:S(2)}, u32[]{:S(2)}) collective-permute-start(bf16[32,64,128]{2,1,0:T(8,128)(2,1)} %collective-permute-done.15.refs_6_), channel_id=1, source_target_pairs={{0,1},{1,0},{2,3},{3,2},{4,5},{5,4},{6,7},{7,6},{8,9},{9,8},{10,11... | collective-permute-start | bytes 1572872 | tf_op jit(solution)/shard_map/ppermute | solution.py:44
  145.0 22.0 %copy-start.1 = (bf16[32,64,128]{2,1,0:T(8,128)(2,1)S(1)}, bf16[32,64,128]{2,1,0:T(8,128)(2,1)}, u32[]{:S(2)}) copy-start(bf16[32,64,128]{2,1,0:T(8,128)(2,1)} %copy-done) | copy-start | bytes 1572868
  152.3 2.2 collective-permute-start.24
  152.4 3.9 %collective-permute-start.25 = (f32[16,128]{1,0:T(8,128)}, f32[16,128]{1,0:T(8,128)S(1)}, u32[]{:S(2)}, u32[]{:S(2)}) collective-permute-start(f32[16,128]{1,0:T(8,128)} %get-tuple-element.35), channel_id=1, source_target_pairs={{0,2},{1,3},{2,0},{3,1},{4,6},{5,7},{6,4},{7,5},{8,10},{9,11},{10,... | collective-permute-start | bytes 24584 | tf_op jit(solution)/shard_map/ppermute | solution.py:117
  154.4 3.3 %collective-permute-start.26 = (f32[16,128]{1,0:T(8,128)}, f32[16,128]{1,0:T(8,128)S(1)}, u32[]{:S(2)}, u32[]{:S(2)}) collective-permute-start(f32[16,128]{1,0:T(8,128)} %get-tuple-element.35), channel_id=1, source_target_pairs={{0,3},{1,2},{2,1},{3,0},{4,7},{5,6},{6,5},{7,4},{8,11},{9,10},{10,... | collective-permute-start | bytes 24584 | tf_op jit(solution)/shard_map/ppermute | solution.py:117
  158.4 5.5 %collective-permute-start.27 = (f32[16,128]{1,0:T(8,128)S(1)}, f32[16,128]{1,0:T(8,128)S(1)}, u32[]{:S(2)}, u32[]{:S(2)}) collective-permute-start(f32[16,128]{1,0:T(8,128)S(1)} %add_add_fusion.1), channel_id=1, source_target_pairs={{0,4},{1,5},{2,6},{3,7},{4,0},{5,1},{6,2},{7,3},{8,12},{9,13},{10,... | collective-permute-start | bytes 24584 | tf_op jit(solution)/shard_map/ppermute | solution.py:117
  161.5 4.5 %collective-permute-start.28 = (f32[16,128]{1,0:T(8,128)S(1)}, f32[16,128]{1,0:T(8,128)S(1)}, u32[]{:S(2)}, u32[]{:S(2)}) collective-permute-start(f32[16,128]{1,0:T(8,128)S(1)} %add_add_fusion.1), channel_id=1, source_target_pairs={{0,8},{1,9},{2,10},{3,11},{4,12},{5,13},{6,14},{7,15},{8,0},{9,1},... | collective-permute-start | bytes 24584 | tf_op jit(solution)/shard_map/ppermute | solution.py:117
  161.5 5.4 %collective-permute-start.29 = (f32[16,128]{1,0:T(8,128)S(1)}, f32[16,128]{1,0:T(8,128)S(1)}, u32[]{:S(2)}, u32[]{:S(2)}) collective-permute-start(f32[16,128]{1,0:T(8,128)S(1)} %add_add_fusion.1), channel_id=1, source_target_pairs={{0,12},{1,13},{2,14},{3,15},{4,8},{5,9},{6,10},{7,11},{8,4},{9,5},... | collective-permute-start | bytes 24584 | tf_op jit(solution)/shard_map/ppermute | solution.py:117
  169.3 15.8 %copy-start.2 = (bf16[32,64,128]{2,1,0:T(8,128)(2,1)}, bf16[32,64,128]{2,1,0:T(8,128)(2,1)S(1)}, u32[]{:S(2)}) copy-start(bf16[32,64,128]{2,1,0:T(8,128)(2,1)S(1)} %get-tuple-element.36.refs_10_) | copy-start | bytes 1572868
  169.3 12.6 %collective-permute-start.30 = (bf16[32,64,128]{2,1,0:T(8,128)(2,1)S(1)}, bf16[32,64,128]{2,1,0:T(8,128)(2,1)S(1)}, u32[]{:S(2)}, u32[]{:S(2)}) collective-permute-start(bf16[32,64,128]{2,1,0:T(8,128)(2,1)S(1)} %get-tuple-element.36.refs_10_), channel_id=1, source_target_pairs={{0,4},{1,5},{2,0},{3,1},{4,8},{5,9},{6,2},{7,3},{8,12},{9,13},{10,... | collective-permute-start | bytes 1572872 | tf_op jit(solution)/shard_map/ppermute | solution.py:44
  169.3 12.5 %collective-permute-start.34 = (bf16[32,64,128]{2,1,0:T(8,128)(2,1)S(1)}, bf16[32,64,128]{2,1,0:T(8,128)(2,1)S(1)}, u32[]{:S(2)}, u32[]{:S(2)}) collective-permute-start(bf16[32,64,128]{2,1,0:T(8,128)(2,1)S(1)} %get-tuple-element.36.refs_10_), channel_id=1, source_target_pairs={{0,2},{1,3},{2,6},{3,7},{4,0},{5,1},{6,10},{7,11},{8,4},{9,5},{10,... | collective-permute-start | bytes 1572872 | tf_op jit(solution)/shard_map/ppermute | solution.py:44
  171.3 13.7 %collective-permute-start.32 = (bf16[32,64,128]{2,1,0:T(8,128)(2,1)S(1)}, bf16[32,64,128]{2,1,0:T(8,128)(2,1)S(1)}, u32[]{:S(2)}, u32[]{:S(2)}) collective-permute-start(bf16[32,64,128]{2,1,0:T(8,128)(2,1)S(1)} %get-tuple-element.36.refs_10_), channel_id=1, source_target_pairs={{0,1},{1,0},{2,3},{3,2},{4,5},{5,4},{6,7},{7,6},{8,9},{9,8},{10,11... | collective-permute-start | bytes 1572872 | tf_op jit(solution)/shard_map/ppermute | solution.py:44
  181.8 3.2 %collective-permute-start.33 = (bf16[32,64,128]{2,1,0:T(8,128)(2,1)S(1)}, bf16[32,64,128]{2,1,0:T(8,128)(2,1)S(1)}, u32[]{:S(2)}, u32[]{:S(2)}) collective-permute-start(bf16[32,64,128]{2,1,0:T(8,128)(2,1)S(1)} %collective-permute-done.30.refs_12_), channel_id=1, source_target_pairs={{0,1},{1,0},{2,3},{3,2},{4,5},{5,4},{6,7},{7,6},{8,9},{9,8},{10,11... | collective-permute-start | bytes 1572872 | tf_op jit(solution)/shard_map/ppermute | solution.py:44
  181.9 3.2 %collective-permute-start.35 = (bf16[32,64,128]{2,1,0:T(8,128)(2,1)S(1)}, bf16[32,64,128]{2,1,0:T(8,128)(2,1)S(1)}, u32[]{:S(2)}, u32[]{:S(2)}) collective-permute-start(bf16[32,64,128]{2,1,0:T(8,128)(2,1)S(1)} %collective-permute-done.34.refs_14_), channel_id=1, source_target_pairs={{0,1},{1,0},{2,3},{3,2},{4,5},{5,4},{6,7},{7,6},{8,9},{9,8},{10,11... | collective-permute-start | bytes 1572872 | tf_op jit(solution)/shard_map/ppermute | solution.py:44
  183.0 14.0 %collective-permute-start.31 = (bf16[32,64,128]{2,1,0:T(8,128)(2,1)S(1)}, bf16[32,64,128]{2,1,0:T(8,128)(2,1)}, u32[]{:S(2)}, u32[]{:S(2)}) collective-permute-start(bf16[32,64,128]{2,1,0:T(8,128)(2,1)S(1)} %collective-permute-done.30.refs_12_), channel_id=1, source_target_pairs={{0,4},{1,5},{2,0},{3,1},{4,8},{5,9},{6,2},{7,3},{8,12},{9,13},{10,... | collective-permute-start | bytes 1572872 | tf_op jit(solution)/shard_map/ppermute | solution.py:44
  184.0 14.1 %collective-permute-start.38 = (bf16[32,64,128]{2,1,0:T(8,128)(2,1)S(1)}, bf16[32,64,128]{2,1,0:T(8,128)(2,1)}, u32[]{:S(2)}, u32[]{:S(2)}) collective-permute-start(bf16[32,64,128]{2,1,0:T(8,128)(2,1)S(1)} %collective-permute-done.34.refs_14_), channel_id=1, source_target_pairs={{0,2},{1,3},{2,6},{3,7},{4,0},{5,1},{6,10},{7,11},{8,4},{9,5},{10,... | collective-permute-start | bytes 1572872 | tf_op jit(solution)/shard_map/ppermute | solution.py:44
  197.0 3.8 %collective-permute-start.37 = (bf16[32,64,128]{2,1,0:T(8,128)(2,1)}, bf16[32,64,128]{2,1,0:T(8,128)(2,1)S(1)}, u32[]{:S(2)}, u32[]{:S(2)}) collective-permute-start(bf16[32,64,128]{2,1,0:T(8,128)(2,1)} %shard_map.80.refs_10_), channel_id=1, source_target_pairs={{0,1},{1,0},{2,3},{3,2},{4,5},{5,4},{6,7},{7,6},{8,9},{9,8},{10,11... | collective-permute-start | bytes 1572872 | tf_op jit(solution)/shard_map/ppermute | solution.py:44
  198.1 2.7 %collective-permute-start.39 = (bf16[32,64,128]{2,1,0:T(8,128)(2,1)}, bf16[32,64,128]{2,1,0:T(8,128)(2,1)S(1)}, u32[]{:S(2)}, u32[]{:S(2)}) collective-permute-start(bf16[32,64,128]{2,1,0:T(8,128)(2,1)} %collective-permute-done.38.refs_12_), channel_id=1, source_target_pairs={{0,1},{1,0},{2,3},{3,2},{4,5},{5,4},{6,7},{7,6},{8,9},{9,8},{10,11... | collective-permute-start | bytes 1572872 | tf_op jit(solution)/shard_map/ppermute | solution.py:44
  198.7 14.7 %collective-permute-start.36 = (bf16[32,64,128]{2,1,0:T(8,128)(2,1)}, bf16[32,64,128]{2,1,0:T(8,128)(2,1)}, u32[]{:S(2)}, u32[]{:S(2)}) collective-permute-start(bf16[32,64,128]{2,1,0:T(8,128)(2,1)} %shard_map.80.refs_10_), channel_id=1, source_target_pairs={{0,4},{1,5},{2,0},{3,1},{4,8},{5,9},{6,2},{7,3},{8,12},{9,13},{10,... | collective-permute-start | bytes 1572872 | tf_op jit(solution)/shard_map/ppermute | solution.py:44
  200.5 14.3 %collective-permute-start.40 = (bf16[32,64,128]{2,1,0:T(8,128)(2,1)}, bf16[32,64,128]{2,1,0:T(8,128)(2,1)S(1)}, u32[]{:S(2)}, u32[]{:S(2)}) collective-permute-start(bf16[32,64,128]{2,1,0:T(8,128)(2,1)} %collective-permute-done.38.refs_12_), channel_id=1, source_target_pairs={{0,2},{1,3},{2,6},{3,7},{4,0},{5,1},{6,10},{7,11},{8,4},{9,5},{10,... | collective-permute-start | bytes 1572872 | tf_op jit(solution)/shard_map/ppermute | solution.py:44
  213.4 5.1 %collective-permute-start.42 = (bf16[32,64,128]{2,1,0:T(8,128)(2,1)}, bf16[32,64,128]{2,1,0:T(8,128)(2,1)S(1)}, u32[]{:S(2)}, u32[]{:S(2)}) collective-permute-start(bf16[32,64,128]{2,1,0:T(8,128)(2,1)} %shard_map.82.lower_ref.refs_10_), channel_id=1, source_target_pairs={{0,1},{1,0},{2,3},{3,2},{4,5},{5,4},{6,7},{7,6},{8,9},{9,8},{10,11... | collective-permute-start | bytes 1572872 | tf_op jit(solution)/shard_map/ppermute | solution.py:44
  214.8 3.7 %collective-permute-start.43 = (bf16[32,64,128]{2,1,0:T(8,128)(2,1)S(1)}, bf16[32,64,128]{2,1,0:T(8,128)(2,1)S(1)}, u32[]{:S(2)}, u32[]{:S(2)}) collective-permute-start(bf16[32,64,128]{2,1,0:T(8,128)(2,1)S(1)} %collective-permute-done.40.upper_ref.refs_12_), channel_id=1, source_target_pairs={{0,1},{1,0},{2,3},{3,2},{4,5},{5,4},{6,7},{7,6},{8,9},{9,8},{10,11... | collective-permute-start | bytes 1572872 | tf_op jit(solution)/shard_map/ppermute | solution.py:44
  217.7 9.4 %collective-permute-start.41 = (bf16[32,64,128]{2,1,0:T(8,128)(2,1)}, bf16[32,64,128]{2,1,0:T(8,128)(2,1)S(1)}, u32[]{:S(2)}, u32[]{:S(2)}) collective-permute-start(bf16[32,64,128]{2,1,0:T(8,128)(2,1)} %shard_map.83), channel_id=1, source_target_pairs={{0,4},{1,3},{2,0},{3,7},{4,8},{5,1},{6,2},{7,11},{8,12},{9,5},{10,... | collective-permute-start | bytes 1572872 | tf_op jit(solution)/shard_map/ppermute | solution.py:44
  227.9 2.1 collective-permute-start.44
  (36 other events, 120.4 us)

commit v16 on v15

--- a/solution.py
+++ b/solution.py
@@ -58,23 +58,6 @@
     return permute(
         value, owners, halves, lambda chip, half: ring[(place[chip] + shifts[half]) % owners]
     )
-
-
-def select_kernel(half_ref, lower_ref, upper_ref, *rest):
-    out_ref = rest[-1]
-    out_ref[...] = jnp.where(half_ref[0] == 0, lower_ref[...], upper_ref[...])
-
-
-def select_half(half, lower, upper, *others):
-    anywhere = pl.BlockSpec(memory_space=pl.ANY)
-    whole = pl.BlockSpec(memory_space=pltpu.VMEM)
-    return pl.pallas_call(
-        select_kernel,
-        out_shape=jax.ShapeDtypeStruct(lower.shape, lower.dtype),
-        in_specs=[pl.BlockSpec(memory_space=pltpu.SMEM), whole, whole] + [anywhere] * len(others),
-        out_specs=whole,
-        cost_estimate=busy(0.8),
-    )(jnp.reshape(half, (1,)).astype(jnp.int32), lower, upper, *others)
 
 
 def after_kernel(*refs):
@@ -244,7 +227,7 @@
     stats_ref[...] = jnp.where((row == device) & (lane < 4), values, 0.0)
 
 
-def apply_kernel(sources, choices, first, end, terms, capacity, ids_ref, *refs):
+def apply_kernel(sources, choices, chosen, first, end, terms, capacity, ids_ref, *refs):
     refs = list(refs)
 
     def take(count):
@@ -300,7 +283,7 @@
         if choices:
             for choice, piece in enumerate(lefts):
 
-                @pl.when(ids_ref[2 + source] == choice)
+                @pl.when(ids_ref[chosen + source] == choice)
                 def _():
                     for copy in left_copies(source, piece):
                         copy.start()
@@ -362,7 +345,7 @@
         store_total.wait()
 
 
-def apply_group(ids, lefts, rights, vectors, total, end, wave=None):
+def apply_group(ids, lefts, rights, vectors, total, end, wave=None, chosen=0):
     blocks, rows, width = vectors[0][0].shape
     terms = rights[0].shape[0]
     parts = lefts[0].shape[0] - 1
@@ -404,9 +387,9 @@
         ),
         "result": (jax.ShapeDtypeStruct((blocks, rows, width), jnp.bfloat16), whole),
     }[end]
-    choices = len(lefts) if ids.shape[0] > 2 else 0
+    choices = len(lefts) if chosen else 0
     return pl.pallas_call(
-        functools.partial(apply_kernel, sources, choices, first, end, terms, capacity),
+        functools.partial(apply_kernel, sources, choices, chosen, first, end, terms, capacity),
         out_shape=out_shape,
         in_specs=[pl.BlockSpec(memory_space=pltpu.SMEM)] + [anywhere] * len(arrays),
         out_specs=out_specs,
@@ -483,44 +466,47 @@
     near = mask_gather(own_rows, lefts, owners, halves)
     far = {m: swap(unit, owners, halves) if m else other_rows for m, unit in near.items()}
 
-    here = [half, me * halves + half]
-    no_choice = jnp.stack(here).astype(jnp.int32)
+    reach = (owners - 1) // 2
+    turn = 1 - 2 * half
+    distances = [0] + [s for step in range(1, reach + 1) for s in (step, -step)] + [owners // 2]
+    whose = [me ^ ring_owner(place - s * turn, owners) for s in distances]
+    numbers = jnp.stack([half, me * halves + half, *whose]).astype(jnp.int32)
     total = None
-    for at in range(0, owners, 2):
-        group = order[at : at + 2]
+    groups = [order[at : at + 2] for at in range(0, owners, 2)]
+    for group in groups:
         total, stats = apply_group(
-            no_choice,
+            numbers,
             [lefts[m] for m in group],
             rights,
             [(near[m], far[m]) for m in group],
             total,
-            "go on" if at + 2 < owners else "stats",
+            "go on" if group is not groups[-1] else "stats",
             own_rows,
         )
 
     entries = blocks * owners * height * width
     stats = spread(stats, owners * halves)
     direction, rayleigh = new_direction(total, own_rows, stats, entries)
-    reach = (owners - 1) // 2
-
     def add_group(total, units, end):
-        choices = [me ^ ring_owner(place - s, owners) for s in units]
-        vectors = [(unit, swap(unit, owners, halves)) for unit in units.values()]
-        ids = jnp.stack(here + choices).astype(jnp.int32)
-        return apply_group(ids, lefts, rights, vectors, total, end)
+        vectors = [(unit, swap(units[-s], owners, halves)) for s, unit in units.items()]
+        chosen = 2 + distances.index(next(iter(units)))
+        return apply_group(numbers, lefts, rights, vectors, total, end, chosen=chosen)
 
     total, waiting = None, {0: direction}
     ahead = behind = direction
     for step in range(1, reach + 1):
-        ahead = ring_send(ahead, owners, halves, (1,) * halves)
-        behind = ring_send(behind, owners, halves, (-1,) * halves)
+        ahead = ring_send(ahead, owners, halves, (1, -1))
+        behind = ring_send(behind, owners, halves, (-1, 1))
         if step > 1:
             total, token = add_group(total, waiting, "go on")
             ahead, waiting = after(ahead, token), {}
         waiting.update({step: ahead, -step: behind})
-    last = ring_send(select_half(half, ahead, behind), owners, halves, (1, -1))
+    last = ring_send(ahead, owners, halves, (1, -1))
     total, token = add_group(total, waiting, "go on")
-    total = add_group(total, {owners // 2: after(last, token)}, "result")
+    last = after(last, token)
+    vectors = [(last, swap(last, owners, halves))]
+    chosen = 2 + distances.index(owners // 2)
+    total = apply_group(numbers, lefts, rights, vectors, total, "result", chosen=chosen)
     return (total, rayleigh[0])
 
 

time: 237 us -> 234 us (0.987)
  other arithmetic: 3.88 us -> 1.31 us
    another operation x4 -> x0, other arithmetic: 2.58 us -> none  [the longest x3 2 us: add_group(): ids = jnp.stack(here + choices).astype(jnp.int32)]
    unnamed x78 -> x80, local copies, waits for them, and re-layouts: 10.7 us -> 9.4 us
    pallas_call x9 -> x8, Pallas kernels: 57.9 us -> 57.7 us  [apply_group(): pl.pallas_call(functools.partial(apply_kernel, sources, choices, chosen,...]
  transfers between devices with their start and end apart: 45 -> 45, of which waited for: 20 -> 21; matrix products, arithmetic and copies ran while one was open for 2% -> 1% of each run, Pallas kernels for 22% -> 22%
where the time goes in v16:
time: 234 us; the launch traced here: 233 us
  waiting for transfers between devices  115 us (49%)
  Pallas kernels  64.3 us (27%)
  starting transfers between devices  38.5 us (16%)
  local copies, waits for them, and re-layouts  12.4 us (5%)
    ppermute x39, waiting for transfers between devices, permute(): return lax.ppermute(value, BOTH, pairs)  108 us
    pallas_call x8, Pallas kernels, apply_group(): pl.pallas_call(functools.partial(apply_kernel, sources, choices, chosen,...  57.7 us
    ppermute x39, starting transfers between devices, permute(): return lax.ppermute(value, BOTH, pairs)  31.3 us
    unnamed x80, local copies, waits for them, and re-layouts  9.4 us
    ppermute x6, starting transfers between devices, spread(): lax.ppermute(value, BOTH, [(d, d ^ m) for d in range(devices)])  7.16 us
    ppermute x6, waiting for transfers between devices, spread(): lax.ppermute(value, BOTH, [(d, d ^ m) for d in range(devices)])  6.79 us
    pallas_call x1, Pallas kernels, pack(): pl.pallas_call(functools.partial(pack_kernel, order, capacity, blocks, te...  5.49 us
  transfers between devices with their start and end apart: 45, of which 21 were waited for; matrix products, arithmetic and copies ran while one was open for 1% of the time, Pallas kernels for 22%

profile of v16, /device:TPU:0, one launch (start us, length us, event | category | flops | bytes accessed | tf_op | source)
XLA Modules:
  0.0 232.8 jit_solution(17629128368047042299)
XLA Ops:
  0.6 1.4 constant_dynamic-slice_fusion.2
  2.7 0.9 constant_dynamic-slice_fusion
  3.5 4.0 %collective-permute-start.13 = (bf16[32,64,128]{2,1,0:T(8,128)(2,1)S(1)}, bf16[32,64,128]{2,1,0:T(8,128)(2,1)}, u32[]{:S(2)}, u32[]{:S(2)}) collective-permute-start(bf16[32,64,128]{2,1,0:T(8,128)(2,1)S(1)} %get-tuple-element.45.refs_4_.refs_8_.wave_ref), channel_id=1, source_target_pairs={{0,8},{1,9},{2,10},{3,11},{4,12},{5,13},{6,14},{7,15},{8,0},{9,1},... | collective-permute-start | bytes 1572872 | tf_op jit(solution)/shard_map/ppermute | solution.py:44
  7.6 1.5 collective-permute-start.21
  10.9 5.5 %shard_map.68 = (bf16[129,16,128]{2,1,0:T(8,128)(2,1)}, bf16[129,16,128]{2,1,0:T(8,128)(2,1)}, bf16[129,16,128]{2,1,0:T(8,128)(2,1)}, bf16[129,16,128]{2,1,0:T(8...) custom-call(s32[2]{0:T(128)} %pad_add_fusion.1.ids_ref, ...), custom_call_target="tpu_custom_call" | custom-call | flops 5750000128 | tf_op jit(solution)/shard_map/pallas_call | solution.py:167
  17.0 1.6 collective-permute-start.10
  18.5 12.6 %collective-permute-done.13.refs_0_ = bf16[32,64,128]{2,1,0:T(8,128)(2,1)} collective-permute-done((bf16[32,64,128]{2,1,0:T(8,128)(2,1)S(1)}, bf16[32,64,128]{2,1,0:T(8,128)(2,1)}, u32[]{:S(2)}, u32[]{:S(2)}) %collective-permute-start.13) | collective-permute-done | bytes 524320 | tf_op jit(solution)/shard_map/ppermute | solution.py:44
  31.2 3.9 %collective-permute-start.6 = (bf16[129,16,128]{2,1,0:T(8,128)(2,1)}, bf16[129,16,128]{2,1,0:T(8,128)(2,1)S(1)}, u32[]{:S(2)}, u32[]{:S(2)}) collective-permute-start(bf16[129,16,128]{2,1,0:T(8,128)(2,1)} %get-tuple-element.28), channel_id=1, source_target_pairs={{0,10},{1,11},{2,8},{3,9},{4,14},{5,15},{6,12},{7,13},{8,2},{9,3},... | collective-permute-start | bytes 1585160 | tf_op jit(solution)/shard_map/ppermute | solution.py:44
  35.1 1.1 collective-permute-start.3
  36.3 7.0 %collective-permute-done.10.refs_0_ = bf16[32,64,128]{2,1,0:T(8,128)(2,1)S(1)} collective-permute-done((bf16[32,64,128]{2,1,0:T(8,128)(2,1)S(1)}, bf16[32,64,128]{2,1,0:T(8,128)(2,1)S(1)}, u32[]{:S(2)}, u32[]{:S(2)}) %collective-permute-start.10) | collective-permute-done | bytes 524320 | tf_op jit(solution)/shard_map/ppermute | solution.py:44
  43.3 26.7 %collective-permute-done.5.refs_1_.refs_4_ = bf16[129,16,128]{2,1,0:T(8,128)(2,1)S(1)} collective-permute-done((bf16[129,16,128]{2,1,0:T(8,128)(2,1)}, bf16[129,16,128]{2,1,0:T(8,128)(2,1)S(1)}, u32[]{:S(2)}, u32[]{:S(2)}) %collective-permute-start.5) | collective-permute-done | bytes 528416 | tf_op jit(solution)/shard_map/ppermute | solution.py:44
  70.0 10.5 %collective-permute-done.6.refs_1_.refs_0_.refs_5_ = bf16[129,16,128]{2,1,0:T(8,128)(2,1)S(1)} collective-permute-done((bf16[129,16,128]{2,1,0:T(8,128)(2,1)}, bf16[129,16,128]{2,1,0:T(8,128)(2,1)S(1)}, u32[]{:S(2)}, u32[]{:S(2)}) %collective-permute-start.6) | collective-permute-done | bytes 528416 | tf_op jit(solution)/shard_map/ppermute | solution.py:44
  82.1 3.9 %collective-permute-done.14.refs_0_ = bf16[32,64,128]{2,1,0:T(8,128)(2,1)S(1)} collective-permute-done((bf16[32,64,128]{2,1,0:T(8,128)(2,1)}, bf16[32,64,128]{2,1,0:T(8,128)(2,1)S(1)}, u32[]{:S(2)}, u32[]{:S(2)}) %collective-permute-start.14) | collective-permute-done | bytes 524320 | tf_op jit(solution)/shard_map/ppermute | solution.py:44
  86.8 1.6 collective-permute-start.11
  88.4 3.5 %collective-permute-start.7 = (bf16[129,16,128]{2,1,0:T(8,128)(2,1)S(1)}, bf16[129,16,128]{2,1,0:T(8,128)(2,1)S(1)}, u32[]{:S(2)}, u32[]{:S(2)}) collective-permute-start(bf16[129,16,128]{2,1,0:T(8,128)(2,1)S(1)} %copy-done.9), channel_id=1, source_target_pairs={{0,12},{1,13},{2,14},{3,15},{4,8},{5,9},{6,10},{7,11},{8,4},{9,5},... | collective-permute-start | bytes 1585160 | tf_op jit(solution)/shard_map/ppermute | solution.py:44
  91.9 3.8 %collective-permute-done.19.refs_4_ = bf16[32,64,128]{2,1,0:T(8,128)(2,1)} collective-permute-done((bf16[32,64,128]{2,1,0:T(8,128)(2,1)}, bf16[32,64,128]{2,1,0:T(8,128)(2,1)}, u32[]{:S(2)}, u32[]{:S(2)}) %collective-permute-start.19) | collective-permute-done | bytes 524320 | tf_op jit(solution)/shard_map/ppermute | solution.py:44
  95.7 7.5 %shard_map.74 = (f32[33,64,128]{2,1,0:T(8,128)}, f32[8,128]{1,0:T(8,128)}) custom-call(s32[10]{0:T(128)} %stack.56.ids_ref, bf16[129,16,128]{2,1,0:T(8,128)(2,1)} %get-tuple-element.23.refs_0_, bf16[129,16,128]{2,1,0:T(8,128)(2,1)} %copy-done.7, bf16[2,32,128,128]{3,2,1,0:T(8,128)(2,1)} %refs_8_.7, ...), custom_call_target="tpu_custom_call" | custom-call | flops 8165000192 | tf_op jit(solution)/shard_map/pallas_call | solution.py:391
  104.0 0.9 collective-permute-start.15
  104.8 7.6 %shard_map.75 = (f32[33,64,128]{2,1,0:T(8,128)}, f32[8,128]{1,0:T(8,128)}) custom-call(s32[10]{0:T(128)} %stack.56.ids_ref, bf16[129,16,128]{2,1,0:T(8,128)(2,1)} %copy-done.4, bf16[129,16,128]{2,1,0:T(8,128)(2,1)} %copy-done.6, bf16[2,32,128,128]{3,2,1,0:T(8,128)(2,1)} %refs_8_.7, bf16[2,32,128,128]{3,2,1,0:T(8,128)(2,1)} %collective-permute-done.9.refs_3_.refs_9_, ...), custom_call_target="tpu_custom_call" | custom-call | flops 8165000192 | tf_op jit(solution)/shard_map/pallas_call | solution.py:391
  113.3 1.3 collective-permute-start.8
  114.6 14.7 %collective-permute-done.15.refs_6_ = bf16[32,64,128]{2,1,0:T(8,128)(2,1)} collective-permute-done((bf16[32,64,128]{2,1,0:T(8,128)(2,1)S(1)}, bf16[32,64,128]{2,1,0:T(8,128)(2,1)}, u32[]{:S(2)}, u32[]{:S(2)}) %collective-permute-start.15) | collective-permute-done | bytes 524320 | tf_op jit(solution)/shard_map/ppermute | solution.py:44
  129.3 7.5 %shard_map.76 = (f32[33,64,128]{2,1,0:T(8,128)}, f32[8,128]{1,0:T(8,128)}) custom-call(s32[10]{0:T(128)} %stack.56.ids_ref, bf16[129,16,128]{2,1,0:T(8,128)(2,1)} %copy-done.8, bf16[129,16,128]{2,1,0:T(8,128)(2,1)} %copy-done.19, bf16[2,32,128,128]{3,2,1,0:T(8,128)(2,1)} %refs_8_.7, bf16[2,32,128,128]{3,2,1,0:T(8,128)(2,1)} %collective-permute-done.9.refs_3_.refs_9_, ...), custom_call_target="tpu_custom_call" | custom-call | flops 8165000192 | tf_op jit(solution)/shard_map/pallas_call | solution.py:391
  136.9 8.1 %collective-permute-done.8.refs_1_.refs_7_ = bf16[129,16,128]{2,1,0:T(8,128)(2,1)} collective-permute-done((bf16[129,16,128]{2,1,0:T(8,128)(2,1)S(1)}, bf16[129,16,128]{2,1,0:T(8,128)(2,1)}, u32[]{:S(2)}, u32[]{:S(2)}) %collective-permute-start.8) | collective-permute-done | bytes 528416 | tf_op jit(solution)/shard_map/ppermute | solution.py:44
  146.0 7.5 %shard_map.77 = (f32[32,64,128]{2,1,0:T(8,128)}, f32[16,128]{1,0:T(8,128)}) custom-call(s32[10]{0:T(128)} %stack.56.ids_ref, bf16[129,16,128]{2,1,0:T(8,128)(2,1)} %copy-done.20, bf16[129,16,128]{2,1,0:T(8,128)(2,1)} %collective-permute-done.8.refs_1_.refs_7_, bf16[2,32,128,128]{3,2,1,0:T(8,128)(2,1)} %refs_8_.7, ...), custom_call_target="tpu_custom_call" | custom-call | flops 8165000192 | tf_op jit(solution)/shard_map/pallas_call | solution.py:391
  153.6 1.6 collective-permute-start.25
  155.5 2.1 collective-permute-done.25
  157.5 1.0 collective-permute-done.26
  159.2 2.9 %collective-permute-start.27 = (f32[16,128]{1,0:T(8,128)S(1)}, f32[16,128]{1,0:T(8,128)S(1)}, u32[]{:S(2)}, u32[]{:S(2)}) collective-permute-start(f32[16,128]{1,0:T(8,128)S(1)} %add_add_fusion.1), channel_id=1, source_target_pairs={{0,4},{1,5},{2,6},{3,7},{4,0},{5,1},{6,2},{7,3},{8,12},{9,13},{10,... | collective-permute-start | bytes 24584 | tf_op jit(solution)/shard_map/ppermute | solution.py:100
  162.7 1.7 collective-permute-start.29
  164.4 2.2 collective-permute-done.28
  166.6 1.6 collective-permute-done.29
  168.2 1.2 copy-done.3
  169.4 1.1 shard_map.78
  170.5 1.0 collective-permute-start.33
  171.5 1.0 collective-permute-start.30
  172.5 10.5 %collective-permute-done.33.refs_14_ = bf16[32,64,128]{2,1,0:T(8,128)(2,1)S(1)} collective-permute-done((bf16[32,64,128]{2,1,0:T(8,128)(2,1)S(1)}, bf16[32,64,128]{2,1,0:T(8,128)(2,1)S(1)}, u32[]{:S(2)}, u32[]{:S(2)}) %collective-permute-start.33) | collective-permute-done | bytes 524320 | tf_op jit(solution)/shard_map/ppermute | solution.py:44
  184.4 1.2 collective-permute-start.37
  187.4 8.3 %shard_map.79 = (f32[33,64,128]{2,1,0:T(8,128)}, f32[8,128]{1,0:T(8,128)}) custom-call(s32[10]{0:T(128)} %stack.56.ids_ref, bf16[129,16,128]{2,1,0:T(8,128)(2,1)} %get-tuple-element.23.refs_0_, bf16[129,16,128]{2,1,0:T(8,128)(2,1)} %copy-done.6, bf16[129,16,128]{2,1,0:T(8,128)(2,1)} %copy-done.8, bf16[129,16,128]{2,1,0:T(8,128)(2,1)} %copy-done.20, ...), custom_call_target="tpu_custom_call" | custom-call | flops 10234999808 | tf_op jit(solution)/shard_map/pallas_call | solution.py:391
  195.7 2.3 collective-permute-done.31.refs_0_
  198.5 1.2 collective-permute-start.36
  199.7 0.8 collective-permute-start.41
  201.6 6.9 %shard_map.81 = (f32[33,64,128]{2,1,0:T(8,128)}, f32[8,128]{1,0:T(8,128)}) custom-call(s32[10]{0:T(128)} %stack.56.ids_ref, bf16[129,16,128]{2,1,0:T(8,128)(2,1)} %get-tuple-element.23.refs_0_, bf16[129,16,128]{2,1,0:T(8,128)(2,1)} %copy-done.6, bf16[129,16,128]{2,1,0:T(8,128)(2,1)} %copy-done.8, bf16[129,16,128]{2,1,0:T(8,128)(2,1)} %copy-done.20, ...), custom_call_target="tpu_custom_call" | custom-call | flops 8165000192 | tf_op jit(solution)/shard_map/pallas_call | solution.py:391
  208.5 4.6 %collective-permute-done.36.refs_0_ = bf16[32,64,128]{2,1,0:T(8,128)(2,1)} collective-permute-done((bf16[32,64,128]{2,1,0:T(8,128)(2,1)}, bf16[32,64,128]{2,1,0:T(8,128)(2,1)}, u32[]{:S(2)}, u32[]{:S(2)}) %collective-permute-start.36) | collective-permute-done | bytes 524320 | tf_op jit(solution)/shard_map/ppermute | solution.py:44
  213.6 1.5 collective-permute-start.40
  216.5 7.4 %shard_map.83 = (f32[33,64,128]{2,1,0:T(8,128)}, f32[8,128]{1,0:T(8,128)}) custom-call(s32[10]{0:T(128)} %stack.56.ids_ref, bf16[129,16,128]{2,1,0:T(8,128)(2,1)} %get-tuple-element.23.refs_0_, bf16[129,16,128]{2,1,0:T(8,128)(2,1)} %copy-done.6, bf16[129,16,128]{2,1,0:T(8,128)(2,1)} %copy-done.8, bf16[129,16,128]{2,1,0:T(8,128)(2,1)} %copy-done.20, ...), custom_call_target="tpu_custom_call" | custom-call | flops 8165000192 | tf_op jit(solution)/shard_map/pallas_call | solution.py:391
  224.7 2.1 collective-permute-done.44.refs_11_
  226.8 0.8 copy-done.38
  227.7 5.0 %shard_map.85 = bf16[32,64,128]{2,1,0:T(8,128)(2,1)} custom-call(s32[10]{0:T(128)} %stack.56.ids_ref, bf16[129,16,128]{2,1,0:T(8,128)(2,1)} %get-tuple-element.23.refs_0_, bf16[129,16,128]{2,1,0:T(8,128)(2,1)} %copy-done.6, bf16[129,16,128]{2,1,0:T(8,128)(2,1)} %copy-done.8, bf16[129,16,128]{2,1,0:T(8,128)(2,1)} %copy-done.20, ...), custom_call_target="tpu_custom_call" | custom-call | flops 6095000064 | tf_op jit(solution)/shard_map/pallas_call | solution.py:391
  (147 shorter events, 16.9 us)
Async XLA Ops:
  2.1 8.3 %collective-permute-start.1 = (bf16[2,32,64,128]{3,2,1,0:T(8,128)(2,1)S(1)}, bf16[2,32,64,128]{3,2,1,0:T(8,128)(2,1)}, u32[]{:S(2)}, u32[]{:S(2)}) collective-permute-start(bf16[2,32,64,128]{3,2,1,0:T(8,128)(2,1)S(1)} %constant_dynamic-slice_fusion.2), channel_id=1, source_target_pairs={{0,1},{1,0},{2,3},{3,2},{4,5},{5,4},{6,7},{7,6},{8,9},{9,8},{10,11... | collective-permute-start | bytes 3145736 | tf_op jit(solution)/shard_map/ppermute | solution.py:44
  2.6 84.2 %collective-permute-start.9 = (bf16[2,32,128,128]{3,2,1,0:T(8,128)(2,1)}, bf16[2,32,128,128]{3,2,1,0:T(8,128)(2,1)}, u32[]{:S(2)}, u32[]{:S(2)}) collective-permute-start(bf16[2,32,128,128]{3,2,1,0:T(8,128)(2,1)} %refs_8_.7), channel_id=1, source_target_pairs={{0,1},{1,0},{2,3},{3,2},{4,5},{5,4},{6,7},{7,6},{8,9},{9,8},{10,11... | collective-permute-start | bytes 6291464 | tf_op jit(solution)/shard_map/ppermute | solution.py:44
  3.5 27.6 %collective-permute-start.13 = (bf16[32,64,128]{2,1,0:T(8,128)(2,1)S(1)}, bf16[32,64,128]{2,1,0:T(8,128)(2,1)}, u32[]{:S(2)}, u32[]{:S(2)}) collective-permute-start(bf16[32,64,128]{2,1,0:T(8,128)(2,1)S(1)} %get-tuple-element.45.refs_4_.refs_8_.wave_ref), channel_id=1, source_target_pairs={{0,8},{1,9},{2,10},{3,11},{4,12},{5,13},{6,14},{7,15},{8,0},{9,1},... | collective-permute-start | bytes 1572872 | tf_op jit(solution)/shard_map/ppermute | solution.py:44
  7.6 23.6 %collective-permute-start.21 = (bf16[32,64,128]{2,1,0:T(8,128)(2,1)S(1)}, bf16[32,64,128]{2,1,0:T(8,128)(2,1)}, u32[]{:S(2)}, u32[]{:S(2)}) collective-permute-start(bf16[32,64,128]{2,1,0:T(8,128)(2,1)S(1)} %get-tuple-element.45.refs_4_.refs_8_.wave_ref), channel_id=1, source_target_pairs={{0,2},{1,3},{2,0},{3,1},{4,6},{5,7},{6,4},{7,5},{8,10},{9,11},{10,... | collective-permute-start | bytes 1572872 | tf_op jit(solution)/shard_map/ppermute | solution.py:44
  9.1 1.2 collective-permute-start
  16.4 18.7 %collective-permute-start.2 = (bf16[129,16,128]{2,1,0:T(8,128)(2,1)}, bf16[129,16,128]{2,1,0:T(8,128)(2,1)S(1)}, u32[]{:S(2)}, u32[]{:S(2)}) collective-permute-start(bf16[129,16,128]{2,1,0:T(8,128)(2,1)} %get-tuple-element.24), channel_id=1, source_target_pairs={{0,2},{1,3},{2,0},{3,1},{4,6},{5,7},{6,4},{7,5},{8,10},{9,11},{10,... | collective-permute-start | bytes 1585160 | tf_op jit(solution)/shard_map/ppermute | solution.py:44
  17.0 26.3 %collective-permute-start.10 = (bf16[32,64,128]{2,1,0:T(8,128)(2,1)S(1)}, bf16[32,64,128]{2,1,0:T(8,128)(2,1)S(1)}, u32[]{:S(2)}, u32[]{:S(2)}) collective-permute-start(bf16[32,64,128]{2,1,0:T(8,128)(2,1)S(1)} %get-tuple-element.45.refs_4_.refs_8_.wave_ref), channel_id=1, source_target_pairs={{0,4},{1,5},{2,6},{3,7},{4,0},{5,1},{6,2},{7,3},{8,12},{9,13},{10,... | collective-permute-start | bytes 1572872 | tf_op jit(solution)/shard_map/ppermute | solution.py:44
  31.2 38.8 %collective-permute-start.5 = (bf16[129,16,128]{2,1,0:T(8,128)(2,1)}, bf16[129,16,128]{2,1,0:T(8,128)(2,1)S(1)}, u32[]{:S(2)}, u32[]{:S(2)}) collective-permute-start(bf16[129,16,128]{2,1,0:T(8,128)(2,1)} %get-tuple-element.27), channel_id=1, source_target_pairs={{0,8},{1,9},{2,10},{3,11},{4,12},{5,13},{6,14},{7,15},{8,0},{9,1},... | collective-permute-start | bytes 1585160 | tf_op jit(solution)/shard_map/ppermute | solution.py:44
  31.2 49.3 %collective-permute-start.6 = (bf16[129,16,128]{2,1,0:T(8,128)(2,1)}, bf16[129,16,128]{2,1,0:T(8,128)(2,1)S(1)}, u32[]{:S(2)}, u32[]{:S(2)}) collective-permute-start(bf16[129,16,128]{2,1,0:T(8,128)(2,1)} %get-tuple-element.28), channel_id=1, source_target_pairs={{0,10},{1,11},{2,8},{3,9},{4,14},{5,15},{6,12},{7,13},{8,2},{9,3},... | collective-permute-start | bytes 1585160 | tf_op jit(solution)/shard_map/ppermute | solution.py:44
  35.1 46.9 %collective-permute-start.3 = (bf16[129,16,128]{2,1,0:T(8,128)(2,1)}, bf16[129,16,128]{2,1,0:T(8,128)(2,1)S(1)}, u32[]{:S(2)}, u32[]{:S(2)}) collective-permute-start(bf16[129,16,128]{2,1,0:T(8,128)(2,1)} %get-tuple-element.25), channel_id=1, source_target_pairs={{0,4},{1,5},{2,6},{3,7},{4,0},{5,1},{6,2},{7,3},{8,12},{9,13},{10,... | collective-permute-start | bytes 1585160 | tf_op jit(solution)/shard_map/ppermute | solution.py:44
  43.3 38.7 %copy-start.11 = (bf16[32,64,128]{2,1,0:T(8,128)(2,1)}, bf16[32,64,128]{2,1,0:T(8,128)(2,1)S(1)}, u32[]{:S(2)}) copy-start(bf16[32,64,128]{2,1,0:T(8,128)(2,1)S(1)} %collective-permute-done.10.refs_0_) | copy-start | bytes 1572868
  43.3 42.7 %collective-permute-start.14 = (bf16[32,64,128]{2,1,0:T(8,128)(2,1)}, bf16[32,64,128]{2,1,0:T(8,128)(2,1)S(1)}, u32[]{:S(2)}, u32[]{:S(2)}) collective-permute-start(bf16[32,64,128]{2,1,0:T(8,128)(2,1)} %shard_map.72.refs_6_), channel_id=1, source_target_pairs={{0,4},{1,5},{2,6},{3,7},{4,0},{5,1},{6,2},{7,3},{8,12},{9,13},{10,... | collective-permute-start | bytes 1572872 | tf_op jit(solution)/shard_map/ppermute | solution.py:44
  70.0 18.4 %collective-permute-start.23 = (bf16[32,64,128]{2,1,0:T(8,128)(2,1)}, bf16[32,64,128]{2,1,0:T(8,128)(2,1)}, u32[]{:S(2)}, u32[]{:S(2)}) collective-permute-start(bf16[32,64,128]{2,1,0:T(8,128)(2,1)} %shard_map.72.refs_6_), channel_id=1, source_target_pairs={{0,1},{1,0},{2,3},{3,2},{4,5},{5,4},{6,7},{7,6},{8,9},{9,8},{10,11... | collective-permute-start | bytes 1572872 | tf_op jit(solution)/shard_map/ppermute | solution.py:44
  80.5 15.2 %collective-permute-start.19 = (bf16[32,64,128]{2,1,0:T(8,128)(2,1)}, bf16[32,64,128]{2,1,0:T(8,128)(2,1)}, u32[]{:S(2)}, u32[]{:S(2)}) collective-permute-start(bf16[32,64,128]{2,1,0:T(8,128)(2,1)} %shard_map.72.refs_6_), channel_id=1, source_target_pairs={{0,2},{1,3},{2,0},{3,1},{4,6},{5,7},{6,4},{7,5},{8,10},{9,11},{10,... | collective-permute-start | bytes 1572872 | tf_op jit(solution)/shard_map/ppermute | solution.py:44
  82.0 21.2 %collective-permute-start.22 = (bf16[32,64,128]{2,1,0:T(8,128)(2,1)}, bf16[32,64,128]{2,1,0:T(8,128)(2,1)S(1)}, u32[]{:S(2)}, u32[]{:S(2)}) collective-permute-start(bf16[32,64,128]{2,1,0:T(8,128)(2,1)} %collective-permute-done.21.refs_6_), channel_id=1, source_target_pairs={{0,1},{1,0},{2,3},{3,2},{4,5},{5,4},{6,7},{7,6},{8,9},{9,8},{10,11... | collective-permute-start | bytes 1572872 | tf_op jit(solution)/shard_map/ppermute | solution.py:44
  86.0 26.5 %collective-permute-start.17 = (bf16[32,64,128]{2,1,0:T(8,128)(2,1)S(1)}, bf16[32,64,128]{2,1,0:T(8,128)(2,1)S(1)}, u32[]{:S(2)}, u32[]{:S(2)}) collective-permute-start(bf16[32,64,128]{2,1,0:T(8,128)(2,1)S(1)} %copy-done.12), channel_id=1, source_target_pairs={{0,1},{1,0},{2,3},{3,2},{4,5},{5,4},{6,7},{7,6},{8,9},{9,8},{10,11... | collective-permute-start | bytes 1572872 | tf_op jit(solution)/shard_map/ppermute | solution.py:44
  86.8 26.5 %collective-permute-start.11 = (bf16[32,64,128]{2,1,0:T(8,128)(2,1)S(1)}, bf16[32,64,128]{2,1,0:T(8,128)(2,1)}, u32[]{:S(2)}, u32[]{:S(2)}) collective-permute-start(bf16[32,64,128]{2,1,0:T(8,128)(2,1)S(1)} %copy-done.12), channel_id=1, source_target_pairs={{0,2},{1,3},{2,0},{3,1},{4,6},{5,7},{6,4},{7,5},{8,10},{9,11},{10,... | collective-permute-start | bytes 1572872 | tf_op jit(solution)/shard_map/ppermute | solution.py:44
  88.4 26.2 %collective-permute-start.7 = (bf16[129,16,128]{2,1,0:T(8,128)(2,1)S(1)}, bf16[129,16,128]{2,1,0:T(8,128)(2,1)S(1)}, u32[]{:S(2)}, u32[]{:S(2)}) collective-permute-start(bf16[129,16,128]{2,1,0:T(8,128)(2,1)S(1)} %copy-done.9), channel_id=1, source_target_pairs={{0,12},{1,13},{2,14},{3,15},{4,8},{5,9},{6,10},{7,11},{8,4},{9,5},... | collective-permute-start | bytes 1585160 | tf_op jit(solution)/shard_map/ppermute | solution.py:44
  95.7 8.3 %collective-permute-start.20 = (bf16[32,64,128]{2,1,0:T(8,128)(2,1)}, bf16[32,64,128]{2,1,0:T(8,128)(2,1)S(1)}, u32[]{:S(2)}, u32[]{:S(2)}) collective-permute-start(bf16[32,64,128]{2,1,0:T(8,128)(2,1)} %collective-permute-done.19.refs_4_), channel_id=1, source_target_pairs={{0,1},{1,0},{2,3},{3,2},{4,5},{5,4},{6,7},{7,6},{8,9},{9,8},{10,11... | collective-permute-start | bytes 1572872 | tf_op jit(solution)/shard_map/ppermute | solution.py:44
  103.3 26.1 %collective-permute-start.18 = (bf16[32,64,128]{2,1,0:T(8,128)(2,1)S(1)}, bf16[32,64,128]{2,1,0:T(8,128)(2,1)}, u32[]{:S(2)}, u32[]{:S(2)}) collective-permute-start(bf16[32,64,128]{2,1,0:T(8,128)(2,1)S(1)} %copy-done.14), channel_id=1, source_target_pairs={{0,1},{1,0},{2,3},{3,2},{4,5},{5,4},{6,7},{7,6},{8,9},{9,8},{10,11... | collective-permute-start | bytes 1572872 | tf_op jit(solution)/shard_map/ppermute | solution.py:44
  104.0 25.4 %collective-permute-start.15 = (bf16[32,64,128]{2,1,0:T(8,128)(2,1)S(1)}, bf16[32,64,128]{2,1,0:T(8,128)(2,1)}, u32[]{:S(2)}, u32[]{:S(2)}) collective-permute-start(bf16[32,64,128]{2,1,0:T(8,128)(2,1)S(1)} %copy-done.14), channel_id=1, source_target_pairs={{0,2},{1,3},{2,0},{3,1},{4,6},{5,7},{6,4},{7,5},{8,10},{9,11},{10,... | collective-permute-start | bytes 1572872 | tf_op jit(solution)/shard_map/ppermute | solution.py:44
  113.3 23.6 %collective-permute-start.4 = (bf16[129,16,128]{2,1,0:T(8,128)(2,1)S(1)}, bf16[129,16,128]{2,1,0:T(8,128)(2,1)S(1)}, u32[]{:S(2)}, u32[]{:S(2)}) collective-permute-start(bf16[129,16,128]{2,1,0:T(8,128)(2,1)S(1)} %copy-done.18), channel_id=1, source_target_pairs={{0,6},{1,7},{2,4},{3,5},{4,2},{5,3},{6,0},{7,1},{8,14},{9,15},{10,... | collective-permute-start | bytes 1585160 | tf_op jit(solution)/shard_map/ppermute | solution.py:44
  113.3 31.7 %collective-permute-start.8 = (bf16[129,16,128]{2,1,0:T(8,128)(2,1)S(1)}, bf16[129,16,128]{2,1,0:T(8,128)(2,1)}, u32[]{:S(2)}, u32[]{:S(2)}) collective-permute-start(bf16[129,16,128]{2,1,0:T(8,128)(2,1)S(1)} %copy-done.10), channel_id=1, source_target_pairs={{0,14},{1,15},{2,12},{3,13},{4,10},{5,11},{6,8},{7,9},{8,6},{9,7},... | collective-permute-start | bytes 1585160 | tf_op jit(solution)/shard_map/ppermute | solution.py:44
  114.6 30.5 %collective-permute-start.12 = (bf16[32,64,128]{2,1,0:T(8,128)(2,1)}, bf16[32,64,128]{2,1,0:T(8,128)(2,1)S(1)}, u32[]{:S(2)}, u32[]{:S(2)}) collective-permute-start(bf16[32,64,128]{2,1,0:T(8,128)(2,1)} %collective-permute-done.11.refs_4_), channel_id=1, source_target_pairs={{0,1},{1,0},{2,3},{3,2},{4,5},{5,4},{6,7},{7,6},{8,9},{9,8},{10,11... | collective-permute-start | bytes 1572872 | tf_op jit(solution)/shard_map/ppermute | solution.py:44
  129.3 15.7 %collective-permute-start.16 = (bf16[32,64,128]{2,1,0:T(8,128)(2,1)}, bf16[32,64,128]{2,1,0:T(8,128)(2,1)S(1)}, u32[]{:S(2)}, u32[]{:S(2)}) collective-permute-start(bf16[32,64,128]{2,1,0:T(8,128)(2,1)} %collective-permute-done.15.refs_6_), channel_id=1, source_target_pairs={{0,1},{1,0},{2,3},{3,2},{4,5},{5,4},{6,7},{7,6},{8,9},{9,8},{10,11... | collective-permute-start | bytes 1572872 | tf_op jit(solution)/shard_map/ppermute | solution.py:44
  146.0 22.2 %copy-start.1 = (bf16[32,64,128]{2,1,0:T(8,128)(2,1)S(1)}, bf16[32,64,128]{2,1,0:T(8,128)(2,1)}, u32[]{:S(2)}) copy-start(bf16[32,64,128]{2,1,0:T(8,128)(2,1)} %copy-done) | copy-start | bytes 1572868
  153.5 1.9 collective-permute-start.24
  153.6 3.9 %collective-permute-start.25 = (f32[16,128]{1,0:T(8,128)}, f32[16,128]{1,0:T(8,128)S(1)}, u32[]{:S(2)}, u32[]{:S(2)}) collective-permute-start(f32[16,128]{1,0:T(8,128)} %get-tuple-element.35), channel_id=1, source_target_pairs={{0,2},{1,3},{2,0},{3,1},{4,6},{5,7},{6,4},{7,5},{8,10},{9,11},{10,... | collective-permute-start | bytes 24584 | tf_op jit(solution)/shard_map/ppermute | solution.py:100
  155.2 3.3 %collective-permute-start.26 = (f32[16,128]{1,0:T(8,128)}, f32[16,128]{1,0:T(8,128)S(1)}, u32[]{:S(2)}, u32[]{:S(2)}) collective-permute-start(f32[16,128]{1,0:T(8,128)} %get-tuple-element.35), channel_id=1, source_target_pairs={{0,3},{1,2},{2,1},{3,0},{4,7},{5,6},{6,5},{7,4},{8,11},{9,10},{10,... | collective-permute-start | bytes 24584 | tf_op jit(solution)/shard_map/ppermute | solution.py:100
  159.2 5.2 %collective-permute-start.27 = (f32[16,128]{1,0:T(8,128)S(1)}, f32[16,128]{1,0:T(8,128)S(1)}, u32[]{:S(2)}, u32[]{:S(2)}) collective-permute-start(f32[16,128]{1,0:T(8,128)S(1)} %add_add_fusion.1), channel_id=1, source_target_pairs={{0,4},{1,5},{2,6},{3,7},{4,0},{5,1},{6,2},{7,3},{8,12},{9,13},{10,... | collective-permute-start | bytes 24584 | tf_op jit(solution)/shard_map/ppermute | solution.py:100
  162.1 4.5 %collective-permute-start.28 = (f32[16,128]{1,0:T(8,128)S(1)}, f32[16,128]{1,0:T(8,128)S(1)}, u32[]{:S(2)}, u32[]{:S(2)}) collective-permute-start(f32[16,128]{1,0:T(8,128)S(1)} %add_add_fusion.1), channel_id=1, source_target_pairs={{0,8},{1,9},{2,10},{3,11},{4,12},{5,13},{6,14},{7,15},{8,0},{9,1},... | collective-permute-start | bytes 24584 | tf_op jit(solution)/shard_map/ppermute | solution.py:100
  162.7 5.4 %collective-permute-start.29 = (f32[16,128]{1,0:T(8,128)S(1)}, f32[16,128]{1,0:T(8,128)S(1)}, u32[]{:S(2)}, u32[]{:S(2)}) collective-permute-start(f32[16,128]{1,0:T(8,128)S(1)} %add_add_fusion.1), channel_id=1, source_target_pairs={{0,12},{1,13},{2,14},{3,15},{4,8},{5,9},{6,10},{7,11},{8,4},{9,5},... | collective-permute-start | bytes 24584 | tf_op jit(solution)/shard_map/ppermute | solution.py:100
  170.5 15.2 %copy-start.2 = (bf16[32,64,128]{2,1,0:T(8,128)(2,1)}, bf16[32,64,128]{2,1,0:T(8,128)(2,1)S(1)}, u32[]{:S(2)}) copy-start(bf16[32,64,128]{2,1,0:T(8,128)(2,1)S(1)} %get-tuple-element.36.refs_10_) | copy-start | bytes 1572868
  170.5 12.6 %collective-permute-start.33 = (bf16[32,64,128]{2,1,0:T(8,128)(2,1)S(1)}, bf16[32,64,128]{2,1,0:T(8,128)(2,1)S(1)}, u32[]{:S(2)}, u32[]{:S(2)}) collective-permute-start(bf16[32,64,128]{2,1,0:T(8,128)(2,1)S(1)} %get-tuple-element.36.refs_10_), channel_id=1, source_target_pairs={{0,2},{1,5},{2,6},{3,1},{4,0},{5,9},{6,10},{7,3},{8,4},{9,13},{10,... | collective-permute-start | bytes 1572872 | tf_op jit(solution)/shard_map/ppermute | solution.py:44
  171.5 11.6 %collective-permute-start.30 = (bf16[32,64,128]{2,1,0:T(8,128)(2,1)S(1)}, bf16[32,64,128]{2,1,0:T(8,128)(2,1)S(1)}, u32[]{:S(2)}, u32[]{:S(2)}) collective-permute-start(bf16[32,64,128]{2,1,0:T(8,128)(2,1)S(1)} %get-tuple-element.36.refs_10_), channel_id=1, source_target_pairs={{0,4},{1,3},{2,0},{3,7},{4,8},{5,1},{6,2},{7,11},{8,12},{9,5},{10,... | collective-permute-start | bytes 1572872 | tf_op jit(solution)/shard_map/ppermute | solution.py:44
  172.5 13.1 %collective-permute-start.32 = (bf16[32,64,128]{2,1,0:T(8,128)(2,1)S(1)}, bf16[32,64,128]{2,1,0:T(8,128)(2,1)S(1)}, u32[]{:S(2)}, u32[]{:S(2)}) collective-permute-start(bf16[32,64,128]{2,1,0:T(8,128)(2,1)S(1)} %get-tuple-element.36.refs_10_), channel_id=1, source_target_pairs={{0,1},{1,0},{2,3},{3,2},{4,5},{5,4},{6,7},{7,6},{8,9},{9,8},{10,11... | collective-permute-start | bytes 1572872 | tf_op jit(solution)/shard_map/ppermute | solution.py:44
  183.1 2.6 %collective-permute-start.34 = (bf16[32,64,128]{2,1,0:T(8,128)(2,1)S(1)}, bf16[32,64,128]{2,1,0:T(8,128)(2,1)S(1)}, u32[]{:S(2)}, u32[]{:S(2)}) collective-permute-start(bf16[32,64,128]{2,1,0:T(8,128)(2,1)S(1)} %collective-permute-done.33.refs_14_), channel_id=1, source_target_pairs={{0,1},{1,0},{2,3},{3,2},{4,5},{5,4},{6,7},{7,6},{8,9},{9,8},{10,11... | collective-permute-start | bytes 1572872 | tf_op jit(solution)/shard_map/ppermute | solution.py:44
  183.1 2.6 %collective-permute-start.35 = (bf16[32,64,128]{2,1,0:T(8,128)(2,1)S(1)}, bf16[32,64,128]{2,1,0:T(8,128)(2,1)S(1)}, u32[]{:S(2)}, u32[]{:S(2)}) collective-permute-start(bf16[32,64,128]{2,1,0:T(8,128)(2,1)S(1)} %collective-permute-done.30.refs_12_), channel_id=1, source_target_pairs={{0,1},{1,0},{2,3},{3,2},{4,5},{5,4},{6,7},{7,6},{8,9},{9,8},{10,11... | collective-permute-start | bytes 1572872 | tf_op jit(solution)/shard_map/ppermute | solution.py:44
  183.6 14.4 %collective-permute-start.31 = (bf16[32,64,128]{2,1,0:T(8,128)(2,1)S(1)}, bf16[32,64,128]{2,1,0:T(8,128)(2,1)}, u32[]{:S(2)}, u32[]{:S(2)}) collective-permute-start(bf16[32,64,128]{2,1,0:T(8,128)(2,1)S(1)} %collective-permute-done.30.refs_12_), channel_id=1, source_target_pairs={{0,4},{1,3},{2,0},{3,7},{4,8},{5,1},{6,2},{7,11},{8,12},{9,5},{10,... | collective-permute-start | bytes 1572872 | tf_op jit(solution)/shard_map/ppermute | solution.py:44
  184.4 13.6 %collective-permute-start.37 = (bf16[32,64,128]{2,1,0:T(8,128)(2,1)S(1)}, bf16[32,64,128]{2,1,0:T(8,128)(2,1)S(1)}, u32[]{:S(2)}, u32[]{:S(2)}) collective-permute-start(bf16[32,64,128]{2,1,0:T(8,128)(2,1)S(1)} %collective-permute-done.33.refs_14_), channel_id=1, source_target_pairs={{0,2},{1,5},{2,6},{3,1},{4,0},{5,9},{6,10},{7,3},{8,4},{9,13},{10,... | collective-permute-start | bytes 1572872 | tf_op jit(solution)/shard_map/ppermute | solution.py:44
  198.0 2.6 %collective-permute-start.39 = (bf16[32,64,128]{2,1,0:T(8,128)(2,1)}, bf16[32,64,128]{2,1,0:T(8,128)(2,1)S(1)}, u32[]{:S(2)}, u32[]{:S(2)}) collective-permute-start(bf16[32,64,128]{2,1,0:T(8,128)(2,1)} %shard_map.80.refs_10_), channel_id=1, source_target_pairs={{0,1},{1,0},{2,3},{3,2},{4,5},{5,4},{6,7},{7,6},{8,9},{9,8},{10,11... | collective-permute-start | bytes 1572872 | tf_op jit(solution)/shard_map/ppermute | solution.py:44
  198.0 2.6 %collective-permute-start.38 = (bf16[32,64,128]{2,1,0:T(8,128)(2,1)S(1)}, bf16[32,64,128]{2,1,0:T(8,128)(2,1)S(1)}, u32[]{:S(2)}, u32[]{:S(2)}) collective-permute-start(bf16[32,64,128]{2,1,0:T(8,128)(2,1)S(1)} %collective-permute-done.37.refs_12_), channel_id=1, source_target_pairs={{0,1},{1,0},{2,3},{3,2},{4,5},{5,4},{6,7},{7,6},{8,9},{9,8},{10,11... | collective-permute-start | bytes 1572872 | tf_op jit(solution)/shard_map/ppermute | solution.py:44
  198.5 14.6 %collective-permute-start.36 = (bf16[32,64,128]{2,1,0:T(8,128)(2,1)}, bf16[32,64,128]{2,1,0:T(8,128)(2,1)}, u32[]{:S(2)}, u32[]{:S(2)}) collective-permute-start(bf16[32,64,128]{2,1,0:T(8,128)(2,1)} %shard_map.80.refs_10_), channel_id=1, source_target_pairs={{0,4},{1,3},{2,0},{3,7},{4,8},{5,1},{6,2},{7,11},{8,12},{9,5},{10,... | collective-permute-start | bytes 1572872 | tf_op jit(solution)/shard_map/ppermute | solution.py:44
  199.7 13.4 %collective-permute-start.41 = (bf16[32,64,128]{2,1,0:T(8,128)(2,1)S(1)}, bf16[32,64,128]{2,1,0:T(8,128)(2,1)S(1)}, u32[]{:S(2)}, u32[]{:S(2)}) collective-permute-start(bf16[32,64,128]{2,1,0:T(8,128)(2,1)S(1)} %collective-permute-done.37.refs_12_), channel_id=1, source_target_pairs={{0,2},{1,5},{2,6},{3,1},{4,0},{5,9},{6,10},{7,3},{8,4},{9,13},{10,... | collective-permute-start | bytes 1572872 | tf_op jit(solution)/shard_map/ppermute | solution.py:44
  213.1 2.1 collective-permute-start.43
  213.1 2.6 %collective-permute-start.42 = (bf16[32,64,128]{2,1,0:T(8,128)(2,1)S(1)}, bf16[32,64,128]{2,1,0:T(8,128)(2,1)S(1)}, u32[]{:S(2)}, u32[]{:S(2)}) collective-permute-start(bf16[32,64,128]{2,1,0:T(8,128)(2,1)S(1)} %collective-permute-done.41.refs_12_), channel_id=1, source_target_pairs={{0,1},{1,0},{2,3},{3,2},{4,5},{5,4},{6,7},{7,6},{8,9},{9,8},{10,11... | collective-permute-start | bytes 1572872 | tf_op jit(solution)/shard_map/ppermute | solution.py:44
  213.6 10.3 %collective-permute-start.40 = (bf16[32,64,128]{2,1,0:T(8,128)(2,1)}, bf16[32,64,128]{2,1,0:T(8,128)(2,1)S(1)}, u32[]{:S(2)}, u32[]{:S(2)}) collective-permute-start(bf16[32,64,128]{2,1,0:T(8,128)(2,1)} %shard_map.82.refs_10_), channel_id=1, source_target_pairs={{0,4},{1,3},{2,0},{3,7},{4,8},{5,1},{6,2},{7,11},{8,12},{9,5},{10,... | collective-permute-start | bytes 1572872 | tf_op jit(solution)/shard_map/ppermute | solution.py:44
  224.7 2.1 collective-permute-start.44
  (37 other events, 132.9 us)

commit v17 on v16

--- a/solution.py
+++ b/solution.py
@@ -10,8 +10,8 @@
 BOTH = ("sec", "term")
 VMEM_LIMIT = 60 * 2**20
 PART = 16
-ORDER = [0, 4, 5, 1, 2, 6, 3, 7]
-WAITS = {4: 1, 2: 5, 6: 2}
+ORDER = [0, 1, 4, 2, 5, 6, 3, 7]
+WAITS = {4: 1, 2: 4, 6: 2}
 PIECE_WAITS = {6: 4, 7: 5}
 RING_BYTES = 24 * 2**20
 

time: 234 us -> 235 us (level)
  starting transfers between devices: 38.5 us -> 44.2 us
  waiting for transfers between devices: 115 us -> 111 us
    ppermute x39, waiting for transfers between devices: 108 us -> 103 us  [permute(): return lax.ppermute(value, BOTH, pairs)]
    ppermute x39, starting transfers between devices: 31.3 us -> 36.9 us  [permute(): return lax.ppermute(value, BOTH, pairs)]
  transfers between devices with their start and end apart: 45 -> 45, of which waited for: 21 -> 18; matrix products, arithmetic and copies ran while one was open for 1% -> 1% of each run, Pallas kernels for 22% -> 22%
where the time goes in v17:
time: 235 us; the launch traced here: 234 us
  waiting for transfers between devices  111 us (47%)
  Pallas kernels  64.8 us (28%)
  starting transfers between devices  44.2 us (19%)
  local copies, waits for them, and re-layouts  11.8 us (5%)
    ppermute x39, waiting for transfers between devices, permute(): return lax.ppermute(value, BOTH, pairs)  103 us
    pallas_call x8, Pallas kernels, apply_group(): pl.pallas_call(functools.partial(apply_kernel, sources, choices, chosen,...  58.3 us
    ppermute x39, starting transfers between devices, permute(): return lax.ppermute(value, BOTH, pairs)  36.9 us
    unnamed x80, local copies, waits for them, and re-layouts  8.9 us
    ppermute x6, waiting for transfers between devices, spread(): lax.ppermute(value, BOTH, [(d, d ^ m) for d in range(devices)])  7.88 us
    ppermute x6, starting transfers between devices, spread(): lax.ppermute(value, BOTH, [(d, d ^ m) for d in range(devices)])  7.28 us
    pallas_call x1, Pallas kernels, pack(): pl.pallas_call(functools.partial(pack_kernel, order, capacity, blocks, te...  5.45 us
  transfers between devices with their start and end apart: 45, of which 18 were waited for; matrix products, arithmetic and copies ran while one was open for 1% of the time, Pallas kernels for 22%

profile of v17, /device:TPU:0, one launch (start us, length us, event | category | flops | bytes accessed | tf_op | source)
XLA Modules:
  0.0 234.2 jit_solution(116758431340865836)
XLA Ops:
  0.6 1.4 constant_dynamic-slice_fusion.2
  2.7 0.9 constant_dynamic-slice_fusion
  3.5 2.9 %collective-permute-start.22 = (bf16[32,64,128]{2,1,0:T(8,128)(2,1)S(1)}, bf16[32,64,128]{2,1,0:T(8,128)(2,1)}, u32[]{:S(2)}, u32[]{:S(2)}) collective-permute-start(bf16[32,64,128]{2,1,0:T(8,128)(2,1)S(1)} %get-tuple-element.45.refs_4_.refs_8_.wave_ref), channel_id=1, source_target_pairs={{0,2},{1,3},{2,0},{3,1},{4,6},{5,7},{6,4},{7,5},{8,10},{9,11},{10,... | collective-permute-start | bytes 1572872 | tf_op jit(solution)/shard_map/ppermute | solution.py:44
  6.5 2.6 %collective-permute-start.13 = (bf16[32,64,128]{2,1,0:T(8,128)(2,1)S(1)}, bf16[32,64,128]{2,1,0:T(8,128)(2,1)S(1)}, u32[]{:S(2)}, u32[]{:S(2)}) collective-permute-start(bf16[32,64,128]{2,1,0:T(8,128)(2,1)S(1)} %get-tuple-element.45.refs_4_.refs_8_.wave_ref), channel_id=1, source_target_pairs={{0,8},{1,9},{2,10},{3,11},{4,12},{5,13},{6,14},{7,15},{8,0},{9,1},... | collective-permute-start | bytes 1572872 | tf_op jit(solution)/shard_map/ppermute | solution.py:44
  10.9 5.4 %shard_map.68 = (bf16[129,16,128]{2,1,0:T(8,128)(2,1)}, bf16[129,16,128]{2,1,0:T(8,128)(2,1)}, bf16[129,16,128]{2,1,0:T(8,128)(2,1)}, bf16[129,16,128]{2,1,0:T(8...) custom-call(s32[2]{0:T(128)} %pad_add_fusion.1.ids_ref, ...), custom_call_target="tpu_custom_call" | custom-call | flops 5750000128 | tf_op jit(solution)/shard_map/pallas_call | solution.py:167
  16.9 2.2 collective-permute-start.5
  19.1 1.9 collective-permute-start.10
  21.0 23.7 %collective-permute-done.13.refs_0_ = bf16[32,64,128]{2,1,0:T(8,128)(2,1)S(1)} collective-permute-done((bf16[32,64,128]{2,1,0:T(8,128)(2,1)S(1)}, bf16[32,64,128]{2,1,0:T(8,128)(2,1)S(1)}, u32[]{:S(2)}, u32[]{:S(2)}) %collective-permute-start.13) | collective-permute-done | bytes 524320 | tf_op jit(solution)/shard_map/ppermute | solution.py:44
  45.7 3.0 %collective-permute-start.3 = (bf16[129,16,128]{2,1,0:T(8,128)(2,1)}, bf16[129,16,128]{2,1,0:T(8,128)(2,1)S(1)}, u32[]{:S(2)}, u32[]{:S(2)}) collective-permute-start(bf16[129,16,128]{2,1,0:T(8,128)(2,1)} %get-tuple-element.25), channel_id=1, source_target_pairs={{0,4},{1,5},{2,6},{3,7},{4,0},{5,1},{6,2},{7,3},{8,12},{9,13},{10,... | collective-permute-start | bytes 1585160 | tf_op jit(solution)/shard_map/ppermute | solution.py:44
  48.7 18.7 %collective-permute-done.5.refs_1_.refs_0_.refs_4_ = bf16[129,16,128]{2,1,0:T(8,128)(2,1)S(1)} collective-permute-done((bf16[129,16,128]{2,1,0:T(8,128)(2,1)}, bf16[129,16,128]{2,1,0:T(8,128)(2,1)S(1)}, u32[]{:S(2)}, u32[]{:S(2)}) %collective-permute-start.5) | collective-permute-done | bytes 528416 | tf_op jit(solution)/shard_map/ppermute | solution.py:44
  67.5 0.8 copy-done.4
  68.3 9.3 %collective-permute-done.6.refs_1_.refs_0_.refs_5_ = bf16[129,16,128]{2,1,0:T(8,128)(2,1)S(1)} collective-permute-done((bf16[129,16,128]{2,1,0:T(8,128)(2,1)}, bf16[129,16,128]{2,1,0:T(8,128)(2,1)S(1)}, u32[]{:S(2)}, u32[]{:S(2)}) %collective-permute-start.6) | collective-permute-done | bytes 528416 | tf_op jit(solution)/shard_map/ppermute | solution.py:44
  77.5 0.8 collective-permute-start.14
  78.4 1.5 collective-permute-start.17
  79.9 7.7 %shard_map.74 = (f32[33,64,128]{2,1,0:T(8,128)}, f32[8,128]{1,0:T(8,128)}) custom-call(s32[10]{0:T(128)} %stack.56.ids_ref, bf16[129,16,128]{2,1,0:T(8,128)(2,1)} %get-tuple-element.23.refs_0_, bf16[129,16,128]{2,1,0:T(8,128)(2,1)} %copy-done.6, bf16[2,32,128,128]{3,2,1,0:T(8,128)(2,1)} %refs_8_.7, ...), custom_call_target="tpu_custom_call" | custom-call | flops 8165000192 | tf_op jit(solution)/shard_map/pallas_call | solution.py:391
  87.9 2.8 %collective-permute-done.14.refs_0_ = bf16[32,64,128]{2,1,0:T(8,128)(2,1)S(1)} collective-permute-done((bf16[32,64,128]{2,1,0:T(8,128)(2,1)S(1)}, bf16[32,64,128]{2,1,0:T(8,128)(2,1)S(1)}, u32[]{:S(2)}, u32[]{:S(2)}) %collective-permute-start.14) | collective-permute-done | bytes 524320 | tf_op jit(solution)/shard_map/ppermute | solution.py:44
  90.6 5.4 %collective-permute-start.7 = (bf16[129,16,128]{2,1,0:T(8,128)(2,1)S(1)}, bf16[129,16,128]{2,1,0:T(8,128)(2,1)}, u32[]{:S(2)}, u32[]{:S(2)}) collective-permute-start(bf16[129,16,128]{2,1,0:T(8,128)(2,1)S(1)} %copy-done.9), channel_id=1, source_target_pairs={{0,12},{1,13},{2,14},{3,15},{4,8},{5,9},{6,10},{7,11},{8,4},{9,5},... | collective-permute-start | bytes 1585160 | tf_op jit(solution)/shard_map/ppermute | solution.py:44
  96.2 1.5 collective-permute-start.15
  97.8 7.6 %shard_map.75 = (f32[33,64,128]{2,1,0:T(8,128)}, f32[8,128]{1,0:T(8,128)}) custom-call(s32[10]{0:T(128)} %stack.56.ids_ref, bf16[129,16,128]{2,1,0:T(8,128)(2,1)} %copy-done.4, bf16[129,16,128]{2,1,0:T(8,128)(2,1)} %copy-done.10, bf16[2,32,128,128]{3,2,1,0:T(8,128)(2,1)} %refs_8_.7, bf16[2,32,128,128]{3,2,1,0:T(8,128)(2,1)} %collective-permute-done.9.refs_3_.refs_9_, ...), custom_call_target="tpu_custom_call" | custom-call | flops 8165000192 | tf_op jit(solution)/shard_map/pallas_call | solution.py:391
  105.5 2.5 %collective-permute-done.7.refs_1_.refs_6_ = bf16[129,16,128]{2,1,0:T(8,128)(2,1)} collective-permute-done((bf16[129,16,128]{2,1,0:T(8,128)(2,1)S(1)}, bf16[129,16,128]{2,1,0:T(8,128)(2,1)}, u32[]{:S(2)}, u32[]{:S(2)}) %collective-permute-start.7) | collective-permute-done | bytes 528416 | tf_op jit(solution)/shard_map/ppermute | solution.py:44
  108.0 5.7 %collective-permute-start.8 = (bf16[129,16,128]{2,1,0:T(8,128)(2,1)S(1)}, bf16[129,16,128]{2,1,0:T(8,128)(2,1)S(1)}, u32[]{:S(2)}, u32[]{:S(2)}) collective-permute-start(bf16[129,16,128]{2,1,0:T(8,128)(2,1)S(1)} %copy-done.8), channel_id=1, source_target_pairs={{0,14},{1,15},{2,12},{3,13},{4,10},{5,11},{6,8},{7,9},{8,6},{9,7},... | collective-permute-start | bytes 1585160 | tf_op jit(solution)/shard_map/ppermute | solution.py:44
  113.7 23.4 %collective-permute-done.15.refs_6_ = bf16[32,64,128]{2,1,0:T(8,128)(2,1)S(1)} collective-permute-done((bf16[32,64,128]{2,1,0:T(8,128)(2,1)}, bf16[32,64,128]{2,1,0:T(8,128)(2,1)S(1)}, u32[]{:S(2)}, u32[]{:S(2)}) %collective-permute-start.15) | collective-permute-done | bytes 524320 | tf_op jit(solution)/shard_map/ppermute | solution.py:44
  137.1 7.6 %shard_map.76 = (f32[33,64,128]{2,1,0:T(8,128)}, f32[8,128]{1,0:T(8,128)}) custom-call(s32[10]{0:T(128)} %stack.56.ids_ref, bf16[129,16,128]{2,1,0:T(8,128)(2,1)} %copy-done.7, bf16[129,16,128]{2,1,0:T(8,128)(2,1)} %collective-permute-done.7.refs_1_.refs_6_, bf16[2,32,128,128]{3,2,1,0:T(8,128)(2,1)} %refs_8_.7, ...), custom_call_target="tpu_custom_call" | custom-call | flops 8165000192 | tf_op jit(solution)/shard_map/pallas_call | solution.py:391
  144.8 0.9 copy-done.30
  146.0 7.6 %shard_map.77 = (f32[32,64,128]{2,1,0:T(8,128)}, f32[16,128]{1,0:T(8,128)}) custom-call(s32[10]{0:T(128)} %stack.56.ids_ref, bf16[129,16,128]{2,1,0:T(8,128)(2,1)} %copy-done.20, bf16[129,16,128]{2,1,0:T(8,128)(2,1)} %copy-done.21, bf16[2,32,128,128]{3,2,1,0:T(8,128)(2,1)} %refs_8_.7, bf16[2,32,128,128]{3,2,1,0:T(8,128)(2,1)} %collective-permute-done.9.refs_3_.refs_9_, ...), custom_call_target="tpu_custom_call" | custom-call | flops 8165000192 | tf_op jit(solution)/shard_map/pallas_call | solution.py:391
  154.2 1.4 collective-permute-start.26
  155.7 2.4 %collective-permute-done.25 = f32[16,128]{1,0:T(8,128)S(1)} collective-permute-done((f32[16,128]{1,0:T(8,128)}, f32[16,128]{1,0:T(8,128)S(1)}, u32[]{:S(2)}, u32[]{:S(2)}) %collective-permute-start.25) | collective-permute-done | bytes 8224 | tf_op jit(solution)/shard_map/ppermute | solution.py:100
  158.1 0.7 add_add_fusion.1
  158.8 5.2 %collective-permute-start.28 = (f32[16,128]{1,0:T(8,128)S(1)}, f32[16,128]{1,0:T(8,128)S(1)}, u32[]{:S(2)}, u32[]{:S(2)}) collective-permute-start(f32[16,128]{1,0:T(8,128)S(1)} %add_add_fusion.1), channel_id=1, source_target_pairs={{0,8},{1,9},{2,10},{3,11},{4,12},{5,13},{6,14},{7,15},{8,0},{9,1},... | collective-permute-start | bytes 24584 | tf_op jit(solution)/shard_map/ppermute | solution.py:100
  164.0 1.6 collective-permute-done.28
  165.7 3.8 %collective-permute-done.29 = f32[16,128]{1,0:T(8,128)S(1)} collective-permute-done((f32[16,128]{1,0:T(8,128)S(1)}, f32[16,128]{1,0:T(8,128)S(1)}, u32[]{:S(2)}, u32[]{:S(2)}) %collective-permute-start.29) | collective-permute-done | bytes 8224 | tf_op jit(solution)/shard_map/ppermute | solution.py:100
  169.5 1.2 copy-done.3
  170.7 1.1 shard_map.78
  172.3 1.5 collective-permute-start.30
  173.8 10.2 %collective-permute-done.33.refs_14_ = bf16[32,64,128]{2,1,0:T(8,128)(2,1)S(1)} collective-permute-done((bf16[32,64,128]{2,1,0:T(8,128)(2,1)S(1)}, bf16[32,64,128]{2,1,0:T(8,128)(2,1)S(1)}, u32[]{:S(2)}, u32[]{:S(2)}) %collective-permute-start.33) | collective-permute-done | bytes 524320 | tf_op jit(solution)/shard_map/ppermute | solution.py:44
  184.5 2.0 collective-permute-start.37
  187.5 0.8 copy-done.34
  188.3 8.2 %shard_map.79 = (f32[33,64,128]{2,1,0:T(8,128)}, f32[8,128]{1,0:T(8,128)}) custom-call(s32[10]{0:T(128)} %stack.56.ids_ref, bf16[129,16,128]{2,1,0:T(8,128)(2,1)} %get-tuple-element.23.refs_0_, bf16[129,16,128]{2,1,0:T(8,128)(2,1)} %copy-done.6, bf16[129,16,128]{2,1,0:T(8,128)(2,1)} %copy-done.10, bf16[129,16,128]{2,1,0:T(8,128)(2,1)} %copy-done.20, ...), custom_call_target="tpu_custom_call" | custom-call | flops 10234999808 | tf_op jit(solution)/shard_map/pallas_call | solution.py:391
  196.6 2.3 collective-permute-done.31.refs_0_
  199.4 2.0 collective-permute-start.41
  202.4 7.0 %shard_map.81 = (f32[33,64,128]{2,1,0:T(8,128)}, f32[8,128]{1,0:T(8,128)}) custom-call(s32[10]{0:T(128)} %stack.56.ids_ref, bf16[129,16,128]{2,1,0:T(8,128)(2,1)} %get-tuple-element.23.refs_0_, bf16[129,16,128]{2,1,0:T(8,128)(2,1)} %copy-done.6, bf16[129,16,128]{2,1,0:T(8,128)(2,1)} %copy-done.10, bf16[129,16,128]{2,1,0:T(8,128)(2,1)} %copy-done.20, ...), custom_call_target="tpu_custom_call" | custom-call | flops 8165000192 | tf_op jit(solution)/shard_map/pallas_call | solution.py:391
  209.4 4.9 %collective-permute-done.36.refs_0_ = bf16[32,64,128]{2,1,0:T(8,128)(2,1)} collective-permute-done((bf16[32,64,128]{2,1,0:T(8,128)(2,1)}, bf16[32,64,128]{2,1,0:T(8,128)(2,1)}, u32[]{:S(2)}, u32[]{:S(2)}) %collective-permute-start.36) | collective-permute-done | bytes 524320 | tf_op jit(solution)/shard_map/ppermute | solution.py:44
  214.8 1.6 collective-permute-done.43.refs_13_
  217.7 7.5 %shard_map.83 = (f32[33,64,128]{2,1,0:T(8,128)}, f32[8,128]{1,0:T(8,128)}) custom-call(s32[10]{0:T(128)} %stack.56.ids_ref, bf16[129,16,128]{2,1,0:T(8,128)(2,1)} %get-tuple-element.23.refs_0_, bf16[129,16,128]{2,1,0:T(8,128)(2,1)} %copy-done.6, bf16[129,16,128]{2,1,0:T(8,128)(2,1)} %copy-done.10, bf16[129,16,128]{2,1,0:T(8,128)(2,1)} %copy-done.20, ...), custom_call_target="tpu_custom_call" | custom-call | flops 8165000192 | tf_op jit(solution)/shard_map/pallas_call | solution.py:391
  225.2 0.8 copy-done.36
  226.0 2.1 collective-permute-done.44.refs_11_
  228.2 0.8 copy-done.38
  229.0 5.0 %shard_map.85 = bf16[32,64,128]{2,1,0:T(8,128)(2,1)} custom-call(s32[10]{0:T(128)} %stack.56.ids_ref, bf16[129,16,128]{2,1,0:T(8,128)(2,1)} %get-tuple-element.23.refs_0_, bf16[129,16,128]{2,1,0:T(8,128)(2,1)} %copy-done.6, bf16[129,16,128]{2,1,0:T(8,128)(2,1)} %copy-done.10, bf16[129,16,128]{2,1,0:T(8,128)(2,1)} %copy-done.20, ...), custom_call_target="tpu_custom_call" | custom-call | flops 6095000064 | tf_op jit(solution)/shard_map/pallas_call | solution.py:391
  (147 shorter events, 10.7 us)
Async XLA Ops:
  2.1 8.3 %collective-permute-start.1 = (bf16[2,32,64,128]{3,2,1,0:T(8,128)(2,1)S(1)}, bf16[2,32,64,128]{3,2,1,0:T(8,128)(2,1)}, u32[]{:S(2)}, u32[]{:S(2)}) collective-permute-start(bf16[2,32,64,128]{3,2,1,0:T(8,128)(2,1)S(1)} %constant_dynamic-slice_fusion.2), channel_id=1, source_target_pairs={{0,1},{1,0},{2,3},{3,2},{4,5},{5,4},{6,7},{7,6},{8,9},{9,8},{10,11... | collective-permute-start | bytes 3145736 | tf_op jit(solution)/shard_map/ppermute | solution.py:44
  2.6 77.3 %collective-permute-start.9 = (bf16[2,32,128,128]{3,2,1,0:T(8,128)(2,1)}, bf16[2,32,128,128]{3,2,1,0:T(8,128)(2,1)}, u32[]{:S(2)}, u32[]{:S(2)}) collective-permute-start(bf16[2,32,128,128]{3,2,1,0:T(8,128)(2,1)} %refs_8_.7), channel_id=1, source_target_pairs={{0,1},{1,0},{2,3},{3,2},{4,5},{5,4},{6,7},{7,6},{8,9},{9,8},{10,11... | collective-permute-start | bytes 6291464 | tf_op jit(solution)/shard_map/ppermute | solution.py:44
  3.5 15.6 %copy-start = (bf16[32,64,128]{2,1,0:T(8,128)(2,1)}, bf16[32,64,128]{2,1,0:T(8,128)(2,1)S(1)}, u32[]{:S(2)}) copy-start(bf16[32,64,128]{2,1,0:T(8,128)(2,1)S(1)} %get-tuple-element.45.refs_4_.refs_8_.wave_ref) | copy-start | bytes 1572868
  3.5 15.6 %collective-permute-start.22 = (bf16[32,64,128]{2,1,0:T(8,128)(2,1)S(1)}, bf16[32,64,128]{2,1,0:T(8,128)(2,1)}, u32[]{:S(2)}, u32[]{:S(2)}) collective-permute-start(bf16[32,64,128]{2,1,0:T(8,128)(2,1)S(1)} %get-tuple-element.45.refs_4_.refs_8_.wave_ref), channel_id=1, source_target_pairs={{0,2},{1,3},{2,0},{3,1},{4,6},{5,7},{6,4},{7,5},{8,10},{9,11},{10,... | collective-permute-start | bytes 1572872 | tf_op jit(solution)/shard_map/ppermute | solution.py:44
  6.5 38.2 %collective-permute-start.13 = (bf16[32,64,128]{2,1,0:T(8,128)(2,1)S(1)}, bf16[32,64,128]{2,1,0:T(8,128)(2,1)S(1)}, u32[]{:S(2)}, u32[]{:S(2)}) collective-permute-start(bf16[32,64,128]{2,1,0:T(8,128)(2,1)S(1)} %get-tuple-element.45.refs_4_.refs_8_.wave_ref), channel_id=1, source_target_pairs={{0,8},{1,9},{2,10},{3,11},{4,12},{5,13},{6,14},{7,15},{8,0},{9,1},... | collective-permute-start | bytes 1572872 | tf_op jit(solution)/shard_map/ppermute | solution.py:44
  9.1 1.2 collective-permute-start
  16.4 28.3 %collective-permute-start.2 = (bf16[129,16,128]{2,1,0:T(8,128)(2,1)}, bf16[129,16,128]{2,1,0:T(8,128)(2,1)S(1)}, u32[]{:S(2)}, u32[]{:S(2)}) collective-permute-start(bf16[129,16,128]{2,1,0:T(8,128)(2,1)} %get-tuple-element.24), channel_id=1, source_target_pairs={{0,2},{1,3},{2,0},{3,1},{4,6},{5,7},{6,4},{7,5},{8,10},{9,11},{10,... | collective-permute-start | bytes 1585160 | tf_op jit(solution)/shard_map/ppermute | solution.py:44
  16.9 50.5 %collective-permute-start.5 = (bf16[129,16,128]{2,1,0:T(8,128)(2,1)}, bf16[129,16,128]{2,1,0:T(8,128)(2,1)S(1)}, u32[]{:S(2)}, u32[]{:S(2)}) collective-permute-start(bf16[129,16,128]{2,1,0:T(8,128)(2,1)} %get-tuple-element.27), channel_id=1, source_target_pairs={{0,8},{1,9},{2,10},{3,11},{4,12},{5,13},{6,14},{7,15},{8,0},{9,1},... | collective-permute-start | bytes 1585160 | tf_op jit(solution)/shard_map/ppermute | solution.py:44
  19.1 26.6 %collective-permute-start.10 = (bf16[32,64,128]{2,1,0:T(8,128)(2,1)S(1)}, bf16[32,64,128]{2,1,0:T(8,128)(2,1)S(1)}, u32[]{:S(2)}, u32[]{:S(2)}) collective-permute-start(bf16[32,64,128]{2,1,0:T(8,128)(2,1)S(1)} %get-tuple-element.45.refs_4_.refs_8_.wave_ref), channel_id=1, source_target_pairs={{0,4},{1,5},{2,6},{3,7},{4,0},{5,1},{6,2},{7,3},{8,12},{9,13},{10,... | collective-permute-start | bytes 1572872 | tf_op jit(solution)/shard_map/ppermute | solution.py:44
  44.7 32.8 %collective-permute-start.6 = (bf16[129,16,128]{2,1,0:T(8,128)(2,1)}, bf16[129,16,128]{2,1,0:T(8,128)(2,1)S(1)}, u32[]{:S(2)}, u32[]{:S(2)}) collective-permute-start(bf16[129,16,128]{2,1,0:T(8,128)(2,1)} %get-tuple-element.28), channel_id=1, source_target_pairs={{0,10},{1,11},{2,8},{3,9},{4,14},{5,15},{6,12},{7,13},{8,2},{9,3},... | collective-permute-start | bytes 1585160 | tf_op jit(solution)/shard_map/ppermute | solution.py:44
  44.7 33.7 %collective-permute-start.23 = (bf16[32,64,128]{2,1,0:T(8,128)(2,1)}, bf16[32,64,128]{2,1,0:T(8,128)(2,1)}, u32[]{:S(2)}, u32[]{:S(2)}) collective-permute-start(bf16[32,64,128]{2,1,0:T(8,128)(2,1)} %collective-permute-done.22.refs_6_), channel_id=1, source_target_pairs={{0,1},{1,0},{2,3},{3,2},{4,5},{5,4},{6,7},{7,6},{8,9},{9,8},{10,11... | collective-permute-start | bytes 1572872 | tf_op jit(solution)/shard_map/ppermute | solution.py:44
  45.7 21.7 %copy-start.13 = (bf16[32,64,128]{2,1,0:T(8,128)(2,1)}, bf16[32,64,128]{2,1,0:T(8,128)(2,1)S(1)}, u32[]{:S(2)}) copy-start(bf16[32,64,128]{2,1,0:T(8,128)(2,1)S(1)} %collective-permute-done.10.refs_0_) | copy-start | bytes 1572868
  45.7 41.9 %collective-permute-start.3 = (bf16[129,16,128]{2,1,0:T(8,128)(2,1)}, bf16[129,16,128]{2,1,0:T(8,128)(2,1)S(1)}, u32[]{:S(2)}, u32[]{:S(2)}) collective-permute-start(bf16[129,16,128]{2,1,0:T(8,128)(2,1)} %get-tuple-element.25), channel_id=1, source_target_pairs={{0,4},{1,5},{2,6},{3,7},{4,0},{5,1},{6,2},{7,3},{8,12},{9,13},{10,... | collective-permute-start | bytes 1585160 | tf_op jit(solution)/shard_map/ppermute | solution.py:44
  67.5 28.6 %collective-permute-start.20 = (bf16[32,64,128]{2,1,0:T(8,128)(2,1)}, bf16[32,64,128]{2,1,0:T(8,128)(2,1)}, u32[]{:S(2)}, u32[]{:S(2)}) collective-permute-start(bf16[32,64,128]{2,1,0:T(8,128)(2,1)} %shard_map.72.refs_4_), channel_id=1, source_target_pairs={{0,1},{1,0},{2,3},{3,2},{4,5},{5,4},{6,7},{7,6},{8,9},{9,8},{10,11... | collective-permute-start | bytes 1572872 | tf_op jit(solution)/shard_map/ppermute | solution.py:44
  77.5 13.1 %collective-permute-start.14 = (bf16[32,64,128]{2,1,0:T(8,128)(2,1)S(1)}, bf16[32,64,128]{2,1,0:T(8,128)(2,1)S(1)}, u32[]{:S(2)}, u32[]{:S(2)}) collective-permute-start(bf16[32,64,128]{2,1,0:T(8,128)(2,1)S(1)} %copy-done.12), channel_id=1, source_target_pairs={{0,4},{1,5},{2,6},{3,7},{4,0},{5,1},{6,2},{7,3},{8,12},{9,13},{10,... | collective-permute-start | bytes 1572872 | tf_op jit(solution)/shard_map/ppermute | solution.py:44
  78.4 19.2 %collective-permute-start.17 = (bf16[32,64,128]{2,1,0:T(8,128)(2,1)S(1)}, bf16[32,64,128]{2,1,0:T(8,128)(2,1)}, u32[]{:S(2)}, u32[]{:S(2)}) collective-permute-start(bf16[32,64,128]{2,1,0:T(8,128)(2,1)S(1)} %copy-done.12), channel_id=1, source_target_pairs={{0,2},{1,3},{2,0},{3,1},{4,6},{5,7},{6,4},{7,5},{8,10},{9,11},{10,... | collective-permute-start | bytes 1572872 | tf_op jit(solution)/shard_map/ppermute | solution.py:44
  79.9 16.2 %collective-permute-start.21 = (bf16[32,64,128]{2,1,0:T(8,128)(2,1)S(1)}, bf16[32,64,128]{2,1,0:T(8,128)(2,1)S(1)}, u32[]{:S(2)}, u32[]{:S(2)}) collective-permute-start(bf16[32,64,128]{2,1,0:T(8,128)(2,1)S(1)} %copy-done.14), channel_id=1, source_target_pairs={{0,1},{1,0},{2,3},{3,2},{4,5},{5,4},{6,7},{7,6},{8,9},{9,8},{10,11... | collective-permute-start | bytes 1572872 | tf_op jit(solution)/shard_map/ppermute | solution.py:44
  87.7 17.8 %collective-permute-start.11 = (bf16[32,64,128]{2,1,0:T(8,128)(2,1)S(1)}, bf16[32,64,128]{2,1,0:T(8,128)(2,1)}, u32[]{:S(2)}, u32[]{:S(2)}) collective-permute-start(bf16[32,64,128]{2,1,0:T(8,128)(2,1)S(1)} %copy-done.14), channel_id=1, source_target_pairs={{0,2},{1,3},{2,0},{3,1},{4,6},{5,7},{6,4},{7,5},{8,10},{9,11},{10,... | collective-permute-start | bytes 1572872 | tf_op jit(solution)/shard_map/ppermute | solution.py:44
  90.6 17.4 %collective-permute-start.7 = (bf16[129,16,128]{2,1,0:T(8,128)(2,1)S(1)}, bf16[129,16,128]{2,1,0:T(8,128)(2,1)}, u32[]{:S(2)}, u32[]{:S(2)}) collective-permute-start(bf16[129,16,128]{2,1,0:T(8,128)(2,1)S(1)} %copy-done.9), channel_id=1, source_target_pairs={{0,12},{1,13},{2,14},{3,15},{4,8},{5,9},{6,10},{7,11},{8,4},{9,5},... | collective-permute-start | bytes 1585160 | tf_op jit(solution)/shard_map/ppermute | solution.py:44
  96.1 17.6 %collective-permute-start.19 = (bf16[32,64,128]{2,1,0:T(8,128)(2,1)}, bf16[32,64,128]{2,1,0:T(8,128)(2,1)}, u32[]{:S(2)}, u32[]{:S(2)}) collective-permute-start(bf16[32,64,128]{2,1,0:T(8,128)(2,1)} %shard_map.73.refs_6_), channel_id=1, source_target_pairs={{0,1},{1,0},{2,3},{3,2},{4,5},{5,4},{6,7},{7,6},{8,9},{9,8},{10,11... | collective-permute-start | bytes 1572872 | tf_op jit(solution)/shard_map/ppermute | solution.py:44
  96.2 40.9 %collective-permute-start.15 = (bf16[32,64,128]{2,1,0:T(8,128)(2,1)}, bf16[32,64,128]{2,1,0:T(8,128)(2,1)S(1)}, u32[]{:S(2)}, u32[]{:S(2)}) collective-permute-start(bf16[32,64,128]{2,1,0:T(8,128)(2,1)} %shard_map.73.refs_6_), channel_id=1, source_target_pairs={{0,2},{1,3},{2,0},{3,1},{4,6},{5,7},{6,4},{7,5},{8,10},{9,11},{10,... | collective-permute-start | bytes 1572872 | tf_op jit(solution)/shard_map/ppermute | solution.py:44
  97.6 39.4 %collective-permute-start.18 = (bf16[32,64,128]{2,1,0:T(8,128)(2,1)}, bf16[32,64,128]{2,1,0:T(8,128)(2,1)}, u32[]{:S(2)}, u32[]{:S(2)}) collective-permute-start(bf16[32,64,128]{2,1,0:T(8,128)(2,1)} %collective-permute-done.17.refs_4_), channel_id=1, source_target_pairs={{0,1},{1,0},{2,3},{3,2},{4,5},{5,4},{6,7},{7,6},{8,9},{9,8},{10,11... | collective-permute-start | bytes 1572872 | tf_op jit(solution)/shard_map/ppermute | solution.py:44
  105.5 39.2 %collective-permute-start.4 = (bf16[129,16,128]{2,1,0:T(8,128)(2,1)S(1)}, bf16[129,16,128]{2,1,0:T(8,128)(2,1)S(1)}, u32[]{:S(2)}, u32[]{:S(2)}) collective-permute-start(bf16[129,16,128]{2,1,0:T(8,128)(2,1)S(1)} %copy-done.19), channel_id=1, source_target_pairs={{0,6},{1,7},{2,4},{3,5},{4,2},{5,3},{6,0},{7,1},{8,14},{9,15},{10,... | collective-permute-start | bytes 1585160 | tf_op jit(solution)/shard_map/ppermute | solution.py:44
  108.0 36.7 %collective-permute-start.8 = (bf16[129,16,128]{2,1,0:T(8,128)(2,1)S(1)}, bf16[129,16,128]{2,1,0:T(8,128)(2,1)S(1)}, u32[]{:S(2)}, u32[]{:S(2)}) collective-permute-start(bf16[129,16,128]{2,1,0:T(8,128)(2,1)S(1)} %copy-done.8), channel_id=1, source_target_pairs={{0,14},{1,15},{2,12},{3,13},{4,10},{5,11},{6,8},{7,9},{8,6},{9,7},... | collective-permute-start | bytes 1585160 | tf_op jit(solution)/shard_map/ppermute | solution.py:44
  113.7 31.0 %collective-permute-start.12 = (bf16[32,64,128]{2,1,0:T(8,128)(2,1)}, bf16[32,64,128]{2,1,0:T(8,128)(2,1)S(1)}, u32[]{:S(2)}, u32[]{:S(2)}) collective-permute-start(bf16[32,64,128]{2,1,0:T(8,128)(2,1)} %collective-permute-done.11.refs_4_), channel_id=1, source_target_pairs={{0,1},{1,0},{2,3},{3,2},{4,5},{5,4},{6,7},{7,6},{8,9},{9,8},{10,11... | collective-permute-start | bytes 1572872 | tf_op jit(solution)/shard_map/ppermute | solution.py:44
  137.1 7.7 %collective-permute-start.16 = (bf16[32,64,128]{2,1,0:T(8,128)(2,1)S(1)}, bf16[32,64,128]{2,1,0:T(8,128)(2,1)S(1)}, u32[]{:S(2)}, u32[]{:S(2)}) collective-permute-start(bf16[32,64,128]{2,1,0:T(8,128)(2,1)S(1)} %collective-permute-done.15.refs_6_), channel_id=1, source_target_pairs={{0,1},{1,0},{2,3},{3,2},{4,5},{5,4},{6,7},{7,6},{8,9},{9,8},{10,11... | collective-permute-start | bytes 1572872 | tf_op jit(solution)/shard_map/ppermute | solution.py:44
  146.0 23.5 %copy-start.1 = (bf16[32,64,128]{2,1,0:T(8,128)(2,1)S(1)}, bf16[32,64,128]{2,1,0:T(8,128)(2,1)}, u32[]{:S(2)}) copy-start(bf16[32,64,128]{2,1,0:T(8,128)(2,1)} %copy-done) | copy-start | bytes 1572868
  153.6 2.1 collective-permute-start.24
  154.2 3.9 %collective-permute-start.25 = (f32[16,128]{1,0:T(8,128)}, f32[16,128]{1,0:T(8,128)S(1)}, u32[]{:S(2)}, u32[]{:S(2)}) collective-permute-start(f32[16,128]{1,0:T(8,128)} %get-tuple-element.35), channel_id=1, source_target_pairs={{0,2},{1,3},{2,0},{3,1},{4,6},{5,7},{6,4},{7,5},{8,10},{9,11},{10,... | collective-permute-start | bytes 24584 | tf_op jit(solution)/shard_map/ppermute | solution.py:100
  154.2 3.9 %collective-permute-start.26 = (f32[16,128]{1,0:T(8,128)}, f32[16,128]{1,0:T(8,128)S(1)}, u32[]{:S(2)}, u32[]{:S(2)}) collective-permute-start(f32[16,128]{1,0:T(8,128)} %get-tuple-element.35), channel_id=1, source_target_pairs={{0,3},{1,2},{2,1},{3,0},{4,7},{5,6},{6,5},{7,4},{8,11},{9,10},{10,... | collective-permute-start | bytes 24584 | tf_op jit(solution)/shard_map/ppermute | solution.py:100
  158.8 5.2 %collective-permute-start.27 = (f32[16,128]{1,0:T(8,128)S(1)}, f32[16,128]{1,0:T(8,128)S(1)}, u32[]{:S(2)}, u32[]{:S(2)}) collective-permute-start(f32[16,128]{1,0:T(8,128)S(1)} %add_add_fusion.1), channel_id=1, source_target_pairs={{0,4},{1,5},{2,6},{3,7},{4,0},{5,1},{6,2},{7,3},{8,12},{9,13},{10,... | collective-permute-start | bytes 24584 | tf_op jit(solution)/shard_map/ppermute | solution.py:100
  158.8 6.9 %collective-permute-start.28 = (f32[16,128]{1,0:T(8,128)S(1)}, f32[16,128]{1,0:T(8,128)S(1)}, u32[]{:S(2)}, u32[]{:S(2)}) collective-permute-start(f32[16,128]{1,0:T(8,128)S(1)} %add_add_fusion.1), channel_id=1, source_target_pairs={{0,8},{1,9},{2,10},{3,11},{4,12},{5,13},{6,14},{7,15},{8,0},{9,1},... | collective-permute-start | bytes 24584 | tf_op jit(solution)/shard_map/ppermute | solution.py:100
  164.0 5.4 %collective-permute-start.29 = (f32[16,128]{1,0:T(8,128)S(1)}, f32[16,128]{1,0:T(8,128)S(1)}, u32[]{:S(2)}, u32[]{:S(2)}) collective-permute-start(f32[16,128]{1,0:T(8,128)S(1)} %add_add_fusion.1), channel_id=1, source_target_pairs={{0,12},{1,13},{2,14},{3,15},{4,8},{5,9},{6,10},{7,11},{8,4},{9,5},... | collective-permute-start | bytes 24584 | tf_op jit(solution)/shard_map/ppermute | solution.py:100
  171.8 12.2 %collective-permute-start.33 = (bf16[32,64,128]{2,1,0:T(8,128)(2,1)S(1)}, bf16[32,64,128]{2,1,0:T(8,128)(2,1)S(1)}, u32[]{:S(2)}, u32[]{:S(2)}) collective-permute-start(bf16[32,64,128]{2,1,0:T(8,128)(2,1)S(1)} %get-tuple-element.36.refs_10_), channel_id=1, source_target_pairs={{0,2},{1,5},{2,6},{3,1},{4,0},{5,9},{6,10},{7,3},{8,4},{9,13},{10,... | collective-permute-start | bytes 1572872 | tf_op jit(solution)/shard_map/ppermute | solution.py:44
  172.3 11.7 %collective-permute-start.30 = (bf16[32,64,128]{2,1,0:T(8,128)(2,1)S(1)}, bf16[32,64,128]{2,1,0:T(8,128)(2,1)S(1)}, u32[]{:S(2)}, u32[]{:S(2)}) collective-permute-start(bf16[32,64,128]{2,1,0:T(8,128)(2,1)S(1)} %get-tuple-element.36.refs_10_), channel_id=1, source_target_pairs={{0,4},{1,3},{2,0},{3,7},{4,8},{5,1},{6,2},{7,11},{8,12},{9,5},{10,... | collective-permute-start | bytes 1572872 | tf_op jit(solution)/shard_map/ppermute | solution.py:44
  173.8 12.7 %collective-permute-start.32 = (bf16[32,64,128]{2,1,0:T(8,128)(2,1)S(1)}, bf16[32,64,128]{2,1,0:T(8,128)(2,1)S(1)}, u32[]{:S(2)}, u32[]{:S(2)}) collective-permute-start(bf16[32,64,128]{2,1,0:T(8,128)(2,1)S(1)} %get-tuple-element.36.refs_10_), channel_id=1, source_target_pairs={{0,1},{1,0},{2,3},{3,2},{4,5},{5,4},{6,7},{7,6},{8,9},{9,8},{10,11... | collective-permute-start | bytes 1572872 | tf_op jit(solution)/shard_map/ppermute | solution.py:44
  184.0 2.6 %collective-permute-start.34 = (bf16[32,64,128]{2,1,0:T(8,128)(2,1)S(1)}, bf16[32,64,128]{2,1,0:T(8,128)(2,1)S(1)}, u32[]{:S(2)}, u32[]{:S(2)}) collective-permute-start(bf16[32,64,128]{2,1,0:T(8,128)(2,1)S(1)} %collective-permute-done.33.refs_14_), channel_id=1, source_target_pairs={{0,1},{1,0},{2,3},{3,2},{4,5},{5,4},{6,7},{7,6},{8,9},{9,8},{10,11... | collective-permute-start | bytes 1572872 | tf_op jit(solution)/shard_map/ppermute | solution.py:44
  184.0 2.6 %collective-permute-start.35 = (bf16[32,64,128]{2,1,0:T(8,128)(2,1)S(1)}, bf16[32,64,128]{2,1,0:T(8,128)(2,1)S(1)}, u32[]{:S(2)}, u32[]{:S(2)}) collective-permute-start(bf16[32,64,128]{2,1,0:T(8,128)(2,1)S(1)} %collective-permute-done.30.refs_12_), channel_id=1, source_target_pairs={{0,1},{1,0},{2,3},{3,2},{4,5},{5,4},{6,7},{7,6},{8,9},{9,8},{10,11... | collective-permute-start | bytes 1572872 | tf_op jit(solution)/shard_map/ppermute | solution.py:44
  184.5 14.4 %collective-permute-start.31 = (bf16[32,64,128]{2,1,0:T(8,128)(2,1)S(1)}, bf16[32,64,128]{2,1,0:T(8,128)(2,1)}, u32[]{:S(2)}, u32[]{:S(2)}) collective-permute-start(bf16[32,64,128]{2,1,0:T(8,128)(2,1)S(1)} %collective-permute-done.30.refs_12_), channel_id=1, source_target_pairs={{0,4},{1,3},{2,0},{3,7},{4,8},{5,1},{6,2},{7,11},{8,12},{9,5},{10,... | collective-permute-start | bytes 1572872 | tf_op jit(solution)/shard_map/ppermute | solution.py:44
  184.5 14.4 %collective-permute-start.37 = (bf16[32,64,128]{2,1,0:T(8,128)(2,1)S(1)}, bf16[32,64,128]{2,1,0:T(8,128)(2,1)S(1)}, u32[]{:S(2)}, u32[]{:S(2)}) collective-permute-start(bf16[32,64,128]{2,1,0:T(8,128)(2,1)S(1)} %collective-permute-done.33.refs_14_), channel_id=1, source_target_pairs={{0,2},{1,5},{2,6},{3,1},{4,0},{5,9},{6,10},{7,3},{8,4},{9,13},{10,... | collective-permute-start | bytes 1572872 | tf_op jit(solution)/shard_map/ppermute | solution.py:44
  198.9 2.5 %collective-permute-start.39 = (bf16[32,64,128]{2,1,0:T(8,128)(2,1)}, bf16[32,64,128]{2,1,0:T(8,128)(2,1)S(1)}, u32[]{:S(2)}, u32[]{:S(2)}) collective-permute-start(bf16[32,64,128]{2,1,0:T(8,128)(2,1)} %shard_map.80.refs_10_), channel_id=1, source_target_pairs={{0,1},{1,0},{2,3},{3,2},{4,5},{5,4},{6,7},{7,6},{8,9},{9,8},{10,11... | collective-permute-start | bytes 1572872 | tf_op jit(solution)/shard_map/ppermute | solution.py:44
  198.9 2.6 %collective-permute-start.38 = (bf16[32,64,128]{2,1,0:T(8,128)(2,1)S(1)}, bf16[32,64,128]{2,1,0:T(8,128)(2,1)S(1)}, u32[]{:S(2)}, u32[]{:S(2)}) collective-permute-start(bf16[32,64,128]{2,1,0:T(8,128)(2,1)S(1)} %collective-permute-done.37.refs_12_), channel_id=1, source_target_pairs={{0,1},{1,0},{2,3},{3,2},{4,5},{5,4},{6,7},{7,6},{8,9},{9,8},{10,11... | collective-permute-start | bytes 1572872 | tf_op jit(solution)/shard_map/ppermute | solution.py:44
  199.4 14.9 %collective-permute-start.36 = (bf16[32,64,128]{2,1,0:T(8,128)(2,1)}, bf16[32,64,128]{2,1,0:T(8,128)(2,1)}, u32[]{:S(2)}, u32[]{:S(2)}) collective-permute-start(bf16[32,64,128]{2,1,0:T(8,128)(2,1)} %shard_map.80.refs_10_), channel_id=1, source_target_pairs={{0,4},{1,3},{2,0},{3,7},{4,8},{5,1},{6,2},{7,11},{8,12},{9,5},{10,... | collective-permute-start | bytes 1572872 | tf_op jit(solution)/shard_map/ppermute | solution.py:44
  199.4 14.9 %collective-permute-start.41 = (bf16[32,64,128]{2,1,0:T(8,128)(2,1)S(1)}, bf16[32,64,128]{2,1,0:T(8,128)(2,1)S(1)}, u32[]{:S(2)}, u32[]{:S(2)}) collective-permute-start(bf16[32,64,128]{2,1,0:T(8,128)(2,1)S(1)} %collective-permute-done.37.refs_12_), channel_id=1, source_target_pairs={{0,2},{1,5},{2,6},{3,1},{4,0},{5,9},{6,10},{7,3},{8,4},{9,13},{10,... | collective-permute-start | bytes 1572872 | tf_op jit(solution)/shard_map/ppermute | solution.py:44
  214.3 2.1 collective-permute-start.43
  214.3 2.6 %collective-permute-start.42 = (bf16[32,64,128]{2,1,0:T(8,128)(2,1)S(1)}, bf16[32,64,128]{2,1,0:T(8,128)(2,1)S(1)}, u32[]{:S(2)}, u32[]{:S(2)}) collective-permute-start(bf16[32,64,128]{2,1,0:T(8,128)(2,1)S(1)} %collective-permute-done.41.refs_12_), channel_id=1, source_target_pairs={{0,1},{1,0},{2,3},{3,2},{4,5},{5,4},{6,7},{7,6},{8,9},{9,8},{10,11... | collective-permute-start | bytes 1572872 | tf_op jit(solution)/shard_map/ppermute | solution.py:44
  214.8 10.4 %collective-permute-start.40 = (bf16[32,64,128]{2,1,0:T(8,128)(2,1)}, bf16[32,64,128]{2,1,0:T(8,128)(2,1)S(1)}, u32[]{:S(2)}, u32[]{:S(2)}) collective-permute-start(bf16[32,64,128]{2,1,0:T(8,128)(2,1)} %shard_map.82.refs_10_), channel_id=1, source_target_pairs={{0,4},{1,3},{2,0},{3,7},{4,8},{5,1},{6,2},{7,11},{8,12},{9,5},{10,... | collective-permute-start | bytes 1572872 | tf_op jit(solution)/shard_map/ppermute | solution.py:44
  226.0 2.1 collective-permute-start.44
  (37 other events, 132.6 us)

commit v18 on v17

--- a/solution.py
+++ b/solution.py
@@ -8,7 +8,7 @@
 from jax.sharding import PartitionSpec as P
 
 BOTH = ("sec", "term")
-VMEM_LIMIT = 60 * 2**20
+VMEM_LIMIT = 64 * 2**20
 PART = 16
 ORDER = [0, 1, 4, 2, 5, 6, 3, 7]
 WAITS = {4: 1, 2: 4, 6: 2}

time: 235 us -> 233 us (level)
  waiting for transfers between devices: 111 us -> 115 us
  local copies, waits for them, and re-layouts: 11.8 us -> 7.92 us
  Pallas kernels: 64.8 us -> 62.3 us
    unnamed x80 -> x24, local copies, waits for them, and re-layouts: 8.9 us -> 4.78 us
    pallas_call x8, Pallas kernels: 58.3 us -> 54.9 us  [apply_group(): pl.pallas_call(functools.partial(apply_kernel, sources, choices, chosen,...]
    ppermute x39, waiting for transfers between devices: 103 us -> 106 us  [permute(): return lax.ppermute(value, BOTH, pairs)]
  transfers between devices with their start and end apart: 45 -> 45, of which waited for: 18 -> 19; matrix products, arithmetic and copies ran while one was open for 1% -> 1% of each run, Pallas kernels for 22% -> 21%
where the time goes in v18:
time: 233 us; the launch traced here: 232 us
  waiting for transfers between devices  115 us (49%)
  Pallas kernels  62.3 us (27%)
  starting transfers between devices  44.7 us (19%)
  local copies, waits for them, and re-layouts  7.92 us (3%)
    ppermute x39, waiting for transfers between devices, permute(): return lax.ppermute(value, BOTH, pairs)  106 us
    pallas_call x8, Pallas kernels, apply_group(): pl.pallas_call(functools.partial(apply_kernel, sources, choices, chosen,...  54.9 us
    ppermute x39, starting transfers between devices, permute(): return lax.ppermute(value, BOTH, pairs)  37.4 us
    ppermute x6, waiting for transfers between devices, spread(): lax.ppermute(value, BOTH, [(d, d ^ m) for d in range(devices)])  8.67 us
    ppermute x6, starting transfers between devices, spread(): lax.ppermute(value, BOTH, [(d, d ^ m) for d in range(devices)])  7.28 us
    pallas_call x1, Pallas kernels, pack(): pl.pallas_call(functools.partial(pack_kernel, order, capacity, blocks, te...  5.33 us
    unnamed x24, local copies, waits for them, and re-layouts  4.78 us
  transfers between devices with their start and end apart: 45, of which 19 were waited for; matrix products, arithmetic and copies ran while one was open for 1% of the time, Pallas kernels for 21%

profile of v18, /device:TPU:0, one launch (start us, length us, event | category | flops | bytes accessed | tf_op | source)
XLA Modules:
  0.0 232.1 jit_solution(3754553750365136937)
XLA Ops:
  0.6 1.4 constant_dynamic-slice_fusion.2
  2.7 1.1 constant_dynamic-slice_fusion
  3.7 2.9 %collective-permute-start.22 = (bf16[32,64,128]{2,1,0:T(8,128)(2,1)}, bf16[32,64,128]{2,1,0:T(8,128)(2,1)}, u32[]{:S(2)}, u32[]{:S(2)}) collective-permute-start(bf16[32,64,128]{2,1,0:T(8,128)(2,1)} %get-tuple-element.45.refs_4_.refs_8_.wave_ref), channel_id=1, source_target_pairs={{0,2},{1,3},{2,0},{3,1},{4,6},{5,7},{6,4},{7,5},{8,10},{9,11},{10,... | collective-permute-start | bytes 1572872 | tf_op jit(solution)/shard_map/ppermute | solution.py:44
  6.7 2.6 %collective-permute-start.13 = (bf16[32,64,128]{2,1,0:T(8,128)(2,1)}, bf16[32,64,128]{2,1,0:T(8,128)(2,1)}, u32[]{:S(2)}, u32[]{:S(2)}) collective-permute-start(bf16[32,64,128]{2,1,0:T(8,128)(2,1)} %get-tuple-element.45.refs_4_.refs_8_.wave_ref), channel_id=1, source_target_pairs={{0,8},{1,9},{2,10},{3,11},{4,12},{5,13},{6,14},{7,15},{8,0},{9,1},... | collective-permute-start | bytes 1572872 | tf_op jit(solution)/shard_map/ppermute | solution.py:44
  11.6 5.3 %shard_map.68 = (bf16[129,16,128]{2,1,0:T(8,128)(2,1)}, bf16[129,16,128]{2,1,0:T(8,128)(2,1)}, bf16[129,16,128]{2,1,0:T(8,128)(2,1)}, bf16[129,16,128]{2,1,0:T(8...) custom-call(s32[2]{0:T(128)} %pad_add_fusion.1.ids_ref, ...), custom_call_target="tpu_custom_call" | custom-call | flops 5750000128 | tf_op jit(solution)/shard_map/pallas_call | solution.py:167
  17.5 1.8 collective-permute-start.5
  19.3 1.6 collective-permute-start.10
  21.0 24.3 %collective-permute-done.13.refs_0_ = bf16[32,64,128]{2,1,0:T(8,128)(2,1)} collective-permute-done((bf16[32,64,128]{2,1,0:T(8,128)(2,1)}, bf16[32,64,128]{2,1,0:T(8,128)(2,1)}, u32[]{:S(2)}, u32[]{:S(2)}) %collective-permute-start.13) | collective-permute-done | bytes 524320 | tf_op jit(solution)/shard_map/ppermute | solution.py:44
  46.2 3.0 %collective-permute-start.3 = (bf16[129,16,128]{2,1,0:T(8,128)(2,1)}, bf16[129,16,128]{2,1,0:T(8,128)(2,1)}, u32[]{:S(2)}, u32[]{:S(2)}) collective-permute-start(bf16[129,16,128]{2,1,0:T(8,128)(2,1)} %get-tuple-element.25), channel_id=1, source_target_pairs={{0,4},{1,5},{2,6},{3,7},{4,0},{5,1},{6,2},{7,3},{8,12},{9,13},{10,... | collective-permute-start | bytes 1585160 | tf_op jit(solution)/shard_map/ppermute | solution.py:44
  49.2 18.7 %collective-permute-done.5.refs_1_.refs_0_.refs_4_ = bf16[129,16,128]{2,1,0:T(8,128)(2,1)S(1)} collective-permute-done((bf16[129,16,128]{2,1,0:T(8,128)(2,1)}, bf16[129,16,128]{2,1,0:T(8,128)(2,1)S(1)}, u32[]{:S(2)}, u32[]{:S(2)}) %collective-permute-start.5) | collective-permute-done | bytes 528416 | tf_op jit(solution)/shard_map/ppermute | solution.py:44
  67.9 0.8 copy-done.2
  68.7 9.3 %collective-permute-done.6.refs_1_.refs_0_.refs_5_ = bf16[129,16,128]{2,1,0:T(8,128)(2,1)S(1)} collective-permute-done((bf16[129,16,128]{2,1,0:T(8,128)(2,1)}, bf16[129,16,128]{2,1,0:T(8,128)(2,1)S(1)}, u32[]{:S(2)}, u32[]{:S(2)}) %collective-permute-start.6) | collective-permute-done | bytes 528416 | tf_op jit(solution)/shard_map/ppermute | solution.py:44
  78.0 0.8 collective-permute-start.14
  78.8 1.6 collective-permute-start.17
  80.3 7.3 %shard_map.74 = (f32[33,64,128]{2,1,0:T(8,128)}, f32[8,128]{1,0:T(8,128)}) custom-call(s32[10]{0:T(128)} %stack.56.ids_ref, bf16[129,16,128]{2,1,0:T(8,128)(2,1)} %get-tuple-element.23.refs_0_, bf16[129,16,128]{2,1,0:T(8,128)(2,1)} %copy-done.4, bf16[2,32,128,128]{3,2,1,0:T(8,128)(2,1)} %refs_8_.7, ...), custom_call_target="tpu_custom_call" | custom-call | flops 8165000192 | tf_op jit(solution)/shard_map/pallas_call | solution.py:391
  88.3 3.0 %collective-permute-done.14.refs_0_ = bf16[32,64,128]{2,1,0:T(8,128)(2,1)} collective-permute-done((bf16[32,64,128]{2,1,0:T(8,128)(2,1)}, bf16[32,64,128]{2,1,0:T(8,128)(2,1)}, u32[]{:S(2)}, u32[]{:S(2)}) %collective-permute-start.14) | collective-permute-done | bytes 524320 | tf_op jit(solution)/shard_map/ppermute | solution.py:44
  91.3 5.1 %collective-permute-start.7 = (bf16[129,16,128]{2,1,0:T(8,128)(2,1)}, bf16[129,16,128]{2,1,0:T(8,128)(2,1)}, u32[]{:S(2)}, u32[]{:S(2)}) collective-permute-start(bf16[129,16,128]{2,1,0:T(8,128)(2,1)} %shard_map.69), channel_id=1, source_target_pairs={{0,12},{1,13},{2,14},{3,15},{4,8},{5,9},{6,10},{7,11},{8,4},{9,5},... | collective-permute-start | bytes 1585160 | tf_op jit(solution)/shard_map/ppermute | solution.py:44
  96.4 1.5 collective-permute-start.15
  98.1 7.1 %shard_map.75 = (f32[33,64,128]{2,1,0:T(8,128)}, f32[8,128]{1,0:T(8,128)}) custom-call(s32[10]{0:T(128)} %stack.56.ids_ref, bf16[129,16,128]{2,1,0:T(8,128)(2,1)} %copy-done.2, bf16[129,16,128]{2,1,0:T(8,128)(2,1)} %collective-permute-done.3.refs_1_.refs_2_, bf16[2,32,128,128]{3,2,1,0:T(8,128)(2,1)} %refs_8_.7, ...), custom_call_target="tpu_custom_call" | custom-call | flops 8165000192 | tf_op jit(solution)/shard_map/pallas_call | solution.py:391
  105.2 1.3 collective-permute-start.4
  106.5 2.4 %collective-permute-done.7.refs_1_.refs_6_ = bf16[129,16,128]{2,1,0:T(8,128)(2,1)} collective-permute-done((bf16[129,16,128]{2,1,0:T(8,128)(2,1)}, bf16[129,16,128]{2,1,0:T(8,128)(2,1)}, u32[]{:S(2)}, u32[]{:S(2)}) %collective-permute-start.7) | collective-permute-done | bytes 528416 | tf_op jit(solution)/shard_map/ppermute | solution.py:44
  109.0 5.4 %collective-permute-start.8 = (bf16[129,16,128]{2,1,0:T(8,128)(2,1)}, bf16[129,16,128]{2,1,0:T(8,128)(2,1)}, u32[]{:S(2)}, u32[]{:S(2)}) collective-permute-start(bf16[129,16,128]{2,1,0:T(8,128)(2,1)} %shard_map.70), channel_id=1, source_target_pairs={{0,14},{1,15},{2,12},{3,13},{4,10},{5,11},{6,8},{7,9},{8,6},{9,7},... | collective-permute-start | bytes 1585160 | tf_op jit(solution)/shard_map/ppermute | solution.py:44
  114.3 23.4 %collective-permute-done.15.refs_6_ = bf16[32,64,128]{2,1,0:T(8,128)(2,1)} collective-permute-done((bf16[32,64,128]{2,1,0:T(8,128)(2,1)}, bf16[32,64,128]{2,1,0:T(8,128)(2,1)}, u32[]{:S(2)}, u32[]{:S(2)}) %collective-permute-start.15) | collective-permute-done | bytes 524320 | tf_op jit(solution)/shard_map/ppermute | solution.py:44
  137.8 7.1 %shard_map.76 = (f32[33,64,128]{2,1,0:T(8,128)}, f32[8,128]{1,0:T(8,128)}) custom-call(s32[10]{0:T(128)} %stack.56.ids_ref, bf16[129,16,128]{2,1,0:T(8,128)(2,1)} %copy-done.5, bf16[129,16,128]{2,1,0:T(8,128)(2,1)} %collective-permute-done.7.refs_1_.refs_6_, bf16[2,32,128,128]{3,2,1,0:T(8,128)(2,1)} %refs_8_.7, ...), custom_call_target="tpu_custom_call" | custom-call | flops 8165000192 | tf_op jit(solution)/shard_map/pallas_call | solution.py:391
  145.0 7.1 %shard_map.77 = (f32[32,64,128]{2,1,0:T(8,128)}, f32[16,128]{1,0:T(8,128)}) custom-call(s32[10]{0:T(128)} %stack.56.ids_ref, bf16[129,16,128]{2,1,0:T(8,128)(2,1)} %collective-permute-done.4.refs_0_.refs_3_, bf16[129,16,128]{2,1,0:T(8,128)(2,1)} %collective-permute-done.8.refs_1_.refs_7_, bf16[2,32,128,128]{3,2,1,0:T(8,128)(2,1)} %refs_8_.7, ...), custom_call_target="tpu_custom_call" | custom-call | flops 8165000192 | tf_op jit(solution)/shard_map/pallas_call | solution.py:391
  152.1 0.8 collective-permute-start.24
  152.9 1.3 collective-permute-start.25
  154.3 2.4 %collective-permute-done.25 = f32[16,128]{1,0:T(8,128)S(1)} collective-permute-done((f32[16,128]{1,0:T(8,128)}, f32[16,128]{1,0:T(8,128)S(1)}, u32[]{:S(2)}, u32[]{:S(2)}) %collective-permute-start.25) | collective-permute-done | bytes 8224 | tf_op jit(solution)/shard_map/ppermute | solution.py:100
  156.8 0.8 collective-permute-done.26
  158.3 5.1 %collective-permute-start.28 = (f32[16,128]{1,0:T(8,128)S(1)}, f32[16,128]{1,0:T(8,128)S(1)}, u32[]{:S(2)}, u32[]{:S(2)}) collective-permute-start(f32[16,128]{1,0:T(8,128)S(1)} %add_add_fusion.1), channel_id=1, source_target_pairs={{0,8},{1,9},{2,10},{3,11},{4,12},{5,13},{6,14},{7,15},{8,0},{9,1},... | collective-permute-start | bytes 24584 | tf_op jit(solution)/shard_map/ppermute | solution.py:100
  163.3 1.6 collective-permute-done.28
  165.0 3.8 %collective-permute-done.29 = f32[16,128]{1,0:T(8,128)S(1)} collective-permute-done((f32[16,128]{1,0:T(8,128)S(1)}, f32[16,128]{1,0:T(8,128)S(1)}, u32[]{:S(2)}, u32[]{:S(2)}) %collective-permute-start.29) | collective-permute-done | bytes 8224 | tf_op jit(solution)/shard_map/ppermute | solution.py:100
  168.8 1.2 copy-done.1
  170.0 2.1 shard_map.78
  172.9 1.3 collective-permute-start.30
  174.2 10.3 %collective-permute-done.33.refs_14_ = bf16[32,64,128]{2,1,0:T(8,128)(2,1)} collective-permute-done((bf16[32,64,128]{2,1,0:T(8,128)(2,1)S(1)}, bf16[32,64,128]{2,1,0:T(8,128)(2,1)}, u32[]{:S(2)}, u32[]{:S(2)}) %collective-permute-start.33) | collective-permute-done | bytes 524320 | tf_op jit(solution)/shard_map/ppermute | solution.py:44
  185.0 2.0 collective-permute-start.37
  187.0 0.8 copy-done.9
  187.8 0.8 copy-done.10
  188.6 7.8 %shard_map.79 = (f32[33,64,128]{2,1,0:T(8,128)}, f32[8,128]{1,0:T(8,128)}) custom-call(s32[10]{0:T(128)} %stack.56.ids_ref, bf16[129,16,128]{2,1,0:T(8,128)(2,1)} %get-tuple-element.23.refs_0_, bf16[129,16,128]{2,1,0:T(8,128)(2,1)} %copy-done.4, bf16[129,16,128]{2,1,0:T(8,128)(2,1)} %collective-permute-done.3.refs_1_.refs_2_, ...), custom_call_target="tpu_custom_call" | custom-call | flops 10234999808 | tf_op jit(solution)/shard_map/pallas_call | solution.py:391
  196.4 3.2 %collective-permute-done.31.refs_0_ = bf16[32,64,128]{2,1,0:T(8,128)(2,1)} collective-permute-done((bf16[32,64,128]{2,1,0:T(8,128)(2,1)}, bf16[32,64,128]{2,1,0:T(8,128)(2,1)}, u32[]{:S(2)}, u32[]{:S(2)}) %collective-permute-start.31) | collective-permute-done | bytes 524320 | tf_op jit(solution)/shard_map/ppermute | solution.py:44
  200.2 2.0 collective-permute-start.41
  202.7 6.7 %shard_map.81 = (f32[33,64,128]{2,1,0:T(8,128)}, f32[8,128]{1,0:T(8,128)}) custom-call(s32[10]{0:T(128)} %stack.56.ids_ref, bf16[129,16,128]{2,1,0:T(8,128)(2,1)} %get-tuple-element.23.refs_0_, bf16[129,16,128]{2,1,0:T(8,128)(2,1)} %copy-done.4, bf16[129,16,128]{2,1,0:T(8,128)(2,1)} %collective-permute-done.3.refs_1_.refs_2_, ...), custom_call_target="tpu_custom_call" | custom-call | flops 8165000192 | tf_op jit(solution)/shard_map/pallas_call | solution.py:391
  209.4 5.5 %collective-permute-done.36.refs_0_ = bf16[32,64,128]{2,1,0:T(8,128)(2,1)} collective-permute-done((bf16[32,64,128]{2,1,0:T(8,128)(2,1)}, bf16[32,64,128]{2,1,0:T(8,128)(2,1)}, u32[]{:S(2)}, u32[]{:S(2)}) %collective-permute-start.36) | collective-permute-done | bytes 524320 | tf_op jit(solution)/shard_map/ppermute | solution.py:44
  215.4 1.7 collective-permute-done.43.refs_13_
  217.9 6.9 %shard_map.83 = (f32[33,64,128]{2,1,0:T(8,128)}, f32[8,128]{1,0:T(8,128)}) custom-call(s32[10]{0:T(128)} %stack.56.ids_ref, bf16[129,16,128]{2,1,0:T(8,128)(2,1)} %get-tuple-element.23.refs_0_, bf16[129,16,128]{2,1,0:T(8,128)(2,1)} %copy-done.4, bf16[129,16,128]{2,1,0:T(8,128)(2,1)} %collective-permute-done.3.refs_1_.refs_2_, ...), custom_call_target="tpu_custom_call" | custom-call | flops 8165000192 | tf_op jit(solution)/shard_map/pallas_call | solution.py:391
  224.9 2.2 collective-permute-done.44.refs_11_
  227.1 4.8 %shard_map.85 = bf16[32,64,128]{2,1,0:T(8,128)(2,1)} custom-call(s32[10]{0:T(128)} %stack.56.ids_ref, bf16[129,16,128]{2,1,0:T(8,128)(2,1)} %get-tuple-element.23.refs_0_, bf16[129,16,128]{2,1,0:T(8,128)(2,1)} %copy-done.4, bf16[129,16,128]{2,1,0:T(8,128)(2,1)} %collective-permute-done.3.refs_1_.refs_2_, ...), custom_call_target="tpu_custom_call" | custom-call | flops 6095000064 | tf_op jit(solution)/shard_map/pallas_call | solution.py:391
  (91 shorter events, 9.6 us)
Async XLA Ops:
  0.6 2.0 copy-start.3
  2.0 7.2 %copy-start.7 = (s32[2,32]{1,0:T(2,128)S(1)}, s32[2,32]{1,0:T(2,128)}, u32[]{:S(2)}) copy-start(s32[2,32]{1,0:T(2,128)} %param.9) | copy-start | bytes 772
  2.1 7.2 %copy-start.8 = (s32[2,32,1]{1,2,0:T(1,128)S(1)}, s32[2,32,1]{1,2,0:T(1,128)}, u32[]{:S(2)}) copy-start(s32[2,32,1]{1,2,0:T(1,128)} %param.8) | copy-start | bytes 772
  2.1 9.5 %collective-permute-start.1 = (bf16[2,32,64,128]{3,2,1,0:T(8,128)(2,1)S(1)}, bf16[2,32,64,128]{3,2,1,0:T(8,128)(2,1)}, u32[]{:S(2)}, u32[]{:S(2)}) collective-permute-start(bf16[2,32,64,128]{3,2,1,0:T(8,128)(2,1)S(1)} %constant_dynamic-slice_fusion.2), channel_id=1, source_target_pairs={{0,1},{1,0},{2,3},{3,2},{4,5},{5,4},{6,7},{7,6},{8,9},{9,8},{10,11... | collective-permute-start | bytes 3145736 | tf_op jit(solution)/shard_map/ppermute | solution.py:44
  2.6 77.7 %collective-permute-start.9 = (bf16[2,32,128,128]{3,2,1,0:T(8,128)(2,1)}, bf16[2,32,128,128]{3,2,1,0:T(8,128)(2,1)}, u32[]{:S(2)}, u32[]{:S(2)}) collective-permute-start(bf16[2,32,128,128]{3,2,1,0:T(8,128)(2,1)} %refs_8_.7), channel_id=1, source_target_pairs={{0,1},{1,0},{2,3},{3,2},{4,5},{5,4},{6,7},{7,6},{8,9},{9,8},{10,11... | collective-permute-start | bytes 6291464 | tf_op jit(solution)/shard_map/ppermute | solution.py:44
  3.7 15.6 %collective-permute-start.22 = (bf16[32,64,128]{2,1,0:T(8,128)(2,1)}, bf16[32,64,128]{2,1,0:T(8,128)(2,1)}, u32[]{:S(2)}, u32[]{:S(2)}) collective-permute-start(bf16[32,64,128]{2,1,0:T(8,128)(2,1)} %get-tuple-element.45.refs_4_.refs_8_.wave_ref), channel_id=1, source_target_pairs={{0,2},{1,3},{2,0},{3,1},{4,6},{5,7},{6,4},{7,5},{8,10},{9,11},{10,... | collective-permute-start | bytes 1572872 | tf_op jit(solution)/shard_map/ppermute | solution.py:44
  6.7 38.5 %collective-permute-start.13 = (bf16[32,64,128]{2,1,0:T(8,128)(2,1)}, bf16[32,64,128]{2,1,0:T(8,128)(2,1)}, u32[]{:S(2)}, u32[]{:S(2)}) collective-permute-start(bf16[32,64,128]{2,1,0:T(8,128)(2,1)} %get-tuple-element.45.refs_4_.refs_8_.wave_ref), channel_id=1, source_target_pairs={{0,8},{1,9},{2,10},{3,11},{4,12},{5,13},{6,14},{7,15},{8,0},{9,1},... | collective-permute-start | bytes 1572872 | tf_op jit(solution)/shard_map/ppermute | solution.py:44
  9.8 1.2 collective-permute-start
  16.9 28.3 %collective-permute-start.2 = (bf16[129,16,128]{2,1,0:T(8,128)(2,1)}, bf16[129,16,128]{2,1,0:T(8,128)(2,1)S(1)}, u32[]{:S(2)}, u32[]{:S(2)}) collective-permute-start(bf16[129,16,128]{2,1,0:T(8,128)(2,1)} %get-tuple-element.24), channel_id=1, source_target_pairs={{0,2},{1,3},{2,0},{3,1},{4,6},{5,7},{6,4},{7,5},{8,10},{9,11},{10,... | collective-permute-start | bytes 1585160 | tf_op jit(solution)/shard_map/ppermute | solution.py:44
  17.5 50.4 %collective-permute-start.5 = (bf16[129,16,128]{2,1,0:T(8,128)(2,1)}, bf16[129,16,128]{2,1,0:T(8,128)(2,1)S(1)}, u32[]{:S(2)}, u32[]{:S(2)}) collective-permute-start(bf16[129,16,128]{2,1,0:T(8,128)(2,1)} %get-tuple-element.27), channel_id=1, source_target_pairs={{0,8},{1,9},{2,10},{3,11},{4,12},{5,13},{6,14},{7,15},{8,0},{9,1},... | collective-permute-start | bytes 1585160 | tf_op jit(solution)/shard_map/ppermute | solution.py:44
  19.3 26.9 %collective-permute-start.10 = (bf16[32,64,128]{2,1,0:T(8,128)(2,1)}, bf16[32,64,128]{2,1,0:T(8,128)(2,1)}, u32[]{:S(2)}, u32[]{:S(2)}) collective-permute-start(bf16[32,64,128]{2,1,0:T(8,128)(2,1)} %get-tuple-element.45.refs_4_.refs_8_.wave_ref), channel_id=1, source_target_pairs={{0,4},{1,5},{2,6},{3,7},{4,0},{5,1},{6,2},{7,3},{8,12},{9,13},{10,... | collective-permute-start | bytes 1572872 | tf_op jit(solution)/shard_map/ppermute | solution.py:44
  45.2 32.7 %collective-permute-start.6 = (bf16[129,16,128]{2,1,0:T(8,128)(2,1)}, bf16[129,16,128]{2,1,0:T(8,128)(2,1)S(1)}, u32[]{:S(2)}, u32[]{:S(2)}) collective-permute-start(bf16[129,16,128]{2,1,0:T(8,128)(2,1)} %get-tuple-element.28), channel_id=1, source_target_pairs={{0,10},{1,11},{2,8},{3,9},{4,14},{5,15},{6,12},{7,13},{8,2},{9,3},... | collective-permute-start | bytes 1585160 | tf_op jit(solution)/shard_map/ppermute | solution.py:44
  45.2 33.5 %collective-permute-start.23 = (bf16[32,64,128]{2,1,0:T(8,128)(2,1)}, bf16[32,64,128]{2,1,0:T(8,128)(2,1)}, u32[]{:S(2)}, u32[]{:S(2)}) collective-permute-start(bf16[32,64,128]{2,1,0:T(8,128)(2,1)} %collective-permute-done.22.refs_6_), channel_id=1, source_target_pairs={{0,1},{1,0},{2,3},{3,2},{4,5},{5,4},{6,7},{7,6},{8,9},{9,8},{10,11... | collective-permute-start | bytes 1572872 | tf_op jit(solution)/shard_map/ppermute | solution.py:44
  46.2 41.4 %collective-permute-start.3 = (bf16[129,16,128]{2,1,0:T(8,128)(2,1)}, bf16[129,16,128]{2,1,0:T(8,128)(2,1)}, u32[]{:S(2)}, u32[]{:S(2)}) collective-permute-start(bf16[129,16,128]{2,1,0:T(8,128)(2,1)} %get-tuple-element.25), channel_id=1, source_target_pairs={{0,4},{1,5},{2,6},{3,7},{4,0},{5,1},{6,2},{7,3},{8,12},{9,13},{10,... | collective-permute-start | bytes 1585160 | tf_op jit(solution)/shard_map/ppermute | solution.py:44
  67.9 28.6 %collective-permute-start.20 = (bf16[32,64,128]{2,1,0:T(8,128)(2,1)}, bf16[32,64,128]{2,1,0:T(8,128)(2,1)}, u32[]{:S(2)}, u32[]{:S(2)}) collective-permute-start(bf16[32,64,128]{2,1,0:T(8,128)(2,1)} %shard_map.72.refs_4_), channel_id=1, source_target_pairs={{0,1},{1,0},{2,3},{3,2},{4,5},{5,4},{6,7},{7,6},{8,9},{9,8},{10,11... | collective-permute-start | bytes 1572872 | tf_op jit(solution)/shard_map/ppermute | solution.py:44
  78.0 13.3 %collective-permute-start.14 = (bf16[32,64,128]{2,1,0:T(8,128)(2,1)}, bf16[32,64,128]{2,1,0:T(8,128)(2,1)}, u32[]{:S(2)}, u32[]{:S(2)}) collective-permute-start(bf16[32,64,128]{2,1,0:T(8,128)(2,1)} %shard_map.72.refs_4_), channel_id=1, source_target_pairs={{0,4},{1,5},{2,6},{3,7},{4,0},{5,1},{6,2},{7,3},{8,12},{9,13},{10,... | collective-permute-start | bytes 1572872 | tf_op jit(solution)/shard_map/ppermute | solution.py:44
  78.8 19.2 %collective-permute-start.17 = (bf16[32,64,128]{2,1,0:T(8,128)(2,1)}, bf16[32,64,128]{2,1,0:T(8,128)(2,1)}, u32[]{:S(2)}, u32[]{:S(2)}) collective-permute-start(bf16[32,64,128]{2,1,0:T(8,128)(2,1)} %shard_map.72.refs_4_), channel_id=1, source_target_pairs={{0,2},{1,3},{2,0},{3,1},{4,6},{5,7},{6,4},{7,5},{8,10},{9,11},{10,... | collective-permute-start | bytes 1572872 | tf_op jit(solution)/shard_map/ppermute | solution.py:44
  80.3 16.1 %collective-permute-start.21 = (bf16[32,64,128]{2,1,0:T(8,128)(2,1)}, bf16[32,64,128]{2,1,0:T(8,128)(2,1)}, u32[]{:S(2)}, u32[]{:S(2)}) collective-permute-start(bf16[32,64,128]{2,1,0:T(8,128)(2,1)} %shard_map.71.refs_6_), channel_id=1, source_target_pairs={{0,1},{1,0},{2,3},{3,2},{4,5},{5,4},{6,7},{7,6},{8,9},{9,8},{10,11... | collective-permute-start | bytes 1572872 | tf_op jit(solution)/shard_map/ppermute | solution.py:44
  87.6 17.6 %collective-permute-start.11 = (bf16[32,64,128]{2,1,0:T(8,128)(2,1)}, bf16[32,64,128]{2,1,0:T(8,128)(2,1)}, u32[]{:S(2)}, u32[]{:S(2)}) collective-permute-start(bf16[32,64,128]{2,1,0:T(8,128)(2,1)} %shard_map.71.refs_6_), channel_id=1, source_target_pairs={{0,2},{1,3},{2,0},{3,1},{4,6},{5,7},{6,4},{7,5},{8,10},{9,11},{10,... | collective-permute-start | bytes 1572872 | tf_op jit(solution)/shard_map/ppermute | solution.py:44
  91.3 17.7 %collective-permute-start.7 = (bf16[129,16,128]{2,1,0:T(8,128)(2,1)}, bf16[129,16,128]{2,1,0:T(8,128)(2,1)}, u32[]{:S(2)}, u32[]{:S(2)}) collective-permute-start(bf16[129,16,128]{2,1,0:T(8,128)(2,1)} %shard_map.69), channel_id=1, source_target_pairs={{0,12},{1,13},{2,14},{3,15},{4,8},{5,9},{6,10},{7,11},{8,4},{9,5},... | collective-permute-start | bytes 1585160 | tf_op jit(solution)/shard_map/ppermute | solution.py:44
  96.4 17.9 %collective-permute-start.19 = (bf16[32,64,128]{2,1,0:T(8,128)(2,1)}, bf16[32,64,128]{2,1,0:T(8,128)(2,1)}, u32[]{:S(2)}, u32[]{:S(2)}) collective-permute-start(bf16[32,64,128]{2,1,0:T(8,128)(2,1)} %shard_map.73.refs_6_), channel_id=1, source_target_pairs={{0,1},{1,0},{2,3},{3,2},{4,5},{5,4},{6,7},{7,6},{8,9},{9,8},{10,11... | collective-permute-start | bytes 1572872 | tf_op jit(solution)/shard_map/ppermute | solution.py:44
  96.4 41.3 %collective-permute-start.15 = (bf16[32,64,128]{2,1,0:T(8,128)(2,1)}, bf16[32,64,128]{2,1,0:T(8,128)(2,1)}, u32[]{:S(2)}, u32[]{:S(2)}) collective-permute-start(bf16[32,64,128]{2,1,0:T(8,128)(2,1)} %shard_map.73.refs_6_), channel_id=1, source_target_pairs={{0,2},{1,3},{2,0},{3,1},{4,6},{5,7},{6,4},{7,5},{8,10},{9,11},{10,... | collective-permute-start | bytes 1572872 | tf_op jit(solution)/shard_map/ppermute | solution.py:44
  97.9 39.8 %collective-permute-start.18 = (bf16[32,64,128]{2,1,0:T(8,128)(2,1)}, bf16[32,64,128]{2,1,0:T(8,128)(2,1)}, u32[]{:S(2)}, u32[]{:S(2)}) collective-permute-start(bf16[32,64,128]{2,1,0:T(8,128)(2,1)} %collective-permute-done.17.refs_4_), channel_id=1, source_target_pairs={{0,1},{1,0},{2,3},{3,2},{4,5},{5,4},{6,7},{7,6},{8,9},{9,8},{10,11... | collective-permute-start | bytes 1572872 | tf_op jit(solution)/shard_map/ppermute | solution.py:44
  105.2 39.7 %collective-permute-start.4 = (bf16[129,16,128]{2,1,0:T(8,128)(2,1)}, bf16[129,16,128]{2,1,0:T(8,128)(2,1)}, u32[]{:S(2)}, u32[]{:S(2)}) collective-permute-start(bf16[129,16,128]{2,1,0:T(8,128)(2,1)} %get-tuple-element.26), channel_id=1, source_target_pairs={{0,6},{1,7},{2,4},{3,5},{4,2},{5,3},{6,0},{7,1},{8,14},{9,15},{10,... | collective-permute-start | bytes 1585160 | tf_op jit(solution)/shard_map/ppermute | solution.py:44
  109.0 36.0 %collective-permute-start.8 = (bf16[129,16,128]{2,1,0:T(8,128)(2,1)}, bf16[129,16,128]{2,1,0:T(8,128)(2,1)}, u32[]{:S(2)}, u32[]{:S(2)}) collective-permute-start(bf16[129,16,128]{2,1,0:T(8,128)(2,1)} %shard_map.70), channel_id=1, source_target_pairs={{0,14},{1,15},{2,12},{3,13},{4,10},{5,11},{6,8},{7,9},{8,6},{9,7},... | collective-permute-start | bytes 1585160 | tf_op jit(solution)/shard_map/ppermute | solution.py:44
  114.3 30.6 %collective-permute-start.12 = (bf16[32,64,128]{2,1,0:T(8,128)(2,1)}, bf16[32,64,128]{2,1,0:T(8,128)(2,1)}, u32[]{:S(2)}, u32[]{:S(2)}) collective-permute-start(bf16[32,64,128]{2,1,0:T(8,128)(2,1)} %collective-permute-done.11.refs_4_), channel_id=1, source_target_pairs={{0,1},{1,0},{2,3},{3,2},{4,5},{5,4},{6,7},{7,6},{8,9},{9,8},{10,11... | collective-permute-start | bytes 1572872 | tf_op jit(solution)/shard_map/ppermute | solution.py:44
  137.8 7.2 %collective-permute-start.16 = (bf16[32,64,128]{2,1,0:T(8,128)(2,1)}, bf16[32,64,128]{2,1,0:T(8,128)(2,1)}, u32[]{:S(2)}, u32[]{:S(2)}) collective-permute-start(bf16[32,64,128]{2,1,0:T(8,128)(2,1)} %collective-permute-done.15.refs_6_), channel_id=1, source_target_pairs={{0,1},{1,0},{2,3},{3,2},{4,5},{5,4},{6,7},{7,6},{8,9},{9,8},{10,11... | collective-permute-start | bytes 1572872 | tf_op jit(solution)/shard_map/ppermute | solution.py:44
  152.1 2.2 collective-permute-start.24
  152.9 3.9 %collective-permute-start.25 = (f32[16,128]{1,0:T(8,128)}, f32[16,128]{1,0:T(8,128)S(1)}, u32[]{:S(2)}, u32[]{:S(2)}) collective-permute-start(f32[16,128]{1,0:T(8,128)} %get-tuple-element.35), channel_id=1, source_target_pairs={{0,2},{1,3},{2,0},{3,1},{4,6},{5,7},{6,4},{7,5},{8,10},{9,11},{10,... | collective-permute-start | bytes 24584 | tf_op jit(solution)/shard_map/ppermute | solution.py:100
  154.2 3.4 %collective-permute-start.26 = (f32[16,128]{1,0:T(8,128)}, f32[16,128]{1,0:T(8,128)S(1)}, u32[]{:S(2)}, u32[]{:S(2)}) collective-permute-start(f32[16,128]{1,0:T(8,128)} %get-tuple-element.35), channel_id=1, source_target_pairs={{0,3},{1,2},{2,1},{3,0},{4,7},{5,6},{6,5},{7,4},{8,11},{9,10},{10,... | collective-permute-start | bytes 24584 | tf_op jit(solution)/shard_map/ppermute | solution.py:100
  158.3 5.1 %collective-permute-start.27 = (f32[16,128]{1,0:T(8,128)S(1)}, f32[16,128]{1,0:T(8,128)S(1)}, u32[]{:S(2)}, u32[]{:S(2)}) collective-permute-start(f32[16,128]{1,0:T(8,128)S(1)} %add_add_fusion.1), channel_id=1, source_target_pairs={{0,4},{1,5},{2,6},{3,7},{4,0},{5,1},{6,2},{7,3},{8,12},{9,13},{10,... | collective-permute-start | bytes 24584 | tf_op jit(solution)/shard_map/ppermute | solution.py:100
  158.3 6.7 %collective-permute-start.28 = (f32[16,128]{1,0:T(8,128)S(1)}, f32[16,128]{1,0:T(8,128)S(1)}, u32[]{:S(2)}, u32[]{:S(2)}) collective-permute-start(f32[16,128]{1,0:T(8,128)S(1)} %add_add_fusion.1), channel_id=1, source_target_pairs={{0,8},{1,9},{2,10},{3,11},{4,12},{5,13},{6,14},{7,15},{8,0},{9,1},... | collective-permute-start | bytes 24584 | tf_op jit(solution)/shard_map/ppermute | solution.py:100
  163.3 5.4 %collective-permute-start.29 = (f32[16,128]{1,0:T(8,128)S(1)}, f32[16,128]{1,0:T(8,128)S(1)}, u32[]{:S(2)}, u32[]{:S(2)}) collective-permute-start(f32[16,128]{1,0:T(8,128)S(1)} %add_add_fusion.1), channel_id=1, source_target_pairs={{0,12},{1,13},{2,14},{3,15},{4,8},{5,9},{6,10},{7,11},{8,4},{9,5},... | collective-permute-start | bytes 24584 | tf_op jit(solution)/shard_map/ppermute | solution.py:100
  172.1 12.3 %collective-permute-start.33 = (bf16[32,64,128]{2,1,0:T(8,128)(2,1)S(1)}, bf16[32,64,128]{2,1,0:T(8,128)(2,1)}, u32[]{:S(2)}, u32[]{:S(2)}) collective-permute-start(bf16[32,64,128]{2,1,0:T(8,128)(2,1)S(1)} %get-tuple-element.36.refs_10_), channel_id=1, source_target_pairs={{0,2},{1,5},{2,6},{3,1},{4,0},{5,9},{6,10},{7,3},{8,4},{9,13},{10,... | collective-permute-start | bytes 1572872 | tf_op jit(solution)/shard_map/ppermute | solution.py:44
  172.9 11.6 %collective-permute-start.30 = (bf16[32,64,128]{2,1,0:T(8,128)(2,1)S(1)}, bf16[32,64,128]{2,1,0:T(8,128)(2,1)}, u32[]{:S(2)}, u32[]{:S(2)}) collective-permute-start(bf16[32,64,128]{2,1,0:T(8,128)(2,1)S(1)} %get-tuple-element.36.refs_10_), channel_id=1, source_target_pairs={{0,4},{1,3},{2,0},{3,7},{4,8},{5,1},{6,2},{7,11},{8,12},{9,5},{10,... | collective-permute-start | bytes 1572872 | tf_op jit(solution)/shard_map/ppermute | solution.py:44
  174.2 12.8 %collective-permute-start.32 = (bf16[32,64,128]{2,1,0:T(8,128)(2,1)S(1)}, bf16[32,64,128]{2,1,0:T(8,128)(2,1)S(1)}, u32[]{:S(2)}, u32[]{:S(2)}) collective-permute-start(bf16[32,64,128]{2,1,0:T(8,128)(2,1)S(1)} %get-tuple-element.36.refs_10_), channel_id=1, source_target_pairs={{0,1},{1,0},{2,3},{3,2},{4,5},{5,4},{6,7},{7,6},{8,9},{9,8},{10,11... | collective-permute-start | bytes 1572872 | tf_op jit(solution)/shard_map/ppermute | solution.py:44
  184.5 3.3 %collective-permute-start.34 = (bf16[32,64,128]{2,1,0:T(8,128)(2,1)}, bf16[32,64,128]{2,1,0:T(8,128)(2,1)S(1)}, u32[]{:S(2)}, u32[]{:S(2)}) collective-permute-start(bf16[32,64,128]{2,1,0:T(8,128)(2,1)} %collective-permute-done.33.refs_14_), channel_id=1, source_target_pairs={{0,1},{1,0},{2,3},{3,2},{4,5},{5,4},{6,7},{7,6},{8,9},{9,8},{10,11... | collective-permute-start | bytes 1572872 | tf_op jit(solution)/shard_map/ppermute | solution.py:44
  184.5 4.1 %collective-permute-start.35 = (bf16[32,64,128]{2,1,0:T(8,128)(2,1)}, bf16[32,64,128]{2,1,0:T(8,128)(2,1)}, u32[]{:S(2)}, u32[]{:S(2)}) collective-permute-start(bf16[32,64,128]{2,1,0:T(8,128)(2,1)} %collective-permute-done.30.refs_12_), channel_id=1, source_target_pairs={{0,1},{1,0},{2,3},{3,2},{4,5},{5,4},{6,7},{7,6},{8,9},{9,8},{10,11... | collective-permute-start | bytes 1572872 | tf_op jit(solution)/shard_map/ppermute | solution.py:44
  185.0 14.7 %collective-permute-start.31 = (bf16[32,64,128]{2,1,0:T(8,128)(2,1)}, bf16[32,64,128]{2,1,0:T(8,128)(2,1)}, u32[]{:S(2)}, u32[]{:S(2)}) collective-permute-start(bf16[32,64,128]{2,1,0:T(8,128)(2,1)} %collective-permute-done.30.refs_12_), channel_id=1, source_target_pairs={{0,4},{1,3},{2,0},{3,7},{4,8},{5,1},{6,2},{7,11},{8,12},{9,5},{10,... | collective-permute-start | bytes 1572872 | tf_op jit(solution)/shard_map/ppermute | solution.py:44
  185.0 14.7 %collective-permute-start.37 = (bf16[32,64,128]{2,1,0:T(8,128)(2,1)}, bf16[32,64,128]{2,1,0:T(8,128)(2,1)}, u32[]{:S(2)}, u32[]{:S(2)}) collective-permute-start(bf16[32,64,128]{2,1,0:T(8,128)(2,1)} %collective-permute-done.33.refs_14_), channel_id=1, source_target_pairs={{0,2},{1,5},{2,6},{3,1},{4,0},{5,9},{6,10},{7,3},{8,4},{9,13},{10,... | collective-permute-start | bytes 1572872 | tf_op jit(solution)/shard_map/ppermute | solution.py:44
  199.7 2.5 %collective-permute-start.39 = (bf16[32,64,128]{2,1,0:T(8,128)(2,1)}, bf16[32,64,128]{2,1,0:T(8,128)(2,1)}, u32[]{:S(2)}, u32[]{:S(2)}) collective-permute-start(bf16[32,64,128]{2,1,0:T(8,128)(2,1)} %shard_map.80.refs_10_), channel_id=1, source_target_pairs={{0,1},{1,0},{2,3},{3,2},{4,5},{5,4},{6,7},{7,6},{8,9},{9,8},{10,11... | collective-permute-start | bytes 1572872 | tf_op jit(solution)/shard_map/ppermute | solution.py:44
  199.7 3.0 %collective-permute-start.38 = (bf16[32,64,128]{2,1,0:T(8,128)(2,1)}, bf16[32,64,128]{2,1,0:T(8,128)(2,1)}, u32[]{:S(2)}, u32[]{:S(2)}) collective-permute-start(bf16[32,64,128]{2,1,0:T(8,128)(2,1)} %collective-permute-done.37.refs_12_), channel_id=1, source_target_pairs={{0,1},{1,0},{2,3},{3,2},{4,5},{5,4},{6,7},{7,6},{8,9},{9,8},{10,11... | collective-permute-start | bytes 1572872 | tf_op jit(solution)/shard_map/ppermute | solution.py:44
  200.2 14.7 %collective-permute-start.36 = (bf16[32,64,128]{2,1,0:T(8,128)(2,1)}, bf16[32,64,128]{2,1,0:T(8,128)(2,1)}, u32[]{:S(2)}, u32[]{:S(2)}) collective-permute-start(bf16[32,64,128]{2,1,0:T(8,128)(2,1)} %shard_map.80.refs_10_), channel_id=1, source_target_pairs={{0,4},{1,3},{2,0},{3,7},{4,8},{5,1},{6,2},{7,11},{8,12},{9,5},{10,... | collective-permute-start | bytes 1572872 | tf_op jit(solution)/shard_map/ppermute | solution.py:44
  200.2 14.7 %collective-permute-start.41 = (bf16[32,64,128]{2,1,0:T(8,128)(2,1)}, bf16[32,64,128]{2,1,0:T(8,128)(2,1)}, u32[]{:S(2)}, u32[]{:S(2)}) collective-permute-start(bf16[32,64,128]{2,1,0:T(8,128)(2,1)} %collective-permute-done.37.refs_12_), channel_id=1, source_target_pairs={{0,2},{1,5},{2,6},{3,1},{4,0},{5,9},{6,10},{7,3},{8,4},{9,13},{10,... | collective-permute-start | bytes 1572872 | tf_op jit(solution)/shard_map/ppermute | solution.py:44
  214.9 2.3 collective-permute-start.43
  214.9 3.0 %collective-permute-start.42 = (bf16[32,64,128]{2,1,0:T(8,128)(2,1)}, bf16[32,64,128]{2,1,0:T(8,128)(2,1)}, u32[]{:S(2)}, u32[]{:S(2)}) collective-permute-start(bf16[32,64,128]{2,1,0:T(8,128)(2,1)} %collective-permute-done.41.refs_12_), channel_id=1, source_target_pairs={{0,1},{1,0},{2,3},{3,2},{4,5},{5,4},{6,7},{7,6},{8,9},{9,8},{10,11... | collective-permute-start | bytes 1572872 | tf_op jit(solution)/shard_map/ppermute | solution.py:44
  215.4 9.5 %collective-permute-start.40 = (bf16[32,64,128]{2,1,0:T(8,128)(2,1)}, bf16[32,64,128]{2,1,0:T(8,128)(2,1)}, u32[]{:S(2)}, u32[]{:S(2)}) collective-permute-start(bf16[32,64,128]{2,1,0:T(8,128)(2,1)} %shard_map.82.refs_10_), channel_id=1, source_target_pairs={{0,4},{1,3},{2,0},{3,7},{4,8},{5,1},{6,2},{7,11},{8,12},{9,5},{10,... | collective-permute-start | bytes 1572872 | tf_op jit(solution)/shard_map/ppermute | solution.py:44
  224.9 2.3 collective-permute-start.44
  (9 other events, 8.6 us)

commit v19 on v18

--- a/solution.py
+++ b/solution.py
@@ -192,11 +192,11 @@
     moved, where = [], []
     for slot in range(terms * capacity):
         at = side * terms * capacity + slot
-        block = vector[:, labels[0, at]].reshape(2 * rows, width)
+        block = vector[:, labels(0, at)].reshape(2 * rows, width)
         piece = left[at * parts : (at + 1) * parts].reshape(rows, width)
         product = jnp.dot(piece, block, preferred_element_type=jnp.float32)
         moved.append(product.astype(jnp.bfloat16))
-        where.append(labels[1, at])
+        where.append(labels(1, at))
     for slot in range(terms * capacity):
         total[where[slot]] += jnp.dot(
             moved[slot], right[slot], preferred_element_type=jnp.float32
@@ -234,6 +234,7 @@
         taken, refs[:count] = refs[:count], []
         return taken
 
+    (known,) = take(1) if choices else (None,)
     lefts = take(choices or sources)
     rights = take(2)
     vectors = [take(2) for _ in range(sources)]
@@ -248,6 +249,11 @@
     blocks = vector.shape[2]
     parts = left.shape[1]
 
+    def labels_of(source):
+        if choices:
+            return lambda row, at: known[ids_ref[chosen + source], row, at]
+        return lambda row, at: labels[source, row, at]
+
     def left_copies(source, piece):
         return [
             pltpu.make_async_copy(piece.at[parts], raw.at[source], raw_sems.at[source]),
@@ -268,7 +274,7 @@
 
     def load_right(source, side):
         for slot in range(terms * capacity):
-            target = jnp.minimum(labels[source, 1, side * terms * capacity + slot], blocks - 1)
+            target = jnp.minimum(labels_of(source)(1, side * terms * capacity + slot), blocks - 1)
             pltpu.make_async_copy(
                 rights[side].at[slot // capacity, target],
                 right.at[source, side, slot],
@@ -285,8 +291,7 @@
 
                 @pl.when(ids_ref[chosen + source] == choice)
                 def _():
-                    for copy in left_copies(source, piece):
-                        copy.start()
+                    left_copies(source, piece)[1].start()
 
         else:
             for copy in left_copies(source, lefts[source]):
@@ -305,12 +310,13 @@
     if end == "go on":
         last_out[...] = jnp.zeros_like(last_out)
 
-    for source in range(sources):
-        left_copies(source, lefts[0])[0].wait()
-    spread_labels[...] = raw[:, :8].astype(jnp.float32).astype(jnp.int32)
-    move_labels = pltpu.make_async_copy(spread_labels, labels, label_sem)
-    move_labels.start()
-    move_labels.wait()
+    if not choices:
+        for source in range(sources):
+            left_copies(source, lefts[0])[0].wait()
+        spread_labels[...] = raw[:, :8].astype(jnp.float32).astype(jnp.int32)
+        move_labels = pltpu.make_async_copy(spread_labels, labels, label_sem)
+        move_labels.start()
+        move_labels.wait()
     for source in range(sources):
         for side in range(2):
             load_right(source, side)
@@ -325,7 +331,7 @@
             wait_right(source, side)
             add_products(
                 left.at[source],
-                labels.at[source],
+                labels_of(source),
                 vector.at[source],
                 right.at[source, side],
                 total,
@@ -345,7 +351,7 @@
         store_total.wait()
 
 
-def apply_group(ids, lefts, rights, vectors, total, end, wave=None, chosen=0):
+def apply_group(ids, lefts, rights, vectors, total, end, wave=None, chosen=0, known=None):
     blocks, rows, width = vectors[0][0].shape
     terms = rights[0].shape[0]
     parts = lefts[0].shape[0] - 1
@@ -388,15 +394,17 @@
         "result": (jax.ShapeDtypeStruct((blocks, rows, width), jnp.bfloat16), whole),
     }[end]
     choices = len(lefts) if chosen else 0
+    scalars = [ids, known] if chosen else [ids]
     return pl.pallas_call(
         functools.partial(apply_kernel, sources, choices, chosen, first, end, terms, capacity),
         out_shape=out_shape,
-        in_specs=[pl.BlockSpec(memory_space=pltpu.SMEM)] + [anywhere] * len(arrays),
+        in_specs=[pl.BlockSpec(memory_space=pltpu.SMEM)] * len(scalars)
+        + [anywhere] * len(arrays),
         out_specs=out_specs,
         scratch_shapes=scratch,
         compiler_params=pltpu.CompilerParams(vmem_limit_bytes=VMEM_LIMIT),
         cost_estimate=busy(3.5 + 1.8 * sources),
-    )(ids, *arrays)
+    )(*scalars, *arrays)
 
 
 def direction_kernel(entries, total_ref, wave_ref, stats_ref, out_ref, rayleigh_ref):
@@ -487,10 +495,12 @@
     entries = blocks * owners * height * width
     stats = spread(stats, owners * halves)
     direction, rayleigh = new_direction(total, own_rows, stats, entries)
+    known = jnp.stack([left[-1, :2] for left in lefts]).astype(jnp.int32)
+
     def add_group(total, units, end):
         vectors = [(unit, swap(units[-s], owners, halves)) for s, unit in units.items()]
         chosen = 2 + distances.index(next(iter(units)))
-        return apply_group(numbers, lefts, rights, vectors, total, end, chosen=chosen)
+        return apply_group(numbers, lefts, rights, vectors, total, end, chosen=chosen, known=known)
 
     total, waiting = None, {0: direction}
     ahead = behind = direction
@@ -506,7 +516,9 @@
     last = after(last, token)
     vectors = [(last, swap(last, owners, halves))]
     chosen = 2 + distances.index(owners // 2)
-    total = apply_group(numbers, lefts, rights, vectors, total, "result", chosen=chosen)
+    total = apply_group(
+        numbers, lefts, rights, vectors, total, "result", chosen=chosen, known=known
+    )
     return (total, rayleigh[0])
 
 

time: 233 us -> 235 us (level)
  local copies, waits for them, and re-layouts: 7.92 us -> 13.2 us
  waiting for transfers between devices: 115 us -> 110 us
    unnamed x24 -> x29, local copies, waits for them, and re-layouts: 4.78 us -> 9.51 us
    ppermute x39, waiting for transfers between devices: 106 us -> 103 us  [permute(): return lax.ppermute(value, BOTH, pairs)]
  transfers between devices with their start and end apart: 45 -> 45, of which waited for: 19 -> 18; matrix products, arithmetic and copies ran while one was open for 1% -> 4% of each run, Pallas kernels for 21% -> 21%
where the time goes in v19:
time: 235 us; the launch traced here: 234 us
  waiting for transfers between devices  110 us (47%)
  Pallas kernels  63.3 us (27%)
  starting transfers between devices  44.3 us (19%)
  local copies, waits for them, and re-layouts  13.2 us (6%)
    ppermute x39, waiting for transfers between devices, permute(): return lax.ppermute(value, BOTH, pairs)  103 us
    pallas_call x8, Pallas kernels, apply_group(): pl.pallas_call(functools.partial(apply_kernel, sources, choices, chosen,...  55.9 us
    ppermute x39, starting transfers between devices, permute(): return lax.ppermute(value, BOTH, pairs)  37.8 us
    unnamed x29, local copies, waits for them, and re-layouts  9.51 us
    ppermute x6, waiting for transfers between devices, spread(): lax.ppermute(value, BOTH, [(d, d ^ m) for d in range(devices)])  7.29 us
    ppermute x6, starting transfers between devices, spread(): lax.ppermute(value, BOTH, [(d, d ^ m) for d in range(devices)])  6.5 us
    pallas_call x1, Pallas kernels, pack(): pl.pallas_call(functools.partial(pack_kernel, order, capacity, blocks, te...  5.33 us
  transfers between devices with their start and end apart: 45, of which 18 were waited for; matrix products, arithmetic and copies ran while one was open for 4% of the time, Pallas kernels for 21%

profile of v19, /device:TPU:0, one launch (start us, length us, event | category | flops | bytes accessed | tf_op | source)
XLA Modules:
  0.0 233.9 jit_solution(11845398507050102527)
XLA Ops:
  0.6 1.4 constant_dynamic-slice_fusion.2
  2.7 1.1 constant_dynamic-slice_fusion
  3.7 2.9 %collective-permute-start.22 = (bf16[32,64,128]{2,1,0:T(8,128)(2,1)}, bf16[32,64,128]{2,1,0:T(8,128)(2,1)}, u32[]{:S(2)}, u32[]{:S(2)}) collective-permute-start(bf16[32,64,128]{2,1,0:T(8,128)(2,1)} %get-tuple-element.45.refs_4_.refs_8_.wave_ref), channel_id=1, source_target_pairs={{0,2},{1,3},{2,0},{3,1},{4,6},{5,7},{6,4},{7,5},{8,10},{9,11},{10,... | collective-permute-start | bytes 1572872 | tf_op jit(solution)/shard_map/ppermute | solution.py:44
  6.7 2.6 %collective-permute-start.13 = (bf16[32,64,128]{2,1,0:T(8,128)(2,1)}, bf16[32,64,128]{2,1,0:T(8,128)(2,1)}, u32[]{:S(2)}, u32[]{:S(2)}) collective-permute-start(bf16[32,64,128]{2,1,0:T(8,128)(2,1)} %get-tuple-element.45.refs_4_.refs_8_.wave_ref), channel_id=1, source_target_pairs={{0,8},{1,9},{2,10},{3,11},{4,12},{5,13},{6,14},{7,15},{8,0},{9,1},... | collective-permute-start | bytes 1572872 | tf_op jit(solution)/shard_map/ppermute | solution.py:44
  11.6 5.3 %shard_map.68 = (bf16[129,16,128]{2,1,0:T(8,128)(2,1)}, bf16[129,16,128]{2,1,0:T(8,128)(2,1)}, bf16[129,16,128]{2,1,0:T(8,128)(2,1)}, bf16[129,16,128]{2,1,0:T(8...) custom-call(s32[2]{0:T(128)} %pad_add_fusion.1.ids_ref, ...), custom_call_target="tpu_custom_call" | custom-call | flops 5750000128 | tf_op jit(solution)/shard_map/pallas_call | solution.py:167
  17.5 1.8 collective-permute-start.5
  19.3 1.6 collective-permute-start.10
  21.0 24.3 %collective-permute-done.13.refs_0_ = bf16[32,64,128]{2,1,0:T(8,128)(2,1)} collective-permute-done((bf16[32,64,128]{2,1,0:T(8,128)(2,1)}, bf16[32,64,128]{2,1,0:T(8,128)(2,1)}, u32[]{:S(2)}, u32[]{:S(2)}) %collective-permute-start.13) | collective-permute-done | bytes 524320 | tf_op jit(solution)/shard_map/ppermute | solution.py:44
  46.0 2.8 %collective-permute-start.3 = (bf16[129,16,128]{2,1,0:T(8,128)(2,1)}, bf16[129,16,128]{2,1,0:T(8,128)(2,1)}, u32[]{:S(2)}, u32[]{:S(2)}) collective-permute-start(bf16[129,16,128]{2,1,0:T(8,128)(2,1)} %get-tuple-element.25), channel_id=1, source_target_pairs={{0,4},{1,5},{2,6},{3,7},{4,0},{5,1},{6,2},{7,3},{8,12},{9,13},{10,... | collective-permute-start | bytes 1585160 | tf_op jit(solution)/shard_map/ppermute | solution.py:44
  48.9 19.0 %collective-permute-done.5.refs_1_.refs_0_.refs_5_ = bf16[129,16,128]{2,1,0:T(8,128)(2,1)S(1)} collective-permute-done((bf16[129,16,128]{2,1,0:T(8,128)(2,1)}, bf16[129,16,128]{2,1,0:T(8,128)(2,1)S(1)}, u32[]{:S(2)}, u32[]{:S(2)}) %collective-permute-start.5) | collective-permute-done | bytes 528416 | tf_op jit(solution)/shard_map/ppermute | solution.py:44
  67.9 0.8 copy-done.2
  68.7 9.3 %collective-permute-done.6.refs_1_.refs_0_.refs_6_ = bf16[129,16,128]{2,1,0:T(8,128)(2,1)S(1)} collective-permute-done((bf16[129,16,128]{2,1,0:T(8,128)(2,1)}, bf16[129,16,128]{2,1,0:T(8,128)(2,1)S(1)}, u32[]{:S(2)}, u32[]{:S(2)}) %collective-permute-start.6) | collective-permute-done | bytes 528416 | tf_op jit(solution)/shard_map/ppermute | solution.py:44
  78.0 0.8 collective-permute-start.14
  78.8 1.6 collective-permute-start.17
  80.3 7.2 %shard_map.74 = (f32[33,64,128]{2,1,0:T(8,128)}, f32[8,128]{1,0:T(8,128)}) custom-call(s32[10]{0:T(128)} %stack.59.ids_ref, bf16[129,16,128]{2,1,0:T(8,128)(2,1)} %get-tuple-element.23.refs_0_.refs_1_, bf16[129,16,128]{2,1,0:T(8,128)(2,1)} %collective-permute-done.2.refs_1_.refs_2_, bf16[2,32,128,128]{3,2,1,0:T(8,128)(2,1)} %refs_9_.7, ...), custom_call_target="tpu_custom_call" | custom-call | flops 8165000192 | tf_op jit(solution)/shard_map/pallas_call | solution.py:398
  87.6 0.9 collective-permute-start.11
  88.4 2.9 %collective-permute-done.14.refs_0_ = bf16[32,64,128]{2,1,0:T(8,128)(2,1)} collective-permute-done((bf16[32,64,128]{2,1,0:T(8,128)(2,1)}, bf16[32,64,128]{2,1,0:T(8,128)(2,1)}, u32[]{:S(2)}, u32[]{:S(2)}) %collective-permute-start.14) | collective-permute-done | bytes 524320 | tf_op jit(solution)/shard_map/ppermute | solution.py:44
  91.3 5.0 %collective-permute-start.7 = (bf16[129,16,128]{2,1,0:T(8,128)(2,1)}, bf16[129,16,128]{2,1,0:T(8,128)(2,1)}, u32[]{:S(2)}, u32[]{:S(2)}) collective-permute-start(bf16[129,16,128]{2,1,0:T(8,128)(2,1)} %shard_map.69), channel_id=1, source_target_pairs={{0,12},{1,13},{2,14},{3,15},{4,8},{5,9},{6,10},{7,11},{8,4},{9,5},... | collective-permute-start | bytes 1585160 | tf_op jit(solution)/shard_map/ppermute | solution.py:44
  96.3 1.6 collective-permute-start.15
  98.0 7.3 %shard_map.75 = (f32[33,64,128]{2,1,0:T(8,128)}, f32[8,128]{1,0:T(8,128)}) custom-call(s32[10]{0:T(128)} %stack.59.ids_ref, bf16[129,16,128]{2,1,0:T(8,128)(2,1)} %copy-done.2, bf16[129,16,128]{2,1,0:T(8,128)(2,1)} %collective-permute-done.3.refs_1_.refs_3_, bf16[2,32,128,128]{3,2,1,0:T(8,128)(2,1)} %refs_9_.7, ...), custom_call_target="tpu_custom_call" | custom-call | flops 8165000192 | tf_op jit(solution)/shard_map/pallas_call | solution.py:398
  105.3 1.2 collective-permute-start.4
  106.6 2.0 collective-permute-done.7.refs_1_.refs_7_
  108.6 5.7 %collective-permute-start.8 = (bf16[129,16,128]{2,1,0:T(8,128)(2,1)}, bf16[129,16,128]{2,1,0:T(8,128)(2,1)}, u32[]{:S(2)}, u32[]{:S(2)}) collective-permute-start(bf16[129,16,128]{2,1,0:T(8,128)(2,1)} %shard_map.70), channel_id=1, source_target_pairs={{0,14},{1,15},{2,12},{3,13},{4,10},{5,11},{6,8},{7,9},{8,6},{9,7},... | collective-permute-start | bytes 1585160 | tf_op jit(solution)/shard_map/ppermute | solution.py:44
  114.3 23.5 %collective-permute-done.15.refs_6_ = bf16[32,64,128]{2,1,0:T(8,128)(2,1)} collective-permute-done((bf16[32,64,128]{2,1,0:T(8,128)(2,1)}, bf16[32,64,128]{2,1,0:T(8,128)(2,1)}, u32[]{:S(2)}, u32[]{:S(2)}) %collective-permute-start.15) | collective-permute-done | bytes 524320 | tf_op jit(solution)/shard_map/ppermute | solution.py:44
  137.8 7.2 %shard_map.76 = (f32[33,64,128]{2,1,0:T(8,128)}, f32[8,128]{1,0:T(8,128)}) custom-call(s32[10]{0:T(128)} %stack.59.ids_ref, bf16[129,16,128]{2,1,0:T(8,128)(2,1)} %copy-done.4, bf16[129,16,128]{2,1,0:T(8,128)(2,1)} %collective-permute-done.7.refs_1_.refs_7_, bf16[2,32,128,128]{3,2,1,0:T(8,128)(2,1)} %refs_9_.7, ...), custom_call_target="tpu_custom_call" | custom-call | flops 8165000192 | tf_op jit(solution)/shard_map/pallas_call | solution.py:398
  145.1 7.2 %shard_map.77 = (f32[32,64,128]{2,1,0:T(8,128)}, f32[16,128]{1,0:T(8,128)}) custom-call(s32[10]{0:T(128)} %stack.59.ids_ref, bf16[129,16,128]{2,1,0:T(8,128)(2,1)} %collective-permute-done.4.refs_0_.refs_4_, bf16[129,16,128]{2,1,0:T(8,128)(2,1)} %collective-permute-done.8.refs_1_.refs_8_, bf16[2,32,128,128]{3,2,1,0:T(8,128)(2,1)} %refs_9_.7, ...), custom_call_target="tpu_custom_call" | custom-call | flops 8165000192 | tf_op jit(solution)/shard_map/pallas_call | solution.py:398
  152.8 1.3 collective-permute-start.25
  154.9 1.8 collective-permute-done.25
  158.2 4.5 %collective-permute-start.28 = (f32[16,128]{1,0:T(8,128)S(1)}, f32[16,128]{1,0:T(8,128)S(1)}, u32[]{:S(2)}, u32[]{:S(2)}) collective-permute-start(f32[16,128]{1,0:T(8,128)S(1)} %add_add_fusion.1), channel_id=1, source_target_pairs={{0,8},{1,9},{2,10},{3,11},{4,12},{5,13},{6,14},{7,15},{8,0},{9,1},... | collective-permute-start | bytes 24584 | tf_op jit(solution)/shard_map/ppermute | solution.py:100
  163.4 0.9 collective-permute-done.28
  164.3 3.8 %collective-permute-done.29 = f32[16,128]{1,0:T(8,128)S(1)} collective-permute-done((f32[16,128]{1,0:T(8,128)S(1)}, f32[16,128]{1,0:T(8,128)S(1)}, u32[]{:S(2)}, u32[]{:S(2)}) %collective-permute-start.29) | collective-permute-done | bytes 8224 | tf_op jit(solution)/shard_map/ppermute | solution.py:100
  168.2 1.2 copy-done.1
  169.4 2.1 shard_map.78
  171.5 1.2 collective-permute-start.33
  172.7 0.9 collective-permute-start.30
  175.6 8.3 %collective-permute-done.33.refs_15_ = bf16[32,64,128]{2,1,0:T(8,128)(2,1)} collective-permute-done((bf16[32,64,128]{2,1,0:T(8,128)(2,1)S(1)}, bf16[32,64,128]{2,1,0:T(8,128)(2,1)}, u32[]{:S(2)}, u32[]{:S(2)}) %collective-permute-start.33) | collective-permute-done | bytes 524320 | tf_op jit(solution)/shard_map/ppermute | solution.py:44
  187.0 2.0 collective-permute-start.37
  189.0 0.8 copy-done.8
  189.8 0.8 copy-done.9
  190.6 7.8 %shard_map.79 = (f32[33,64,128]{2,1,0:T(8,128)}, f32[8,128]{1,0:T(8,128)}) custom-call(s32[10]{0:T(128)} %stack.59.ids_ref, s32[8,2,128]{2,1,0:T(2,128)} %convert_element_type.3.refs_0_, bf16[129,16,128]{2,1,0:T(8,128)(2,1)} %get-tuple-element.23.refs_0_.refs_1_, bf16[129,16,128]{2,1,0:T(8,128)(2,1)} %collective-permute-done.2.refs_1_.refs_2_, ...), custom_call_target="tpu_custom_call" | custom-call | flops 10234999808 | tf_op jit(solution)/shard_map/pallas_call | solution.py:398
  198.4 3.2 %collective-permute-done.31.refs_0_ = bf16[32,64,128]{2,1,0:T(8,128)(2,1)} collective-permute-done((bf16[32,64,128]{2,1,0:T(8,128)(2,1)}, bf16[32,64,128]{2,1,0:T(8,128)(2,1)}, u32[]{:S(2)}, u32[]{:S(2)}) %collective-permute-start.31) | collective-permute-done | bytes 524320 | tf_op jit(solution)/shard_map/ppermute | solution.py:44
  202.2 2.1 collective-permute-start.41
  204.6 7.2 %shard_map.81 = (f32[33,64,128]{2,1,0:T(8,128)}, f32[8,128]{1,0:T(8,128)}) custom-call(s32[10]{0:T(128)} %stack.59.ids_ref, s32[8,2,128]{2,1,0:T(2,128)} %convert_element_type.3.refs_0_, bf16[129,16,128]{2,1,0:T(8,128)(2,1)} %get-tuple-element.23.refs_0_.refs_1_, bf16[129,16,128]{2,1,0:T(8,128)(2,1)} %collective-permute-done.2.refs_1_.refs_2_, ...), custom_call_target="tpu_custom_call" | custom-call | flops 8165000192 | tf_op jit(solution)/shard_map/pallas_call | solution.py:398
  211.8 4.7 %collective-permute-done.36.refs_0_ = bf16[32,64,128]{2,1,0:T(8,128)(2,1)} collective-permute-done((bf16[32,64,128]{2,1,0:T(8,128)(2,1)}, bf16[32,64,128]{2,1,0:T(8,128)(2,1)}, u32[]{:S(2)}, u32[]{:S(2)}) %collective-permute-start.36) | collective-permute-done | bytes 524320 | tf_op jit(solution)/shard_map/ppermute | solution.py:44
  217.2 1.6 collective-permute-done.43.refs_14_
  219.5 7.2 %shard_map.83 = (f32[33,64,128]{2,1,0:T(8,128)}, f32[8,128]{1,0:T(8,128)}) custom-call(s32[10]{0:T(128)} %stack.59.ids_ref, s32[8,2,128]{2,1,0:T(2,128)} %convert_element_type.3.refs_0_, bf16[129,16,128]{2,1,0:T(8,128)(2,1)} %get-tuple-element.23.refs_0_.refs_1_, bf16[129,16,128]{2,1,0:T(8,128)(2,1)} %collective-permute-done.2.refs_1_.refs_2_, ...), custom_call_target="tpu_custom_call" | custom-call | flops 8165000192 | tf_op jit(solution)/shard_map/pallas_call | solution.py:398
  226.9 2.1 collective-permute-done.44.refs_12_
  229.0 4.7 %shard_map.85 = bf16[32,64,128]{2,1,0:T(8,128)(2,1)} custom-call(s32[10]{0:T(128)} %stack.59.ids_ref, s32[8,2,128]{2,1,0:T(2,128)} %convert_element_type.3.refs_0_, bf16[129,16,128]{2,1,0:T(8,128)(2,1)} %get-tuple-element.23.refs_0_.refs_1_, bf16[129,16,128]{2,1,0:T(8,128)(2,1)} %collective-permute-done.2.refs_1_.refs_2_, ...), custom_call_target="tpu_custom_call" | custom-call | flops 6095000064 | tf_op jit(solution)/shard_map/pallas_call | solution.py:398
  (98 shorter events, 15.5 us)
Async XLA Ops:
  2.0 7.2 %copy-start.6 = (s32[2,32]{1,0:T(2,128)S(1)}, s32[2,32]{1,0:T(2,128)}, u32[]{:S(2)}) copy-start(s32[2,32]{1,0:T(2,128)} %param.9) | copy-start | bytes 772
  2.1 7.2 %copy-start.7 = (s32[2,32,1]{1,2,0:T(1,128)S(1)}, s32[2,32,1]{1,2,0:T(1,128)}, u32[]{:S(2)}) copy-start(s32[2,32,1]{1,2,0:T(1,128)} %param.8) | copy-start | bytes 772
  2.1 9.5 %collective-permute-start.1 = (bf16[2,32,64,128]{3,2,1,0:T(8,128)(2,1)S(1)}, bf16[2,32,64,128]{3,2,1,0:T(8,128)(2,1)}, u32[]{:S(2)}, u32[]{:S(2)}) collective-permute-start(bf16[2,32,64,128]{3,2,1,0:T(8,128)(2,1)S(1)} %constant_dynamic-slice_fusion.2), channel_id=1, source_target_pairs={{0,1},{1,0},{2,3},{3,2},{4,5},{5,4},{6,7},{7,6},{8,9},{9,8},{10,11... | collective-permute-start | bytes 3145736 | tf_op jit(solution)/shard_map/ppermute | solution.py:44
  2.6 77.7 %collective-permute-start.9 = (bf16[2,32,128,128]{3,2,1,0:T(8,128)(2,1)}, bf16[2,32,128,128]{3,2,1,0:T(8,128)(2,1)}, u32[]{:S(2)}, u32[]{:S(2)}) collective-permute-start(bf16[2,32,128,128]{3,2,1,0:T(8,128)(2,1)} %refs_9_.7), channel_id=1, source_target_pairs={{0,1},{1,0},{2,3},{3,2},{4,5},{5,4},{6,7},{7,6},{8,9},{9,8},{10,11... | collective-permute-start | bytes 6291464 | tf_op jit(solution)/shard_map/ppermute | solution.py:44
  3.7 15.6 %collective-permute-start.22 = (bf16[32,64,128]{2,1,0:T(8,128)(2,1)}, bf16[32,64,128]{2,1,0:T(8,128)(2,1)}, u32[]{:S(2)}, u32[]{:S(2)}) collective-permute-start(bf16[32,64,128]{2,1,0:T(8,128)(2,1)} %get-tuple-element.45.refs_4_.refs_8_.wave_ref), channel_id=1, source_target_pairs={{0,2},{1,3},{2,0},{3,1},{4,6},{5,7},{6,4},{7,5},{8,10},{9,11},{10,... | collective-permute-start | bytes 1572872 | tf_op jit(solution)/shard_map/ppermute | solution.py:44
  6.7 38.5 %collective-permute-start.13 = (bf16[32,64,128]{2,1,0:T(8,128)(2,1)}, bf16[32,64,128]{2,1,0:T(8,128)(2,1)}, u32[]{:S(2)}, u32[]{:S(2)}) collective-permute-start(bf16[32,64,128]{2,1,0:T(8,128)(2,1)} %get-tuple-element.45.refs_4_.refs_8_.wave_ref), channel_id=1, source_target_pairs={{0,8},{1,9},{2,10},{3,11},{4,12},{5,13},{6,14},{7,15},{8,0},{9,1},... | collective-permute-start | bytes 1572872 | tf_op jit(solution)/shard_map/ppermute | solution.py:44
  9.9 1.2 collective-permute-start
  16.9 28.3 %collective-permute-start.2 = (bf16[129,16,128]{2,1,0:T(8,128)(2,1)}, bf16[129,16,128]{2,1,0:T(8,128)(2,1)}, u32[]{:S(2)}, u32[]{:S(2)}) collective-permute-start(bf16[129,16,128]{2,1,0:T(8,128)(2,1)} %get-tuple-element.24), channel_id=1, source_target_pairs={{0,2},{1,3},{2,0},{3,1},{4,6},{5,7},{6,4},{7,5},{8,10},{9,11},{10,... | collective-permute-start | bytes 1585160 | tf_op jit(solution)/shard_map/ppermute | solution.py:44
  17.5 50.4 %collective-permute-start.5 = (bf16[129,16,128]{2,1,0:T(8,128)(2,1)}, bf16[129,16,128]{2,1,0:T(8,128)(2,1)S(1)}, u32[]{:S(2)}, u32[]{:S(2)}) collective-permute-start(bf16[129,16,128]{2,1,0:T(8,128)(2,1)} %get-tuple-element.27), channel_id=1, source_target_pairs={{0,8},{1,9},{2,10},{3,11},{4,12},{5,13},{6,14},{7,15},{8,0},{9,1},... | collective-permute-start | bytes 1585160 | tf_op jit(solution)/shard_map/ppermute | solution.py:44
  19.3 26.7 %collective-permute-start.10 = (bf16[32,64,128]{2,1,0:T(8,128)(2,1)}, bf16[32,64,128]{2,1,0:T(8,128)(2,1)}, u32[]{:S(2)}, u32[]{:S(2)}) collective-permute-start(bf16[32,64,128]{2,1,0:T(8,128)(2,1)} %get-tuple-element.45.refs_4_.refs_8_.wave_ref), channel_id=1, source_target_pairs={{0,4},{1,5},{2,6},{3,7},{4,0},{5,1},{6,2},{7,3},{8,12},{9,13},{10,... | collective-permute-start | bytes 1572872 | tf_op jit(solution)/shard_map/ppermute | solution.py:44
  45.2 32.8 %collective-permute-start.6 = (bf16[129,16,128]{2,1,0:T(8,128)(2,1)}, bf16[129,16,128]{2,1,0:T(8,128)(2,1)S(1)}, u32[]{:S(2)}, u32[]{:S(2)}) collective-permute-start(bf16[129,16,128]{2,1,0:T(8,128)(2,1)} %get-tuple-element.28), channel_id=1, source_target_pairs={{0,10},{1,11},{2,8},{3,9},{4,14},{5,15},{6,12},{7,13},{8,2},{9,3},... | collective-permute-start | bytes 1585160 | tf_op jit(solution)/shard_map/ppermute | solution.py:44
  45.2 33.5 %collective-permute-start.23 = (bf16[32,64,128]{2,1,0:T(8,128)(2,1)}, bf16[32,64,128]{2,1,0:T(8,128)(2,1)}, u32[]{:S(2)}, u32[]{:S(2)}) collective-permute-start(bf16[32,64,128]{2,1,0:T(8,128)(2,1)} %collective-permute-done.22.refs_6_), channel_id=1, source_target_pairs={{0,1},{1,0},{2,3},{3,2},{4,5},{5,4},{6,7},{7,6},{8,9},{9,8},{10,11... | collective-permute-start | bytes 1572872 | tf_op jit(solution)/shard_map/ppermute | solution.py:44
  46.0 41.5 %collective-permute-start.3 = (bf16[129,16,128]{2,1,0:T(8,128)(2,1)}, bf16[129,16,128]{2,1,0:T(8,128)(2,1)}, u32[]{:S(2)}, u32[]{:S(2)}) collective-permute-start(bf16[129,16,128]{2,1,0:T(8,128)(2,1)} %get-tuple-element.25), channel_id=1, source_target_pairs={{0,4},{1,5},{2,6},{3,7},{4,0},{5,1},{6,2},{7,3},{8,12},{9,13},{10,... | collective-permute-start | bytes 1585160 | tf_op jit(solution)/shard_map/ppermute | solution.py:44
  67.9 28.4 %collective-permute-start.20 = (bf16[32,64,128]{2,1,0:T(8,128)(2,1)}, bf16[32,64,128]{2,1,0:T(8,128)(2,1)}, u32[]{:S(2)}, u32[]{:S(2)}) collective-permute-start(bf16[32,64,128]{2,1,0:T(8,128)(2,1)} %shard_map.72.refs_4_), channel_id=1, source_target_pairs={{0,1},{1,0},{2,3},{3,2},{4,5},{5,4},{6,7},{7,6},{8,9},{9,8},{10,11... | collective-permute-start | bytes 1572872 | tf_op jit(solution)/shard_map/ppermute | solution.py:44
  78.0 13.3 %collective-permute-start.14 = (bf16[32,64,128]{2,1,0:T(8,128)(2,1)}, bf16[32,64,128]{2,1,0:T(8,128)(2,1)}, u32[]{:S(2)}, u32[]{:S(2)}) collective-permute-start(bf16[32,64,128]{2,1,0:T(8,128)(2,1)} %shard_map.72.refs_4_), channel_id=1, source_target_pairs={{0,4},{1,5},{2,6},{3,7},{4,0},{5,1},{6,2},{7,3},{8,12},{9,13},{10,... | collective-permute-start | bytes 1572872 | tf_op jit(solution)/shard_map/ppermute | solution.py:44
  78.8 19.1 %collective-permute-start.17 = (bf16[32,64,128]{2,1,0:T(8,128)(2,1)}, bf16[32,64,128]{2,1,0:T(8,128)(2,1)}, u32[]{:S(2)}, u32[]{:S(2)}) collective-permute-start(bf16[32,64,128]{2,1,0:T(8,128)(2,1)} %shard_map.72.refs_4_), channel_id=1, source_target_pairs={{0,2},{1,3},{2,0},{3,1},{4,6},{5,7},{6,4},{7,5},{8,10},{9,11},{10,... | collective-permute-start | bytes 1572872 | tf_op jit(solution)/shard_map/ppermute | solution.py:44
  80.3 16.0 %collective-permute-start.21 = (bf16[32,64,128]{2,1,0:T(8,128)(2,1)}, bf16[32,64,128]{2,1,0:T(8,128)(2,1)}, u32[]{:S(2)}, u32[]{:S(2)}) collective-permute-start(bf16[32,64,128]{2,1,0:T(8,128)(2,1)} %shard_map.71.refs_6_), channel_id=1, source_target_pairs={{0,1},{1,0},{2,3},{3,2},{4,5},{5,4},{6,7},{7,6},{8,9},{9,8},{10,11... | collective-permute-start | bytes 1572872 | tf_op jit(solution)/shard_map/ppermute | solution.py:44
  87.6 17.8 %collective-permute-start.11 = (bf16[32,64,128]{2,1,0:T(8,128)(2,1)}, bf16[32,64,128]{2,1,0:T(8,128)(2,1)}, u32[]{:S(2)}, u32[]{:S(2)}) collective-permute-start(bf16[32,64,128]{2,1,0:T(8,128)(2,1)} %shard_map.71.refs_6_), channel_id=1, source_target_pairs={{0,2},{1,3},{2,0},{3,1},{4,6},{5,7},{6,4},{7,5},{8,10},{9,11},{10,... | collective-permute-start | bytes 1572872 | tf_op jit(solution)/shard_map/ppermute | solution.py:44
  91.3 17.3 %collective-permute-start.7 = (bf16[129,16,128]{2,1,0:T(8,128)(2,1)}, bf16[129,16,128]{2,1,0:T(8,128)(2,1)}, u32[]{:S(2)}, u32[]{:S(2)}) collective-permute-start(bf16[129,16,128]{2,1,0:T(8,128)(2,1)} %shard_map.69), channel_id=1, source_target_pairs={{0,12},{1,13},{2,14},{3,15},{4,8},{5,9},{6,10},{7,11},{8,4},{9,5},... | collective-permute-start | bytes 1585160 | tf_op jit(solution)/shard_map/ppermute | solution.py:44
  96.3 18.0 %collective-permute-start.19 = (bf16[32,64,128]{2,1,0:T(8,128)(2,1)}, bf16[32,64,128]{2,1,0:T(8,128)(2,1)}, u32[]{:S(2)}, u32[]{:S(2)}) collective-permute-start(bf16[32,64,128]{2,1,0:T(8,128)(2,1)} %shard_map.73.refs_6_), channel_id=1, source_target_pairs={{0,1},{1,0},{2,3},{3,2},{4,5},{5,4},{6,7},{7,6},{8,9},{9,8},{10,11... | collective-permute-start | bytes 1572872 | tf_op jit(solution)/shard_map/ppermute | solution.py:44
  96.3 41.5 %collective-permute-start.15 = (bf16[32,64,128]{2,1,0:T(8,128)(2,1)}, bf16[32,64,128]{2,1,0:T(8,128)(2,1)}, u32[]{:S(2)}, u32[]{:S(2)}) collective-permute-start(bf16[32,64,128]{2,1,0:T(8,128)(2,1)} %shard_map.73.refs_6_), channel_id=1, source_target_pairs={{0,2},{1,3},{2,0},{3,1},{4,6},{5,7},{6,4},{7,5},{8,10},{9,11},{10,... | collective-permute-start | bytes 1572872 | tf_op jit(solution)/shard_map/ppermute | solution.py:44
  97.9 39.9 %collective-permute-start.18 = (bf16[32,64,128]{2,1,0:T(8,128)(2,1)}, bf16[32,64,128]{2,1,0:T(8,128)(2,1)}, u32[]{:S(2)}, u32[]{:S(2)}) collective-permute-start(bf16[32,64,128]{2,1,0:T(8,128)(2,1)} %collective-permute-done.17.refs_4_), channel_id=1, source_target_pairs={{0,1},{1,0},{2,3},{3,2},{4,5},{5,4},{6,7},{7,6},{8,9},{9,8},{10,11... | collective-permute-start | bytes 1572872 | tf_op jit(solution)/shard_map/ppermute | solution.py:44
  105.3 39.7 %collective-permute-start.4 = (bf16[129,16,128]{2,1,0:T(8,128)(2,1)}, bf16[129,16,128]{2,1,0:T(8,128)(2,1)}, u32[]{:S(2)}, u32[]{:S(2)}) collective-permute-start(bf16[129,16,128]{2,1,0:T(8,128)(2,1)} %get-tuple-element.26), channel_id=1, source_target_pairs={{0,6},{1,7},{2,4},{3,5},{4,2},{5,3},{6,0},{7,1},{8,14},{9,15},{10,... | collective-permute-start | bytes 1585160 | tf_op jit(solution)/shard_map/ppermute | solution.py:44
  108.6 36.4 %collective-permute-start.8 = (bf16[129,16,128]{2,1,0:T(8,128)(2,1)}, bf16[129,16,128]{2,1,0:T(8,128)(2,1)}, u32[]{:S(2)}, u32[]{:S(2)}) collective-permute-start(bf16[129,16,128]{2,1,0:T(8,128)(2,1)} %shard_map.70), channel_id=1, source_target_pairs={{0,14},{1,15},{2,12},{3,13},{4,10},{5,11},{6,8},{7,9},{8,6},{9,7},... | collective-permute-start | bytes 1585160 | tf_op jit(solution)/shard_map/ppermute | solution.py:44
  114.2 30.8 %collective-permute-start.12 = (bf16[32,64,128]{2,1,0:T(8,128)(2,1)}, bf16[32,64,128]{2,1,0:T(8,128)(2,1)}, u32[]{:S(2)}, u32[]{:S(2)}) collective-permute-start(bf16[32,64,128]{2,1,0:T(8,128)(2,1)} %collective-permute-done.11.refs_4_), channel_id=1, source_target_pairs={{0,1},{1,0},{2,3},{3,2},{4,5},{5,4},{6,7},{7,6},{8,9},{9,8},{10,11... | collective-permute-start | bytes 1572872 | tf_op jit(solution)/shard_map/ppermute | solution.py:44
  137.8 7.3 %collective-permute-start.16 = (bf16[32,64,128]{2,1,0:T(8,128)(2,1)}, bf16[32,64,128]{2,1,0:T(8,128)(2,1)}, u32[]{:S(2)}, u32[]{:S(2)}) collective-permute-start(bf16[32,64,128]{2,1,0:T(8,128)(2,1)} %collective-permute-done.15.refs_6_), channel_id=1, source_target_pairs={{0,1},{1,0},{2,3},{3,2},{4,5},{5,4},{6,7},{7,6},{8,9},{9,8},{10,11... | collective-permute-start | bytes 1572872 | tf_op jit(solution)/shard_map/ppermute | solution.py:44
  152.3 2.6 %collective-permute-start.24 = (f32[16,128]{1,0:T(8,128)}, f32[16,128]{1,0:T(8,128)S(1)}, u32[]{:S(2)}, u32[]{:S(2)}) collective-permute-start(f32[16,128]{1,0:T(8,128)} %get-tuple-element.35), channel_id=1, source_target_pairs={{0,1},{1,0},{2,3},{3,2},{4,5},{5,4},{6,7},{7,6},{8,9},{9,8},{10,11... | collective-permute-start | bytes 24584 | tf_op jit(solution)/shard_map/ppermute | solution.py:100
  152.8 3.9 %collective-permute-start.25 = (f32[16,128]{1,0:T(8,128)}, f32[16,128]{1,0:T(8,128)S(1)}, u32[]{:S(2)}, u32[]{:S(2)}) collective-permute-start(f32[16,128]{1,0:T(8,128)} %get-tuple-element.35), channel_id=1, source_target_pairs={{0,2},{1,3},{2,0},{3,1},{4,6},{5,7},{6,4},{7,5},{8,10},{9,11},{10,... | collective-permute-start | bytes 24584 | tf_op jit(solution)/shard_map/ppermute | solution.py:100
  154.1 3.3 %collective-permute-start.26 = (f32[16,128]{1,0:T(8,128)}, f32[16,128]{1,0:T(8,128)S(1)}, u32[]{:S(2)}, u32[]{:S(2)}) collective-permute-start(f32[16,128]{1,0:T(8,128)} %get-tuple-element.35), channel_id=1, source_target_pairs={{0,3},{1,2},{2,1},{3,0},{4,7},{5,6},{6,5},{7,4},{8,11},{9,10},{10,... | collective-permute-start | bytes 24584 | tf_op jit(solution)/shard_map/ppermute | solution.py:100
  158.2 5.2 %collective-permute-start.27 = (f32[16,128]{1,0:T(8,128)S(1)}, f32[16,128]{1,0:T(8,128)S(1)}, u32[]{:S(2)}, u32[]{:S(2)}) collective-permute-start(f32[16,128]{1,0:T(8,128)S(1)} %add_add_fusion.1), channel_id=1, source_target_pairs={{0,4},{1,5},{2,6},{3,7},{4,0},{5,1},{6,2},{7,3},{8,12},{9,13},{10,... | collective-permute-start | bytes 24584 | tf_op jit(solution)/shard_map/ppermute | solution.py:100
  158.2 6.2 %collective-permute-start.28 = (f32[16,128]{1,0:T(8,128)S(1)}, f32[16,128]{1,0:T(8,128)S(1)}, u32[]{:S(2)}, u32[]{:S(2)}) collective-permute-start(f32[16,128]{1,0:T(8,128)S(1)} %add_add_fusion.1), channel_id=1, source_target_pairs={{0,8},{1,9},{2,10},{3,11},{4,12},{5,13},{6,14},{7,15},{8,0},{9,1},... | collective-permute-start | bytes 24584 | tf_op jit(solution)/shard_map/ppermute | solution.py:100
  162.7 5.4 %collective-permute-start.29 = (f32[16,128]{1,0:T(8,128)S(1)}, f32[16,128]{1,0:T(8,128)S(1)}, u32[]{:S(2)}, u32[]{:S(2)}) collective-permute-start(f32[16,128]{1,0:T(8,128)S(1)} %add_add_fusion.1), channel_id=1, source_target_pairs={{0,12},{1,13},{2,14},{3,15},{4,8},{5,9},{6,10},{7,11},{8,4},{9,5},... | collective-permute-start | bytes 24584 | tf_op jit(solution)/shard_map/ppermute | solution.py:100
  171.5 4.1 %copy-start = (bf16[32,64,128]{2,1,0:T(8,128)(2,1)}, bf16[32,64,128]{2,1,0:T(8,128)(2,1)S(1)}, u32[]{:S(2)}) copy-start(bf16[32,64,128]{2,1,0:T(8,128)(2,1)S(1)} %get-tuple-element.36.refs_11_) | copy-start | bytes 1572868
  171.5 12.3 %collective-permute-start.33 = (bf16[32,64,128]{2,1,0:T(8,128)(2,1)S(1)}, bf16[32,64,128]{2,1,0:T(8,128)(2,1)}, u32[]{:S(2)}, u32[]{:S(2)}) collective-permute-start(bf16[32,64,128]{2,1,0:T(8,128)(2,1)S(1)} %get-tuple-element.36.refs_11_), channel_id=1, source_target_pairs={{0,2},{1,5},{2,6},{3,1},{4,0},{5,9},{6,10},{7,3},{8,4},{9,13},{10,... | collective-permute-start | bytes 1572872 | tf_op jit(solution)/shard_map/ppermute | solution.py:44
  172.7 11.2 %collective-permute-start.30 = (bf16[32,64,128]{2,1,0:T(8,128)(2,1)S(1)}, bf16[32,64,128]{2,1,0:T(8,128)(2,1)}, u32[]{:S(2)}, u32[]{:S(2)}) collective-permute-start(bf16[32,64,128]{2,1,0:T(8,128)(2,1)S(1)} %get-tuple-element.36.refs_11_), channel_id=1, source_target_pairs={{0,4},{1,3},{2,0},{3,7},{4,8},{5,1},{6,2},{7,11},{8,12},{9,5},{10,... | collective-permute-start | bytes 1572872 | tf_op jit(solution)/shard_map/ppermute | solution.py:44
  175.6 13.4 %collective-permute-start.32 = (bf16[32,64,128]{2,1,0:T(8,128)(2,1)S(1)}, bf16[32,64,128]{2,1,0:T(8,128)(2,1)S(1)}, u32[]{:S(2)}, u32[]{:S(2)}) collective-permute-start(bf16[32,64,128]{2,1,0:T(8,128)(2,1)S(1)} %get-tuple-element.36.refs_11_), channel_id=1, source_target_pairs={{0,1},{1,0},{2,3},{3,2},{4,5},{5,4},{6,7},{7,6},{8,9},{9,8},{10,11... | collective-permute-start | bytes 1572872 | tf_op jit(solution)/shard_map/ppermute | solution.py:44
  183.8 6.0 %collective-permute-start.34 = (bf16[32,64,128]{2,1,0:T(8,128)(2,1)}, bf16[32,64,128]{2,1,0:T(8,128)(2,1)S(1)}, u32[]{:S(2)}, u32[]{:S(2)}) collective-permute-start(bf16[32,64,128]{2,1,0:T(8,128)(2,1)} %collective-permute-done.33.refs_15_), channel_id=1, source_target_pairs={{0,1},{1,0},{2,3},{3,2},{4,5},{5,4},{6,7},{7,6},{8,9},{9,8},{10,11... | collective-permute-start | bytes 1572872 | tf_op jit(solution)/shard_map/ppermute | solution.py:44
  183.8 6.8 %collective-permute-start.35 = (bf16[32,64,128]{2,1,0:T(8,128)(2,1)}, bf16[32,64,128]{2,1,0:T(8,128)(2,1)}, u32[]{:S(2)}, u32[]{:S(2)}) collective-permute-start(bf16[32,64,128]{2,1,0:T(8,128)(2,1)} %collective-permute-done.30.refs_13_), channel_id=1, source_target_pairs={{0,1},{1,0},{2,3},{3,2},{4,5},{5,4},{6,7},{7,6},{8,9},{9,8},{10,11... | collective-permute-start | bytes 1572872 | tf_op jit(solution)/shard_map/ppermute | solution.py:44
  187.0 14.7 %collective-permute-start.31 = (bf16[32,64,128]{2,1,0:T(8,128)(2,1)}, bf16[32,64,128]{2,1,0:T(8,128)(2,1)}, u32[]{:S(2)}, u32[]{:S(2)}) collective-permute-start(bf16[32,64,128]{2,1,0:T(8,128)(2,1)} %collective-permute-done.30.refs_13_), channel_id=1, source_target_pairs={{0,4},{1,3},{2,0},{3,7},{4,8},{5,1},{6,2},{7,11},{8,12},{9,5},{10,... | collective-permute-start | bytes 1572872 | tf_op jit(solution)/shard_map/ppermute | solution.py:44
  187.0 14.7 %collective-permute-start.37 = (bf16[32,64,128]{2,1,0:T(8,128)(2,1)}, bf16[32,64,128]{2,1,0:T(8,128)(2,1)}, u32[]{:S(2)}, u32[]{:S(2)}) collective-permute-start(bf16[32,64,128]{2,1,0:T(8,128)(2,1)} %collective-permute-done.33.refs_15_), channel_id=1, source_target_pairs={{0,2},{1,5},{2,6},{3,1},{4,0},{5,9},{6,10},{7,3},{8,4},{9,13},{10,... | collective-permute-start | bytes 1572872 | tf_op jit(solution)/shard_map/ppermute | solution.py:44
  201.6 2.6 %collective-permute-start.39 = (bf16[32,64,128]{2,1,0:T(8,128)(2,1)}, bf16[32,64,128]{2,1,0:T(8,128)(2,1)}, u32[]{:S(2)}, u32[]{:S(2)}) collective-permute-start(bf16[32,64,128]{2,1,0:T(8,128)(2,1)} %shard_map.80.refs_11_), channel_id=1, source_target_pairs={{0,1},{1,0},{2,3},{3,2},{4,5},{5,4},{6,7},{7,6},{8,9},{9,8},{10,11... | collective-permute-start | bytes 1572872 | tf_op jit(solution)/shard_map/ppermute | solution.py:44
  201.7 3.0 %collective-permute-start.38 = (bf16[32,64,128]{2,1,0:T(8,128)(2,1)}, bf16[32,64,128]{2,1,0:T(8,128)(2,1)}, u32[]{:S(2)}, u32[]{:S(2)}) collective-permute-start(bf16[32,64,128]{2,1,0:T(8,128)(2,1)} %collective-permute-done.37.refs_13_), channel_id=1, source_target_pairs={{0,1},{1,0},{2,3},{3,2},{4,5},{5,4},{6,7},{7,6},{8,9},{9,8},{10,11... | collective-permute-start | bytes 1572872 | tf_op jit(solution)/shard_map/ppermute | solution.py:44
  202.2 14.4 %collective-permute-start.36 = (bf16[32,64,128]{2,1,0:T(8,128)(2,1)}, bf16[32,64,128]{2,1,0:T(8,128)(2,1)}, u32[]{:S(2)}, u32[]{:S(2)}) collective-permute-start(bf16[32,64,128]{2,1,0:T(8,128)(2,1)} %shard_map.80.refs_11_), channel_id=1, source_target_pairs={{0,4},{1,3},{2,0},{3,7},{4,8},{5,1},{6,2},{7,11},{8,12},{9,5},{10,... | collective-permute-start | bytes 1572872 | tf_op jit(solution)/shard_map/ppermute | solution.py:44
  202.2 14.4 %collective-permute-start.41 = (bf16[32,64,128]{2,1,0:T(8,128)(2,1)}, bf16[32,64,128]{2,1,0:T(8,128)(2,1)}, u32[]{:S(2)}, u32[]{:S(2)}) collective-permute-start(bf16[32,64,128]{2,1,0:T(8,128)(2,1)} %collective-permute-done.37.refs_13_), channel_id=1, source_target_pairs={{0,2},{1,5},{2,6},{3,1},{4,0},{5,9},{6,10},{7,3},{8,4},{9,13},{10,... | collective-permute-start | bytes 1572872 | tf_op jit(solution)/shard_map/ppermute | solution.py:44
  216.5 2.3 collective-permute-start.43
  216.5 3.0 %collective-permute-start.42 = (bf16[32,64,128]{2,1,0:T(8,128)(2,1)}, bf16[32,64,128]{2,1,0:T(8,128)(2,1)}, u32[]{:S(2)}, u32[]{:S(2)}) collective-permute-start(bf16[32,64,128]{2,1,0:T(8,128)(2,1)} %collective-permute-done.41.refs_13_), channel_id=1, source_target_pairs={{0,1},{1,0},{2,3},{3,2},{4,5},{5,4},{6,7},{7,6},{8,9},{9,8},{10,11... | collective-permute-start | bytes 1572872 | tf_op jit(solution)/shard_map/ppermute | solution.py:44
  217.2 9.5 %collective-permute-start.40 = (bf16[32,64,128]{2,1,0:T(8,128)(2,1)}, bf16[32,64,128]{2,1,0:T(8,128)(2,1)}, u32[]{:S(2)}, u32[]{:S(2)}) collective-permute-start(bf16[32,64,128]{2,1,0:T(8,128)(2,1)} %shard_map.82.refs_11_), channel_id=1, source_target_pairs={{0,4},{1,3},{2,0},{3,7},{4,8},{5,1},{6,2},{7,11},{8,12},{9,5},{10,... | collective-permute-start | bytes 1572872 | tf_op jit(solution)/shard_map/ppermute | solution.py:44
  226.7 2.3 collective-permute-start.44
  (8 other events, 7.6 us)

commit v20 on v16

--- a/solution.py
+++ b/solution.py
@@ -8,7 +8,7 @@
 from jax.sharding import PartitionSpec as P
 
 BOTH = ("sec", "term")
-VMEM_LIMIT = 60 * 2**20
+VMEM_LIMIT = 64 * 2**20
 PART = 16
 ORDER = [0, 4, 5, 1, 2, 6, 3, 7]
 WAITS = {4: 1, 2: 5, 6: 2}

time: 234 us -> 232 us (level)
  local copies, waits for them, and re-layouts: 12.4 us -> 7.13 us
  waiting for transfers between devices: 115 us -> 119 us
    unnamed x80 -> x26, local copies, waits for them, and re-layouts: 9.4 us -> 4.02 us
    ppermute x39, waiting for transfers between devices: 108 us -> 113 us  [permute(): return lax.ppermute(value, BOTH, pairs)]
  transfers between devices with their start and end apart: 45 -> 45, of which waited for: 21 -> 19; matrix products, arithmetic and copies ran while one was open for 1% -> 1% of each run, Pallas kernels for 22% -> 22%
where the time goes in v20:
time: 232 us; the launch traced here: 231 us
  waiting for transfers between devices  119 us (51%)
  Pallas kernels  64.3 us (28%)
  starting transfers between devices  37.8 us (16%)
  local copies, waits for them, and re-layouts  7.13 us (3%)
    ppermute x39, waiting for transfers between devices, permute(): return lax.ppermute(value, BOTH, pairs)  113 us
    pallas_call x8, Pallas kernels, apply_group(): pl.pallas_call(functools.partial(apply_kernel, sources, choices, chosen,...  56.8 us
    ppermute x39, starting transfers between devices, permute(): return lax.ppermute(value, BOTH, pairs)  30.1 us
    ppermute x6, starting transfers between devices, spread(): lax.ppermute(value, BOTH, [(d, d ^ m) for d in range(devices)])  7.7 us
    ppermute x6, waiting for transfers between devices, spread(): lax.ppermute(value, BOTH, [(d, d ^ m) for d in range(devices)])  6.05 us
    pallas_call x1, Pallas kernels, pack(): pl.pallas_call(functools.partial(pack_kernel, order, capacity, blocks, te...  5.35 us
  transfers between devices with their start and end apart: 45, of which 19 were waited for; matrix products, arithmetic and copies ran while one was open for 1% of the time, Pallas kernels for 22%

profile of v20, /device:TPU:0, one launch (start us, length us, event | category | flops | bytes accessed | tf_op | source)
XLA Modules:
  0.0 230.8 jit_solution(16439874164898491925)
XLA Ops:
  0.6 1.4 constant_dynamic-slice_fusion.2
  2.7 1.0 constant_dynamic-slice_fusion
  3.7 4.0 %collective-permute-start.13 = (bf16[32,64,128]{2,1,0:T(8,128)(2,1)}, bf16[32,64,128]{2,1,0:T(8,128)(2,1)}, u32[]{:S(2)}, u32[]{:S(2)}) collective-permute-start(bf16[32,64,128]{2,1,0:T(8,128)(2,1)} %get-tuple-element.45.refs_4_.refs_8_.wave_ref), channel_id=1, source_target_pairs={{0,8},{1,9},{2,10},{3,11},{4,12},{5,13},{6,14},{7,15},{8,0},{9,1},... | collective-permute-start | bytes 1572872 | tf_op jit(solution)/shard_map/ppermute | solution.py:44
  7.7 1.5 collective-permute-start.21
  11.6 5.4 %shard_map.68 = (bf16[129,16,128]{2,1,0:T(8,128)(2,1)}, bf16[129,16,128]{2,1,0:T(8,128)(2,1)}, bf16[129,16,128]{2,1,0:T(8,128)(2,1)}, bf16[129,16,128]{2,1,0:T(8...) custom-call(s32[2]{0:T(128)} %pad_add_fusion.1.ids_ref, ...), custom_call_target="tpu_custom_call" | custom-call | flops 5750000128 | tf_op jit(solution)/shard_map/pallas_call | solution.py:167
  17.5 1.6 collective-permute-start.10
  19.1 12.5 %collective-permute-done.13.refs_0_ = bf16[32,64,128]{2,1,0:T(8,128)(2,1)} collective-permute-done((bf16[32,64,128]{2,1,0:T(8,128)(2,1)}, bf16[32,64,128]{2,1,0:T(8,128)(2,1)}, u32[]{:S(2)}, u32[]{:S(2)}) %collective-permute-start.13) | collective-permute-done | bytes 524320 | tf_op jit(solution)/shard_map/ppermute | solution.py:44
  31.6 3.9 %collective-permute-start.6 = (bf16[129,16,128]{2,1,0:T(8,128)(2,1)}, bf16[129,16,128]{2,1,0:T(8,128)(2,1)S(1)}, u32[]{:S(2)}, u32[]{:S(2)}) collective-permute-start(bf16[129,16,128]{2,1,0:T(8,128)(2,1)} %get-tuple-element.28), channel_id=1, source_target_pairs={{0,10},{1,11},{2,8},{3,9},{4,14},{5,15},{6,12},{7,13},{8,2},{9,3},... | collective-permute-start | bytes 1585160 | tf_op jit(solution)/shard_map/ppermute | solution.py:44
  35.5 1.1 collective-permute-start.3
  36.6 7.5 %collective-permute-done.10.refs_0_ = bf16[32,64,128]{2,1,0:T(8,128)(2,1)} collective-permute-done((bf16[32,64,128]{2,1,0:T(8,128)(2,1)}, bf16[32,64,128]{2,1,0:T(8,128)(2,1)}, u32[]{:S(2)}, u32[]{:S(2)}) %collective-permute-start.10) | collective-permute-done | bytes 524320 | tf_op jit(solution)/shard_map/ppermute | solution.py:44
  44.1 26.2 %collective-permute-done.5.refs_1_.refs_4_ = bf16[129,16,128]{2,1,0:T(8,128)(2,1)S(1)} collective-permute-done((bf16[129,16,128]{2,1,0:T(8,128)(2,1)}, bf16[129,16,128]{2,1,0:T(8,128)(2,1)S(1)}, u32[]{:S(2)}, u32[]{:S(2)}) %collective-permute-start.5) | collective-permute-done | bytes 528416 | tf_op jit(solution)/shard_map/ppermute | solution.py:44
  70.4 10.5 %collective-permute-done.6.refs_1_.refs_0_.refs_5_ = bf16[129,16,128]{2,1,0:T(8,128)(2,1)S(1)} collective-permute-done((bf16[129,16,128]{2,1,0:T(8,128)(2,1)}, bf16[129,16,128]{2,1,0:T(8,128)(2,1)S(1)}, u32[]{:S(2)}, u32[]{:S(2)}) %collective-permute-start.6) | collective-permute-done | bytes 528416 | tf_op jit(solution)/shard_map/ppermute | solution.py:44
  82.4 4.4 %collective-permute-done.14.refs_0_ = bf16[32,64,128]{2,1,0:T(8,128)(2,1)} collective-permute-done((bf16[32,64,128]{2,1,0:T(8,128)(2,1)}, bf16[32,64,128]{2,1,0:T(8,128)(2,1)}, u32[]{:S(2)}, u32[]{:S(2)}) %collective-permute-start.14) | collective-permute-done | bytes 524320 | tf_op jit(solution)/shard_map/ppermute | solution.py:44
  86.8 1.6 collective-permute-start.11
  88.5 2.8 %collective-permute-start.7 = (bf16[129,16,128]{2,1,0:T(8,128)(2,1)}, bf16[129,16,128]{2,1,0:T(8,128)(2,1)}, u32[]{:S(2)}, u32[]{:S(2)}) collective-permute-start(bf16[129,16,128]{2,1,0:T(8,128)(2,1)} %shard_map.69), channel_id=1, source_target_pairs={{0,12},{1,13},{2,14},{3,15},{4,8},{5,9},{6,10},{7,11},{8,4},{9,5},... | collective-permute-start | bytes 1585160 | tf_op jit(solution)/shard_map/ppermute | solution.py:44
  91.3 4.8 %collective-permute-done.19.refs_4_ = bf16[32,64,128]{2,1,0:T(8,128)(2,1)} collective-permute-done((bf16[32,64,128]{2,1,0:T(8,128)(2,1)}, bf16[32,64,128]{2,1,0:T(8,128)(2,1)}, u32[]{:S(2)}, u32[]{:S(2)}) %collective-permute-start.19) | collective-permute-done | bytes 524320 | tf_op jit(solution)/shard_map/ppermute | solution.py:44
  96.1 7.5 %shard_map.74 = (f32[33,64,128]{2,1,0:T(8,128)}, f32[8,128]{1,0:T(8,128)}) custom-call(s32[10]{0:T(128)} %stack.56.ids_ref, bf16[129,16,128]{2,1,0:T(8,128)(2,1)} %get-tuple-element.23.refs_0_, bf16[129,16,128]{2,1,0:T(8,128)(2,1)} %copy-done.5, bf16[2,32,128,128]{3,2,1,0:T(8,128)(2,1)} %refs_8_.7, ...), custom_call_target="tpu_custom_call" | custom-call | flops 8165000192 | tf_op jit(solution)/shard_map/pallas_call | solution.py:391
  104.2 0.8 collective-permute-start.15
  105.0 7.5 %shard_map.75 = (f32[33,64,128]{2,1,0:T(8,128)}, f32[8,128]{1,0:T(8,128)}) custom-call(s32[10]{0:T(128)} %stack.56.ids_ref, bf16[129,16,128]{2,1,0:T(8,128)(2,1)} %copy-done.2, bf16[129,16,128]{2,1,0:T(8,128)(2,1)} %copy-done.4, bf16[2,32,128,128]{3,2,1,0:T(8,128)(2,1)} %refs_8_.7, bf16[2,32,128,128]{3,2,1,0:T(8,128)(2,1)} %collective-permute-done.9.refs_3_.refs_9_, ...), custom_call_target="tpu_custom_call" | custom-call | flops 8165000192 | tf_op jit(solution)/shard_map/pallas_call | solution.py:391
  112.5 1.3 collective-permute-start.8
  113.8 15.9 %collective-permute-done.15.refs_6_ = bf16[32,64,128]{2,1,0:T(8,128)(2,1)} collective-permute-done((bf16[32,64,128]{2,1,0:T(8,128)(2,1)}, bf16[32,64,128]{2,1,0:T(8,128)(2,1)}, u32[]{:S(2)}, u32[]{:S(2)}) %collective-permute-start.15) | collective-permute-done | bytes 524320 | tf_op jit(solution)/shard_map/ppermute | solution.py:44
  129.7 7.4 %shard_map.76 = (f32[33,64,128]{2,1,0:T(8,128)}, f32[8,128]{1,0:T(8,128)}) custom-call(s32[10]{0:T(128)} %stack.56.ids_ref, bf16[129,16,128]{2,1,0:T(8,128)(2,1)} %copy-done.6, bf16[129,16,128]{2,1,0:T(8,128)(2,1)} %collective-permute-done.7.refs_1_.refs_6_, bf16[2,32,128,128]{3,2,1,0:T(8,128)(2,1)} %refs_8_.7, ...), custom_call_target="tpu_custom_call" | custom-call | flops 8165000192 | tf_op jit(solution)/shard_map/pallas_call | solution.py:391
  137.2 7.6 %collective-permute-done.8.refs_1_.refs_7_ = bf16[129,16,128]{2,1,0:T(8,128)(2,1)} collective-permute-done((bf16[129,16,128]{2,1,0:T(8,128)(2,1)}, bf16[129,16,128]{2,1,0:T(8,128)(2,1)}, u32[]{:S(2)}, u32[]{:S(2)}) %collective-permute-start.8) | collective-permute-done | bytes 528416 | tf_op jit(solution)/shard_map/ppermute | solution.py:44
  144.8 7.4 %shard_map.77 = (f32[32,64,128]{2,1,0:T(8,128)}, f32[16,128]{1,0:T(8,128)}) custom-call(s32[10]{0:T(128)} %stack.56.ids_ref, bf16[129,16,128]{2,1,0:T(8,128)(2,1)} %collective-permute-done.4.refs_0_.refs_3_, bf16[129,16,128]{2,1,0:T(8,128)(2,1)} %collective-permute-done.8.refs_1_.refs_7_, bf16[2,32,128,128]{3,2,1,0:T(8,128)(2,1)} %refs_8_.7, ...), custom_call_target="tpu_custom_call" | custom-call | flops 8165000192 | tf_op jit(solution)/shard_map/pallas_call | solution.py:391
  152.8 1.4 collective-permute-start.26
  154.1 2.1 collective-permute-done.25
  156.9 3.2 %collective-permute-start.27 = (f32[16,128]{1,0:T(8,128)S(1)}, f32[16,128]{1,0:T(8,128)S(1)}, u32[]{:S(2)}, u32[]{:S(2)}) collective-permute-start(f32[16,128]{1,0:T(8,128)S(1)} %add_add_fusion.1), channel_id=1, source_target_pairs={{0,4},{1,5},{2,6},{3,7},{4,0},{5,1},{6,2},{7,3},{8,12},{9,13},{10,... | collective-permute-start | bytes 24584 | tf_op jit(solution)/shard_map/ppermute | solution.py:100
  160.1 1.1 collective-permute-start.28
  161.2 1.5 collective-permute-start.29
  162.7 1.9 collective-permute-done.28
  164.6 2.0 collective-permute-done.29
  166.7 1.2 copy-done.1
  167.9 2.1 shard_map.78
  170.7 1.4 collective-permute-start.30
  172.0 10.6 %collective-permute-done.33.refs_14_ = bf16[32,64,128]{2,1,0:T(8,128)(2,1)} collective-permute-done((bf16[32,64,128]{2,1,0:T(8,128)(2,1)S(1)}, bf16[32,64,128]{2,1,0:T(8,128)(2,1)}, u32[]{:S(2)}, u32[]{:S(2)}) %collective-permute-start.33) | collective-permute-done | bytes 524320 | tf_op jit(solution)/shard_map/ppermute | solution.py:44
  183.8 1.5 collective-permute-start.37
  185.2 0.8 copy-done.10
  186.0 0.8 copy-done.11
  186.8 8.0 %shard_map.79 = (f32[33,64,128]{2,1,0:T(8,128)}, f32[8,128]{1,0:T(8,128)}) custom-call(s32[10]{0:T(128)} %stack.56.ids_ref, bf16[129,16,128]{2,1,0:T(8,128)(2,1)} %get-tuple-element.23.refs_0_, bf16[129,16,128]{2,1,0:T(8,128)(2,1)} %copy-done.4, bf16[129,16,128]{2,1,0:T(8,128)(2,1)} %copy-done.6, ...), custom_call_target="tpu_custom_call" | custom-call | flops 10234999808 | tf_op jit(solution)/shard_map/pallas_call | solution.py:391
  194.9 3.0 %collective-permute-done.31.refs_0_ = bf16[32,64,128]{2,1,0:T(8,128)(2,1)} collective-permute-done((bf16[32,64,128]{2,1,0:T(8,128)(2,1)}, bf16[32,64,128]{2,1,0:T(8,128)(2,1)}, u32[]{:S(2)}, u32[]{:S(2)}) %collective-permute-start.31) | collective-permute-done | bytes 524320 | tf_op jit(solution)/shard_map/ppermute | solution.py:44
  198.4 0.8 collective-permute-start.36
  199.2 1.3 collective-permute-start.41
  200.9 6.9 %shard_map.81 = (f32[33,64,128]{2,1,0:T(8,128)}, f32[8,128]{1,0:T(8,128)}) custom-call(s32[10]{0:T(128)} %stack.56.ids_ref, bf16[129,16,128]{2,1,0:T(8,128)(2,1)} %get-tuple-element.23.refs_0_, bf16[129,16,128]{2,1,0:T(8,128)(2,1)} %copy-done.4, bf16[129,16,128]{2,1,0:T(8,128)(2,1)} %copy-done.6, ...), custom_call_target="tpu_custom_call" | custom-call | flops 8165000192 | tf_op jit(solution)/shard_map/pallas_call | solution.py:391
  207.8 5.4 %collective-permute-done.36.refs_0_ = bf16[32,64,128]{2,1,0:T(8,128)(2,1)} collective-permute-done((bf16[32,64,128]{2,1,0:T(8,128)(2,1)}, bf16[32,64,128]{2,1,0:T(8,128)(2,1)}, u32[]{:S(2)}, u32[]{:S(2)}) %collective-permute-start.36) | collective-permute-done | bytes 524320 | tf_op jit(solution)/shard_map/ppermute | solution.py:44
  213.7 1.0 collective-permute-start.40
  216.2 7.2 %shard_map.83 = (f32[33,64,128]{2,1,0:T(8,128)}, f32[8,128]{1,0:T(8,128)}) custom-call(s32[10]{0:T(128)} %stack.56.ids_ref, bf16[129,16,128]{2,1,0:T(8,128)(2,1)} %get-tuple-element.23.refs_0_, bf16[129,16,128]{2,1,0:T(8,128)(2,1)} %copy-done.4, bf16[129,16,128]{2,1,0:T(8,128)(2,1)} %copy-done.6, ...), custom_call_target="tpu_custom_call" | custom-call | flops 8165000192 | tf_op jit(solution)/shard_map/pallas_call | solution.py:391
  223.5 2.2 collective-permute-done.44.refs_11_
  225.8 4.9 %shard_map.85 = bf16[32,64,128]{2,1,0:T(8,128)(2,1)} custom-call(s32[10]{0:T(128)} %stack.56.ids_ref, bf16[129,16,128]{2,1,0:T(8,128)(2,1)} %get-tuple-element.23.refs_0_, bf16[129,16,128]{2,1,0:T(8,128)(2,1)} %copy-done.4, bf16[129,16,128]{2,1,0:T(8,128)(2,1)} %copy-done.6, bf16[129,16,128]{2,1,0:T(8,128)(2,1)} %collective-permute-done.4.refs_0_.refs_3_, ...), custom_call_target="tpu_custom_call" | custom-call | flops 6095000064 | tf_op jit(solution)/shard_map/pallas_call | solution.py:391
  (93 shorter events, 11.9 us)
Async XLA Ops:
  2.0 7.2 %copy-start.8 = (s32[2,32]{1,0:T(2,128)S(1)}, s32[2,32]{1,0:T(2,128)}, u32[]{:S(2)}) copy-start(s32[2,32]{1,0:T(2,128)} %param.9) | copy-start | bytes 772
  2.1 7.2 %copy-start.9 = (s32[2,32,1]{1,2,0:T(1,128)S(1)}, s32[2,32,1]{1,2,0:T(1,128)}, u32[]{:S(2)}) copy-start(s32[2,32,1]{1,2,0:T(1,128)} %param.8) | copy-start | bytes 772
  2.1 9.5 %collective-permute-start.1 = (bf16[2,32,64,128]{3,2,1,0:T(8,128)(2,1)S(1)}, bf16[2,32,64,128]{3,2,1,0:T(8,128)(2,1)}, u32[]{:S(2)}, u32[]{:S(2)}) collective-permute-start(bf16[2,32,64,128]{3,2,1,0:T(8,128)(2,1)S(1)} %constant_dynamic-slice_fusion.2), channel_id=1, source_target_pairs={{0,1},{1,0},{2,3},{3,2},{4,5},{5,4},{6,7},{7,6},{8,9},{9,8},{10,11... | collective-permute-start | bytes 3145736 | tf_op jit(solution)/shard_map/ppermute | solution.py:44
  2.6 84.3 %collective-permute-start.9 = (bf16[2,32,128,128]{3,2,1,0:T(8,128)(2,1)}, bf16[2,32,128,128]{3,2,1,0:T(8,128)(2,1)}, u32[]{:S(2)}, u32[]{:S(2)}) collective-permute-start(bf16[2,32,128,128]{3,2,1,0:T(8,128)(2,1)} %refs_8_.7), channel_id=1, source_target_pairs={{0,1},{1,0},{2,3},{3,2},{4,5},{5,4},{6,7},{7,6},{8,9},{9,8},{10,11... | collective-permute-start | bytes 6291464 | tf_op jit(solution)/shard_map/ppermute | solution.py:44
  3.7 27.8 %collective-permute-start.13 = (bf16[32,64,128]{2,1,0:T(8,128)(2,1)}, bf16[32,64,128]{2,1,0:T(8,128)(2,1)}, u32[]{:S(2)}, u32[]{:S(2)}) collective-permute-start(bf16[32,64,128]{2,1,0:T(8,128)(2,1)} %get-tuple-element.45.refs_4_.refs_8_.wave_ref), channel_id=1, source_target_pairs={{0,8},{1,9},{2,10},{3,11},{4,12},{5,13},{6,14},{7,15},{8,0},{9,1},... | collective-permute-start | bytes 1572872 | tf_op jit(solution)/shard_map/ppermute | solution.py:44
  7.7 23.8 %collective-permute-start.21 = (bf16[32,64,128]{2,1,0:T(8,128)(2,1)}, bf16[32,64,128]{2,1,0:T(8,128)(2,1)}, u32[]{:S(2)}, u32[]{:S(2)}) collective-permute-start(bf16[32,64,128]{2,1,0:T(8,128)(2,1)} %get-tuple-element.45.refs_4_.refs_8_.wave_ref), channel_id=1, source_target_pairs={{0,2},{1,3},{2,0},{3,1},{4,6},{5,7},{6,4},{7,5},{8,10},{9,11},{10,... | collective-permute-start | bytes 1572872 | tf_op jit(solution)/shard_map/ppermute | solution.py:44
  9.9 1.2 collective-permute-start
  17.0 18.5 %collective-permute-start.2 = (bf16[129,16,128]{2,1,0:T(8,128)(2,1)}, bf16[129,16,128]{2,1,0:T(8,128)(2,1)S(1)}, u32[]{:S(2)}, u32[]{:S(2)}) collective-permute-start(bf16[129,16,128]{2,1,0:T(8,128)(2,1)} %get-tuple-element.24), channel_id=1, source_target_pairs={{0,2},{1,3},{2,0},{3,1},{4,6},{5,7},{6,4},{7,5},{8,10},{9,11},{10,... | collective-permute-start | bytes 1585160 | tf_op jit(solution)/shard_map/ppermute | solution.py:44
  17.5 26.6 %collective-permute-start.10 = (bf16[32,64,128]{2,1,0:T(8,128)(2,1)}, bf16[32,64,128]{2,1,0:T(8,128)(2,1)}, u32[]{:S(2)}, u32[]{:S(2)}) collective-permute-start(bf16[32,64,128]{2,1,0:T(8,128)(2,1)} %get-tuple-element.45.refs_4_.refs_8_.wave_ref), channel_id=1, source_target_pairs={{0,4},{1,5},{2,6},{3,7},{4,0},{5,1},{6,2},{7,3},{8,12},{9,13},{10,... | collective-permute-start | bytes 1572872 | tf_op jit(solution)/shard_map/ppermute | solution.py:44
  31.6 38.8 %collective-permute-start.5 = (bf16[129,16,128]{2,1,0:T(8,128)(2,1)}, bf16[129,16,128]{2,1,0:T(8,128)(2,1)S(1)}, u32[]{:S(2)}, u32[]{:S(2)}) collective-permute-start(bf16[129,16,128]{2,1,0:T(8,128)(2,1)} %get-tuple-element.27), channel_id=1, source_target_pairs={{0,8},{1,9},{2,10},{3,11},{4,12},{5,13},{6,14},{7,15},{8,0},{9,1},... | collective-permute-start | bytes 1585160 | tf_op jit(solution)/shard_map/ppermute | solution.py:44
  31.6 49.3 %collective-permute-start.6 = (bf16[129,16,128]{2,1,0:T(8,128)(2,1)}, bf16[129,16,128]{2,1,0:T(8,128)(2,1)S(1)}, u32[]{:S(2)}, u32[]{:S(2)}) collective-permute-start(bf16[129,16,128]{2,1,0:T(8,128)(2,1)} %get-tuple-element.28), channel_id=1, source_target_pairs={{0,10},{1,11},{2,8},{3,9},{4,14},{5,15},{6,12},{7,13},{8,2},{9,3},... | collective-permute-start | bytes 1585160 | tf_op jit(solution)/shard_map/ppermute | solution.py:44
  35.5 46.8 %collective-permute-start.3 = (bf16[129,16,128]{2,1,0:T(8,128)(2,1)}, bf16[129,16,128]{2,1,0:T(8,128)(2,1)S(1)}, u32[]{:S(2)}, u32[]{:S(2)}) collective-permute-start(bf16[129,16,128]{2,1,0:T(8,128)(2,1)} %get-tuple-element.25), channel_id=1, source_target_pairs={{0,4},{1,5},{2,6},{3,7},{4,0},{5,1},{6,2},{7,3},{8,12},{9,13},{10,... | collective-permute-start | bytes 1585160 | tf_op jit(solution)/shard_map/ppermute | solution.py:44
  44.1 42.7 %collective-permute-start.14 = (bf16[32,64,128]{2,1,0:T(8,128)(2,1)}, bf16[32,64,128]{2,1,0:T(8,128)(2,1)}, u32[]{:S(2)}, u32[]{:S(2)}) collective-permute-start(bf16[32,64,128]{2,1,0:T(8,128)(2,1)} %shard_map.72.refs_6_), channel_id=1, source_target_pairs={{0,4},{1,5},{2,6},{3,7},{4,0},{5,1},{6,2},{7,3},{8,12},{9,13},{10,... | collective-permute-start | bytes 1572872 | tf_op jit(solution)/shard_map/ppermute | solution.py:44
  70.4 12.0 %copy-start.5 = (bf16[129,16,128]{2,1,0:T(8,128)(2,1)}, bf16[129,16,128]{2,1,0:T(8,128)(2,1)S(1)}, u32[]{:S(2)}) copy-start(bf16[129,16,128]{2,1,0:T(8,128)(2,1)S(1)} %collective-permute-done.5.refs_1_.refs_4_) | copy-start | bytes 1585156
  70.4 18.1 %collective-permute-start.23 = (bf16[32,64,128]{2,1,0:T(8,128)(2,1)}, bf16[32,64,128]{2,1,0:T(8,128)(2,1)}, u32[]{:S(2)}, u32[]{:S(2)}) collective-permute-start(bf16[32,64,128]{2,1,0:T(8,128)(2,1)} %shard_map.72.refs_6_), channel_id=1, source_target_pairs={{0,1},{1,0},{2,3},{3,2},{4,5},{5,4},{6,7},{7,6},{8,9},{9,8},{10,11... | collective-permute-start | bytes 1572872 | tf_op jit(solution)/shard_map/ppermute | solution.py:44
  80.9 15.2 %collective-permute-start.19 = (bf16[32,64,128]{2,1,0:T(8,128)(2,1)}, bf16[32,64,128]{2,1,0:T(8,128)(2,1)}, u32[]{:S(2)}, u32[]{:S(2)}) collective-permute-start(bf16[32,64,128]{2,1,0:T(8,128)(2,1)} %shard_map.72.refs_6_), channel_id=1, source_target_pairs={{0,2},{1,3},{2,0},{3,1},{4,6},{5,7},{6,4},{7,5},{8,10},{9,11},{10,... | collective-permute-start | bytes 1572872 | tf_op jit(solution)/shard_map/ppermute | solution.py:44
  82.4 21.2 %collective-permute-start.22 = (bf16[32,64,128]{2,1,0:T(8,128)(2,1)}, bf16[32,64,128]{2,1,0:T(8,128)(2,1)}, u32[]{:S(2)}, u32[]{:S(2)}) collective-permute-start(bf16[32,64,128]{2,1,0:T(8,128)(2,1)} %collective-permute-done.21.refs_6_), channel_id=1, source_target_pairs={{0,1},{1,0},{2,3},{3,2},{4,5},{5,4},{6,7},{7,6},{8,9},{9,8},{10,11... | collective-permute-start | bytes 1572872 | tf_op jit(solution)/shard_map/ppermute | solution.py:44
  86.8 25.6 %collective-permute-start.17 = (bf16[32,64,128]{2,1,0:T(8,128)(2,1)}, bf16[32,64,128]{2,1,0:T(8,128)(2,1)}, u32[]{:S(2)}, u32[]{:S(2)}) collective-permute-start(bf16[32,64,128]{2,1,0:T(8,128)(2,1)} %shard_map.71.refs_4_), channel_id=1, source_target_pairs={{0,1},{1,0},{2,3},{3,2},{4,5},{5,4},{6,7},{7,6},{8,9},{9,8},{10,11... | collective-permute-start | bytes 1572872 | tf_op jit(solution)/shard_map/ppermute | solution.py:44
  86.8 25.7 %collective-permute-start.11 = (bf16[32,64,128]{2,1,0:T(8,128)(2,1)}, bf16[32,64,128]{2,1,0:T(8,128)(2,1)}, u32[]{:S(2)}, u32[]{:S(2)}) collective-permute-start(bf16[32,64,128]{2,1,0:T(8,128)(2,1)} %shard_map.71.refs_4_), channel_id=1, source_target_pairs={{0,2},{1,3},{2,0},{3,1},{4,6},{5,7},{6,4},{7,5},{8,10},{9,11},{10,... | collective-permute-start | bytes 1572872 | tf_op jit(solution)/shard_map/ppermute | solution.py:44
  88.5 25.3 %collective-permute-start.7 = (bf16[129,16,128]{2,1,0:T(8,128)(2,1)}, bf16[129,16,128]{2,1,0:T(8,128)(2,1)}, u32[]{:S(2)}, u32[]{:S(2)}) collective-permute-start(bf16[129,16,128]{2,1,0:T(8,128)(2,1)} %shard_map.69), channel_id=1, source_target_pairs={{0,12},{1,13},{2,14},{3,15},{4,8},{5,9},{6,10},{7,11},{8,4},{9,5},... | collective-permute-start | bytes 1585160 | tf_op jit(solution)/shard_map/ppermute | solution.py:44
  96.1 8.1 %collective-permute-start.20 = (bf16[32,64,128]{2,1,0:T(8,128)(2,1)}, bf16[32,64,128]{2,1,0:T(8,128)(2,1)}, u32[]{:S(2)}, u32[]{:S(2)}) collective-permute-start(bf16[32,64,128]{2,1,0:T(8,128)(2,1)} %collective-permute-done.19.refs_4_), channel_id=1, source_target_pairs={{0,1},{1,0},{2,3},{3,2},{4,5},{5,4},{6,7},{7,6},{8,9},{9,8},{10,11... | collective-permute-start | bytes 1572872 | tf_op jit(solution)/shard_map/ppermute | solution.py:44
  103.5 26.2 %collective-permute-start.18 = (bf16[32,64,128]{2,1,0:T(8,128)(2,1)}, bf16[32,64,128]{2,1,0:T(8,128)(2,1)}, u32[]{:S(2)}, u32[]{:S(2)}) collective-permute-start(bf16[32,64,128]{2,1,0:T(8,128)(2,1)} %shard_map.73.refs_6_), channel_id=1, source_target_pairs={{0,1},{1,0},{2,3},{3,2},{4,5},{5,4},{6,7},{7,6},{8,9},{9,8},{10,11... | collective-permute-start | bytes 1572872 | tf_op jit(solution)/shard_map/ppermute | solution.py:44
  104.2 25.6 %collective-permute-start.15 = (bf16[32,64,128]{2,1,0:T(8,128)(2,1)}, bf16[32,64,128]{2,1,0:T(8,128)(2,1)}, u32[]{:S(2)}, u32[]{:S(2)}) collective-permute-start(bf16[32,64,128]{2,1,0:T(8,128)(2,1)} %shard_map.73.refs_6_), channel_id=1, source_target_pairs={{0,2},{1,3},{2,0},{3,1},{4,6},{5,7},{6,4},{7,5},{8,10},{9,11},{10,... | collective-permute-start | bytes 1572872 | tf_op jit(solution)/shard_map/ppermute | solution.py:44
  112.5 24.7 %collective-permute-start.4 = (bf16[129,16,128]{2,1,0:T(8,128)(2,1)}, bf16[129,16,128]{2,1,0:T(8,128)(2,1)}, u32[]{:S(2)}, u32[]{:S(2)}) collective-permute-start(bf16[129,16,128]{2,1,0:T(8,128)(2,1)} %get-tuple-element.26), channel_id=1, source_target_pairs={{0,6},{1,7},{2,4},{3,5},{4,2},{5,3},{6,0},{7,1},{8,14},{9,15},{10,... | collective-permute-start | bytes 1585160 | tf_op jit(solution)/shard_map/ppermute | solution.py:44
  112.5 32.2 %collective-permute-start.8 = (bf16[129,16,128]{2,1,0:T(8,128)(2,1)}, bf16[129,16,128]{2,1,0:T(8,128)(2,1)}, u32[]{:S(2)}, u32[]{:S(2)}) collective-permute-start(bf16[129,16,128]{2,1,0:T(8,128)(2,1)} %shard_map.70), channel_id=1, source_target_pairs={{0,14},{1,15},{2,12},{3,13},{4,10},{5,11},{6,8},{7,9},{8,6},{9,7},... | collective-permute-start | bytes 1585160 | tf_op jit(solution)/shard_map/ppermute | solution.py:44
  113.8 30.9 %collective-permute-start.12 = (bf16[32,64,128]{2,1,0:T(8,128)(2,1)}, bf16[32,64,128]{2,1,0:T(8,128)(2,1)}, u32[]{:S(2)}, u32[]{:S(2)}) collective-permute-start(bf16[32,64,128]{2,1,0:T(8,128)(2,1)} %collective-permute-done.11.refs_4_), channel_id=1, source_target_pairs={{0,1},{1,0},{2,3},{3,2},{4,5},{5,4},{6,7},{7,6},{8,9},{9,8},{10,11... | collective-permute-start | bytes 1572872 | tf_op jit(solution)/shard_map/ppermute | solution.py:44
  129.7 15.0 %collective-permute-start.16 = (bf16[32,64,128]{2,1,0:T(8,128)(2,1)}, bf16[32,64,128]{2,1,0:T(8,128)(2,1)}, u32[]{:S(2)}, u32[]{:S(2)}) collective-permute-start(bf16[32,64,128]{2,1,0:T(8,128)(2,1)} %collective-permute-done.15.refs_6_), channel_id=1, source_target_pairs={{0,1},{1,0},{2,3},{3,2},{4,5},{5,4},{6,7},{7,6},{8,9},{9,8},{10,11... | collective-permute-start | bytes 1572872 | tf_op jit(solution)/shard_map/ppermute | solution.py:44
  152.2 1.9 collective-permute-start.24
  152.3 3.9 %collective-permute-start.25 = (f32[16,128]{1,0:T(8,128)}, f32[16,128]{1,0:T(8,128)S(1)}, u32[]{:S(2)}, u32[]{:S(2)}) collective-permute-start(f32[16,128]{1,0:T(8,128)} %get-tuple-element.35), channel_id=1, source_target_pairs={{0,2},{1,3},{2,0},{3,1},{4,6},{5,7},{6,4},{7,5},{8,10},{9,11},{10,... | collective-permute-start | bytes 24584 | tf_op jit(solution)/shard_map/ppermute | solution.py:100
  152.8 3.4 %collective-permute-start.26 = (f32[16,128]{1,0:T(8,128)}, f32[16,128]{1,0:T(8,128)S(1)}, u32[]{:S(2)}, u32[]{:S(2)}) collective-permute-start(f32[16,128]{1,0:T(8,128)} %get-tuple-element.35), channel_id=1, source_target_pairs={{0,3},{1,2},{2,1},{3,0},{4,7},{5,6},{6,5},{7,4},{8,11},{9,10},{10,... | collective-permute-start | bytes 24584 | tf_op jit(solution)/shard_map/ppermute | solution.py:100
  156.9 5.8 %collective-permute-start.27 = (f32[16,128]{1,0:T(8,128)S(1)}, f32[16,128]{1,0:T(8,128)S(1)}, u32[]{:S(2)}, u32[]{:S(2)}) collective-permute-start(f32[16,128]{1,0:T(8,128)S(1)} %add_add_fusion.1), channel_id=1, source_target_pairs={{0,4},{1,5},{2,6},{3,7},{4,0},{5,1},{6,2},{7,3},{8,12},{9,13},{10,... | collective-permute-start | bytes 24584 | tf_op jit(solution)/shard_map/ppermute | solution.py:100
  160.1 4.5 %collective-permute-start.28 = (f32[16,128]{1,0:T(8,128)S(1)}, f32[16,128]{1,0:T(8,128)S(1)}, u32[]{:S(2)}, u32[]{:S(2)}) collective-permute-start(f32[16,128]{1,0:T(8,128)S(1)} %add_add_fusion.1), channel_id=1, source_target_pairs={{0,8},{1,9},{2,10},{3,11},{4,12},{5,13},{6,14},{7,15},{8,0},{9,1},... | collective-permute-start | bytes 24584 | tf_op jit(solution)/shard_map/ppermute | solution.py:100
  161.2 5.4 %collective-permute-start.29 = (f32[16,128]{1,0:T(8,128)S(1)}, f32[16,128]{1,0:T(8,128)S(1)}, u32[]{:S(2)}, u32[]{:S(2)}) collective-permute-start(f32[16,128]{1,0:T(8,128)S(1)} %add_add_fusion.1), channel_id=1, source_target_pairs={{0,12},{1,13},{2,14},{3,15},{4,8},{5,9},{6,10},{7,11},{8,4},{9,5},... | collective-permute-start | bytes 24584 | tf_op jit(solution)/shard_map/ppermute | solution.py:100
  170.0 12.7 %collective-permute-start.33 = (bf16[32,64,128]{2,1,0:T(8,128)(2,1)S(1)}, bf16[32,64,128]{2,1,0:T(8,128)(2,1)}, u32[]{:S(2)}, u32[]{:S(2)}) collective-permute-start(bf16[32,64,128]{2,1,0:T(8,128)(2,1)S(1)} %get-tuple-element.36.refs_10_), channel_id=1, source_target_pairs={{0,2},{1,5},{2,6},{3,1},{4,0},{5,9},{6,10},{7,3},{8,4},{9,13},{10,... | collective-permute-start | bytes 1572872 | tf_op jit(solution)/shard_map/ppermute | solution.py:44
  170.7 12.0 %collective-permute-start.30 = (bf16[32,64,128]{2,1,0:T(8,128)(2,1)S(1)}, bf16[32,64,128]{2,1,0:T(8,128)(2,1)}, u32[]{:S(2)}, u32[]{:S(2)}) collective-permute-start(bf16[32,64,128]{2,1,0:T(8,128)(2,1)S(1)} %get-tuple-element.36.refs_10_), channel_id=1, source_target_pairs={{0,4},{1,3},{2,0},{3,7},{4,8},{5,1},{6,2},{7,11},{8,12},{9,5},{10,... | collective-permute-start | bytes 1572872 | tf_op jit(solution)/shard_map/ppermute | solution.py:44
  172.0 13.2 %collective-permute-start.32 = (bf16[32,64,128]{2,1,0:T(8,128)(2,1)S(1)}, bf16[32,64,128]{2,1,0:T(8,128)(2,1)S(1)}, u32[]{:S(2)}, u32[]{:S(2)}) collective-permute-start(bf16[32,64,128]{2,1,0:T(8,128)(2,1)S(1)} %get-tuple-element.36.refs_10_), channel_id=1, source_target_pairs={{0,1},{1,0},{2,3},{3,2},{4,5},{5,4},{6,7},{7,6},{8,9},{9,8},{10,11... | collective-permute-start | bytes 1572872 | tf_op jit(solution)/shard_map/ppermute | solution.py:44
  182.7 3.3 %collective-permute-start.34 = (bf16[32,64,128]{2,1,0:T(8,128)(2,1)}, bf16[32,64,128]{2,1,0:T(8,128)(2,1)S(1)}, u32[]{:S(2)}, u32[]{:S(2)}) collective-permute-start(bf16[32,64,128]{2,1,0:T(8,128)(2,1)} %collective-permute-done.33.refs_14_), channel_id=1, source_target_pairs={{0,1},{1,0},{2,3},{3,2},{4,5},{5,4},{6,7},{7,6},{8,9},{9,8},{10,11... | collective-permute-start | bytes 1572872 | tf_op jit(solution)/shard_map/ppermute | solution.py:44
  182.7 4.1 %collective-permute-start.35 = (bf16[32,64,128]{2,1,0:T(8,128)(2,1)}, bf16[32,64,128]{2,1,0:T(8,128)(2,1)}, u32[]{:S(2)}, u32[]{:S(2)}) collective-permute-start(bf16[32,64,128]{2,1,0:T(8,128)(2,1)} %collective-permute-done.30.refs_12_), channel_id=1, source_target_pairs={{0,1},{1,0},{2,3},{3,2},{4,5},{5,4},{6,7},{7,6},{8,9},{9,8},{10,11... | collective-permute-start | bytes 1572872 | tf_op jit(solution)/shard_map/ppermute | solution.py:44
  183.2 14.7 %collective-permute-start.31 = (bf16[32,64,128]{2,1,0:T(8,128)(2,1)}, bf16[32,64,128]{2,1,0:T(8,128)(2,1)}, u32[]{:S(2)}, u32[]{:S(2)}) collective-permute-start(bf16[32,64,128]{2,1,0:T(8,128)(2,1)} %collective-permute-done.30.refs_12_), channel_id=1, source_target_pairs={{0,4},{1,3},{2,0},{3,7},{4,8},{5,1},{6,2},{7,11},{8,12},{9,5},{10,... | collective-permute-start | bytes 1572872 | tf_op jit(solution)/shard_map/ppermute | solution.py:44
  183.8 14.1 %collective-permute-start.37 = (bf16[32,64,128]{2,1,0:T(8,128)(2,1)}, bf16[32,64,128]{2,1,0:T(8,128)(2,1)}, u32[]{:S(2)}, u32[]{:S(2)}) collective-permute-start(bf16[32,64,128]{2,1,0:T(8,128)(2,1)} %collective-permute-done.33.refs_14_), channel_id=1, source_target_pairs={{0,2},{1,5},{2,6},{3,1},{4,0},{5,9},{6,10},{7,3},{8,4},{9,13},{10,... | collective-permute-start | bytes 1572872 | tf_op jit(solution)/shard_map/ppermute | solution.py:44
  197.9 2.5 %collective-permute-start.39 = (bf16[32,64,128]{2,1,0:T(8,128)(2,1)}, bf16[32,64,128]{2,1,0:T(8,128)(2,1)}, u32[]{:S(2)}, u32[]{:S(2)}) collective-permute-start(bf16[32,64,128]{2,1,0:T(8,128)(2,1)} %shard_map.80.refs_10_), channel_id=1, source_target_pairs={{0,1},{1,0},{2,3},{3,2},{4,5},{5,4},{6,7},{7,6},{8,9},{9,8},{10,11... | collective-permute-start | bytes 1572872 | tf_op jit(solution)/shard_map/ppermute | solution.py:44
  197.9 3.0 %collective-permute-start.38 = (bf16[32,64,128]{2,1,0:T(8,128)(2,1)}, bf16[32,64,128]{2,1,0:T(8,128)(2,1)}, u32[]{:S(2)}, u32[]{:S(2)}) collective-permute-start(bf16[32,64,128]{2,1,0:T(8,128)(2,1)} %collective-permute-done.37.refs_12_), channel_id=1, source_target_pairs={{0,1},{1,0},{2,3},{3,2},{4,5},{5,4},{6,7},{7,6},{8,9},{9,8},{10,11... | collective-permute-start | bytes 1572872 | tf_op jit(solution)/shard_map/ppermute | solution.py:44
  198.4 14.8 %collective-permute-start.36 = (bf16[32,64,128]{2,1,0:T(8,128)(2,1)}, bf16[32,64,128]{2,1,0:T(8,128)(2,1)}, u32[]{:S(2)}, u32[]{:S(2)}) collective-permute-start(bf16[32,64,128]{2,1,0:T(8,128)(2,1)} %shard_map.80.refs_10_), channel_id=1, source_target_pairs={{0,4},{1,3},{2,0},{3,7},{4,8},{5,1},{6,2},{7,11},{8,12},{9,5},{10,... | collective-permute-start | bytes 1572872 | tf_op jit(solution)/shard_map/ppermute | solution.py:44
  199.2 14.0 %collective-permute-start.41 = (bf16[32,64,128]{2,1,0:T(8,128)(2,1)}, bf16[32,64,128]{2,1,0:T(8,128)(2,1)}, u32[]{:S(2)}, u32[]{:S(2)}) collective-permute-start(bf16[32,64,128]{2,1,0:T(8,128)(2,1)} %collective-permute-done.37.refs_12_), channel_id=1, source_target_pairs={{0,2},{1,5},{2,6},{3,1},{4,0},{5,9},{6,10},{7,3},{8,4},{9,13},{10,... | collective-permute-start | bytes 1572872 | tf_op jit(solution)/shard_map/ppermute | solution.py:44
  213.2 2.3 collective-permute-start.43
  213.2 3.0 %collective-permute-start.42 = (bf16[32,64,128]{2,1,0:T(8,128)(2,1)}, bf16[32,64,128]{2,1,0:T(8,128)(2,1)}, u32[]{:S(2)}, u32[]{:S(2)}) collective-permute-start(bf16[32,64,128]{2,1,0:T(8,128)(2,1)} %collective-permute-done.41.refs_12_), channel_id=1, source_target_pairs={{0,1},{1,0},{2,3},{3,2},{4,5},{5,4},{6,7},{7,6},{8,9},{9,8},{10,11... | collective-permute-start | bytes 1572872 | tf_op jit(solution)/shard_map/ppermute | solution.py:44
  213.7 9.7 %collective-permute-start.40 = (bf16[32,64,128]{2,1,0:T(8,128)(2,1)}, bf16[32,64,128]{2,1,0:T(8,128)(2,1)}, u32[]{:S(2)}, u32[]{:S(2)}) collective-permute-start(bf16[32,64,128]{2,1,0:T(8,128)(2,1)} %shard_map.82.refs_10_), channel_id=1, source_target_pairs={{0,4},{1,3},{2,0},{3,7},{4,8},{5,1},{6,2},{7,11},{8,12},{9,5},{10,... | collective-permute-start | bytes 1572872 | tf_op jit(solution)/shard_map/ppermute | solution.py:44
  223.4 2.3 %collective-permute-start.44 = (bf16[32,64,128]{2,1,0:T(8,128)(2,1)}, bf16[32,64,128]{2,1,0:T(8,128)(2,1)}, u32[]{:S(2)}, u32[]{:S(2)}) collective-permute-start(bf16[32,64,128]{2,1,0:T(8,128)(2,1)} %shard_map.84.refs_10_), channel_id=1, source_target_pairs={{0,1},{1,0},{2,3},{3,2},{4,5},{5,4},{6,7},{7,6},{8,9},{9,8},{10,11... | collective-permute-start | bytes 1572872 | tf_op jit(solution)/shard_map/ppermute | solution.py:44
  (10 other events, 15.1 us)

commit v21 on v20

--- a/solution.py
+++ b/solution.py
@@ -279,18 +279,17 @@
         whole = right.at[source, side]
         pltpu.make_async_copy(whole, whole, right_sems.at[source, side]).wait()
 
-    for source in range(sources):
-        if choices:
-            for choice, piece in enumerate(lefts):
-
-                @pl.when(ids_ref[chosen + source] == choice)
-                def _():
-                    for copy in left_copies(source, piece):
-                        copy.start()
-
-        else:
-            for copy in left_copies(source, lefts[source]):
-                copy.start()
+    for which in range(2):
+        for source in range(sources):
+            if choices:
+                for choice, piece in enumerate(lefts):
+
+                    @pl.when(ids_ref[chosen + source] == choice)
+                    def _():
+                        left_copies(source, piece)[which].start()
+
+            else:
+                left_copies(source, lefts[source])[which].start()
     for source in range(sources):
         for copy in vector_copies(source):
             copy.start()

time: 232 us -> 231 us (level)
  transfers between devices with their start and end apart: 45 -> 45, of which waited for: 19 -> 20; matrix products, arithmetic and copies ran while one was open for 1% -> 1% of each run, Pallas kernels for 22% -> 21%
where the time goes in v21:
time: 231 us; the launch traced here: 230 us
  waiting for transfers between devices  118 us (51%)
  Pallas kernels  63.2 us (27%)
  starting transfers between devices  39 us (17%)
  local copies, waits for them, and re-layouts  7.13 us (3%)
    ppermute x39, waiting for transfers between devices, permute(): return lax.ppermute(value, BOTH, pairs)  112 us
    pallas_call x8, Pallas kernels, apply_group(): pl.pallas_call(functools.partial(apply_kernel, sources, choices, chosen,...  55.7 us
    ppermute x39, starting transfers between devices, permute(): return lax.ppermute(value, BOTH, pairs)  31.6 us
    ppermute x6, starting transfers between devices, spread(): lax.ppermute(value, BOTH, [(d, d ^ m) for d in range(devices)])  7.32 us
    ppermute x6, waiting for transfers between devices, spread(): lax.ppermute(value, BOTH, [(d, d ^ m) for d in range(devices)])  5.82 us
    pallas_call x1, Pallas kernels, pack(): pl.pallas_call(functools.partial(pack_kernel, order, capacity, blocks, te...  5.35 us
  transfers between devices with their start and end apart: 45, of which 20 were waited for; matrix products, arithmetic and copies ran while one was open for 1% of the time, Pallas kernels for 21%

profile of v21, /device:TPU:0, one launch (start us, length us, event | category | flops | bytes accessed | tf_op | source)
XLA Modules:
  0.0 229.9 jit_solution(16439874164898491925)
XLA Ops:
  0.6 1.4 constant_dynamic-slice_fusion.2
  2.7 1.0 constant_dynamic-slice_fusion
  3.7 4.0 %collective-permute-start.13 = (bf16[32,64,128]{2,1,0:T(8,128)(2,1)}, bf16[32,64,128]{2,1,0:T(8,128)(2,1)}, u32[]{:S(2)}, u32[]{:S(2)}) collective-permute-start(bf16[32,64,128]{2,1,0:T(8,128)(2,1)} %get-tuple-element.45.refs_4_.refs_8_.wave_ref), channel_id=1, source_target_pairs={{0,8},{1,9},{2,10},{3,11},{4,12},{5,13},{6,14},{7,15},{8,0},{9,1},... | collective-permute-start | bytes 1572872 | tf_op jit(solution)/shard_map/ppermute | solution.py:44
  7.7 1.5 collective-permute-start.21
  11.6 5.4 %shard_map.68 = (bf16[129,16,128]{2,1,0:T(8,128)(2,1)}, bf16[129,16,128]{2,1,0:T(8,128)(2,1)}, bf16[129,16,128]{2,1,0:T(8,128)(2,1)}, bf16[129,16,128]{2,1,0:T(8...) custom-call(s32[2]{0:T(128)} %pad_add_fusion.1.ids_ref, ...), custom_call_target="tpu_custom_call" | custom-call | flops 5750000128 | tf_op jit(solution)/shard_map/pallas_call | solution.py:167
  17.5 1.6 collective-permute-start.10
  19.1 12.5 %collective-permute-done.13.refs_0_ = bf16[32,64,128]{2,1,0:T(8,128)(2,1)} collective-permute-done((bf16[32,64,128]{2,1,0:T(8,128)(2,1)}, bf16[32,64,128]{2,1,0:T(8,128)(2,1)}, u32[]{:S(2)}, u32[]{:S(2)}) %collective-permute-start.13) | collective-permute-done | bytes 524320 | tf_op jit(solution)/shard_map/ppermute | solution.py:44
  31.6 3.9 %collective-permute-start.6 = (bf16[129,16,128]{2,1,0:T(8,128)(2,1)}, bf16[129,16,128]{2,1,0:T(8,128)(2,1)S(1)}, u32[]{:S(2)}, u32[]{:S(2)}) collective-permute-start(bf16[129,16,128]{2,1,0:T(8,128)(2,1)} %get-tuple-element.28), channel_id=1, source_target_pairs={{0,10},{1,11},{2,8},{3,9},{4,14},{5,15},{6,12},{7,13},{8,2},{9,3},... | collective-permute-start | bytes 1585160 | tf_op jit(solution)/shard_map/ppermute | solution.py:44
  35.5 1.1 collective-permute-start.3
  36.6 7.5 %collective-permute-done.10.refs_0_ = bf16[32,64,128]{2,1,0:T(8,128)(2,1)} collective-permute-done((bf16[32,64,128]{2,1,0:T(8,128)(2,1)}, bf16[32,64,128]{2,1,0:T(8,128)(2,1)}, u32[]{:S(2)}, u32[]{:S(2)}) %collective-permute-start.10) | collective-permute-done | bytes 524320 | tf_op jit(solution)/shard_map/ppermute | solution.py:44
  44.1 26.2 %collective-permute-done.5.refs_1_.refs_4_ = bf16[129,16,128]{2,1,0:T(8,128)(2,1)S(1)} collective-permute-done((bf16[129,16,128]{2,1,0:T(8,128)(2,1)}, bf16[129,16,128]{2,1,0:T(8,128)(2,1)S(1)}, u32[]{:S(2)}, u32[]{:S(2)}) %collective-permute-start.5) | collective-permute-done | bytes 528416 | tf_op jit(solution)/shard_map/ppermute | solution.py:44
  70.4 10.5 %collective-permute-done.6.refs_1_.refs_0_.refs_5_ = bf16[129,16,128]{2,1,0:T(8,128)(2,1)S(1)} collective-permute-done((bf16[129,16,128]{2,1,0:T(8,128)(2,1)}, bf16[129,16,128]{2,1,0:T(8,128)(2,1)S(1)}, u32[]{:S(2)}, u32[]{:S(2)}) %collective-permute-start.6) | collective-permute-done | bytes 528416 | tf_op jit(solution)/shard_map/ppermute | solution.py:44
  82.4 4.4 %collective-permute-done.14.refs_0_ = bf16[32,64,128]{2,1,0:T(8,128)(2,1)} collective-permute-done((bf16[32,64,128]{2,1,0:T(8,128)(2,1)}, bf16[32,64,128]{2,1,0:T(8,128)(2,1)}, u32[]{:S(2)}, u32[]{:S(2)}) %collective-permute-start.14) | collective-permute-done | bytes 524320 | tf_op jit(solution)/shard_map/ppermute | solution.py:44
  86.8 1.6 collective-permute-start.11
  88.5 2.8 %collective-permute-start.7 = (bf16[129,16,128]{2,1,0:T(8,128)(2,1)}, bf16[129,16,128]{2,1,0:T(8,128)(2,1)}, u32[]{:S(2)}, u32[]{:S(2)}) collective-permute-start(bf16[129,16,128]{2,1,0:T(8,128)(2,1)} %shard_map.69), channel_id=1, source_target_pairs={{0,12},{1,13},{2,14},{3,15},{4,8},{5,9},{6,10},{7,11},{8,4},{9,5},... | collective-permute-start | bytes 1585160 | tf_op jit(solution)/shard_map/ppermute | solution.py:44
  91.3 4.8 %collective-permute-done.19.refs_4_ = bf16[32,64,128]{2,1,0:T(8,128)(2,1)} collective-permute-done((bf16[32,64,128]{2,1,0:T(8,128)(2,1)}, bf16[32,64,128]{2,1,0:T(8,128)(2,1)}, u32[]{:S(2)}, u32[]{:S(2)}) %collective-permute-start.19) | collective-permute-done | bytes 524320 | tf_op jit(solution)/shard_map/ppermute | solution.py:44
  96.1 7.4 %shard_map.74 = (f32[33,64,128]{2,1,0:T(8,128)}, f32[8,128]{1,0:T(8,128)}) custom-call(s32[10]{0:T(128)} %stack.56.ids_ref, bf16[129,16,128]{2,1,0:T(8,128)(2,1)} %get-tuple-element.23.refs_0_, bf16[129,16,128]{2,1,0:T(8,128)(2,1)} %copy-done.5, bf16[2,32,128,128]{3,2,1,0:T(8,128)(2,1)} %refs_8_.7, ...), custom_call_target="tpu_custom_call" | custom-call | flops 8165000192 | tf_op jit(solution)/shard_map/pallas_call | solution.py:390
  104.0 1.1 collective-permute-start.15
  105.1 7.3 %shard_map.75 = (f32[33,64,128]{2,1,0:T(8,128)}, f32[8,128]{1,0:T(8,128)}) custom-call(s32[10]{0:T(128)} %stack.56.ids_ref, bf16[129,16,128]{2,1,0:T(8,128)(2,1)} %copy-done.2, bf16[129,16,128]{2,1,0:T(8,128)(2,1)} %copy-done.4, bf16[2,32,128,128]{3,2,1,0:T(8,128)(2,1)} %refs_8_.7, bf16[2,32,128,128]{3,2,1,0:T(8,128)(2,1)} %collective-permute-done.9.refs_3_.refs_9_, ...), custom_call_target="tpu_custom_call" | custom-call | flops 8165000192 | tf_op jit(solution)/shard_map/pallas_call | solution.py:390
  112.5 1.6 collective-permute-start.8
  114.2 15.4 %collective-permute-done.15.refs_6_ = bf16[32,64,128]{2,1,0:T(8,128)(2,1)} collective-permute-done((bf16[32,64,128]{2,1,0:T(8,128)(2,1)}, bf16[32,64,128]{2,1,0:T(8,128)(2,1)}, u32[]{:S(2)}, u32[]{:S(2)}) %collective-permute-start.15) | collective-permute-done | bytes 524320 | tf_op jit(solution)/shard_map/ppermute | solution.py:44
  129.5 7.1 %shard_map.76 = (f32[33,64,128]{2,1,0:T(8,128)}, f32[8,128]{1,0:T(8,128)}) custom-call(s32[10]{0:T(128)} %stack.56.ids_ref, bf16[129,16,128]{2,1,0:T(8,128)(2,1)} %copy-done.6, bf16[129,16,128]{2,1,0:T(8,128)(2,1)} %collective-permute-done.7.refs_1_.refs_6_, bf16[2,32,128,128]{3,2,1,0:T(8,128)(2,1)} %refs_8_.7, ...), custom_call_target="tpu_custom_call" | custom-call | flops 8165000192 | tf_op jit(solution)/shard_map/pallas_call | solution.py:390
  136.7 8.6 %collective-permute-done.8.refs_1_.refs_7_ = bf16[129,16,128]{2,1,0:T(8,128)(2,1)} collective-permute-done((bf16[129,16,128]{2,1,0:T(8,128)(2,1)}, bf16[129,16,128]{2,1,0:T(8,128)(2,1)}, u32[]{:S(2)}, u32[]{:S(2)}) %collective-permute-start.8) | collective-permute-done | bytes 528416 | tf_op jit(solution)/shard_map/ppermute | solution.py:44
  145.3 7.4 %shard_map.77 = (f32[32,64,128]{2,1,0:T(8,128)}, f32[16,128]{1,0:T(8,128)}) custom-call(s32[10]{0:T(128)} %stack.56.ids_ref, bf16[129,16,128]{2,1,0:T(8,128)(2,1)} %collective-permute-done.4.refs_0_.refs_3_, bf16[129,16,128]{2,1,0:T(8,128)(2,1)} %collective-permute-done.8.refs_1_.refs_7_, bf16[2,32,128,128]{3,2,1,0:T(8,128)(2,1)} %refs_8_.7, ...), custom_call_target="tpu_custom_call" | custom-call | flops 8165000192 | tf_op jit(solution)/shard_map/pallas_call | solution.py:390
  152.7 0.9 collective-permute-start.25
  153.6 1.0 collective-permute-start.26
  154.6 2.1 collective-permute-done.25
  157.6 3.0 %collective-permute-start.27 = (f32[16,128]{1,0:T(8,128)S(1)}, f32[16,128]{1,0:T(8,128)S(1)}, u32[]{:S(2)}, u32[]{:S(2)}) collective-permute-start(f32[16,128]{1,0:T(8,128)S(1)} %add_add_fusion.1), channel_id=1, source_target_pairs={{0,4},{1,5},{2,6},{3,7},{4,0},{5,1},{6,2},{7,3},{8,12},{9,13},{10,... | collective-permute-start | bytes 24584 | tf_op jit(solution)/shard_map/ppermute | solution.py:100
  161.1 2.0 collective-permute-start.29
  163.0 2.2 collective-permute-done.28
  165.2 1.3 collective-permute-done.29
  166.5 1.2 copy-done.1
  167.8 2.1 shard_map.78
  169.9 1.0 collective-permute-start.33
  170.8 1.1 collective-permute-start.30
  171.9 10.4 %collective-permute-done.33.refs_14_ = bf16[32,64,128]{2,1,0:T(8,128)(2,1)} collective-permute-done((bf16[32,64,128]{2,1,0:T(8,128)(2,1)S(1)}, bf16[32,64,128]{2,1,0:T(8,128)(2,1)}, u32[]{:S(2)}, u32[]{:S(2)}) %collective-permute-start.33) | collective-permute-done | bytes 524320 | tf_op jit(solution)/shard_map/ppermute | solution.py:44
  182.8 1.3 collective-permute-start.31
  185.6 0.8 copy-done.11
  186.4 7.9 %shard_map.79 = (f32[33,64,128]{2,1,0:T(8,128)}, f32[8,128]{1,0:T(8,128)}) custom-call(s32[10]{0:T(128)} %stack.56.ids_ref, bf16[129,16,128]{2,1,0:T(8,128)(2,1)} %get-tuple-element.23.refs_0_, bf16[129,16,128]{2,1,0:T(8,128)(2,1)} %copy-done.4, bf16[129,16,128]{2,1,0:T(8,128)(2,1)} %copy-done.6, ...), custom_call_target="tpu_custom_call" | custom-call | flops 10234999808 | tf_op jit(solution)/shard_map/pallas_call | solution.py:390
  194.3 3.1 %collective-permute-done.31.refs_0_ = bf16[32,64,128]{2,1,0:T(8,128)(2,1)} collective-permute-done((bf16[32,64,128]{2,1,0:T(8,128)(2,1)}, bf16[32,64,128]{2,1,0:T(8,128)(2,1)}, u32[]{:S(2)}, u32[]{:S(2)}) %collective-permute-start.31) | collective-permute-done | bytes 524320 | tf_op jit(solution)/shard_map/ppermute | solution.py:44
  198.0 1.2 collective-permute-start.36
  199.2 0.9 collective-permute-start.41
  200.5 6.8 %shard_map.81 = (f32[33,64,128]{2,1,0:T(8,128)}, f32[8,128]{1,0:T(8,128)}) custom-call(s32[10]{0:T(128)} %stack.56.ids_ref, bf16[129,16,128]{2,1,0:T(8,128)(2,1)} %get-tuple-element.23.refs_0_, bf16[129,16,128]{2,1,0:T(8,128)(2,1)} %copy-done.4, bf16[129,16,128]{2,1,0:T(8,128)(2,1)} %copy-done.6, ...), custom_call_target="tpu_custom_call" | custom-call | flops 8165000192 | tf_op jit(solution)/shard_map/pallas_call | solution.py:390
  207.3 5.2 %collective-permute-done.36.refs_0_ = bf16[32,64,128]{2,1,0:T(8,128)(2,1)} collective-permute-done((bf16[32,64,128]{2,1,0:T(8,128)(2,1)}, bf16[32,64,128]{2,1,0:T(8,128)(2,1)}, u32[]{:S(2)}, u32[]{:S(2)}) %collective-permute-start.36) | collective-permute-done | bytes 524320 | tf_op jit(solution)/shard_map/ppermute | solution.py:44
  213.1 1.7 collective-permute-start.40
  215.4 7.0 %shard_map.83 = (f32[33,64,128]{2,1,0:T(8,128)}, f32[8,128]{1,0:T(8,128)}) custom-call(s32[10]{0:T(128)} %stack.56.ids_ref, bf16[129,16,128]{2,1,0:T(8,128)(2,1)} %get-tuple-element.23.refs_0_, bf16[129,16,128]{2,1,0:T(8,128)(2,1)} %copy-done.4, bf16[129,16,128]{2,1,0:T(8,128)(2,1)} %copy-done.6, ...), custom_call_target="tpu_custom_call" | custom-call | flops 8165000192 | tf_op jit(solution)/shard_map/pallas_call | solution.py:390
  222.6 2.2 collective-permute-done.44.refs_11_
  224.8 4.9 %shard_map.85 = bf16[32,64,128]{2,1,0:T(8,128)(2,1)} custom-call(s32[10]{0:T(128)} %stack.56.ids_ref, bf16[129,16,128]{2,1,0:T(8,128)(2,1)} %get-tuple-element.23.refs_0_, bf16[129,16,128]{2,1,0:T(8,128)(2,1)} %copy-done.4, bf16[129,16,128]{2,1,0:T(8,128)(2,1)} %copy-done.6, bf16[129,16,128]{2,1,0:T(8,128)(2,1)} %collective-permute-done.4.refs_0_.refs_3_, ...), custom_call_target="tpu_custom_call" | custom-call | flops 6095000064 | tf_op jit(solution)/shard_map/pallas_call | solution.py:390
  (93 shorter events, 11.4 us)
Async XLA Ops:
  2.0 7.2 %copy-start.8 = (s32[2,32]{1,0:T(2,128)S(1)}, s32[2,32]{1,0:T(2,128)}, u32[]{:S(2)}) copy-start(s32[2,32]{1,0:T(2,128)} %param.9) | copy-start | bytes 772
  2.1 7.2 %copy-start.9 = (s32[2,32,1]{1,2,0:T(1,128)S(1)}, s32[2,32,1]{1,2,0:T(1,128)}, u32[]{:S(2)}) copy-start(s32[2,32,1]{1,2,0:T(1,128)} %param.8) | copy-start | bytes 772
  2.1 9.5 %collective-permute-start.1 = (bf16[2,32,64,128]{3,2,1,0:T(8,128)(2,1)S(1)}, bf16[2,32,64,128]{3,2,1,0:T(8,128)(2,1)}, u32[]{:S(2)}, u32[]{:S(2)}) collective-permute-start(bf16[2,32,64,128]{3,2,1,0:T(8,128)(2,1)S(1)} %constant_dynamic-slice_fusion.2), channel_id=1, source_target_pairs={{0,1},{1,0},{2,3},{3,2},{4,5},{5,4},{6,7},{7,6},{8,9},{9,8},{10,11... | collective-permute-start | bytes 3145736 | tf_op jit(solution)/shard_map/ppermute | solution.py:44
  2.6 84.3 %collective-permute-start.9 = (bf16[2,32,128,128]{3,2,1,0:T(8,128)(2,1)}, bf16[2,32,128,128]{3,2,1,0:T(8,128)(2,1)}, u32[]{:S(2)}, u32[]{:S(2)}) collective-permute-start(bf16[2,32,128,128]{3,2,1,0:T(8,128)(2,1)} %refs_8_.7), channel_id=1, source_target_pairs={{0,1},{1,0},{2,3},{3,2},{4,5},{5,4},{6,7},{7,6},{8,9},{9,8},{10,11... | collective-permute-start | bytes 6291464 | tf_op jit(solution)/shard_map/ppermute | solution.py:44
  3.7 27.8 %collective-permute-start.13 = (bf16[32,64,128]{2,1,0:T(8,128)(2,1)}, bf16[32,64,128]{2,1,0:T(8,128)(2,1)}, u32[]{:S(2)}, u32[]{:S(2)}) collective-permute-start(bf16[32,64,128]{2,1,0:T(8,128)(2,1)} %get-tuple-element.45.refs_4_.refs_8_.wave_ref), channel_id=1, source_target_pairs={{0,8},{1,9},{2,10},{3,11},{4,12},{5,13},{6,14},{7,15},{8,0},{9,1},... | collective-permute-start | bytes 1572872 | tf_op jit(solution)/shard_map/ppermute | solution.py:44
  7.7 23.8 %collective-permute-start.21 = (bf16[32,64,128]{2,1,0:T(8,128)(2,1)}, bf16[32,64,128]{2,1,0:T(8,128)(2,1)}, u32[]{:S(2)}, u32[]{:S(2)}) collective-permute-start(bf16[32,64,128]{2,1,0:T(8,128)(2,1)} %get-tuple-element.45.refs_4_.refs_8_.wave_ref), channel_id=1, source_target_pairs={{0,2},{1,3},{2,0},{3,1},{4,6},{5,7},{6,4},{7,5},{8,10},{9,11},{10,... | collective-permute-start | bytes 1572872 | tf_op jit(solution)/shard_map/ppermute | solution.py:44
  9.9 1.2 collective-permute-start
  17.0 18.5 %collective-permute-start.2 = (bf16[129,16,128]{2,1,0:T(8,128)(2,1)}, bf16[129,16,128]{2,1,0:T(8,128)(2,1)S(1)}, u32[]{:S(2)}, u32[]{:S(2)}) collective-permute-start(bf16[129,16,128]{2,1,0:T(8,128)(2,1)} %get-tuple-element.24), channel_id=1, source_target_pairs={{0,2},{1,3},{2,0},{3,1},{4,6},{5,7},{6,4},{7,5},{8,10},{9,11},{10,... | collective-permute-start | bytes 1585160 | tf_op jit(solution)/shard_map/ppermute | solution.py:44
  17.5 26.6 %collective-permute-start.10 = (bf16[32,64,128]{2,1,0:T(8,128)(2,1)}, bf16[32,64,128]{2,1,0:T(8,128)(2,1)}, u32[]{:S(2)}, u32[]{:S(2)}) collective-permute-start(bf16[32,64,128]{2,1,0:T(8,128)(2,1)} %get-tuple-element.45.refs_4_.refs_8_.wave_ref), channel_id=1, source_target_pairs={{0,4},{1,5},{2,6},{3,7},{4,0},{5,1},{6,2},{7,3},{8,12},{9,13},{10,... | collective-permute-start | bytes 1572872 | tf_op jit(solution)/shard_map/ppermute | solution.py:44
  31.6 38.8 %collective-permute-start.5 = (bf16[129,16,128]{2,1,0:T(8,128)(2,1)}, bf16[129,16,128]{2,1,0:T(8,128)(2,1)S(1)}, u32[]{:S(2)}, u32[]{:S(2)}) collective-permute-start(bf16[129,16,128]{2,1,0:T(8,128)(2,1)} %get-tuple-element.27), channel_id=1, source_target_pairs={{0,8},{1,9},{2,10},{3,11},{4,12},{5,13},{6,14},{7,15},{8,0},{9,1},... | collective-permute-start | bytes 1585160 | tf_op jit(solution)/shard_map/ppermute | solution.py:44
  31.6 49.3 %collective-permute-start.6 = (bf16[129,16,128]{2,1,0:T(8,128)(2,1)}, bf16[129,16,128]{2,1,0:T(8,128)(2,1)S(1)}, u32[]{:S(2)}, u32[]{:S(2)}) collective-permute-start(bf16[129,16,128]{2,1,0:T(8,128)(2,1)} %get-tuple-element.28), channel_id=1, source_target_pairs={{0,10},{1,11},{2,8},{3,9},{4,14},{5,15},{6,12},{7,13},{8,2},{9,3},... | collective-permute-start | bytes 1585160 | tf_op jit(solution)/shard_map/ppermute | solution.py:44
  35.5 46.8 %collective-permute-start.3 = (bf16[129,16,128]{2,1,0:T(8,128)(2,1)}, bf16[129,16,128]{2,1,0:T(8,128)(2,1)S(1)}, u32[]{:S(2)}, u32[]{:S(2)}) collective-permute-start(bf16[129,16,128]{2,1,0:T(8,128)(2,1)} %get-tuple-element.25), channel_id=1, source_target_pairs={{0,4},{1,5},{2,6},{3,7},{4,0},{5,1},{6,2},{7,3},{8,12},{9,13},{10,... | collective-permute-start | bytes 1585160 | tf_op jit(solution)/shard_map/ppermute | solution.py:44
  44.1 42.7 %collective-permute-start.14 = (bf16[32,64,128]{2,1,0:T(8,128)(2,1)}, bf16[32,64,128]{2,1,0:T(8,128)(2,1)}, u32[]{:S(2)}, u32[]{:S(2)}) collective-permute-start(bf16[32,64,128]{2,1,0:T(8,128)(2,1)} %shard_map.72.refs_6_), channel_id=1, source_target_pairs={{0,4},{1,5},{2,6},{3,7},{4,0},{5,1},{6,2},{7,3},{8,12},{9,13},{10,... | collective-permute-start | bytes 1572872 | tf_op jit(solution)/shard_map/ppermute | solution.py:44
  70.4 12.0 %copy-start.5 = (bf16[129,16,128]{2,1,0:T(8,128)(2,1)}, bf16[129,16,128]{2,1,0:T(8,128)(2,1)S(1)}, u32[]{:S(2)}) copy-start(bf16[129,16,128]{2,1,0:T(8,128)(2,1)S(1)} %collective-permute-done.5.refs_1_.refs_4_) | copy-start | bytes 1585156
  70.4 18.1 %collective-permute-start.23 = (bf16[32,64,128]{2,1,0:T(8,128)(2,1)}, bf16[32,64,128]{2,1,0:T(8,128)(2,1)}, u32[]{:S(2)}, u32[]{:S(2)}) collective-permute-start(bf16[32,64,128]{2,1,0:T(8,128)(2,1)} %shard_map.72.refs_6_), channel_id=1, source_target_pairs={{0,1},{1,0},{2,3},{3,2},{4,5},{5,4},{6,7},{7,6},{8,9},{9,8},{10,11... | collective-permute-start | bytes 1572872 | tf_op jit(solution)/shard_map/ppermute | solution.py:44
  80.9 15.2 %collective-permute-start.19 = (bf16[32,64,128]{2,1,0:T(8,128)(2,1)}, bf16[32,64,128]{2,1,0:T(8,128)(2,1)}, u32[]{:S(2)}, u32[]{:S(2)}) collective-permute-start(bf16[32,64,128]{2,1,0:T(8,128)(2,1)} %shard_map.72.refs_6_), channel_id=1, source_target_pairs={{0,2},{1,3},{2,0},{3,1},{4,6},{5,7},{6,4},{7,5},{8,10},{9,11},{10,... | collective-permute-start | bytes 1572872 | tf_op jit(solution)/shard_map/ppermute | solution.py:44
  82.4 21.1 %collective-permute-start.22 = (bf16[32,64,128]{2,1,0:T(8,128)(2,1)}, bf16[32,64,128]{2,1,0:T(8,128)(2,1)}, u32[]{:S(2)}, u32[]{:S(2)}) collective-permute-start(bf16[32,64,128]{2,1,0:T(8,128)(2,1)} %collective-permute-done.21.refs_6_), channel_id=1, source_target_pairs={{0,1},{1,0},{2,3},{3,2},{4,5},{5,4},{6,7},{7,6},{8,9},{9,8},{10,11... | collective-permute-start | bytes 1572872 | tf_op jit(solution)/shard_map/ppermute | solution.py:44
  86.8 25.6 %collective-permute-start.17 = (bf16[32,64,128]{2,1,0:T(8,128)(2,1)}, bf16[32,64,128]{2,1,0:T(8,128)(2,1)}, u32[]{:S(2)}, u32[]{:S(2)}) collective-permute-start(bf16[32,64,128]{2,1,0:T(8,128)(2,1)} %shard_map.71.refs_4_), channel_id=1, source_target_pairs={{0,1},{1,0},{2,3},{3,2},{4,5},{5,4},{6,7},{7,6},{8,9},{9,8},{10,11... | collective-permute-start | bytes 1572872 | tf_op jit(solution)/shard_map/ppermute | solution.py:44
  86.8 25.7 %collective-permute-start.11 = (bf16[32,64,128]{2,1,0:T(8,128)(2,1)}, bf16[32,64,128]{2,1,0:T(8,128)(2,1)}, u32[]{:S(2)}, u32[]{:S(2)}) collective-permute-start(bf16[32,64,128]{2,1,0:T(8,128)(2,1)} %shard_map.71.refs_4_), channel_id=1, source_target_pairs={{0,2},{1,3},{2,0},{3,1},{4,6},{5,7},{6,4},{7,5},{8,10},{9,11},{10,... | collective-permute-start | bytes 1572872 | tf_op jit(solution)/shard_map/ppermute | solution.py:44
  88.5 25.7 %collective-permute-start.7 = (bf16[129,16,128]{2,1,0:T(8,128)(2,1)}, bf16[129,16,128]{2,1,0:T(8,128)(2,1)}, u32[]{:S(2)}, u32[]{:S(2)}) collective-permute-start(bf16[129,16,128]{2,1,0:T(8,128)(2,1)} %shard_map.69), channel_id=1, source_target_pairs={{0,12},{1,13},{2,14},{3,15},{4,8},{5,9},{6,10},{7,11},{8,4},{9,5},... | collective-permute-start | bytes 1585160 | tf_op jit(solution)/shard_map/ppermute | solution.py:44
  96.1 7.9 %collective-permute-start.20 = (bf16[32,64,128]{2,1,0:T(8,128)(2,1)}, bf16[32,64,128]{2,1,0:T(8,128)(2,1)}, u32[]{:S(2)}, u32[]{:S(2)}) collective-permute-start(bf16[32,64,128]{2,1,0:T(8,128)(2,1)} %collective-permute-done.19.refs_4_), channel_id=1, source_target_pairs={{0,1},{1,0},{2,3},{3,2},{4,5},{5,4},{6,7},{7,6},{8,9},{9,8},{10,11... | collective-permute-start | bytes 1572872 | tf_op jit(solution)/shard_map/ppermute | solution.py:44
  103.4 26.1 %collective-permute-start.18 = (bf16[32,64,128]{2,1,0:T(8,128)(2,1)}, bf16[32,64,128]{2,1,0:T(8,128)(2,1)}, u32[]{:S(2)}, u32[]{:S(2)}) collective-permute-start(bf16[32,64,128]{2,1,0:T(8,128)(2,1)} %shard_map.73.refs_6_), channel_id=1, source_target_pairs={{0,1},{1,0},{2,3},{3,2},{4,5},{5,4},{6,7},{7,6},{8,9},{9,8},{10,11... | collective-permute-start | bytes 1572872 | tf_op jit(solution)/shard_map/ppermute | solution.py:44
  104.0 25.6 %collective-permute-start.15 = (bf16[32,64,128]{2,1,0:T(8,128)(2,1)}, bf16[32,64,128]{2,1,0:T(8,128)(2,1)}, u32[]{:S(2)}, u32[]{:S(2)}) collective-permute-start(bf16[32,64,128]{2,1,0:T(8,128)(2,1)} %shard_map.73.refs_6_), channel_id=1, source_target_pairs={{0,2},{1,3},{2,0},{3,1},{4,6},{5,7},{6,4},{7,5},{8,10},{9,11},{10,... | collective-permute-start | bytes 1572872 | tf_op jit(solution)/shard_map/ppermute | solution.py:44
  112.5 24.2 %collective-permute-start.4 = (bf16[129,16,128]{2,1,0:T(8,128)(2,1)}, bf16[129,16,128]{2,1,0:T(8,128)(2,1)}, u32[]{:S(2)}, u32[]{:S(2)}) collective-permute-start(bf16[129,16,128]{2,1,0:T(8,128)(2,1)} %get-tuple-element.26), channel_id=1, source_target_pairs={{0,6},{1,7},{2,4},{3,5},{4,2},{5,3},{6,0},{7,1},{8,14},{9,15},{10,... | collective-permute-start | bytes 1585160 | tf_op jit(solution)/shard_map/ppermute | solution.py:44
  112.5 32.8 %collective-permute-start.8 = (bf16[129,16,128]{2,1,0:T(8,128)(2,1)}, bf16[129,16,128]{2,1,0:T(8,128)(2,1)}, u32[]{:S(2)}, u32[]{:S(2)}) collective-permute-start(bf16[129,16,128]{2,1,0:T(8,128)(2,1)} %shard_map.70), channel_id=1, source_target_pairs={{0,14},{1,15},{2,12},{3,13},{4,10},{5,11},{6,8},{7,9},{8,6},{9,7},... | collective-permute-start | bytes 1585160 | tf_op jit(solution)/shard_map/ppermute | solution.py:44
  114.2 31.1 %collective-permute-start.12 = (bf16[32,64,128]{2,1,0:T(8,128)(2,1)}, bf16[32,64,128]{2,1,0:T(8,128)(2,1)}, u32[]{:S(2)}, u32[]{:S(2)}) collective-permute-start(bf16[32,64,128]{2,1,0:T(8,128)(2,1)} %collective-permute-done.11.refs_4_), channel_id=1, source_target_pairs={{0,1},{1,0},{2,3},{3,2},{4,5},{5,4},{6,7},{7,6},{8,9},{9,8},{10,11... | collective-permute-start | bytes 1572872 | tf_op jit(solution)/shard_map/ppermute | solution.py:44
  129.5 15.8 %collective-permute-start.16 = (bf16[32,64,128]{2,1,0:T(8,128)(2,1)}, bf16[32,64,128]{2,1,0:T(8,128)(2,1)}, u32[]{:S(2)}, u32[]{:S(2)}) collective-permute-start(bf16[32,64,128]{2,1,0:T(8,128)(2,1)} %collective-permute-done.15.refs_6_), channel_id=1, source_target_pairs={{0,1},{1,0},{2,3},{3,2},{4,5},{5,4},{6,7},{7,6},{8,9},{9,8},{10,11... | collective-permute-start | bytes 1572872 | tf_op jit(solution)/shard_map/ppermute | solution.py:44
  152.7 1.9 collective-permute-start.24
  152.7 3.9 %collective-permute-start.25 = (f32[16,128]{1,0:T(8,128)}, f32[16,128]{1,0:T(8,128)S(1)}, u32[]{:S(2)}, u32[]{:S(2)}) collective-permute-start(f32[16,128]{1,0:T(8,128)} %get-tuple-element.35), channel_id=1, source_target_pairs={{0,2},{1,3},{2,0},{3,1},{4,6},{5,7},{6,4},{7,5},{8,10},{9,11},{10,... | collective-permute-start | bytes 24584 | tf_op jit(solution)/shard_map/ppermute | solution.py:100
  153.6 3.3 %collective-permute-start.26 = (f32[16,128]{1,0:T(8,128)}, f32[16,128]{1,0:T(8,128)S(1)}, u32[]{:S(2)}, u32[]{:S(2)}) collective-permute-start(f32[16,128]{1,0:T(8,128)} %get-tuple-element.35), channel_id=1, source_target_pairs={{0,3},{1,2},{2,1},{3,0},{4,7},{5,6},{6,5},{7,4},{8,11},{9,10},{10,... | collective-permute-start | bytes 24584 | tf_op jit(solution)/shard_map/ppermute | solution.py:100
  157.6 5.4 %collective-permute-start.27 = (f32[16,128]{1,0:T(8,128)S(1)}, f32[16,128]{1,0:T(8,128)S(1)}, u32[]{:S(2)}, u32[]{:S(2)}) collective-permute-start(f32[16,128]{1,0:T(8,128)S(1)} %add_add_fusion.1), channel_id=1, source_target_pairs={{0,4},{1,5},{2,6},{3,7},{4,0},{5,1},{6,2},{7,3},{8,12},{9,13},{10,... | collective-permute-start | bytes 24584 | tf_op jit(solution)/shard_map/ppermute | solution.py:100
  160.7 4.6 %collective-permute-start.28 = (f32[16,128]{1,0:T(8,128)S(1)}, f32[16,128]{1,0:T(8,128)S(1)}, u32[]{:S(2)}, u32[]{:S(2)}) collective-permute-start(f32[16,128]{1,0:T(8,128)S(1)} %add_add_fusion.1), channel_id=1, source_target_pairs={{0,8},{1,9},{2,10},{3,11},{4,12},{5,13},{6,14},{7,15},{8,0},{9,1},... | collective-permute-start | bytes 24584 | tf_op jit(solution)/shard_map/ppermute | solution.py:100
  161.1 5.4 %collective-permute-start.29 = (f32[16,128]{1,0:T(8,128)S(1)}, f32[16,128]{1,0:T(8,128)S(1)}, u32[]{:S(2)}, u32[]{:S(2)}) collective-permute-start(f32[16,128]{1,0:T(8,128)S(1)} %add_add_fusion.1), channel_id=1, source_target_pairs={{0,12},{1,13},{2,14},{3,15},{4,8},{5,9},{6,10},{7,11},{8,4},{9,5},... | collective-permute-start | bytes 24584 | tf_op jit(solution)/shard_map/ppermute | solution.py:100
  169.9 12.4 %collective-permute-start.33 = (bf16[32,64,128]{2,1,0:T(8,128)(2,1)S(1)}, bf16[32,64,128]{2,1,0:T(8,128)(2,1)}, u32[]{:S(2)}, u32[]{:S(2)}) collective-permute-start(bf16[32,64,128]{2,1,0:T(8,128)(2,1)S(1)} %get-tuple-element.36.refs_10_), channel_id=1, source_target_pairs={{0,2},{1,5},{2,6},{3,1},{4,0},{5,9},{6,10},{7,3},{8,4},{9,13},{10,... | collective-permute-start | bytes 1572872 | tf_op jit(solution)/shard_map/ppermute | solution.py:44
  170.8 11.4 %collective-permute-start.30 = (bf16[32,64,128]{2,1,0:T(8,128)(2,1)S(1)}, bf16[32,64,128]{2,1,0:T(8,128)(2,1)}, u32[]{:S(2)}, u32[]{:S(2)}) collective-permute-start(bf16[32,64,128]{2,1,0:T(8,128)(2,1)S(1)} %get-tuple-element.36.refs_10_), channel_id=1, source_target_pairs={{0,4},{1,3},{2,0},{3,7},{4,8},{5,1},{6,2},{7,11},{8,12},{9,5},{10,... | collective-permute-start | bytes 1572872 | tf_op jit(solution)/shard_map/ppermute | solution.py:44
  171.9 12.9 %collective-permute-start.32 = (bf16[32,64,128]{2,1,0:T(8,128)(2,1)S(1)}, bf16[32,64,128]{2,1,0:T(8,128)(2,1)S(1)}, u32[]{:S(2)}, u32[]{:S(2)}) collective-permute-start(bf16[32,64,128]{2,1,0:T(8,128)(2,1)S(1)} %get-tuple-element.36.refs_10_), channel_id=1, source_target_pairs={{0,1},{1,0},{2,3},{3,2},{4,5},{5,4},{6,7},{7,6},{8,9},{9,8},{10,11... | collective-permute-start | bytes 1572872 | tf_op jit(solution)/shard_map/ppermute | solution.py:44
  182.3 3.3 %collective-permute-start.34 = (bf16[32,64,128]{2,1,0:T(8,128)(2,1)}, bf16[32,64,128]{2,1,0:T(8,128)(2,1)S(1)}, u32[]{:S(2)}, u32[]{:S(2)}) collective-permute-start(bf16[32,64,128]{2,1,0:T(8,128)(2,1)} %collective-permute-done.33.refs_14_), channel_id=1, source_target_pairs={{0,1},{1,0},{2,3},{3,2},{4,5},{5,4},{6,7},{7,6},{8,9},{9,8},{10,11... | collective-permute-start | bytes 1572872 | tf_op jit(solution)/shard_map/ppermute | solution.py:44
  182.3 4.1 %collective-permute-start.35 = (bf16[32,64,128]{2,1,0:T(8,128)(2,1)}, bf16[32,64,128]{2,1,0:T(8,128)(2,1)}, u32[]{:S(2)}, u32[]{:S(2)}) collective-permute-start(bf16[32,64,128]{2,1,0:T(8,128)(2,1)} %collective-permute-done.30.refs_12_), channel_id=1, source_target_pairs={{0,1},{1,0},{2,3},{3,2},{4,5},{5,4},{6,7},{7,6},{8,9},{9,8},{10,11... | collective-permute-start | bytes 1572872 | tf_op jit(solution)/shard_map/ppermute | solution.py:44
  182.8 14.7 %collective-permute-start.31 = (bf16[32,64,128]{2,1,0:T(8,128)(2,1)}, bf16[32,64,128]{2,1,0:T(8,128)(2,1)}, u32[]{:S(2)}, u32[]{:S(2)}) collective-permute-start(bf16[32,64,128]{2,1,0:T(8,128)(2,1)} %collective-permute-done.30.refs_12_), channel_id=1, source_target_pairs={{0,4},{1,3},{2,0},{3,7},{4,8},{5,1},{6,2},{7,11},{8,12},{9,5},{10,... | collective-permute-start | bytes 1572872 | tf_op jit(solution)/shard_map/ppermute | solution.py:44
  184.1 13.4 %collective-permute-start.37 = (bf16[32,64,128]{2,1,0:T(8,128)(2,1)}, bf16[32,64,128]{2,1,0:T(8,128)(2,1)}, u32[]{:S(2)}, u32[]{:S(2)}) collective-permute-start(bf16[32,64,128]{2,1,0:T(8,128)(2,1)} %collective-permute-done.33.refs_14_), channel_id=1, source_target_pairs={{0,2},{1,5},{2,6},{3,1},{4,0},{5,9},{6,10},{7,3},{8,4},{9,13},{10,... | collective-permute-start | bytes 1572872 | tf_op jit(solution)/shard_map/ppermute | solution.py:44
  197.5 2.7 %collective-permute-start.39 = (bf16[32,64,128]{2,1,0:T(8,128)(2,1)}, bf16[32,64,128]{2,1,0:T(8,128)(2,1)}, u32[]{:S(2)}, u32[]{:S(2)}) collective-permute-start(bf16[32,64,128]{2,1,0:T(8,128)(2,1)} %shard_map.80.refs_10_), channel_id=1, source_target_pairs={{0,1},{1,0},{2,3},{3,2},{4,5},{5,4},{6,7},{7,6},{8,9},{9,8},{10,11... | collective-permute-start | bytes 1572872 | tf_op jit(solution)/shard_map/ppermute | solution.py:44
  197.5 3.0 %collective-permute-start.38 = (bf16[32,64,128]{2,1,0:T(8,128)(2,1)}, bf16[32,64,128]{2,1,0:T(8,128)(2,1)}, u32[]{:S(2)}, u32[]{:S(2)}) collective-permute-start(bf16[32,64,128]{2,1,0:T(8,128)(2,1)} %collective-permute-done.37.refs_12_), channel_id=1, source_target_pairs={{0,1},{1,0},{2,3},{3,2},{4,5},{5,4},{6,7},{7,6},{8,9},{9,8},{10,11... | collective-permute-start | bytes 1572872 | tf_op jit(solution)/shard_map/ppermute | solution.py:44
  198.0 14.4 %collective-permute-start.36 = (bf16[32,64,128]{2,1,0:T(8,128)(2,1)}, bf16[32,64,128]{2,1,0:T(8,128)(2,1)}, u32[]{:S(2)}, u32[]{:S(2)}) collective-permute-start(bf16[32,64,128]{2,1,0:T(8,128)(2,1)} %shard_map.80.refs_10_), channel_id=1, source_target_pairs={{0,4},{1,3},{2,0},{3,7},{4,8},{5,1},{6,2},{7,11},{8,12},{9,5},{10,... | collective-permute-start | bytes 1572872 | tf_op jit(solution)/shard_map/ppermute | solution.py:44
  199.2 13.2 %collective-permute-start.41 = (bf16[32,64,128]{2,1,0:T(8,128)(2,1)}, bf16[32,64,128]{2,1,0:T(8,128)(2,1)}, u32[]{:S(2)}, u32[]{:S(2)}) collective-permute-start(bf16[32,64,128]{2,1,0:T(8,128)(2,1)} %collective-permute-done.37.refs_12_), channel_id=1, source_target_pairs={{0,2},{1,5},{2,6},{3,1},{4,0},{5,9},{6,10},{7,3},{8,4},{9,13},{10,... | collective-permute-start | bytes 1572872 | tf_op jit(solution)/shard_map/ppermute | solution.py:44
  212.4 2.4 %collective-permute-start.43 = (bf16[32,64,128]{2,1,0:T(8,128)(2,1)}, bf16[32,64,128]{2,1,0:T(8,128)(2,1)}, u32[]{:S(2)}, u32[]{:S(2)}) collective-permute-start(bf16[32,64,128]{2,1,0:T(8,128)(2,1)} %shard_map.82.refs_10_), channel_id=1, source_target_pairs={{0,1},{1,0},{2,3},{3,2},{4,5},{5,4},{6,7},{7,6},{8,9},{9,8},{10,11... | collective-permute-start | bytes 1572872 | tf_op jit(solution)/shard_map/ppermute | solution.py:44
  212.4 3.0 %collective-permute-start.42 = (bf16[32,64,128]{2,1,0:T(8,128)(2,1)}, bf16[32,64,128]{2,1,0:T(8,128)(2,1)}, u32[]{:S(2)}, u32[]{:S(2)}) collective-permute-start(bf16[32,64,128]{2,1,0:T(8,128)(2,1)} %collective-permute-done.41.refs_12_), channel_id=1, source_target_pairs={{0,1},{1,0},{2,3},{3,2},{4,5},{5,4},{6,7},{7,6},{8,9},{9,8},{10,11... | collective-permute-start | bytes 1572872 | tf_op jit(solution)/shard_map/ppermute | solution.py:44
  213.1 9.5 %collective-permute-start.40 = (bf16[32,64,128]{2,1,0:T(8,128)(2,1)}, bf16[32,64,128]{2,1,0:T(8,128)(2,1)}, u32[]{:S(2)}, u32[]{:S(2)}) collective-permute-start(bf16[32,64,128]{2,1,0:T(8,128)(2,1)} %shard_map.82.refs_10_), channel_id=1, source_target_pairs={{0,4},{1,3},{2,0},{3,7},{4,8},{5,1},{6,2},{7,11},{8,12},{9,5},{10,... | collective-permute-start | bytes 1572872 | tf_op jit(solution)/shard_map/ppermute | solution.py:44
  222.6 2.3 collective-permute-start.44
  (10 other events, 15.1 us)

commit v22 on v20

--- a/solution.py
+++ b/solution.py
@@ -10,8 +10,8 @@
 BOTH = ("sec", "term")
 VMEM_LIMIT = 64 * 2**20
 PART = 16
-ORDER = [0, 4, 5, 1, 2, 6, 3, 7]
-WAITS = {4: 1, 2: 5, 6: 2}
+ORDER = [0, 1, 4, 5, 2, 6, 3, 7]
+WAITS = {4: 1, 2: 4}
 PIECE_WAITS = {6: 4, 7: 5}
 RING_BYTES = 24 * 2**20
 

time: 232 us -> 238 us (1.026)
  waiting for transfers between devices: 119 us -> 123 us
    ppermute x39, waiting for transfers between devices: 113 us -> 119 us  [permute(): return lax.ppermute(value, BOTH, pairs)]
    unnamed x26 -> x24, local copies, waits for them, and re-layouts: 4.02 us -> 5.5 us
  transfers between devices with their start and end apart: 45 -> 45, of which waited for: 19 -> 18; matrix products, arithmetic and copies ran while one was open for 1% -> 1% of each run, Pallas kernels for 22% -> 21%
where the time goes in v22:
time: 238 us; the launch traced here: 236 us
  waiting for transfers between devices  123 us (52%)
  Pallas kernels  64 us (27%)
  starting transfers between devices  37.8 us (16%)
  local copies, waits for them, and re-layouts  8.6 us (4%)
    ppermute x39, waiting for transfers between devices, permute(): return lax.ppermute(value, BOTH, pairs)  119 us
    pallas_call x8, Pallas kernels, apply_group(): pl.pallas_call(functools.partial(apply_kernel, sources, choices, chosen,...  56.4 us
    ppermute x39, starting transfers between devices, permute(): return lax.ppermute(value, BOTH, pairs)  31.4 us
    ppermute x6, starting transfers between devices, spread(): lax.ppermute(value, BOTH, [(d, d ^ m) for d in range(devices)])  6.36 us
    pallas_call x1, Pallas kernels, pack(): pl.pallas_call(functools.partial(pack_kernel, order, capacity, blocks, te...  5.51 us
    unnamed x24, local copies, waits for them, and re-layouts  5.5 us
  transfers between devices with their start and end apart: 45, of which 18 were waited for; matrix products, arithmetic and copies ran while one was open for 1% of the time, Pallas kernels for 21%

profile of v22, /device:TPU:0, one launch (start us, length us, event | category | flops | bytes accessed | tf_op | source)
XLA Modules:
  0.0 235.8 jit_solution(703823531341057169)
XLA Ops:
  0.6 1.4 constant_dynamic-slice_fusion.2
  2.7 1.1 constant_dynamic-slice_fusion
  3.7 2.9 %collective-permute-start.22 = (bf16[32,64,128]{2,1,0:T(8,128)(2,1)}, bf16[32,64,128]{2,1,0:T(8,128)(2,1)}, u32[]{:S(2)}, u32[]{:S(2)}) collective-permute-start(bf16[32,64,128]{2,1,0:T(8,128)(2,1)} %get-tuple-element.45.refs_4_.refs_8_.wave_ref), channel_id=1, source_target_pairs={{0,2},{1,3},{2,0},{3,1},{4,6},{5,7},{6,4},{7,5},{8,10},{9,11},{10,... | collective-permute-start | bytes 1572872 | tf_op jit(solution)/shard_map/ppermute | solution.py:44
  6.7 2.6 %collective-permute-start.13 = (bf16[32,64,128]{2,1,0:T(8,128)(2,1)}, bf16[32,64,128]{2,1,0:T(8,128)(2,1)}, u32[]{:S(2)}, u32[]{:S(2)}) collective-permute-start(bf16[32,64,128]{2,1,0:T(8,128)(2,1)} %get-tuple-element.45.refs_4_.refs_8_.wave_ref), channel_id=1, source_target_pairs={{0,8},{1,9},{2,10},{3,11},{4,12},{5,13},{6,14},{7,15},{8,0},{9,1},... | collective-permute-start | bytes 1572872 | tf_op jit(solution)/shard_map/ppermute | solution.py:44
  9.8 0.7 pad_add_fusion.1.ids_ref
  11.6 5.5 %shard_map.68 = (bf16[129,16,128]{2,1,0:T(8,128)(2,1)}, bf16[129,16,128]{2,1,0:T(8,128)(2,1)}, bf16[129,16,128]{2,1,0:T(8,128)(2,1)}, bf16[129,16,128]{2,1,0:T(8...) custom-call(s32[2]{0:T(128)} %pad_add_fusion.1.ids_ref, ...), custom_call_target="tpu_custom_call" | custom-call | flops 5750000128 | tf_op jit(solution)/shard_map/pallas_call | solution.py:167
  17.7 1.8 collective-permute-start.5
  19.5 1.6 collective-permute-start.10
  21.1 24.1 %collective-permute-done.13.refs_0_ = bf16[32,64,128]{2,1,0:T(8,128)(2,1)} collective-permute-done((bf16[32,64,128]{2,1,0:T(8,128)(2,1)}, bf16[32,64,128]{2,1,0:T(8,128)(2,1)}, u32[]{:S(2)}, u32[]{:S(2)}) %collective-permute-start.13) | collective-permute-done | bytes 524320 | tf_op jit(solution)/shard_map/ppermute | solution.py:44
  45.3 0.7 copy-done.4
  46.0 21.7 %collective-permute-done.5.refs_1_.refs_0_.refs_4_ = bf16[129,16,128]{2,1,0:T(8,128)(2,1)S(1)} collective-permute-done((bf16[129,16,128]{2,1,0:T(8,128)(2,1)}, bf16[129,16,128]{2,1,0:T(8,128)(2,1)S(1)}, u32[]{:S(2)}, u32[]{:S(2)}) %collective-permute-start.5) | collective-permute-done | bytes 528416 | tf_op jit(solution)/shard_map/ppermute | solution.py:44
  68.7 9.4 %collective-permute-done.6.refs_1_.refs_5_ = bf16[129,16,128]{2,1,0:T(8,128)(2,1)S(1)} collective-permute-done((bf16[129,16,128]{2,1,0:T(8,128)(2,1)}, bf16[129,16,128]{2,1,0:T(8,128)(2,1)S(1)}, u32[]{:S(2)}, u32[]{:S(2)}) %collective-permute-start.6) | collective-permute-done | bytes 528416 | tf_op jit(solution)/shard_map/ppermute | solution.py:44
  78.1 0.8 copy-done.5
  78.9 0.7 collective-permute-start.14
  79.6 9.6 %collective-permute-done.20.refs_6_ = bf16[32,64,128]{2,1,0:T(8,128)(2,1)} collective-permute-done((bf16[32,64,128]{2,1,0:T(8,128)(2,1)}, bf16[32,64,128]{2,1,0:T(8,128)(2,1)}, u32[]{:S(2)}, u32[]{:S(2)}) %collective-permute-start.20) | collective-permute-done | bytes 524320 | tf_op jit(solution)/shard_map/ppermute | solution.py:44
  89.2 7.3 %shard_map.73 = (f32[33,64,128]{2,1,0:T(8,128)}, f32[8,128]{1,0:T(8,128)}) custom-call(s32[10]{0:T(128)} %stack.56.ids_ref, bf16[129,16,128]{2,1,0:T(8,128)(2,1)} %get-tuple-element.23.refs_0_, bf16[129,16,128]{2,1,0:T(8,128)(2,1)} %copy-done.4, bf16[2,32,128,128]{3,2,1,0:T(8,128)(2,1)} %refs_8_.7, ...), custom_call_target="tpu_custom_call" | custom-call | flops 8165000192 | tf_op jit(solution)/shard_map/pallas_call | solution.py:391
  96.5 1.5 collective-permute-start.11
  98.0 3.9 %collective-permute-start.7 = (bf16[129,16,128]{2,1,0:T(8,128)(2,1)}, bf16[129,16,128]{2,1,0:T(8,128)(2,1)}, u32[]{:S(2)}, u32[]{:S(2)}) collective-permute-start(bf16[129,16,128]{2,1,0:T(8,128)(2,1)} %shard_map.69), channel_id=1, source_target_pairs={{0,12},{1,13},{2,14},{3,15},{4,8},{5,9},{6,10},{7,11},{8,4},{9,5},... | collective-permute-start | bytes 1585160 | tf_op jit(solution)/shard_map/ppermute | solution.py:44
  102.4 7.4 %shard_map.74 = (f32[33,64,128]{2,1,0:T(8,128)}, f32[8,128]{1,0:T(8,128)}) custom-call(s32[10]{0:T(128)} %stack.56.ids_ref, bf16[129,16,128]{2,1,0:T(8,128)(2,1)} %copy-done.2, bf16[129,16,128]{2,1,0:T(8,128)(2,1)} %copy-done.5, bf16[2,32,128,128]{3,2,1,0:T(8,128)(2,1)} %refs_8_.7, bf16[2,32,128,128]{3,2,1,0:T(8,128)(2,1)} %collective-permute-done.9.refs_3_.refs_9_, ...), custom_call_target="tpu_custom_call" | custom-call | flops 8165000192 | tf_op jit(solution)/shard_map/pallas_call | solution.py:391
  110.0 1.7 collective-permute-done.11.refs_4_
  111.7 4.7 %collective-permute-start.8 = (bf16[129,16,128]{2,1,0:T(8,128)(2,1)}, bf16[129,16,128]{2,1,0:T(8,128)(2,1)}, u32[]{:S(2)}, u32[]{:S(2)}) collective-permute-start(bf16[129,16,128]{2,1,0:T(8,128)(2,1)} %shard_map.70), channel_id=1, source_target_pairs={{0,14},{1,15},{2,12},{3,13},{4,10},{5,11},{6,8},{7,9},{8,6},{9,7},... | collective-permute-start | bytes 1585160 | tf_op jit(solution)/shard_map/ppermute | solution.py:44
  116.4 28.9 %collective-permute-done.15.refs_6_ = bf16[32,64,128]{2,1,0:T(8,128)(2,1)} collective-permute-done((bf16[32,64,128]{2,1,0:T(8,128)(2,1)}, bf16[32,64,128]{2,1,0:T(8,128)(2,1)}, u32[]{:S(2)}, u32[]{:S(2)}) %collective-permute-start.15) | collective-permute-done | bytes 524320 | tf_op jit(solution)/shard_map/ppermute | solution.py:44
  145.3 7.4 %shard_map.75 = (f32[33,64,128]{2,1,0:T(8,128)}, f32[8,128]{1,0:T(8,128)}) custom-call(s32[10]{0:T(128)} %stack.56.ids_ref, bf16[129,16,128]{2,1,0:T(8,128)(2,1)} %collective-permute-done.3.refs_0_.refs_2_, bf16[129,16,128]{2,1,0:T(8,128)(2,1)} %collective-permute-done.7.refs_1_.refs_6_, bf16[2,32,128,128]{3,2,1,0:T(8,128)(2,1)} %refs_8_.7, ...), custom_call_target="tpu_custom_call" | custom-call | flops 8165000192 | tf_op jit(solution)/shard_map/pallas_call | solution.py:391
  152.7 7.3 %shard_map.76 = (f32[32,64,128]{2,1,0:T(8,128)}, f32[16,128]{1,0:T(8,128)}) custom-call(s32[10]{0:T(128)} %stack.56.ids_ref, bf16[129,16,128]{2,1,0:T(8,128)(2,1)} %collective-permute-done.4.refs_0_.refs_3_, bf16[129,16,128]{2,1,0:T(8,128)(2,1)} %collective-permute-done.8.refs_1_.refs_7_, bf16[2,32,128,128]{3,2,1,0:T(8,128)(2,1)} %refs_8_.7, ...), custom_call_target="tpu_custom_call" | custom-call | flops 8165000192 | tf_op jit(solution)/shard_map/pallas_call | solution.py:391
  160.6 0.7 collective-permute-start.25
  161.3 0.7 collective-permute-start.26
  162.1 2.4 %collective-permute-done.25 = f32[16,128]{1,0:T(8,128)S(1)} collective-permute-done((f32[16,128]{1,0:T(8,128)}, f32[16,128]{1,0:T(8,128)S(1)}, u32[]{:S(2)}, u32[]{:S(2)}) %collective-permute-start.25) | collective-permute-done | bytes 8224 | tf_op jit(solution)/shard_map/ppermute | solution.py:100
  164.7 0.7 add_add_fusion.1
  165.4 4.4 %collective-permute-start.29 = (f32[16,128]{1,0:T(8,128)S(1)}, f32[16,128]{1,0:T(8,128)S(1)}, u32[]{:S(2)}, u32[]{:S(2)}) collective-permute-start(f32[16,128]{1,0:T(8,128)S(1)} %add_add_fusion.1), channel_id=1, source_target_pairs={{0,12},{1,13},{2,14},{3,15},{4,8},{5,9},{6,10},{7,11},{8,4},{9,5},... | collective-permute-start | bytes 24584 | tf_op jit(solution)/shard_map/ppermute | solution.py:100
  169.9 1.5 collective-permute-done.29
  171.5 1.2 copy-done.1
  172.7 2.1 shard_map.77
  174.8 1.3 collective-permute-start.33
  176.2 0.7 collective-permute-start.30
  176.9 10.8 %collective-permute-done.33.refs_14_ = bf16[32,64,128]{2,1,0:T(8,128)(2,1)} collective-permute-done((bf16[32,64,128]{2,1,0:T(8,128)(2,1)S(1)}, bf16[32,64,128]{2,1,0:T(8,128)(2,1)}, u32[]{:S(2)}, u32[]{:S(2)}) %collective-permute-start.33) | collective-permute-done | bytes 524320 | tf_op jit(solution)/shard_map/ppermute | solution.py:44
  188.1 2.4 %collective-permute-start.31 = (bf16[32,64,128]{2,1,0:T(8,128)(2,1)}, bf16[32,64,128]{2,1,0:T(8,128)(2,1)}, u32[]{:S(2)}, u32[]{:S(2)}) collective-permute-start(bf16[32,64,128]{2,1,0:T(8,128)(2,1)} %collective-permute-done.30.refs_12_), channel_id=1, source_target_pairs={{0,4},{1,3},{2,0},{3,7},{4,8},{5,1},{6,2},{7,11},{8,12},{9,5},{10,... | collective-permute-start | bytes 1572872 | tf_op jit(solution)/shard_map/ppermute | solution.py:44
  190.5 0.8 copy-done.9
  191.3 0.8 copy-done.10
  192.1 7.9 %shard_map.78 = (f32[33,64,128]{2,1,0:T(8,128)}, f32[8,128]{1,0:T(8,128)}) custom-call(s32[10]{0:T(128)} %stack.56.ids_ref, bf16[129,16,128]{2,1,0:T(8,128)(2,1)} %get-tuple-element.23.refs_0_, bf16[129,16,128]{2,1,0:T(8,128)(2,1)} %copy-done.4, bf16[129,16,128]{2,1,0:T(8,128)(2,1)} %collective-permute-done.3.refs_0_.refs_2_, ...), custom_call_target="tpu_custom_call" | custom-call | flops 10234999808 | tf_op jit(solution)/shard_map/pallas_call | solution.py:391
  200.0 2.9 %collective-permute-done.31.refs_0_ = bf16[32,64,128]{2,1,0:T(8,128)(2,1)} collective-permute-done((bf16[32,64,128]{2,1,0:T(8,128)(2,1)}, bf16[32,64,128]{2,1,0:T(8,128)(2,1)}, u32[]{:S(2)}, u32[]{:S(2)}) %collective-permute-start.31) | collective-permute-done | bytes 524320 | tf_op jit(solution)/shard_map/ppermute | solution.py:44
  203.5 1.9 collective-permute-start.36
  206.0 6.8 %shard_map.80 = (f32[33,64,128]{2,1,0:T(8,128)}, f32[8,128]{1,0:T(8,128)}) custom-call(s32[10]{0:T(128)} %stack.56.ids_ref, bf16[129,16,128]{2,1,0:T(8,128)(2,1)} %get-tuple-element.23.refs_0_, bf16[129,16,128]{2,1,0:T(8,128)(2,1)} %copy-done.4, bf16[129,16,128]{2,1,0:T(8,128)(2,1)} %collective-permute-done.3.refs_0_.refs_2_, ...), custom_call_target="tpu_custom_call" | custom-call | flops 8165000192 | tf_op jit(solution)/shard_map/pallas_call | solution.py:391
  212.8 5.3 %collective-permute-done.36.refs_0_ = bf16[32,64,128]{2,1,0:T(8,128)(2,1)} collective-permute-done((bf16[32,64,128]{2,1,0:T(8,128)(2,1)}, bf16[32,64,128]{2,1,0:T(8,128)(2,1)}, u32[]{:S(2)}, u32[]{:S(2)}) %collective-permute-start.36) | collective-permute-done | bytes 524320 | tf_op jit(solution)/shard_map/ppermute | solution.py:44
  218.6 1.5 collective-permute-start.40
  220.3 0.7 collective-permute-done.42.refs_11_
  221.1 7.2 %shard_map.82 = (f32[33,64,128]{2,1,0:T(8,128)}, f32[8,128]{1,0:T(8,128)}) custom-call(s32[10]{0:T(128)} %stack.56.ids_ref, bf16[129,16,128]{2,1,0:T(8,128)(2,1)} %get-tuple-element.23.refs_0_, bf16[129,16,128]{2,1,0:T(8,128)(2,1)} %copy-done.4, bf16[129,16,128]{2,1,0:T(8,128)(2,1)} %collective-permute-done.3.refs_0_.refs_2_, ...), custom_call_target="tpu_custom_call" | custom-call | flops 8165000192 | tf_op jit(solution)/shard_map/pallas_call | solution.py:391
  228.4 2.2 collective-permute-done.44.refs_11_
  230.6 5.0 %shard_map.84 = bf16[32,64,128]{2,1,0:T(8,128)(2,1)} custom-call(s32[10]{0:T(128)} %stack.56.ids_ref, bf16[129,16,128]{2,1,0:T(8,128)(2,1)} %get-tuple-element.23.refs_0_, bf16[129,16,128]{2,1,0:T(8,128)(2,1)} %copy-done.4, bf16[129,16,128]{2,1,0:T(8,128)(2,1)} %collective-permute-done.3.refs_0_.refs_2_, ...), custom_call_target="tpu_custom_call" | custom-call | flops 6095000064 | tf_op jit(solution)/shard_map/pallas_call | solution.py:391
  (90 shorter events, 7.8 us)
Async XLA Ops:
  0.6 2.0 copy-start.3
  2.0 7.2 %copy-start.7 = (s32[2,32]{1,0:T(2,128)S(1)}, s32[2,32]{1,0:T(2,128)}, u32[]{:S(2)}) copy-start(s32[2,32]{1,0:T(2,128)} %param.9) | copy-start | bytes 772
  2.1 7.2 %copy-start.8 = (s32[2,32,1]{1,2,0:T(1,128)S(1)}, s32[2,32,1]{1,2,0:T(1,128)}, u32[]{:S(2)}) copy-start(s32[2,32,1]{1,2,0:T(1,128)} %param.8) | copy-start | bytes 772
  2.1 9.5 %collective-permute-start.1 = (bf16[2,32,64,128]{3,2,1,0:T(8,128)(2,1)S(1)}, bf16[2,32,64,128]{3,2,1,0:T(8,128)(2,1)}, u32[]{:S(2)}, u32[]{:S(2)}) collective-permute-start(bf16[2,32,64,128]{3,2,1,0:T(8,128)(2,1)S(1)} %constant_dynamic-slice_fusion.2), channel_id=1, source_target_pairs={{0,1},{1,0},{2,3},{3,2},{4,5},{5,4},{6,7},{7,6},{8,9},{9,8},{10,11... | collective-permute-start | bytes 3145736 | tf_op jit(solution)/shard_map/ppermute | solution.py:44
  2.6 77.0 %collective-permute-start.9 = (bf16[2,32,128,128]{3,2,1,0:T(8,128)(2,1)}, bf16[2,32,128,128]{3,2,1,0:T(8,128)(2,1)}, u32[]{:S(2)}, u32[]{:S(2)}) collective-permute-start(bf16[2,32,128,128]{3,2,1,0:T(8,128)(2,1)} %refs_8_.7), channel_id=1, source_target_pairs={{0,1},{1,0},{2,3},{3,2},{4,5},{5,4},{6,7},{7,6},{8,9},{9,8},{10,11... | collective-permute-start | bytes 6291464 | tf_op jit(solution)/shard_map/ppermute | solution.py:44
  3.7 15.8 %collective-permute-start.22 = (bf16[32,64,128]{2,1,0:T(8,128)(2,1)}, bf16[32,64,128]{2,1,0:T(8,128)(2,1)}, u32[]{:S(2)}, u32[]{:S(2)}) collective-permute-start(bf16[32,64,128]{2,1,0:T(8,128)(2,1)} %get-tuple-element.45.refs_4_.refs_8_.wave_ref), channel_id=1, source_target_pairs={{0,2},{1,3},{2,0},{3,1},{4,6},{5,7},{6,4},{7,5},{8,10},{9,11},{10,... | collective-permute-start | bytes 1572872 | tf_op jit(solution)/shard_map/ppermute | solution.py:44
  6.7 38.5 %collective-permute-start.13 = (bf16[32,64,128]{2,1,0:T(8,128)(2,1)}, bf16[32,64,128]{2,1,0:T(8,128)(2,1)}, u32[]{:S(2)}, u32[]{:S(2)}) collective-permute-start(bf16[32,64,128]{2,1,0:T(8,128)(2,1)} %get-tuple-element.45.refs_4_.refs_8_.wave_ref), channel_id=1, source_target_pairs={{0,8},{1,9},{2,10},{3,11},{4,12},{5,13},{6,14},{7,15},{8,0},{9,1},... | collective-permute-start | bytes 1572872 | tf_op jit(solution)/shard_map/ppermute | solution.py:44
  9.8 1.2 collective-permute-start
  17.1 28.1 %collective-permute-start.2 = (bf16[129,16,128]{2,1,0:T(8,128)(2,1)}, bf16[129,16,128]{2,1,0:T(8,128)(2,1)S(1)}, u32[]{:S(2)}, u32[]{:S(2)}) collective-permute-start(bf16[129,16,128]{2,1,0:T(8,128)(2,1)} %get-tuple-element.24), channel_id=1, source_target_pairs={{0,2},{1,3},{2,0},{3,1},{4,6},{5,7},{6,4},{7,5},{8,10},{9,11},{10,... | collective-permute-start | bytes 1585160 | tf_op jit(solution)/shard_map/ppermute | solution.py:44
  17.7 50.1 %collective-permute-start.5 = (bf16[129,16,128]{2,1,0:T(8,128)(2,1)}, bf16[129,16,128]{2,1,0:T(8,128)(2,1)S(1)}, u32[]{:S(2)}, u32[]{:S(2)}) collective-permute-start(bf16[129,16,128]{2,1,0:T(8,128)(2,1)} %get-tuple-element.27), channel_id=1, source_target_pairs={{0,8},{1,9},{2,10},{3,11},{4,12},{5,13},{6,14},{7,15},{8,0},{9,1},... | collective-permute-start | bytes 1585160 | tf_op jit(solution)/shard_map/ppermute | solution.py:44
  19.5 49.1 %collective-permute-start.10 = (bf16[32,64,128]{2,1,0:T(8,128)(2,1)}, bf16[32,64,128]{2,1,0:T(8,128)(2,1)}, u32[]{:S(2)}, u32[]{:S(2)}) collective-permute-start(bf16[32,64,128]{2,1,0:T(8,128)(2,1)} %get-tuple-element.45.refs_4_.refs_8_.wave_ref), channel_id=1, source_target_pairs={{0,4},{1,5},{2,6},{3,7},{4,0},{5,1},{6,2},{7,3},{8,12},{9,13},{10,... | collective-permute-start | bytes 1572872 | tf_op jit(solution)/shard_map/ppermute | solution.py:44
  45.2 32.8 %collective-permute-start.6 = (bf16[129,16,128]{2,1,0:T(8,128)(2,1)}, bf16[129,16,128]{2,1,0:T(8,128)(2,1)S(1)}, u32[]{:S(2)}, u32[]{:S(2)}) collective-permute-start(bf16[129,16,128]{2,1,0:T(8,128)(2,1)} %get-tuple-element.28), channel_id=1, source_target_pairs={{0,10},{1,11},{2,8},{3,9},{4,14},{5,15},{6,12},{7,13},{8,2},{9,3},... | collective-permute-start | bytes 1585160 | tf_op jit(solution)/shard_map/ppermute | solution.py:44
  45.2 33.6 %collective-permute-start.23 = (bf16[32,64,128]{2,1,0:T(8,128)(2,1)}, bf16[32,64,128]{2,1,0:T(8,128)(2,1)}, u32[]{:S(2)}, u32[]{:S(2)}) collective-permute-start(bf16[32,64,128]{2,1,0:T(8,128)(2,1)} %collective-permute-done.22.refs_6_), channel_id=1, source_target_pairs={{0,1},{1,0},{2,3},{3,2},{4,5},{5,4},{6,7},{7,6},{8,9},{9,8},{10,11... | collective-permute-start | bytes 1572872 | tf_op jit(solution)/shard_map/ppermute | solution.py:44
  67.8 21.4 %collective-permute-start.20 = (bf16[32,64,128]{2,1,0:T(8,128)(2,1)}, bf16[32,64,128]{2,1,0:T(8,128)(2,1)}, u32[]{:S(2)}, u32[]{:S(2)}) collective-permute-start(bf16[32,64,128]{2,1,0:T(8,128)(2,1)} %shard_map.72.refs_4_), channel_id=1, source_target_pairs={{0,2},{1,3},{2,0},{3,1},{4,6},{5,7},{6,4},{7,5},{8,10},{9,11},{10,... | collective-permute-start | bytes 1572872 | tf_op jit(solution)/shard_map/ppermute | solution.py:44
  68.6 27.9 %collective-permute-start.3 = (bf16[129,16,128]{2,1,0:T(8,128)(2,1)}, bf16[129,16,128]{2,1,0:T(8,128)(2,1)}, u32[]{:S(2)}, u32[]{:S(2)}) collective-permute-start(bf16[129,16,128]{2,1,0:T(8,128)(2,1)} %get-tuple-element.25), channel_id=1, source_target_pairs={{0,4},{1,5},{2,6},{3,7},{4,0},{5,1},{6,2},{7,3},{8,12},{9,13},{10,... | collective-permute-start | bytes 1585160 | tf_op jit(solution)/shard_map/ppermute | solution.py:44
  78.1 19.9 %collective-permute-start.19 = (bf16[32,64,128]{2,1,0:T(8,128)(2,1)}, bf16[32,64,128]{2,1,0:T(8,128)(2,1)}, u32[]{:S(2)}, u32[]{:S(2)}) collective-permute-start(bf16[32,64,128]{2,1,0:T(8,128)(2,1)} %shard_map.72.refs_4_), channel_id=1, source_target_pairs={{0,1},{1,0},{2,3},{3,2},{4,5},{5,4},{6,7},{7,6},{8,9},{9,8},{10,11... | collective-permute-start | bytes 1572872 | tf_op jit(solution)/shard_map/ppermute | solution.py:44
  78.9 23.0 %collective-permute-start.14 = (bf16[32,64,128]{2,1,0:T(8,128)(2,1)}, bf16[32,64,128]{2,1,0:T(8,128)(2,1)}, u32[]{:S(2)}, u32[]{:S(2)}) collective-permute-start(bf16[32,64,128]{2,1,0:T(8,128)(2,1)} %shard_map.72.refs_4_), channel_id=1, source_target_pairs={{0,4},{1,5},{2,6},{3,7},{4,0},{5,1},{6,2},{7,3},{8,12},{9,13},{10,... | collective-permute-start | bytes 1572872 | tf_op jit(solution)/shard_map/ppermute | solution.py:44
  79.6 30.3 %collective-permute-start.17 = (bf16[32,64,128]{2,1,0:T(8,128)(2,1)}, bf16[32,64,128]{2,1,0:T(8,128)(2,1)}, u32[]{:S(2)}, u32[]{:S(2)}) collective-permute-start(bf16[32,64,128]{2,1,0:T(8,128)(2,1)} %shard_map.71.refs_4_), channel_id=1, source_target_pairs={{0,1},{1,0},{2,3},{3,2},{4,5},{5,4},{6,7},{7,6},{8,9},{9,8},{10,11... | collective-permute-start | bytes 1572872 | tf_op jit(solution)/shard_map/ppermute | solution.py:44
  89.2 12.7 %collective-permute-start.21 = (bf16[32,64,128]{2,1,0:T(8,128)(2,1)}, bf16[32,64,128]{2,1,0:T(8,128)(2,1)}, u32[]{:S(2)}, u32[]{:S(2)}) collective-permute-start(bf16[32,64,128]{2,1,0:T(8,128)(2,1)} %collective-permute-done.20.refs_6_), channel_id=1, source_target_pairs={{0,1},{1,0},{2,3},{3,2},{4,5},{5,4},{6,7},{7,6},{8,9},{9,8},{10,11... | collective-permute-start | bytes 1572872 | tf_op jit(solution)/shard_map/ppermute | solution.py:44
  96.5 15.2 %collective-permute-start.11 = (bf16[32,64,128]{2,1,0:T(8,128)(2,1)}, bf16[32,64,128]{2,1,0:T(8,128)(2,1)}, u32[]{:S(2)}, u32[]{:S(2)}) collective-permute-start(bf16[32,64,128]{2,1,0:T(8,128)(2,1)} %shard_map.71.refs_4_), channel_id=1, source_target_pairs={{0,2},{1,3},{2,0},{3,1},{4,6},{5,7},{6,4},{7,5},{8,10},{9,11},{10,... | collective-permute-start | bytes 1572872 | tf_op jit(solution)/shard_map/ppermute | solution.py:44
  98.0 18.4 %collective-permute-start.7 = (bf16[129,16,128]{2,1,0:T(8,128)(2,1)}, bf16[129,16,128]{2,1,0:T(8,128)(2,1)}, u32[]{:S(2)}, u32[]{:S(2)}) collective-permute-start(bf16[129,16,128]{2,1,0:T(8,128)(2,1)} %shard_map.69), channel_id=1, source_target_pairs={{0,12},{1,13},{2,14},{3,15},{4,8},{5,9},{6,10},{7,11},{8,4},{9,5},... | collective-permute-start | bytes 1585160 | tf_op jit(solution)/shard_map/ppermute | solution.py:44
  101.9 43.4 %collective-permute-start.18 = (bf16[32,64,128]{2,1,0:T(8,128)(2,1)}, bf16[32,64,128]{2,1,0:T(8,128)(2,1)}, u32[]{:S(2)}, u32[]{:S(2)}) collective-permute-start(bf16[32,64,128]{2,1,0:T(8,128)(2,1)} %collective-permute-done.14.refs_6_), channel_id=1, source_target_pairs={{0,1},{1,0},{2,3},{3,2},{4,5},{5,4},{6,7},{7,6},{8,9},{9,8},{10,11... | collective-permute-start | bytes 1572872 | tf_op jit(solution)/shard_map/ppermute | solution.py:44
  101.9 43.4 %collective-permute-start.15 = (bf16[32,64,128]{2,1,0:T(8,128)(2,1)}, bf16[32,64,128]{2,1,0:T(8,128)(2,1)}, u32[]{:S(2)}, u32[]{:S(2)}) collective-permute-start(bf16[32,64,128]{2,1,0:T(8,128)(2,1)} %collective-permute-done.14.refs_6_), channel_id=1, source_target_pairs={{0,2},{1,3},{2,0},{3,1},{4,6},{5,7},{6,4},{7,5},{8,10},{9,11},{10,... | collective-permute-start | bytes 1572872 | tf_op jit(solution)/shard_map/ppermute | solution.py:44
  109.9 42.8 %collective-permute-start.4 = (bf16[129,16,128]{2,1,0:T(8,128)(2,1)}, bf16[129,16,128]{2,1,0:T(8,128)(2,1)}, u32[]{:S(2)}, u32[]{:S(2)}) collective-permute-start(bf16[129,16,128]{2,1,0:T(8,128)(2,1)} %get-tuple-element.26), channel_id=1, source_target_pairs={{0,6},{1,7},{2,4},{3,5},{4,2},{5,3},{6,0},{7,1},{8,14},{9,15},{10,... | collective-permute-start | bytes 1585160 | tf_op jit(solution)/shard_map/ppermute | solution.py:44
  111.7 41.0 %collective-permute-start.8 = (bf16[129,16,128]{2,1,0:T(8,128)(2,1)}, bf16[129,16,128]{2,1,0:T(8,128)(2,1)}, u32[]{:S(2)}, u32[]{:S(2)}) collective-permute-start(bf16[129,16,128]{2,1,0:T(8,128)(2,1)} %shard_map.70), channel_id=1, source_target_pairs={{0,14},{1,15},{2,12},{3,13},{4,10},{5,11},{6,8},{7,9},{8,6},{9,7},... | collective-permute-start | bytes 1585160 | tf_op jit(solution)/shard_map/ppermute | solution.py:44
  116.4 36.3 %collective-permute-start.12 = (bf16[32,64,128]{2,1,0:T(8,128)(2,1)}, bf16[32,64,128]{2,1,0:T(8,128)(2,1)}, u32[]{:S(2)}, u32[]{:S(2)}) collective-permute-start(bf16[32,64,128]{2,1,0:T(8,128)(2,1)} %collective-permute-done.11.refs_4_), channel_id=1, source_target_pairs={{0,1},{1,0},{2,3},{3,2},{4,5},{5,4},{6,7},{7,6},{8,9},{9,8},{10,11... | collective-permute-start | bytes 1572872 | tf_op jit(solution)/shard_map/ppermute | solution.py:44
  145.3 7.4 %collective-permute-start.16 = (bf16[32,64,128]{2,1,0:T(8,128)(2,1)}, bf16[32,64,128]{2,1,0:T(8,128)(2,1)}, u32[]{:S(2)}, u32[]{:S(2)}) collective-permute-start(bf16[32,64,128]{2,1,0:T(8,128)(2,1)} %collective-permute-done.15.refs_6_), channel_id=1, source_target_pairs={{0,1},{1,0},{2,3},{3,2},{4,5},{5,4},{6,7},{7,6},{8,9},{9,8},{10,11... | collective-permute-start | bytes 1572872 | tf_op jit(solution)/shard_map/ppermute | solution.py:44
  160.1 2.0 collective-permute-start.24
  160.6 3.9 %collective-permute-start.25 = (f32[16,128]{1,0:T(8,128)}, f32[16,128]{1,0:T(8,128)S(1)}, u32[]{:S(2)}, u32[]{:S(2)}) collective-permute-start(f32[16,128]{1,0:T(8,128)} %get-tuple-element.35), channel_id=1, source_target_pairs={{0,2},{1,3},{2,0},{3,1},{4,6},{5,7},{6,4},{7,5},{8,10},{9,11},{10,... | collective-permute-start | bytes 24584 | tf_op jit(solution)/shard_map/ppermute | solution.py:100
  161.3 3.4 %collective-permute-start.26 = (f32[16,128]{1,0:T(8,128)}, f32[16,128]{1,0:T(8,128)S(1)}, u32[]{:S(2)}, u32[]{:S(2)}) collective-permute-start(f32[16,128]{1,0:T(8,128)} %get-tuple-element.35), channel_id=1, source_target_pairs={{0,3},{1,2},{2,1},{3,0},{4,7},{5,6},{6,5},{7,4},{8,11},{9,10},{10,... | collective-permute-start | bytes 24584 | tf_op jit(solution)/shard_map/ppermute | solution.py:100
  165.4 4.4 %collective-permute-start.27 = (f32[16,128]{1,0:T(8,128)S(1)}, f32[16,128]{1,0:T(8,128)S(1)}, u32[]{:S(2)}, u32[]{:S(2)}) collective-permute-start(f32[16,128]{1,0:T(8,128)S(1)} %add_add_fusion.1), channel_id=1, source_target_pairs={{0,4},{1,5},{2,6},{3,7},{4,0},{5,1},{6,2},{7,3},{8,12},{9,13},{10,... | collective-permute-start | bytes 24584 | tf_op jit(solution)/shard_map/ppermute | solution.py:100
  165.4 4.5 %collective-permute-start.28 = (f32[16,128]{1,0:T(8,128)S(1)}, f32[16,128]{1,0:T(8,128)S(1)}, u32[]{:S(2)}, u32[]{:S(2)}) collective-permute-start(f32[16,128]{1,0:T(8,128)S(1)} %add_add_fusion.1), channel_id=1, source_target_pairs={{0,8},{1,9},{2,10},{3,11},{4,12},{5,13},{6,14},{7,15},{8,0},{9,1},... | collective-permute-start | bytes 24584 | tf_op jit(solution)/shard_map/ppermute | solution.py:100
  165.4 6.1 %collective-permute-start.29 = (f32[16,128]{1,0:T(8,128)S(1)}, f32[16,128]{1,0:T(8,128)S(1)}, u32[]{:S(2)}, u32[]{:S(2)}) collective-permute-start(f32[16,128]{1,0:T(8,128)S(1)} %add_add_fusion.1), channel_id=1, source_target_pairs={{0,12},{1,13},{2,14},{3,15},{4,8},{5,9},{6,10},{7,11},{8,4},{9,5},... | collective-permute-start | bytes 24584 | tf_op jit(solution)/shard_map/ppermute | solution.py:100
  174.8 12.8 %collective-permute-start.33 = (bf16[32,64,128]{2,1,0:T(8,128)(2,1)S(1)}, bf16[32,64,128]{2,1,0:T(8,128)(2,1)}, u32[]{:S(2)}, u32[]{:S(2)}) collective-permute-start(bf16[32,64,128]{2,1,0:T(8,128)(2,1)S(1)} %get-tuple-element.36.refs_10_), channel_id=1, source_target_pairs={{0,2},{1,5},{2,6},{3,1},{4,0},{5,9},{6,10},{7,3},{8,4},{9,13},{10,... | collective-permute-start | bytes 1572872 | tf_op jit(solution)/shard_map/ppermute | solution.py:44
  176.2 11.5 %collective-permute-start.30 = (bf16[32,64,128]{2,1,0:T(8,128)(2,1)S(1)}, bf16[32,64,128]{2,1,0:T(8,128)(2,1)}, u32[]{:S(2)}, u32[]{:S(2)}) collective-permute-start(bf16[32,64,128]{2,1,0:T(8,128)(2,1)S(1)} %get-tuple-element.36.refs_10_), channel_id=1, source_target_pairs={{0,4},{1,3},{2,0},{3,7},{4,8},{5,1},{6,2},{7,11},{8,12},{9,5},{10,... | collective-permute-start | bytes 1572872 | tf_op jit(solution)/shard_map/ppermute | solution.py:44
  176.9 13.6 %collective-permute-start.32 = (bf16[32,64,128]{2,1,0:T(8,128)(2,1)S(1)}, bf16[32,64,128]{2,1,0:T(8,128)(2,1)S(1)}, u32[]{:S(2)}, u32[]{:S(2)}) collective-permute-start(bf16[32,64,128]{2,1,0:T(8,128)(2,1)S(1)} %get-tuple-element.36.refs_10_), channel_id=1, source_target_pairs={{0,1},{1,0},{2,3},{3,2},{4,5},{5,4},{6,7},{7,6},{8,9},{9,8},{10,11... | collective-permute-start | bytes 1572872 | tf_op jit(solution)/shard_map/ppermute | solution.py:44
  187.6 3.7 %collective-permute-start.34 = (bf16[32,64,128]{2,1,0:T(8,128)(2,1)}, bf16[32,64,128]{2,1,0:T(8,128)(2,1)S(1)}, u32[]{:S(2)}, u32[]{:S(2)}) collective-permute-start(bf16[32,64,128]{2,1,0:T(8,128)(2,1)} %collective-permute-done.33.refs_14_), channel_id=1, source_target_pairs={{0,1},{1,0},{2,3},{3,2},{4,5},{5,4},{6,7},{7,6},{8,9},{9,8},{10,11... | collective-permute-start | bytes 1572872 | tf_op jit(solution)/shard_map/ppermute | solution.py:44
  187.6 4.5 %collective-permute-start.35 = (bf16[32,64,128]{2,1,0:T(8,128)(2,1)}, bf16[32,64,128]{2,1,0:T(8,128)(2,1)}, u32[]{:S(2)}, u32[]{:S(2)}) collective-permute-start(bf16[32,64,128]{2,1,0:T(8,128)(2,1)} %collective-permute-done.30.refs_12_), channel_id=1, source_target_pairs={{0,1},{1,0},{2,3},{3,2},{4,5},{5,4},{6,7},{7,6},{8,9},{9,8},{10,11... | collective-permute-start | bytes 1572872 | tf_op jit(solution)/shard_map/ppermute | solution.py:44
  188.1 14.8 %collective-permute-start.31 = (bf16[32,64,128]{2,1,0:T(8,128)(2,1)}, bf16[32,64,128]{2,1,0:T(8,128)(2,1)}, u32[]{:S(2)}, u32[]{:S(2)}) collective-permute-start(bf16[32,64,128]{2,1,0:T(8,128)(2,1)} %collective-permute-done.30.refs_12_), channel_id=1, source_target_pairs={{0,4},{1,3},{2,0},{3,7},{4,8},{5,1},{6,2},{7,11},{8,12},{9,5},{10,... | collective-permute-start | bytes 1572872 | tf_op jit(solution)/shard_map/ppermute | solution.py:44
  190.5 12.5 %collective-permute-start.37 = (bf16[32,64,128]{2,1,0:T(8,128)(2,1)}, bf16[32,64,128]{2,1,0:T(8,128)(2,1)}, u32[]{:S(2)}, u32[]{:S(2)}) collective-permute-start(bf16[32,64,128]{2,1,0:T(8,128)(2,1)} %collective-permute-done.33.refs_14_), channel_id=1, source_target_pairs={{0,2},{1,5},{2,6},{3,1},{4,0},{5,9},{6,10},{7,3},{8,4},{9,13},{10,... | collective-permute-start | bytes 1572872 | tf_op jit(solution)/shard_map/ppermute | solution.py:44
  203.0 2.5 %collective-permute-start.39 = (bf16[32,64,128]{2,1,0:T(8,128)(2,1)}, bf16[32,64,128]{2,1,0:T(8,128)(2,1)}, u32[]{:S(2)}, u32[]{:S(2)}) collective-permute-start(bf16[32,64,128]{2,1,0:T(8,128)(2,1)} %shard_map.79.refs_10_), channel_id=1, source_target_pairs={{0,1},{1,0},{2,3},{3,2},{4,5},{5,4},{6,7},{7,6},{8,9},{9,8},{10,11... | collective-permute-start | bytes 1572872 | tf_op jit(solution)/shard_map/ppermute | solution.py:44
  203.0 3.0 %collective-permute-start.38 = (bf16[32,64,128]{2,1,0:T(8,128)(2,1)}, bf16[32,64,128]{2,1,0:T(8,128)(2,1)}, u32[]{:S(2)}, u32[]{:S(2)}) collective-permute-start(bf16[32,64,128]{2,1,0:T(8,128)(2,1)} %collective-permute-done.37.refs_12_), channel_id=1, source_target_pairs={{0,1},{1,0},{2,3},{3,2},{4,5},{5,4},{6,7},{7,6},{8,9},{9,8},{10,11... | collective-permute-start | bytes 1572872 | tf_op jit(solution)/shard_map/ppermute | solution.py:44
  203.5 14.6 %collective-permute-start.36 = (bf16[32,64,128]{2,1,0:T(8,128)(2,1)}, bf16[32,64,128]{2,1,0:T(8,128)(2,1)}, u32[]{:S(2)}, u32[]{:S(2)}) collective-permute-start(bf16[32,64,128]{2,1,0:T(8,128)(2,1)} %shard_map.79.refs_10_), channel_id=1, source_target_pairs={{0,4},{1,3},{2,0},{3,7},{4,8},{5,1},{6,2},{7,11},{8,12},{9,5},{10,... | collective-permute-start | bytes 1572872 | tf_op jit(solution)/shard_map/ppermute | solution.py:44
  205.4 12.7 %collective-permute-start.41 = (bf16[32,64,128]{2,1,0:T(8,128)(2,1)}, bf16[32,64,128]{2,1,0:T(8,128)(2,1)}, u32[]{:S(2)}, u32[]{:S(2)}) collective-permute-start(bf16[32,64,128]{2,1,0:T(8,128)(2,1)} %collective-permute-done.37.refs_12_), channel_id=1, source_target_pairs={{0,2},{1,5},{2,6},{3,1},{4,0},{5,9},{6,10},{7,3},{8,4},{9,13},{10,... | collective-permute-start | bytes 1572872 | tf_op jit(solution)/shard_map/ppermute | solution.py:44
  218.1 2.3 collective-permute-start.43
  218.1 3.0 %collective-permute-start.42 = (bf16[32,64,128]{2,1,0:T(8,128)(2,1)}, bf16[32,64,128]{2,1,0:T(8,128)(2,1)}, u32[]{:S(2)}, u32[]{:S(2)}) collective-permute-start(bf16[32,64,128]{2,1,0:T(8,128)(2,1)} %collective-permute-done.41.refs_12_), channel_id=1, source_target_pairs={{0,1},{1,0},{2,3},{3,2},{4,5},{5,4},{6,7},{7,6},{8,9},{9,8},{10,11... | collective-permute-start | bytes 1572872 | tf_op jit(solution)/shard_map/ppermute | solution.py:44
  218.6 9.7 %collective-permute-start.40 = (bf16[32,64,128]{2,1,0:T(8,128)(2,1)}, bf16[32,64,128]{2,1,0:T(8,128)(2,1)}, u32[]{:S(2)}, u32[]{:S(2)}) collective-permute-start(bf16[32,64,128]{2,1,0:T(8,128)(2,1)} %shard_map.81.refs_10_), channel_id=1, source_target_pairs={{0,4},{1,3},{2,0},{3,7},{4,8},{5,1},{6,2},{7,11},{8,12},{9,5},{10,... | collective-permute-start | bytes 1572872 | tf_op jit(solution)/shard_map/ppermute | solution.py:44
  228.3 2.3 collective-permute-start.44
  (9 other events, 8.5 us)
